TPU v7x, 32 devices: a whole 2x2x4 slice. The times are simulated.
32 devices in a mesh: seq: 4 (over z), expert: 4 (over y, core), rep: 2 (over x).
Axes of the slice: x: 2, y: 2, z: 4, core: 2. Of those that a mesh axis runs over, the one named last changes fastest.
Arguments:
- query_rows: bfloat16 [4, 1024, 512], P('expert', ('seq', 'rep')), may hold values from -150 to 150
- key_rows: bfloat16 [4, 1024, 512], P('expert', ('seq', 'rep')), may hold values from -150 to 150
- value_rows: bfloat16 [4, 1024, 512], P('expert', ('seq', 'rep')), may hold values from -6 to 6
- doc_lengths: int32 [4, 8], P('expert'), may hold values from 1 to 512, 1024 in all within a row
- residual: bfloat16 [4, 1024, 512], P('expert', ('seq', 'rep')), may hold values from -6 to 6
- out_proj: bfloat16 [512, 512], replicated, may hold values from -0.25 to 0.25
- router: bfloat16 [512, 4], replicated, may hold values from -0.5 to 0.5
- expert_choice: int32 [4, 1024, 1], P('expert', ('seq', 'rep')), may hold values from 0 to 3, as said below
- weight_in: bfloat16 [4, 512, 512], P('expert'), may hold values from -0.25 to 0.25
- weight_out: bfloat16 [4, 512, 512], P('expert'), may hold values from -0.5 to 0.5
- grad_out: bfloat16 [4, 1024, 512], P('expert', ('seq', 'rep')), may hold values from -6 to 6
Outputs:
- layer_out: bfloat16 [4, 1024, 512], P('expert', ('seq', 'rep'))
- grad_mixed: bfloat16 [4, 1024, 512], P('expert', ('seq', 'rep'))
- grad_weight_in: float32 [4, 512, 512], P('expert', ('seq', 'rep'))
- grad_weight_out: float32 [4, 512, 512], P('expert', ('seq', 'rep'))
Inputs may be any that keep to these rules, and one draw needn't show every extreme that they name: `expert_choice`: A routing group is one index of seq and one of rep; each group has one hot expert, the same on all of the group's devices. Among one device's tokens, its group's hot expert is named between 49 and 64 times, exactly 64 times on some device and 48 + 1 times on some device; every other expert is named at most 48 times, and on every device some expert other than the hot one is named exactly 48 times. `doc_lengths`: each sequence's lengths sum to 1024; the longest is exactly half of 1024.
All inputs are finite; a program needn't handle non-finite values.
Results may differ from a plain program's by a relative error of at most 0.02.
Values may be sent and summed in bfloat16 or wider, within the bound.
No kernel may reach another device: no remote copies, remote signals or barrier semaphores. Data moves between devices by JAX's collectives and lax.ppermute only.
A program may use at most 64 MiB of HBM per device.

v0:
```python
import math

import jax
import jax.numpy as jnp
from jax import lax
from jax.sharding import PartitionSpec as P

D = 512
H = 16
HD = 32


norm_eps = 1e-06
masked_score = -1e30


def document_ids(lengths, positions):
    boundaries = jnp.cumsum(lengths)
    return jnp.sum((positions[:, None] >= boundaries[None, :-1]).astype(jnp.int32), axis=1)


def expert_pass(token_rows, grad_rows, weight_up, weight_down):
    hidden_pre = jnp.dot(token_rows, weight_up, preferred_element_type=jnp.float32)
    sigmoid_pre = jax.nn.sigmoid(hidden_pre)
    activated = (hidden_pre * sigmoid_pre).astype(jnp.bfloat16)
    produced = jnp.dot(activated, weight_down, preferred_element_type=jnp.float32).astype(
        jnp.bfloat16
    )
    act_grad = jnp.dot(grad_rows, weight_down.T, preferred_element_type=jnp.float32)
    pre_grad = (act_grad * sigmoid_pre * (1.0 + hidden_pre * (1.0 - sigmoid_pre))).astype(
        jnp.bfloat16
    )
    token_grad = jnp.dot(pre_grad, weight_up.T, preferred_element_type=jnp.float32).astype(
        jnp.bfloat16
    )
    up_grad = jnp.dot(token_rows.T, pre_grad, preferred_element_type=jnp.float32)
    down_grad = jnp.dot(activated.T, grad_rows, preferred_element_type=jnp.float32)
    return (produced, token_grad, up_grad, down_grad)


def empty_state(head_count, row_count):
    return (
        jnp.full((head_count, row_count), masked_score, jnp.float32),
        jnp.zeros((head_count, row_count), jnp.float32),
        jnp.zeros((head_count, row_count, HD), jnp.float32),
    )


def attend_fold(
    fold_state, query_heads, query_pos, query_docs, key_heads, value_heads, key_pos, key_docs
):
    maxima, totals, accum = fold_state
    scores = jnp.einsum(
        "qhd,khd->hqk", query_heads, key_heads, preferred_element_type=jnp.float32
    ) * (1.0 / math.sqrt(HD))
    visible = (key_pos[None, :] <= query_pos[:, None]) & (key_docs[None, :] == query_docs[:, None])
    scores = jnp.where(visible[None], scores, masked_score)
    new_max = jnp.maximum(maxima, jnp.max(scores, axis=2))
    weights = jnp.where(visible[None], jnp.exp(scores - new_max[:, :, None]), 0.0)
    factor = jnp.exp(maxima - new_max)
    totals = totals * factor + jnp.sum(weights, axis=2)
    accum = accum * factor[:, :, None] + jnp.einsum(
        "hqk,khd->hqd",
        weights.astype(jnp.bfloat16),
        value_heads,
        preferred_element_type=jnp.float32,
    )
    return (new_max, totals, accum)


def finish_heads(fold_state):
    maxima, totals, accum = fold_state
    result = accum / totals[:, :, None]
    return result.transpose(1, 0, 2).reshape(result.shape[1], -1).astype(jnp.bfloat16)


def local(
    query_rows,
    key_rows,
    value_rows,
    doc_lengths,
    residual,
    out_proj,
    router,
    expert_choice,
    weight_in,
    weight_out,
    grad_out,
):
    tok_count = query_rows.shape[1]
    seq_rank = lax.axis_index(("seq", "rep"))
    lengths = doc_lengths[0]
    query_pos = seq_rank * tok_count + jnp.arange(tok_count, dtype=jnp.int32)
    query_heads = query_rows[0].reshape(tok_count, H, HD)
    query_docs = document_ids(lengths, query_pos)
    key_part = lax.all_gather(key_rows, ("seq", "rep"), axis=1, tiled=True)
    value_part = lax.all_gather(value_rows, ("seq", "rep"), axis=1, tiled=True)
    span = key_part.shape[1]
    block = math.gcd(span, 512)

    def key_block(state, block_index):
        first_row = block_index * block
        key_block_rows = lax.dynamic_slice_in_dim(key_part[0], first_row, block, 0).reshape(
            block, H, HD
        )
        value_block_rows = lax.dynamic_slice_in_dim(value_part[0], first_row, block, 0).reshape(
            block, H, HD
        )
        key_pos = first_row + jnp.arange(block, dtype=jnp.int32)
        return (
            attend_fold(
                state,
                query_heads,
                query_pos,
                query_docs,
                key_block_rows,
                value_block_rows,
                key_pos,
                document_ids(lengths, key_pos),
            ),
            None,
        )

    result_state, unused = lax.scan(
        key_block, empty_state(H, tok_count), jnp.arange(span // block, dtype=jnp.int32)
    )
    attended = finish_heads(result_state)
    mixed = (
        residual[0].astype(jnp.float32)
        + jnp.dot(attended, out_proj, preferred_element_type=jnp.float32)
    ).astype(jnp.bfloat16)
    mixed_f = mixed.astype(jnp.float32)
    inv_rms = lax.rsqrt(jnp.mean(mixed_f * mixed_f, axis=1, keepdims=True) + norm_eps)
    normed = (mixed_f * inv_rms).astype(jnp.bfloat16)
    expert_count = router.shape[1]
    chosen = expert_choice[0, :, 0]
    expert_ids = jnp.arange(expert_count, dtype=jnp.int32)
    one_hot = chosen[:, None] == expert_ids[None, :]
    logits = jnp.dot(normed, router, preferred_element_type=jnp.float32)
    gate_value = jax.nn.sigmoid(jnp.sum(jnp.where(one_hot, logits, 0.0), axis=1))
    grad_rows = grad_out[0]
    scaled_grad = (gate_value[:, None] * grad_rows.astype(jnp.float32)).astype(jnp.bfloat16)
    capacity = max(2, (3 * tok_count + 2 * expert_count - 1) // (2 * expert_count))
    hot_capacity = min(4 * capacity, tok_count // 2)
    is_hot = chosen < 0
    cold_token = jnp.logical_not(is_hot)
    cold_hits = (one_hot & cold_token[:, None]).astype(jnp.int32)
    slot_rank = jnp.sum(jnp.cumsum(cold_hits, axis=0) * cold_hits, axis=1) - 1
    slots = jnp.where(cold_token, chosen * hot_capacity + slot_rank, expert_count * hot_capacity)
    send_rows = (
        jnp.zeros((expert_count * hot_capacity, D), jnp.bfloat16)
        .at[slots]
        .set(normed, mode="drop")
        .reshape(expert_count, hot_capacity, D)
    )
    send_grads = (
        jnp.zeros((expert_count * hot_capacity, D), jnp.bfloat16)
        .at[slots]
        .set(scaled_grad, mode="drop")
        .reshape(expert_count, hot_capacity, D)
    )
    got_rows, got_grads = (
        lax.all_to_all(send_rows, "expert", split_axis=0, concat_axis=0, tiled=True),
        lax.all_to_all(send_grads, "expert", split_axis=0, concat_axis=0, tiled=True),
    )
    produced, token_grads, grad_in_own, grad_out_own = expert_pass(
        got_rows.reshape(-1, D), got_grads.reshape(-1, D), weight_in[0], weight_out[0]
    )
    back_out, back_grad = (
        lax.all_to_all(
            produced.reshape(expert_count, hot_capacity, D),
            "expert",
            split_axis=0,
            concat_axis=0,
            tiled=True,
        ),
        lax.all_to_all(
            token_grads.reshape(expert_count, hot_capacity, D),
            "expert",
            split_axis=0,
            concat_axis=0,
            tiled=True,
        ),
    )
    safe_slots = jnp.clip(slots, 0, expert_count * hot_capacity - 1)
    expert_result = back_out.reshape(-1, D)[safe_slots]
    normed_grad = back_grad.reshape(-1, D)[safe_slots]
    result_f = expert_result.astype(jnp.float32)
    layer_out = (mixed_f + gate_value[:, None] * result_f).astype(jnp.bfloat16)
    gate_grad = jnp.sum(grad_rows.astype(jnp.float32) * result_f, axis=1)
    logit_grad = gate_grad * gate_value * (1.0 - gate_value)
    router_cols = jnp.dot(
        one_hot.astype(jnp.bfloat16), router.T, preferred_element_type=jnp.float32
    )
    total_grad = normed_grad.astype(jnp.float32) + logit_grad[:, None] * router_cols
    mean_term = jnp.mean(total_grad * mixed_f, axis=1, keepdims=True)
    input_grad = inv_rms * total_grad - mixed_f * inv_rms * inv_rms * inv_rms * mean_term
    grad_mixed = (grad_rows.astype(jnp.float32) + input_grad).astype(jnp.bfloat16)
    share_in, share_out = (
        lax.psum_scatter(
            grad_in_own.astype(jnp.bfloat16), ("seq", "rep"), scatter_dimension=0, tiled=True
        ).astype(jnp.float32),
        lax.psum_scatter(
            grad_out_own.astype(jnp.bfloat16), ("seq", "rep"), scatter_dimension=0, tiled=True
        ).astype(jnp.float32),
    )
    return (layer_out[None], grad_mixed[None], share_in[None], share_out[None])


def solution(mesh):
    in_specs = (
        P("expert", ("seq", "rep"), None),
        P("expert", ("seq", "rep"), None),
        P("expert", ("seq", "rep"), None),
        P("expert", None),
        P("expert", ("seq", "rep"), None),
        P(),
        P(),
        P("expert", ("seq", "rep"), None),
        P("expert", None, None),
        P("expert", None, None),
        P("expert", ("seq", "rep"), None),
    )
    out_specs = (
        P("expert", ("seq", "rep"), None),
        P("expert", ("seq", "rep"), None),
        P("expert", ("seq", "rep"), None),
        P("expert", ("seq", "rep"), None),
    )
    return jax.shard_map(local, mesh=mesh, in_specs=in_specs, out_specs=out_specs, check_vma=False)
```

profile of v0, /device:TPU:0, one launch (start us, length us, event | category | flops | bytes accessed | tf_op | source)
XLA Modules:
  0.0 281.1 jit_solution(3071479818868768176)
XLA Ops:
  7.2 1.7 copy.22
  9.0 1.7 copy.24
  11.6 1.0 copy.23
  15.7 37.2 %all-gather.3.cloned.1.call-done = bf16[1,1024,512]{1,2,0:T(8,128)(2,1)} async-done(((bf16[1,128,512]{1,2,0:T(8,128)(2,1)}), bf16[1,1024,512]{1,2,0:T(8,128)(2,1)}) %all-gather.3.cloned.1.call-update) | async-done | bytes 1048592 | tf_op jit(solution)/shard_map/all_gather | solution.py:96
  52.9 41.1 %all-gather.5.cloned.1.call-done = bf16[1,1024,512]{1,2,0:T(8,128)(2,1)} async-done(((bf16[1,128,512]{1,2,0:T(8,128)(2,1)}), bf16[1,1024,512]{1,2,0:T(8,128)(2,1)}) %all-gather.5.cloned.1.call-update) | async-done | bytes 1048592 | tf_op jit(solution)/shard_map/all_gather | solution.py:97
  94.0 21.1 %while.17 = (s32[]{:T(128)}, f32[16,128]{1,0:T(8,128)S(1)}, f32[16,128]{1,0:T(8,128)S(1)}, f32[16,128,32]{1,2,0:T(8,128)S(1)}, s32[2]{0:T(128)S(1)}, /*index=5*/...) while((s32[]{:T(128)}, f32[16,128]{1,0:T(8,128)S(1)}, ...), condition=%wide.region_6.7_spmd.clone, body=%wide.region_2.6_spmd.clone.sunk | while | flops 148263552 | bytes 33566540 | solution.py:124
  95.3 1.3 constant_dynamic-slice_fusion.3
  96.9 2.9 %fusion.70 = (f32[16,128]{1,0:T(8,128)S(1)}, f32[16,512,128]{2,1,0:T(8,128)}) fusion(pred[128,512]{0,1:T(8,128)(4,1)S(1)} %compare_and_fusion.2, bf16[512,16,32]{0,2,1:T(8,128)(2,1)S(1)} %bitcast.114, bf16[128,16,32]{0,2,1:T(8,128)(2,1)S(1)} %get-tuple-element.328), kind=kOutput, calls=%fused_computation.7.clone.1 | convolution fusion | flops 70252544 | bytes 4923392 | tf_op jit(solution)/shard_map/while/body/eval_jaxpr/qhd,khd->hqk/dot_general | solution.py:53
  99.8 3.3 %fusion.71 = f32[16,128]{1,0:T(8,128)S(1)} fusion(f32[16,512,128]{2,1,0:T(8,128)} %get-tuple-element.286, f32[16,128]{1,0:T(8,128)S(1)} %select_maximum_fusion.2, pred[128,512]{0,1:T(8,128)(4,1)S(1)} %compare_and_fusion.2), kind=kLoop, calls=%fused_computation.9.clone.1 | loop fusion | flops 5240832 | bytes 4276224 | tf_op jit(solution)/shard_map/while/body/eval_jaxpr/reduce_sum | solution.py:61
  103.2 1.3 fusion.73
  105.8 1.3 constant_dynamic-slice_fusion.3
  107.4 2.9 %fusion.70 = (f32[16,128]{1,0:T(8,128)S(1)}, f32[16,512,128]{2,1,0:T(8,128)}) fusion(pred[128,512]{0,1:T(8,128)(4,1)S(1)} %compare_and_fusion.2, bf16[512,16,32]{0,2,1:T(8,128)(2,1)S(1)} %bitcast.114, bf16[128,16,32]{0,2,1:T(8,128)(2,1)S(1)} %get-tuple-element.328), kind=kOutput, calls=%fused_computation.7.clone.1 | convolution fusion | flops 70252544 | bytes 4923392 | tf_op jit(solution)/shard_map/while/body/eval_jaxpr/qhd,khd->hqk/dot_general | solution.py:53
  110.4 3.3 %fusion.71 = f32[16,128]{1,0:T(8,128)S(1)} fusion(f32[16,512,128]{2,1,0:T(8,128)} %get-tuple-element.286, f32[16,128]{1,0:T(8,128)S(1)} %select_maximum_fusion.2, pred[128,512]{0,1:T(8,128)(4,1)S(1)} %compare_and_fusion.2), kind=kLoop, calls=%fused_computation.9.clone.1 | loop fusion | flops 5240832 | bytes 4276224 | tf_op jit(solution)/shard_map/while/body/eval_jaxpr/reduce_sum | solution.py:61
  113.8 1.3 fusion.73
  115.6 1.2 scatter_custom_fusion
  116.8 8.6 %all_to_all.20 = bf16[4,64,512]{2,1,0:T(8,128)(2,1)S(1)} all-to-all(bf16[4,64,512]{2,1,0:T(8,128)(2,1)S(1)} %bitcast.122), channel_id=1, replica_groups=mesh['seq'=4,'expert'=4,'rep'=2] {'expert'}, dimensions={0} | all-to-all | bytes 524288 | tf_op jit(solution)/shard_map/all_to_all | solution.py:163
  125.8 1.0 convolution_convert_fusion.3
  126.8 3.4 %all-to-all-start.1 = ((bf16[4,64,512]{2,1,0:T(8,128)(2,1)}), bf16[4,64,512]{2,1,0:T(8,128)(2,1)S(1)}, u32[]{:S(2)}, u32[]{:S(2)}) async-start(bf16[4,64,512]{2,1,0:T(8,128)(2,1)} %bitcast.15), calls=%async_computation.1 | async-start | bytes 524288 | tf_op jit(solution)/shard_map/all_to_all | solution.py:170
  130.5 5.7 %all-to-all-done.1 = bf16[4,64,512]{2,1,0:T(8,128)(2,1)S(1)} async-done(((bf16[4,64,512]{2,1,0:T(8,128)(2,1)}), bf16[4,64,512]{2,1,0:T(8,128)(2,1)S(1)}, u32[]{:S(2)}, u32[]{:S(2)}) %all-to-all-start.1) | async-done | bytes 262176 | tf_op jit(solution)/shard_map/all_to_all | solution.py:170
  136.2 0.8 gather_fusion
  137.2 1.2 scatter_custom_fusion.1
  138.4 8.4 %all_to_all.21 = bf16[4,64,512]{2,1,0:T(8,128)(2,1)S(1)} all-to-all(bf16[4,64,512]{2,1,0:T(8,128)(2,1)S(1)} %bitcast.121), channel_id=1, replica_groups=mesh['seq'=4,'expert'=4,'rep'=2] {'expert'}, dimensions={0} | all-to-all | bytes 524288 | tf_op jit(solution)/shard_map/all_to_all | solution.py:164
  146.9 1.2 convolution_convert_fusion
  148.4 1.1 convolution_convert_fusion.2
  149.5 3.4 %all-to-all-start.3 = ((bf16[4,64,512]{2,1,0:T(8,128)(2,1)}), bf16[4,64,512]{2,1,0:T(8,128)(2,1)S(1)}, u32[]{:S(2)}, u32[]{:S(2)}) async-start(bf16[4,64,512]{2,1,0:T(8,128)(2,1)} %bitcast.23), calls=%async_computation.3 | async-start | bytes 524288 | tf_op jit(solution)/shard_map/all_to_all | solution.py:177
  153.0 1.1 convolution_convert_fusion.1
  154.1 4.8 %all-to-all-done.3 = bf16[4,64,512]{2,1,0:T(8,128)(2,1)S(1)} async-done(((bf16[4,64,512]{2,1,0:T(8,128)(2,1)}), bf16[4,64,512]{2,1,0:T(8,128)(2,1)S(1)}, u32[]{:S(2)}, u32[]{:S(2)}) %all-to-all-start.3) | async-done | bytes 262176 | tf_op jit(solution)/shard_map/all_to_all | solution.py:177
  160.1 0.9 fusion.31
  161.0 47.5 %reduce-scatter.5.cloned.1.call-done = bf16[64,512]{1,0:T(8,128)(2,1)} async-done(((bf16[512,512]{1,0:T(8,128)(2,1)}), bf16[64,512]{1,0:T(8,128)(2,1)}) %reduce-scatter.5.cloned.1.call-update) | async-done | bytes 65552 | tf_op jit(solution)/shard_map/reduce_scatter | solution.py:203
  208.4 1.5 bitcast_convert_fusion
  209.9 63.1 %reduce-scatter.3.cloned.1.call-done = bf16[64,512]{1,0:T(8,128)(2,1)} async-done(((bf16[512,512]{1,0:T(8,128)(2,1)}), bf16[64,512]{1,0:T(8,128)(2,1)}) %reduce-scatter.3.cloned.1.call-update) | async-done | bytes 65552 | tf_op jit(solution)/shard_map/reduce_scatter | solution.py:200
  273.0 1.5 bitcast_convert_fusion.1
  (72 shorter events, 8.8 us)
Async XLA Ops:
  7.2 118.6 %copy-start = (bf16[1,512,512]{2,1,0:T(8,128)(2,1)S(1)}, bf16[1,512,512]{2,1,0:T(8,128)(2,1)}, u32[]{:S(2)}) copy-start(bf16[1,512,512]{2,1,0:T(8,128)(2,1)} %param.22) | copy-start | bytes 1572868
  7.2 45.8 %all-gather.3.cloned.1.call-start = ((), (), s32[]{:S(2)}) async-start(), calls=%async_computation.6 | async-start | bytes 1179648 | tf_op jit(solution)/shard_map/all_gather | solution.py:96
  9.0 85.0 %all-gather.5.cloned.1.call-start = ((), (), s32[]{:S(2)}) async-start(), calls=%async_computation.7 | async-start | bytes 1179648 | tf_op jit(solution)/shard_map/all_gather | solution.py:97
  94.0 21.2 %copy-start.4 = (bf16[512,512]{1,0:T(8,128)(2,1)S(1)}, bf16[512,512]{1,0:T(8,128)(2,1)}, u32[]{:S(2)}) copy-start(bf16[512,512]{1,0:T(8,128)(2,1)} %param.18) | copy-start | bytes 1572868
  94.0 21.2 %copy-start.5 = (bf16[1,128,512]{2,1,0:T(8,128)(2,1)S(1)}, bf16[1,128,512]{2,1,0:T(8,128)(2,1)}, u32[]{:S(2)}) copy-start(bf16[1,128,512]{2,1,0:T(8,128)(2,1)} %param.17) | copy-start | bytes 393220
  94.0 31.5 %copy-start.2 = (bf16[1,512,512]{2,1,0:T(8,128)(2,1)S(1)}, bf16[1,512,512]{2,1,0:T(8,128)(2,1)}, u32[]{:S(2)}) copy-start(bf16[1,512,512]{2,1,0:T(8,128)(2,1)} %param.21) | copy-start | bytes 1572868
  99.8 3.4 %copy-start.1 = (f32[16,512,128]{2,1,0:T(8,128)S(1)}, f32[16,512,128]{2,1,0:T(8,128)}, u32[]{:S(2)}) copy-start(f32[16,512,128]{2,1,0:T(8,128)} %get-tuple-element.286) | copy-start | bytes 12582916 | tf_op jit(solution)/shard_map/while
  110.4 3.4 %copy-start.1 = (f32[16,512,128]{2,1,0:T(8,128)S(1)}, f32[16,512,128]{2,1,0:T(8,128)}, u32[]{:S(2)}) copy-start(f32[16,512,128]{2,1,0:T(8,128)} %get-tuple-element.286) | copy-start | bytes 12582916 | tf_op jit(solution)/shard_map/while
  115.2 15.1 %copy-start.6 = (bf16[512,4]{0,1:T(4,128)(2,1)S(1)}, bf16[512,4]{0,1:T(4,128)(2,1)}, u32[]{:S(2)}) copy-start(bf16[512,4]{0,1:T(4,128)(2,1)} %param.19) | copy-start | bytes 12292
  115.2 15.1 %copy-start.7 = (s32[1,128,1]{1,2,0:T(1,128)S(1)}, s32[1,128,1]{1,2,0:T(1,128)}, u32[]{:S(2)}) copy-start(s32[1,128,1]{1,2,0:T(1,128)} %param.20) | copy-start | bytes 1540
  115.2 21.8 %copy-start.3 = (bf16[1,128,512]{2,1,0:T(8,128)(2,1)S(1)}, bf16[1,128,512]{2,1,0:T(8,128)(2,1)}, u32[]{:S(2)}) copy-start(bf16[1,128,512]{2,1,0:T(8,128)(2,1)} %param.23) | copy-start | bytes 393220
  126.8 9.4 %all-to-all-start.1 = ((bf16[4,64,512]{2,1,0:T(8,128)(2,1)}), bf16[4,64,512]{2,1,0:T(8,128)(2,1)S(1)}, u32[]{:S(2)}, u32[]{:S(2)}) async-start(bf16[4,64,512]{2,1,0:T(8,128)(2,1)} %bitcast.15), calls=%async_computation.1 | async-start | bytes 524288 | tf_op jit(solution)/shard_map/all_to_all | solution.py:170
  130.2 78.2 %reduce-scatter.5.cloned.1.call-start = ((), (), s32[]{:S(2)}) async-start(), calls=%async_computation.9 | async-start | bytes 589824 | tf_op jit(solution)/shard_map/reduce_scatter | solution.py:203
  149.5 9.4 %all-to-all-start.3 = ((bf16[4,64,512]{2,1,0:T(8,128)(2,1)}), bf16[4,64,512]{2,1,0:T(8,128)(2,1)S(1)}, u32[]{:S(2)}, u32[]{:S(2)}) async-start(bf16[4,64,512]{2,1,0:T(8,128)(2,1)} %bitcast.23), calls=%async_computation.3 | async-start | bytes 524288 | tf_op jit(solution)/shard_map/all_to_all | solution.py:177
  152.9 120.1 %reduce-scatter.3.cloned.1.call-start = ((), (), s32[]{:S(2)}) async-start(), calls=%async_computation.8 | async-start | bytes 589824 | tf_op jit(solution)/shard_map/reduce_scatter | solution.py:200
Sparse Core Ops, SparseCore 0:
  10.6 42.2 all-gather.2
  55.6 38.4 all-gather.4
  148.2 60.2 reduce-scatter.4
  212.0 61.0 reduce-scatter.2
where the time goes:
time: 282 us; the launch traced here: 281 us
  waiting for transfers between devices  199 us (71%)
  other arithmetic  17.5 us (6%)
  blocking collectives  17.1 us (6%)
  matrix products  14.5 us (5%)
  between operations  14 us (5%)
  local copies, waits for them, and re-layouts  10.2 us (4%)
  starting transfers between devices  6.97 us (2%)
    reduce_scatter x1, waiting for transfers between devices, local(): lax.psum_scatter(grad_in_own.astype(jnp.bfloat16), ('seq', 'rep'), scatte...  63.1 us
    reduce_scatter x1, waiting for transfers between devices, local(): lax.psum_scatter(grad_out_own.astype(jnp.bfloat16), ('seq', 'rep'), scatt...  47.5 us
    all_gather x1, waiting for transfers between devices, local(): value_part = lax.all_gather(value_rows, ('seq', 'rep'), axis=1, tiled=True)  41.1 us
    all_gather x1, waiting for transfers between devices, local(): key_part = lax.all_gather(key_rows, ('seq', 'rep'), axis=1, tiled=True)  37.2 us
    all_to_all x1, blocking collectives, local(): lax.all_to_all(send_rows, 'expert', split_axis=0, concat_axis=0, tiled=True)  8.64 us
    all_to_all x1, blocking collectives, local(): lax.all_to_all(send_grads, 'expert', split_axis=0, concat_axis=0, tiled=T...  8.42 us
    reduce_sum x2, other arithmetic, attend_fold(): totals = totals * factor + jnp.sum(weights, axis=2)  6.65 us
    dot_general x2, matrix products, attend_fold(): jnp.einsum('qhd,khd->hqk', query_heads, key_heads, preferred_element_type...  5.82 us
  transfers between devices with their start and end apart: 6, of which 6 were waited for; matrix products, arithmetic and copies ran while one was open for 5% of the time, Pallas kernels for 0%

commit v1 on v0

v1 whole, which is shorter than its diff:
```python
import functools
import math

import jax
import jax.numpy as jnp
from jax import lax
from jax.experimental import pallas as pl
from jax.experimental.pallas import tpu as pltpu
from jax.sharding import PartitionSpec as P

HD = 32
norm_eps = 1e-06
masked_score = -1e30
VMEM_LIMIT = 48 * 1024 * 1024
NT = (((1,), (1,)), ((), ()))
TN = (((0,), (0,)), ((), ()))


def whole_vmem(count):
    return [pl.BlockSpec(memory_space=pltpu.VMEM)] * count


def params():
    return pltpu.CompilerParams(vmem_limit_bytes=VMEM_LIMIT)


def dot(a, b, dims=None):
    if dims is None:
        return jnp.dot(a, b, preferred_element_type=jnp.float32)
    return lax.dot_general(a, b, dims, preferred_element_type=jnp.float32)


def slot_matrix(choice, expert_count, hot_capacity):
    tok = choice.shape[1]
    one_hot = lax.broadcasted_iota(jnp.int32, (expert_count, tok), 0) == choice
    hits = one_hot.astype(jnp.float32).astype(jnp.bfloat16)
    earlier = lax.broadcasted_iota(jnp.int32, (tok, tok), 0) <= lax.broadcasted_iota(
        jnp.int32, (tok, tok), 1
    )
    counted = dot(hits, earlier.astype(jnp.float32).astype(jnp.bfloat16))
    rank = jnp.sum(jnp.where(one_hot, counted, 0.0), axis=0, keepdims=True) - 1.0
    slots = choice * hot_capacity + rank.astype(jnp.int32)
    rows = lax.broadcasted_iota(jnp.int32, (expert_count * hot_capacity, tok), 0)
    return (rows == slots).astype(jnp.float32).astype(jnp.bfloat16)


def pack_kernel(query_ref, key_ref, value_ref, sent_ref):
    ranks = sent_ref.shape[0]
    width = sent_ref.shape[1] // 3
    for place, ref in enumerate((query_ref, key_ref, value_ref)):
        turned = ref[...].T
        for rank in range(ranks):
            sent_ref[rank, place * width : (place + 1) * width, :] = turned[
                rank * width : (rank + 1) * width, :
            ]


def grad_dispatch_kernel(expert_count, hot_capacity, choice_ref, grad_ref, sent_ref):
    placed = slot_matrix(choice_ref[...], expert_count, hot_capacity)
    rows = dot(placed, grad_ref[...]).astype(jnp.bfloat16)
    for rep in range(sent_ref.shape[0]):
        sent_ref[rep] = rows


def attend_kernel(lengths_ref, got_ref, out_ref, keys_ref):
    ranks, width3, tok = got_ref.shape
    width = width3 // 3
    heads = width // HD
    reach = (ranks + 1) // 2
    for rank in range(ranks):
        keys_ref[rank * tok : (rank + 1) * tok, :] = got_ref[rank, width : 2 * width, :].T
    bounds = []
    total = jnp.int32(0)
    for doc in range(lengths_ref.shape[1] - 1):
        total = total + lengths_ref[0, doc]
        bounds.append(total)
    scale = math.log2(math.e) / math.sqrt(HD)
    head_of_row = lax.broadcasted_iota(jnp.int32, (width, tok), 0) // HD
    for block in range(ranks):
        first = max(0, block - reach)
        span = (block - first + 1) * tok
        query = got_ref[block, 0:width, :]
        spread = jnp.concatenate(
            [jnp.where(head_of_row == head, query, jnp.zeros_like(query)) for head in range(heads)],
            axis=1,
        )
        position = block * tok + lax.broadcasted_iota(jnp.int32, (1, tok), 1)
        begin = jnp.zeros((1, tok), jnp.int32)
        for bound in bounds:
            begin = jnp.maximum(begin, jnp.where(position >= bound, bound, 0))
        key_position = first * tok + lax.broadcasted_iota(jnp.int32, (span, tok), 0)
        visible = (key_position >= begin) & (key_position <= position)
        scores = dot(keys_ref[first * tok : first * tok + span, :], spread)
        values = jnp.concatenate(
            [got_ref[rank, 2 * width : 3 * width, :] for rank in range(first, block + 1)], axis=1
        )
        for head in range(heads):
            part = jnp.where(visible, scores[:, head * tok : (head + 1) * tok], masked_score)
            top = jnp.max(part, axis=0, keepdims=True)
            weights = jnp.exp2((part - top) * scale)
            totals = jnp.sum(weights, axis=0, keepdims=True)
            summed = dot(
                values[head * HD : (head + 1) * HD, :], weights.astype(jnp.bfloat16)
            )
            out_ref[block, head * HD : (head + 1) * HD, :] = (summed / totals).astype(jnp.bfloat16)


def mix_kernel(
    expert_count, hot_capacity, turned_ref, residual_ref, proj_ref, choice_ref, mixed_ref, sent_ref
):
    attended = turned_ref[...].T
    mixed = (residual_ref[...].astype(jnp.float32) + dot(attended, proj_ref[...])).astype(
        jnp.bfloat16
    )
    mixed_ref[...] = mixed
    mixed_f = mixed.astype(jnp.float32)
    inv_rms = lax.rsqrt(jnp.mean(mixed_f * mixed_f, axis=1, keepdims=True) + norm_eps)
    normed = (mixed_f * inv_rms).astype(jnp.bfloat16)
    placed = slot_matrix(choice_ref[...], expert_count, hot_capacity)
    rows = dot(placed, normed).astype(jnp.bfloat16)
    for rep in range(sent_ref.shape[0]):
        sent_ref[rep] = rows


def expert_kernel(
    ids_ref, rows_ref, grads_ref, up_ref, down_ref, router_ref, back_ref, terms_ref, up_acc, down_acc
):
    reps, count, width = rows_ref.shape
    sources, unused, capacity, unused_width = back_ref.shape
    parts, kinds, strip, unused_hidden = terms_ref.shape
    expert = ids_ref[0]
    own = ids_ref[1]
    up = up_ref[...]
    down = down_ref[...]
    router = router_ref[...]
    expert_lane = lax.broadcasted_iota(jnp.int32, (count, router.shape[0]), 1) == expert

    def chunk(rep, first):
        rows = rows_ref[rep]
        pre = dot(rows, up)
        sigmoid_pre = jax.nn.sigmoid(pre)
        activated = (pre * sigmoid_pre).astype(jnp.bfloat16)
        logits = dot(rows, router, NT)
        gate = jax.nn.sigmoid(
            jnp.sum(jnp.where(expert_lane, logits, 0.0), axis=1, keepdims=True)
        )
        scaled = (gate * grads_ref[rep].astype(jnp.float32)).astype(jnp.bfloat16)
        act_grad = dot(scaled, down, NT)
        pre_grad = (act_grad * sigmoid_pre * (1.0 + pre * (1.0 - sigmoid_pre))).astype(
            jnp.bfloat16
        )
        up_term = dot(rows, pre_grad, TN)
        down_term = dot(activated, scaled, TN)
        if first:
            up_acc[...] = up_term
            down_acc[...] = down_term
            produced = dot(activated, down).astype(jnp.bfloat16)
            token_grad = dot(pre_grad, up, NT).astype(jnp.bfloat16)
            for source in range(sources):
                back_ref[source, 0] = produced[source * capacity : (source + 1) * capacity]
                back_ref[source, 1] = token_grad[source * capacity : (source + 1) * capacity]
        else:
            up_acc[...] += up_term
            down_acc[...] += down_term

    chunk(own, True)

    def other(step, carry):
        chunk(lax.rem(own + step, reps), False)
        return carry

    if reps > 1:
        lax.fori_loop(1, reps, other, 0)
    for part in range(parts):
        first_row = pl.multiple_of((part * reps + own) * strip, strip)
        terms_ref[part, 0] = up_acc[pl.ds(first_row, strip), :].astype(jnp.bfloat16)
        terms_ref[part, 1] = down_acc[pl.ds(first_row, strip), :].astype(jnp.bfloat16)


def finish_kernel(
    hot_capacity, back_ref, mixed_ref, grad_ref, choice_ref, router_ref, layer_ref, grad_mixed_ref
):
    sources, kinds, capacity, width = back_ref.shape
    tok = mixed_ref.shape[0]
    choice = choice_ref[...]
    placed = slot_matrix(choice, sources, hot_capacity)
    router = router_ref[...]
    mixed_f = mixed_ref[...].astype(jnp.float32)
    inv_rms = lax.rsqrt(jnp.mean(mixed_f * mixed_f, axis=1, keepdims=True) + norm_eps)
    normed = (mixed_f * inv_rms).astype(jnp.bfloat16)
    one_hot = lax.broadcasted_iota(jnp.int32, (sources, tok), 0) == choice
    logits = dot(router, normed, NT)
    logit_row = jnp.sum(jnp.where(one_hot, logits, 0.0), axis=0, keepdims=True)
    logit = jnp.broadcast_to(logit_row, (8, tok)).T[:, 0:1]
    gate = jax.nn.sigmoid(logit)
    results = jnp.concatenate([back_ref[source, 0] for source in range(sources)], axis=0)
    grads = jnp.concatenate([back_ref[source, 1] for source in range(sources)], axis=0)
    result_f = dot(placed, results, TN)
    normed_grad = dot(placed, grads, TN)
    grad_f = grad_ref[...].astype(jnp.float32)
    layer_ref[...] = (mixed_f + gate * result_f).astype(jnp.bfloat16)
    gate_grad = jnp.sum(grad_f * result_f, axis=1, keepdims=True)
    logit_grad = gate_grad * gate * (1.0 - gate)
    router_cols = dot(one_hot.astype(jnp.float32).astype(jnp.bfloat16), router, TN)
    total_grad = normed_grad + logit_grad * router_cols
    mean_term = jnp.mean(total_grad * mixed_f, axis=1, keepdims=True)
    input_grad = inv_rms * total_grad - mixed_f * inv_rms * inv_rms * inv_rms * mean_term
    grad_mixed_ref[...] = (grad_f + input_grad).astype(jnp.bfloat16)


def sum_kernel(terms_ref, up_ref, down_ref):
    up_ref[...] = jnp.sum(terms_ref[:, 0].astype(jnp.float32), axis=0)
    down_ref[...] = jnp.sum(terms_ref[:, 1].astype(jnp.float32), axis=0)


def shape(dims, dtype=jnp.bfloat16):
    return jax.ShapeDtypeStruct(dims, dtype)


def local(
    seq_count,
    rep_count,
    query_rows,
    key_rows,
    value_rows,
    doc_lengths,
    residual,
    out_proj,
    router,
    expert_choice,
    weight_in,
    weight_out,
    grad_out,
):
    tok, width = query_rows.shape[1:]
    hidden = weight_in.shape[2]
    ranks = seq_count * rep_count
    share = width // ranks
    expert_count = router.shape[1]
    capacity = max(2, (3 * tok + 2 * expert_count - 1) // (2 * expert_count))
    hot_capacity = min(4 * capacity, tok // 2)
    slots = expert_count * hot_capacity
    choice = expert_choice.reshape(1, tok)
    router_rows = router.T

    def call(body, out_shape, specs, scratch=()):
        return pl.pallas_call(
            body,
            out_shape=out_shape,
            in_specs=specs,
            out_specs=jax.tree.map(lambda unused: pl.BlockSpec(memory_space=pltpu.VMEM), out_shape),
            scratch_shapes=list(scratch),
            compiler_params=params(),
        )

    packed = call(pack_kernel, shape((ranks, 3 * share, tok)), whole_vmem(3))(
        query_rows[0], key_rows[0], value_rows[0]
    )
    got = lax.all_to_all(packed, ("seq", "rep"), split_axis=0, concat_axis=0, tiled=True)
    sent_grads = call(
        functools.partial(grad_dispatch_kernel, expert_count, hot_capacity),
        shape((rep_count, slots, width)),
        whole_vmem(2),
    )(choice, grad_out[0])
    got_grads = lax.all_to_all(
        sent_grads.reshape(rep_count * expert_count, hot_capacity, width),
        ("rep", "expert"),
        split_axis=0,
        concat_axis=0,
        tiled=True,
    ).reshape(rep_count, slots, width)
    smem = pl.BlockSpec(memory_space=pltpu.SMEM)
    attended = call(
        attend_kernel,
        shape((ranks, share, tok)),
        [smem] + whole_vmem(1),
        [pltpu.VMEM((ranks * tok, share), jnp.bfloat16)],
    )(doc_lengths, got)
    turned = lax.all_to_all(
        attended, ("seq", "rep"), split_axis=0, concat_axis=0, tiled=True
    ).reshape(width, tok)
    mixed, sent_rows = call(
        functools.partial(mix_kernel, expert_count, hot_capacity),
        (shape((tok, width)), shape((rep_count, slots, width))),
        whole_vmem(4),
    )(turned, residual[0], out_proj, choice)
    got_rows = lax.all_to_all(
        sent_rows.reshape(rep_count * expert_count, hot_capacity, width),
        ("rep", "expert"),
        split_axis=0,
        concat_axis=0,
        tiled=True,
    ).reshape(rep_count, slots, width)
    ids = jnp.stack([lax.axis_index("expert"), lax.axis_index("rep")]).astype(jnp.int32)
    strip = width // ranks
    back, terms = call(
        expert_kernel,
        (
            shape((expert_count, 2, hot_capacity, width)),
            shape((seq_count, 2, strip, hidden)),
        ),
        [smem] + whole_vmem(5),
        [pltpu.VMEM((width, hidden), jnp.float32), pltpu.VMEM((hidden, width), jnp.float32)],
    )(ids, got_rows, got_grads, weight_in[0], weight_out[0], router_rows)
    got_terms = lax.all_to_all(terms, "seq", split_axis=0, concat_axis=0, tiled=True)
    got_back = lax.all_to_all(back, "expert", split_axis=0, concat_axis=0, tiled=True)
    layer_out, grad_mixed = call(
        functools.partial(finish_kernel, hot_capacity),
        (shape((tok, width)), shape((tok, width))),
        whole_vmem(5),
    )(got_back, mixed, grad_out[0], choice, router_rows)
    share_in, share_out = call(
        sum_kernel,
        (shape((strip, hidden), jnp.float32), shape((strip, width), jnp.float32)),
        whole_vmem(1),
    )(got_terms)
    return (layer_out[None], grad_mixed[None], share_in[None], share_out[None])


def solution(mesh):
    rows = P("expert", ("seq", "rep"), None)
    in_specs = (
        rows,
        rows,
        rows,
        P("expert", None),
        rows,
        P(),
        P(),
        rows,
        P("expert", None, None),
        P("expert", None, None),
        rows,
    )
    body = functools.partial(local, mesh.shape["seq"], mesh.shape["rep"])
    return jax.shard_map(
        body, mesh=mesh, in_specs=in_specs, out_specs=(rows, rows, rows, rows), check_vma=False
    )
```

time: 282 us -> 97.6 us (0.35)
  waiting for transfers between devices: 199 us -> 34.5 us
  other arithmetic: 17.5 us -> 0.08 us
  matrix products: 14.5 us -> 0 us
  blocking collectives: 17.1 us -> 30.5 us
  between operations: 14 us -> 0.73 us
  Pallas kernels: 0 us -> 12.9 us
  starting transfers between devices: 6.97 us -> 14.2 us
  local copies, waits for them, and re-layouts: 10.2 us -> 4.05 us
    reduce_scatter x2 -> x0, waiting for transfers between devices: 111 us -> none  [the longest x1 63.1 us: local(): lax.psum_scatter(grad_in_own.astype(jnp.bfloat16), ('seq', 'rep'), scatte...]
    all_gather x2 -> x0, waiting for transfers between devices: 78.3 us -> none  [the longest x1 41.1 us: local(): value_part = lax.all_gather(value_rows, ('seq', 'rep'), axis=1, tiled=True)]
    all_to_all x2 -> x4, waiting for transfers between devices: 10.5 us -> 34.5 us  [the longest x1 13 us: local(): lax.all_to_all(terms, 'seq', split_axis=0, concat_axis=0, tiled=True)]
    dot_general x13 -> x0, matrix products: 14.5 us -> none  [the longest x2 5.82 us: attend_fold(): jnp.einsum('qhd,khd->hqk', query_heads, key_heads, preferred_element_type...]
    all_to_all x2, blocking collectives: 17.1 us -> 30.5 us  [the longest x1 19.1 us: local(): lax.all_to_all(packed, ('seq', 'rep'), split_axis=0, concat_axis=0, tiled...]
    pallas_call x0 -> x7, Pallas kernels: none -> 12.9 us  [the longest x1 4.29 us: local(): call(attend_kernel, shape((ranks, share, tok)), [smem] + whole_vmem(1), [...]
    reduce_sum x7 -> x0, other arithmetic: 7.72 us -> none  [the longest x2 6.65 us: attend_fold(): totals = totals * factor + jnp.sum(weights, axis=2)]
    all_to_all x2 -> x4, starting transfers between devices: 6.81 us -> 14.2 us  [the longest x1 3.62 us: local(): lax.all_to_all(sent_grads.reshape(rep_count * expert_count, hot_capacity,...]
  transfers between devices with their start and end apart: 6 -> 4, of which waited for: 6 -> 4; matrix products, arithmetic and copies ran while one was open for 5% -> 0% of each run, Pallas kernels for 0% -> 4%
where the time goes in v1:
time: 97.6 us; the launch traced here: 97 us
  waiting for transfers between devices  34.5 us (35%)
  blocking collectives  30.5 us (31%)
  starting transfers between devices  14.2 us (15%)
  Pallas kernels  12.9 us (13%)
  local copies, waits for them, and re-layouts  4.05 us (4%)
    all_to_all x1, blocking collectives, local(): lax.all_to_all(packed, ('seq', 'rep'), split_axis=0, concat_axis=0, tiled...  19.1 us
    all_to_all x1, waiting for transfers between devices, local(): lax.all_to_all(terms, 'seq', split_axis=0, concat_axis=0, tiled=True)  13 us
    all_to_all x1, blocking collectives, local(): lax.all_to_all(back, 'expert', split_axis=0, concat_axis=0, tiled=True)  11.4 us
    all_to_all x1, waiting for transfers between devices, local(): lax.all_to_all(sent_rows.reshape(rep_count * expert_count, hot_capacity,...  8.68 us
    all_to_all x1, waiting for transfers between devices, local(): lax.all_to_all(sent_grads.reshape(rep_count * expert_count, hot_capacity,...  7.36 us
    all_to_all x1, waiting for transfers between devices, local(): lax.all_to_all(attended, ('seq', 'rep'), split_axis=0, concat_axis=0, til...  5.47 us
    pallas_call x1, Pallas kernels, local(): call(attend_kernel, shape((ranks, share, tok)), [smem] + whole_vmem(1), [...  4.29 us
    unnamed x22, local copies, waits for them, and re-layouts  4.05 us
  transfers between devices with their start and end apart: 4, of which 4 were waited for; matrix products, arithmetic and copies ran while one was open for 0% of the time, Pallas kernels for 4%

profile of v1, /device:TPU:0, one launch (start us, length us, event | category | flops | bytes accessed | tf_op | source)
XLA Modules:
  0.0 97.0 jit_solution(3917677014333413876)
XLA Ops:
  0.6 0.0 copy-start.4
  0.6 0.9 copy-done.4
  1.5 0.9 copy-done.5
  2.4 0.9 copy-done.6
  3.3 0.2 shard_map.138
  3.5 0.0 copy-start.10
  3.5 19.1 %all_to_all.30.got_ref = bf16[8,192,128]{2,1,0:T(8,128)(2,1)S(1)} all-to-all(bf16[8,192,128]{2,1,0:T(8,128)(2,1)S(1)} %shard_map.138), channel_id=1, replica_groups=mesh['seq'=4,'expert'=4,'rep'=2] {'seq','rep'}, dimensions={0} | all-to-all | bytes 786432 | tf_op jit(solution)/shard_map/all_to_all | solution.py:259
  22.7 0.0 copy-done.10
  22.7 4.3 %shard_map.139 = bf16[8,64,128]{2,1,0:T(8,128)(2,1)} custom-call(s32[1,8]{1,0:T(1,128)S(1)} %copy-done.10, bf16[8,192,128]{2,1,0:T(8,128)(2,1)S(1)} %all_to_all.30.got_ref), custom_call_target="tpu_custom_call" | custom-call | tf_op jit(solution)/shard_map/pallas_call | solution.py:273
  27.0 3.5 %all-to-all-start.1 = ((bf16[8,64,128]{2,1,0:T(8,128)(2,1)}), bf16[8,64,128]{2,1,0:T(8,128)(2,1)S(1)}, u32[]{:S(2)}, u32[]{:S(2)}) async-start(bf16[8,64,128]{2,1,0:T(8,128)(2,1)} %shard_map.139), calls=%async_computation.1 | async-start | bytes 262144 | tf_op jit(solution)/shard_map/all_to_all | solution.py:279
  30.5 0.0 copy-start.9
  30.5 0.0 copy-done.3
  30.5 0.6 copy-done.9
  31.1 1.1 %shard_map.141 = bf16[2,256,512]{2,1,0:T(8,128)(2,1)} custom-call(s32[1,128]{1,0:T(1,128)S(1)} %bitcast.33, bf16[128,512]{1,0:T(8,128)(2,1)S(1)} %bitcast.25), custom_call_target="tpu_custom_call" | custom-call | tf_op jit(solution)/shard_map/pallas_call | solution.py:260
  32.3 5.5 %all-to-all-done.1 = bf16[8,64,128]{2,1,0:T(8,128)(2,1)S(1)} async-done(((bf16[8,64,128]{2,1,0:T(8,128)(2,1)}), bf16[8,64,128]{2,1,0:T(8,128)(2,1)S(1)}, u32[]{:S(2)}, u32[]{:S(2)}) %all-to-all-start.1) | async-done | bytes 131104 | tf_op jit(solution)/shard_map/all_to_all | solution.py:279
  37.8 3.6 %all-to-all-start.3 = ((bf16[8,64,512]{2,1,0:T(8,128)(2,1)}), bf16[8,64,512]{2,1,0:T(8,128)(2,1)S(1)}, u32[]{:S(2)}, u32[]{:S(2)}) async-start(bf16[8,64,512]{2,1,0:T(8,128)(2,1)} %bitcast.11), calls=%async_computation.3 | async-start | bytes 1048576 | tf_op jit(solution)/shard_map/all_to_all | solution.py:265
  41.4 0.0 copy-done.2
  41.4 0.0 copy-done.7
  41.4 1.4 %shard_map.140 = (bf16[128,512]{1,0:T(8,128)(2,1)S(1)}, bf16[2,256,512]{2,1,0:T(8,128)(2,1)}) custom-call(bf16[512,128]{1,0:T(8,128)(2,1)S(1)} %bitcast.24, bf16[128,512]{1,0:T(8,128)(2,1)S(1)} %bitcast.30, bf16[512,512]{1,0:T(8,128)(2,1)S(1)} %copy-done.2, s32[1,128]{1,0:T(1,128)S(1)} %bitcast.34), custom_call_target="tpu_custom_call" | custom-call | tf_op jit(solution)/shard_map/pallas_call | solution.py:282
  42.8 7.4 %all-to-all-done.3 = bf16[8,64,512]{2,1,0:T(8,128)(2,1)S(1)} async-done(((bf16[8,64,512]{2,1,0:T(8,128)(2,1)}), bf16[8,64,512]{2,1,0:T(8,128)(2,1)S(1)}, u32[]{:S(2)}, u32[]{:S(2)}) %all-to-all-start.3) | async-done | bytes 524320 | tf_op jit(solution)/shard_map/all_to_all | solution.py:265
  50.1 3.6 %all-to-all-start.2 = ((bf16[8,64,512]{2,1,0:T(8,128)(2,1)}), bf16[8,64,512]{2,1,0:T(8,128)(2,1)S(1)}, u32[]{:S(2)}, u32[]{:S(2)}) async-start(bf16[8,64,512]{2,1,0:T(8,128)(2,1)} %bitcast.8), calls=%async_computation.2 | async-start | bytes 1048576 | tf_op jit(solution)/shard_map/all_to_all | solution.py:287
  53.8 0.1 pad_add_fusion.ids_ref
  53.9 8.7 %all-to-all-done.2 = bf16[8,64,512]{2,1,0:T(8,128)(2,1)S(1)} async-done(((bf16[8,64,512]{2,1,0:T(8,128)(2,1)}), bf16[8,64,512]{2,1,0:T(8,128)(2,1)S(1)}, u32[]{:S(2)}, u32[]{:S(2)}) %all-to-all-start.2) | async-done | bytes 524320 | tf_op jit(solution)/shard_map/all_to_all | solution.py:287
  62.5 0.0 copy-done
  62.5 0.0 copy-done.1
  62.5 0.7 copy-done.8
  63.2 3.8 %shard_map.142 = (bf16[4,2,64,512]{3,2,1,0:T(8,128)(2,1)S(1)}, bf16[4,2,64,512]{3,2,1,0:T(8,128)(2,1)}) custom-call(s32[2]{0:T(128)S(1)} %pad_add_fusion.ids_ref, bf16[2,256,512]{2,1,0:T(8,128)(2,1)S(1)} %bitcast.21, bf16[2,256,512]{2,1,0:T(8,128)(2,1)S(1)} %bitcast.20, bf16[512,512]{1,0:T(8,128)(2,1)S(1)} %bitcast.22, bf16[512,512]{1,0:T(8,128)(2,1)S(1)} %bitcast.23, ...), custom_call_target="tpu_custom_call" | custom-call | tf_op jit(solution)/shard_map/pallas_call | solution.py:296
  67.0 11.4 %all_to_all.31.back_ref = bf16[4,2,64,512]{3,2,1,0:T(8,128)(2,1)S(1)} all-to-all(bf16[4,2,64,512]{3,2,1,0:T(8,128)(2,1)S(1)} %get-tuple-element.13), channel_id=1, replica_groups=mesh['seq'=4,'expert'=4,'rep'=2] {'expert'}, dimensions={0} | all-to-all | bytes 1048576 | tf_op jit(solution)/shard_map/all_to_all | solution.py:306
  78.4 3.5 %all-to-all-start.5 = ((bf16[4,2,64,512]{3,2,1,0:T(8,128)(2,1)}), bf16[4,2,64,512]{3,2,1,0:T(8,128)(2,1)S(1)}, u32[]{:S(2)}, u32[]{:S(2)}) async-start(bf16[4,2,64,512]{3,2,1,0:T(8,128)(2,1)} %get-tuple-element.17), calls=%async_computation.5 | async-start | bytes 1048576 | tf_op jit(solution)/shard_map/all_to_all | solution.py:305
  81.9 1.4 %shard_map.143 = (bf16[128,512]{1,0:T(8,128)(2,1)}, bf16[128,512]{1,0:T(8,128)(2,1)}) custom-call(bf16[4,2,64,512]{3,2,1,0:T(8,128)(2,1)S(1)} %all_to_all.31.back_ref, bf16[128,512]{1,0:T(8,128)(2,1)S(1)} %get-tuple-element.14.mixed_ref, bf16[128,512]{1,0:T(8,128)(2,1)S(1)} %bitcast.26, s32[1,128]{1,0:T(1,128)S(1)} %bitcast.35, bf16[4,512]{1,0:T(4,128)(2,1)S(1)} %bitcast.32), custom_call_target="tpu_custom_call" | custom-call | tf_op jit(solution)/shard_map/pallas_call | solution.py:307
  83.3 13.0 %all-to-all-done.5.terms_ref = bf16[4,2,64,512]{3,2,1,0:T(8,128)(2,1)S(1)} async-done(((bf16[4,2,64,512]{3,2,1,0:T(8,128)(2,1)}), bf16[4,2,64,512]{3,2,1,0:T(8,128)(2,1)S(1)}, u32[]{:S(2)}, u32[]{:S(2)}) %all-to-all-start.5) | async-done | bytes 524320 | tf_op jit(solution)/shard_map/all_to_all | solution.py:305
  96.3 0.7 shard_map.144
  (8 shorter events, 0.0 us)
Async XLA Ops:
  0.6 0.9 copy-start.4
  1.5 0.9 copy-start.5
  2.4 0.9 copy-start.6
  3.5 19.2 %copy-start.10 = (s32[1,8]{1,0:T(1,128)S(1)}, s32[1,8]{1,0:T(1,128)}, u32[]{:S(2)}) copy-start(s32[1,8]{1,0:T(1,128)} %lengths_ref.1) | copy-start | bytes 100
  27.0 3.5 %copy-start.3 = (bf16[1,128,512]{2,1,0:T(8,128)(2,1)S(1)}, bf16[1,128,512]{2,1,0:T(8,128)(2,1)}, u32[]{:S(2)}) copy-start(bf16[1,128,512]{2,1,0:T(8,128)(2,1)} %param.21) | copy-start | bytes 393220
  27.0 10.8 %all-to-all-start.1 = ((bf16[8,64,128]{2,1,0:T(8,128)(2,1)}), bf16[8,64,128]{2,1,0:T(8,128)(2,1)S(1)}, u32[]{:S(2)}, u32[]{:S(2)}) async-start(bf16[8,64,128]{2,1,0:T(8,128)(2,1)} %shard_map.139), calls=%async_computation.1 | async-start | bytes 262144 | tf_op jit(solution)/shard_map/all_to_all | solution.py:279
  30.5 0.7 copy-start.9
  37.7 3.6 %copy-start.2 = (bf16[512,512]{1,0:T(8,128)(2,1)S(1)}, bf16[512,512]{1,0:T(8,128)(2,1)}, u32[]{:S(2)}) copy-start(bf16[512,512]{1,0:T(8,128)(2,1)} %proj_ref.1) | copy-start | bytes 1572868
  37.7 3.6 %copy-start.7 = (bf16[1,128,512]{2,1,0:T(8,128)(2,1)S(1)}, bf16[1,128,512]{2,1,0:T(8,128)(2,1)}, u32[]{:S(2)}) copy-start(bf16[1,128,512]{2,1,0:T(8,128)(2,1)} %param.15) | copy-start | bytes 393220
  37.8 12.4 %all-to-all-start.3 = ((bf16[8,64,512]{2,1,0:T(8,128)(2,1)}), bf16[8,64,512]{2,1,0:T(8,128)(2,1)S(1)}, u32[]{:S(2)}, u32[]{:S(2)}) async-start(bf16[8,64,512]{2,1,0:T(8,128)(2,1)} %bitcast.11), calls=%async_computation.3 | async-start | bytes 1048576 | tf_op jit(solution)/shard_map/all_to_all | solution.py:265
  50.1 12.4 %copy-start = (bf16[1,512,512]{2,1,0:T(8,128)(2,1)S(1)}, bf16[1,512,512]{2,1,0:T(8,128)(2,1)}, u32[]{:S(2)}) copy-start(bf16[1,512,512]{2,1,0:T(8,128)(2,1)} %param.19) | copy-start | bytes 1572868
  50.1 12.4 %copy-start.1 = (bf16[1,512,512]{2,1,0:T(8,128)(2,1)S(1)}, bf16[1,512,512]{2,1,0:T(8,128)(2,1)}, u32[]{:S(2)}) copy-start(bf16[1,512,512]{2,1,0:T(8,128)(2,1)} %param.20) | copy-start | bytes 1572868
  50.1 12.4 %all-to-all-start.2 = ((bf16[8,64,512]{2,1,0:T(8,128)(2,1)}), bf16[8,64,512]{2,1,0:T(8,128)(2,1)S(1)}, u32[]{:S(2)}, u32[]{:S(2)}) async-start(bf16[8,64,512]{2,1,0:T(8,128)(2,1)} %bitcast.8), calls=%async_computation.2 | async-start | bytes 1048576 | tf_op jit(solution)/shard_map/all_to_all | solution.py:287
  62.5 0.7 copy-start.8
  78.4 17.8 %all-to-all-start.5 = ((bf16[4,2,64,512]{3,2,1,0:T(8,128)(2,1)}), bf16[4,2,64,512]{3,2,1,0:T(8,128)(2,1)S(1)}, u32[]{:S(2)}, u32[]{:S(2)}) async-start(bf16[4,2,64,512]{3,2,1,0:T(8,128)(2,1)} %get-tuple-element.17), calls=%async_computation.5 | async-start | bytes 1048576 | tf_op jit(solution)/shard_map/all_to_all | solution.py:305

commit v2 on v1

v2 whole, which is shorter than its diff:
```python
import functools
import math

import jax
import jax.numpy as jnp
from jax import lax
from jax.experimental import pallas as pl
from jax.experimental.pallas import tpu as pltpu
from jax.sharding import PartitionSpec as P

HD = 32
norm_eps = 1e-06
masked_score = -1e30
VMEM_LIMIT = 48 * 1024 * 1024
MOST_PERMUTES = 16
NT = (((1,), (1,)), ((), ()))
TN = (((0,), (0,)), ((), ()))


def dot(a, b, dims=None):
    if dims is None:
        return jnp.dot(a, b, preferred_element_type=jnp.float32)
    return lax.dot_general(a, b, dims, preferred_element_type=jnp.float32)


def away(index, offset, size):
    if size & (size - 1) == 0:
        return index ^ offset
    return (index + offset) % size


def back_from(index, offset, size):
    if size & (size - 1) == 0:
        return index ^ offset
    return (index - offset + size) % size


class Group:
    def __init__(self, axes, sizes):
        self.axes, self.sizes = tuple(axes), tuple(sizes)
        self.count = math.prod(sizes)

    def split(self, flat):
        coords = []
        for size in reversed(self.sizes):
            coords.append(flat % size)
            flat = flat // size
        return coords[::-1]

    def moved(self, flat, offset, step):
        place = 0
        for coord, part, size in zip(self.split(flat), self.split(offset), self.sizes):
            place = place * size + step(coord, part, size)
        return place

    def target(self, flat, offset):
        return self.moved(flat, offset, away)

    def source(self, flat, offset):
        return self.moved(flat, offset, back_from)

    def exchange(self, chunks, inverse=False):
        to, start = (self.source, self.target) if inverse else (self.target, self.source)
        if self.count <= MOST_PERMUTES:
            order = sorted(range(1, self.count), key=lambda k: -k)
            got = {0: chunks[0]}
            for k in order:
                pairs = [(i, to(i, k)) for i in range(self.count)]
                got[k] = lax.ppermute(chunks[k], self.axes, pairs)
            return [got[k] for k in range(self.count)]
        me = lax.axis_index(self.axes)
        steps = jnp.arange(self.count, dtype=jnp.int32)
        sent_to = jax.vmap(lambda k: to(me, k))(steps)
        placed = jnp.zeros((self.count,), jnp.int32).at[sent_to].set(steps)
        stacked = jnp.stack(chunks)[placed]
        got = lax.all_to_all(stacked, self.axes, split_axis=0, concat_axis=0, tiled=True)
        came_from = jax.vmap(lambda k: start(me, k))(steps)
        ordered = got[came_from]
        return [ordered[k] for k in range(self.count)]


def merged(chunks, most):
    if len(chunks) <= most:
        return list(chunks)
    return [jnp.concatenate(chunks, axis=0)]


def rows_of(refs):
    if len(refs) == 1:
        return refs[0][...]
    return jnp.concatenate([ref[...] for ref in refs], axis=0)


def slot_matrix(choice, own, expert_count, hot_capacity):
    tok = choice.shape[1]
    offset = back_from(choice, own, expert_count)
    one_hot = lax.broadcasted_iota(jnp.int32, (expert_count, tok), 0) == offset
    hits = one_hot.astype(jnp.float32).astype(jnp.bfloat16)
    earlier = lax.broadcasted_iota(jnp.int32, (tok, tok), 0) <= lax.broadcasted_iota(
        jnp.int32, (tok, tok), 1
    )
    counted = dot(hits, earlier.astype(jnp.float32).astype(jnp.bfloat16))
    rank = jnp.sum(jnp.where(one_hot, counted, 0.0), axis=0, keepdims=True) - 1.0
    slots = offset * hot_capacity + rank.astype(jnp.int32)
    rows = lax.broadcasted_iota(jnp.int32, (expert_count * hot_capacity, tok), 0)
    return (rows == slots).astype(jnp.float32).astype(jnp.bfloat16)


def pack_kernel(share, to_ref, query_ref, key_ref, value_ref, *refs):
    sent_refs, (held_ref, turned_ref, sems) = refs[:-3], refs[-3:]
    copies = [
        pltpu.make_async_copy(ref, held_ref.at[place], sems.at[place])
        for place, ref in enumerate((query_ref, key_ref, value_ref))
    ]
    for copy in copies:
        copy.start()
    for place, copy in enumerate(copies):
        copy.wait()
        turned_ref[place] = held_ref[place].T
        for k, sent_ref in enumerate(sent_refs):
            first = pl.multiple_of(to_ref[k] * share, share)
            sent_ref[place * share : (place + 1) * share, :] = turned_ref[
                place, pl.ds(first, share), :
            ]


def grad_dispatch_kernel(hot_capacity, own_ref, choice_ref, grad_ref, *sent_refs):
    placed = slot_matrix(choice_ref[...], own_ref[0], len(sent_refs), hot_capacity)
    rows = dot(placed, grad_ref[...]).astype(jnp.bfloat16)
    for k, sent_ref in enumerate(sent_refs):
        sent_ref[...] = rows[k * hot_capacity : (k + 1) * hot_capacity]


def attend_kernel(ranks, to_ref, from_ref, lengths_ref, *refs):
    got_refs, out_refs = refs[:ranks], refs[ranks : 2 * ranks]
    query_ref, keys_ref, values_ref, result_ref = refs[2 * ranks :]
    width, tok = out_refs[0].shape
    heads = width // HD
    reach = (ranks + 1) // 2
    for k, got_ref in enumerate(got_refs):
        rank = from_ref[k]
        query_ref[rank] = got_ref[0:width, :]
        keys_ref[pl.ds(pl.multiple_of(rank * tok, tok), tok), :] = got_ref[width : 2 * width, :].T
        values_ref[rank] = got_ref[2 * width : 3 * width, :]
    bounds = []
    total = jnp.int32(0)
    for doc in range(lengths_ref.shape[1] - 1):
        total = total + lengths_ref[0, doc]
        bounds.append(total)
    scale = math.log2(math.e) / math.sqrt(HD)
    head_of_row = lax.broadcasted_iota(jnp.int32, (width, tok), 0) // HD
    for block in range(ranks):
        first = max(0, block - reach)
        span = (block - first + 1) * tok
        query = query_ref[block]
        spread = jnp.concatenate(
            [jnp.where(head_of_row == head, query, jnp.zeros_like(query)) for head in range(heads)],
            axis=1,
        )
        position = block * tok + lax.broadcasted_iota(jnp.int32, (1, tok), 1)
        begin = jnp.zeros((1, tok), jnp.int32)
        for bound in bounds:
            begin = jnp.maximum(begin, jnp.where(position >= bound, bound, 0))
        key_position = first * tok + lax.broadcasted_iota(jnp.int32, (span, tok), 0)
        visible = (key_position >= begin) & (key_position <= position)
        scores = dot(keys_ref[first * tok : first * tok + span, :], spread)
        values = jnp.concatenate([values_ref[rank] for rank in range(first, block + 1)], axis=1)
        for head in range(heads):
            part = jnp.where(visible, scores[:, head * tok : (head + 1) * tok], masked_score)
            top = jnp.max(part, axis=0, keepdims=True)
            weights = jnp.exp2((part - top) * scale)
            totals = jnp.sum(weights, axis=0, keepdims=True)
            summed = dot(
                values[head * HD : (head + 1) * HD, :], weights.astype(jnp.bfloat16)
            )
            result_ref[block, head * HD : (head + 1) * HD, :] = (summed / totals).astype(
                jnp.bfloat16
            )
    for k, out_ref in enumerate(out_refs):
        out_ref[...] = result_ref[to_ref[k]]


def mix_kernel(
    ranks, hot_capacity, from_ref, own_ref, choice_ref, residual_ref, proj_ref, *refs
):
    got_refs, mixed_ref, sent_refs, turned_ref = refs[:ranks], refs[ranks], refs[ranks + 1 : -1], refs[-1]
    share = got_refs[0].shape[0]
    for k, got_ref in enumerate(got_refs):
        turned_ref[pl.ds(pl.multiple_of(from_ref[k] * share, share), share), :] = got_ref[...]
    attended = turned_ref[...].T
    mixed = (residual_ref[...].astype(jnp.float32) + dot(attended, proj_ref[...])).astype(
        jnp.bfloat16
    )
    mixed_ref[...] = mixed
    mixed_f = mixed.astype(jnp.float32)
    inv_rms = lax.rsqrt(jnp.mean(mixed_f * mixed_f, axis=1, keepdims=True) + norm_eps)
    normed = (mixed_f * inv_rms).astype(jnp.bfloat16)
    placed = slot_matrix(choice_ref[...], own_ref[0], len(sent_refs), hot_capacity)
    rows = dot(placed, normed).astype(jnp.bfloat16)
    for k, sent_ref in enumerate(sent_refs):
        sent_ref[...] = rows[k * hot_capacity : (k + 1) * hot_capacity]


def expert_kernel(
    reps, sources, parts, strip, own_ref, part_ref, up_ref, down_ref, router_ref, *refs
):
    per_rep = (len(refs) - 2 - sources - parts) // (2 * reps)
    row_refs = [refs[rep * per_rep : (rep + 1) * per_rep] for rep in range(reps)]
    refs = refs[reps * per_rep :]
    grad_refs = [refs[rep * per_rep : (rep + 1) * per_rep] for rep in range(reps)]
    refs = refs[reps * per_rep :]
    back_refs, term_refs, (kept_ref, up_acc, down_acc) = refs[:sources], refs[sources:-3], refs[-3:]
    capacity = back_refs[0].shape[0] // 2
    count = sources * capacity
    up = up_ref[...]
    down = down_ref[...]
    router = router_ref[...]
    expert_lane = lax.broadcasted_iota(jnp.int32, (count, router.shape[0]), 1) == own_ref[0]
    for rep in range(reps):
        rows = rows_of(row_refs[rep])
        pre = dot(rows, up)
        sigmoid_pre = jax.nn.sigmoid(pre)
        activated = (pre * sigmoid_pre).astype(jnp.bfloat16)
        logits = dot(rows, router, NT)
        gate = jax.nn.sigmoid(
            jnp.sum(jnp.where(expert_lane, logits, 0.0), axis=1, keepdims=True)
        )
        scaled = (gate * rows_of(grad_refs[rep]).astype(jnp.float32)).astype(jnp.bfloat16)
        act_grad = dot(scaled, down, NT)
        pre_grad = (act_grad * sigmoid_pre * (1.0 + pre * (1.0 - sigmoid_pre))).astype(
            jnp.bfloat16
        )
        up_term = dot(rows, pre_grad, TN)
        down_term = dot(activated, scaled, TN)
        if rep == 0:
            up_acc[...] = up_term
            down_acc[...] = down_term
            produced = dot(activated, down).astype(jnp.bfloat16)
            token_grad = dot(pre_grad, up, NT).astype(jnp.bfloat16)
            for k, back_ref in enumerate(back_refs):
                back_ref[0:capacity] = produced[k * capacity : (k + 1) * capacity]
                back_ref[capacity : 2 * capacity] = token_grad[k * capacity : (k + 1) * capacity]
        else:
            up_acc[...] += up_term
            down_acc[...] += down_term
    for k in range(parts):
        first = pl.multiple_of(part_ref[k] * strip, strip)
        up_part = up_acc[pl.ds(first, strip), :]
        down_part = down_acc[pl.ds(first, strip), :]
        if k == 0:
            kept_ref[0] = up_part
            kept_ref[1] = down_part
        else:
            term_refs[k - 1][0] = up_part.astype(jnp.bfloat16)
            term_refs[k - 1][1] = down_part.astype(jnp.bfloat16)


def finish_kernel(
    hot_capacity, own_ref, choice_ref, router_ref, mixed_ref, grad_ref, *refs
):
    back_refs, (layer_ref, grad_mixed_ref) = refs[:-2], refs[-2:]
    expert_count = router_ref.shape[0]
    tok = mixed_ref.shape[0]
    choice = choice_ref[...]
    placed = slot_matrix(choice, own_ref[0], expert_count, hot_capacity)
    router = router_ref[...]
    mixed_f = mixed_ref[...].astype(jnp.float32)
    inv_rms = lax.rsqrt(jnp.mean(mixed_f * mixed_f, axis=1, keepdims=True) + norm_eps)
    normed = (mixed_f * inv_rms).astype(jnp.bfloat16)
    one_hot = lax.broadcasted_iota(jnp.int32, (expert_count, tok), 0) == choice
    logits = dot(router, normed, NT)
    logit_row = jnp.sum(jnp.where(one_hot, logits, 0.0), axis=0, keepdims=True)
    logit = jnp.broadcast_to(logit_row, (8, tok)).T[:, 0:1]
    gate = jax.nn.sigmoid(logit)
    pair = 2 * hot_capacity
    chunks = [
        ref[first : first + pair] for ref in back_refs for first in range(0, ref.shape[0], pair)
    ]
    results = jnp.concatenate([chunk[:hot_capacity] for chunk in chunks], axis=0)
    grads = jnp.concatenate([chunk[hot_capacity:] for chunk in chunks], axis=0)
    result_f = dot(placed, results, TN)
    normed_grad = dot(placed, grads, TN)
    grad_f = grad_ref[...].astype(jnp.float32)
    layer_ref[...] = (mixed_f + gate * result_f).astype(jnp.bfloat16)
    gate_grad = jnp.sum(grad_f * result_f, axis=1, keepdims=True)
    logit_grad = gate_grad * gate * (1.0 - gate)
    router_cols = dot(one_hot.astype(jnp.float32).astype(jnp.bfloat16), router, TN)
    total_grad = normed_grad + logit_grad * router_cols
    mean_term = jnp.mean(total_grad * mixed_f, axis=1, keepdims=True)
    input_grad = inv_rms * total_grad - mixed_f * inv_rms * inv_rms * inv_rms * mean_term
    grad_mixed_ref[...] = (grad_f + input_grad).astype(jnp.bfloat16)


def sum_kernel(kept_ref, *refs):
    term_refs, (up_ref, down_ref) = refs[:-2], refs[-2:]
    for kind, out_ref in enumerate((up_ref, down_ref)):
        total = kept_ref[kind]
        for ref in term_refs:
            total = total + ref[kind].astype(jnp.float32)
        out_ref[...] = total


def shape(dims, dtype=jnp.bfloat16):
    return jax.ShapeDtypeStruct(dims, dtype)


SMEM = pl.BlockSpec(memory_space=pltpu.SMEM)
VMEM = pl.BlockSpec(memory_space=pltpu.VMEM)
HBM = pl.BlockSpec(memory_space=pltpu.HBM)


def call(body, out_shape, specs, scratch=()):
    return pl.pallas_call(
        body,
        out_shape=out_shape,
        in_specs=specs,
        out_specs=jax.tree.map(lambda unused: VMEM, out_shape),
        scratch_shapes=list(scratch),
        compiler_params=pltpu.CompilerParams(vmem_limit_bytes=VMEM_LIMIT),
    )


def local(
    seq_count,
    expert_count,
    rep_count,
    query_rows,
    key_rows,
    value_rows,
    doc_lengths,
    residual,
    out_proj,
    router,
    expert_choice,
    weight_in,
    weight_out,
    grad_out,
):
    tok, width = query_rows.shape[1:]
    hidden = weight_in.shape[2]
    positions = Group(("seq", "rep"), (seq_count, rep_count))
    owners = Group(("expert", "rep"), (expert_count, rep_count))
    experts = Group(("expert",), (expert_count,))
    parts = Group(("seq",), (seq_count,))
    ranks = positions.count
    share = width // ranks
    strip = width // ranks
    capacity = max(2, (3 * tok + 2 * expert_count - 1) // (2 * expert_count))
    hot_capacity = min(4 * capacity, tok // 2)
    choice = expert_choice.reshape(1, tok)
    router_rows = router.T
    seq_index = lax.axis_index("seq")
    rep_index = lax.axis_index("rep")
    rank = seq_index * rep_count + rep_index
    own = jnp.stack([lax.axis_index("expert")]).astype(jnp.int32)
    rank_to = jnp.stack([positions.target(rank, k) for k in range(ranks)]).astype(jnp.int32)
    rank_from = jnp.stack([positions.source(rank, k) for k in range(ranks)]).astype(jnp.int32)
    part_to = jnp.stack(
        [parts.target(seq_index, k) * rep_count + rep_index for k in range(seq_count)]
    ).astype(jnp.int32)

    packed = call(
        functools.partial(pack_kernel, share),
        [shape((3 * share, tok))] * ranks,
        [SMEM, HBM, HBM, HBM],
        [
            pltpu.VMEM((3, tok, width), jnp.bfloat16),
            pltpu.VMEM((3, width, tok), jnp.bfloat16),
            pltpu.SemaphoreType.DMA((3,)),
        ],
    )(rank_to, query_rows[0], key_rows[0], value_rows[0])
    got = positions.exchange(packed)

    def to_owners(chunks):
        arrived = owners.exchange([chunks[k // rep_count] for k in range(owners.count)])
        spread = []
        for rep in range(rep_count):
            spread += merged(arrived[rep::rep_count], MOST_PERMUTES)
        return spread

    sent_grads = call(
        functools.partial(grad_dispatch_kernel, hot_capacity),
        [shape((hot_capacity, width))] * expert_count,
        [SMEM, VMEM, VMEM],
    )(own, choice, grad_out[0])
    got_grads = to_owners(sent_grads)
    attended = call(
        functools.partial(attend_kernel, ranks),
        [shape((share, tok))] * ranks,
        [SMEM, SMEM, SMEM] + [VMEM] * ranks,
        [
            pltpu.VMEM((ranks, share, tok), jnp.bfloat16),
            pltpu.VMEM((ranks * tok, share), jnp.bfloat16),
            pltpu.VMEM((ranks, share, tok), jnp.bfloat16),
            pltpu.VMEM((ranks, share, tok), jnp.bfloat16),
        ],
    )(rank_to, rank_from, doc_lengths, *got)
    turned = positions.exchange(attended)
    mixed, *sent_rows = call(
        functools.partial(mix_kernel, ranks, hot_capacity),
        [shape((tok, width))] + [shape((hot_capacity, width))] * expert_count,
        [SMEM, SMEM] + [VMEM] * (3 + ranks),
        [pltpu.VMEM((width, tok), jnp.bfloat16)],
    )(rank_from, own, choice, residual[0], out_proj, *turned)
    got_rows = to_owners(sent_rows)
    outs = call(
        functools.partial(expert_kernel, rep_count, expert_count, seq_count, strip),
        [shape((2 * hot_capacity, width))] * expert_count
        + [shape((2, strip, hidden))] * (seq_count - 1)
        + [shape((2, strip, hidden), jnp.float32)],
        [SMEM, SMEM] + [VMEM] * (3 + len(got_rows) + len(got_grads)),
        [pltpu.VMEM((width, hidden), jnp.float32), pltpu.VMEM((hidden, width), jnp.float32)],
    )(own, part_to, weight_in[0], weight_out[0], router_rows, *got_rows, *got_grads)
    back, terms, kept = outs[:expert_count], outs[expert_count:-1], outs[-1]
    got_terms = parts.exchange([None] + list(terms))[1:]
    got_back = merged(experts.exchange(back, inverse=True), MOST_PERMUTES)
    layer_out, grad_mixed = call(
        functools.partial(finish_kernel, hot_capacity),
        [shape((tok, width)), shape((tok, width))],
        [SMEM] + [VMEM] * (4 + len(got_back)),
    )(own, choice, router_rows, mixed, grad_out[0], *got_back)
    share_in, share_out = call(
        sum_kernel,
        [shape((strip, hidden), jnp.float32), shape((strip, width), jnp.float32)],
        [VMEM] * seq_count,
    )(kept, *got_terms)
    return (layer_out[None], grad_mixed[None], share_in[None], share_out[None])


def solution(mesh):
    rows = P("expert", ("seq", "rep"), None)
    in_specs = (
        rows,
        rows,
        rows,
        P("expert", None),
        rows,
        P(),
        P(),
        rows,
        P("expert", None, None),
        P("expert", None, None),
        rows,
    )
    body = functools.partial(
        local, mesh.shape["seq"], mesh.shape["expert"], mesh.shape["rep"]
    )
    return jax.shard_map(
        body, mesh=mesh, in_specs=in_specs, out_specs=(rows, rows, rows, rows), check_vma=False
    )
```

time: 97.6 us -> 91.2 us (0.934)
  starting transfers between devices: 14.2 us -> 44.7 us
  blocking collectives: 30.5 us -> 0 us
  waiting for transfers between devices: 34.5 us -> 27.4 us
  local copies, waits for them, and re-layouts: 4.05 us -> 6.19 us
  Pallas kernels: 12.9 us -> 11.7 us
    ppermute x0 -> x34, starting transfers between devices: none -> 44.7 us  [exchange(): got[k] = lax.ppermute(chunks[k], self.axes, pairs)]
    all_to_all x4 -> x0, waiting for transfers between devices: 34.5 us -> none  [the longest x1 13 us: local(): lax.all_to_all(terms, 'seq', split_axis=0, concat_axis=0, tiled=True)]
    all_to_all x2 -> x0, blocking collectives: 30.5 us -> none  [the longest x1 19.1 us: local(): lax.all_to_all(packed, ('seq', 'rep'), split_axis=0, concat_axis=0, tiled...]
    ppermute x0 -> x34, waiting for transfers between devices: none -> 27.4 us  [exchange(): got[k] = lax.ppermute(chunks[k], self.axes, pairs)]
    all_to_all x4 -> x0, starting transfers between devices: 14.2 us -> none  [the longest x1 3.62 us: local(): lax.all_to_all(sent_grads.reshape(rep_count * expert_count, hot_capacity,...]
    unnamed x22 -> x26, local copies, waits for them, and re-layouts: 4.05 us -> 6.1 us
    pallas_call x7, Pallas kernels: 12.9 us -> 11.7 us  [the longest x1 3.71 us: local(): call(functools.partial(attend_kernel, ranks), [shape((share, tok))] * ran...]
  transfers between devices with their start and end apart: 4 -> 34, of which waited for: 4 -> 11; matrix products, arithmetic and copies ran while one was open for 0% -> 0% of each run, Pallas kernels for 4% -> 2%
where the time goes in v2:
time: 91.2 us; the launch traced here: 90.9 us
  starting transfers between devices  44.7 us (49%)
  waiting for transfers between devices  27.4 us (30%)
  Pallas kernels  11.7 us (13%)
  local copies, waits for them, and re-layouts  6.19 us (7%)
    ppermute x34, starting transfers between devices, exchange(): got[k] = lax.ppermute(chunks[k], self.axes, pairs)  44.7 us
    ppermute x34, waiting for transfers between devices, exchange(): got[k] = lax.ppermute(chunks[k], self.axes, pairs)  27.4 us
    unnamed x26, local copies, waits for them, and re-layouts  6.1 us
    pallas_call x1, Pallas kernels, local(): call(functools.partial(attend_kernel, ranks), [shape((share, tok))] * ran...  3.71 us
    pallas_call x1, Pallas kernels, local(): call(functools.partial(expert_kernel, rep_count, expert_count, seq_count,...  3.04 us
  transfers between devices with their start and end apart: 34, of which 11 were waited for; matrix products, arithmetic and copies ran while one was open for 0% of the time, Pallas kernels for 2%

profile of v2, /device:TPU:0, one launch (start us, length us, event | category | flops | bytes accessed | tf_op | source)
XLA Modules:
  0.0 90.9 jit_solution(9399753478522430190)
XLA Ops:
  3.3 1.4 %shard_map.138 = (bf16[192,128]{1,0:T(8,128)(2,1)S(1)}, bf16[192,128]{1,0:T(8,128)(2,1)S(1)}, bf16[192,128]{1,0:T(8,128)(2,1)S(1)}, bf16[192,128]{1,0:T(8,128)(2...) custom-call(s32[8]{0:T(128)S(1)} %stack.63.to_ref.from_ref, ...), custom_call_target="tpu_custom_call" | custom-call | tf_op jit(solution)/shard_map/pallas_call | solution.py:362
  4.7 3.0 %collective-permute-start = (bf16[192,128]{1,0:T(8,128)(2,1)S(1)}, bf16[192,128]{1,0:T(8,128)(2,1)S(1)}, u32[]{:S(2)}, u32[]{:S(2)}) collective-permute-start(bf16[192,128]{1,0:T(8,128)(2,1)S(1)} %get-tuple-element.42), channel_id=1, source_target_pairs={{0,1},{1,0},{8,9},{9,8},{16,17},{17,16},{24,25},{25,24},{2,3},{3,2... | collective-permute-start | bytes 147464 | tf_op jit(solution)/shard_map/ppermute | solution.py:69
  7.7 1.6 %collective-permute-start.1 = (bf16[192,128]{1,0:T(8,128)(2,1)S(1)}, bf16[192,128]{1,0:T(8,128)(2,1)S(1)}, u32[]{:S(2)}, u32[]{:S(2)}) collective-permute-start(bf16[192,128]{1,0:T(8,128)(2,1)S(1)} %get-tuple-element.43), channel_id=1, source_target_pairs={{0,8},{1,9},{8,0},{9,1},{16,24},{17,25},{24,16},{25,17},{2,10},{3,... | collective-permute-start | bytes 147464 | tf_op jit(solution)/shard_map/ppermute | solution.py:69
  9.3 3.0 %collective-permute-start.3 = (bf16[192,128]{1,0:T(8,128)(2,1)S(1)}, bf16[192,128]{1,0:T(8,128)(2,1)S(1)}, u32[]{:S(2)}, u32[]{:S(2)}) collective-permute-start(bf16[192,128]{1,0:T(8,128)(2,1)S(1)} %get-tuple-element.45), channel_id=1, source_target_pairs={{0,16},{1,17},{8,24},{9,25},{16,0},{17,1},{24,8},{25,9},{2,18},{3,... | collective-permute-start | bytes 147464 | tf_op jit(solution)/shard_map/ppermute | solution.py:69
  12.3 1.3 %collective-permute-start.4 = (bf16[192,128]{1,0:T(8,128)(2,1)S(1)}, bf16[192,128]{1,0:T(8,128)(2,1)S(1)}, u32[]{:S(2)}, u32[]{:S(2)}) collective-permute-start(bf16[192,128]{1,0:T(8,128)(2,1)S(1)} %get-tuple-element.46), channel_id=1, source_target_pairs={{0,17},{1,16},{8,25},{9,24},{16,1},{17,0},{24,9},{25,8},{2,19},{3,... | collective-permute-start | bytes 147464 | tf_op jit(solution)/shard_map/ppermute | solution.py:69
  13.6 3.6 %collective-permute-start.5 = (bf16[192,128]{1,0:T(8,128)(2,1)S(1)}, bf16[192,128]{1,0:T(8,128)(2,1)S(1)}, u32[]{:S(2)}, u32[]{:S(2)}) collective-permute-start(bf16[192,128]{1,0:T(8,128)(2,1)S(1)} %get-tuple-element.47), channel_id=1, source_target_pairs={{0,24},{1,25},{8,16},{9,17},{16,8},{17,9},{24,0},{25,1},{2,26},{3,... | collective-permute-start | bytes 147464 | tf_op jit(solution)/shard_map/ppermute | solution.py:69
  17.2 2.9 %collective-permute-done.4.refs_5_ = bf16[192,128]{1,0:T(8,128)(2,1)S(1)} collective-permute-done((bf16[192,128]{1,0:T(8,128)(2,1)S(1)}, bf16[192,128]{1,0:T(8,128)(2,1)S(1)}, u32[]{:S(2)}, u32[]{:S(2)}) %collective-permute-start.4) | collective-permute-done | bytes 49184 | tf_op jit(solution)/shard_map/ppermute | solution.py:69
  20.2 3.8 %collective-permute-done.6.refs_7_ = bf16[192,128]{1,0:T(8,128)(2,1)S(1)} collective-permute-done((bf16[192,128]{1,0:T(8,128)(2,1)S(1)}, bf16[192,128]{1,0:T(8,128)(2,1)S(1)}, u32[]{:S(2)}, u32[]{:S(2)}) %collective-permute-start.6) | collective-permute-done | bytes 49184 | tf_op jit(solution)/shard_map/ppermute | solution.py:69
  24.6 3.7 %shard_map.139 = (bf16[64,128]{1,0:T(8,128)(2,1)S(1)}, bf16[64,128]{1,0:T(8,128)(2,1)S(1)}, bf16[64,128]{1,0:T(8,128)(2,1)S(1)}, bf16[64,128]{1,0:T(8,128)(2,1)S...) custom-call(s32[8]{0:T(128)S(1)} %stack.63.to_ref.from_ref, ...), custom_call_target="tpu_custom_call" | custom-call | tf_op jit(solution)/shard_map/pallas_call | solution.py:387
  29.0 3.0 %collective-permute-start.9 = (bf16[64,128]{1,0:T(8,128)(2,1)S(1)}, bf16[64,128]{1,0:T(8,128)(2,1)S(1)}, u32[]{:S(2)}, u32[]{:S(2)}) collective-permute-start(bf16[64,128]{1,0:T(8,128)(2,1)S(1)} %get-tuple-element.52), channel_id=1, source_target_pairs={{0,9},{1,8},{8,1},{9,0},{16,25},{17,24},{24,17},{25,16},{2,11},{3,... | collective-permute-start | bytes 49160 | tf_op jit(solution)/shard_map/ppermute | solution.py:69
  33.7 1.6 %collective-permute-start.21 = (bf16[64,512]{1,0:T(8,128)(2,1)S(1)}, bf16[64,512]{1,0:T(8,128)(2,1)S(1)}, u32[]{:S(2)}, u32[]{:S(2)}) collective-permute-start(bf16[64,512]{1,0:T(8,128)(2,1)S(1)} %get-tuple-element.63), channel_id=1, source_target_pairs={{0,2},{1,3},{2,0},{3,1},{4,6},{5,7},{6,4},{7,5},{8,10},{9,11},{10,... | collective-permute-start | bytes 196616 | tf_op jit(solution)/shard_map/ppermute | solution.py:69
  35.3 1.5 %collective-permute-start.26 = (bf16[64,512]{1,0:T(8,128)(2,1)S(1)}, bf16[64,512]{1,0:T(8,128)(2,1)S(1)}, u32[]{:S(2)}, u32[]{:S(2)}) collective-permute-start(bf16[64,512]{1,0:T(8,128)(2,1)S(1)} %get-tuple-element.64), channel_id=1, source_target_pairs={{0,5},{1,4},{2,7},{3,6},{4,1},{5,0},{6,3},{7,2},{8,13},{9,12},{10,... | collective-permute-start | bytes 196616 | tf_op jit(solution)/shard_map/ppermute | solution.py:69
  36.8 3.7 %collective-permute-start.11 = (bf16[64,128]{1,0:T(8,128)(2,1)S(1)}, bf16[64,128]{1,0:T(8,128)(2,1)S(1)}, u32[]{:S(2)}, u32[]{:S(2)}) collective-permute-start(bf16[64,128]{1,0:T(8,128)(2,1)S(1)} %get-tuple-element.54), channel_id=1, source_target_pairs={{0,17},{1,16},{8,25},{9,24},{16,1},{17,0},{24,9},{25,8},{2,19},{3,... | collective-permute-start | bytes 49160 | tf_op jit(solution)/shard_map/ppermute | solution.py:69
  40.5 1.9 %collective-permute-done.11.refs_5_ = bf16[64,128]{1,0:T(8,128)(2,1)S(1)} collective-permute-done((bf16[64,128]{1,0:T(8,128)(2,1)S(1)}, bf16[64,128]{1,0:T(8,128)(2,1)S(1)}, u32[]{:S(2)}, u32[]{:S(2)}) %collective-permute-start.11) | collective-permute-done | bytes 16416 | tf_op jit(solution)/shard_map/ppermute | solution.py:69
  42.4 2.2 %collective-permute-start.12 = (bf16[64,128]{1,0:T(8,128)(2,1)S(1)}, bf16[64,128]{1,0:T(8,128)(2,1)S(1)}, u32[]{:S(2)}, u32[]{:S(2)}) collective-permute-start(bf16[64,128]{1,0:T(8,128)(2,1)S(1)} %get-tuple-element.55), channel_id=1, source_target_pairs={{0,24},{1,25},{8,16},{9,17},{16,8},{17,9},{24,0},{25,1},{2,26},{3,... | collective-permute-start | bytes 49160 | tf_op jit(solution)/shard_map/ppermute | solution.py:69
  44.6 3.3 %collective-permute-done.12.refs_6_ = bf16[64,128]{1,0:T(8,128)(2,1)S(1)} collective-permute-done((bf16[64,128]{1,0:T(8,128)(2,1)S(1)}, bf16[64,128]{1,0:T(8,128)(2,1)S(1)}, u32[]{:S(2)}, u32[]{:S(2)}) %collective-permute-start.12) | collective-permute-done | bytes 16416 | tf_op jit(solution)/shard_map/ppermute | solution.py:69
  47.9 3.2 %collective-permute-start.13 = (bf16[64,128]{1,0:T(8,128)(2,1)S(1)}, bf16[64,128]{1,0:T(8,128)(2,1)S(1)}, u32[]{:S(2)}, u32[]{:S(2)}) collective-permute-start(bf16[64,128]{1,0:T(8,128)(2,1)S(1)} %get-tuple-element.56), channel_id=1, source_target_pairs={{0,25},{1,24},{8,17},{9,16},{16,9},{17,8},{24,1},{25,0},{2,27},{3,... | collective-permute-start | bytes 49160 | tf_op jit(solution)/shard_map/ppermute | solution.py:69
  51.1 3.3 %collective-permute-done.13.refs_7_ = bf16[64,128]{1,0:T(8,128)(2,1)S(1)} collective-permute-done((bf16[64,128]{1,0:T(8,128)(2,1)S(1)}, bf16[64,128]{1,0:T(8,128)(2,1)S(1)}, u32[]{:S(2)}, u32[]{:S(2)}) %collective-permute-start.13) | collective-permute-done | bytes 16416 | tf_op jit(solution)/shard_map/ppermute | solution.py:69
  54.4 1.4 %collective-permute-start.22 = (bf16[64,512]{1,0:T(8,128)(2,1)S(1)}, bf16[64,512]{1,0:T(8,128)(2,1)S(1)}, u32[]{:S(2)}, u32[]{:S(2)}) collective-permute-start(bf16[64,512]{1,0:T(8,128)(2,1)S(1)} %get-tuple-element.64), channel_id=1, source_target_pairs={{0,4},{1,5},{2,6},{3,7},{4,0},{5,1},{6,2},{7,3},{8,12},{9,13},{10,... | collective-permute-start | bytes 196616 | tf_op jit(solution)/shard_map/ppermute | solution.py:69
  57.3 1.1 %shard_map.140 = (bf16[128,512]{1,0:T(8,128)(2,1)S(1)}, bf16[64,512]{1,0:T(8,128)(2,1)S(1)}, bf16[64,512]{1,0:T(8,128)(2,1)S(1)}, bf16[64,512]{1,0:T(8,128)(2,1)S(1)}, bf16[64,512]{1,0:T(8,128)(2,1)S(1)}) custom-call(s32[8]{0:T(128)S(1)} %stack.63.to_ref.from_ref, s32[1]{0:T(128)} %bitcast.own_ref, s32[1,128]{1,0:T(1,128)S(1)} %bitcast.37, ...), custom_call_target="tpu_custom_call" | custom-call | tf_op jit(solution)/shard_map/pallas_call | solution.py:399
  58.5 1.8 %collective-permute-start.23 = (bf16[64,512]{1,0:T(8,128)(2,1)S(1)}, bf16[64,512]{1,0:T(8,128)(2,1)S(1)}, u32[]{:S(2)}, u32[]{:S(2)}) collective-permute-start(bf16[64,512]{1,0:T(8,128)(2,1)S(1)} %get-tuple-element.65), channel_id=1, source_target_pairs={{0,6},{1,7},{2,4},{3,5},{4,2},{5,3},{6,0},{7,1},{8,14},{9,15},{10,... | collective-permute-start | bytes 196616 | tf_op jit(solution)/shard_map/ppermute | solution.py:69
  60.3 1.4 %collective-permute-start.17 = (bf16[64,512]{1,0:T(8,128)(2,1)S(1)}, bf16[64,512]{1,0:T(8,128)(2,1)S(1)}, u32[]{:S(2)}, u32[]{:S(2)}) collective-permute-start(bf16[64,512]{1,0:T(8,128)(2,1)S(1)} %get-tuple-element.58.refs_0_), channel_id=1, source_target_pairs={{0,1},{1,0},{2,3},{3,2},{4,5},{5,4},{6,7},{7,6},{8,9},{9,8},{10,11... | collective-permute-start | bytes 196616 | tf_op jit(solution)/shard_map/ppermute | solution.py:69
  63.1 1.6 %collective-permute-start.19 = (bf16[64,512]{1,0:T(8,128)(2,1)S(1)}, bf16[64,512]{1,0:T(8,128)(2,1)S(1)}, u32[]{:S(2)}, u32[]{:S(2)}) collective-permute-start(bf16[64,512]{1,0:T(8,128)(2,1)S(1)} %get-tuple-element.60), channel_id=1, source_target_pairs={{0,5},{1,4},{2,7},{3,6},{4,1},{5,0},{6,3},{7,2},{8,13},{9,12},{10,... | collective-permute-start | bytes 196616 | tf_op jit(solution)/shard_map/ppermute | solution.py:69
  66.0 1.8 %collective-permute-start.16 = (bf16[64,512]{1,0:T(8,128)(2,1)S(1)}, bf16[64,512]{1,0:T(8,128)(2,1)S(1)}, u32[]{:S(2)}, u32[]{:S(2)}) collective-permute-start(bf16[64,512]{1,0:T(8,128)(2,1)S(1)} %get-tuple-element.61), channel_id=1, source_target_pairs={{0,6},{1,7},{2,4},{3,5},{4,2},{5,3},{6,0},{7,1},{8,14},{9,15},{10,... | collective-permute-start | bytes 196616 | tf_op jit(solution)/shard_map/ppermute | solution.py:69
  68.4 2.8 %collective-permute-done.15.refs_2_ = bf16[64,512]{1,0:T(8,128)(2,1)S(1)} collective-permute-done((bf16[64,512]{1,0:T(8,128)(2,1)S(1)}, bf16[64,512]{1,0:T(8,128)(2,1)S(1)}, u32[]{:S(2)}, u32[]{:S(2)}) %collective-permute-start.15) | collective-permute-done | bytes 65568 | tf_op jit(solution)/shard_map/ppermute | solution.py:69
  71.9 3.0 %shard_map.142 = (bf16[128,512]{1,0:T(8,128)(2,1)S(1)}, bf16[128,512]{1,0:T(8,128)(2,1)S(1)}, bf16[128,512]{1,0:T(8,128)(2,1)S(1)}, bf16[128,512]{1,0:T(8,128)(2...) custom-call(s32[1]{0:T(128)} %bitcast.own_ref, ...), custom_call_target="tpu_custom_call" | custom-call | tf_op jit(solution)/shard_map/pallas_call | solution.py:406
  75.3 2.7 %collective-permute-start.32 = (bf16[2,64,512]{2,1,0:T(8,128)(2,1)S(1)}, bf16[2,64,512]{2,1,0:T(8,128)(2,1)S(1)}, u32[]{:S(2)}, u32[]{:S(2)}) collective-permute-start(bf16[2,64,512]{2,1,0:T(8,128)(2,1)S(1)} %get-tuple-element.74), channel_id=1, source_target_pairs={{0,16},{8,24},{16,0},{24,8},{1,17},{9,25},{17,1},{25,9},{2,18},{10... | collective-permute-start | bytes 393224 | tf_op jit(solution)/shard_map/ppermute | solution.py:69
  78.0 1.4 %collective-permute-start.33 = (bf16[2,64,512]{2,1,0:T(8,128)(2,1)S(1)}, bf16[2,64,512]{2,1,0:T(8,128)(2,1)S(1)}, u32[]{:S(2)}, u32[]{:S(2)}) collective-permute-start(bf16[2,64,512]{2,1,0:T(8,128)(2,1)S(1)} %get-tuple-element.75), channel_id=1, source_target_pairs={{0,24},{8,16},{16,8},{24,0},{1,25},{9,17},{17,9},{25,1},{2,26},{10... | collective-permute-start | bytes 393224 | tf_op jit(solution)/shard_map/ppermute | solution.py:69
  79.4 1.2 %collective-permute-start.29 = (bf16[128,512]{1,0:T(8,128)(2,1)S(1)}, bf16[128,512]{1,0:T(8,128)(2,1)S(1)}, u32[]{:S(2)}, u32[]{:S(2)}) collective-permute-start(bf16[128,512]{1,0:T(8,128)(2,1)S(1)} %get-tuple-element.68), channel_id=1, source_target_pairs={{0,4},{2,6},{4,0},{6,2},{1,5},{3,7},{5,1},{7,3},{8,12},{10,14},{12... | collective-permute-start | bytes 393224 | tf_op jit(solution)/shard_map/ppermute | solution.py:69
  80.6 1.9 %collective-permute-done.31.refs_0_ = bf16[2,64,512]{2,1,0:T(8,128)(2,1)S(1)} collective-permute-done((bf16[2,64,512]{2,1,0:T(8,128)(2,1)S(1)}, bf16[2,64,512]{2,1,0:T(8,128)(2,1)S(1)}, u32[]{:S(2)}, u32[]{:S(2)}) %collective-permute-start.31) | collective-permute-done | bytes 131104 | tf_op jit(solution)/shard_map/ppermute | solution.py:69
  82.5 5.6 %collective-permute-done.32.refs_1_ = bf16[2,64,512]{2,1,0:T(8,128)(2,1)S(1)} collective-permute-done((bf16[2,64,512]{2,1,0:T(8,128)(2,1)S(1)}, bf16[2,64,512]{2,1,0:T(8,128)(2,1)S(1)}, u32[]{:S(2)}, u32[]{:S(2)}) %collective-permute-start.32) | collective-permute-done | bytes 131104 | tf_op jit(solution)/shard_map/ppermute | solution.py:69
  89.5 1.4 %shard_map.143 = (bf16[128,512]{1,0:T(8,128)(2,1)}, bf16[128,512]{1,0:T(8,128)(2,1)}) custom-call(s32[1]{0:T(128)} %bitcast.own_ref, s32[1,128]{1,0:T(1,128)S(1)} %bitcast.38, bf16[4,512]{1,0:T(4,128)(2,1)S(1)} %bitcast.35, bf16[128,512]{1,0:T(8,128)(2,1)S(1)} %get-tuple-element.57.mixed_ref, bf16[128,512]{1,0:T(8,128)(2,1)S(1)} %bitcast.27, ...), custom_call_target="tpu_custom_call" | custom-call | tf_op jit(solution)/shard_map/pallas_call | solution.py:417
  (71 shorter events, 13.1 us)
Async XLA Ops:
  4.7 8.9 %collective-permute-start = (bf16[192,128]{1,0:T(8,128)(2,1)S(1)}, bf16[192,128]{1,0:T(8,128)(2,1)S(1)}, u32[]{:S(2)}, u32[]{:S(2)}) collective-permute-start(bf16[192,128]{1,0:T(8,128)(2,1)S(1)} %get-tuple-element.42), channel_id=1, source_target_pairs={{0,1},{1,0},{8,9},{9,8},{16,17},{17,16},{24,25},{25,24},{2,3},{3,2... | collective-permute-start | bytes 147464 | tf_op jit(solution)/shard_map/ppermute | solution.py:69
  7.7 9.5 %collective-permute-start.1 = (bf16[192,128]{1,0:T(8,128)(2,1)S(1)}, bf16[192,128]{1,0:T(8,128)(2,1)S(1)}, u32[]{:S(2)}, u32[]{:S(2)}) collective-permute-start(bf16[192,128]{1,0:T(8,128)(2,1)S(1)} %get-tuple-element.43), channel_id=1, source_target_pairs={{0,8},{1,9},{8,0},{9,1},{16,24},{17,25},{24,16},{25,17},{2,10},{3,... | collective-permute-start | bytes 147464 | tf_op jit(solution)/shard_map/ppermute | solution.py:69
  9.3 7.9 %collective-permute-start.2 = (bf16[192,128]{1,0:T(8,128)(2,1)S(1)}, bf16[192,128]{1,0:T(8,128)(2,1)S(1)}, u32[]{:S(2)}, u32[]{:S(2)}) collective-permute-start(bf16[192,128]{1,0:T(8,128)(2,1)S(1)} %get-tuple-element.44), channel_id=1, source_target_pairs={{0,9},{1,8},{8,1},{9,0},{16,25},{17,24},{24,17},{25,16},{2,11},{3,... | collective-permute-start | bytes 147464 | tf_op jit(solution)/shard_map/ppermute | solution.py:69
  9.3 7.9 %collective-permute-start.3 = (bf16[192,128]{1,0:T(8,128)(2,1)S(1)}, bf16[192,128]{1,0:T(8,128)(2,1)S(1)}, u32[]{:S(2)}, u32[]{:S(2)}) collective-permute-start(bf16[192,128]{1,0:T(8,128)(2,1)S(1)} %get-tuple-element.45), channel_id=1, source_target_pairs={{0,16},{1,17},{8,24},{9,25},{16,0},{17,1},{24,8},{25,9},{2,18},{3,... | collective-permute-start | bytes 147464 | tf_op jit(solution)/shard_map/ppermute | solution.py:69
  12.3 7.9 %collective-permute-start.4 = (bf16[192,128]{1,0:T(8,128)(2,1)S(1)}, bf16[192,128]{1,0:T(8,128)(2,1)S(1)}, u32[]{:S(2)}, u32[]{:S(2)}) collective-permute-start(bf16[192,128]{1,0:T(8,128)(2,1)S(1)} %get-tuple-element.46), channel_id=1, source_target_pairs={{0,17},{1,16},{8,25},{9,24},{16,1},{17,0},{24,9},{25,8},{2,19},{3,... | collective-permute-start | bytes 147464 | tf_op jit(solution)/shard_map/ppermute | solution.py:69
  13.6 6.6 %collective-permute-start.5 = (bf16[192,128]{1,0:T(8,128)(2,1)S(1)}, bf16[192,128]{1,0:T(8,128)(2,1)S(1)}, u32[]{:S(2)}, u32[]{:S(2)}) collective-permute-start(bf16[192,128]{1,0:T(8,128)(2,1)S(1)} %get-tuple-element.47), channel_id=1, source_target_pairs={{0,24},{1,25},{8,16},{9,17},{16,8},{17,9},{24,0},{25,1},{2,26},{3,... | collective-permute-start | bytes 147464 | tf_op jit(solution)/shard_map/ppermute | solution.py:69
  17.2 6.8 %collective-permute-start.6 = (bf16[192,128]{1,0:T(8,128)(2,1)S(1)}, bf16[192,128]{1,0:T(8,128)(2,1)S(1)}, u32[]{:S(2)}, u32[]{:S(2)}) collective-permute-start(bf16[192,128]{1,0:T(8,128)(2,1)S(1)} %get-tuple-element.48), channel_id=1, source_target_pairs={{0,25},{1,24},{8,17},{9,16},{16,9},{17,8},{24,1},{25,0},{2,27},{3,... | collective-permute-start | bytes 147464 | tf_op jit(solution)/shard_map/ppermute | solution.py:69
  28.4 5.4 %collective-permute-start.7 = (bf16[64,128]{1,0:T(8,128)(2,1)S(1)}, bf16[64,128]{1,0:T(8,128)(2,1)S(1)}, u32[]{:S(2)}, u32[]{:S(2)}) collective-permute-start(bf16[64,128]{1,0:T(8,128)(2,1)S(1)} %get-tuple-element.50), channel_id=1, source_target_pairs={{0,1},{1,0},{8,9},{9,8},{16,17},{17,16},{24,25},{25,24},{2,3},{3,2... | collective-permute-start | bytes 49160 | tf_op jit(solution)/shard_map/ppermute | solution.py:69
  29.0 4.8 %collective-permute-start.8 = (bf16[64,128]{1,0:T(8,128)(2,1)S(1)}, bf16[64,128]{1,0:T(8,128)(2,1)S(1)}, u32[]{:S(2)}, u32[]{:S(2)}) collective-permute-start(bf16[64,128]{1,0:T(8,128)(2,1)S(1)} %get-tuple-element.51), channel_id=1, source_target_pairs={{0,8},{1,9},{8,0},{9,1},{16,24},{17,25},{24,16},{25,17},{2,10},{3,... | collective-permute-start | bytes 49160 | tf_op jit(solution)/shard_map/ppermute | solution.py:69
  29.0 6.4 %collective-permute-start.9 = (bf16[64,128]{1,0:T(8,128)(2,1)S(1)}, bf16[64,128]{1,0:T(8,128)(2,1)S(1)}, u32[]{:S(2)}, u32[]{:S(2)}) collective-permute-start(bf16[64,128]{1,0:T(8,128)(2,1)S(1)} %get-tuple-element.52), channel_id=1, source_target_pairs={{0,9},{1,8},{8,1},{9,0},{16,25},{17,24},{24,17},{25,16},{2,11},{3,... | collective-permute-start | bytes 49160 | tf_op jit(solution)/shard_map/ppermute | solution.py:69
  31.9 4.9 %collective-permute-start.10 = (bf16[64,128]{1,0:T(8,128)(2,1)S(1)}, bf16[64,128]{1,0:T(8,128)(2,1)S(1)}, u32[]{:S(2)}, u32[]{:S(2)}) collective-permute-start(bf16[64,128]{1,0:T(8,128)(2,1)S(1)} %get-tuple-element.53), channel_id=1, source_target_pairs={{0,16},{1,17},{8,24},{9,25},{16,0},{17,1},{24,8},{25,9},{2,18},{3,... | collective-permute-start | bytes 49160 | tf_op jit(solution)/shard_map/ppermute | solution.py:69
  33.1 25.3 %collective-permute-start.24 = (bf16[64,512]{1,0:T(8,128)(2,1)S(1)}, bf16[64,512]{1,0:T(8,128)(2,1)S(1)}, u32[]{:S(2)}, u32[]{:S(2)}) collective-permute-start(bf16[64,512]{1,0:T(8,128)(2,1)S(1)} %get-tuple-element.62.refs_8_), channel_id=1, source_target_pairs={{0,1},{1,0},{2,3},{3,2},{4,5},{5,4},{6,7},{7,6},{8,9},{9,8},{10,11... | collective-permute-start | bytes 196616 | tf_op jit(solution)/shard_map/ppermute | solution.py:69
  33.7 24.8 %collective-permute-start.25 = (bf16[64,512]{1,0:T(8,128)(2,1)S(1)}, bf16[64,512]{1,0:T(8,128)(2,1)S(1)}, u32[]{:S(2)}, u32[]{:S(2)}) collective-permute-start(bf16[64,512]{1,0:T(8,128)(2,1)S(1)} %get-tuple-element.63), channel_id=1, source_target_pairs={{0,3},{1,2},{2,1},{3,0},{4,7},{5,6},{6,5},{7,4},{8,11},{9,10},{10,... | collective-permute-start | bytes 196616 | tf_op jit(solution)/shard_map/ppermute | solution.py:69
  33.7 26.6 %collective-permute-start.21 = (bf16[64,512]{1,0:T(8,128)(2,1)S(1)}, bf16[64,512]{1,0:T(8,128)(2,1)S(1)}, u32[]{:S(2)}, u32[]{:S(2)}) collective-permute-start(bf16[64,512]{1,0:T(8,128)(2,1)S(1)} %get-tuple-element.63), channel_id=1, source_target_pairs={{0,2},{1,3},{2,0},{3,1},{4,6},{5,7},{6,4},{7,5},{8,10},{9,11},{10,... | collective-permute-start | bytes 196616 | tf_op jit(solution)/shard_map/ppermute | solution.py:69
  35.3 26.4 %collective-permute-start.26 = (bf16[64,512]{1,0:T(8,128)(2,1)S(1)}, bf16[64,512]{1,0:T(8,128)(2,1)S(1)}, u32[]{:S(2)}, u32[]{:S(2)}) collective-permute-start(bf16[64,512]{1,0:T(8,128)(2,1)S(1)} %get-tuple-element.64), channel_id=1, source_target_pairs={{0,5},{1,4},{2,7},{3,6},{4,1},{5,0},{6,3},{7,2},{8,13},{9,12},{10,... | collective-permute-start | bytes 196616 | tf_op jit(solution)/shard_map/ppermute | solution.py:69
  36.8 5.5 %collective-permute-start.11 = (bf16[64,128]{1,0:T(8,128)(2,1)S(1)}, bf16[64,128]{1,0:T(8,128)(2,1)S(1)}, u32[]{:S(2)}, u32[]{:S(2)}) collective-permute-start(bf16[64,128]{1,0:T(8,128)(2,1)S(1)} %get-tuple-element.54), channel_id=1, source_target_pairs={{0,17},{1,16},{8,25},{9,24},{16,1},{17,0},{24,9},{25,8},{2,19},{3,... | collective-permute-start | bytes 49160 | tf_op jit(solution)/shard_map/ppermute | solution.py:69
  42.4 5.5 %collective-permute-start.12 = (bf16[64,128]{1,0:T(8,128)(2,1)S(1)}, bf16[64,128]{1,0:T(8,128)(2,1)S(1)}, u32[]{:S(2)}, u32[]{:S(2)}) collective-permute-start(bf16[64,128]{1,0:T(8,128)(2,1)S(1)} %get-tuple-element.55), channel_id=1, source_target_pairs={{0,24},{1,25},{8,16},{9,17},{16,8},{17,9},{24,0},{25,1},{2,26},{3,... | collective-permute-start | bytes 49160 | tf_op jit(solution)/shard_map/ppermute | solution.py:69
  47.9 6.4 %collective-permute-start.13 = (bf16[64,128]{1,0:T(8,128)(2,1)S(1)}, bf16[64,128]{1,0:T(8,128)(2,1)S(1)}, u32[]{:S(2)}, u32[]{:S(2)}) collective-permute-start(bf16[64,128]{1,0:T(8,128)(2,1)S(1)} %get-tuple-element.56), channel_id=1, source_target_pairs={{0,25},{1,24},{8,17},{9,16},{16,9},{17,8},{24,1},{25,0},{2,27},{3,... | collective-permute-start | bytes 49160 | tf_op jit(solution)/shard_map/ppermute | solution.py:69
  54.4 7.4 %collective-permute-start.22 = (bf16[64,512]{1,0:T(8,128)(2,1)S(1)}, bf16[64,512]{1,0:T(8,128)(2,1)S(1)}, u32[]{:S(2)}, u32[]{:S(2)}) collective-permute-start(bf16[64,512]{1,0:T(8,128)(2,1)S(1)} %get-tuple-element.64), channel_id=1, source_target_pairs={{0,4},{1,5},{2,6},{3,7},{4,0},{5,1},{6,2},{7,3},{8,12},{9,13},{10,... | collective-permute-start | bytes 196616 | tf_op jit(solution)/shard_map/ppermute | solution.py:69
  58.5 6.2 %collective-permute-start.23 = (bf16[64,512]{1,0:T(8,128)(2,1)S(1)}, bf16[64,512]{1,0:T(8,128)(2,1)S(1)}, u32[]{:S(2)}, u32[]{:S(2)}) collective-permute-start(bf16[64,512]{1,0:T(8,128)(2,1)S(1)} %get-tuple-element.65), channel_id=1, source_target_pairs={{0,6},{1,7},{2,4},{3,5},{4,2},{5,3},{6,0},{7,1},{8,14},{9,15},{10,... | collective-permute-start | bytes 196616 | tf_op jit(solution)/shard_map/ppermute | solution.py:69
  60.3 5.0 %collective-permute-start.17 = (bf16[64,512]{1,0:T(8,128)(2,1)S(1)}, bf16[64,512]{1,0:T(8,128)(2,1)S(1)}, u32[]{:S(2)}, u32[]{:S(2)}) collective-permute-start(bf16[64,512]{1,0:T(8,128)(2,1)S(1)} %get-tuple-element.58.refs_0_), channel_id=1, source_target_pairs={{0,1},{1,0},{2,3},{3,2},{4,5},{5,4},{6,7},{7,6},{8,9},{9,8},{10,11... | collective-permute-start | bytes 196616 | tf_op jit(solution)/shard_map/ppermute | solution.py:69
  61.7 6.2 %collective-permute-start.14 = (bf16[64,512]{1,0:T(8,128)(2,1)S(1)}, bf16[64,512]{1,0:T(8,128)(2,1)S(1)}, u32[]{:S(2)}, u32[]{:S(2)}) collective-permute-start(bf16[64,512]{1,0:T(8,128)(2,1)S(1)} %get-tuple-element.59), channel_id=1, source_target_pairs={{0,2},{1,3},{2,0},{3,1},{4,6},{5,7},{6,4},{7,5},{8,10},{9,11},{10,... | collective-permute-start | bytes 196616 | tf_op jit(solution)/shard_map/ppermute | solution.py:69
  63.1 5.3 %collective-permute-start.19 = (bf16[64,512]{1,0:T(8,128)(2,1)S(1)}, bf16[64,512]{1,0:T(8,128)(2,1)S(1)}, u32[]{:S(2)}, u32[]{:S(2)}) collective-permute-start(bf16[64,512]{1,0:T(8,128)(2,1)S(1)} %get-tuple-element.60), channel_id=1, source_target_pairs={{0,5},{1,4},{2,7},{3,6},{4,1},{5,0},{6,3},{7,2},{8,13},{9,12},{10,... | collective-permute-start | bytes 196616 | tf_op jit(solution)/shard_map/ppermute | solution.py:69
  64.7 6.5 %collective-permute-start.15 = (bf16[64,512]{1,0:T(8,128)(2,1)S(1)}, bf16[64,512]{1,0:T(8,128)(2,1)S(1)}, u32[]{:S(2)}, u32[]{:S(2)}) collective-permute-start(bf16[64,512]{1,0:T(8,128)(2,1)S(1)} %get-tuple-element.60), channel_id=1, source_target_pairs={{0,4},{1,5},{2,6},{3,7},{4,0},{5,1},{6,2},{7,3},{8,12},{9,13},{10,... | collective-permute-start | bytes 196616 | tf_op jit(solution)/shard_map/ppermute | solution.py:69
  65.3 5.9 %collective-permute-start.20 = (bf16[64,512]{1,0:T(8,128)(2,1)S(1)}, bf16[64,512]{1,0:T(8,128)(2,1)S(1)}, u32[]{:S(2)}, u32[]{:S(2)}) collective-permute-start(bf16[64,512]{1,0:T(8,128)(2,1)S(1)} %get-tuple-element.61), channel_id=1, source_target_pairs={{0,7},{1,6},{2,5},{3,4},{4,3},{5,2},{6,1},{7,0},{8,15},{9,14},{10,... | collective-permute-start | bytes 196616 | tf_op jit(solution)/shard_map/ppermute | solution.py:69
  66.0 5.8 %collective-permute-start.16 = (bf16[64,512]{1,0:T(8,128)(2,1)S(1)}, bf16[64,512]{1,0:T(8,128)(2,1)S(1)}, u32[]{:S(2)}, u32[]{:S(2)}) collective-permute-start(bf16[64,512]{1,0:T(8,128)(2,1)S(1)} %get-tuple-element.61), channel_id=1, source_target_pairs={{0,6},{1,7},{2,4},{3,5},{4,2},{5,3},{6,0},{7,1},{8,14},{9,15},{10,... | collective-permute-start | bytes 196616 | tf_op jit(solution)/shard_map/ppermute | solution.py:69
  74.9 7.6 %collective-permute-start.31 = (bf16[2,64,512]{2,1,0:T(8,128)(2,1)S(1)}, bf16[2,64,512]{2,1,0:T(8,128)(2,1)S(1)}, u32[]{:S(2)}, u32[]{:S(2)}) collective-permute-start(bf16[2,64,512]{2,1,0:T(8,128)(2,1)S(1)} %get-tuple-element.73), channel_id=1, source_target_pairs={{0,8},{8,0},{16,24},{24,16},{1,9},{9,1},{17,25},{25,17},{2,10},{10... | collective-permute-start | bytes 393224 | tf_op jit(solution)/shard_map/ppermute | solution.py:69
  75.0 13.9 %collective-permute-start.28 = (bf16[128,512]{1,0:T(8,128)(2,1)S(1)}, bf16[128,512]{1,0:T(8,128)(2,1)S(1)}, u32[]{:S(2)}, u32[]{:S(2)}) collective-permute-start(bf16[128,512]{1,0:T(8,128)(2,1)S(1)} %get-tuple-element.67), channel_id=1, source_target_pairs={{0,2},{2,0},{4,6},{6,4},{1,3},{3,1},{5,7},{7,5},{8,10},{10,8},{12,... | collective-permute-start | bytes 393224 | tf_op jit(solution)/shard_map/ppermute | solution.py:69
  75.3 12.8 %collective-permute-start.32 = (bf16[2,64,512]{2,1,0:T(8,128)(2,1)S(1)}, bf16[2,64,512]{2,1,0:T(8,128)(2,1)S(1)}, u32[]{:S(2)}, u32[]{:S(2)}) collective-permute-start(bf16[2,64,512]{2,1,0:T(8,128)(2,1)S(1)} %get-tuple-element.74), channel_id=1, source_target_pairs={{0,16},{8,24},{16,0},{24,8},{1,17},{9,25},{17,1},{25,9},{2,18},{10... | collective-permute-start | bytes 393224 | tf_op jit(solution)/shard_map/ppermute | solution.py:69
  78.0 10.1 %collective-permute-start.33 = (bf16[2,64,512]{2,1,0:T(8,128)(2,1)S(1)}, bf16[2,64,512]{2,1,0:T(8,128)(2,1)S(1)}, u32[]{:S(2)}, u32[]{:S(2)}) collective-permute-start(bf16[2,64,512]{2,1,0:T(8,128)(2,1)S(1)} %get-tuple-element.75), channel_id=1, source_target_pairs={{0,24},{8,16},{16,8},{24,0},{1,25},{9,17},{17,9},{25,1},{2,26},{10... | collective-permute-start | bytes 393224 | tf_op jit(solution)/shard_map/ppermute | solution.py:69
  79.4 9.5 %collective-permute-start.29 = (bf16[128,512]{1,0:T(8,128)(2,1)S(1)}, bf16[128,512]{1,0:T(8,128)(2,1)S(1)}, u32[]{:S(2)}, u32[]{:S(2)}) collective-permute-start(bf16[128,512]{1,0:T(8,128)(2,1)S(1)} %get-tuple-element.68), channel_id=1, source_target_pairs={{0,4},{2,6},{4,0},{6,2},{1,5},{3,7},{5,1},{7,3},{8,12},{10,14},{12... | collective-permute-start | bytes 393224 | tf_op jit(solution)/shard_map/ppermute | solution.py:69
  82.5 6.4 %collective-permute-start.30 = (bf16[128,512]{1,0:T(8,128)(2,1)S(1)}, bf16[128,512]{1,0:T(8,128)(2,1)S(1)}, u32[]{:S(2)}, u32[]{:S(2)}) collective-permute-start(bf16[128,512]{1,0:T(8,128)(2,1)S(1)} %get-tuple-element.69), channel_id=1, source_target_pairs={{0,6},{2,4},{4,2},{6,0},{1,7},{3,5},{5,3},{7,1},{8,14},{10,12},{12... | collective-permute-start | bytes 393224 | tf_op jit(solution)/shard_map/ppermute | solution.py:69
  (15 other events, 172.5 us)

commit v3 on v2

v3 whole, which is shorter than its diff:
```python
import functools
import math

import jax
import jax.numpy as jnp
from jax import lax
from jax.experimental import pallas as pl
from jax.experimental.pallas import tpu as pltpu
from jax.sharding import PartitionSpec as P

HD = 32
norm_eps = 1e-06
masked_score = -1e30
VMEM_LIMIT = 48 * 1024 * 1024
MOST_PERMUTES = 16
NT = (((1,), (1,)), ((), ()))
TN = (((0,), (0,)), ((), ()))


def dot(a, b, dims=None):
    if dims is None:
        return jnp.dot(a, b, preferred_element_type=jnp.float32)
    return lax.dot_general(a, b, dims, preferred_element_type=jnp.float32)


def away(index, offset, size):
    if size & (size - 1) == 0:
        return index ^ offset
    return (index + offset) % size


def back_from(index, offset, size):
    if size & (size - 1) == 0:
        return index ^ offset
    return (index - offset + size) % size


class Group:
    def __init__(self, axes, sizes):
        self.axes, self.sizes = tuple(axes), tuple(sizes)
        self.count = math.prod(sizes)

    def split(self, flat):
        coords = []
        for size in reversed(self.sizes):
            coords.append(flat % size)
            flat = flat // size
        return coords[::-1]

    def moved(self, flat, offset, step):
        place = 0
        for coord, part, size in zip(self.split(flat), self.split(offset), self.sizes):
            place = place * size + step(coord, part, size)
        return place

    def target(self, flat, offset):
        return self.moved(flat, offset, away)

    def source(self, flat, offset):
        return self.moved(flat, offset, back_from)

    def exchange(self, chunks, inverse=False):
        to, start = (self.source, self.target) if inverse else (self.target, self.source)
        if self.count <= MOST_PERMUTES:
            order = sorted(range(1, self.count), key=lambda k: -k)
            got = {0: chunks[0]}
            for k in order:
                pairs = [(i, to(i, k)) for i in range(self.count)]
                got[k] = lax.ppermute(chunks[k], self.axes, pairs)
            return [got[k] for k in range(self.count)]
        me = lax.axis_index(self.axes)
        steps = jnp.arange(self.count, dtype=jnp.int32)
        sent_to = jax.vmap(lambda k: to(me, k))(steps)
        placed = jnp.zeros((self.count,), jnp.int32).at[sent_to].set(steps)
        stacked = jnp.stack(chunks)[placed]
        got = lax.all_to_all(stacked, self.axes, split_axis=0, concat_axis=0, tiled=True)
        came_from = jax.vmap(lambda k: start(me, k))(steps)
        ordered = got[came_from]
        return [ordered[k] for k in range(self.count)]


def merged(chunks, most):
    if len(chunks) <= most:
        return list(chunks)
    return [jnp.concatenate(chunks, axis=0)]


def chunk_rows(refs, count, low, high):
    size = sum(ref.shape[0] for ref in refs) // count
    parts = []
    for chunk in range(count):
        ref, first = (refs[chunk], 0) if len(refs) == count else (refs[0], chunk * size)
        parts.append(ref[first + low : first + high, :])
    return parts[0] if count == 1 else jnp.concatenate(parts, axis=0)


def slot_matrix(choice, own, expert_count, hot_capacity):
    tok = choice.shape[1]
    offset = back_from(choice, own, expert_count)
    one_hot = lax.broadcasted_iota(jnp.int32, (expert_count, tok), 0) == offset
    hits = one_hot.astype(jnp.float32).astype(jnp.bfloat16)
    earlier = lax.broadcasted_iota(jnp.int32, (tok, tok), 0) <= lax.broadcasted_iota(
        jnp.int32, (tok, tok), 1
    )
    counted = dot(hits, earlier.astype(jnp.float32).astype(jnp.bfloat16))
    rank = jnp.sum(jnp.where(one_hot, counted, 0.0), axis=0, keepdims=True) - 1.0
    slots = offset * hot_capacity + rank.astype(jnp.int32)
    rows = lax.broadcasted_iota(jnp.int32, (expert_count * hot_capacity, tok), 0)
    return (rows == slots).astype(jnp.float32).astype(jnp.bfloat16)


def stack_kernel(key_ref, value_ref, out_ref, sems):
    tok = key_ref.shape[0]
    copies = [
        pltpu.make_async_copy(ref, out_ref.at[pl.ds(place * tok, tok), :], sems.at[place])
        for place, ref in enumerate((key_ref, value_ref))
    ]
    for copy in copies:
        copy.start()
    for copy in copies:
        copy.wait()


def dispatch_kernel(reps, hot_capacity, own_ref, *refs):
    choice_refs, row_refs, sent_refs = refs[:reps], refs[reps : 2 * reps], refs[2 * reps :]
    for rep in range(reps):
        placed = slot_matrix(choice_refs[rep][...], own_ref[0], len(sent_refs), hot_capacity)
        rows = dot(placed, row_refs[rep][...]).astype(jnp.bfloat16)
        for k, sent_ref in enumerate(sent_refs):
            sent_ref[rep * hot_capacity : (rep + 1) * hot_capacity] = rows[
                k * hot_capacity : (k + 1) * hot_capacity
            ]


def attend_blocks(block_ref, lengths_ref, query_ref, pair_refs, state_refs, bias_ref, first):
    top_ref, total_ref, sum_ref = state_refs
    tok, width = query_ref.shape
    lanes = 128
    per = lanes // HD
    scale = math.log2(math.e) / math.sqrt(HD)
    turned = query_ref[...].T
    head_of_row = lax.broadcasted_iota(jnp.int32, (lanes, tok), 0) // HD
    spread = []
    for group in range(width // lanes):
        part = turned[group * lanes : (group + 1) * lanes]
        spread.append(
            jnp.concatenate(
                [jnp.where(head_of_row == head, part, jnp.zeros_like(part)) for head in range(per)],
                axis=1,
            )
        )
    position = block_ref[0] * tok + lax.broadcasted_iota(jnp.int32, (1, tok), 1)
    begin = jnp.zeros((1, tok), jnp.int32)
    bound = jnp.int32(0)
    for doc in range(lengths_ref.shape[1] - 1):
        bound = bound + lengths_ref[0, doc]
        begin = jnp.maximum(begin, jnp.where(position >= bound, bound, 0))

    def fold(pair_ref, block, fresh):
        key_position = block * tok + lax.broadcasted_iota(jnp.int32, (tok, tok), 0)
        visible = (key_position >= begin) & (key_position <= position)
        bias_ref[...] = jnp.where(visible, 0.0, masked_score)
        bias = bias_ref[...]
        values = pair_ref[tok : 2 * tok, :].T
        for group in range(width // lanes):
            columns = slice(group * lanes, (group + 1) * lanes)
            scores = dot(pair_ref[0:tok, columns], spread[group])
            weights, factors = [], []
            for head in range(per):
                row = group * per + head
                part = scores[:, head * tok : (head + 1) * tok] + bias
                top = jnp.max(part, axis=0, keepdims=True)
                if not fresh:
                    old = top_ref[row : row + 1, :]
                    top = jnp.maximum(top, old)
                    factors.append(jnp.exp2((old - top) * scale))
                weight = jnp.exp2((part - top) * scale)
                total = jnp.sum(weight, axis=0, keepdims=True)
                if not fresh:
                    total = total + total_ref[row : row + 1, :] * factors[head]
                top_ref[row : row + 1, :] = top
                total_ref[row : row + 1, :] = total
                weights.append(weight.astype(jnp.bfloat16))
            summed = dot(values[columns], jnp.concatenate(weights, axis=1))
            for head in range(per):
                rows = slice((group * per + head) * HD, (group * per + head + 1) * HD)
                piece = summed[head * HD : (head + 1) * HD, head * tok : (head + 1) * tok]
                if not fresh:
                    piece = piece + sum_ref[rows, :] * factors[head]
                sum_ref[rows, :] = piece

    for place, pair_ref in enumerate(pair_refs):
        block = block_ref[1 + place]
        if first and place == 0:
            fold(pair_ref, block, True)
        else:

            @pl.when(block >= 0)
            def unused(pair_ref=pair_ref, block=block):
                fold(pair_ref, block, False)


def attend_kernel(count, first, block_ref, lengths_ref, query_ref, *refs):
    pair_refs, refs = refs[:count], refs[count:]
    if not first:
        for old_ref, new_ref in zip(refs[0:3], refs[3:6]):
            new_ref[...] = old_ref[...]
        refs = refs[3:]
    attend_blocks(block_ref, lengths_ref, query_ref, pair_refs, refs[0:3], refs[3], first)


def mix_kernel(
    count,
    hot_capacity,
    block_ref,
    own_ref,
    lengths_ref,
    query_ref,
    choice_ref,
    residual_ref,
    proj_ref,
    *refs,
):
    pair_refs, refs = refs[:count], refs[count:]
    old_refs, mixed_ref, normed_ref = refs[0:3], refs[3], refs[4]
    sent_refs, state_refs, bias_ref = refs[5:-4], refs[-4:-1], refs[-1]
    for old_ref, new_ref in zip(old_refs, state_refs):
        new_ref[...] = old_ref[...]
    attend_blocks(block_ref, lengths_ref, query_ref, pair_refs, state_refs, bias_ref, False)
    unused_top, total_ref, sum_ref = state_refs
    pieces = [
        (sum_ref[head * HD : (head + 1) * HD, :] / total_ref[head : head + 1, :]).astype(
            jnp.bfloat16
        )
        for head in range(total_ref.shape[0])
    ]
    attended = jnp.concatenate(pieces, axis=0).T
    mixed = (residual_ref[...].astype(jnp.float32) + dot(attended, proj_ref[...])).astype(
        jnp.bfloat16
    )
    mixed_ref[...] = mixed
    mixed_f = mixed.astype(jnp.float32)
    inv_rms = lax.rsqrt(jnp.mean(mixed_f * mixed_f, axis=1, keepdims=True) + norm_eps)
    normed = (mixed_f * inv_rms).astype(jnp.bfloat16)
    normed_ref[...] = normed
    placed = slot_matrix(choice_ref[...], own_ref[0], len(sent_refs), hot_capacity)
    rows = dot(placed, normed).astype(jnp.bfloat16)
    for k, sent_ref in enumerate(sent_refs):
        sent_ref[...] = rows[k * hot_capacity : (k + 1) * hot_capacity]


def expert_kernel(
    reps,
    rep_list,
    sources,
    strip,
    counts,
    own_ref,
    part_ref,
    up_ref,
    down_ref,
    router_ref,
    *refs,
):
    row_count, grad_count = counts
    row_refs, refs = refs[:row_count], refs[row_count:]
    grad_refs, refs = refs[:grad_count], refs[grad_count:]
    own_rows = rep_list[0] == 0
    held_ref, refs = refs[-1], refs[:-1]
    if own_rows:
        back_refs, (up_acc, down_acc) = refs[:-2], refs[-2:]
    else:
        up_old, down_old = refs[:2]
        term_refs, kept_ref = refs[2:-1], refs[-1]
    total_grads = sum(ref.shape[0] for ref in grad_refs)
    capacity = total_grads // (sources * reps)
    count = sources * capacity
    parts = part_ref.shape[0]
    up = up_ref[...]
    down = down_ref[...]
    router = router_ref[...]
    expert_lane = lax.broadcasted_iota(jnp.int32, (count, router.shape[0]), 1) == own_ref[0]

    def strips(rows, place):
        held_ref[place] = rows.T
        taken = []
        for k in range(parts):
            first = pl.multiple_of(part_ref[k] * strip, strip)
            taken.append(held_ref[place, pl.ds(first, strip), :])
        return jnp.concatenate(taken, axis=0)

    up_term = down_term = None
    for place, rep in enumerate(rep_list):
        rows = chunk_rows(row_refs, sources, place * capacity, (place + 1) * capacity)
        grads = chunk_rows(grad_refs, sources, rep * capacity, (rep + 1) * capacity)
        pre = dot(rows, up)
        sigmoid_pre = jax.nn.sigmoid(pre)
        activated = (pre * sigmoid_pre).astype(jnp.bfloat16)
        logits = dot(rows, router, NT)
        gate = jax.nn.sigmoid(
            jnp.sum(jnp.where(expert_lane, logits, 0.0), axis=1, keepdims=True)
        )
        scaled = (gate * grads.astype(jnp.float32)).astype(jnp.bfloat16)
        act_grad = dot(scaled, down, NT)
        pre_grad = (act_grad * sigmoid_pre * (1.0 + pre * (1.0 - sigmoid_pre))).astype(
            jnp.bfloat16
        )
        if own_rows:
            produced = dot(activated, down).astype(jnp.bfloat16)
            token_grad = dot(pre_grad, up, NT).astype(jnp.bfloat16)
            for k, back_ref in enumerate(back_refs):
                back_ref[0:capacity] = produced[k * capacity : (k + 1) * capacity]
                back_ref[capacity : 2 * capacity] = token_grad[k * capacity : (k + 1) * capacity]
        more_up = dot(strips(rows, 2 * place), pre_grad)
        more_down = dot(strips(activated, 2 * place + 1), scaled)
        up_term = more_up if up_term is None else up_term + more_up
        down_term = more_down if down_term is None else down_term + more_down
    if own_rows:
        up_acc[...] = up_term
        down_acc[...] = down_term
        return
    up_term = up_term + up_old[...]
    down_term = down_term + down_old[...]
    for k in range(parts):
        rows = slice(k * strip, (k + 1) * strip)
        if k == 0:
            kept_ref[0] = up_term[rows]
            kept_ref[1] = down_term[rows]
        else:
            term_refs[k - 1][0] = up_term[rows].astype(jnp.bfloat16)
            term_refs[k - 1][1] = down_term[rows].astype(jnp.bfloat16)


def finish_kernel(
    hot_capacity, own_ref, choice_ref, router_ref, mixed_ref, grad_ref, *refs
):
    back_refs, (layer_ref, grad_mixed_ref) = refs[:-2], refs[-2:]
    expert_count = router_ref.shape[0]
    tok = mixed_ref.shape[0]
    choice = choice_ref[...]
    placed = slot_matrix(choice, own_ref[0], expert_count, hot_capacity)
    router = router_ref[...]
    mixed_f = mixed_ref[...].astype(jnp.float32)
    inv_rms = lax.rsqrt(jnp.mean(mixed_f * mixed_f, axis=1, keepdims=True) + norm_eps)
    normed = (mixed_f * inv_rms).astype(jnp.bfloat16)
    one_hot = lax.broadcasted_iota(jnp.int32, (expert_count, tok), 0) == choice
    logits = dot(router, normed, NT)
    logit_row = jnp.sum(jnp.where(one_hot, logits, 0.0), axis=0, keepdims=True)
    logit = jnp.broadcast_to(logit_row, (8, tok)).T[:, 0:1]
    gate = jax.nn.sigmoid(logit)
    pair = 2 * hot_capacity
    chunks = [
        ref[first : first + pair] for ref in back_refs for first in range(0, ref.shape[0], pair)
    ]
    results = jnp.concatenate([chunk[:hot_capacity] for chunk in chunks], axis=0)
    grads = jnp.concatenate([chunk[hot_capacity:] for chunk in chunks], axis=0)
    result_f = dot(placed, results, TN)
    normed_grad = dot(placed, grads, TN)
    grad_f = grad_ref[...].astype(jnp.float32)
    layer_ref[...] = (mixed_f + gate * result_f).astype(jnp.bfloat16)
    gate_grad = jnp.sum(grad_f * result_f, axis=1, keepdims=True)
    logit_grad = gate_grad * gate * (1.0 - gate)
    router_cols = dot(one_hot.astype(jnp.float32).astype(jnp.bfloat16), router, TN)
    total_grad = normed_grad + logit_grad * router_cols
    mean_term = jnp.mean(total_grad * mixed_f, axis=1, keepdims=True)
    input_grad = inv_rms * total_grad - mixed_f * inv_rms * inv_rms * inv_rms * mean_term
    grad_mixed_ref[...] = (grad_f + input_grad).astype(jnp.bfloat16)


def sum_kernel(kept_ref, *refs):
    term_refs, (up_ref, down_ref) = refs[:-2], refs[-2:]
    for kind, out_ref in enumerate((up_ref, down_ref)):
        total = kept_ref[kind]
        for ref in term_refs:
            total = total + ref[kind].astype(jnp.float32)
        out_ref[...] = total


def shape(dims, dtype=jnp.bfloat16):
    return jax.ShapeDtypeStruct(dims, dtype)


SMEM = pl.BlockSpec(memory_space=pltpu.SMEM)
VMEM = pl.BlockSpec(memory_space=pltpu.VMEM)
HBM = pl.BlockSpec(memory_space=pltpu.HBM)


def call(body, out_shape, specs, scratch=()):
    return pl.pallas_call(
        body,
        out_shape=out_shape,
        in_specs=specs,
        out_specs=jax.tree.map(lambda unused: VMEM, out_shape),
        scratch_shapes=list(scratch),
        compiler_params=pltpu.CompilerParams(vmem_limit_bytes=VMEM_LIMIT),
    )


def local(
    seq_count,
    expert_count,
    rep_count,
    query_rows,
    key_rows,
    value_rows,
    doc_lengths,
    residual,
    out_proj,
    router,
    expert_choice,
    weight_in,
    weight_out,
    grad_out,
):
    tok, width = query_rows.shape[1:]
    hidden = weight_in.shape[2]
    heads = width // HD
    experts = Group(("expert",), (expert_count,))
    reps = Group(("rep",), (rep_count,))
    parts = Group(("seq",), (seq_count,))
    strip = width // (seq_count * rep_count)
    capacity = max(2, (3 * tok + 2 * expert_count - 1) // (2 * expert_count))
    hot_capacity = min(4 * capacity, tok // 2)
    choice = expert_choice.reshape(1, tok)
    router_rows = router.T
    seq_index = lax.axis_index("seq")
    rep_index = lax.axis_index("rep")
    rank = seq_index * rep_count + rep_index
    own = jnp.stack([lax.axis_index("expert")]).astype(jnp.int32)
    part_to = jnp.stack(
        [parts.target(seq_index, k) * rep_count + rep_index for k in range(seq_count)]
    ).astype(jnp.int32)

    def send(array, least_seq, seq_step, rep_step, wrap):
        pairs = []
        for s in range(least_seq, seq_count - seq_step):
            for r in range(rep_count):
                to = r + rep_step
                if wrap or 0 <= to < rep_count:
                    pairs.append(
                        (s * rep_count + r, (s + seq_step) * rep_count + to % rep_count)
                    )
        return lax.ppermute(array, ("seq", "rep"), pairs)

    def block_ids(entries):
        ids = [rank]
        for seq_back, rep, needed in entries:
            block = (seq_index - seq_back) * rep_count + rep
            ids.append(jnp.where(needed & (seq_index >= seq_back), block, -1))
        return jnp.stack(ids).astype(jnp.int32)

    pair = call(
        stack_kernel,
        shape((2 * tok, width)),
        [HBM, HBM],
        [pltpu.SemaphoreType.DMA((2,))],
    )(key_rows[0], value_rows[0])
    always = rep_index >= 0
    reach = (seq_count + 1) // 2
    rounds = [([pair], [(0, rep_index, always)])]
    line = pair
    for step in range(1, reach + 1):
        arrays, entries = [], []
        ahead = send(line, step - 1, 1, 0, False)
        arrays.append(ahead)
        entries.append((step, rep_index, always))
        for d in range(1, rep_count):
            if step == 1:
                arrays.append(send(line, 0, 0, d, False))
                entries.append((0, rep_index - d, rep_index >= d))
            else:
                arrays.append(send(line, step - 1, 0, d, True))
                entries.append((step - 1, (rep_index - d) % rep_count, always))
            if step == reach:
                arrays.append(send(line, step - 1, 1, -d, False))
                entries.append((step, rep_index + d, rep_index + d < rep_count))
        rounds.append((arrays, entries))
        line = ahead

    choices = [choice] + [
        lax.ppermute(choice, "rep", [(i, reps.target(i, k)) for i in range(rep_count)])
        for k in range(1, rep_count)
    ]
    grads = reps.exchange([grad_out[0]] * rep_count)
    sent_grads = call(
        functools.partial(dispatch_kernel, rep_count, hot_capacity),
        [shape((rep_count * hot_capacity, width))] * expert_count,
        [SMEM] + [VMEM] * (2 * rep_count),
    )(own, *choices, *grads)
    got_grads = merged(experts.exchange(sent_grads), MOST_PERMUTES)

    state_shapes = [
        shape((heads, tok), jnp.float32),
        shape((heads, tok), jnp.float32),
        shape((width, tok), jnp.float32),
    ]
    bias = pltpu.VMEM((tok, tok), jnp.float32)
    query = query_rows[0]
    state = ()
    for place, (arrays, entries) in enumerate(rounds[:-1]):
        state = call(
            functools.partial(attend_kernel, len(arrays), place == 0),
            state_shapes,
            [SMEM, SMEM] + [VMEM] * (1 + len(arrays) + len(state)),
            [bias],
        )(block_ids(entries), doc_lengths, query, *arrays, *state)
    arrays, entries = rounds[-1]
    mixed, normed, *sent_rows = call(
        functools.partial(mix_kernel, len(arrays), hot_capacity),
        [shape((tok, width))] * 2 + [shape((hot_capacity, width))] * expert_count,
        [SMEM, SMEM, SMEM] + [VMEM] * (7 + len(arrays)),
        [pltpu.VMEM(one.shape, one.dtype) for one in state_shapes] + [bias],
    )(block_ids(entries), own, doc_lengths, query, choice, residual[0], out_proj, *arrays, *state)

    others = reps.exchange([normed] * rep_count)[1:]
    got_rows = merged(experts.exchange(sent_rows), MOST_PERMUTES)
    more_rows = call(
        functools.partial(dispatch_kernel, rep_count - 1, hot_capacity),
        [shape(((rep_count - 1) * hot_capacity, width))] * expert_count,
        [SMEM] + [VMEM] * (2 * (rep_count - 1)),
    )(own, *choices[1:], *others)
    got_more = merged(experts.exchange(more_rows), MOST_PERMUTES)

    def expert_call(rep_list, rows, out_shape, extra):
        return call(
            functools.partial(
                expert_kernel,
                rep_count,
                rep_list,
                expert_count,
                strip,
                (len(rows), len(got_grads)),
            ),
            out_shape,
            [SMEM, SMEM] + [VMEM] * (3 + len(rows) + len(got_grads) + len(extra)),
            [pltpu.VMEM((2 * len(rep_list), width, expert_count * hot_capacity), jnp.bfloat16)],
        )(own, part_to, weight_in[0], weight_out[0], router_rows, *rows, *got_grads, *extra)

    *back, up_acc, down_acc = expert_call(
        (0,),
        got_rows,
        [shape((2 * hot_capacity, width))] * expert_count
        + [shape((seq_count * strip, hidden), jnp.float32)]
        + [shape((seq_count * strip, width), jnp.float32)],
        [],
    )
    got_back = merged(experts.exchange(back, inverse=True), MOST_PERMUTES)
    *terms, kept = expert_call(
        tuple(range(1, rep_count)),
        got_more,
        [shape((2, strip, hidden))] * (seq_count - 1)
        + [shape((2, strip, hidden), jnp.float32)],
        [up_acc, down_acc],
    )
    got_terms = parts.exchange([None] + terms)[1:]
    layer_out, grad_mixed = call(
        functools.partial(finish_kernel, hot_capacity),
        [shape((tok, width)), shape((tok, width))],
        [SMEM] + [VMEM] * (4 + len(got_back)),
    )(own, choice, router_rows, mixed, grad_out[0], *got_back)
    share_in, share_out = call(
        sum_kernel,
        [shape((strip, hidden), jnp.float32), shape((strip, width), jnp.float32)],
        [VMEM] * seq_count,
    )(kept, *got_terms)
    return (layer_out[None], grad_mixed[None], share_in[None], share_out[None])


def solution(mesh):
    rows = P("expert", ("seq", "rep"), None)
    in_specs = (
        rows,
        rows,
        rows,
        P("expert", None),
        rows,
        P(),
        P(),
        rows,
        P("expert", None, None),
        P("expert", None, None),
        rows,
    )
    body = functools.partial(
        local, mesh.shape["seq"], mesh.shape["expert"], mesh.shape["rep"]
    )
    return jax.shard_map(
        body, mesh=mesh, in_specs=in_specs, out_specs=(rows, rows, rows, rows), check_vma=False
    )
```

time: 91.2 us -> 70.4 us (0.77)
  waiting for transfers between devices: 27.4 us -> 16.3 us
  starting transfers between devices: 44.7 us -> 38.2 us
  local copies, waits for them, and re-layouts: 6.19 us -> 3.54 us
  Pallas kernels: 11.7 us -> 10.4 us
    ppermute x34 -> x17, starting transfers between devices: 44.7 us -> 27.3 us  [exchange(): got[k] = lax.ppermute(chunks[k], self.axes, pairs)]
    ppermute x34 -> x17, waiting for transfers between devices: 27.4 us -> 11.7 us  [exchange(): got[k] = lax.ppermute(chunks[k], self.axes, pairs)]
    ppermute x0 -> x6, starting transfers between devices: none -> 10.9 us  [the longest x5 10.4 us: send(): return lax.ppermute(array, ('seq', 'rep'), pairs)]
    ppermute x0 -> x6, waiting for transfers between devices: none -> 4.61 us  [the longest x1 2.49 us: local(): lax.ppermute(choice, 'rep', [(i, reps.target(i, k)) for i in range(rep_co...]
    unnamed x26 -> x22, local copies, waits for them, and re-layouts: 6.1 us -> 3.54 us
    pallas_call x5 -> x8, Pallas kernels: 9.58 us -> 8.29 us  [the longest x2 3.47 us: expert_call(): call(functools.partial(expert_kernel, rep_count, rep_list, expert_count,...]
  transfers between devices with their start and end apart: 34 -> 23, of which waited for: 11 -> 8; matrix products, arithmetic and copies ran while one was open for 0% -> 0% of each run, Pallas kernels for 2% -> 13%
where the time goes in v3:
time: 70.4 us; the launch traced here: 69.6 us
  starting transfers between devices  38.2 us (54%)
  waiting for transfers between devices  16.3 us (23%)
  Pallas kernels  10.4 us (15%)
  local copies, waits for them, and re-layouts  3.54 us (5%)
  between operations  0.84 us (1%)
    ppermute x17, starting transfers between devices, exchange(): got[k] = lax.ppermute(chunks[k], self.axes, pairs)  27.3 us
    ppermute x17, waiting for transfers between devices, exchange(): got[k] = lax.ppermute(chunks[k], self.axes, pairs)  11.7 us
    ppermute x5, starting transfers between devices, send(): return lax.ppermute(array, ('seq', 'rep'), pairs)  10.4 us
    unnamed x22, local copies, waits for them, and re-layouts  3.54 us
    pallas_call x2, Pallas kernels, expert_call(): call(functools.partial(expert_kernel, rep_count, rep_list, expert_count,...  3.47 us
    ppermute x1, waiting for transfers between devices, local(): lax.ppermute(choice, 'rep', [(i, reps.target(i, k)) for i in range(rep_co...  2.49 us
    pallas_call x2, Pallas kernels, local(): call(functools.partial(attend_kernel, len(arrays), place == 0), state_sha...  2.38 us
    ppermute x5, waiting for transfers between devices, send(): return lax.ppermute(array, ('seq', 'rep'), pairs)  2.12 us
  transfers between devices with their start and end apart: 23, of which 8 were waited for; matrix products, arithmetic and copies ran while one was open for 0% of the time, Pallas kernels for 13%

profile of v3, /device:TPU:0, one launch (start us, length us, event | category | flops | bytes accessed | tf_op | source)
XLA Modules:
  0.0 69.6 jit_solution(12452451216014978990)
XLA Ops:
  0.6 0.9 %copy-done.6 = bf16[1,128,512]{2,1,0:T(8,128)(2,1)S(1)} copy-done((bf16[1,128,512]{2,1,0:T(8,128)(2,1)S(1)}, bf16[1,128,512]{2,1,0:T(8,128)(2,1)}, u32[]{:S(2)}) %copy-start.6) | copy-done | bytes 131096
  1.5 0.9 %copy-done.7 = bf16[1,128,512]{2,1,0:T(8,128)(2,1)S(1)} copy-done((bf16[1,128,512]{2,1,0:T(8,128)(2,1)S(1)}, bf16[1,128,512]{2,1,0:T(8,128)(2,1)}, u32[]{:S(2)}) %copy-start.7) | copy-done | bytes 131096
  2.8 4.9 %collective-permute-start = (bf16[256,512]{1,0:T(8,128)(2,1)S(1)}, bf16[256,512]{1,0:T(8,128)(2,1)S(1)}, u32[]{:S(2)}, u32[]{:S(2)}) collective-permute-start(bf16[256,512]{1,0:T(8,128)(2,1)S(1)} %shard_map.138.refs_0_), channel_id=1, source_target_pairs={{0,8},{1,9},{8,16},{9,17},{16,24},{17,25},{2,10},{3,11},{10,18},{1... | collective-permute-start | bytes 786440 | tf_op jit(solution)/shard_map/ppermute | solution.py:443
  7.7 3.4 %collective-permute-start.4 = (bf16[256,512]{1,0:T(8,128)(2,1)S(1)}, bf16[256,512]{1,0:T(8,128)(2,1)S(1)}, u32[]{:S(2)}, u32[]{:S(2)}) collective-permute-start(bf16[256,512]{1,0:T(8,128)(2,1)S(1)} %shard_map.138.refs_0_), channel_id=1, source_target_pairs={{0,1},{8,9},{16,17},{24,25},{2,3},{10,11},{18,19},{26,27},{4,5},{1... | collective-permute-start | bytes 786440 | tf_op jit(solution)/shard_map/ppermute | solution.py:443
  11.2 2.1 %collective-permute-done.refs_0_ = bf16[256,512]{1,0:T(8,128)(2,1)S(1)} collective-permute-done((bf16[256,512]{1,0:T(8,128)(2,1)S(1)}, bf16[256,512]{1,0:T(8,128)(2,1)S(1)}, u32[]{:S(2)}, u32[]{:S(2)}) %collective-permute-start) | collective-permute-done | bytes 262176 | tf_op jit(solution)/shard_map/ppermute | solution.py:443
  13.3 0.7 collective-permute-start.1
  14.0 1.6 %collective-permute-start.9 = (bf16[128,512]{1,0:T(8,128)(2,1)S(1)}, bf16[128,512]{1,0:T(8,128)(2,1)S(1)}, u32[]{:S(2)}, u32[]{:S(2)}) collective-permute-start(bf16[128,512]{1,0:T(8,128)(2,1)S(1)} %bitcast.32), channel_id=1, source_target_pairs={{0,1},{1,0},{2,3},{3,2},{4,5},{5,4},{6,7},{7,6},{8,9},{9,8},{10,11... | collective-permute-start | bytes 393224 | tf_op jit(solution)/shard_map/ppermute | solution.py:69
  16.1 0.7 collective-permute-start.2
  16.8 2.5 %collective-permute-done.8.refs_1_.refs_0_ = s32[1,128]{1,0:T(1,128)S(1)} collective-permute-done((s32[1,128]{1,0:T(1,128)S(1)}, s32[1,128]{1,0:T(1,128)S(1)}, u32[]{:S(2)}, u32[]{:S(2)}) %collective-permute-start.8) | collective-permute-done | bytes 544 | tf_op jit(solution)/shard_map/ppermute | solution.py:481
  19.3 0.7 collective-permute-start.3
  20.7 1.6 %collective-permute-start.11 = (bf16[128,512]{1,0:T(8,128)(2,1)S(1)}, bf16[128,512]{1,0:T(8,128)(2,1)S(1)}, u32[]{:S(2)}, u32[]{:S(2)}) collective-permute-start(bf16[128,512]{1,0:T(8,128)(2,1)S(1)} %get-tuple-element.51), channel_id=1, source_target_pairs={{0,4},{2,6},{4,0},{6,2},{1,5},{3,7},{5,1},{7,3},{8,12},{10,14},{12... | collective-permute-start | bytes 393224 | tf_op jit(solution)/shard_map/ppermute | solution.py:69
  22.7 0.7 copy-done.9
  23.4 1.7 %shard_map.139 = (f32[16,128]{1,0:T(8,128)S(1)}, f32[16,128]{1,0:T(8,128)S(1)}, f32[512,128]{1,0:T(8,128)S(1)}) custom-call(s32[2]{0:T(128)S(1)} %pad_add_fusion.2.block_ref, s32[1,8]{1,0:T(1,128)S(1)} %copy-done.9, bf16[128,512]{1,0:T(8,128)(2,1)S(1)} %bitcast.29, bf16[256,512]{1,0:T(8,128)(2,1)S(1)} %shard_map.138.refs_0_), custom_call_target="tpu_custom_call" | custom-call | tf_op jit(solution)/shard_map/pallas_call | solution.py:501
  25.2 0.6 shard_map.140
  26.2 1.2 %shard_map.141 = (bf16[128,512]{1,0:T(8,128)(2,1)S(1)}, bf16[128,512]{1,0:T(8,128)(2,1)S(1)}, bf16[64,512]{1,0:T(8,128)(2,1)S(1)}, bf16[64,512]{1,0:T(8,128)(2,1...) custom-call(s32[4]{0:T(128)S(1)} %pad_add_fusion.block_ref, s32[1]{0:T(128)} %bitcast.own_ref, ...), custom_call_target="tpu_custom_call" | custom-call | tf_op jit(solution)/shard_map/pallas_call | solution.py:508
  27.9 1.5 %collective-permute-start.6 = (bf16[64,512]{1,0:T(8,128)(2,1)S(1)}, bf16[64,512]{1,0:T(8,128)(2,1)S(1)}, u32[]{:S(2)}, u32[]{:S(2)}) collective-permute-start(bf16[64,512]{1,0:T(8,128)(2,1)S(1)} %get-tuple-element.47), channel_id=1, source_target_pairs={{0,4},{2,6},{4,0},{6,2},{1,5},{3,7},{5,1},{7,3},{8,12},{10,14},{12... | collective-permute-start | bytes 196616 | tf_op jit(solution)/shard_map/ppermute | solution.py:69
  29.4 3.4 %collective-permute-start.16 = (bf16[128,512]{1,0:T(8,128)(2,1)S(1)}, bf16[128,512]{1,0:T(8,128)(2,1)S(1)}, u32[]{:S(2)}, u32[]{:S(2)}) collective-permute-start(bf16[128,512]{1,0:T(8,128)(2,1)S(1)} %get-tuple-element.59), channel_id=1, source_target_pairs={{0,1},{1,0},{2,3},{3,2},{4,5},{5,4},{6,7},{7,6},{8,9},{9,8},{10,11... | collective-permute-start | bytes 393224 | tf_op jit(solution)/shard_map/ppermute | solution.py:69
  32.9 0.8 %collective-permute-done.7.refs_3_ = bf16[64,512]{1,0:T(8,128)(2,1)S(1)} collective-permute-done((bf16[64,512]{1,0:T(8,128)(2,1)S(1)}, bf16[64,512]{1,0:T(8,128)(2,1)S(1)}, u32[]{:S(2)}, u32[]{:S(2)}) %collective-permute-start.7) | collective-permute-done | bytes 65568 | tf_op jit(solution)/shard_map/ppermute | solution.py:69
  33.8 0.7 copy-done.8
  34.4 1.8 %shard_map.143 = (bf16[128,512]{1,0:T(8,128)(2,1)S(1)}, bf16[128,512]{1,0:T(8,128)(2,1)S(1)}, bf16[128,512]{1,0:T(8,128)(2,1)S(1)}, bf16[128,512]{1,0:T(8,128)(2...) custom-call(s32[1]{0:T(128)} %bitcast.own_ref, s32[4]{0:T(128)S(1)} %pad_add_fusion.3.part_ref, ...), custom_call_target="tpu_custom_call" | custom-call | tf_op jit(solution)/shard_map/pallas_call | solution.py:525
  37.5 1.6 %collective-permute-start.18 = (bf16[64,512]{1,0:T(8,128)(2,1)S(1)}, bf16[64,512]{1,0:T(8,128)(2,1)S(1)}, u32[]{:S(2)}, u32[]{:S(2)}) collective-permute-start(bf16[64,512]{1,0:T(8,128)(2,1)S(1)} %get-tuple-element.62), channel_id=1, source_target_pairs={{0,4},{2,6},{4,0},{6,2},{1,5},{3,7},{5,1},{7,3},{8,12},{10,14},{12... | collective-permute-start | bytes 196616 | tf_op jit(solution)/shard_map/ppermute | solution.py:69
  39.3 1.5 %collective-permute-start.14 = (bf16[128,512]{1,0:T(8,128)(2,1)S(1)}, bf16[128,512]{1,0:T(8,128)(2,1)S(1)}, u32[]{:S(2)}, u32[]{:S(2)}) collective-permute-start(bf16[128,512]{1,0:T(8,128)(2,1)S(1)} %get-tuple-element.55), channel_id=1, source_target_pairs={{0,4},{2,6},{4,0},{6,2},{1,5},{3,7},{5,1},{7,3},{8,12},{10,14},{12... | collective-permute-start | bytes 393224 | tf_op jit(solution)/shard_map/ppermute | solution.py:69
  41.0 0.9 %collective-permute-done.18.refs_2_ = bf16[64,512]{1,0:T(8,128)(2,1)S(1)} collective-permute-done((bf16[64,512]{1,0:T(8,128)(2,1)S(1)}, bf16[64,512]{1,0:T(8,128)(2,1)S(1)}, u32[]{:S(2)}, u32[]{:S(2)}) %collective-permute-start.18) | collective-permute-done | bytes 65568 | tf_op jit(solution)/shard_map/ppermute | solution.py:69
  42.0 1.1 %collective-permute-done.19.refs_3_ = bf16[64,512]{1,0:T(8,128)(2,1)S(1)} collective-permute-done((bf16[64,512]{1,0:T(8,128)(2,1)S(1)}, bf16[64,512]{1,0:T(8,128)(2,1)S(1)}, u32[]{:S(2)}, u32[]{:S(2)}) %collective-permute-start.19) | collective-permute-done | bytes 65568 | tf_op jit(solution)/shard_map/ppermute | solution.py:69
  43.1 1.6 %shard_map.146 = (bf16[2,64,512]{2,1,0:T(8,128)(2,1)S(1)}, bf16[2,64,512]{2,1,0:T(8,128)(2,1)S(1)}, bf16[2,64,512]{2,1,0:T(8,128)(2,1)S(1)}, f32[2,64,512]{2,1,0:T(8,128)S(1)}) custom-call(s32[1]{0:T(128)} %bitcast.own_ref, s32[4]{0:T(128)S(1)} %pad_add_fusion.3.part_ref, bf16[512,512]{1,0:T(8,128)(2,1)S(1)} %bitcast.26, bf16[512,512]{1,0:T(8,128)(2,1)S(1)} %bitcast.28, ...), custom_call_target="tpu_custom_call" | custom-call | tf_op jit(solution)/shard_map/pallas_call | solution.py:525
  44.7 9.7 %collective-permute-start.20 = (bf16[2,64,512]{2,1,0:T(8,128)(2,1)S(1)}, bf16[2,64,512]{2,1,0:T(8,128)(2,1)S(1)}, u32[]{:S(2)}, u32[]{:S(2)}) collective-permute-start(bf16[2,64,512]{2,1,0:T(8,128)(2,1)S(1)} %get-tuple-element.67), channel_id=1, source_target_pairs={{0,8},{8,0},{16,24},{24,16},{1,9},{9,1},{17,25},{25,17},{2,10},{10... | collective-permute-start | bytes 393224 | tf_op jit(solution)/shard_map/ppermute | solution.py:69
  54.5 3.4 %collective-permute-start.21 = (bf16[2,64,512]{2,1,0:T(8,128)(2,1)S(1)}, bf16[2,64,512]{2,1,0:T(8,128)(2,1)S(1)}, u32[]{:S(2)}, u32[]{:S(2)}) collective-permute-start(bf16[2,64,512]{2,1,0:T(8,128)(2,1)S(1)} %get-tuple-element.68), channel_id=1, source_target_pairs={{0,16},{8,24},{16,0},{24,8},{1,17},{9,25},{17,1},{25,9},{2,18},{10... | collective-permute-start | bytes 393224 | tf_op jit(solution)/shard_map/ppermute | solution.py:69
  57.9 1.4 %collective-permute-start.22 = (bf16[2,64,512]{2,1,0:T(8,128)(2,1)S(1)}, bf16[2,64,512]{2,1,0:T(8,128)(2,1)S(1)}, u32[]{:S(2)}, u32[]{:S(2)}) collective-permute-start(bf16[2,64,512]{2,1,0:T(8,128)(2,1)S(1)} %get-tuple-element.69), channel_id=1, source_target_pairs={{0,24},{8,16},{16,8},{24,0},{1,25},{9,17},{17,9},{25,1},{2,26},{10... | collective-permute-start | bytes 393224 | tf_op jit(solution)/shard_map/ppermute | solution.py:69
  59.3 1.4 %shard_map.144 = (bf16[128,512]{1,0:T(8,128)(2,1)}, bf16[128,512]{1,0:T(8,128)(2,1)}) custom-call(s32[1]{0:T(128)} %bitcast.own_ref, s32[1,128]{1,0:T(1,128)S(1)} %bitcast.44, bf16[4,512]{1,0:T(4,128)(2,1)S(1)} %bitcast.40, bf16[128,512]{1,0:T(8,128)(2,1)S(1)} %get-tuple-element.44.mixed_ref, bf16[128,512]{1,0:T(8,128)(2,1)S(1)} %bitcast.34, ...), custom_call_target="tpu_custom_call" | custom-call | tf_op jit(solution)/shard_map/pallas_call | solution.py:556
  60.7 1.5 %collective-permute-done.21.refs_1_ = bf16[2,64,512]{2,1,0:T(8,128)(2,1)S(1)} collective-permute-done((bf16[2,64,512]{2,1,0:T(8,128)(2,1)S(1)}, bf16[2,64,512]{2,1,0:T(8,128)(2,1)S(1)}, u32[]{:S(2)}, u32[]{:S(2)}) %collective-permute-start.21) | collective-permute-done | bytes 131104 | tf_op jit(solution)/shard_map/ppermute | solution.py:69
  62.2 6.6 %collective-permute-done.22.refs_2_ = bf16[2,64,512]{2,1,0:T(8,128)(2,1)S(1)} collective-permute-done((bf16[2,64,512]{2,1,0:T(8,128)(2,1)S(1)}, bf16[2,64,512]{2,1,0:T(8,128)(2,1)S(1)}, u32[]{:S(2)}, u32[]{:S(2)}) %collective-permute-start.22) | collective-permute-done | bytes 131104 | tf_op jit(solution)/shard_map/ppermute | solution.py:69
  68.9 0.7 %shard_map.147 = (f32[64,512]{1,0:T(8,128)}, f32[64,512]{1,0:T(8,128)}) custom-call(f32[2,64,512]{2,1,0:T(8,128)S(1)} %get-tuple-element.66.kept_ref, bf16[2,64,512]{2,1,0:T(8,128)(2,1)S(1)} %collective-permute-done.20.refs_0_, bf16[2,64,512]{2,1,0:T(8,128)(2,1)S(1)} %collective-permute-done.21.refs_1_, bf16[2,64,512]{2,1,0:T(8,128)(2,1)S(1)} %collective-permute-done.22.refs_2_), custom_call_target="tpu_custom_call" | custom-call | tf_op jit(solution)/shard_map/pallas_call | solution.py:561
  (50 shorter events, 4.6 us)
Async XLA Ops:
  0.6 0.9 %copy-start.6 = (bf16[1,128,512]{2,1,0:T(8,128)(2,1)S(1)}, bf16[1,128,512]{2,1,0:T(8,128)(2,1)}, u32[]{:S(2)}) copy-start(bf16[1,128,512]{2,1,0:T(8,128)(2,1)} %param.12) | copy-start | bytes 393220
  1.5 0.9 %copy-start.7 = (bf16[1,128,512]{2,1,0:T(8,128)(2,1)S(1)}, bf16[1,128,512]{2,1,0:T(8,128)(2,1)}, u32[]{:S(2)}) copy-start(bf16[1,128,512]{2,1,0:T(8,128)(2,1)} %param.13) | copy-start | bytes 393220
  2.4 11.5 %copy-start.4 = (bf16[1,128,512]{2,1,0:T(8,128)(2,1)S(1)}, bf16[1,128,512]{2,1,0:T(8,128)(2,1)}, u32[]{:S(2)}) copy-start(bf16[1,128,512]{2,1,0:T(8,128)(2,1)} %param.21) | copy-start | bytes 393220
  2.8 10.5 %collective-permute-start = (bf16[256,512]{1,0:T(8,128)(2,1)S(1)}, bf16[256,512]{1,0:T(8,128)(2,1)S(1)}, u32[]{:S(2)}, u32[]{:S(2)}) collective-permute-start(bf16[256,512]{1,0:T(8,128)(2,1)S(1)} %shard_map.138.refs_0_), channel_id=1, source_target_pairs={{0,8},{1,9},{8,16},{9,17},{16,24},{17,25},{2,10},{3,11},{10,18},{1... | collective-permute-start | bytes 786440 | tf_op jit(solution)/shard_map/ppermute | solution.py:443
  7.7 12.9 %collective-permute-start.4 = (bf16[256,512]{1,0:T(8,128)(2,1)S(1)}, bf16[256,512]{1,0:T(8,128)(2,1)S(1)}, u32[]{:S(2)}, u32[]{:S(2)}) collective-permute-start(bf16[256,512]{1,0:T(8,128)(2,1)S(1)} %shard_map.138.refs_0_), channel_id=1, source_target_pairs={{0,1},{8,9},{16,17},{24,25},{2,3},{10,11},{18,19},{26,27},{4,5},{1... | collective-permute-start | bytes 786440 | tf_op jit(solution)/shard_map/ppermute | solution.py:443
  13.3 9.1 %collective-permute-start.1 = (bf16[256,512]{1,0:T(8,128)(2,1)S(1)}, bf16[256,512]{1,0:T(8,128)(2,1)S(1)}, u32[]{:S(2)}, u32[]{:S(2)}) collective-permute-start(bf16[256,512]{1,0:T(8,128)(2,1)S(1)} %collective-permute-done.refs_0_), channel_id=1, source_target_pairs={{8,16},{9,17},{16,24},{17,25},{10,18},{11,19},{18,26},{19,27},{12,... | collective-permute-start | bytes 786440 | tf_op jit(solution)/shard_map/ppermute | solution.py:443
  13.9 1.6 %copy-start.10 = (s32[1,128,1]{1,2,0:T(1,128)S(1)}, s32[1,128,1]{1,2,0:T(1,128)}, u32[]{:S(2)}) copy-start(s32[1,128,1]{1,2,0:T(1,128)} %param.18) | copy-start | bytes 1540
  14.0 6.1 %collective-permute-start.9 = (bf16[128,512]{1,0:T(8,128)(2,1)S(1)}, bf16[128,512]{1,0:T(8,128)(2,1)S(1)}, u32[]{:S(2)}, u32[]{:S(2)}) collective-permute-start(bf16[128,512]{1,0:T(8,128)(2,1)S(1)} %bitcast.32), channel_id=1, source_target_pairs={{0,1},{1,0},{2,3},{3,2},{4,5},{5,4},{6,7},{7,6},{8,9},{9,8},{10,11... | collective-permute-start | bytes 393224 | tf_op jit(solution)/shard_map/ppermute | solution.py:69
  15.5 3.7 %collective-permute-start.8 = (s32[1,128]{1,0:T(1,128)S(1)}, s32[1,128]{1,0:T(1,128)S(1)}, u32[]{:S(2)}, u32[]{:S(2)}) collective-permute-start(s32[1,128]{1,0:T(1,128)S(1)} %bitcast.41), channel_id=1, source_target_pairs={{0,1},{1,0},{2,3},{3,2},{4,5},{5,4},{6,7},{7,6},{8,9},{9,8},{10,11... | collective-permute-start | bytes 1544 | tf_op jit(solution)/shard_map/ppermute | solution.py:481
  16.1 9.7 %collective-permute-start.2 = (bf16[256,512]{1,0:T(8,128)(2,1)S(1)}, bf16[256,512]{1,0:T(8,128)(2,1)S(1)}, u32[]{:S(2)}, u32[]{:S(2)}) collective-permute-start(bf16[256,512]{1,0:T(8,128)(2,1)S(1)} %collective-permute-done.refs_0_), channel_id=1, source_target_pairs={{8,9},{9,8},{16,17},{17,16},{24,25},{25,24},{10,11},{11,10},{18,19... | collective-permute-start | bytes 786440 | tf_op jit(solution)/shard_map/ppermute | solution.py:443
  19.3 6.6 %collective-permute-start.3 = (bf16[256,512]{1,0:T(8,128)(2,1)S(1)}, bf16[256,512]{1,0:T(8,128)(2,1)S(1)}, u32[]{:S(2)}, u32[]{:S(2)}) collective-permute-start(bf16[256,512]{1,0:T(8,128)(2,1)S(1)} %collective-permute-done.refs_0_), channel_id=1, source_target_pairs={{9,16},{17,24},{11,18},{19,26},{13,20},{21,28},{15,22},{23,30}} | collective-permute-start | bytes 786440 | tf_op jit(solution)/shard_map/ppermute | solution.py:443
  20.0 2.7 %copy-start.2 = (bf16[1,128,512]{2,1,0:T(8,128)(2,1)S(1)}, bf16[1,128,512]{2,1,0:T(8,128)(2,1)}, u32[]{:S(2)}) copy-start(bf16[1,128,512]{2,1,0:T(8,128)(2,1)} %param.11) | copy-start | bytes 393220
  20.6 8.8 %collective-permute-start.10 = (bf16[128,512]{1,0:T(8,128)(2,1)S(1)}, bf16[128,512]{1,0:T(8,128)(2,1)S(1)}, u32[]{:S(2)}, u32[]{:S(2)}) collective-permute-start(bf16[128,512]{1,0:T(8,128)(2,1)S(1)} %get-tuple-element.50), channel_id=1, source_target_pairs={{0,2},{2,0},{4,6},{6,4},{1,3},{3,1},{5,7},{7,5},{8,10},{10,8},{12,... | collective-permute-start | bytes 393224 | tf_op jit(solution)/shard_map/ppermute | solution.py:69
  20.7 8.7 %collective-permute-start.11 = (bf16[128,512]{1,0:T(8,128)(2,1)S(1)}, bf16[128,512]{1,0:T(8,128)(2,1)S(1)}, u32[]{:S(2)}, u32[]{:S(2)}) collective-permute-start(bf16[128,512]{1,0:T(8,128)(2,1)S(1)} %get-tuple-element.51), channel_id=1, source_target_pairs={{0,4},{2,6},{4,0},{6,2},{1,5},{3,7},{5,1},{7,3},{8,12},{10,14},{12... | collective-permute-start | bytes 393224 | tf_op jit(solution)/shard_map/ppermute | solution.py:69
  22.3 10.6 %collective-permute-start.12 = (bf16[128,512]{1,0:T(8,128)(2,1)S(1)}, bf16[128,512]{1,0:T(8,128)(2,1)S(1)}, u32[]{:S(2)}, u32[]{:S(2)}) collective-permute-start(bf16[128,512]{1,0:T(8,128)(2,1)S(1)} %get-tuple-element.52), channel_id=1, source_target_pairs={{0,6},{2,4},{4,2},{6,0},{1,7},{3,5},{5,3},{7,1},{8,14},{10,12},{12... | collective-permute-start | bytes 393224 | tf_op jit(solution)/shard_map/ppermute | solution.py:69
  25.1 1.0 %copy-start.3 = (bf16[512,512]{1,0:T(8,128)(2,1)S(1)}, bf16[512,512]{1,0:T(8,128)(2,1)}, u32[]{:S(2)}) copy-start(bf16[512,512]{1,0:T(8,128)(2,1)} %proj_ref.1) | copy-start | bytes 1572868
  25.1 1.1 %copy-start.5 = (bf16[1,128,512]{2,1,0:T(8,128)(2,1)S(1)}, bf16[1,128,512]{2,1,0:T(8,128)(2,1)}, u32[]{:S(2)}) copy-start(bf16[1,128,512]{2,1,0:T(8,128)(2,1)} %param.15) | copy-start | bytes 393220
  26.2 7.6 %copy-start = (bf16[1,512,512]{2,1,0:T(8,128)(2,1)S(1)}, bf16[1,512,512]{2,1,0:T(8,128)(2,1)}, u32[]{:S(2)}) copy-start(bf16[1,512,512]{2,1,0:T(8,128)(2,1)} %param.19) | copy-start | bytes 1572868
  26.2 7.6 %copy-start.1 = (bf16[1,512,512]{2,1,0:T(8,128)(2,1)S(1)}, bf16[1,512,512]{2,1,0:T(8,128)(2,1)}, u32[]{:S(2)}) copy-start(bf16[1,512,512]{2,1,0:T(8,128)(2,1)} %param.20) | copy-start | bytes 1572868
  27.4 5.5 %collective-permute-start.5 = (bf16[64,512]{1,0:T(8,128)(2,1)S(1)}, bf16[64,512]{1,0:T(8,128)(2,1)S(1)}, u32[]{:S(2)}, u32[]{:S(2)}) collective-permute-start(bf16[64,512]{1,0:T(8,128)(2,1)S(1)} %get-tuple-element.46), channel_id=1, source_target_pairs={{0,2},{2,0},{4,6},{6,4},{1,3},{3,1},{5,7},{7,5},{8,10},{10,8},{12,... | collective-permute-start | bytes 196616 | tf_op jit(solution)/shard_map/ppermute | solution.py:69
  27.9 5.1 %collective-permute-start.6 = (bf16[64,512]{1,0:T(8,128)(2,1)S(1)}, bf16[64,512]{1,0:T(8,128)(2,1)S(1)}, u32[]{:S(2)}, u32[]{:S(2)}) collective-permute-start(bf16[64,512]{1,0:T(8,128)(2,1)S(1)} %get-tuple-element.47), channel_id=1, source_target_pairs={{0,4},{2,6},{4,0},{6,2},{1,5},{3,7},{5,1},{7,3},{8,12},{10,14},{12... | collective-permute-start | bytes 196616 | tf_op jit(solution)/shard_map/ppermute | solution.py:69
  29.4 4.4 %collective-permute-start.7 = (bf16[64,512]{1,0:T(8,128)(2,1)S(1)}, bf16[64,512]{1,0:T(8,128)(2,1)S(1)}, u32[]{:S(2)}, u32[]{:S(2)}) collective-permute-start(bf16[64,512]{1,0:T(8,128)(2,1)S(1)} %get-tuple-element.48), channel_id=1, source_target_pairs={{0,6},{2,4},{4,2},{6,0},{1,7},{3,5},{5,3},{7,1},{8,14},{10,12},{12... | collective-permute-start | bytes 196616 | tf_op jit(solution)/shard_map/ppermute | solution.py:69
  29.4 7.6 %collective-permute-start.16 = (bf16[128,512]{1,0:T(8,128)(2,1)S(1)}, bf16[128,512]{1,0:T(8,128)(2,1)S(1)}, u32[]{:S(2)}, u32[]{:S(2)}) collective-permute-start(bf16[128,512]{1,0:T(8,128)(2,1)S(1)} %get-tuple-element.59), channel_id=1, source_target_pairs={{0,1},{1,0},{2,3},{3,2},{4,5},{5,4},{6,7},{7,6},{8,9},{9,8},{10,11... | collective-permute-start | bytes 393224 | tf_op jit(solution)/shard_map/ppermute | solution.py:69
  36.3 21.6 %collective-permute-start.13 = (bf16[128,512]{1,0:T(8,128)(2,1)S(1)}, bf16[128,512]{1,0:T(8,128)(2,1)S(1)}, u32[]{:S(2)}, u32[]{:S(2)}) collective-permute-start(bf16[128,512]{1,0:T(8,128)(2,1)S(1)} %get-tuple-element.54), channel_id=1, source_target_pairs={{0,2},{2,0},{4,6},{6,4},{1,3},{3,1},{5,7},{7,5},{8,10},{10,8},{12,... | collective-permute-start | bytes 393224 | tf_op jit(solution)/shard_map/ppermute | solution.py:69
  37.4 3.5 %collective-permute-start.17 = (bf16[64,512]{1,0:T(8,128)(2,1)S(1)}, bf16[64,512]{1,0:T(8,128)(2,1)S(1)}, u32[]{:S(2)}, u32[]{:S(2)}) collective-permute-start(bf16[64,512]{1,0:T(8,128)(2,1)S(1)} %get-tuple-element.61), channel_id=1, source_target_pairs={{0,2},{2,0},{4,6},{6,4},{1,3},{3,1},{5,7},{7,5},{8,10},{10,8},{12,... | collective-permute-start | bytes 196616 | tf_op jit(solution)/shard_map/ppermute | solution.py:69
  37.5 4.5 %collective-permute-start.18 = (bf16[64,512]{1,0:T(8,128)(2,1)S(1)}, bf16[64,512]{1,0:T(8,128)(2,1)S(1)}, u32[]{:S(2)}, u32[]{:S(2)}) collective-permute-start(bf16[64,512]{1,0:T(8,128)(2,1)S(1)} %get-tuple-element.62), channel_id=1, source_target_pairs={{0,4},{2,6},{4,0},{6,2},{1,5},{3,7},{5,1},{7,3},{8,12},{10,14},{12... | collective-permute-start | bytes 196616 | tf_op jit(solution)/shard_map/ppermute | solution.py:69
  39.1 4.0 %collective-permute-start.19 = (bf16[64,512]{1,0:T(8,128)(2,1)S(1)}, bf16[64,512]{1,0:T(8,128)(2,1)S(1)}, u32[]{:S(2)}, u32[]{:S(2)}) collective-permute-start(bf16[64,512]{1,0:T(8,128)(2,1)S(1)} %get-tuple-element.63), channel_id=1, source_target_pairs={{0,6},{2,4},{4,2},{6,0},{1,7},{3,5},{5,3},{7,1},{8,14},{10,12},{12... | collective-permute-start | bytes 196616 | tf_op jit(solution)/shard_map/ppermute | solution.py:69
  39.3 20.0 %collective-permute-start.14 = (bf16[128,512]{1,0:T(8,128)(2,1)S(1)}, bf16[128,512]{1,0:T(8,128)(2,1)S(1)}, u32[]{:S(2)}, u32[]{:S(2)}) collective-permute-start(bf16[128,512]{1,0:T(8,128)(2,1)S(1)} %get-tuple-element.55), channel_id=1, source_target_pairs={{0,4},{2,6},{4,0},{6,2},{1,5},{3,7},{5,1},{7,3},{8,12},{10,14},{12... | collective-permute-start | bytes 393224 | tf_op jit(solution)/shard_map/ppermute | solution.py:69
  40.9 18.4 %collective-permute-start.15 = (bf16[128,512]{1,0:T(8,128)(2,1)S(1)}, bf16[128,512]{1,0:T(8,128)(2,1)S(1)}, u32[]{:S(2)}, u32[]{:S(2)}) collective-permute-start(bf16[128,512]{1,0:T(8,128)(2,1)S(1)} %get-tuple-element.56), channel_id=1, source_target_pairs={{0,6},{2,4},{4,2},{6,0},{1,7},{3,5},{5,3},{7,1},{8,14},{10,12},{12... | collective-permute-start | bytes 393224 | tf_op jit(solution)/shard_map/ppermute | solution.py:69
  44.7 16.0 %collective-permute-start.20 = (bf16[2,64,512]{2,1,0:T(8,128)(2,1)S(1)}, bf16[2,64,512]{2,1,0:T(8,128)(2,1)S(1)}, u32[]{:S(2)}, u32[]{:S(2)}) collective-permute-start(bf16[2,64,512]{2,1,0:T(8,128)(2,1)S(1)} %get-tuple-element.67), channel_id=1, source_target_pairs={{0,8},{8,0},{16,24},{24,16},{1,9},{9,1},{17,25},{25,17},{2,10},{10... | collective-permute-start | bytes 393224 | tf_op jit(solution)/shard_map/ppermute | solution.py:69
  54.5 7.8 %collective-permute-start.21 = (bf16[2,64,512]{2,1,0:T(8,128)(2,1)S(1)}, bf16[2,64,512]{2,1,0:T(8,128)(2,1)S(1)}, u32[]{:S(2)}, u32[]{:S(2)}) collective-permute-start(bf16[2,64,512]{2,1,0:T(8,128)(2,1)S(1)} %get-tuple-element.68), channel_id=1, source_target_pairs={{0,16},{8,24},{16,0},{24,8},{1,17},{9,25},{17,1},{25,9},{2,18},{10... | collective-permute-start | bytes 393224 | tf_op jit(solution)/shard_map/ppermute | solution.py:69
  57.9 11.0 %collective-permute-start.22 = (bf16[2,64,512]{2,1,0:T(8,128)(2,1)S(1)}, bf16[2,64,512]{2,1,0:T(8,128)(2,1)S(1)}, u32[]{:S(2)}, u32[]{:S(2)}) collective-permute-start(bf16[2,64,512]{2,1,0:T(8,128)(2,1)S(1)} %get-tuple-element.69), channel_id=1, source_target_pairs={{0,24},{8,16},{16,8},{24,0},{1,25},{9,17},{17,9},{25,1},{2,26},{10... | collective-permute-start | bytes 393224 | tf_op jit(solution)/shard_map/ppermute | solution.py:69
  (2 other events, 1.3 us)

commit v4 on v3

--- a/solution.py
+++ b/solution.py
@@ -109,30 +109,81 @@
     return (rows == slots).astype(jnp.float32).astype(jnp.bfloat16)
 
 
-def stack_kernel(key_ref, value_ref, out_ref, sems):
-    tok = key_ref.shape[0]
+def stack_kernel(
+    rank_ref,
+    choice_ref,
+    lengths_ref,
+    router_ref,
+    key_ref,
+    value_ref,
+    grad_ref,
+    pair_ref,
+    extended_ref,
+    begin_ref,
+    chosen_ref,
+    held_router_ref,
+    held_lengths_ref,
+    sems,
+):
+    tok, width = key_ref.shape
+    targets = (
+        (choice_ref, chosen_ref),
+        (lengths_ref, held_lengths_ref),
+        (key_ref, pair_ref.at[pl.ds(0, tok), :]),
+        (value_ref, pair_ref.at[pl.ds(tok, tok), :]),
+        (grad_ref, extended_ref.at[pl.ds(0, tok), :]),
+        (router_ref, held_router_ref),
+    )
     copies = [
-        pltpu.make_async_copy(ref, out_ref.at[pl.ds(place * tok, tok), :], sems.at[place])
-        for place, ref in enumerate((key_ref, value_ref))
+        pltpu.make_async_copy(source, target, sems.at[place])
+        for place, (source, target) in enumerate(targets)
     ]
     for copy in copies:
         copy.start()
-    for copy in copies:
+    copies[0].wait()
+    chosen = jnp.broadcast_to(chosen_ref[...].astype(jnp.float32), (16, tok))
+    extended_ref[tok : tok + 16, 0:tok] = chosen.astype(jnp.bfloat16)
+    extended_ref[tok : tok + 16, tok:width] = jnp.zeros((16, width - tok), jnp.bfloat16)
+    copies[1].wait()
+    position = rank_ref[0] * tok + lax.broadcasted_iota(jnp.int32, (1, tok), 1)
+    begin = jnp.zeros((1, tok), jnp.int32)
+    bound = jnp.int32(0)
+    for doc in range(held_lengths_ref.shape[1] - 1):
+        bound = bound + held_lengths_ref[0, doc]
+        begin = jnp.maximum(begin, jnp.where(position >= bound, bound, 0))
+    begin_ref[...] = begin
+    copies[5].wait()
+    routed = held_router_ref[...].astype(jnp.float32)
+    spare = extended_ref.shape[0] - tok - 16 - routed.shape[0]
+    if spare:
+        routed = jnp.concatenate([routed, jnp.zeros((spare, width), jnp.float32)], axis=0)
+    extended_ref[tok + 16 :, :] = routed.astype(jnp.bfloat16)
+    for copy in copies[2:5]:
         copy.wait()
 
 
-def dispatch_kernel(reps, hot_capacity, own_ref, *refs):
-    choice_refs, row_refs, sent_refs = refs[:reps], refs[reps : 2 * reps], refs[2 * reps :]
+def chosen_of(extended_ref, tok):
+    return extended_ref[tok : tok + 16, 0:tok].astype(jnp.float32)[0:1].astype(jnp.int32)
+
+
+def router_of(extended_ref, tok, expert_count):
+    whole = extended_ref[tok + 16 :, :].astype(jnp.float32)
+    return whole[0:expert_count].astype(jnp.bfloat16)
+
+
+def dispatch_kernel(reps, tok, hot_capacity, own_ref, *refs):
+    extended_refs, row_refs, sent_refs = refs[:reps], refs[reps : 2 * reps], refs[2 * reps :]
     for rep in range(reps):
-        placed = slot_matrix(choice_refs[rep][...], own_ref[0], len(sent_refs), hot_capacity)
-        rows = dot(placed, row_refs[rep][...]).astype(jnp.bfloat16)
+        choice = chosen_of(extended_refs[rep], tok)
+        placed = slot_matrix(choice, own_ref[0], len(sent_refs), hot_capacity)
+        rows = dot(placed, row_refs[rep][0:tok, :]).astype(jnp.bfloat16)
         for k, sent_ref in enumerate(sent_refs):
             sent_ref[rep * hot_capacity : (rep + 1) * hot_capacity] = rows[
                 k * hot_capacity : (k + 1) * hot_capacity
             ]
 
 
-def attend_blocks(block_ref, lengths_ref, query_ref, pair_refs, state_refs, bias_ref, first):
+def attend_blocks(block_ref, begin_ref, query_ref, pair_refs, state_refs, bias_ref, first):
     top_ref, total_ref, sum_ref = state_refs
     tok, width = query_ref.shape
     lanes = 128
@@ -150,11 +201,8 @@
             )
         )
     position = block_ref[0] * tok + lax.broadcasted_iota(jnp.int32, (1, tok), 1)
-    begin = jnp.zeros((1, tok), jnp.int32)
-    bound = jnp.int32(0)
-    for doc in range(lengths_ref.shape[1] - 1):
-        bound = bound + lengths_ref[0, doc]
-        begin = jnp.maximum(begin, jnp.where(position >= bound, bound, 0))
+    begin = begin_ref[...]
+    lowest = jnp.min(begin)
 
     def fold(pair_ref, block, fresh):
         key_position = block * tok + lax.broadcasted_iota(jnp.int32, (tok, tok), 0)
@@ -195,38 +243,27 @@
             fold(pair_ref, block, True)
         else:
 
-            @pl.when(block >= 0)
+            @pl.when((block >= 0) & ((block + 1) * tok > lowest))
             def unused(pair_ref=pair_ref, block=block):
                 fold(pair_ref, block, False)
 
 
-def attend_kernel(count, first, block_ref, lengths_ref, query_ref, *refs):
+def attend_kernel(count, first, block_ref, begin_ref, query_ref, *refs):
     pair_refs, refs = refs[:count], refs[count:]
     if not first:
         for old_ref, new_ref in zip(refs[0:3], refs[3:6]):
             new_ref[...] = old_ref[...]
         refs = refs[3:]
-    attend_blocks(block_ref, lengths_ref, query_ref, pair_refs, refs[0:3], refs[3], first)
-
-
-def mix_kernel(
-    count,
-    hot_capacity,
-    block_ref,
-    own_ref,
-    lengths_ref,
-    query_ref,
-    choice_ref,
-    residual_ref,
-    proj_ref,
-    *refs,
-):
+    attend_blocks(block_ref, begin_ref, query_ref, pair_refs, refs[0:3], refs[3], first)
+
+
+def mix_kernel(count, block_ref, begin_ref, query_ref, residual_ref, proj_ref, *refs):
     pair_refs, refs = refs[:count], refs[count:]
     old_refs, mixed_ref, normed_ref = refs[0:3], refs[3], refs[4]
-    sent_refs, state_refs, bias_ref = refs[5:-4], refs[-4:-1], refs[-1]
+    state_refs, bias_ref = refs[-4:-1], refs[-1]
     for old_ref, new_ref in zip(old_refs, state_refs):
         new_ref[...] = old_ref[...]
-    attend_blocks(block_ref, lengths_ref, query_ref, pair_refs, state_refs, bias_ref, False)
+    attend_blocks(block_ref, begin_ref, query_ref, pair_refs, state_refs, bias_ref, False)
     unused_top, total_ref, sum_ref = state_refs
     pieces = [
         (sum_ref[head * HD : (head + 1) * HD, :] / total_ref[head : head + 1, :]).astype(
@@ -243,23 +280,20 @@
     inv_rms = lax.rsqrt(jnp.mean(mixed_f * mixed_f, axis=1, keepdims=True) + norm_eps)
     normed = (mixed_f * inv_rms).astype(jnp.bfloat16)
     normed_ref[...] = normed
-    placed = slot_matrix(choice_ref[...], own_ref[0], len(sent_refs), hot_capacity)
-    rows = dot(placed, normed).astype(jnp.bfloat16)
-    for k, sent_ref in enumerate(sent_refs):
-        sent_ref[...] = rows[k * hot_capacity : (k + 1) * hot_capacity]
 
 
 def expert_kernel(
     reps,
     rep_list,
     sources,
+    tok,
     strip,
     counts,
     own_ref,
     part_ref,
     up_ref,
     down_ref,
-    router_ref,
+    extended_ref,
     *refs,
 ):
     row_count, grad_count = counts
@@ -278,7 +312,7 @@
     parts = part_ref.shape[0]
     up = up_ref[...]
     down = down_ref[...]
-    router = router_ref[...]
+    router = router_of(extended_ref, tok, sources)
     expert_lane = lax.broadcasted_iota(jnp.int32, (count, router.shape[0]), 1) == own_ref[0]
 
     def strips(rows, place):
@@ -332,14 +366,13 @@
 
 
 def finish_kernel(
-    hot_capacity, own_ref, choice_ref, router_ref, mixed_ref, grad_ref, *refs
+    hot_capacity, expert_count, own_ref, mixed_ref, extended_ref, *refs
 ):
     back_refs, (layer_ref, grad_mixed_ref) = refs[:-2], refs[-2:]
-    expert_count = router_ref.shape[0]
     tok = mixed_ref.shape[0]
-    choice = choice_ref[...]
+    choice = chosen_of(extended_ref, tok)
     placed = slot_matrix(choice, own_ref[0], expert_count, hot_capacity)
-    router = router_ref[...]
+    router = router_of(extended_ref, tok, expert_count)
     mixed_f = mixed_ref[...].astype(jnp.float32)
     inv_rms = lax.rsqrt(jnp.mean(mixed_f * mixed_f, axis=1, keepdims=True) + norm_eps)
     normed = (mixed_f * inv_rms).astype(jnp.bfloat16)
@@ -356,7 +389,7 @@
     grads = jnp.concatenate([chunk[hot_capacity:] for chunk in chunks], axis=0)
     result_f = dot(placed, results, TN)
     normed_grad = dot(placed, grads, TN)
-    grad_f = grad_ref[...].astype(jnp.float32)
+    grad_f = extended_ref[0:tok, :].astype(jnp.float32)
     layer_ref[...] = (mixed_f + gate * result_f).astype(jnp.bfloat16)
     gate_grad = jnp.sum(grad_f * result_f, axis=1, keepdims=True)
     logit_grad = gate_grad * gate * (1.0 - gate)
@@ -385,9 +418,12 @@
 HBM = pl.BlockSpec(memory_space=pltpu.HBM)
 
 
-def call(body, out_shape, specs, scratch=()):
+def call(body, out_shape, specs, scratch=(), cost=0.5):
     return pl.pallas_call(
         body,
+        cost_estimate=pl.CostEstimate(
+            flops=int(cost * 1e9), bytes_accessed=0, transcendentals=0
+        ),
         out_shape=out_shape,
         in_specs=specs,
         out_specs=jax.tree.map(lambda unused: VMEM, out_shape),
@@ -422,7 +458,6 @@
     capacity = max(2, (3 * tok + 2 * expert_count - 1) // (2 * expert_count))
     hot_capacity = min(4 * capacity, tok // 2)
     choice = expert_choice.reshape(1, tok)
-    router_rows = router.T
     seq_index = lax.axis_index("seq")
     rep_index = lax.axis_index("rep")
     rank = seq_index * rep_count + rep_index
@@ -449,46 +484,6 @@
             ids.append(jnp.where(needed & (seq_index >= seq_back), block, -1))
         return jnp.stack(ids).astype(jnp.int32)
 
-    pair = call(
-        stack_kernel,
-        shape((2 * tok, width)),
-        [HBM, HBM],
-        [pltpu.SemaphoreType.DMA((2,))],
-    )(key_rows[0], value_rows[0])
-    always = rep_index >= 0
-    reach = (seq_count + 1) // 2
-    rounds = [([pair], [(0, rep_index, always)])]
-    line = pair
-    for step in range(1, reach + 1):
-        arrays, entries = [], []
-        ahead = send(line, step - 1, 1, 0, False)
-        arrays.append(ahead)
-        entries.append((step, rep_index, always))
-        for d in range(1, rep_count):
-            if step == 1:
-                arrays.append(send(line, 0, 0, d, False))
-                entries.append((0, rep_index - d, rep_index >= d))
-            else:
-                arrays.append(send(line, step - 1, 0, d, True))
-                entries.append((step - 1, (rep_index - d) % rep_count, always))
-            if step == reach:
-                arrays.append(send(line, step - 1, 1, -d, False))
-                entries.append((step, rep_index + d, rep_index + d < rep_count))
-        rounds.append((arrays, entries))
-        line = ahead
-
-    choices = [choice] + [
-        lax.ppermute(choice, "rep", [(i, reps.target(i, k)) for i in range(rep_count)])
-        for k in range(1, rep_count)
-    ]
-    grads = reps.exchange([grad_out[0]] * rep_count)
-    sent_grads = call(
-        functools.partial(dispatch_kernel, rep_count, hot_capacity),
-        [shape((rep_count * hot_capacity, width))] * expert_count,
-        [SMEM] + [VMEM] * (2 * rep_count),
-    )(own, *choices, *grads)
-    got_grads = merged(experts.exchange(sent_grads), MOST_PERMUTES)
-
     state_shapes = [
         shape((heads, tok), jnp.float32),
         shape((heads, tok), jnp.float32),
@@ -496,29 +491,100 @@
     ]
     bias = pltpu.VMEM((tok, tok), jnp.float32)
     query = query_rows[0]
+
+    def attend(blocks, state):
+        arrays, entries = blocks
+        return call(
+            functools.partial(attend_kernel, len(arrays), not state),
+            state_shapes,
+            [SMEM] + [VMEM] * (2 + len(arrays) + len(state)),
+            [bias],
+            cost=2.0,
+        )(block_ids(entries), begin, query, *arrays, *state)
+
+    pair, extended, begin = pl.pallas_call(
+        stack_kernel,
+        out_shape=[
+            shape((2 * tok, width)),
+            shape((tok + 16 + -(-expert_count // 16) * 16, width)),
+            shape((1, tok), jnp.int32),
+        ],
+        in_specs=[SMEM] + [HBM] * 6,
+        out_specs=[VMEM] * 3,
+        scratch_shapes=[
+            pltpu.VMEM((1, tok), jnp.int32),
+            pltpu.VMEM((expert_count, width), jnp.bfloat16),
+            pltpu.SMEM(doc_lengths.shape, jnp.int32),
+            pltpu.SemaphoreType.DMA((6,)),
+        ],
+        compiler_params=pltpu.CompilerParams(vmem_limit_bytes=60 * 1024 * 1024),
+    )(
+        jnp.stack([rank]).astype(jnp.int32),
+        choice,
+        doc_lengths,
+        router.T,
+        key_rows[0],
+        value_rows[0],
+        grad_out[0],
+    )
+    always = rep_index >= 0
+    reach = (seq_count + 1) // 2
+    rounds = [([pair], [(0, rep_index, always)])]
+    line = pair
+    extendeds = None
     state = ()
-    for place, (arrays, entries) in enumerate(rounds[:-1]):
-        state = call(
-            functools.partial(attend_kernel, len(arrays), place == 0),
-            state_shapes,
-            [SMEM, SMEM] + [VMEM] * (1 + len(arrays) + len(state)),
-            [bias],
-        )(block_ids(entries), doc_lengths, query, *arrays, *state)
+    for step in range(1, reach + 1):
+        ahead = send(line, step - 1, 1, 0, False)
+        arrays, entries = [ahead], [(step, rep_index, always)]
+        for d in range(1, rep_count):
+            if step == reach:
+                arrays.append(send(line, step - 1, 1, -d, False))
+                entries.append((step, rep_index + d, rep_index + d < rep_count))
+            if step == 1:
+                arrays.append(send(line, 0, 0, d, False))
+                entries.append((0, rep_index - d, rep_index >= d))
+            else:
+                arrays.append(send(line, step - 1, 0, d, True))
+                entries.append((step - 1, (rep_index - d) % rep_count, always))
+        if step == 1:
+            extendeds = reps.exchange([extended] * rep_count)
+        state = attend(rounds[-1], state)
+        rounds.append((arrays, entries))
+        if step < reach:
+            line, *held = lax.optimization_barrier((ahead, *state, *extendeds))
+            arrays[0], state, extendeds = line, held[:3], held[3:]
+
+    *state, pinned = lax.optimization_barrier((*state, extendeds[0]))
+    extendeds = [pinned] + list(extendeds[1:])
+    sent_grads = call(
+        functools.partial(dispatch_kernel, rep_count, tok, hot_capacity),
+        [shape((rep_count * hot_capacity, width))] * expert_count,
+        [SMEM] + [VMEM] * (2 * rep_count),
+    )(own, *extendeds, *extendeds)
+    got_grads = merged(experts.exchange(sent_grads), MOST_PERMUTES)
+
     arrays, entries = rounds[-1]
-    mixed, normed, *sent_rows = call(
-        functools.partial(mix_kernel, len(arrays), hot_capacity),
-        [shape((tok, width))] * 2 + [shape((hot_capacity, width))] * expert_count,
-        [SMEM, SMEM, SMEM] + [VMEM] * (7 + len(arrays)),
+    mixed, normed = call(
+        functools.partial(mix_kernel, len(arrays)),
+        [shape((tok, width))] * 2,
+        [SMEM] + [VMEM] * (7 + len(arrays)),
         [pltpu.VMEM(one.shape, one.dtype) for one in state_shapes] + [bias],
-    )(block_ids(entries), own, doc_lengths, query, choice, residual[0], out_proj, *arrays, *state)
+        cost=5.0,
+    )(block_ids(entries), begin, query, residual[0], out_proj, *arrays, *state)
+
+    normed, got_grads = lax.optimization_barrier((normed, got_grads))
+
+    def dispatch(own_arrays, rows):
+        return call(
+            functools.partial(dispatch_kernel, len(rows), tok, hot_capacity),
+            [shape((len(rows) * hot_capacity, width))] * expert_count,
+            [SMEM] + [VMEM] * (2 * len(rows)),
+        )(own, *own_arrays, *rows)
 
     others = reps.exchange([normed] * rep_count)[1:]
-    got_rows = merged(experts.exchange(sent_rows), MOST_PERMUTES)
-    more_rows = call(
-        functools.partial(dispatch_kernel, rep_count - 1, hot_capacity),
-        [shape(((rep_count - 1) * hot_capacity, width))] * expert_count,
-        [SMEM] + [VMEM] * (2 * (rep_count - 1)),
-    )(own, *choices[1:], *others)
+    got_rows = merged(experts.exchange(dispatch(extendeds[:1], [normed])), MOST_PERMUTES)
+    more_rows = dispatch(extendeds[1:], others)
+    more_rows, got_rows = lax.optimization_barrier((more_rows, got_rows))
     got_more = merged(experts.exchange(more_rows), MOST_PERMUTES)
 
     def expert_call(rep_list, rows, out_shape, extra):
@@ -528,13 +594,15 @@
                 rep_count,
                 rep_list,
                 expert_count,
+                tok,
                 strip,
                 (len(rows), len(got_grads)),
             ),
             out_shape,
             [SMEM, SMEM] + [VMEM] * (3 + len(rows) + len(got_grads) + len(extra)),
             [pltpu.VMEM((2 * len(rep_list), width, expert_count * hot_capacity), jnp.bfloat16)],
-        )(own, part_to, weight_in[0], weight_out[0], router_rows, *rows, *got_grads, *extra)
+            cost=2.0,
+        )(own, part_to, weight_in[0], weight_out[0], extendeds[0], *rows, *got_grads, *extra)
 
     *back, up_acc, down_acc = expert_call(
         (0,),
@@ -554,10 +622,11 @@
     )
     got_terms = parts.exchange([None] + terms)[1:]
     layer_out, grad_mixed = call(
-        functools.partial(finish_kernel, hot_capacity),
+        functools.partial(finish_kernel, hot_capacity, expert_count),
         [shape((tok, width)), shape((tok, width))],
-        [SMEM] + [VMEM] * (4 + len(got_back)),
-    )(own, choice, router_rows, mixed, grad_out[0], *got_back)
+        [SMEM] + [VMEM] * (2 + len(got_back)),
+        cost=1.5,
+    )(own, mixed, extended, *got_back)
     share_in, share_out = call(
         sum_kernel,
         [shape((strip, hidden), jnp.float32), shape((strip, width), jnp.float32)],

time: 70.4 us -> 70.2 us (level)
  starting transfers between devices: 38.2 us -> 31 us
  waiting for transfers between devices: 16.3 us -> 22.6 us
  Pallas kernels: 10.4 us -> 12.4 us
  local copies, waits for them, and re-layouts: 3.54 us -> 1.77 us
    ppermute x17, waiting for transfers between devices: 11.7 us -> 22.6 us  [exchange(): got[k] = lax.ppermute(chunks[k], self.axes, pairs)]
    ppermute x17, starting transfers between devices: 27.3 us -> 20.6 us  [exchange(): got[k] = lax.ppermute(chunks[k], self.axes, pairs)]
    ppermute x1 -> x0, waiting for transfers between devices: 2.49 us -> none  [local(): lax.ppermute(choice, 'rep', [(i, reps.target(i, k)) for i in range(rep_co...]
    ppermute x5, waiting for transfers between devices: 2.12 us -> 0.01 us  [send(): return lax.ppermute(array, ('seq', 'rep'), pairs)]
    pallas_call x7 -> x8, Pallas kernels: 6.24 us -> 8.19 us  [the longest x2 2.49 us: attend(): call(functools.partial(attend_kernel, len(arrays), not state), state_shap...]
    unnamed x22 -> x16, local copies, waits for them, and re-layouts: 3.54 us -> 1.77 us
  transfers between devices with their start and end apart: 23 -> 22, of which waited for: 8 -> 9; matrix products, arithmetic and copies ran while one was open for 0% -> 0% of each run, Pallas kernels for 13% -> 14%
where the time goes in v4:
time: 70.2 us; the launch traced here: 68.9 us
  starting transfers between devices  31 us (44%)
  waiting for transfers between devices  22.6 us (32%)
  Pallas kernels  12.4 us (18%)
  local copies, waits for them, and re-layouts  1.77 us (3%)
  between operations  0.88 us (1%)
    ppermute x17, waiting for transfers between devices, exchange(): got[k] = lax.ppermute(chunks[k], self.axes, pairs)  22.6 us
    ppermute x17, starting transfers between devices, exchange(): got[k] = lax.ppermute(chunks[k], self.axes, pairs)  20.6 us
    ppermute x5, starting transfers between devices, send(): return lax.ppermute(array, ('seq', 'rep'), pairs)  10.4 us
    pallas_call x2, Pallas kernels, expert_call(): call(functools.partial(expert_kernel, rep_count, rep_list, expert_count,...  3.47 us
    pallas_call x2, Pallas kernels, attend(): call(functools.partial(attend_kernel, len(arrays), not state), state_shap...  2.49 us
    pallas_call x1, Pallas kernels, local(): pl.pallas_call(stack_kernel, out_shape=[shape((2 * tok, width)), shape((t...  1.91 us
    unnamed x16, local copies, waits for them, and re-layouts  1.77 us
    pallas_call x1, Pallas kernels, local(): call(functools.partial(finish_kernel, hot_capacity, expert_count), [shape...  1.42 us
  transfers between devices with their start and end apart: 22, of which 9 were waited for; matrix products, arithmetic and copies ran while one was open for 0% of the time, Pallas kernels for 14%

profile of v4, /device:TPU:0, one launch (start us, length us, event | category | flops | bytes accessed | tf_op | source)
XLA Modules:
  0.0 68.9 jit_solution(8912701347835765534)
XLA Ops:
  0.7 1.9 %shard_map.138 = (bf16[256,512]{1,0:T(8,128)(2,1)}, bf16[160,512]{1,0:T(8,128)(2,1)}, s32[1,128]{1,0:T(1,128)}) custom-call(s32[1]{0:T(128)} %bitcast.1.rank_ref, s32[1,128]{1,0:T(1,128)} %bitcast.37, s32[1,8]{1,0:T(1,128)} %lengths_ref.1, bf16[4,512]{1,0:T(4,128)(2,1)} %bitcast.36, bf16[128,512]{1,0:T(8,128)(2,1)} %bitcast.33, bf16[128,512]{1,0:T(8,128)(2,1)} %bitcast.34, ...), custom_call_target="tpu_custom_call" | custom-call | tf_op jit(solution)/shard_map/pallas_call | solution.py:505
  2.6 4.9 %collective-permute-start = (bf16[256,512]{1,0:T(8,128)(2,1)}, bf16[256,512]{1,0:T(8,128)(2,1)S(1)}, u32[]{:S(2)}, u32[]{:S(2)}) collective-permute-start(bf16[256,512]{1,0:T(8,128)(2,1)} %get-tuple-element.65.refs_0_), channel_id=1, source_target_pairs={{0,8},{1,9},{8,16},{9,17},{16,24},{17,25},{2,10},{3,11},{10,18},{1... | collective-permute-start | bytes 786440 | tf_op jit(solution)/shard_map/ppermute | solution.py:478
  7.5 3.4 %collective-permute-start.5 = (bf16[256,512]{1,0:T(8,128)(2,1)}, bf16[256,512]{1,0:T(8,128)(2,1)S(1)}, u32[]{:S(2)}, u32[]{:S(2)}) collective-permute-start(bf16[256,512]{1,0:T(8,128)(2,1)} %get-tuple-element.65.refs_0_), channel_id=1, source_target_pairs={{0,1},{8,9},{16,17},{24,25},{2,3},{10,11},{18,19},{26,27},{4,5},{1... | collective-permute-start | bytes 786440 | tf_op jit(solution)/shard_map/ppermute | solution.py:478
  11.1 0.7 copy-done.7
  11.8 0.9 %copy-done.3 = bf16[256,512]{1,0:T(8,128)(2,1)S(1)} copy-done((bf16[256,512]{1,0:T(8,128)(2,1)S(1)}, bf16[256,512]{1,0:T(8,128)(2,1)}, u32[]{:S(2)}) %copy-start.3) | copy-done | bytes 262168
  12.7 1.7 %shard_map.139 = (f32[16,128]{1,0:T(8,128)S(1)}, f32[16,128]{1,0:T(8,128)S(1)}, f32[512,128]{1,0:T(8,128)S(1)}) custom-call(s32[2]{0:T(128)S(1)} %pad_add_fusion.1.block_ref, s32[1,128]{1,0:T(1,128)S(1)} %copy-done.7, bf16[128,512]{1,0:T(8,128)(2,1)S(1)} %bitcast.29, bf16[256,512]{1,0:T(8,128)(2,1)S(1)} %copy-done.3), custom_call_target="tpu_custom_call" | custom-call | flops 2000000000 | tf_op jit(solution)/shard_map/pallas_call | solution.py:497
  14.6 5.4 %collective-permute-done.1.refs_1_.refs_3_.refs_0_ = bf16[160,512]{1,0:T(8,128)(2,1)S(1)} collective-permute-done((bf16[160,512]{1,0:T(8,128)(2,1)}, bf16[160,512]{1,0:T(8,128)(2,1)S(1)}, u32[]{:S(2)}, u32[]{:S(2)}) %collective-permute-start.1) | collective-permute-done | bytes 163872 | tf_op jit(solution)/shard_map/ppermute | solution.py:69
  20.0 0.7 collective-permute-start.2
  20.7 0.7 collective-permute-start.3
  21.4 0.7 collective-permute-start.4
  22.2 0.8 %shard_map.140 = (f32[16,128]{1,0:T(8,128)S(1)}, f32[16,128]{1,0:T(8,128)S(1)}, f32[512,128]{1,0:T(8,128)S(1)}) custom-call(s32[3]{0:T(128)S(1)} %pad_add_fusion.2.block_ref, s32[1,128]{1,0:T(1,128)S(1)} %copy-done.7, bf16[128,512]{1,0:T(8,128)(2,1)S(1)} %bitcast.30, bf16[256,512]{1,0:T(8,128)(2,1)S(1)} %collective-permute-done.refs_0_, ...), custom_call_target="tpu_custom_call" | custom-call | flops 2000000000 | tf_op jit(solution)/shard_map/pallas_call | solution.py:497
  23.1 0.5 shard_map.142
  23.7 1.6 %collective-permute-start.7 = (bf16[128,512]{1,0:T(8,128)(2,1)S(1)}, bf16[128,512]{1,0:T(8,128)(2,1)S(1)}, u32[]{:S(2)}, u32[]{:S(2)}) collective-permute-start(bf16[128,512]{1,0:T(8,128)(2,1)S(1)} %get-tuple-element.87), channel_id=1, source_target_pairs={{0,4},{2,6},{4,0},{6,2},{1,5},{3,7},{5,1},{7,3},{8,12},{10,14},{12... | collective-permute-start | bytes 393224 | tf_op jit(solution)/shard_map/ppermute | solution.py:69
  25.6 1.1 %shard_map.141 = (bf16[128,512]{1,0:T(8,128)(2,1)S(1)}, bf16[128,512]{1,0:T(8,128)(2,1)S(1)}) custom-call(s32[4]{0:T(128)S(1)} %pad_add_fusion.block_ref, s32[1,128]{1,0:T(1,128)S(1)} %copy-done.7, bf16[128,512]{1,0:T(8,128)(2,1)S(1)} %bitcast.31, bf16[128,512]{1,0:T(8,128)(2,1)S(1)} %bitcast.32, bf16[512,512]{1,0:T(8,128)(2,1)S(1)} %copy-done, ...), custom_call_target="tpu_custom_call" | custom-call | flops 5000000000 | tf_op jit(solution)/shard_map/pallas_call | solution.py:567
  26.7 3.3 %collective-permute-done.7.refs_6_ = bf16[128,512]{1,0:T(8,128)(2,1)S(1)} collective-permute-done((bf16[128,512]{1,0:T(8,128)(2,1)S(1)}, bf16[128,512]{1,0:T(8,128)(2,1)S(1)}, u32[]{:S(2)}, u32[]{:S(2)}) %collective-permute-start.7) | collective-permute-done | bytes 131104 | tf_op jit(solution)/shard_map/ppermute | solution.py:69
  30.1 1.9 %collective-permute-done.8.refs_7_ = bf16[128,512]{1,0:T(8,128)(2,1)S(1)} collective-permute-done((bf16[128,512]{1,0:T(8,128)(2,1)S(1)}, bf16[128,512]{1,0:T(8,128)(2,1)S(1)}, u32[]{:S(2)}, u32[]{:S(2)}) %collective-permute-start.8) | collective-permute-done | bytes 131104 | tf_op jit(solution)/shard_map/ppermute | solution.py:69
  32.0 3.4 %collective-permute-start.9 = (bf16[128,512]{1,0:T(8,128)(2,1)S(1)}, bf16[128,512]{1,0:T(8,128)(2,1)S(1)}, u32[]{:S(2)}, u32[]{:S(2)}) collective-permute-start(bf16[128,512]{1,0:T(8,128)(2,1)S(1)} %get-tuple-element.89.refs_1_), channel_id=1, source_target_pairs={{0,1},{1,0},{2,3},{3,2},{4,5},{5,4},{6,7},{7,6},{8,9},{9,8},{10,11... | collective-permute-start | bytes 393224 | tf_op jit(solution)/shard_map/ppermute | solution.py:69
  35.8 1.6 %collective-permute-start.11 = (bf16[64,512]{1,0:T(8,128)(2,1)S(1)}, bf16[64,512]{1,0:T(8,128)(2,1)S(1)}, u32[]{:S(2)}, u32[]{:S(2)}) collective-permute-start(bf16[64,512]{1,0:T(8,128)(2,1)S(1)} %get-tuple-element.96), channel_id=1, source_target_pairs={{0,4},{2,6},{4,0},{6,2},{1,5},{3,7},{5,1},{7,3},{8,12},{10,14},{12... | collective-permute-start | bytes 196616 | tf_op jit(solution)/shard_map/ppermute | solution.py:69
  37.8 1.6 %collective-permute-done.9.refs_1_ = bf16[128,512]{1,0:T(8,128)(2,1)S(1)} collective-permute-done((bf16[128,512]{1,0:T(8,128)(2,1)S(1)}, bf16[128,512]{1,0:T(8,128)(2,1)S(1)}, u32[]{:S(2)}, u32[]{:S(2)}) %collective-permute-start.9) | collective-permute-done | bytes 131104 | tf_op jit(solution)/shard_map/ppermute | solution.py:69
  39.7 0.6 collective-permute-done.11.refs_2_
  40.3 1.1 %collective-permute-done.12.refs_3_ = bf16[64,512]{1,0:T(8,128)(2,1)S(1)} collective-permute-done((bf16[64,512]{1,0:T(8,128)(2,1)S(1)}, bf16[64,512]{1,0:T(8,128)(2,1)S(1)}, u32[]{:S(2)}, u32[]{:S(2)}) %collective-permute-start.12) | collective-permute-done | bytes 65568 | tf_op jit(solution)/shard_map/ppermute | solution.py:69
  41.6 1.5 %collective-permute-start.17 = (bf16[64,512]{1,0:T(8,128)(2,1)S(1)}, bf16[64,512]{1,0:T(8,128)(2,1)S(1)}, u32[]{:S(2)}, u32[]{:S(2)}) collective-permute-start(bf16[64,512]{1,0:T(8,128)(2,1)S(1)} %get-tuple-element.114), channel_id=1, source_target_pairs={{0,4},{2,6},{4,0},{6,2},{1,5},{3,7},{5,1},{7,3},{8,12},{10,14},{12... | collective-permute-start | bytes 196616 | tf_op jit(solution)/shard_map/ppermute | solution.py:69
  43.3 1.8 %shard_map.145 = (bf16[128,512]{1,0:T(8,128)(2,1)S(1)}, bf16[128,512]{1,0:T(8,128)(2,1)S(1)}, bf16[128,512]{1,0:T(8,128)(2,1)S(1)}, bf16[128,512]{1,0:T(8,128)(2...) custom-call(s32[1]{0:T(128)} %bitcast.own_ref, s32[4]{0:T(128)S(1)} %pad_add_fusion.3.part_ref, ...), custom_call_target="tpu_custom_call" | custom-call | flops 2000000000 | tf_op jit(solution)/shard_map/pallas_call | solution.py:591
  45.7 1.5 %collective-permute-start.14 = (bf16[128,512]{1,0:T(8,128)(2,1)S(1)}, bf16[128,512]{1,0:T(8,128)(2,1)S(1)}, u32[]{:S(2)}, u32[]{:S(2)}) collective-permute-start(bf16[128,512]{1,0:T(8,128)(2,1)S(1)} %get-tuple-element.108), channel_id=1, source_target_pairs={{0,4},{2,6},{4,0},{6,2},{1,5},{3,7},{5,1},{7,3},{8,12},{10,14},{12... | collective-permute-start | bytes 393224 | tf_op jit(solution)/shard_map/ppermute | solution.py:69
  47.3 1.6 %shard_map.147 = (bf16[2,64,512]{2,1,0:T(8,128)(2,1)S(1)}, bf16[2,64,512]{2,1,0:T(8,128)(2,1)S(1)}, bf16[2,64,512]{2,1,0:T(8,128)(2,1)S(1)}, f32[2,64,512]{2,1,0:T(8,128)S(1)}) custom-call(s32[1]{0:T(128)} %bitcast.own_ref, s32[4]{0:T(128)S(1)} %pad_add_fusion.3.part_ref, bf16[512,512]{1,0:T(8,128)(2,1)S(1)} %bitcast.26, bf16[512,512]{1,0:T(8,128)(2,1)S(1)} %bitcast.28, ...), custom_call_target="tpu_custom_call" | custom-call | flops 2000000000 | tf_op jit(solution)/shard_map/pallas_call | solution.py:591
  49.0 6.3 %collective-permute-start.19 = (bf16[2,64,512]{2,1,0:T(8,128)(2,1)S(1)}, bf16[2,64,512]{2,1,0:T(8,128)(2,1)S(1)}, u32[]{:S(2)}, u32[]{:S(2)}) collective-permute-start(bf16[2,64,512]{2,1,0:T(8,128)(2,1)S(1)} %get-tuple-element.119), channel_id=1, source_target_pairs={{0,8},{8,0},{16,24},{24,16},{1,9},{9,1},{17,25},{25,17},{2,10},{10... | collective-permute-start | bytes 393224 | tf_op jit(solution)/shard_map/ppermute | solution.py:69
  55.3 1.7 %collective-permute-start.20 = (bf16[2,64,512]{2,1,0:T(8,128)(2,1)S(1)}, bf16[2,64,512]{2,1,0:T(8,128)(2,1)S(1)}, u32[]{:S(2)}, u32[]{:S(2)}) collective-permute-start(bf16[2,64,512]{2,1,0:T(8,128)(2,1)S(1)} %get-tuple-element.120), channel_id=1, source_target_pairs={{0,16},{8,24},{16,0},{24,8},{1,17},{9,25},{17,1},{25,9},{2,18},{10... | collective-permute-start | bytes 393224 | tf_op jit(solution)/shard_map/ppermute | solution.py:69
  57.0 1.4 %collective-permute-start.21 = (bf16[2,64,512]{2,1,0:T(8,128)(2,1)S(1)}, bf16[2,64,512]{2,1,0:T(8,128)(2,1)S(1)}, u32[]{:S(2)}, u32[]{:S(2)}) collective-permute-start(bf16[2,64,512]{2,1,0:T(8,128)(2,1)S(1)} %get-tuple-element.121), channel_id=1, source_target_pairs={{0,24},{8,16},{16,8},{24,0},{1,25},{9,17},{17,9},{25,1},{2,26},{10... | collective-permute-start | bytes 393224 | tf_op jit(solution)/shard_map/ppermute | solution.py:69
  58.4 1.4 %shard_map.146 = (bf16[128,512]{1,0:T(8,128)(2,1)}, bf16[128,512]{1,0:T(8,128)(2,1)}) custom-call(s32[1]{0:T(128)} %bitcast.own_ref, bf16[128,512]{1,0:T(8,128)(2,1)S(1)} %get-tuple-element.81.mixed_ref, bf16[160,512]{1,0:T(8,128)(2,1)S(1)} %copy-done.4, bf16[128,512]{1,0:T(8,128)(2,1)S(1)} %get-tuple-element.106.refs_0_, ...), custom_call_target="tpu_custom_call" | custom-call | flops 1500000000 | tf_op jit(solution)/shard_map/pallas_call | solution.py:624
  59.8 2.1 %collective-permute-done.19.refs_0_ = bf16[2,64,512]{2,1,0:T(8,128)(2,1)S(1)} collective-permute-done((bf16[2,64,512]{2,1,0:T(8,128)(2,1)S(1)}, bf16[2,64,512]{2,1,0:T(8,128)(2,1)S(1)}, u32[]{:S(2)}, u32[]{:S(2)}) %collective-permute-start.19) | collective-permute-done | bytes 131104 | tf_op jit(solution)/shard_map/ppermute | solution.py:69
  61.9 6.3 %collective-permute-done.20.refs_1_ = bf16[2,64,512]{2,1,0:T(8,128)(2,1)S(1)} collective-permute-done((bf16[2,64,512]{2,1,0:T(8,128)(2,1)S(1)}, bf16[2,64,512]{2,1,0:T(8,128)(2,1)S(1)}, u32[]{:S(2)}, u32[]{:S(2)}) %collective-permute-start.20) | collective-permute-done | bytes 131104 | tf_op jit(solution)/shard_map/ppermute | solution.py:69
  68.2 0.7 %shard_map.148 = (f32[64,512]{1,0:T(8,128)}, f32[64,512]{1,0:T(8,128)}) custom-call(f32[2,64,512]{2,1,0:T(8,128)S(1)} %get-tuple-element.118.kept_ref, bf16[2,64,512]{2,1,0:T(8,128)(2,1)S(1)} %collective-permute-done.19.refs_0_, bf16[2,64,512]{2,1,0:T(8,128)(2,1)S(1)} %collective-permute-done.20.refs_1_, bf16[2,64,512]{2,1,0:T(8,128)(2,1)S(1)} %collective-permute-done.21.refs_2_), custom_call_target="tpu_custom_call" | custom-call | flops 500000000 | tf_op jit(solution)/shard_map/pallas_call | solution.py:630
  (43 shorter events, 3.1 us)
Async XLA Ops:
  0.6 10.5 %copy-start.5 = (bf16[1,128,512]{2,1,0:T(8,128)(2,1)S(1)}, bf16[1,128,512]{2,1,0:T(8,128)(2,1)}, u32[]{:S(2)}) copy-start(bf16[1,128,512]{2,1,0:T(8,128)(2,1)} %param.11) | copy-start | bytes 393220
  2.6 17.4 %collective-permute-start = (bf16[256,512]{1,0:T(8,128)(2,1)}, bf16[256,512]{1,0:T(8,128)(2,1)S(1)}, u32[]{:S(2)}, u32[]{:S(2)}) collective-permute-start(bf16[256,512]{1,0:T(8,128)(2,1)} %get-tuple-element.65.refs_0_), channel_id=1, source_target_pairs={{0,8},{1,9},{8,16},{9,17},{16,24},{17,25},{2,10},{3,11},{10,18},{1... | collective-permute-start | bytes 786440 | tf_op jit(solution)/shard_map/ppermute | solution.py:478
  7.5 14.6 %collective-permute-start.5 = (bf16[256,512]{1,0:T(8,128)(2,1)}, bf16[256,512]{1,0:T(8,128)(2,1)S(1)}, u32[]{:S(2)}, u32[]{:S(2)}) collective-permute-start(bf16[256,512]{1,0:T(8,128)(2,1)} %get-tuple-element.65.refs_0_), channel_id=1, source_target_pairs={{0,1},{8,9},{16,17},{24,25},{2,3},{10,11},{18,19},{26,27},{4,5},{1... | collective-permute-start | bytes 786440 | tf_op jit(solution)/shard_map/ppermute | solution.py:478
  10.9 9.1 %collective-permute-start.1 = (bf16[160,512]{1,0:T(8,128)(2,1)}, bf16[160,512]{1,0:T(8,128)(2,1)S(1)}, u32[]{:S(2)}, u32[]{:S(2)}) collective-permute-start(bf16[160,512]{1,0:T(8,128)(2,1)} %get-tuple-element.82.refs_0_.refs_2_.extended_ref), channel_id=1, source_target_pairs={{0,1},{1,0},{2,3},{3,2},{4,5},{5,4},{6,7},{7,6},{8,9},{9,8},{10,11... | collective-permute-start | bytes 491528 | tf_op jit(solution)/shard_map/ppermute | solution.py:69
  11.1 0.7 copy-start.7
  11.8 0.9 %copy-start.3 = (bf16[256,512]{1,0:T(8,128)(2,1)S(1)}, bf16[256,512]{1,0:T(8,128)(2,1)}, u32[]{:S(2)}) copy-start(bf16[256,512]{1,0:T(8,128)(2,1)} %get-tuple-element.65.refs_0_) | copy-start | bytes 786436
  20.0 5.3 %collective-permute-start.2 = (bf16[256,512]{1,0:T(8,128)(2,1)S(1)}, bf16[256,512]{1,0:T(8,128)(2,1)S(1)}, u32[]{:S(2)}, u32[]{:S(2)}) collective-permute-start(bf16[256,512]{1,0:T(8,128)(2,1)S(1)} %collective-permute-done.refs_0_), channel_id=1, source_target_pairs={{8,16},{9,17},{16,24},{17,25},{10,18},{11,19},{18,26},{19,27},{12,... | collective-permute-start | bytes 786440 | tf_op jit(solution)/shard_map/ppermute | solution.py:478
  20.7 4.9 %collective-permute-start.3 = (bf16[256,512]{1,0:T(8,128)(2,1)S(1)}, bf16[256,512]{1,0:T(8,128)(2,1)S(1)}, u32[]{:S(2)}, u32[]{:S(2)}) collective-permute-start(bf16[256,512]{1,0:T(8,128)(2,1)S(1)} %collective-permute-done.refs_0_), channel_id=1, source_target_pairs={{9,16},{17,24},{11,18},{19,26},{13,20},{21,28},{15,22},{23,30}} | collective-permute-start | bytes 786440 | tf_op jit(solution)/shard_map/ppermute | solution.py:478
  21.4 4.2 %collective-permute-start.4 = (bf16[256,512]{1,0:T(8,128)(2,1)S(1)}, bf16[256,512]{1,0:T(8,128)(2,1)S(1)}, u32[]{:S(2)}, u32[]{:S(2)}) collective-permute-start(bf16[256,512]{1,0:T(8,128)(2,1)S(1)} %collective-permute-done.refs_0_), channel_id=1, source_target_pairs={{8,9},{9,8},{16,17},{17,16},{24,25},{25,24},{10,11},{11,10},{18,19... | collective-permute-start | bytes 786440 | tf_op jit(solution)/shard_map/ppermute | solution.py:478
  22.1 0.9 %copy-start.4 = (bf16[160,512]{1,0:T(8,128)(2,1)S(1)}, bf16[160,512]{1,0:T(8,128)(2,1)}, u32[]{:S(2)}) copy-start(bf16[160,512]{1,0:T(8,128)(2,1)} %get-tuple-element.82.refs_0_.refs_2_.extended_ref) | copy-start | bytes 491524
  23.1 2.5 %copy-start = (bf16[512,512]{1,0:T(8,128)(2,1)S(1)}, bf16[512,512]{1,0:T(8,128)(2,1)}, u32[]{:S(2)}) copy-start(bf16[512,512]{1,0:T(8,128)(2,1)} %proj_ref.1) | copy-start | bytes 1572868
  23.1 2.5 %copy-start.6 = (bf16[1,128,512]{2,1,0:T(8,128)(2,1)S(1)}, bf16[1,128,512]{2,1,0:T(8,128)(2,1)}, u32[]{:S(2)}) copy-start(bf16[1,128,512]{2,1,0:T(8,128)(2,1)} %param.15) | copy-start | bytes 393220
  23.6 3.1 %collective-permute-start.6 = (bf16[128,512]{1,0:T(8,128)(2,1)S(1)}, bf16[128,512]{1,0:T(8,128)(2,1)S(1)}, u32[]{:S(2)}, u32[]{:S(2)}) collective-permute-start(bf16[128,512]{1,0:T(8,128)(2,1)S(1)} %get-tuple-element.86), channel_id=1, source_target_pairs={{0,2},{2,0},{4,6},{6,4},{1,3},{3,1},{5,7},{7,5},{8,10},{10,8},{12,... | collective-permute-start | bytes 393224 | tf_op jit(solution)/shard_map/ppermute | solution.py:69
  23.7 6.4 %collective-permute-start.7 = (bf16[128,512]{1,0:T(8,128)(2,1)S(1)}, bf16[128,512]{1,0:T(8,128)(2,1)S(1)}, u32[]{:S(2)}, u32[]{:S(2)}) collective-permute-start(bf16[128,512]{1,0:T(8,128)(2,1)S(1)} %get-tuple-element.87), channel_id=1, source_target_pairs={{0,4},{2,6},{4,0},{6,2},{1,5},{3,7},{5,1},{7,3},{8,12},{10,14},{12... | collective-permute-start | bytes 393224 | tf_op jit(solution)/shard_map/ppermute | solution.py:69
  25.3 6.7 %collective-permute-start.8 = (bf16[128,512]{1,0:T(8,128)(2,1)S(1)}, bf16[128,512]{1,0:T(8,128)(2,1)S(1)}, u32[]{:S(2)}, u32[]{:S(2)}) collective-permute-start(bf16[128,512]{1,0:T(8,128)(2,1)S(1)} %get-tuple-element.88), channel_id=1, source_target_pairs={{0,6},{2,4},{4,2},{6,0},{1,7},{3,5},{5,3},{7,1},{8,14},{10,12},{12... | collective-permute-start | bytes 393224 | tf_op jit(solution)/shard_map/ppermute | solution.py:69
  32.0 7.4 %collective-permute-start.9 = (bf16[128,512]{1,0:T(8,128)(2,1)S(1)}, bf16[128,512]{1,0:T(8,128)(2,1)S(1)}, u32[]{:S(2)}, u32[]{:S(2)}) collective-permute-start(bf16[128,512]{1,0:T(8,128)(2,1)S(1)} %get-tuple-element.89.refs_1_), channel_id=1, source_target_pairs={{0,1},{1,0},{2,3},{3,2},{4,5},{5,4},{6,7},{7,6},{8,9},{9,8},{10,11... | collective-permute-start | bytes 393224 | tf_op jit(solution)/shard_map/ppermute | solution.py:69
  35.8 3.9 %collective-permute-start.10 = (bf16[64,512]{1,0:T(8,128)(2,1)S(1)}, bf16[64,512]{1,0:T(8,128)(2,1)S(1)}, u32[]{:S(2)}, u32[]{:S(2)}) collective-permute-start(bf16[64,512]{1,0:T(8,128)(2,1)S(1)} %get-tuple-element.95), channel_id=1, source_target_pairs={{0,2},{2,0},{4,6},{6,4},{1,3},{3,1},{5,7},{7,5},{8,10},{10,8},{12,... | collective-permute-start | bytes 196616 | tf_op jit(solution)/shard_map/ppermute | solution.py:69
  35.8 4.5 %collective-permute-start.11 = (bf16[64,512]{1,0:T(8,128)(2,1)S(1)}, bf16[64,512]{1,0:T(8,128)(2,1)S(1)}, u32[]{:S(2)}, u32[]{:S(2)}) collective-permute-start(bf16[64,512]{1,0:T(8,128)(2,1)S(1)} %get-tuple-element.96), channel_id=1, source_target_pairs={{0,4},{2,6},{4,0},{6,2},{1,5},{3,7},{5,1},{7,3},{8,12},{10,14},{12... | collective-permute-start | bytes 196616 | tf_op jit(solution)/shard_map/ppermute | solution.py:69
  37.4 4.0 %collective-permute-start.12 = (bf16[64,512]{1,0:T(8,128)(2,1)S(1)}, bf16[64,512]{1,0:T(8,128)(2,1)S(1)}, u32[]{:S(2)}, u32[]{:S(2)}) collective-permute-start(bf16[64,512]{1,0:T(8,128)(2,1)S(1)} %get-tuple-element.97), channel_id=1, source_target_pairs={{0,6},{2,4},{4,2},{6,0},{1,7},{3,5},{5,3},{7,1},{8,14},{10,12},{12... | collective-permute-start | bytes 196616 | tf_op jit(solution)/shard_map/ppermute | solution.py:69
  37.8 5.6 %copy-start.1 = (bf16[1,512,512]{2,1,0:T(8,128)(2,1)S(1)}, bf16[1,512,512]{2,1,0:T(8,128)(2,1)}, u32[]{:S(2)}) copy-start(bf16[1,512,512]{2,1,0:T(8,128)(2,1)} %param.19) | copy-start | bytes 1572868
  37.8 5.6 %copy-start.2 = (bf16[1,512,512]{2,1,0:T(8,128)(2,1)S(1)}, bf16[1,512,512]{2,1,0:T(8,128)(2,1)}, u32[]{:S(2)}) copy-start(bf16[1,512,512]{2,1,0:T(8,128)(2,1)} %param.20) | copy-start | bytes 1572868
  41.5 5.7 %collective-permute-start.16 = (bf16[64,512]{1,0:T(8,128)(2,1)S(1)}, bf16[64,512]{1,0:T(8,128)(2,1)S(1)}, u32[]{:S(2)}, u32[]{:S(2)}) collective-permute-start(bf16[64,512]{1,0:T(8,128)(2,1)S(1)} %get-tuple-element.113), channel_id=1, source_target_pairs={{0,2},{2,0},{4,6},{6,4},{1,3},{3,1},{5,7},{7,5},{8,10},{10,8},{12,... | collective-permute-start | bytes 196616 | tf_op jit(solution)/shard_map/ppermute | solution.py:69
  41.6 5.5 %collective-permute-start.17 = (bf16[64,512]{1,0:T(8,128)(2,1)S(1)}, bf16[64,512]{1,0:T(8,128)(2,1)S(1)}, u32[]{:S(2)}, u32[]{:S(2)}) collective-permute-start(bf16[64,512]{1,0:T(8,128)(2,1)S(1)} %get-tuple-element.114), channel_id=1, source_target_pairs={{0,4},{2,6},{4,0},{6,2},{1,5},{3,7},{5,1},{7,3},{8,12},{10,14},{12... | collective-permute-start | bytes 196616 | tf_op jit(solution)/shard_map/ppermute | solution.py:69
  43.1 4.3 %collective-permute-start.18 = (bf16[64,512]{1,0:T(8,128)(2,1)S(1)}, bf16[64,512]{1,0:T(8,128)(2,1)S(1)}, u32[]{:S(2)}, u32[]{:S(2)}) collective-permute-start(bf16[64,512]{1,0:T(8,128)(2,1)S(1)} %get-tuple-element.115), channel_id=1, source_target_pairs={{0,6},{2,4},{4,2},{6,0},{1,7},{3,5},{5,3},{7,1},{8,14},{10,12},{12... | collective-permute-start | bytes 196616 | tf_op jit(solution)/shard_map/ppermute | solution.py:69
  45.2 11.8 %collective-permute-start.13 = (bf16[128,512]{1,0:T(8,128)(2,1)S(1)}, bf16[128,512]{1,0:T(8,128)(2,1)S(1)}, u32[]{:S(2)}, u32[]{:S(2)}) collective-permute-start(bf16[128,512]{1,0:T(8,128)(2,1)S(1)} %get-tuple-element.107), channel_id=1, source_target_pairs={{0,2},{2,0},{4,6},{6,4},{1,3},{3,1},{5,7},{7,5},{8,10},{10,8},{12,... | collective-permute-start | bytes 393224 | tf_op jit(solution)/shard_map/ppermute | solution.py:69
  45.7 12.7 %collective-permute-start.14 = (bf16[128,512]{1,0:T(8,128)(2,1)S(1)}, bf16[128,512]{1,0:T(8,128)(2,1)S(1)}, u32[]{:S(2)}, u32[]{:S(2)}) collective-permute-start(bf16[128,512]{1,0:T(8,128)(2,1)S(1)} %get-tuple-element.108), channel_id=1, source_target_pairs={{0,4},{2,6},{4,0},{6,2},{1,5},{3,7},{5,1},{7,3},{8,12},{10,14},{12... | collective-permute-start | bytes 393224 | tf_op jit(solution)/shard_map/ppermute | solution.py:69
  47.2 11.2 %collective-permute-start.15 = (bf16[128,512]{1,0:T(8,128)(2,1)S(1)}, bf16[128,512]{1,0:T(8,128)(2,1)S(1)}, u32[]{:S(2)}, u32[]{:S(2)}) collective-permute-start(bf16[128,512]{1,0:T(8,128)(2,1)S(1)} %get-tuple-element.109), channel_id=1, source_target_pairs={{0,6},{2,4},{4,2},{6,0},{1,7},{3,5},{5,3},{7,1},{8,14},{10,12},{12... | collective-permute-start | bytes 393224 | tf_op jit(solution)/shard_map/ppermute | solution.py:69
  49.0 12.9 %collective-permute-start.19 = (bf16[2,64,512]{2,1,0:T(8,128)(2,1)S(1)}, bf16[2,64,512]{2,1,0:T(8,128)(2,1)S(1)}, u32[]{:S(2)}, u32[]{:S(2)}) collective-permute-start(bf16[2,64,512]{2,1,0:T(8,128)(2,1)S(1)} %get-tuple-element.119), channel_id=1, source_target_pairs={{0,8},{8,0},{16,24},{24,16},{1,9},{9,1},{17,25},{25,17},{2,10},{10... | collective-permute-start | bytes 393224 | tf_op jit(solution)/shard_map/ppermute | solution.py:69
  55.3 12.9 %collective-permute-start.20 = (bf16[2,64,512]{2,1,0:T(8,128)(2,1)S(1)}, bf16[2,64,512]{2,1,0:T(8,128)(2,1)S(1)}, u32[]{:S(2)}, u32[]{:S(2)}) collective-permute-start(bf16[2,64,512]{2,1,0:T(8,128)(2,1)S(1)} %get-tuple-element.120), channel_id=1, source_target_pairs={{0,16},{8,24},{16,0},{24,8},{1,17},{9,25},{17,1},{25,9},{2,18},{10... | collective-permute-start | bytes 393224 | tf_op jit(solution)/shard_map/ppermute | solution.py:69
  57.0 11.2 %collective-permute-start.21 = (bf16[2,64,512]{2,1,0:T(8,128)(2,1)S(1)}, bf16[2,64,512]{2,1,0:T(8,128)(2,1)S(1)}, u32[]{:S(2)}, u32[]{:S(2)}) collective-permute-start(bf16[2,64,512]{2,1,0:T(8,128)(2,1)S(1)} %get-tuple-element.121), channel_id=1, source_target_pairs={{0,24},{8,16},{16,8},{24,0},{1,25},{9,17},{17,9},{25,1},{2,26},{10... | collective-permute-start | bytes 393224 | tf_op jit(solution)/shard_map/ppermute | solution.py:69

commit v5 on v4

--- a/solution.py
+++ b/solution.py
@@ -551,11 +551,11 @@
         state = attend(rounds[-1], state)
         rounds.append((arrays, entries))
         if step < reach:
-            line, *held = lax.optimization_barrier((ahead, *state, *extendeds))
-            arrays[0], state, extendeds = line, held[:3], held[3:]
-
-    *state, pinned = lax.optimization_barrier((*state, extendeds[0]))
-    extendeds = [pinned] + list(extendeds[1:])
+            line, *state = lax.optimization_barrier((ahead, *state))
+            arrays[0] = line
+
+    *held, pinned = lax.optimization_barrier((*state, extendeds[0]))
+    state, extendeds = held, [pinned] + list(extendeds[1:])
     sent_grads = call(
         functools.partial(dispatch_kernel, rep_count, tok, hot_capacity),
         [shape((rep_count * hot_capacity, width))] * expert_count,
@@ -627,11 +627,12 @@
         [SMEM] + [VMEM] * (2 + len(got_back)),
         cost=1.5,
     )(own, mixed, extended, *got_back)
+    kept, layer_out = lax.optimization_barrier((kept, layer_out))
     share_in, share_out = call(
         sum_kernel,
         [shape((strip, hidden), jnp.float32), shape((strip, width), jnp.float32)],
         [VMEM] * seq_count,
-    )(kept, *got_terms)
+    )(kept, *got_terms[::-1])
     return (layer_out[None], grad_mixed[None], share_in[None], share_out[None])
 
 

time: 70.2 us -> 65.5 us (0.933); the launches traced: 68.9 us -> 65.5 us
  waiting for transfers between devices: 22.6 us -> 20.9 us
  starting transfers between devices: 31 us -> 29.4 us
    ppermute x17, waiting for transfers between devices: 22.6 us -> 19.6 us  [exchange(): got[k] = lax.ppermute(chunks[k], self.axes, pairs)]
    ppermute x17, starting transfers between devices: 20.6 us -> 19 us  [exchange(): got[k] = lax.ppermute(chunks[k], self.axes, pairs)]
    ppermute x5, waiting for transfers between devices: 0.01 us -> 1.27 us  [send(): return lax.ppermute(array, ('seq', 'rep'), pairs)]
  transfers between devices with their start and end apart: 22 -> 22, of which waited for: 9 -> 10; matrix products, arithmetic and copies ran while one was open for 0% -> 0% of each run, Pallas kernels for 14% -> 15%
where the time goes in v5:
time: 65.5 us
  starting transfers between devices  29.4 us (45%)
  waiting for transfers between devices  20.9 us (32%)
  Pallas kernels  12.4 us (19%)
  local copies, waits for them, and re-layouts  1.62 us (2%)
  between operations  0.88 us (1%)
    ppermute x17, waiting for transfers between devices, exchange(): got[k] = lax.ppermute(chunks[k], self.axes, pairs)  19.6 us
    ppermute x17, starting transfers between devices, exchange(): got[k] = lax.ppermute(chunks[k], self.axes, pairs)  19 us
    ppermute x5, starting transfers between devices, send(): return lax.ppermute(array, ('seq', 'rep'), pairs)  10.4 us
    pallas_call x2, Pallas kernels, expert_call(): call(functools.partial(expert_kernel, rep_count, rep_list, expert_count,...  3.47 us
    pallas_call x2, Pallas kernels, attend(): call(functools.partial(attend_kernel, len(arrays), not state), state_shap...  2.49 us
    pallas_call x1, Pallas kernels, local(): pl.pallas_call(stack_kernel, out_shape=[shape((2 * tok, width)), shape((t...  1.91 us
    unnamed x16, local copies, waits for them, and re-layouts  1.62 us
    pallas_call x1, Pallas kernels, local(): call(functools.partial(finish_kernel, hot_capacity, expert_count), [shape...  1.42 us
  transfers between devices with their start and end apart: 22, of which 10 were waited for; matrix products, arithmetic and copies ran while one was open for 0% of the time, Pallas kernels for 15%

profile of v5, /device:TPU:0, one launch (start us, length us, event | category | flops | bytes accessed | tf_op | source)
XLA Modules:
  0.0 65.5 jit_solution(3560738087253990646)
XLA Ops:
  0.7 1.9 %shard_map.138 = (bf16[256,512]{1,0:T(8,128)(2,1)}, bf16[160,512]{1,0:T(8,128)(2,1)}, s32[1,128]{1,0:T(1,128)}) custom-call(s32[1]{0:T(128)} %bitcast.7.rank_ref, s32[1,128]{1,0:T(1,128)} %bitcast.37, s32[1,8]{1,0:T(1,128)} %lengths_ref.1, bf16[4,512]{1,0:T(4,128)(2,1)} %bitcast.36, bf16[128,512]{1,0:T(8,128)(2,1)} %bitcast.33, bf16[128,512]{1,0:T(8,128)(2,1)} %bitcast.34, ...), custom_call_target="tpu_custom_call" | custom-call | tf_op jit(solution)/shard_map/pallas_call | solution.py:505
  2.6 4.9 %collective-permute-start = (bf16[256,512]{1,0:T(8,128)(2,1)}, bf16[256,512]{1,0:T(8,128)(2,1)S(1)}, u32[]{:S(2)}, u32[]{:S(2)}) collective-permute-start(bf16[256,512]{1,0:T(8,128)(2,1)} %get-tuple-element.65.refs_0_), channel_id=1, source_target_pairs={{0,8},{1,9},{8,16},{9,17},{16,24},{17,25},{2,10},{3,11},{10,18},{1... | collective-permute-start | bytes 786440 | tf_op jit(solution)/shard_map/ppermute | solution.py:478
  7.5 3.4 %collective-permute-start.1 = (bf16[256,512]{1,0:T(8,128)(2,1)}, bf16[256,512]{1,0:T(8,128)(2,1)S(1)}, u32[]{:S(2)}, u32[]{:S(2)}) collective-permute-start(bf16[256,512]{1,0:T(8,128)(2,1)} %get-tuple-element.65.refs_0_), channel_id=1, source_target_pairs={{0,1},{8,9},{16,17},{24,25},{2,3},{10,11},{18,19},{26,27},{4,5},{1... | collective-permute-start | bytes 786440 | tf_op jit(solution)/shard_map/ppermute | solution.py:478
  11.1 0.7 copy-done.7
  11.8 0.9 %copy-done.3 = bf16[256,512]{1,0:T(8,128)(2,1)S(1)} copy-done((bf16[256,512]{1,0:T(8,128)(2,1)S(1)}, bf16[256,512]{1,0:T(8,128)(2,1)}, u32[]{:S(2)}) %copy-start.3) | copy-done | bytes 262168
  12.7 1.7 %shard_map.139 = (f32[16,128]{1,0:T(8,128)S(1)}, f32[16,128]{1,0:T(8,128)S(1)}, f32[512,128]{1,0:T(8,128)S(1)}) custom-call(s32[2]{0:T(128)S(1)} %pad_add_fusion.2.block_ref, s32[1,128]{1,0:T(1,128)S(1)} %copy-done.7, bf16[128,512]{1,0:T(8,128)(2,1)S(1)} %bitcast.29, bf16[256,512]{1,0:T(8,128)(2,1)S(1)} %copy-done.3), custom_call_target="tpu_custom_call" | custom-call | flops 2000000000 | tf_op jit(solution)/shard_map/pallas_call | solution.py:497
  14.6 0.7 %collective-permute-start.3 = (bf16[256,512]{1,0:T(8,128)(2,1)S(1)}, bf16[256,512]{1,0:T(8,128)(2,1)S(1)}, u32[]{:S(2)}, u32[]{:S(2)}) collective-permute-start(bf16[256,512]{1,0:T(8,128)(2,1)S(1)} %collective-permute-done.refs_0_), channel_id=1, source_target_pairs={{8,16},{9,17},{16,24},{17,25},{10,18},{11,19},{18,26},{19,27},{12,... | collective-permute-start | bytes 786440 | tf_op jit(solution)/shard_map/ppermute | solution.py:478
  15.3 0.7 %collective-permute-start.4 = (bf16[256,512]{1,0:T(8,128)(2,1)S(1)}, bf16[256,512]{1,0:T(8,128)(2,1)S(1)}, u32[]{:S(2)}, u32[]{:S(2)}) collective-permute-start(bf16[256,512]{1,0:T(8,128)(2,1)S(1)} %collective-permute-done.refs_0_), channel_id=1, source_target_pairs={{9,16},{17,24},{11,18},{19,26},{13,20},{21,28},{15,22},{23,30}} | collective-permute-start | bytes 786440 | tf_op jit(solution)/shard_map/ppermute | solution.py:478
  15.9 0.7 %collective-permute-start.5 = (bf16[256,512]{1,0:T(8,128)(2,1)S(1)}, bf16[256,512]{1,0:T(8,128)(2,1)S(1)}, u32[]{:S(2)}, u32[]{:S(2)}) collective-permute-start(bf16[256,512]{1,0:T(8,128)(2,1)S(1)} %collective-permute-done.refs_0_), channel_id=1, source_target_pairs={{8,9},{9,8},{16,17},{17,16},{24,25},{25,24},{10,11},{11,10},{18,19... | collective-permute-start | bytes 786440 | tf_op jit(solution)/shard_map/ppermute | solution.py:478
  16.7 1.3 %collective-permute-done.1.refs_1_ = bf16[256,512]{1,0:T(8,128)(2,1)S(1)} collective-permute-done((bf16[256,512]{1,0:T(8,128)(2,1)}, bf16[256,512]{1,0:T(8,128)(2,1)S(1)}, u32[]{:S(2)}, u32[]{:S(2)}) %collective-permute-start.1) | collective-permute-done | bytes 262176 | tf_op jit(solution)/shard_map/ppermute | solution.py:478
  18.0 0.8 %shard_map.140 = (f32[16,128]{1,0:T(8,128)S(1)}, f32[16,128]{1,0:T(8,128)S(1)}, f32[512,128]{1,0:T(8,128)S(1)}) custom-call(s32[3]{0:T(128)S(1)} %pad_add_fusion.1.block_ref, s32[1,128]{1,0:T(1,128)S(1)} %copy-done.7, bf16[128,512]{1,0:T(8,128)(2,1)S(1)} %bitcast.30, bf16[256,512]{1,0:T(8,128)(2,1)S(1)} %collective-permute-done.refs_0_, ...), custom_call_target="tpu_custom_call" | custom-call | flops 2000000000 | tf_op jit(solution)/shard_map/pallas_call | solution.py:497
  18.7 1.3 %collective-permute-done.2.refs_1_.refs_3_.refs_0_ = bf16[160,512]{1,0:T(8,128)(2,1)S(1)} collective-permute-done((bf16[160,512]{1,0:T(8,128)(2,1)}, bf16[160,512]{1,0:T(8,128)(2,1)S(1)}, u32[]{:S(2)}, u32[]{:S(2)}) %collective-permute-start.2) | collective-permute-done | bytes 163872 | tf_op jit(solution)/shard_map/ppermute | solution.py:69
  20.0 0.6 shard_map.142
  20.7 1.6 %collective-permute-start.7 = (bf16[128,512]{1,0:T(8,128)(2,1)S(1)}, bf16[128,512]{1,0:T(8,128)(2,1)S(1)}, u32[]{:S(2)}, u32[]{:S(2)}) collective-permute-start(bf16[128,512]{1,0:T(8,128)(2,1)S(1)} %get-tuple-element.84), channel_id=1, source_target_pairs={{0,4},{2,6},{4,0},{6,2},{1,5},{3,7},{5,1},{7,3},{8,12},{10,14},{12... | collective-permute-start | bytes 393224 | tf_op jit(solution)/shard_map/ppermute | solution.py:69
  22.6 1.1 %shard_map.141 = (bf16[128,512]{1,0:T(8,128)(2,1)S(1)}, bf16[128,512]{1,0:T(8,128)(2,1)S(1)}) custom-call(s32[4]{0:T(128)S(1)} %pad_add_fusion.3.block_ref, s32[1,128]{1,0:T(1,128)S(1)} %copy-done.7, bf16[128,512]{1,0:T(8,128)(2,1)S(1)} %bitcast.31, bf16[128,512]{1,0:T(8,128)(2,1)S(1)} %bitcast.32, bf16[512,512]{1,0:T(8,128)(2,1)S(1)} %copy-done, ...), custom_call_target="tpu_custom_call" | custom-call | flops 5000000000 | tf_op jit(solution)/shard_map/pallas_call | solution.py:567
  23.7 3.3 %collective-permute-done.7.refs_6_ = bf16[128,512]{1,0:T(8,128)(2,1)S(1)} collective-permute-done((bf16[128,512]{1,0:T(8,128)(2,1)S(1)}, bf16[128,512]{1,0:T(8,128)(2,1)S(1)}, u32[]{:S(2)}, u32[]{:S(2)}) %collective-permute-start.7) | collective-permute-done | bytes 131104 | tf_op jit(solution)/shard_map/ppermute | solution.py:69
  27.0 1.9 %collective-permute-done.8.refs_7_ = bf16[128,512]{1,0:T(8,128)(2,1)S(1)} collective-permute-done((bf16[128,512]{1,0:T(8,128)(2,1)S(1)}, bf16[128,512]{1,0:T(8,128)(2,1)S(1)}, u32[]{:S(2)}, u32[]{:S(2)}) %collective-permute-start.8) | collective-permute-done | bytes 131104 | tf_op jit(solution)/shard_map/ppermute | solution.py:69
  28.9 2.4 %collective-permute-start.9 = (bf16[128,512]{1,0:T(8,128)(2,1)S(1)}, bf16[128,512]{1,0:T(8,128)(2,1)S(1)}, u32[]{:S(2)}, u32[]{:S(2)}) collective-permute-start(bf16[128,512]{1,0:T(8,128)(2,1)S(1)} %get-tuple-element.86.refs_1_), channel_id=1, source_target_pairs={{0,1},{1,0},{2,3},{3,2},{4,5},{5,4},{6,7},{7,6},{8,9},{9,8},{10,11... | collective-permute-start | bytes 393224 | tf_op jit(solution)/shard_map/ppermute | solution.py:69
  31.7 1.6 %collective-permute-start.11 = (bf16[64,512]{1,0:T(8,128)(2,1)S(1)}, bf16[64,512]{1,0:T(8,128)(2,1)S(1)}, u32[]{:S(2)}, u32[]{:S(2)}) collective-permute-start(bf16[64,512]{1,0:T(8,128)(2,1)S(1)} %get-tuple-element.93), channel_id=1, source_target_pairs={{0,4},{2,6},{4,0},{6,2},{1,5},{3,7},{5,1},{7,3},{8,12},{10,14},{12... | collective-permute-start | bytes 196616 | tf_op jit(solution)/shard_map/ppermute | solution.py:69
  33.7 1.6 %collective-permute-done.9.refs_1_ = bf16[128,512]{1,0:T(8,128)(2,1)S(1)} collective-permute-done((bf16[128,512]{1,0:T(8,128)(2,1)S(1)}, bf16[128,512]{1,0:T(8,128)(2,1)S(1)}, u32[]{:S(2)}, u32[]{:S(2)}) %collective-permute-start.9) | collective-permute-done | bytes 131104 | tf_op jit(solution)/shard_map/ppermute | solution.py:69
  35.6 0.6 collective-permute-done.11.refs_2_
  36.2 1.1 %collective-permute-done.12.refs_3_ = bf16[64,512]{1,0:T(8,128)(2,1)S(1)} collective-permute-done((bf16[64,512]{1,0:T(8,128)(2,1)S(1)}, bf16[64,512]{1,0:T(8,128)(2,1)S(1)}, u32[]{:S(2)}, u32[]{:S(2)}) %collective-permute-start.12) | collective-permute-done | bytes 65568 | tf_op jit(solution)/shard_map/ppermute | solution.py:69
  37.5 1.5 %collective-permute-start.14 = (bf16[64,512]{1,0:T(8,128)(2,1)S(1)}, bf16[64,512]{1,0:T(8,128)(2,1)S(1)}, u32[]{:S(2)}, u32[]{:S(2)}) collective-permute-start(bf16[64,512]{1,0:T(8,128)(2,1)S(1)} %get-tuple-element.97), channel_id=1, source_target_pairs={{0,4},{2,6},{4,0},{6,2},{1,5},{3,7},{5,1},{7,3},{8,12},{10,14},{12... | collective-permute-start | bytes 196616 | tf_op jit(solution)/shard_map/ppermute | solution.py:69
  39.2 1.8 %shard_map.145 = (bf16[128,512]{1,0:T(8,128)(2,1)S(1)}, bf16[128,512]{1,0:T(8,128)(2,1)S(1)}, bf16[128,512]{1,0:T(8,128)(2,1)S(1)}, bf16[128,512]{1,0:T(8,128)(2...) custom-call(s32[1]{0:T(128)} %bitcast.own_ref, s32[4]{0:T(128)S(1)} %pad_add_fusion.part_ref, ...), custom_call_target="tpu_custom_call" | custom-call | flops 2000000000 | tf_op jit(solution)/shard_map/pallas_call | solution.py:591
  41.6 1.5 %collective-permute-start.17 = (bf16[128,512]{1,0:T(8,128)(2,1)S(1)}, bf16[128,512]{1,0:T(8,128)(2,1)S(1)}, u32[]{:S(2)}, u32[]{:S(2)}) collective-permute-start(bf16[128,512]{1,0:T(8,128)(2,1)S(1)} %get-tuple-element.113), channel_id=1, source_target_pairs={{0,4},{2,6},{4,0},{6,2},{1,5},{3,7},{5,1},{7,3},{8,12},{10,14},{12... | collective-permute-start | bytes 393224 | tf_op jit(solution)/shard_map/ppermute | solution.py:69
  43.3 1.6 %shard_map.146 = (bf16[2,64,512]{2,1,0:T(8,128)(2,1)S(1)}, bf16[2,64,512]{2,1,0:T(8,128)(2,1)S(1)}, bf16[2,64,512]{2,1,0:T(8,128)(2,1)S(1)}, f32[2,64,512]{2,1,0:T(8,128)S(1)}) custom-call(s32[1]{0:T(128)} %bitcast.own_ref, s32[4]{0:T(128)S(1)} %pad_add_fusion.part_ref, bf16[512,512]{1,0:T(8,128)(2,1)S(1)} %bitcast.26, bf16[512,512]{1,0:T(8,128)(2,1)S(1)} %bitcast.28, ...), custom_call_target="tpu_custom_call" | custom-call | flops 2000000000 | tf_op jit(solution)/shard_map/pallas_call | solution.py:591
  44.9 7.1 %collective-permute-start.19 = (bf16[2,64,512]{2,1,0:T(8,128)(2,1)S(1)}, bf16[2,64,512]{2,1,0:T(8,128)(2,1)S(1)}, u32[]{:S(2)}, u32[]{:S(2)}) collective-permute-start(bf16[2,64,512]{2,1,0:T(8,128)(2,1)S(1)} %get-tuple-element.119), channel_id=1, source_target_pairs={{0,24},{8,16},{16,8},{24,0},{1,25},{9,17},{17,9},{25,1},{2,26},{10... | collective-permute-start | bytes 393224 | tf_op jit(solution)/shard_map/ppermute | solution.py:69
  52.0 1.4 %collective-permute-start.20 = (bf16[2,64,512]{2,1,0:T(8,128)(2,1)S(1)}, bf16[2,64,512]{2,1,0:T(8,128)(2,1)S(1)}, u32[]{:S(2)}, u32[]{:S(2)}) collective-permute-start(bf16[2,64,512]{2,1,0:T(8,128)(2,1)S(1)} %get-tuple-element.120), channel_id=1, source_target_pairs={{0,16},{8,24},{16,0},{24,8},{1,17},{9,25},{17,1},{25,9},{2,18},{10... | collective-permute-start | bytes 393224 | tf_op jit(solution)/shard_map/ppermute | solution.py:69
  53.7 1.4 %shard_map.147 = (bf16[128,512]{1,0:T(8,128)(2,1)}, bf16[128,512]{1,0:T(8,128)(2,1)}) custom-call(s32[1]{0:T(128)} %bitcast.own_ref, bf16[128,512]{1,0:T(8,128)(2,1)S(1)} %get-tuple-element.110.mixed_ref, bf16[160,512]{1,0:T(8,128)(2,1)S(1)} %copy-done.4, bf16[128,512]{1,0:T(8,128)(2,1)S(1)} %get-tuple-element.111.refs_0_, ...), custom_call_target="tpu_custom_call" | custom-call | flops 1500000000 | tf_op jit(solution)/shard_map/pallas_call | solution.py:624
  55.2 1.3 %collective-permute-done.19.refs_0_ = bf16[2,64,512]{2,1,0:T(8,128)(2,1)S(1)} collective-permute-done((bf16[2,64,512]{2,1,0:T(8,128)(2,1)S(1)}, bf16[2,64,512]{2,1,0:T(8,128)(2,1)S(1)}, u32[]{:S(2)}, u32[]{:S(2)}) %collective-permute-start.19) | collective-permute-done | bytes 131104 | tf_op jit(solution)/shard_map/ppermute | solution.py:69
  56.4 8.3 %collective-permute-done.20.refs_1_ = bf16[2,64,512]{2,1,0:T(8,128)(2,1)S(1)} collective-permute-done((bf16[2,64,512]{2,1,0:T(8,128)(2,1)S(1)}, bf16[2,64,512]{2,1,0:T(8,128)(2,1)S(1)}, u32[]{:S(2)}, u32[]{:S(2)}) %collective-permute-start.20) | collective-permute-done | bytes 131104 | tf_op jit(solution)/shard_map/ppermute | solution.py:69
  64.8 0.7 %shard_map.148 = (f32[64,512]{1,0:T(8,128)}, f32[64,512]{1,0:T(8,128)}) custom-call(f32[2,64,512]{2,1,0:T(8,128)S(1)} %get-tuple-element.118.kept_ref, bf16[2,64,512]{2,1,0:T(8,128)(2,1)S(1)} %collective-permute-done.19.refs_0_, bf16[2,64,512]{2,1,0:T(8,128)(2,1)S(1)} %collective-permute-done.20.refs_1_, bf16[2,64,512]{2,1,0:T(8,128)(2,1)S(1)} %collective-permute-done.21.refs_2_), custom_call_target="tpu_custom_call" | custom-call | flops 500000000 | tf_op jit(solution)/shard_map/pallas_call | solution.py:631
  (43 shorter events, 3.3 us)
Async XLA Ops:
  0.6 10.5 %copy-start.5 = (bf16[1,128,512]{2,1,0:T(8,128)(2,1)S(1)}, bf16[1,128,512]{2,1,0:T(8,128)(2,1)}, u32[]{:S(2)}) copy-start(bf16[1,128,512]{2,1,0:T(8,128)(2,1)} %param.11) | copy-start | bytes 393220
  2.6 12.0 %collective-permute-start = (bf16[256,512]{1,0:T(8,128)(2,1)}, bf16[256,512]{1,0:T(8,128)(2,1)S(1)}, u32[]{:S(2)}, u32[]{:S(2)}) collective-permute-start(bf16[256,512]{1,0:T(8,128)(2,1)} %get-tuple-element.65.refs_0_), channel_id=1, source_target_pairs={{0,8},{1,9},{8,16},{9,17},{16,24},{17,25},{2,10},{3,11},{10,18},{1... | collective-permute-start | bytes 786440 | tf_op jit(solution)/shard_map/ppermute | solution.py:478
  7.5 10.4 %collective-permute-start.1 = (bf16[256,512]{1,0:T(8,128)(2,1)}, bf16[256,512]{1,0:T(8,128)(2,1)S(1)}, u32[]{:S(2)}, u32[]{:S(2)}) collective-permute-start(bf16[256,512]{1,0:T(8,128)(2,1)} %get-tuple-element.65.refs_0_), channel_id=1, source_target_pairs={{0,1},{8,9},{16,17},{24,25},{2,3},{10,11},{18,19},{26,27},{4,5},{1... | collective-permute-start | bytes 786440 | tf_op jit(solution)/shard_map/ppermute | solution.py:478
  10.9 9.1 %collective-permute-start.2 = (bf16[160,512]{1,0:T(8,128)(2,1)}, bf16[160,512]{1,0:T(8,128)(2,1)S(1)}, u32[]{:S(2)}, u32[]{:S(2)}) collective-permute-start(bf16[160,512]{1,0:T(8,128)(2,1)} %get-tuple-element.77.refs_0_.refs_2_.extended_ref), channel_id=1, source_target_pairs={{0,1},{1,0},{2,3},{3,2},{4,5},{5,4},{6,7},{7,6},{8,9},{9,8},{10,11... | collective-permute-start | bytes 491528 | tf_op jit(solution)/shard_map/ppermute | solution.py:69
  11.1 0.7 %copy-start.7 = (s32[1,128]{1,0:T(1,128)S(1)}, s32[1,128]{1,0:T(1,128)}, u32[]{:S(2)}) copy-start(s32[1,128]{1,0:T(1,128)} %get-tuple-element.64.begin_ref) | copy-start | bytes 1540
  11.8 0.9 %copy-start.3 = (bf16[256,512]{1,0:T(8,128)(2,1)S(1)}, bf16[256,512]{1,0:T(8,128)(2,1)}, u32[]{:S(2)}) copy-start(bf16[256,512]{1,0:T(8,128)(2,1)} %get-tuple-element.65.refs_0_) | copy-start | bytes 786436
  14.6 7.7 %collective-permute-start.3 = (bf16[256,512]{1,0:T(8,128)(2,1)S(1)}, bf16[256,512]{1,0:T(8,128)(2,1)S(1)}, u32[]{:S(2)}, u32[]{:S(2)}) collective-permute-start(bf16[256,512]{1,0:T(8,128)(2,1)S(1)} %collective-permute-done.refs_0_), channel_id=1, source_target_pairs={{8,16},{9,17},{16,24},{17,25},{10,18},{11,19},{18,26},{19,27},{12,... | collective-permute-start | bytes 786440 | tf_op jit(solution)/shard_map/ppermute | solution.py:478
  15.3 7.3 %collective-permute-start.4 = (bf16[256,512]{1,0:T(8,128)(2,1)S(1)}, bf16[256,512]{1,0:T(8,128)(2,1)S(1)}, u32[]{:S(2)}, u32[]{:S(2)}) collective-permute-start(bf16[256,512]{1,0:T(8,128)(2,1)S(1)} %collective-permute-done.refs_0_), channel_id=1, source_target_pairs={{9,16},{17,24},{11,18},{19,26},{13,20},{21,28},{15,22},{23,30}} | collective-permute-start | bytes 786440 | tf_op jit(solution)/shard_map/ppermute | solution.py:478
  15.9 6.6 %collective-permute-start.5 = (bf16[256,512]{1,0:T(8,128)(2,1)S(1)}, bf16[256,512]{1,0:T(8,128)(2,1)S(1)}, u32[]{:S(2)}, u32[]{:S(2)}) collective-permute-start(bf16[256,512]{1,0:T(8,128)(2,1)S(1)} %collective-permute-done.refs_0_), channel_id=1, source_target_pairs={{8,9},{9,8},{16,17},{17,16},{24,25},{25,24},{10,11},{11,10},{18,19... | collective-permute-start | bytes 786440 | tf_op jit(solution)/shard_map/ppermute | solution.py:478
  16.7 3.3 %copy-start.4 = (bf16[160,512]{1,0:T(8,128)(2,1)S(1)}, bf16[160,512]{1,0:T(8,128)(2,1)}, u32[]{:S(2)}) copy-start(bf16[160,512]{1,0:T(8,128)(2,1)} %get-tuple-element.77.refs_0_.refs_2_.extended_ref) | copy-start | bytes 491524
  20.0 2.5 %copy-start = (bf16[512,512]{1,0:T(8,128)(2,1)S(1)}, bf16[512,512]{1,0:T(8,128)(2,1)}, u32[]{:S(2)}) copy-start(bf16[512,512]{1,0:T(8,128)(2,1)} %proj_ref.1) | copy-start | bytes 1572868
  20.0 2.5 %copy-start.6 = (bf16[1,128,512]{2,1,0:T(8,128)(2,1)S(1)}, bf16[1,128,512]{2,1,0:T(8,128)(2,1)}, u32[]{:S(2)}) copy-start(bf16[1,128,512]{2,1,0:T(8,128)(2,1)} %param.15) | copy-start | bytes 393220
  20.6 3.1 %collective-permute-start.6 = (bf16[128,512]{1,0:T(8,128)(2,1)S(1)}, bf16[128,512]{1,0:T(8,128)(2,1)S(1)}, u32[]{:S(2)}, u32[]{:S(2)}) collective-permute-start(bf16[128,512]{1,0:T(8,128)(2,1)S(1)} %get-tuple-element.83), channel_id=1, source_target_pairs={{0,2},{2,0},{4,6},{6,4},{1,3},{3,1},{5,7},{7,5},{8,10},{10,8},{12,... | collective-permute-start | bytes 393224 | tf_op jit(solution)/shard_map/ppermute | solution.py:69
  20.7 6.4 %collective-permute-start.7 = (bf16[128,512]{1,0:T(8,128)(2,1)S(1)}, bf16[128,512]{1,0:T(8,128)(2,1)S(1)}, u32[]{:S(2)}, u32[]{:S(2)}) collective-permute-start(bf16[128,512]{1,0:T(8,128)(2,1)S(1)} %get-tuple-element.84), channel_id=1, source_target_pairs={{0,4},{2,6},{4,0},{6,2},{1,5},{3,7},{5,1},{7,3},{8,12},{10,14},{12... | collective-permute-start | bytes 393224 | tf_op jit(solution)/shard_map/ppermute | solution.py:69
  22.3 6.7 %collective-permute-start.8 = (bf16[128,512]{1,0:T(8,128)(2,1)S(1)}, bf16[128,512]{1,0:T(8,128)(2,1)S(1)}, u32[]{:S(2)}, u32[]{:S(2)}) collective-permute-start(bf16[128,512]{1,0:T(8,128)(2,1)S(1)} %get-tuple-element.85), channel_id=1, source_target_pairs={{0,6},{2,4},{4,2},{6,0},{1,7},{3,5},{5,3},{7,1},{8,14},{10,12},{12... | collective-permute-start | bytes 393224 | tf_op jit(solution)/shard_map/ppermute | solution.py:69
  28.9 6.3 %collective-permute-start.9 = (bf16[128,512]{1,0:T(8,128)(2,1)S(1)}, bf16[128,512]{1,0:T(8,128)(2,1)S(1)}, u32[]{:S(2)}, u32[]{:S(2)}) collective-permute-start(bf16[128,512]{1,0:T(8,128)(2,1)S(1)} %get-tuple-element.86.refs_1_), channel_id=1, source_target_pairs={{0,1},{1,0},{2,3},{3,2},{4,5},{5,4},{6,7},{7,6},{8,9},{9,8},{10,11... | collective-permute-start | bytes 393224 | tf_op jit(solution)/shard_map/ppermute | solution.py:69
  31.7 3.9 %collective-permute-start.10 = (bf16[64,512]{1,0:T(8,128)(2,1)S(1)}, bf16[64,512]{1,0:T(8,128)(2,1)S(1)}, u32[]{:S(2)}, u32[]{:S(2)}) collective-permute-start(bf16[64,512]{1,0:T(8,128)(2,1)S(1)} %get-tuple-element.92), channel_id=1, source_target_pairs={{0,2},{2,0},{4,6},{6,4},{1,3},{3,1},{5,7},{7,5},{8,10},{10,8},{12,... | collective-permute-start | bytes 196616 | tf_op jit(solution)/shard_map/ppermute | solution.py:69
  31.7 4.5 %collective-permute-start.11 = (bf16[64,512]{1,0:T(8,128)(2,1)S(1)}, bf16[64,512]{1,0:T(8,128)(2,1)S(1)}, u32[]{:S(2)}, u32[]{:S(2)}) collective-permute-start(bf16[64,512]{1,0:T(8,128)(2,1)S(1)} %get-tuple-element.93), channel_id=1, source_target_pairs={{0,4},{2,6},{4,0},{6,2},{1,5},{3,7},{5,1},{7,3},{8,12},{10,14},{12... | collective-permute-start | bytes 196616 | tf_op jit(solution)/shard_map/ppermute | solution.py:69
  33.3 4.0 %collective-permute-start.12 = (bf16[64,512]{1,0:T(8,128)(2,1)S(1)}, bf16[64,512]{1,0:T(8,128)(2,1)S(1)}, u32[]{:S(2)}, u32[]{:S(2)}) collective-permute-start(bf16[64,512]{1,0:T(8,128)(2,1)S(1)} %get-tuple-element.94), channel_id=1, source_target_pairs={{0,6},{2,4},{4,2},{6,0},{1,7},{3,5},{5,3},{7,1},{8,14},{10,12},{12... | collective-permute-start | bytes 196616 | tf_op jit(solution)/shard_map/ppermute | solution.py:69
  33.7 5.6 %copy-start.1 = (bf16[1,512,512]{2,1,0:T(8,128)(2,1)S(1)}, bf16[1,512,512]{2,1,0:T(8,128)(2,1)}, u32[]{:S(2)}) copy-start(bf16[1,512,512]{2,1,0:T(8,128)(2,1)} %param.19) | copy-start | bytes 1572868
  33.7 5.6 %copy-start.2 = (bf16[1,512,512]{2,1,0:T(8,128)(2,1)S(1)}, bf16[1,512,512]{2,1,0:T(8,128)(2,1)}, u32[]{:S(2)}) copy-start(bf16[1,512,512]{2,1,0:T(8,128)(2,1)} %param.20) | copy-start | bytes 1572868
  37.4 5.7 %collective-permute-start.13 = (bf16[64,512]{1,0:T(8,128)(2,1)S(1)}, bf16[64,512]{1,0:T(8,128)(2,1)S(1)}, u32[]{:S(2)}, u32[]{:S(2)}) collective-permute-start(bf16[64,512]{1,0:T(8,128)(2,1)S(1)} %get-tuple-element.96), channel_id=1, source_target_pairs={{0,2},{2,0},{4,6},{6,4},{1,3},{3,1},{5,7},{7,5},{8,10},{10,8},{12,... | collective-permute-start | bytes 196616 | tf_op jit(solution)/shard_map/ppermute | solution.py:69
  37.5 5.5 %collective-permute-start.14 = (bf16[64,512]{1,0:T(8,128)(2,1)S(1)}, bf16[64,512]{1,0:T(8,128)(2,1)S(1)}, u32[]{:S(2)}, u32[]{:S(2)}) collective-permute-start(bf16[64,512]{1,0:T(8,128)(2,1)S(1)} %get-tuple-element.97), channel_id=1, source_target_pairs={{0,4},{2,6},{4,0},{6,2},{1,5},{3,7},{5,1},{7,3},{8,12},{10,14},{12... | collective-permute-start | bytes 196616 | tf_op jit(solution)/shard_map/ppermute | solution.py:69
  39.0 4.3 %collective-permute-start.15 = (bf16[64,512]{1,0:T(8,128)(2,1)S(1)}, bf16[64,512]{1,0:T(8,128)(2,1)S(1)}, u32[]{:S(2)}, u32[]{:S(2)}) collective-permute-start(bf16[64,512]{1,0:T(8,128)(2,1)S(1)} %get-tuple-element.98), channel_id=1, source_target_pairs={{0,6},{2,4},{4,2},{6,0},{1,7},{3,5},{5,3},{7,1},{8,14},{10,12},{12... | collective-permute-start | bytes 196616 | tf_op jit(solution)/shard_map/ppermute | solution.py:69
  41.1 12.3 %collective-permute-start.16 = (bf16[128,512]{1,0:T(8,128)(2,1)S(1)}, bf16[128,512]{1,0:T(8,128)(2,1)S(1)}, u32[]{:S(2)}, u32[]{:S(2)}) collective-permute-start(bf16[128,512]{1,0:T(8,128)(2,1)S(1)} %get-tuple-element.112), channel_id=1, source_target_pairs={{0,2},{2,0},{4,6},{6,4},{1,3},{3,1},{5,7},{7,5},{8,10},{10,8},{12,... | collective-permute-start | bytes 393224 | tf_op jit(solution)/shard_map/ppermute | solution.py:69
  41.6 12.1 %collective-permute-start.17 = (bf16[128,512]{1,0:T(8,128)(2,1)S(1)}, bf16[128,512]{1,0:T(8,128)(2,1)S(1)}, u32[]{:S(2)}, u32[]{:S(2)}) collective-permute-start(bf16[128,512]{1,0:T(8,128)(2,1)S(1)} %get-tuple-element.113), channel_id=1, source_target_pairs={{0,4},{2,6},{4,0},{6,2},{1,5},{3,7},{5,1},{7,3},{8,12},{10,14},{12... | collective-permute-start | bytes 393224 | tf_op jit(solution)/shard_map/ppermute | solution.py:69
  43.1 10.7 %collective-permute-start.18 = (bf16[128,512]{1,0:T(8,128)(2,1)S(1)}, bf16[128,512]{1,0:T(8,128)(2,1)S(1)}, u32[]{:S(2)}, u32[]{:S(2)}) collective-permute-start(bf16[128,512]{1,0:T(8,128)(2,1)S(1)} %get-tuple-element.114), channel_id=1, source_target_pairs={{0,6},{2,4},{4,2},{6,0},{1,7},{3,5},{5,3},{7,1},{8,14},{10,12},{12... | collective-permute-start | bytes 393224 | tf_op jit(solution)/shard_map/ppermute | solution.py:69
  44.9 11.6 %collective-permute-start.19 = (bf16[2,64,512]{2,1,0:T(8,128)(2,1)S(1)}, bf16[2,64,512]{2,1,0:T(8,128)(2,1)S(1)}, u32[]{:S(2)}, u32[]{:S(2)}) collective-permute-start(bf16[2,64,512]{2,1,0:T(8,128)(2,1)S(1)} %get-tuple-element.119), channel_id=1, source_target_pairs={{0,24},{8,16},{16,8},{24,0},{1,25},{9,17},{17,9},{25,1},{2,26},{10... | collective-permute-start | bytes 393224 | tf_op jit(solution)/shard_map/ppermute | solution.py:69
  52.0 12.8 %collective-permute-start.20 = (bf16[2,64,512]{2,1,0:T(8,128)(2,1)S(1)}, bf16[2,64,512]{2,1,0:T(8,128)(2,1)S(1)}, u32[]{:S(2)}, u32[]{:S(2)}) collective-permute-start(bf16[2,64,512]{2,1,0:T(8,128)(2,1)S(1)} %get-tuple-element.120), channel_id=1, source_target_pairs={{0,16},{8,24},{16,0},{24,8},{1,17},{9,25},{17,1},{25,9},{2,18},{10... | collective-permute-start | bytes 393224 | tf_op jit(solution)/shard_map/ppermute | solution.py:69
  53.4 11.4 %collective-permute-start.21 = (bf16[2,64,512]{2,1,0:T(8,128)(2,1)S(1)}, bf16[2,64,512]{2,1,0:T(8,128)(2,1)S(1)}, u32[]{:S(2)}, u32[]{:S(2)}) collective-permute-start(bf16[2,64,512]{2,1,0:T(8,128)(2,1)S(1)} %get-tuple-element.121), channel_id=1, source_target_pairs={{0,8},{8,0},{16,24},{24,16},{1,9},{9,1},{17,25},{25,17},{2,10},{10... | collective-permute-start | bytes 393224 | tf_op jit(solution)/shard_map/ppermute | solution.py:69

commit v6 on v5

--- a/solution.py
+++ b/solution.py
@@ -122,29 +122,39 @@
     begin_ref,
     chosen_ref,
     held_router_ref,
+    tail_ref,
     held_lengths_ref,
     sems,
 ):
     tok, width = key_ref.shape
+    rest = tail_ref.shape[0]
     targets = (
         (choice_ref, chosen_ref),
+        (router_ref, held_router_ref),
         (lengths_ref, held_lengths_ref),
         (key_ref, pair_ref.at[pl.ds(0, tok), :]),
         (value_ref, pair_ref.at[pl.ds(tok, tok), :]),
         (grad_ref, extended_ref.at[pl.ds(0, tok), :]),
-        (router_ref, held_router_ref),
+        (tail_ref, extended_ref.at[pl.ds(tok, rest), :]),
     )
     copies = [
         pltpu.make_async_copy(source, target, sems.at[place])
         for place, (source, target) in enumerate(targets)
     ]
-    for copy in copies:
+    for copy in copies[:-1]:
         copy.start()
     copies[0].wait()
     chosen = jnp.broadcast_to(chosen_ref[...].astype(jnp.float32), (16, tok))
-    extended_ref[tok : tok + 16, 0:tok] = chosen.astype(jnp.bfloat16)
-    extended_ref[tok : tok + 16, tok:width] = jnp.zeros((16, width - tok), jnp.bfloat16)
+    tail_ref[0:16, 0:tok] = chosen.astype(jnp.bfloat16)
+    tail_ref[0:16, tok:width] = jnp.zeros((16, width - tok), jnp.bfloat16)
     copies[1].wait()
+    routed = held_router_ref[...].astype(jnp.float32)
+    spare = rest - 16 - routed.shape[0]
+    if spare:
+        routed = jnp.concatenate([routed, jnp.zeros((spare, width), jnp.float32)], axis=0)
+    tail_ref[16:rest, :] = routed.astype(jnp.bfloat16)
+    copies[-1].start()
+    copies[2].wait()
     position = rank_ref[0] * tok + lax.broadcasted_iota(jnp.int32, (1, tok), 1)
     begin = jnp.zeros((1, tok), jnp.int32)
     bound = jnp.int32(0)
@@ -152,13 +162,7 @@
         bound = bound + held_lengths_ref[0, doc]
         begin = jnp.maximum(begin, jnp.where(position >= bound, bound, 0))
     begin_ref[...] = begin
-    copies[5].wait()
-    routed = held_router_ref[...].astype(jnp.float32)
-    spare = extended_ref.shape[0] - tok - 16 - routed.shape[0]
-    if spare:
-        routed = jnp.concatenate([routed, jnp.zeros((spare, width), jnp.float32)], axis=0)
-    extended_ref[tok + 16 :, :] = routed.astype(jnp.bfloat16)
-    for copy in copies[2:5]:
+    for copy in copies[3:]:
         copy.wait()
 
 
@@ -302,7 +306,7 @@
     own_rows = rep_list[0] == 0
     held_ref, refs = refs[-1], refs[:-1]
     if own_rows:
-        back_refs, (up_acc, down_acc) = refs[:-2], refs[-2:]
+        back_refs, (up_acc, down_acc) = refs[1:-2], refs[-2:]
     else:
         up_old, down_old = refs[:2]
         term_refs, kept_ref = refs[2:-1], refs[-1]
@@ -502,20 +506,22 @@
             cost=2.0,
         )(block_ids(entries), begin, query, *arrays, *state)
 
+    tail = 16 + -(-expert_count // 16) * 16
     pair, extended, begin = pl.pallas_call(
         stack_kernel,
         out_shape=[
             shape((2 * tok, width)),
-            shape((tok + 16 + -(-expert_count // 16) * 16, width)),
+            shape((tok + tail, width)),
             shape((1, tok), jnp.int32),
         ],
         in_specs=[SMEM] + [HBM] * 6,
-        out_specs=[VMEM] * 3,
+        out_specs=[HBM, HBM, VMEM],
         scratch_shapes=[
             pltpu.VMEM((1, tok), jnp.int32),
             pltpu.VMEM((expert_count, width), jnp.bfloat16),
+            pltpu.VMEM((tail, width), jnp.bfloat16),
             pltpu.SMEM(doc_lengths.shape, jnp.int32),
-            pltpu.SemaphoreType.DMA((6,)),
+            pltpu.SemaphoreType.DMA((7,)),
         ],
         compiler_params=pltpu.CompilerParams(vmem_limit_bytes=60 * 1024 * 1024),
     )(
@@ -534,25 +540,29 @@
     extendeds = None
     state = ()
     for step in range(1, reach + 1):
-        ahead = send(line, step - 1, 1, 0, False)
-        arrays, entries = [ahead], [(step, rep_index, always)]
-        for d in range(1, rep_count):
-            if step == reach:
+        arrays, entries = [], []
+        if step > 1:
+            for d in range(1, rep_count):
+                arrays.append(send(line, step - 1, 0, d, True))
+                entries.append((step - 1, (rep_index - d) % rep_count, always))
+        if step == reach:
+            for d in range(1, rep_count):
                 arrays.append(send(line, step - 1, 1, -d, False))
                 entries.append((step, rep_index + d, rep_index + d < rep_count))
-            if step == 1:
+        ahead = send(line, step - 1, 1, 0, False)
+        arrays.append(ahead)
+        entries.append((step, rep_index, always))
+        if step == 1:
+            for d in range(1, rep_count):
                 arrays.append(send(line, 0, 0, d, False))
                 entries.append((0, rep_index - d, rep_index >= d))
-            else:
-                arrays.append(send(line, step - 1, 0, d, True))
-                entries.append((step - 1, (rep_index - d) % rep_count, always))
-        if step == 1:
             extendeds = reps.exchange([extended] * rep_count)
-        state = attend(rounds[-1], state)
-        rounds.append((arrays, entries))
         if step < reach:
-            line, *state = lax.optimization_barrier((ahead, *state))
-            arrays[0] = line
+            rounds[-1] = (rounds[-1][0] + arrays, rounds[-1][1] + entries)
+        else:
+            rounds.append((arrays, entries))
+        line = ahead
+    state = attend(rounds[0], state)
 
     *held, pinned = lax.optimization_barrier((*state, extendeds[0]))
     state, extendeds = held, [pinned] + list(extendeds[1:])
@@ -584,7 +594,6 @@
     others = reps.exchange([normed] * rep_count)[1:]
     got_rows = merged(experts.exchange(dispatch(extendeds[:1], [normed])), MOST_PERMUTES)
     more_rows = dispatch(extendeds[1:], others)
-    more_rows, got_rows = lax.optimization_barrier((more_rows, got_rows))
     got_more = merged(experts.exchange(more_rows), MOST_PERMUTES)
 
     def expert_call(rep_list, rows, out_shape, extra):
@@ -610,7 +619,7 @@
         [shape((2 * hot_capacity, width))] * expert_count
         + [shape((seq_count * strip, hidden), jnp.float32)]
         + [shape((seq_count * strip, width), jnp.float32)],
-        [],
+        [more_rows[0]],
     )
     got_back = merged(experts.exchange(back, inverse=True), MOST_PERMUTES)
     *terms, kept = expert_call(

time: 65.5 us -> 77.9 us (1.19)
  Pallas kernels: 12.4 us -> 23.4 us
  starting transfers between devices: 29.4 us -> 31.9 us
  waiting for transfers between devices: 20.9 us -> 19.7 us
    pallas_call x1, Pallas kernels: 1.91 us -> 13.6 us  [local(): pl.pallas_call(stack_kernel, out_shape=[shape((2 * tok, width)), shape((t...]
    ppermute x17, waiting for transfers between devices: 19.6 us -> 15 us  [exchange(): got[k] = lax.ppermute(chunks[k], self.axes, pairs)]
    ppermute x5, waiting for transfers between devices: 1.27 us -> 4.71 us  [send(): return lax.ppermute(array, ('seq', 'rep'), pairs)]
    ppermute x17, starting transfers between devices: 19 us -> 21.4 us  [exchange(): got[k] = lax.ppermute(chunks[k], self.axes, pairs)]
    pallas_call x2 -> x1, Pallas kernels: 2.49 us -> 1.76 us  [attend(): call(functools.partial(attend_kernel, len(arrays), not state), state_shap...]
  transfers between devices with their start and end apart: 22 -> 22, of which waited for: 10 -> 6; matrix products, arithmetic and copies ran while one was open for 0% -> 0% of each run, Pallas kernels for 15% -> 12%
where the time goes in v6:
time: 77.9 us; the launch traced here: 77.7 us
  starting transfers between devices  31.9 us (41%)
  Pallas kernels  23.4 us (30%)
  waiting for transfers between devices  19.7 us (25%)
  local copies, waits for them, and re-layouts  1.6 us (2%)
  between operations  0.92 us (1%)
    ppermute x17, starting transfers between devices, exchange(): got[k] = lax.ppermute(chunks[k], self.axes, pairs)  21.4 us
    ppermute x17, waiting for transfers between devices, exchange(): got[k] = lax.ppermute(chunks[k], self.axes, pairs)  15 us
    pallas_call x1, Pallas kernels, local(): pl.pallas_call(stack_kernel, out_shape=[shape((2 * tok, width)), shape((t...  13.6 us
    ppermute x5, starting transfers between devices, send(): return lax.ppermute(array, ('seq', 'rep'), pairs)  10.5 us
    ppermute x5, waiting for transfers between devices, send(): return lax.ppermute(array, ('seq', 'rep'), pairs)  4.71 us
    pallas_call x2, Pallas kernels, expert_call(): call(functools.partial(expert_kernel, rep_count, rep_list, expert_count,...  3.48 us
    pallas_call x1, Pallas kernels, attend(): call(functools.partial(attend_kernel, len(arrays), not state), state_shap...  1.76 us
    unnamed x16, local copies, waits for them, and re-layouts  1.6 us
  transfers between devices with their start and end apart: 22, of which 6 were waited for; matrix products, arithmetic and copies ran while one was open for 0% of the time, Pallas kernels for 12%

profile of v6, /device:TPU:0, one launch (start us, length us, event | category | flops | bytes accessed | tf_op | source)
XLA Modules:
  0.0 77.7 jit_solution(11899477659375329798)
XLA Ops:
  0.6 13.6 %shard_map.138 = (bf16[256,512]{1,0:T(8,128)(2,1)}, bf16[160,512]{1,0:T(8,128)(2,1)}, s32[1,128]{1,0:T(1,128)}) custom-call(s32[1]{0:T(128)} %bitcast.7.rank_ref, s32[1,128]{1,0:T(1,128)} %bitcast.36, s32[1,8]{1,0:T(1,128)} %lengths_ref.1, bf16[4,512]{1,0:T(4,128)(2,1)} %bitcast.35, bf16[128,512]{1,0:T(8,128)(2,1)} %bitcast.32, bf16[128,512]{1,0:T(8,128)(2,1)} %bitcast.33, ...), custom_call_target="tpu_custom_call" | custom-call | tf_op jit(solution)/shard_map/pallas_call | solution.py:510
  14.3 5.1 %collective-permute-start = (bf16[256,512]{1,0:T(8,128)(2,1)}, bf16[256,512]{1,0:T(8,128)(2,1)S(1)}, u32[]{:S(2)}, u32[]{:S(2)}) collective-permute-start(bf16[256,512]{1,0:T(8,128)(2,1)} %get-tuple-element.50.refs_0_), channel_id=1, source_target_pairs={{0,8},{1,9},{8,16},{9,17},{16,24},{17,25},{2,10},{3,11},{10,18},{1... | collective-permute-start | bytes 786440 | tf_op jit(solution)/shard_map/ppermute | solution.py:482
  19.4 3.4 %collective-permute-start.1 = (bf16[256,512]{1,0:T(8,128)(2,1)}, bf16[256,512]{1,0:T(8,128)(2,1)S(1)}, u32[]{:S(2)}, u32[]{:S(2)}) collective-permute-start(bf16[256,512]{1,0:T(8,128)(2,1)} %get-tuple-element.50.refs_0_), channel_id=1, source_target_pairs={{0,1},{8,9},{16,17},{24,25},{2,3},{10,11},{18,19},{26,27},{4,5},{1... | collective-permute-start | bytes 786440 | tf_op jit(solution)/shard_map/ppermute | solution.py:482
  23.0 2.2 %collective-permute-done.refs_1_ = bf16[256,512]{1,0:T(8,128)(2,1)S(1)} collective-permute-done((bf16[256,512]{1,0:T(8,128)(2,1)}, bf16[256,512]{1,0:T(8,128)(2,1)S(1)}, u32[]{:S(2)}, u32[]{:S(2)}) %collective-permute-start) | collective-permute-done | bytes 262176 | tf_op jit(solution)/shard_map/ppermute | solution.py:482
  25.2 0.7 collective-permute-start.3
  25.9 0.7 collective-permute-start.4
  26.6 0.7 collective-permute-start.5
  27.3 2.5 %collective-permute-done.1.refs_2_ = bf16[256,512]{1,0:T(8,128)(2,1)S(1)} collective-permute-done((bf16[256,512]{1,0:T(8,128)(2,1)}, bf16[256,512]{1,0:T(8,128)(2,1)S(1)}, u32[]{:S(2)}, u32[]{:S(2)}) %collective-permute-start.1) | collective-permute-done | bytes 262176 | tf_op jit(solution)/shard_map/ppermute | solution.py:482
  29.8 0.6 copy-done.7
  30.4 0.9 %copy-done.3 = bf16[256,512]{1,0:T(8,128)(2,1)S(1)} copy-done((bf16[256,512]{1,0:T(8,128)(2,1)S(1)}, bf16[256,512]{1,0:T(8,128)(2,1)}, u32[]{:S(2)}) %copy-start.3) | copy-done | bytes 262168
  31.4 1.8 %shard_map.139 = (f32[16,128]{1,0:T(8,128)S(1)}, f32[16,128]{1,0:T(8,128)S(1)}, f32[512,128]{1,0:T(8,128)S(1)}) custom-call(s32[4]{0:T(128)S(1)} %pad_add_fusion.1.block_ref, s32[1,128]{1,0:T(1,128)S(1)} %copy-done.7, bf16[128,512]{1,0:T(8,128)(2,1)S(1)} %bitcast.29, bf16[256,512]{1,0:T(8,128)(2,1)S(1)} %copy-done.3, ...), custom_call_target="tpu_custom_call" | custom-call | flops 2000000000 | tf_op jit(solution)/shard_map/pallas_call | solution.py:501
  33.2 0.5 shard_map.141
  33.8 1.6 %collective-permute-start.7 = (bf16[128,512]{1,0:T(8,128)(2,1)S(1)}, bf16[128,512]{1,0:T(8,128)(2,1)S(1)}, u32[]{:S(2)}, u32[]{:S(2)}) collective-permute-start(bf16[128,512]{1,0:T(8,128)(2,1)S(1)} %get-tuple-element.62), channel_id=1, source_target_pairs={{0,4},{2,6},{4,0},{6,2},{1,5},{3,7},{5,1},{7,3},{8,12},{10,14},{12... | collective-permute-start | bytes 393224 | tf_op jit(solution)/shard_map/ppermute | solution.py:69
  35.4 0.3 collective-permute-start.8
  35.7 1.1 %shard_map.140 = (bf16[128,512]{1,0:T(8,128)(2,1)S(1)}, bf16[128,512]{1,0:T(8,128)(2,1)S(1)}) custom-call(s32[4]{0:T(128)S(1)} %pad_add_fusion.2.block_ref, s32[1,128]{1,0:T(1,128)S(1)} %copy-done.7, bf16[128,512]{1,0:T(8,128)(2,1)S(1)} %bitcast.30, bf16[128,512]{1,0:T(8,128)(2,1)S(1)} %bitcast.31, bf16[512,512]{1,0:T(8,128)(2,1)S(1)} %copy-done, ...), custom_call_target="tpu_custom_call" | custom-call | flops 5000000000 | tf_op jit(solution)/shard_map/pallas_call | solution.py:577
  36.9 3.3 %collective-permute-done.7.refs_6_ = bf16[128,512]{1,0:T(8,128)(2,1)S(1)} collective-permute-done((bf16[128,512]{1,0:T(8,128)(2,1)S(1)}, bf16[128,512]{1,0:T(8,128)(2,1)S(1)}, u32[]{:S(2)}, u32[]{:S(2)}) %collective-permute-start.7) | collective-permute-done | bytes 131104 | tf_op jit(solution)/shard_map/ppermute | solution.py:69
  40.2 1.9 %collective-permute-done.8.refs_7_ = bf16[128,512]{1,0:T(8,128)(2,1)S(1)} collective-permute-done((bf16[128,512]{1,0:T(8,128)(2,1)S(1)}, bf16[128,512]{1,0:T(8,128)(2,1)S(1)}, u32[]{:S(2)}, u32[]{:S(2)}) %collective-permute-start.8) | collective-permute-done | bytes 131104 | tf_op jit(solution)/shard_map/ppermute | solution.py:69
  42.1 3.5 %collective-permute-start.9 = (bf16[128,512]{1,0:T(8,128)(2,1)S(1)}, bf16[128,512]{1,0:T(8,128)(2,1)S(1)}, u32[]{:S(2)}, u32[]{:S(2)}) collective-permute-start(bf16[128,512]{1,0:T(8,128)(2,1)S(1)} %get-tuple-element.64.refs_1_), channel_id=1, source_target_pairs={{0,1},{1,0},{2,3},{3,2},{4,5},{5,4},{6,7},{7,6},{8,9},{9,8},{10,11... | collective-permute-start | bytes 393224 | tf_op jit(solution)/shard_map/ppermute | solution.py:69
  45.6 0.3 shard_map.143
  46.1 1.6 %collective-permute-start.14 = (bf16[64,512]{1,0:T(8,128)(2,1)S(1)}, bf16[64,512]{1,0:T(8,128)(2,1)S(1)}, u32[]{:S(2)}, u32[]{:S(2)}) collective-permute-start(bf16[64,512]{1,0:T(8,128)(2,1)S(1)} %get-tuple-element.75), channel_id=1, source_target_pairs={{0,4},{2,6},{4,0},{6,2},{1,5},{3,7},{5,1},{7,3},{8,12},{10,14},{12... | collective-permute-start | bytes 196616 | tf_op jit(solution)/shard_map/ppermute | solution.py:69
  48.0 1.6 %collective-permute-done.9.refs_1_ = bf16[128,512]{1,0:T(8,128)(2,1)S(1)} collective-permute-done((bf16[128,512]{1,0:T(8,128)(2,1)S(1)}, bf16[128,512]{1,0:T(8,128)(2,1)S(1)}, u32[]{:S(2)}, u32[]{:S(2)}) %collective-permute-start.9) | collective-permute-done | bytes 131104 | tf_op jit(solution)/shard_map/ppermute | solution.py:69
  49.6 0.3 shard_map.142
  50.0 1.6 %collective-permute-start.11 = (bf16[64,512]{1,0:T(8,128)(2,1)S(1)}, bf16[64,512]{1,0:T(8,128)(2,1)S(1)}, u32[]{:S(2)}, u32[]{:S(2)}) collective-permute-start(bf16[64,512]{1,0:T(8,128)(2,1)S(1)} %get-tuple-element.67), channel_id=1, source_target_pairs={{0,4},{2,6},{4,0},{6,2},{1,5},{3,7},{5,1},{7,3},{8,12},{10,14},{12... | collective-permute-start | bytes 196616 | tf_op jit(solution)/shard_map/ppermute | solution.py:69
  51.9 1.9 %shard_map.144 = (bf16[128,512]{1,0:T(8,128)(2,1)S(1)}, bf16[128,512]{1,0:T(8,128)(2,1)S(1)}, bf16[128,512]{1,0:T(8,128)(2,1)S(1)}, bf16[128,512]{1,0:T(8,128)(2...) custom-call(s32[1]{0:T(128)} %bitcast.own_ref, s32[4]{0:T(128)S(1)} %pad_add_fusion.part_ref, ...), custom_call_target="tpu_custom_call" | custom-call | flops 2000000000 | tf_op jit(solution)/shard_map/pallas_call | solution.py:600
  53.7 0.4 collective-permute-start.16
  54.2 1.5 %collective-permute-start.17 = (bf16[128,512]{1,0:T(8,128)(2,1)S(1)}, bf16[128,512]{1,0:T(8,128)(2,1)S(1)}, u32[]{:S(2)}, u32[]{:S(2)}) collective-permute-start(bf16[128,512]{1,0:T(8,128)(2,1)S(1)} %get-tuple-element.83), channel_id=1, source_target_pairs={{0,4},{2,6},{4,0},{6,2},{1,5},{3,7},{5,1},{7,3},{8,12},{10,14},{12... | collective-permute-start | bytes 393224 | tf_op jit(solution)/shard_map/ppermute | solution.py:69
  55.7 1.6 %shard_map.145 = (bf16[2,64,512]{2,1,0:T(8,128)(2,1)S(1)}, bf16[2,64,512]{2,1,0:T(8,128)(2,1)S(1)}, bf16[2,64,512]{2,1,0:T(8,128)(2,1)S(1)}, f32[2,64,512]{2,1,0:T(8,128)S(1)}) custom-call(s32[1]{0:T(128)} %bitcast.own_ref, s32[4]{0:T(128)S(1)} %pad_add_fusion.part_ref, bf16[512,512]{1,0:T(8,128)(2,1)S(1)} %bitcast.26, bf16[512,512]{1,0:T(8,128)(2,1)S(1)} %bitcast.28, ...), custom_call_target="tpu_custom_call" | custom-call | flops 2000000000 | tf_op jit(solution)/shard_map/pallas_call | solution.py:600
  57.3 5.8 %collective-permute-start.19 = (bf16[2,64,512]{2,1,0:T(8,128)(2,1)S(1)}, bf16[2,64,512]{2,1,0:T(8,128)(2,1)S(1)}, u32[]{:S(2)}, u32[]{:S(2)}) collective-permute-start(bf16[2,64,512]{2,1,0:T(8,128)(2,1)S(1)} %get-tuple-element.89), channel_id=1, source_target_pairs={{0,24},{8,16},{16,8},{24,0},{1,25},{9,17},{17,9},{25,1},{2,26},{10... | collective-permute-start | bytes 393224 | tf_op jit(solution)/shard_map/ppermute | solution.py:69
  63.1 4.3 %collective-permute-start.20 = (bf16[2,64,512]{2,1,0:T(8,128)(2,1)S(1)}, bf16[2,64,512]{2,1,0:T(8,128)(2,1)S(1)}, u32[]{:S(2)}, u32[]{:S(2)}) collective-permute-start(bf16[2,64,512]{2,1,0:T(8,128)(2,1)S(1)} %get-tuple-element.90), channel_id=1, source_target_pairs={{0,16},{8,24},{16,0},{24,8},{1,17},{9,25},{17,1},{25,9},{2,18},{10... | collective-permute-start | bytes 393224 | tf_op jit(solution)/shard_map/ppermute | solution.py:69
  67.4 1.4 %shard_map.146 = (bf16[128,512]{1,0:T(8,128)(2,1)}, bf16[128,512]{1,0:T(8,128)(2,1)}) custom-call(s32[1]{0:T(128)} %bitcast.own_ref, bf16[128,512]{1,0:T(8,128)(2,1)S(1)} %get-tuple-element.80.mixed_ref, bf16[160,512]{1,0:T(8,128)(2,1)S(1)} %copy-done.4, bf16[128,512]{1,0:T(8,128)(2,1)S(1)} %get-tuple-element.81.refs_0_, ...), custom_call_target="tpu_custom_call" | custom-call | flops 1500000000 | tf_op jit(solution)/shard_map/pallas_call | solution.py:633
  68.8 8.2 %collective-permute-done.20.refs_1_ = bf16[2,64,512]{2,1,0:T(8,128)(2,1)S(1)} collective-permute-done((bf16[2,64,512]{2,1,0:T(8,128)(2,1)S(1)}, bf16[2,64,512]{2,1,0:T(8,128)(2,1)S(1)}, u32[]{:S(2)}, u32[]{:S(2)}) %collective-permute-start.20) | collective-permute-done | bytes 131104 | tf_op jit(solution)/shard_map/ppermute | solution.py:69
  77.0 0.7 shard_map.147
  (41 shorter events, 1.2 us)
Async XLA Ops:
  14.3 15.5 %copy-start.5 = (bf16[1,128,512]{2,1,0:T(8,128)(2,1)S(1)}, bf16[1,128,512]{2,1,0:T(8,128)(2,1)}, u32[]{:S(2)}) copy-start(bf16[1,128,512]{2,1,0:T(8,128)(2,1)} %param.11) | copy-start | bytes 393220
  14.3 10.9 %collective-permute-start = (bf16[256,512]{1,0:T(8,128)(2,1)}, bf16[256,512]{1,0:T(8,128)(2,1)S(1)}, u32[]{:S(2)}, u32[]{:S(2)}) collective-permute-start(bf16[256,512]{1,0:T(8,128)(2,1)} %get-tuple-element.50.refs_0_), channel_id=1, source_target_pairs={{0,8},{1,9},{8,16},{9,17},{16,24},{17,25},{2,10},{3,11},{10,18},{1... | collective-permute-start | bytes 786440 | tf_op jit(solution)/shard_map/ppermute | solution.py:482
  19.4 10.4 %collective-permute-start.1 = (bf16[256,512]{1,0:T(8,128)(2,1)}, bf16[256,512]{1,0:T(8,128)(2,1)S(1)}, u32[]{:S(2)}, u32[]{:S(2)}) collective-permute-start(bf16[256,512]{1,0:T(8,128)(2,1)} %get-tuple-element.50.refs_0_), channel_id=1, source_target_pairs={{0,1},{8,9},{16,17},{24,25},{2,3},{10,11},{18,19},{26,27},{4,5},{1... | collective-permute-start | bytes 786440 | tf_op jit(solution)/shard_map/ppermute | solution.py:482
  22.8 10.4 %collective-permute-start.2 = (bf16[160,512]{1,0:T(8,128)(2,1)}, bf16[160,512]{1,0:T(8,128)(2,1)S(1)}, u32[]{:S(2)}, u32[]{:S(2)}) collective-permute-start(bf16[160,512]{1,0:T(8,128)(2,1)} %get-tuple-element.55.refs_0_.refs_2_.extended_ref), channel_id=1, source_target_pairs={{0,1},{1,0},{2,3},{3,2},{4,5},{5,4},{6,7},{7,6},{8,9},{9,8},{10,11... | collective-permute-start | bytes 491528 | tf_op jit(solution)/shard_map/ppermute | solution.py:69
  25.2 10.2 %collective-permute-start.3 = (bf16[256,512]{1,0:T(8,128)(2,1)S(1)}, bf16[256,512]{1,0:T(8,128)(2,1)S(1)}, u32[]{:S(2)}, u32[]{:S(2)}) collective-permute-start(bf16[256,512]{1,0:T(8,128)(2,1)S(1)} %collective-permute-done.refs_1_), channel_id=1, source_target_pairs={{8,9},{9,8},{16,17},{17,16},{24,25},{25,24},{10,11},{11,10},{18,19... | collective-permute-start | bytes 786440 | tf_op jit(solution)/shard_map/ppermute | solution.py:482
  25.9 9.8 %collective-permute-start.4 = (bf16[256,512]{1,0:T(8,128)(2,1)S(1)}, bf16[256,512]{1,0:T(8,128)(2,1)S(1)}, u32[]{:S(2)}, u32[]{:S(2)}) collective-permute-start(bf16[256,512]{1,0:T(8,128)(2,1)S(1)} %collective-permute-done.refs_1_), channel_id=1, source_target_pairs={{9,16},{17,24},{11,18},{19,26},{13,20},{21,28},{15,22},{23,30}} | collective-permute-start | bytes 786440 | tf_op jit(solution)/shard_map/ppermute | solution.py:482
  26.6 9.1 %collective-permute-start.5 = (bf16[256,512]{1,0:T(8,128)(2,1)S(1)}, bf16[256,512]{1,0:T(8,128)(2,1)S(1)}, u32[]{:S(2)}, u32[]{:S(2)}) collective-permute-start(bf16[256,512]{1,0:T(8,128)(2,1)S(1)} %collective-permute-done.refs_1_), channel_id=1, source_target_pairs={{8,16},{9,17},{16,24},{17,25},{10,18},{11,19},{18,26},{19,27},{12,... | collective-permute-start | bytes 786440 | tf_op jit(solution)/shard_map/ppermute | solution.py:482
  29.8 0.6 copy-start.7
  30.4 0.9 %copy-start.3 = (bf16[256,512]{1,0:T(8,128)(2,1)S(1)}, bf16[256,512]{1,0:T(8,128)(2,1)}, u32[]{:S(2)}) copy-start(bf16[256,512]{1,0:T(8,128)(2,1)} %get-tuple-element.50.refs_0_) | copy-start | bytes 786436
  31.4 1.8 %copy-start.4 = (bf16[160,512]{1,0:T(8,128)(2,1)S(1)}, bf16[160,512]{1,0:T(8,128)(2,1)}, u32[]{:S(2)}) copy-start(bf16[160,512]{1,0:T(8,128)(2,1)} %get-tuple-element.55.refs_0_.refs_2_.extended_ref) | copy-start | bytes 491524
  33.2 2.5 %copy-start = (bf16[512,512]{1,0:T(8,128)(2,1)S(1)}, bf16[512,512]{1,0:T(8,128)(2,1)}, u32[]{:S(2)}) copy-start(bf16[512,512]{1,0:T(8,128)(2,1)} %proj_ref.1) | copy-start | bytes 1572868
  33.2 2.5 %copy-start.6 = (bf16[1,128,512]{2,1,0:T(8,128)(2,1)S(1)}, bf16[1,128,512]{2,1,0:T(8,128)(2,1)}, u32[]{:S(2)}) copy-start(bf16[1,128,512]{2,1,0:T(8,128)(2,1)} %param.15) | copy-start | bytes 393220
  33.8 3.1 %collective-permute-start.6 = (bf16[128,512]{1,0:T(8,128)(2,1)S(1)}, bf16[128,512]{1,0:T(8,128)(2,1)S(1)}, u32[]{:S(2)}, u32[]{:S(2)}) collective-permute-start(bf16[128,512]{1,0:T(8,128)(2,1)S(1)} %get-tuple-element.61), channel_id=1, source_target_pairs={{0,2},{2,0},{4,6},{6,4},{1,3},{3,1},{5,7},{7,5},{8,10},{10,8},{12,... | collective-permute-start | bytes 393224 | tf_op jit(solution)/shard_map/ppermute | solution.py:69
  33.8 6.4 %collective-permute-start.7 = (bf16[128,512]{1,0:T(8,128)(2,1)S(1)}, bf16[128,512]{1,0:T(8,128)(2,1)S(1)}, u32[]{:S(2)}, u32[]{:S(2)}) collective-permute-start(bf16[128,512]{1,0:T(8,128)(2,1)S(1)} %get-tuple-element.62), channel_id=1, source_target_pairs={{0,4},{2,6},{4,0},{6,2},{1,5},{3,7},{5,1},{7,3},{8,12},{10,14},{12... | collective-permute-start | bytes 393224 | tf_op jit(solution)/shard_map/ppermute | solution.py:69
  35.4 6.7 %collective-permute-start.8 = (bf16[128,512]{1,0:T(8,128)(2,1)S(1)}, bf16[128,512]{1,0:T(8,128)(2,1)S(1)}, u32[]{:S(2)}, u32[]{:S(2)}) collective-permute-start(bf16[128,512]{1,0:T(8,128)(2,1)S(1)} %get-tuple-element.63), channel_id=1, source_target_pairs={{0,6},{2,4},{4,2},{6,0},{1,7},{3,5},{5,3},{7,1},{8,14},{10,12},{12... | collective-permute-start | bytes 393224 | tf_op jit(solution)/shard_map/ppermute | solution.py:69
  42.1 7.5 %collective-permute-start.9 = (bf16[128,512]{1,0:T(8,128)(2,1)S(1)}, bf16[128,512]{1,0:T(8,128)(2,1)S(1)}, u32[]{:S(2)}, u32[]{:S(2)}) collective-permute-start(bf16[128,512]{1,0:T(8,128)(2,1)S(1)} %get-tuple-element.64.refs_1_), channel_id=1, source_target_pairs={{0,1},{1,0},{2,3},{3,2},{4,5},{5,4},{6,7},{7,6},{8,9},{9,8},{10,11... | collective-permute-start | bytes 393224 | tf_op jit(solution)/shard_map/ppermute | solution.py:69
  46.0 5.6 %collective-permute-start.13 = (bf16[64,512]{1,0:T(8,128)(2,1)S(1)}, bf16[64,512]{1,0:T(8,128)(2,1)S(1)}, u32[]{:S(2)}, u32[]{:S(2)}) collective-permute-start(bf16[64,512]{1,0:T(8,128)(2,1)S(1)} %get-tuple-element.74), channel_id=1, source_target_pairs={{0,2},{2,0},{4,6},{6,4},{1,3},{3,1},{5,7},{7,5},{8,10},{10,8},{12,... | collective-permute-start | bytes 196616 | tf_op jit(solution)/shard_map/ppermute | solution.py:69
  46.1 5.8 %collective-permute-start.14 = (bf16[64,512]{1,0:T(8,128)(2,1)S(1)}, bf16[64,512]{1,0:T(8,128)(2,1)S(1)}, u32[]{:S(2)}, u32[]{:S(2)}) collective-permute-start(bf16[64,512]{1,0:T(8,128)(2,1)S(1)} %get-tuple-element.75), channel_id=1, source_target_pairs={{0,4},{2,6},{4,0},{6,2},{1,5},{3,7},{5,1},{7,3},{8,12},{10,14},{12... | collective-permute-start | bytes 196616 | tf_op jit(solution)/shard_map/ppermute | solution.py:69
  47.7 4.2 %collective-permute-start.15 = (bf16[64,512]{1,0:T(8,128)(2,1)S(1)}, bf16[64,512]{1,0:T(8,128)(2,1)S(1)}, u32[]{:S(2)}, u32[]{:S(2)}) collective-permute-start(bf16[64,512]{1,0:T(8,128)(2,1)S(1)} %get-tuple-element.76), channel_id=1, source_target_pairs={{0,6},{2,4},{4,2},{6,0},{1,7},{3,5},{5,3},{7,1},{8,14},{10,12},{12... | collective-permute-start | bytes 196616 | tf_op jit(solution)/shard_map/ppermute | solution.py:69
  48.0 3.9 %copy-start.1 = (bf16[1,512,512]{2,1,0:T(8,128)(2,1)S(1)}, bf16[1,512,512]{2,1,0:T(8,128)(2,1)}, u32[]{:S(2)}) copy-start(bf16[1,512,512]{2,1,0:T(8,128)(2,1)} %param.19) | copy-start | bytes 1572868
  48.0 3.9 %copy-start.2 = (bf16[1,512,512]{2,1,0:T(8,128)(2,1)S(1)}, bf16[1,512,512]{2,1,0:T(8,128)(2,1)}, u32[]{:S(2)}) copy-start(bf16[1,512,512]{2,1,0:T(8,128)(2,1)} %param.20) | copy-start | bytes 1572868
  49.9 5.8 %collective-permute-start.10 = (bf16[64,512]{1,0:T(8,128)(2,1)S(1)}, bf16[64,512]{1,0:T(8,128)(2,1)S(1)}, u32[]{:S(2)}, u32[]{:S(2)}) collective-permute-start(bf16[64,512]{1,0:T(8,128)(2,1)S(1)} %get-tuple-element.66), channel_id=1, source_target_pairs={{0,2},{2,0},{4,6},{6,4},{1,3},{3,1},{5,7},{7,5},{8,10},{10,8},{12,... | collective-permute-start | bytes 196616 | tf_op jit(solution)/shard_map/ppermute | solution.py:69
  50.0 5.7 %collective-permute-start.11 = (bf16[64,512]{1,0:T(8,128)(2,1)S(1)}, bf16[64,512]{1,0:T(8,128)(2,1)S(1)}, u32[]{:S(2)}, u32[]{:S(2)}) collective-permute-start(bf16[64,512]{1,0:T(8,128)(2,1)S(1)} %get-tuple-element.67), channel_id=1, source_target_pairs={{0,4},{2,6},{4,0},{6,2},{1,5},{3,7},{5,1},{7,3},{8,12},{10,14},{12... | collective-permute-start | bytes 196616 | tf_op jit(solution)/shard_map/ppermute | solution.py:69
  51.6 4.1 %collective-permute-start.12 = (bf16[64,512]{1,0:T(8,128)(2,1)S(1)}, bf16[64,512]{1,0:T(8,128)(2,1)S(1)}, u32[]{:S(2)}, u32[]{:S(2)}) collective-permute-start(bf16[64,512]{1,0:T(8,128)(2,1)S(1)} %get-tuple-element.68), channel_id=1, source_target_pairs={{0,6},{2,4},{4,2},{6,0},{1,7},{3,5},{5,3},{7,1},{8,14},{10,12},{12... | collective-permute-start | bytes 196616 | tf_op jit(solution)/shard_map/ppermute | solution.py:69
  53.7 13.6 %collective-permute-start.16 = (bf16[128,512]{1,0:T(8,128)(2,1)S(1)}, bf16[128,512]{1,0:T(8,128)(2,1)S(1)}, u32[]{:S(2)}, u32[]{:S(2)}) collective-permute-start(bf16[128,512]{1,0:T(8,128)(2,1)S(1)} %get-tuple-element.82), channel_id=1, source_target_pairs={{0,2},{2,0},{4,6},{6,4},{1,3},{3,1},{5,7},{7,5},{8,10},{10,8},{12,... | collective-permute-start | bytes 393224 | tf_op jit(solution)/shard_map/ppermute | solution.py:69
  54.2 13.2 %collective-permute-start.17 = (bf16[128,512]{1,0:T(8,128)(2,1)S(1)}, bf16[128,512]{1,0:T(8,128)(2,1)S(1)}, u32[]{:S(2)}, u32[]{:S(2)}) collective-permute-start(bf16[128,512]{1,0:T(8,128)(2,1)S(1)} %get-tuple-element.83), channel_id=1, source_target_pairs={{0,4},{2,6},{4,0},{6,2},{1,5},{3,7},{5,1},{7,3},{8,12},{10,14},{12... | collective-permute-start | bytes 393224 | tf_op jit(solution)/shard_map/ppermute | solution.py:69
  55.7 11.7 %collective-permute-start.18 = (bf16[128,512]{1,0:T(8,128)(2,1)S(1)}, bf16[128,512]{1,0:T(8,128)(2,1)S(1)}, u32[]{:S(2)}, u32[]{:S(2)}) collective-permute-start(bf16[128,512]{1,0:T(8,128)(2,1)S(1)} %get-tuple-element.84), channel_id=1, source_target_pairs={{0,6},{2,4},{4,2},{6,0},{1,7},{3,5},{5,3},{7,1},{8,14},{10,12},{12... | collective-permute-start | bytes 393224 | tf_op jit(solution)/shard_map/ppermute | solution.py:69
  57.3 11.5 %collective-permute-start.19 = (bf16[2,64,512]{2,1,0:T(8,128)(2,1)S(1)}, bf16[2,64,512]{2,1,0:T(8,128)(2,1)S(1)}, u32[]{:S(2)}, u32[]{:S(2)}) collective-permute-start(bf16[2,64,512]{2,1,0:T(8,128)(2,1)S(1)} %get-tuple-element.89), channel_id=1, source_target_pairs={{0,24},{8,16},{16,8},{24,0},{1,25},{9,17},{17,9},{25,1},{2,26},{10... | collective-permute-start | bytes 393224 | tf_op jit(solution)/shard_map/ppermute | solution.py:69
  63.1 13.9 %collective-permute-start.20 = (bf16[2,64,512]{2,1,0:T(8,128)(2,1)S(1)}, bf16[2,64,512]{2,1,0:T(8,128)(2,1)S(1)}, u32[]{:S(2)}, u32[]{:S(2)}) collective-permute-start(bf16[2,64,512]{2,1,0:T(8,128)(2,1)S(1)} %get-tuple-element.90), channel_id=1, source_target_pairs={{0,16},{8,24},{16,0},{24,8},{1,17},{9,25},{17,1},{25,9},{2,18},{10... | collective-permute-start | bytes 393224 | tf_op jit(solution)/shard_map/ppermute | solution.py:69
  67.4 9.6 %collective-permute-start.21 = (bf16[2,64,512]{2,1,0:T(8,128)(2,1)S(1)}, bf16[2,64,512]{2,1,0:T(8,128)(2,1)S(1)}, u32[]{:S(2)}, u32[]{:S(2)}) collective-permute-start(bf16[2,64,512]{2,1,0:T(8,128)(2,1)S(1)} %get-tuple-element.91), channel_id=1, source_target_pairs={{0,8},{8,0},{16,24},{24,16},{1,9},{9,1},{17,25},{25,17},{2,10},{10... | collective-permute-start | bytes 393224 | tf_op jit(solution)/shard_map/ppermute | solution.py:69

commit v7 on v6

--- a/solution.py
+++ b/solution.py
@@ -122,39 +122,29 @@
     begin_ref,
     chosen_ref,
     held_router_ref,
-    tail_ref,
     held_lengths_ref,
     sems,
 ):
     tok, width = key_ref.shape
-    rest = tail_ref.shape[0]
     targets = (
         (choice_ref, chosen_ref),
-        (router_ref, held_router_ref),
         (lengths_ref, held_lengths_ref),
         (key_ref, pair_ref.at[pl.ds(0, tok), :]),
         (value_ref, pair_ref.at[pl.ds(tok, tok), :]),
         (grad_ref, extended_ref.at[pl.ds(0, tok), :]),
-        (tail_ref, extended_ref.at[pl.ds(tok, rest), :]),
+        (router_ref, held_router_ref),
     )
     copies = [
         pltpu.make_async_copy(source, target, sems.at[place])
         for place, (source, target) in enumerate(targets)
     ]
-    for copy in copies[:-1]:
+    for copy in copies:
         copy.start()
     copies[0].wait()
     chosen = jnp.broadcast_to(chosen_ref[...].astype(jnp.float32), (16, tok))
-    tail_ref[0:16, 0:tok] = chosen.astype(jnp.bfloat16)
-    tail_ref[0:16, tok:width] = jnp.zeros((16, width - tok), jnp.bfloat16)
+    extended_ref[tok : tok + 16, 0:tok] = chosen.astype(jnp.bfloat16)
+    extended_ref[tok : tok + 16, tok:width] = jnp.zeros((16, width - tok), jnp.bfloat16)
     copies[1].wait()
-    routed = held_router_ref[...].astype(jnp.float32)
-    spare = rest - 16 - routed.shape[0]
-    if spare:
-        routed = jnp.concatenate([routed, jnp.zeros((spare, width), jnp.float32)], axis=0)
-    tail_ref[16:rest, :] = routed.astype(jnp.bfloat16)
-    copies[-1].start()
-    copies[2].wait()
     position = rank_ref[0] * tok + lax.broadcasted_iota(jnp.int32, (1, tok), 1)
     begin = jnp.zeros((1, tok), jnp.int32)
     bound = jnp.int32(0)
@@ -162,7 +152,13 @@
         bound = bound + held_lengths_ref[0, doc]
         begin = jnp.maximum(begin, jnp.where(position >= bound, bound, 0))
     begin_ref[...] = begin
-    for copy in copies[3:]:
+    copies[5].wait()
+    routed = held_router_ref[...].astype(jnp.float32)
+    spare = extended_ref.shape[0] - tok - 16 - routed.shape[0]
+    if spare:
+        routed = jnp.concatenate([routed, jnp.zeros((spare, width), jnp.float32)], axis=0)
+    extended_ref[tok + 16 :, :] = routed.astype(jnp.bfloat16)
+    for copy in copies[2:5]:
         copy.wait()
 
 
@@ -302,7 +298,7 @@
 ):
     row_count, grad_count = counts
     row_refs, refs = refs[:row_count], refs[row_count:]
-    grad_refs, refs = refs[:grad_count], refs[grad_count:]
+    grad_refs, refs = refs[:grad_count][::-1], refs[grad_count:]
     own_rows = rep_list[0] == 0
     held_ref, refs = refs[-1], refs[:-1]
     if own_rows:
@@ -515,13 +511,12 @@
             shape((1, tok), jnp.int32),
         ],
         in_specs=[SMEM] + [HBM] * 6,
-        out_specs=[HBM, HBM, VMEM],
+        out_specs=[VMEM] * 3,
         scratch_shapes=[
             pltpu.VMEM((1, tok), jnp.int32),
             pltpu.VMEM((expert_count, width), jnp.bfloat16),
-            pltpu.VMEM((tail, width), jnp.bfloat16),
             pltpu.SMEM(doc_lengths.shape, jnp.int32),
-            pltpu.SemaphoreType.DMA((7,)),
+            pltpu.SemaphoreType.DMA((6,)),
         ],
         compiler_params=pltpu.CompilerParams(vmem_limit_bytes=60 * 1024 * 1024),
     )(
@@ -562,16 +557,17 @@
         else:
             rounds.append((arrays, entries))
         line = ahead
+    arrays = rounds[0][0]
+    arrays[-1], pinned = lax.optimization_barrier((arrays[-1], extendeds[0]))
+    extendeds = [pinned] + list(extendeds[1:])
     state = attend(rounds[0], state)
 
-    *held, pinned = lax.optimization_barrier((*state, extendeds[0]))
-    state, extendeds = held, [pinned] + list(extendeds[1:])
     sent_grads = call(
         functools.partial(dispatch_kernel, rep_count, tok, hot_capacity),
         [shape((rep_count * hot_capacity, width))] * expert_count,
         [SMEM] + [VMEM] * (2 * rep_count),
     )(own, *extendeds, *extendeds)
-    got_grads = merged(experts.exchange(sent_grads), MOST_PERMUTES)
+    got_grads = merged(experts.exchange(sent_grads), MOST_PERMUTES)[::-1]
 
     arrays, entries = rounds[-1]
     mixed, normed = call(

time: 77.9 us -> 64 us (0.82)
  Pallas kernels: 23.4 us -> 11.6 us
  starting transfers between devices: 31.9 us -> 28.3 us
    pallas_call x1, Pallas kernels: 13.6 us -> 1.88 us  [local(): pl.pallas_call(stack_kernel, out_shape=[shape((2 * tok, width)), shape((t...]
    ppermute x17, starting transfers between devices: 21.4 us -> 18 us  [exchange(): got[k] = lax.ppermute(chunks[k], self.axes, pairs)]
    unnamed x16 -> x18, local copies, waits for them, and re-layouts: 1.6 us -> 1.6 us
  transfers between devices with their start and end apart: 22 -> 22, of which waited for: 6 -> 8; matrix products, arithmetic and copies ran while one was open for 0% -> 0% of each run, Pallas kernels for 12% -> 14%
where the time goes in v7:
time: 64 us; the launch traced here: 63.1 us
  starting transfers between devices  28.3 us (44%)
  waiting for transfers between devices  20.4 us (32%)
  Pallas kernels  11.6 us (18%)
  local copies, waits for them, and re-layouts  1.6 us (2%)
  between operations  0.85 us (1%)
    ppermute x17, starting transfers between devices, exchange(): got[k] = lax.ppermute(chunks[k], self.axes, pairs)  18 us
    ppermute x17, waiting for transfers between devices, exchange(): got[k] = lax.ppermute(chunks[k], self.axes, pairs)  15.7 us
    ppermute x5, starting transfers between devices, send(): return lax.ppermute(array, ('seq', 'rep'), pairs)  10.4 us
    ppermute x5, waiting for transfers between devices, send(): return lax.ppermute(array, ('seq', 'rep'), pairs)  4.73 us
    pallas_call x2, Pallas kernels, expert_call(): call(functools.partial(expert_kernel, rep_count, rep_list, expert_count,...  3.49 us
    pallas_call x1, Pallas kernels, local(): pl.pallas_call(stack_kernel, out_shape=[shape((2 * tok, width)), shape((t...  1.88 us
    pallas_call x1, Pallas kernels, attend(): call(functools.partial(attend_kernel, len(arrays), not state), state_shap...  1.75 us
    unnamed x18, local copies, waits for them, and re-layouts  1.6 us
  transfers between devices with their start and end apart: 22, of which 8 were waited for; matrix products, arithmetic and copies ran while one was open for 0% of the time, Pallas kernels for 14%

profile of v7, /device:TPU:0, one launch (start us, length us, event | category | flops | bytes accessed | tf_op | source)
XLA Modules:
  0.0 63.1 jit_solution(1018089169788948262)
XLA Ops:
  0.6 1.9 %shard_map.138 = (bf16[256,512]{1,0:T(8,128)(2,1)}, bf16[160,512]{1,0:T(8,128)(2,1)}, s32[1,128]{1,0:T(1,128)}) custom-call(s32[1]{0:T(128)} %bitcast.7.rank_ref, s32[1,128]{1,0:T(1,128)} %bitcast.36, s32[1,8]{1,0:T(1,128)} %lengths_ref.1, bf16[4,512]{1,0:T(4,128)(2,1)} %bitcast.35, bf16[128,512]{1,0:T(8,128)(2,1)} %bitcast.32, bf16[128,512]{1,0:T(8,128)(2,1)} %bitcast.33, ...), custom_call_target="tpu_custom_call" | custom-call | tf_op jit(solution)/shard_map/pallas_call | solution.py:506
  2.5 4.9 %collective-permute-start.2 = (bf16[256,512]{1,0:T(8,128)(2,1)}, bf16[256,512]{1,0:T(8,128)(2,1)S(1)}, u32[]{:S(2)}, u32[]{:S(2)}) collective-permute-start(bf16[256,512]{1,0:T(8,128)(2,1)} %get-tuple-element.47.refs_0_), channel_id=1, source_target_pairs={{0,8},{1,9},{8,16},{9,17},{16,24},{17,25},{2,10},{3,11},{10,18},{1... | collective-permute-start | bytes 786440 | tf_op jit(solution)/shard_map/ppermute | solution.py:478
  7.5 3.4 %collective-permute-start = (bf16[256,512]{1,0:T(8,128)(2,1)}, bf16[256,512]{1,0:T(8,128)(2,1)S(1)}, u32[]{:S(2)}, u32[]{:S(2)}) collective-permute-start(bf16[256,512]{1,0:T(8,128)(2,1)} %get-tuple-element.47.refs_0_), channel_id=1, source_target_pairs={{0,1},{8,9},{16,17},{24,25},{2,3},{10,11},{18,19},{26,27},{4,5},{1... | collective-permute-start | bytes 786440 | tf_op jit(solution)/shard_map/ppermute | solution.py:478
  11.1 2.2 %collective-permute-done.2.refs_1_ = bf16[256,512]{1,0:T(8,128)(2,1)S(1)} collective-permute-done((bf16[256,512]{1,0:T(8,128)(2,1)}, bf16[256,512]{1,0:T(8,128)(2,1)S(1)}, u32[]{:S(2)}, u32[]{:S(2)}) %collective-permute-start.2) | collective-permute-done | bytes 262176 | tf_op jit(solution)/shard_map/ppermute | solution.py:478
  13.3 0.7 %collective-permute-start.3 = (bf16[256,512]{1,0:T(8,128)(2,1)S(1)}, bf16[256,512]{1,0:T(8,128)(2,1)S(1)}, u32[]{:S(2)}, u32[]{:S(2)}) collective-permute-start(bf16[256,512]{1,0:T(8,128)(2,1)S(1)} %collective-permute-done.2.refs_1_), channel_id=1, source_target_pairs={{8,9},{9,8},{16,17},{17,16},{24,25},{25,24},{10,11},{11,10},{18,19... | collective-permute-start | bytes 786440 | tf_op jit(solution)/shard_map/ppermute | solution.py:478
  14.0 0.7 %collective-permute-start.4 = (bf16[256,512]{1,0:T(8,128)(2,1)S(1)}, bf16[256,512]{1,0:T(8,128)(2,1)S(1)}, u32[]{:S(2)}, u32[]{:S(2)}) collective-permute-start(bf16[256,512]{1,0:T(8,128)(2,1)S(1)} %collective-permute-done.2.refs_1_), channel_id=1, source_target_pairs={{9,16},{17,24},{11,18},{19,26},{13,20},{21,28},{15,22},{23,30}} | collective-permute-start | bytes 786440 | tf_op jit(solution)/shard_map/ppermute | solution.py:478
  14.7 0.7 %collective-permute-start.5 = (bf16[256,512]{1,0:T(8,128)(2,1)S(1)}, bf16[256,512]{1,0:T(8,128)(2,1)S(1)}, u32[]{:S(2)}, u32[]{:S(2)}) collective-permute-start(bf16[256,512]{1,0:T(8,128)(2,1)S(1)} %collective-permute-done.2.refs_1_), channel_id=1, source_target_pairs={{8,16},{9,17},{16,24},{17,25},{10,18},{11,19},{18,26},{19,27},{12,... | collective-permute-start | bytes 786440 | tf_op jit(solution)/shard_map/ppermute | solution.py:478
  15.4 2.5 %collective-permute-done.refs_2_ = bf16[256,512]{1,0:T(8,128)(2,1)S(1)} collective-permute-done((bf16[256,512]{1,0:T(8,128)(2,1)}, bf16[256,512]{1,0:T(8,128)(2,1)S(1)}, u32[]{:S(2)}, u32[]{:S(2)}) %collective-permute-start) | collective-permute-done | bytes 262176 | tf_op jit(solution)/shard_map/ppermute | solution.py:478
  17.9 2.0 %collective-permute-done.1.refs_1_.refs_3_.refs_0_ = bf16[160,512]{1,0:T(8,128)(2,1)S(1)} collective-permute-done((bf16[160,512]{1,0:T(8,128)(2,1)}, bf16[160,512]{1,0:T(8,128)(2,1)S(1)}, u32[]{:S(2)}, u32[]{:S(2)}) %collective-permute-start.1) | collective-permute-done | bytes 163872 | tf_op jit(solution)/shard_map/ppermute | solution.py:69
  20.0 0.9 %copy-done.4 = bf16[160,512]{1,0:T(8,128)(2,1)S(1)} copy-done((bf16[160,512]{1,0:T(8,128)(2,1)S(1)}, bf16[160,512]{1,0:T(8,128)(2,1)}, u32[]{:S(2)}) %copy-start.4) | copy-done | bytes 163864
  20.9 0.6 shard_map.141
  21.5 1.6 %collective-permute-start.7 = (bf16[128,512]{1,0:T(8,128)(2,1)S(1)}, bf16[128,512]{1,0:T(8,128)(2,1)S(1)}, u32[]{:S(2)}, u32[]{:S(2)}) collective-permute-start(bf16[128,512]{1,0:T(8,128)(2,1)S(1)} %get-tuple-element.57), channel_id=1, source_target_pairs={{0,4},{2,6},{4,0},{6,2},{1,5},{3,7},{5,1},{7,3},{8,12},{10,14},{12... | collective-permute-start | bytes 393224 | tf_op jit(solution)/shard_map/ppermute | solution.py:69
  23.1 0.7 %copy-done.8 = s32[1,128]{1,0:T(1,128)S(1)} copy-done((s32[1,128]{1,0:T(1,128)S(1)}, s32[1,128]{1,0:T(1,128)}, u32[]{:S(2)}) %copy-start.8) | copy-done | bytes 536
  23.8 1.8 %shard_map.139 = (f32[16,128]{1,0:T(8,128)S(1)}, f32[16,128]{1,0:T(8,128)S(1)}, f32[512,128]{1,0:T(8,128)S(1)}) custom-call(s32[4]{0:T(128)S(1)} %pad_add_fusion.2.block_ref, s32[1,128]{1,0:T(1,128)S(1)} %copy-done.8, bf16[128,512]{1,0:T(8,128)(2,1)S(1)} %bitcast.29, bf16[256,512]{1,0:T(8,128)(2,1)S(1)} %copy-done.3, ...), custom_call_target="tpu_custom_call" | custom-call | flops 2000000000 | tf_op jit(solution)/shard_map/pallas_call | solution.py:497
  25.9 1.1 %shard_map.140 = (bf16[128,512]{1,0:T(8,128)(2,1)S(1)}, bf16[128,512]{1,0:T(8,128)(2,1)S(1)}) custom-call(s32[4]{0:T(128)S(1)} %pad_add_fusion.1.block_ref, s32[1,128]{1,0:T(1,128)S(1)} %copy-done.8, bf16[128,512]{1,0:T(8,128)(2,1)S(1)} %bitcast.30, bf16[128,512]{1,0:T(8,128)(2,1)S(1)} %bitcast.31, bf16[512,512]{1,0:T(8,128)(2,1)S(1)} %copy-done, ...), custom_call_target="tpu_custom_call" | custom-call | flops 5000000000 | tf_op jit(solution)/shard_map/pallas_call | solution.py:573
  27.2 2.9 %collective-permute-done.7.refs_5_ = bf16[128,512]{1,0:T(8,128)(2,1)S(1)} collective-permute-done((bf16[128,512]{1,0:T(8,128)(2,1)S(1)}, bf16[128,512]{1,0:T(8,128)(2,1)S(1)}, u32[]{:S(2)}, u32[]{:S(2)}) %collective-permute-start.7) | collective-permute-done | bytes 131104 | tf_op jit(solution)/shard_map/ppermute | solution.py:69
  30.1 2.4 %collective-permute-start.9 = (bf16[128,512]{1,0:T(8,128)(2,1)S(1)}, bf16[128,512]{1,0:T(8,128)(2,1)S(1)}, u32[]{:S(2)}, u32[]{:S(2)}) collective-permute-start(bf16[128,512]{1,0:T(8,128)(2,1)S(1)} %get-tuple-element.60.refs_1_), channel_id=1, source_target_pairs={{0,1},{1,0},{2,3},{3,2},{4,5},{5,4},{6,7},{7,6},{8,9},{9,8},{10,11... | collective-permute-start | bytes 393224 | tf_op jit(solution)/shard_map/ppermute | solution.py:69
  33.0 1.7 %collective-permute-start.15 = (bf16[64,512]{1,0:T(8,128)(2,1)S(1)}, bf16[64,512]{1,0:T(8,128)(2,1)S(1)}, u32[]{:S(2)}, u32[]{:S(2)}) collective-permute-start(bf16[64,512]{1,0:T(8,128)(2,1)S(1)} %get-tuple-element.72), channel_id=1, source_target_pairs={{0,6},{2,4},{4,2},{6,0},{1,7},{3,5},{5,3},{7,1},{8,14},{10,12},{12... | collective-permute-start | bytes 196616 | tf_op jit(solution)/shard_map/ppermute | solution.py:69
  34.9 1.3 %collective-permute-done.9.refs_1_ = bf16[128,512]{1,0:T(8,128)(2,1)S(1)} collective-permute-done((bf16[128,512]{1,0:T(8,128)(2,1)S(1)}, bf16[128,512]{1,0:T(8,128)(2,1)S(1)}, u32[]{:S(2)}, u32[]{:S(2)}) %collective-permute-start.9) | collective-permute-done | bytes 131104 | tf_op jit(solution)/shard_map/ppermute | solution.py:69
  36.6 0.5 collective-permute-start.11
  37.1 1.4 %collective-permute-start.12 = (bf16[64,512]{1,0:T(8,128)(2,1)S(1)}, bf16[64,512]{1,0:T(8,128)(2,1)S(1)}, u32[]{:S(2)}, u32[]{:S(2)}) collective-permute-start(bf16[64,512]{1,0:T(8,128)(2,1)S(1)} %get-tuple-element.64), channel_id=1, source_target_pairs={{0,6},{2,4},{4,2},{6,0},{1,7},{3,5},{5,3},{7,1},{8,14},{10,12},{12... | collective-permute-start | bytes 196616 | tf_op jit(solution)/shard_map/ppermute | solution.py:69
  38.5 1.9 %shard_map.144 = (bf16[128,512]{1,0:T(8,128)(2,1)S(1)}, bf16[128,512]{1,0:T(8,128)(2,1)S(1)}, bf16[128,512]{1,0:T(8,128)(2,1)S(1)}, bf16[128,512]{1,0:T(8,128)(2...) custom-call(s32[1]{0:T(128)} %bitcast.own_ref, s32[4]{0:T(128)S(1)} %pad_add_fusion.part_ref, ...), custom_call_target="tpu_custom_call" | custom-call | flops 2000000000 | tf_op jit(solution)/shard_map/pallas_call | solution.py:596
  40.4 0.4 collective-permute-start.16
  40.8 0.4 collective-permute-start.17
  41.2 1.1 %collective-permute-start.18 = (bf16[128,512]{1,0:T(8,128)(2,1)S(1)}, bf16[128,512]{1,0:T(8,128)(2,1)S(1)}, u32[]{:S(2)}, u32[]{:S(2)}) collective-permute-start(bf16[128,512]{1,0:T(8,128)(2,1)S(1)} %get-tuple-element.80), channel_id=1, source_target_pairs={{0,6},{2,4},{4,2},{6,0},{1,7},{3,5},{5,3},{7,1},{8,14},{10,12},{12... | collective-permute-start | bytes 393224 | tf_op jit(solution)/shard_map/ppermute | solution.py:69
  42.3 1.6 %shard_map.145 = (bf16[2,64,512]{2,1,0:T(8,128)(2,1)S(1)}, bf16[2,64,512]{2,1,0:T(8,128)(2,1)S(1)}, bf16[2,64,512]{2,1,0:T(8,128)(2,1)S(1)}, f32[2,64,512]{2,1,0:T(8,128)S(1)}) custom-call(s32[1]{0:T(128)} %bitcast.own_ref, s32[4]{0:T(128)S(1)} %pad_add_fusion.part_ref, bf16[512,512]{1,0:T(8,128)(2,1)S(1)} %bitcast.26, bf16[512,512]{1,0:T(8,128)(2,1)S(1)} %bitcast.28, ...), custom_call_target="tpu_custom_call" | custom-call | flops 2000000000 | tf_op jit(solution)/shard_map/pallas_call | solution.py:596
  44.0 6.0 %collective-permute-start.19 = (bf16[2,64,512]{2,1,0:T(8,128)(2,1)S(1)}, bf16[2,64,512]{2,1,0:T(8,128)(2,1)S(1)}, u32[]{:S(2)}, u32[]{:S(2)}) collective-permute-start(bf16[2,64,512]{2,1,0:T(8,128)(2,1)S(1)} %get-tuple-element.85), channel_id=1, source_target_pairs={{0,24},{8,16},{16,8},{24,0},{1,25},{9,17},{17,9},{25,1},{2,26},{10... | collective-permute-start | bytes 393224 | tf_op jit(solution)/shard_map/ppermute | solution.py:69
  49.9 1.4 %collective-permute-start.20 = (bf16[2,64,512]{2,1,0:T(8,128)(2,1)S(1)}, bf16[2,64,512]{2,1,0:T(8,128)(2,1)S(1)}, u32[]{:S(2)}, u32[]{:S(2)}) collective-permute-start(bf16[2,64,512]{2,1,0:T(8,128)(2,1)S(1)} %get-tuple-element.86), channel_id=1, source_target_pairs={{0,16},{8,24},{16,0},{24,8},{1,17},{9,25},{17,1},{25,9},{2,18},{10... | collective-permute-start | bytes 393224 | tf_op jit(solution)/shard_map/ppermute | solution.py:69
  51.7 1.4 %shard_map.146 = (bf16[128,512]{1,0:T(8,128)(2,1)}, bf16[128,512]{1,0:T(8,128)(2,1)}) custom-call(s32[1]{0:T(128)} %bitcast.own_ref, bf16[128,512]{1,0:T(8,128)(2,1)S(1)} %get-tuple-element.76.mixed_ref, bf16[160,512]{1,0:T(8,128)(2,1)S(1)} %copy-done.5, bf16[128,512]{1,0:T(8,128)(2,1)S(1)} %get-tuple-element.77.refs_0_, ...), custom_call_target="tpu_custom_call" | custom-call | flops 1500000000 | tf_op jit(solution)/shard_map/pallas_call | solution.py:629
  53.1 0.9 %collective-permute-done.19.refs_0_ = bf16[2,64,512]{2,1,0:T(8,128)(2,1)S(1)} collective-permute-done((bf16[2,64,512]{2,1,0:T(8,128)(2,1)S(1)}, bf16[2,64,512]{2,1,0:T(8,128)(2,1)S(1)}, u32[]{:S(2)}, u32[]{:S(2)}) %collective-permute-start.19) | collective-permute-done | bytes 131104 | tf_op jit(solution)/shard_map/ppermute | solution.py:69
  54.0 8.3 %collective-permute-done.20.refs_1_ = bf16[2,64,512]{2,1,0:T(8,128)(2,1)S(1)} collective-permute-done((bf16[2,64,512]{2,1,0:T(8,128)(2,1)S(1)}, bf16[2,64,512]{2,1,0:T(8,128)(2,1)S(1)}, u32[]{:S(2)}, u32[]{:S(2)}) %collective-permute-start.20) | collective-permute-done | bytes 131104 | tf_op jit(solution)/shard_map/ppermute | solution.py:69
  62.4 0.7 %shard_map.147 = (f32[64,512]{1,0:T(8,128)}, f32[64,512]{1,0:T(8,128)}) custom-call(f32[2,64,512]{2,1,0:T(8,128)S(1)} %get-tuple-element.84.kept_ref, bf16[2,64,512]{2,1,0:T(8,128)(2,1)S(1)} %collective-permute-done.19.refs_0_, bf16[2,64,512]{2,1,0:T(8,128)(2,1)S(1)} %collective-permute-done.20.refs_1_, bf16[2,64,512]{2,1,0:T(8,128)(2,1)S(1)} %collective-permute-done.21.refs_2_), custom_call_target="tpu_custom_call" | custom-call | flops 500000000 | tf_op jit(solution)/shard_map/pallas_call | solution.py:636
  (43 shorter events, 2.3 us)
Async XLA Ops:
  2.5 10.8 %collective-permute-start.2 = (bf16[256,512]{1,0:T(8,128)(2,1)}, bf16[256,512]{1,0:T(8,128)(2,1)S(1)}, u32[]{:S(2)}, u32[]{:S(2)}) collective-permute-start(bf16[256,512]{1,0:T(8,128)(2,1)} %get-tuple-element.47.refs_0_), channel_id=1, source_target_pairs={{0,8},{1,9},{8,16},{9,17},{16,24},{17,25},{2,10},{3,11},{10,18},{1... | collective-permute-start | bytes 786440 | tf_op jit(solution)/shard_map/ppermute | solution.py:478
  7.5 10.4 %collective-permute-start = (bf16[256,512]{1,0:T(8,128)(2,1)}, bf16[256,512]{1,0:T(8,128)(2,1)S(1)}, u32[]{:S(2)}, u32[]{:S(2)}) collective-permute-start(bf16[256,512]{1,0:T(8,128)(2,1)} %get-tuple-element.47.refs_0_), channel_id=1, source_target_pairs={{0,1},{8,9},{16,17},{24,25},{2,3},{10,11},{18,19},{26,27},{4,5},{1... | collective-permute-start | bytes 786440 | tf_op jit(solution)/shard_map/ppermute | solution.py:478
  10.9 9.1 %collective-permute-start.1 = (bf16[160,512]{1,0:T(8,128)(2,1)}, bf16[160,512]{1,0:T(8,128)(2,1)S(1)}, u32[]{:S(2)}, u32[]{:S(2)}) collective-permute-start(bf16[160,512]{1,0:T(8,128)(2,1)} %get-tuple-element.49.refs_0_.refs_2_.extended_ref), channel_id=1, source_target_pairs={{0,1},{1,0},{2,3},{3,2},{4,5},{5,4},{6,7},{7,6},{8,9},{9,8},{10,11... | collective-permute-start | bytes 491528 | tf_op jit(solution)/shard_map/ppermute | solution.py:69
  13.3 12.2 %collective-permute-start.3 = (bf16[256,512]{1,0:T(8,128)(2,1)S(1)}, bf16[256,512]{1,0:T(8,128)(2,1)S(1)}, u32[]{:S(2)}, u32[]{:S(2)}) collective-permute-start(bf16[256,512]{1,0:T(8,128)(2,1)S(1)} %collective-permute-done.2.refs_1_), channel_id=1, source_target_pairs={{8,9},{9,8},{16,17},{17,16},{24,25},{25,24},{10,11},{11,10},{18,19... | collective-permute-start | bytes 786440 | tf_op jit(solution)/shard_map/ppermute | solution.py:478
  14.0 11.9 %collective-permute-start.4 = (bf16[256,512]{1,0:T(8,128)(2,1)S(1)}, bf16[256,512]{1,0:T(8,128)(2,1)S(1)}, u32[]{:S(2)}, u32[]{:S(2)}) collective-permute-start(bf16[256,512]{1,0:T(8,128)(2,1)S(1)} %collective-permute-done.2.refs_1_), channel_id=1, source_target_pairs={{9,16},{17,24},{11,18},{19,26},{13,20},{21,28},{15,22},{23,30}} | collective-permute-start | bytes 786440 | tf_op jit(solution)/shard_map/ppermute | solution.py:478
  14.7 11.2 %collective-permute-start.5 = (bf16[256,512]{1,0:T(8,128)(2,1)S(1)}, bf16[256,512]{1,0:T(8,128)(2,1)S(1)}, u32[]{:S(2)}, u32[]{:S(2)}) collective-permute-start(bf16[256,512]{1,0:T(8,128)(2,1)S(1)} %collective-permute-done.2.refs_1_), channel_id=1, source_target_pairs={{8,16},{9,17},{16,24},{17,25},{10,18},{11,19},{18,26},{19,27},{12,... | collective-permute-start | bytes 786440 | tf_op jit(solution)/shard_map/ppermute | solution.py:478
  20.0 0.9 %copy-start.4 = (bf16[160,512]{1,0:T(8,128)(2,1)S(1)}, bf16[160,512]{1,0:T(8,128)(2,1)}, u32[]{:S(2)}) copy-start(bf16[160,512]{1,0:T(8,128)(2,1)} %get-tuple-element.49.refs_0_.refs_2_.extended_ref) | copy-start | bytes 491524
  20.9 2.2 %copy-start.3 = (bf16[256,512]{1,0:T(8,128)(2,1)S(1)}, bf16[256,512]{1,0:T(8,128)(2,1)}, u32[]{:S(2)}) copy-start(bf16[256,512]{1,0:T(8,128)(2,1)} %get-tuple-element.47.refs_0_) | copy-start | bytes 786436
  20.9 2.2 %copy-start.6 = (bf16[1,128,512]{2,1,0:T(8,128)(2,1)S(1)}, bf16[1,128,512]{2,1,0:T(8,128)(2,1)}, u32[]{:S(2)}) copy-start(bf16[1,128,512]{2,1,0:T(8,128)(2,1)} %param.11) | copy-start | bytes 393220
  21.5 5.8 %collective-permute-start.6 = (bf16[128,512]{1,0:T(8,128)(2,1)S(1)}, bf16[128,512]{1,0:T(8,128)(2,1)S(1)}, u32[]{:S(2)}, u32[]{:S(2)}) collective-permute-start(bf16[128,512]{1,0:T(8,128)(2,1)S(1)} %get-tuple-element.56), channel_id=1, source_target_pairs={{0,6},{2,4},{4,2},{6,0},{1,7},{3,5},{5,3},{7,1},{8,14},{10,12},{12... | collective-permute-start | bytes 393224 | tf_op jit(solution)/shard_map/ppermute | solution.py:69
  21.5 8.6 %collective-permute-start.7 = (bf16[128,512]{1,0:T(8,128)(2,1)S(1)}, bf16[128,512]{1,0:T(8,128)(2,1)S(1)}, u32[]{:S(2)}, u32[]{:S(2)}) collective-permute-start(bf16[128,512]{1,0:T(8,128)(2,1)S(1)} %get-tuple-element.57), channel_id=1, source_target_pairs={{0,4},{2,6},{4,0},{6,2},{1,5},{3,7},{5,1},{7,3},{8,12},{10,14},{12... | collective-permute-start | bytes 393224 | tf_op jit(solution)/shard_map/ppermute | solution.py:69
  23.1 0.7 %copy-start.8 = (s32[1,128]{1,0:T(1,128)S(1)}, s32[1,128]{1,0:T(1,128)}, u32[]{:S(2)}) copy-start(s32[1,128]{1,0:T(1,128)} %get-tuple-element.50.begin_ref) | copy-start | bytes 1540
  23.8 2.1 %copy-start = (bf16[512,512]{1,0:T(8,128)(2,1)S(1)}, bf16[512,512]{1,0:T(8,128)(2,1)}, u32[]{:S(2)}) copy-start(bf16[512,512]{1,0:T(8,128)(2,1)} %proj_ref.1) | copy-start | bytes 1572868
  23.8 2.1 %copy-start.7 = (bf16[1,128,512]{2,1,0:T(8,128)(2,1)S(1)}, bf16[1,128,512]{2,1,0:T(8,128)(2,1)}, u32[]{:S(2)}) copy-start(bf16[1,128,512]{2,1,0:T(8,128)(2,1)} %param.15) | copy-start | bytes 393220
  25.6 4.6 %collective-permute-start.8 = (bf16[128,512]{1,0:T(8,128)(2,1)S(1)}, bf16[128,512]{1,0:T(8,128)(2,1)S(1)}, u32[]{:S(2)}, u32[]{:S(2)}) collective-permute-start(bf16[128,512]{1,0:T(8,128)(2,1)S(1)} %get-tuple-element.58), channel_id=1, source_target_pairs={{0,2},{2,0},{4,6},{6,4},{1,3},{3,1},{5,7},{7,5},{8,10},{10,8},{12,... | collective-permute-start | bytes 393224 | tf_op jit(solution)/shard_map/ppermute | solution.py:69
  25.9 6.6 %copy-start.5 = (bf16[160,512]{1,0:T(8,128)(2,1)S(1)}, bf16[160,512]{1,0:T(8,128)(2,1)}, u32[]{:S(2)}) copy-start(bf16[160,512]{1,0:T(8,128)(2,1)} %get-tuple-element.49.refs_0_.refs_2_.extended_ref) | copy-start | bytes 491524
  30.1 6.1 %collective-permute-start.9 = (bf16[128,512]{1,0:T(8,128)(2,1)S(1)}, bf16[128,512]{1,0:T(8,128)(2,1)S(1)}, u32[]{:S(2)}, u32[]{:S(2)}) collective-permute-start(bf16[128,512]{1,0:T(8,128)(2,1)S(1)} %get-tuple-element.60.refs_1_), channel_id=1, source_target_pairs={{0,1},{1,0},{2,3},{3,2},{4,5},{5,4},{6,7},{7,6},{8,9},{9,8},{10,11... | collective-permute-start | bytes 393224 | tf_op jit(solution)/shard_map/ppermute | solution.py:69
  32.9 4.2 %collective-permute-start.13 = (bf16[64,512]{1,0:T(8,128)(2,1)S(1)}, bf16[64,512]{1,0:T(8,128)(2,1)S(1)}, u32[]{:S(2)}, u32[]{:S(2)}) collective-permute-start(bf16[64,512]{1,0:T(8,128)(2,1)S(1)} %get-tuple-element.70), channel_id=1, source_target_pairs={{0,2},{2,0},{4,6},{6,4},{1,3},{3,1},{5,7},{7,5},{8,10},{10,8},{12,... | collective-permute-start | bytes 196616 | tf_op jit(solution)/shard_map/ppermute | solution.py:69
  32.9 5.6 %collective-permute-start.14 = (bf16[64,512]{1,0:T(8,128)(2,1)S(1)}, bf16[64,512]{1,0:T(8,128)(2,1)S(1)}, u32[]{:S(2)}, u32[]{:S(2)}) collective-permute-start(bf16[64,512]{1,0:T(8,128)(2,1)S(1)} %get-tuple-element.71), channel_id=1, source_target_pairs={{0,4},{2,6},{4,0},{6,2},{1,5},{3,7},{5,1},{7,3},{8,12},{10,14},{12... | collective-permute-start | bytes 196616 | tf_op jit(solution)/shard_map/ppermute | solution.py:69
  33.0 5.5 %collective-permute-start.15 = (bf16[64,512]{1,0:T(8,128)(2,1)S(1)}, bf16[64,512]{1,0:T(8,128)(2,1)S(1)}, u32[]{:S(2)}, u32[]{:S(2)}) collective-permute-start(bf16[64,512]{1,0:T(8,128)(2,1)S(1)} %get-tuple-element.72), channel_id=1, source_target_pairs={{0,6},{2,4},{4,2},{6,0},{1,7},{3,5},{5,3},{7,1},{8,14},{10,12},{12... | collective-permute-start | bytes 196616 | tf_op jit(solution)/shard_map/ppermute | solution.py:69
  34.9 3.6 %copy-start.1 = (bf16[1,512,512]{2,1,0:T(8,128)(2,1)S(1)}, bf16[1,512,512]{2,1,0:T(8,128)(2,1)}, u32[]{:S(2)}) copy-start(bf16[1,512,512]{2,1,0:T(8,128)(2,1)} %param.19) | copy-start | bytes 1572868
  34.9 3.6 %copy-start.2 = (bf16[1,512,512]{2,1,0:T(8,128)(2,1)S(1)}, bf16[1,512,512]{2,1,0:T(8,128)(2,1)}, u32[]{:S(2)}) copy-start(bf16[1,512,512]{2,1,0:T(8,128)(2,1)} %param.20) | copy-start | bytes 1572868
  36.6 4.6 %collective-permute-start.10 = (bf16[64,512]{1,0:T(8,128)(2,1)S(1)}, bf16[64,512]{1,0:T(8,128)(2,1)S(1)}, u32[]{:S(2)}, u32[]{:S(2)}) collective-permute-start(bf16[64,512]{1,0:T(8,128)(2,1)S(1)} %get-tuple-element.62), channel_id=1, source_target_pairs={{0,2},{2,0},{4,6},{6,4},{1,3},{3,1},{5,7},{7,5},{8,10},{10,8},{12,... | collective-permute-start | bytes 196616 | tf_op jit(solution)/shard_map/ppermute | solution.py:69
  36.6 5.7 %collective-permute-start.11 = (bf16[64,512]{1,0:T(8,128)(2,1)S(1)}, bf16[64,512]{1,0:T(8,128)(2,1)S(1)}, u32[]{:S(2)}, u32[]{:S(2)}) collective-permute-start(bf16[64,512]{1,0:T(8,128)(2,1)S(1)} %get-tuple-element.63), channel_id=1, source_target_pairs={{0,4},{2,6},{4,0},{6,2},{1,5},{3,7},{5,1},{7,3},{8,12},{10,14},{12... | collective-permute-start | bytes 196616 | tf_op jit(solution)/shard_map/ppermute | solution.py:69
  37.1 5.2 %collective-permute-start.12 = (bf16[64,512]{1,0:T(8,128)(2,1)S(1)}, bf16[64,512]{1,0:T(8,128)(2,1)S(1)}, u32[]{:S(2)}, u32[]{:S(2)}) collective-permute-start(bf16[64,512]{1,0:T(8,128)(2,1)S(1)} %get-tuple-element.64), channel_id=1, source_target_pairs={{0,6},{2,4},{4,2},{6,0},{1,7},{3,5},{5,3},{7,1},{8,14},{10,12},{12... | collective-permute-start | bytes 196616 | tf_op jit(solution)/shard_map/ppermute | solution.py:69
  40.4 11.0 %collective-permute-start.16 = (bf16[128,512]{1,0:T(8,128)(2,1)S(1)}, bf16[128,512]{1,0:T(8,128)(2,1)S(1)}, u32[]{:S(2)}, u32[]{:S(2)}) collective-permute-start(bf16[128,512]{1,0:T(8,128)(2,1)S(1)} %get-tuple-element.78), channel_id=1, source_target_pairs={{0,2},{2,0},{4,6},{6,4},{1,3},{3,1},{5,7},{7,5},{8,10},{10,8},{12,... | collective-permute-start | bytes 393224 | tf_op jit(solution)/shard_map/ppermute | solution.py:69
  40.8 10.9 %collective-permute-start.17 = (bf16[128,512]{1,0:T(8,128)(2,1)S(1)}, bf16[128,512]{1,0:T(8,128)(2,1)S(1)}, u32[]{:S(2)}, u32[]{:S(2)}) collective-permute-start(bf16[128,512]{1,0:T(8,128)(2,1)S(1)} %get-tuple-element.79), channel_id=1, source_target_pairs={{0,4},{2,6},{4,0},{6,2},{1,5},{3,7},{5,1},{7,3},{8,12},{10,14},{12... | collective-permute-start | bytes 393224 | tf_op jit(solution)/shard_map/ppermute | solution.py:69
  41.2 10.5 %collective-permute-start.18 = (bf16[128,512]{1,0:T(8,128)(2,1)S(1)}, bf16[128,512]{1,0:T(8,128)(2,1)S(1)}, u32[]{:S(2)}, u32[]{:S(2)}) collective-permute-start(bf16[128,512]{1,0:T(8,128)(2,1)S(1)} %get-tuple-element.80), channel_id=1, source_target_pairs={{0,6},{2,4},{4,2},{6,0},{1,7},{3,5},{5,3},{7,1},{8,14},{10,12},{12... | collective-permute-start | bytes 393224 | tf_op jit(solution)/shard_map/ppermute | solution.py:69
  44.0 10.1 %collective-permute-start.19 = (bf16[2,64,512]{2,1,0:T(8,128)(2,1)S(1)}, bf16[2,64,512]{2,1,0:T(8,128)(2,1)S(1)}, u32[]{:S(2)}, u32[]{:S(2)}) collective-permute-start(bf16[2,64,512]{2,1,0:T(8,128)(2,1)S(1)} %get-tuple-element.85), channel_id=1, source_target_pairs={{0,24},{8,16},{16,8},{24,0},{1,25},{9,17},{17,9},{25,1},{2,26},{10... | collective-permute-start | bytes 393224 | tf_op jit(solution)/shard_map/ppermute | solution.py:69
  49.9 12.4 %collective-permute-start.20 = (bf16[2,64,512]{2,1,0:T(8,128)(2,1)S(1)}, bf16[2,64,512]{2,1,0:T(8,128)(2,1)S(1)}, u32[]{:S(2)}, u32[]{:S(2)}) collective-permute-start(bf16[2,64,512]{2,1,0:T(8,128)(2,1)S(1)} %get-tuple-element.86), channel_id=1, source_target_pairs={{0,16},{8,24},{16,0},{24,8},{1,17},{9,25},{17,1},{25,9},{2,18},{10... | collective-permute-start | bytes 393224 | tf_op jit(solution)/shard_map/ppermute | solution.py:69
  51.3 11.0 %collective-permute-start.21 = (bf16[2,64,512]{2,1,0:T(8,128)(2,1)S(1)}, bf16[2,64,512]{2,1,0:T(8,128)(2,1)S(1)}, u32[]{:S(2)}, u32[]{:S(2)}) collective-permute-start(bf16[2,64,512]{2,1,0:T(8,128)(2,1)S(1)} %get-tuple-element.87), channel_id=1, source_target_pairs={{0,8},{8,0},{16,24},{24,16},{1,9},{9,1},{17,25},{25,17},{2,10},{10... | collective-permute-start | bytes 393224 | tf_op jit(solution)/shard_map/ppermute | solution.py:69

commit v8 on v5

--- a/solution.py
+++ b/solution.py
@@ -110,13 +110,14 @@
 
 
 def stack_kernel(
-    rank_ref,
+    ranks_ref,
     choice_ref,
     lengths_ref,
     router_ref,
     key_ref,
     value_ref,
     grad_ref,
+    query_ref,
     pair_ref,
     extended_ref,
     begin_ref,
@@ -132,6 +133,7 @@
         (key_ref, pair_ref.at[pl.ds(0, tok), :]),
         (value_ref, pair_ref.at[pl.ds(tok, tok), :]),
         (grad_ref, extended_ref.at[pl.ds(0, tok), :]),
+        (query_ref, extended_ref.at[pl.ds(tok, tok), :]),
         (router_ref, held_router_ref),
     )
     copies = [
@@ -142,77 +144,84 @@
         copy.start()
     copies[0].wait()
     chosen = jnp.broadcast_to(chosen_ref[...].astype(jnp.float32), (16, tok))
-    extended_ref[tok : tok + 16, 0:tok] = chosen.astype(jnp.bfloat16)
-    extended_ref[tok : tok + 16, tok:width] = jnp.zeros((16, width - tok), jnp.bfloat16)
+    extended_ref[2 * tok : 2 * tok + 16, 0:tok] = chosen.astype(jnp.bfloat16)
+    extended_ref[2 * tok : 2 * tok + 16, tok:width] = jnp.zeros((16, width - tok), jnp.bfloat16)
     copies[1].wait()
-    position = rank_ref[0] * tok + lax.broadcasted_iota(jnp.int32, (1, tok), 1)
-    begin = jnp.zeros((1, tok), jnp.int32)
-    bound = jnp.int32(0)
-    for doc in range(held_lengths_ref.shape[1] - 1):
-        bound = bound + held_lengths_ref[0, doc]
-        begin = jnp.maximum(begin, jnp.where(position >= bound, bound, 0))
-    begin_ref[...] = begin
-    copies[5].wait()
+    for k in range(begin_ref.shape[0]):
+        position = ranks_ref[k] * tok + lax.broadcasted_iota(jnp.int32, (1, tok), 1)
+        begin = jnp.zeros((1, tok), jnp.int32)
+        bound = jnp.int32(0)
+        for doc in range(held_lengths_ref.shape[1] - 1):
+            bound = bound + held_lengths_ref[0, doc]
+            begin = jnp.maximum(begin, jnp.where(position >= bound, bound, 0))
+        begin_ref[k : k + 1, :] = begin
+    copies[6].wait()
     routed = held_router_ref[...].astype(jnp.float32)
-    spare = extended_ref.shape[0] - tok - 16 - routed.shape[0]
+    spare = extended_ref.shape[0] - 2 * tok - 16 - routed.shape[0]
     if spare:
         routed = jnp.concatenate([routed, jnp.zeros((spare, width), jnp.float32)], axis=0)
-    extended_ref[tok + 16 :, :] = routed.astype(jnp.bfloat16)
-    for copy in copies[2:5]:
+    extended_ref[2 * tok + 16 :, :] = routed.astype(jnp.bfloat16)
+    for copy in copies[2:6]:
         copy.wait()
 
 
 def chosen_of(extended_ref, tok):
-    return extended_ref[tok : tok + 16, 0:tok].astype(jnp.float32)[0:1].astype(jnp.int32)
+    return extended_ref[2 * tok : 2 * tok + 16, 0:tok].astype(jnp.float32)[0:1].astype(jnp.int32)
 
 
 def router_of(extended_ref, tok, expert_count):
-    whole = extended_ref[tok + 16 :, :].astype(jnp.float32)
+    whole = extended_ref[2 * tok + 16 :, :].astype(jnp.float32)
     return whole[0:expert_count].astype(jnp.bfloat16)
 
 
 def dispatch_kernel(reps, tok, hot_capacity, own_ref, *refs):
-    extended_refs, row_refs, sent_refs = refs[:reps], refs[reps : 2 * reps], refs[2 * reps :]
+    extended_refs, sent_refs = refs[:reps], refs[reps:]
     for rep in range(reps):
         choice = chosen_of(extended_refs[rep], tok)
         placed = slot_matrix(choice, own_ref[0], len(sent_refs), hot_capacity)
-        rows = dot(placed, row_refs[rep][0:tok, :]).astype(jnp.bfloat16)
+        rows = dot(placed, extended_refs[rep][0:tok, :]).astype(jnp.bfloat16)
         for k, sent_ref in enumerate(sent_refs):
             sent_ref[rep * hot_capacity : (rep + 1) * hot_capacity] = rows[
                 k * hot_capacity : (k + 1) * hot_capacity
             ]
 
 
-def attend_blocks(block_ref, begin_ref, query_ref, pair_refs, state_refs, bias_ref, first):
-    top_ref, total_ref, sum_ref = state_refs
-    tok, width = query_ref.shape
+def fold_blocks(ids_ref, begin_ref, tasks, reps, states, bias_ref):
     lanes = 128
     per = lanes // HD
     scale = math.log2(math.e) / math.sqrt(HD)
-    turned = query_ref[...].T
-    head_of_row = lax.broadcasted_iota(jnp.int32, (lanes, tok), 0) // HD
-    spread = []
-    for group in range(width // lanes):
-        part = turned[group * lanes : (group + 1) * lanes]
-        spread.append(
-            jnp.concatenate(
-                [jnp.where(head_of_row == head, part, jnp.zeros_like(part)) for head in range(per)],
-                axis=1,
+    spreads = {}
+    for k, extended_ref, unused_pair, unused_first in tasks:
+        if k in spreads:
+            continue
+        tok = begin_ref.shape[1]
+        turned = extended_ref[tok : 2 * tok, :].T
+        head_of_row = lax.broadcasted_iota(jnp.int32, (lanes, tok), 0) // HD
+        spreads[k] = []
+        for group in range(turned.shape[0] // lanes):
+            part = turned[group * lanes : (group + 1) * lanes]
+            spreads[k].append(
+                jnp.concatenate(
+                    [
+                        jnp.where(head_of_row == head, part, jnp.zeros_like(part))
+                        for head in range(per)
+                    ],
+                    axis=1,
+                )
             )
-        )
-    position = block_ref[0] * tok + lax.broadcasted_iota(jnp.int32, (1, tok), 1)
-    begin = begin_ref[...]
-    lowest = jnp.min(begin)
-
-    def fold(pair_ref, block, fresh):
+
+    def fold(place, k, pair_ref, block, begin, fresh):
+        top_ref, total_ref, sum_ref = states[k]
+        tok = begin.shape[1]
+        position = ids_ref[k] * tok + lax.broadcasted_iota(jnp.int32, (1, tok), 1)
         key_position = block * tok + lax.broadcasted_iota(jnp.int32, (tok, tok), 0)
         visible = (key_position >= begin) & (key_position <= position)
-        bias_ref[...] = jnp.where(visible, 0.0, masked_score)
-        bias = bias_ref[...]
+        bias_ref[place] = jnp.where(visible, 0.0, masked_score)
+        bias = bias_ref[place]
         values = pair_ref[tok : 2 * tok, :].T
-        for group in range(width // lanes):
+        for group, spread in enumerate(spreads[k]):
             columns = slice(group * lanes, (group + 1) * lanes)
-            scores = dot(pair_ref[0:tok, columns], spread[group])
+            scores = dot(pair_ref[0:tok, columns], spread)
             weights, factors = [], []
             for head in range(per):
                 row = group * per + head
@@ -237,40 +246,78 @@
                     piece = piece + sum_ref[rows, :] * factors[head]
                 sum_ref[rows, :] = piece
 
-    for place, pair_ref in enumerate(pair_refs):
-        block = block_ref[1 + place]
-        if first and place == 0:
-            fold(pair_ref, block, True)
-        else:
-
-            @pl.when((block >= 0) & ((block + 1) * tok > lowest))
-            def unused(pair_ref=pair_ref, block=block):
-                fold(pair_ref, block, False)
-
-
-def attend_kernel(count, first, block_ref, begin_ref, query_ref, *refs):
-    pair_refs, refs = refs[:count], refs[count:]
-    if not first:
-        for old_ref, new_ref in zip(refs[0:3], refs[3:6]):
+    for place, (k, unused_extended, pair_ref, first) in enumerate(tasks):
+        block = ids_ref[reps + place]
+        begin = begin_ref[k : k + 1, :]
+        tok = begin.shape[1]
+        if first and k == 0:
+            fold(place, k, pair_ref, block, begin, True)
+            continue
+        if first:
+            top_ref, total_ref, sum_ref = states[k]
+            top_ref[...] = jnp.full(top_ref.shape, masked_score, jnp.float32)
+            total_ref[...] = jnp.zeros(total_ref.shape, jnp.float32)
+            sum_ref[...] = jnp.zeros(sum_ref.shape, jnp.float32)
+
+        @pl.when((block >= 0) & ((block + 1) * tok > jnp.min(begin)))
+        def unused(place=place, k=k, pair_ref=pair_ref, block=block, begin=begin):
+            fold(place, k, pair_ref, block, begin, False)
+
+
+def attend_kernel(plan, reps, counts, packed, ids_ref, begin_ref, *refs):
+    ks = sorted({k for k, unused_pair, unused_first in plan})
+    old_ks = [k for k in ks if not any(first for j, unused_pair, first in plan if j == k)]
+    extended_refs, refs = dict(zip(ks, refs)), refs[len(ks) :]
+    pair_refs, refs = refs[:counts], refs[counts:]
+    old_refs, refs = refs[: 3 * len(old_ks)], refs[3 * len(old_ks) :]
+    bias_ref, refs = refs[-1], refs[:-1]
+    packed_refs, state_refs = (refs[: len(ks)], refs[len(ks) :]) if packed else ((), refs)
+    states = {k: state_refs[3 * place : 3 * place + 3] for place, k in enumerate(ks)}
+    for place, k in enumerate(old_ks):
+        for old_ref, new_ref in zip(old_refs[3 * place : 3 * place + 3], states[k]):
             new_ref[...] = old_ref[...]
-        refs = refs[3:]
-    attend_blocks(block_ref, begin_ref, query_ref, pair_refs, refs[0:3], refs[3], first)
-
-
-def mix_kernel(count, block_ref, begin_ref, query_ref, residual_ref, proj_ref, *refs):
-    pair_refs, refs = refs[:count], refs[count:]
-    old_refs, mixed_ref, normed_ref = refs[0:3], refs[3], refs[4]
-    state_refs, bias_ref = refs[-4:-1], refs[-1]
-    for old_ref, new_ref in zip(old_refs, state_refs):
-        new_ref[...] = old_ref[...]
-    attend_blocks(block_ref, begin_ref, query_ref, pair_refs, state_refs, bias_ref, False)
-    unused_top, total_ref, sum_ref = state_refs
-    pieces = [
-        (sum_ref[head * HD : (head + 1) * HD, :] / total_ref[head : head + 1, :]).astype(
-            jnp.bfloat16
-        )
-        for head in range(total_ref.shape[0])
-    ]
+    tasks = [(k, extended_refs[k], pair_refs[pair], first) for k, pair, first in plan]
+    fold_blocks(ids_ref, begin_ref, tasks, reps, states, bias_ref)
+    for k, packed_ref in zip(ks, packed_refs):
+        top_ref, total_ref, sum_ref = states[k]
+        heads, width = top_ref.shape[0], sum_ref.shape[0]
+        packed_ref[0:width, :] = sum_ref[...].astype(jnp.bfloat16)
+        first = width
+        for ref, pieces in ((top_ref, 3), (total_ref, 2)):
+            rest = ref[...]
+            for unused in range(pieces):
+                piece = rest.astype(jnp.bfloat16)
+                packed_ref[first : first + heads, :] = piece
+                rest = rest - piece.astype(jnp.float32)
+                first += heads
+
+
+def mix_kernel(expert_count, hot_capacity, own_ref, extended_ref, residual_ref, proj_ref, *refs):
+    top_ref, total_ref, sum_ref = refs[0:3]
+    mixed_ref, sent_refs = refs[-1 - expert_count], refs[len(refs) - expert_count :]
+    packed_refs = refs[3 : -1 - expert_count]
+    tok, width = mixed_ref.shape
+    heads = top_ref.shape[0]
+    scale = math.log2(math.e) / math.sqrt(HD)
+    tops, totals = [top_ref[...]], [total_ref[...]]
+    for packed_ref in packed_refs:
+        pieces = [
+            packed_ref[width + place * heads : width + (place + 1) * heads, :].astype(jnp.float32)
+            for place in range(5)
+        ]
+        tops.append((pieces[0] + pieces[1]) + pieces[2])
+        totals.append(pieces[3] + pieces[4])
+    top = functools.reduce(jnp.maximum, tops)
+    factors = [jnp.exp2((one - top) * scale) for one in tops]
+    total = sum(one * factor for one, factor in zip(totals, factors))
+    factors = [factor / total for factor in factors]
+    pieces = []
+    for head in range(heads):
+        rows = slice(head * HD, (head + 1) * HD)
+        piece = sum_ref[rows, :] * factors[0][head : head + 1, :]
+        for packed_ref, factor in zip(packed_refs, factors[1:]):
+            piece = piece + packed_ref[rows, :].astype(jnp.float32) * factor[head : head + 1, :]
+        pieces.append(piece.astype(jnp.bfloat16))
     attended = jnp.concatenate(pieces, axis=0).T
     mixed = (residual_ref[...].astype(jnp.float32) + dot(attended, proj_ref[...])).astype(
         jnp.bfloat16
@@ -279,7 +326,10 @@
     mixed_f = mixed.astype(jnp.float32)
     inv_rms = lax.rsqrt(jnp.mean(mixed_f * mixed_f, axis=1, keepdims=True) + norm_eps)
     normed = (mixed_f * inv_rms).astype(jnp.bfloat16)
-    normed_ref[...] = normed
+    placed = slot_matrix(chosen_of(extended_ref, tok), own_ref[0], len(sent_refs), hot_capacity)
+    rows = dot(placed, normed).astype(jnp.bfloat16)
+    for k, sent_ref in enumerate(sent_refs):
+        sent_ref[...] = rows[k * hot_capacity : (k + 1) * hot_capacity]
 
 
 def expert_kernel(
@@ -298,7 +348,8 @@
 ):
     row_count, grad_count = counts
     row_refs, refs = refs[:row_count], refs[row_count:]
-    grad_refs, refs = refs[:grad_count], refs[grad_count:]
+    per_rep = row_count // len(rep_list)
+    grad_refs, refs = refs[:grad_count][::-1], refs[grad_count:]
     own_rows = rep_list[0] == 0
     held_ref, refs = refs[-1], refs[:-1]
     if own_rows:
@@ -325,7 +376,9 @@
 
     up_term = down_term = None
     for place, rep in enumerate(rep_list):
-        rows = chunk_rows(row_refs, sources, place * capacity, (place + 1) * capacity)
+        rows = chunk_rows(
+            row_refs[place * per_rep : (place + 1) * per_rep], sources, 0, capacity
+        )
         grads = chunk_rows(grad_refs, sources, rep * capacity, (rep + 1) * capacity)
         pre = dot(rows, up)
         sigmoid_pre = jax.nn.sigmoid(pre)
@@ -453,6 +506,7 @@
     heads = width // HD
     experts = Group(("expert",), (expert_count,))
     reps = Group(("rep",), (rep_count,))
+    owners = Group(("expert", "rep"), (expert_count, rep_count))
     parts = Group(("seq",), (seq_count,))
     strip = width // (seq_count * rep_count)
     capacity = max(2, (3 * tok + 2 * expert_count - 1) // (2 * expert_count))
@@ -477,11 +531,18 @@
                     )
         return lax.ppermute(array, ("seq", "rep"), pairs)
 
-    def block_ids(entries):
-        ids = [rank]
-        for seq_back, rep, needed in entries:
-            block = (seq_index - seq_back) * rep_count + rep
-            ids.append(jnp.where(needed & (seq_index >= seq_back), block, -1))
+    reach = (seq_count + 1) // 2
+    longest = (seq_count * rep_count + 1) // 2
+    query_ranks = [
+        seq_index * rep_count + reps.source(rep_index, k) for k in range(rep_count)
+    ]
+
+    def task_ids(plan, steps):
+        ids = list(query_ranks)
+        for k, pair, unused_first in plan:
+            block = rank - steps[pair] * rep_count
+            behind = query_ranks[k] - block
+            ids.append(jnp.where((block >= 0) & (behind >= 0) & (behind <= longest), block, -1))
         return jnp.stack(ids).astype(jnp.int32)
 
     state_shapes = [
@@ -489,103 +550,90 @@
         shape((heads, tok), jnp.float32),
         shape((width, tok), jnp.float32),
     ]
-    bias = pltpu.VMEM((tok, tok), jnp.float32)
-    query = query_rows[0]
-
-    def attend(blocks, state):
-        arrays, entries = blocks
-        return call(
-            functools.partial(attend_kernel, len(arrays), not state),
-            state_shapes,
-            [SMEM] + [VMEM] * (2 + len(arrays) + len(state)),
-            [bias],
-            cost=2.0,
-        )(block_ids(entries), begin, query, *arrays, *state)
-
+    tail = 16 + -(-expert_count // 16) * 16
     pair, extended, begin = pl.pallas_call(
         stack_kernel,
         out_shape=[
             shape((2 * tok, width)),
-            shape((tok + 16 + -(-expert_count // 16) * 16, width)),
-            shape((1, tok), jnp.int32),
+            shape((2 * tok + tail, width)),
+            shape((rep_count, tok), jnp.int32),
         ],
-        in_specs=[SMEM] + [HBM] * 6,
+        in_specs=[SMEM] + [HBM] * 7,
         out_specs=[VMEM] * 3,
         scratch_shapes=[
             pltpu.VMEM((1, tok), jnp.int32),
             pltpu.VMEM((expert_count, width), jnp.bfloat16),
             pltpu.SMEM(doc_lengths.shape, jnp.int32),
-            pltpu.SemaphoreType.DMA((6,)),
+            pltpu.SemaphoreType.DMA((7,)),
         ],
         compiler_params=pltpu.CompilerParams(vmem_limit_bytes=60 * 1024 * 1024),
     )(
-        jnp.stack([rank]).astype(jnp.int32),
+        jnp.stack(query_ranks).astype(jnp.int32),
         choice,
         doc_lengths,
         router.T,
         key_rows[0],
         value_rows[0],
         grad_out[0],
-    )
-    always = rep_index >= 0
-    reach = (seq_count + 1) // 2
-    rounds = [([pair], [(0, rep_index, always)])]
-    line = pair
-    extendeds = None
-    state = ()
-    for step in range(1, reach + 1):
-        ahead = send(line, step - 1, 1, 0, False)
-        arrays, entries = [ahead], [(step, rep_index, always)]
-        for d in range(1, rep_count):
-            if step == reach:
-                arrays.append(send(line, step - 1, 1, -d, False))
-                entries.append((step, rep_index + d, rep_index + d < rep_count))
-            if step == 1:
-                arrays.append(send(line, 0, 0, d, False))
-                entries.append((0, rep_index - d, rep_index >= d))
-            else:
-                arrays.append(send(line, step - 1, 0, d, True))
-                entries.append((step - 1, (rep_index - d) % rep_count, always))
-        if step == 1:
-            extendeds = reps.exchange([extended] * rep_count)
-        state = attend(rounds[-1], state)
-        rounds.append((arrays, entries))
-        if step < reach:
-            line, *state = lax.optimization_barrier((ahead, *state))
-            arrays[0] = line
-
-    *held, pinned = lax.optimization_barrier((*state, extendeds[0]))
-    state, extendeds = held, [pinned] + list(extendeds[1:])
+        query_rows[0],
+    )
+
+    def attend(plan, pairs, steps, extendeds, states, packed, cost):
+        ks = sorted({k for k, unused_pair, unused_first in plan})
+        old = [one for k in ks if k in states for one in states[k]]
+        state_out = state_shapes * len(ks)
+        if packed:
+            out_shape = [shape((width + 5 * heads, tok))] * len(ks)
+            scratch = [pltpu.VMEM(one.shape, one.dtype) for one in state_out]
+        else:
+            out_shape, scratch = state_out, []
+        outs = call(
+            functools.partial(attend_kernel, plan, rep_count, len(pairs), packed),
+            out_shape,
+            [SMEM] + [VMEM] * (1 + len(ks) + len(pairs) + len(old)),
+            scratch + [pltpu.VMEM((len(plan), tok, tok), jnp.float32)],
+            cost=cost,
+        )(task_ids(plan, steps), begin, *[extendeds[k] for k in ks], *pairs, *old)
+        if packed:
+            return dict(zip(ks, outs))
+        return {k: list(outs[3 * place : 3 * place + 3]) for place, k in enumerate(ks)}
+
+    others = range(1, rep_count)
+    lines = [pair, send(pair, 0, 1, 0, False)]
+    extendeds = reps.exchange([extended] * rep_count)
+    states = attend(((0, 0, True),), [pair], [0], [extended], {}, False, 2.0)
+    lines[1], *states[0] = lax.optimization_barrier((lines[1], *states[0]))
+    for step in range(2, reach + 1):
+        lines.append(send(lines[-1], step - 1, 1, 0, False))
+    middle = tuple((0, step, False) for step in range(1, reach)) + tuple(
+        (k, step, step == 0) for k in others for step in range(reach)
+    )
+    states = attend(middle, lines[:-1], list(range(reach)), extendeds, states, False, 4.0)
+    partial = attend(
+        tuple((k, 0, False) for k in others), lines[-1:], [reach], extendeds, states, True, 1.5
+    )
+    partial[1], *extendeds[1:] = lax.optimization_barrier((partial[1], *extendeds[1:]))
+    returned = reps.exchange([None] + [partial[k] for k in others], inverse=True)[1:]
+    states = attend(((0, 0, False),), lines[-1:], [reach], extendeds, states, False, 1.5)
     sent_grads = call(
         functools.partial(dispatch_kernel, rep_count, tok, hot_capacity),
         [shape((rep_count * hot_capacity, width))] * expert_count,
-        [SMEM] + [VMEM] * (2 * rep_count),
-    )(own, *extendeds, *extendeds)
-    got_grads = merged(experts.exchange(sent_grads), MOST_PERMUTES)
-
-    arrays, entries = rounds[-1]
-    mixed, normed = call(
-        functools.partial(mix_kernel, len(arrays)),
-        [shape((tok, width))] * 2,
-        [SMEM] + [VMEM] * (7 + len(arrays)),
-        [pltpu.VMEM(one.shape, one.dtype) for one in state_shapes] + [bias],
-        cost=5.0,
-    )(block_ids(entries), begin, query, residual[0], out_proj, *arrays, *state)
-
-    normed, got_grads = lax.optimization_barrier((normed, got_grads))
-
-    def dispatch(own_arrays, rows):
-        return call(
-            functools.partial(dispatch_kernel, len(rows), tok, hot_capacity),
-            [shape((len(rows) * hot_capacity, width))] * expert_count,
-            [SMEM] + [VMEM] * (2 * len(rows)),
-        )(own, *own_arrays, *rows)
-
-    others = reps.exchange([normed] * rep_count)[1:]
-    got_rows = merged(experts.exchange(dispatch(extendeds[:1], [normed])), MOST_PERMUTES)
-    more_rows = dispatch(extendeds[1:], others)
-    more_rows, got_rows = lax.optimization_barrier((more_rows, got_rows))
-    got_more = merged(experts.exchange(more_rows), MOST_PERMUTES)
+        [SMEM] + [VMEM] * rep_count,
+    )(own, *extendeds)
+    got_grads = merged(experts.exchange(sent_grads), MOST_PERMUTES)[::-1]
+
+    mixed, *sent_rows = call(
+        functools.partial(mix_kernel, expert_count, hot_capacity),
+        [shape((tok, width))] + [shape((hot_capacity, width))] * expert_count,
+        [SMEM] + [VMEM] * (6 + len(returned)),
+        cost=2.0,
+    )(own, extendeds[0], residual[0], out_proj, *states[0], *returned)
+    *sent_rows, got_grads = lax.optimization_barrier((*sent_rows, got_grads))
+    arrived = owners.exchange([sent_rows[k // rep_count] for k in range(owners.count)])
+    got_rows = merged(arrived[0::rep_count], MOST_PERMUTES)
+    got_more = [
+        one for k in others for one in merged(arrived[k::rep_count], MOST_PERMUTES)
+    ]
 
     def expert_call(rep_list, rows, out_shape, extra):
         return call(

time: 65.5 us -> 66.5 us (1.015)
  Pallas kernels: 12.4 us -> 15 us
  waiting for transfers between devices: 20.9 us -> 18.9 us
  starting transfers between devices: 29.4 us -> 28 us
  local copies, waits for them, and re-layouts: 1.62 us -> 2.7 us
    ppermute x5 -> x2, starting transfers between devices: 10.4 us -> 5.62 us  [send(): return lax.ppermute(array, ('seq', 'rep'), pairs)]
    ppermute x17 -> x18, starting transfers between devices: 19 us -> 22.4 us  [exchange(): got[k] = lax.ppermute(chunks[k], self.axes, pairs)]
    pallas_call x6, Pallas kernels: 6.23 us -> 8.82 us  [the longest x4 5.57 us: attend(): call(functools.partial(attend_kernel, plan, rep_count, len(pairs), packed...]
    ppermute x5 -> x2, waiting for transfers between devices: 1.27 us -> 0.01 us  [send(): return lax.ppermute(array, ('seq', 'rep'), pairs)]
    unnamed x16, local copies, waits for them, and re-layouts: 1.62 us -> 2.61 us
    ppermute x17 -> x18, waiting for transfers between devices: 19.6 us -> 18.9 us  [exchange(): got[k] = lax.ppermute(chunks[k], self.axes, pairs)]
  transfers between devices with their start and end apart: 22 -> 20, of which waited for: 10 -> 7; matrix products, arithmetic and copies ran while one was open for 0% -> 0% of each run, Pallas kernels for 15% -> 16%
where the time goes in v8:
time: 66.5 us; the launch traced here: 66.2 us
  starting transfers between devices  28 us (42%)
  waiting for transfers between devices  18.9 us (28%)
  Pallas kernels  15 us (23%)
  local copies, waits for them, and re-layouts  2.7 us (4%)
  other arithmetic  0.81 us (1%)
  between operations  0.81 us (1%)
    ppermute x18, starting transfers between devices, exchange(): got[k] = lax.ppermute(chunks[k], self.axes, pairs)  22.4 us
    ppermute x18, waiting for transfers between devices, exchange(): got[k] = lax.ppermute(chunks[k], self.axes, pairs)  18.9 us
    ppermute x2, starting transfers between devices, send(): return lax.ppermute(array, ('seq', 'rep'), pairs)  5.62 us
    pallas_call x4, Pallas kernels, attend(): call(functools.partial(attend_kernel, plan, rep_count, len(pairs), packed...  5.57 us
    pallas_call x2, Pallas kernels, expert_call(): call(functools.partial(expert_kernel, rep_count, rep_list, expert_count,...  3.47 us
    pallas_call x1, Pallas kernels, local(): pl.pallas_call(stack_kernel, out_shape=[shape((2 * tok, width)), shape((2...  2.64 us
    unnamed x16, local copies, waits for them, and re-layouts  2.61 us
    pallas_call x1, Pallas kernels, local(): call(functools.partial(finish_kernel, hot_capacity, expert_count), [shape...  1.42 us
  transfers between devices with their start and end apart: 20, of which 7 were waited for; matrix products, arithmetic and copies ran while one was open for 0% of the time, Pallas kernels for 16%

profile of v8, /device:TPU:0, one launch (start us, length us, event | category | flops | bytes accessed | tf_op | source)
XLA Modules:
  0.0 66.2 jit_solution(6303330656269611620)
XLA Ops:
  0.6 0.6 pad_add_fusion.1.ranks_ref
  1.2 2.6 %shard_map.138 = (bf16[256,512]{1,0:T(8,128)(2,1)}, bf16[288,512]{1,0:T(8,128)(2,1)}, s32[2,128]{1,0:T(2,128)}) custom-call(s32[2]{0:T(128)} %pad_add_fusion.1.ranks_ref, s32[1,128]{1,0:T(1,128)} %bitcast.36, s32[1,8]{1,0:T(1,128)} %lengths_ref.1, bf16[4,512]{1,0:T(4,128)(2,1)} %bitcast.35, bf16[128,512]{1,0:T(8,128)(2,1)} %bitcast.31, ...), custom_call_target="tpu_custom_call" | custom-call | tf_op jit(solution)/shard_map/pallas_call | solution.py:554
  3.9 4.9 %collective-permute-start = (bf16[256,512]{1,0:T(8,128)(2,1)}, bf16[256,512]{1,0:T(8,128)(2,1)S(1)}, u32[]{:S(2)}, u32[]{:S(2)}) collective-permute-start(bf16[256,512]{1,0:T(8,128)(2,1)} %get-tuple-element.60.refs_1_.refs_2_), channel_id=1, source_target_pairs={{0,8},{1,9},{8,16},{9,17},{16,24},{17,25},{2,10},{3,11},{10,18},{1... | collective-permute-start | bytes 786440 | tf_op jit(solution)/shard_map/ppermute | solution.py:532
  8.8 1.6 %collective-permute-start.2 = (bf16[288,512]{1,0:T(8,128)(2,1)}, bf16[288,512]{1,0:T(8,128)(2,1)S(1)}, u32[]{:S(2)}, u32[]{:S(2)}) collective-permute-start(bf16[288,512]{1,0:T(8,128)(2,1)} %get-tuple-element.58.refs_0_.extended_ref), channel_id=1, source_target_pairs={{0,1},{1,0},{2,3},{3,2},{4,5},{5,4},{6,7},{7,6},{8,9},{9,8},{10,11... | collective-permute-start | bytes 884744 | tf_op jit(solution)/shard_map/ppermute | solution.py:69
  10.6 0.7 %copy-done.7 = s32[2,128]{1,0:T(2,128)S(1)} copy-done((s32[2,128]{1,0:T(2,128)S(1)}, s32[2,128]{1,0:T(2,128)}, u32[]{:S(2)}) %copy-start.7) | copy-done | bytes 1048
  11.3 1.0 %copy-done.3 = bf16[288,512]{1,0:T(8,128)(2,1)S(1)} copy-done((bf16[288,512]{1,0:T(8,128)(2,1)S(1)}, bf16[288,512]{1,0:T(8,128)(2,1)}, u32[]{:S(2)}) %copy-start.3) | copy-done | bytes 294936
  12.3 0.9 %copy-done.5 = bf16[256,512]{1,0:T(8,128)(2,1)S(1)} copy-done((bf16[256,512]{1,0:T(8,128)(2,1)S(1)}, bf16[256,512]{1,0:T(8,128)(2,1)}, u32[]{:S(2)}) %copy-start.5) | copy-done | bytes 262168
  13.2 1.7 %shard_map.139 = (f32[16,128]{1,0:T(8,128)S(1)}, f32[16,128]{1,0:T(8,128)S(1)}, f32[512,128]{1,0:T(8,128)S(1)}) custom-call(s32[3]{0:T(128)S(1)} %pad_add_fusion.4.ids_ref, s32[2,128]{1,0:T(2,128)S(1)} %copy-done.7, bf16[288,512]{1,0:T(8,128)(2,1)S(1)} %copy-done.3, bf16[256,512]{1,0:T(8,128)(2,1)S(1)} %copy-done.5), custom_call_target="tpu_custom_call" | custom-call | flops 2000000000 | tf_op jit(solution)/shard_map/pallas_call | solution.py:590
  15.0 0.7 %collective-permute-start.1 = (bf16[256,512]{1,0:T(8,128)(2,1)S(1)}, bf16[256,512]{1,0:T(8,128)(2,1)S(1)}, u32[]{:S(2)}, u32[]{:S(2)}) collective-permute-start(bf16[256,512]{1,0:T(8,128)(2,1)S(1)} %collective-permute-done.refs_3_), channel_id=1, source_target_pairs={{8,16},{9,17},{16,24},{17,25},{10,18},{11,19},{18,26},{19,27},{12,... | collective-permute-start | bytes 786440 | tf_op jit(solution)/shard_map/ppermute | solution.py:532
  15.7 1.9 %collective-permute-done.2.refs_1_.refs_0_ = bf16[288,512]{1,0:T(8,128)(2,1)S(1)} collective-permute-done((bf16[288,512]{1,0:T(8,128)(2,1)}, bf16[288,512]{1,0:T(8,128)(2,1)S(1)}, u32[]{:S(2)}, u32[]{:S(2)}) %collective-permute-start.2) | collective-permute-done | bytes 294944 | tf_op jit(solution)/shard_map/ppermute | solution.py:69
  17.6 2.3 %shard_map.140 = (f32[16,128]{1,0:T(8,128)S(1)}, f32[16,128]{1,0:T(8,128)S(1)}, f32[512,128]{1,0:T(8,128)S(1)}, f32[16,128]{1,0:T(8,128)S(1)}, f32[16,128]{1,0:T(8,128)S(1)}, /*index=5*/f32[512,128]{1,0:T(8,128)S(1)}) custom-call(s32[5]{0:T(128)S(1)} %stack.81.ids_ref, s32[2,128]{1,0:T(2,128)S(1)} %copy-done.7, bf16[288,512]{1,0:T(8,128)(2,1)S(1)} %copy-done.3, ...), custom_call_target="tpu_custom_call" | custom-call | flops 4000000000 | tf_op jit(solution)/shard_map/pallas_call | solution.py:590
  19.9 0.8 %shard_map.142 = bf16[592,128]{1,0:T(8,128)(2,1)S(1)} custom-call(s32[3]{0:T(128)S(1)} %get-tuple-element.113.ids_ref, s32[2,128]{1,0:T(2,128)S(1)} %copy-done.7, bf16[288,512]{1,0:T(8,128)(2,1)S(1)} %collective-permute-done.2.refs_1_.refs_0_, bf16[256,512]{1,0:T(8,128)(2,1)S(1)} %collective-permute-done.1.refs_1_, f32[16,128]{1,0:T(8,128)S(1)} %get-tuple-element.74.refs_2_, ...), custom_call_target="tpu_custom_call" | custom-call | flops 1500000000 | tf_op jit(solution)/shard_map/pallas_call | solution.py:590
  21.1 0.6 shard_map.144
  21.7 1.6 %collective-permute-start.5 = (bf16[128,512]{1,0:T(8,128)(2,1)S(1)}, bf16[128,512]{1,0:T(8,128)(2,1)S(1)}, u32[]{:S(2)}, u32[]{:S(2)}) collective-permute-start(bf16[128,512]{1,0:T(8,128)(2,1)S(1)} %get-tuple-element.84), channel_id=1, source_target_pairs={{0,4},{2,6},{4,0},{6,2},{1,5},{3,7},{5,1},{7,3},{8,12},{10,14},{12... | collective-permute-start | bytes 393224 | tf_op jit(solution)/shard_map/ppermute | solution.py:69
  23.6 0.7 %shard_map.141 = (f32[16,128]{1,0:T(8,128)S(1)}, f32[16,128]{1,0:T(8,128)S(1)}, f32[512,128]{1,0:T(8,128)S(1)}) custom-call(s32[3]{0:T(128)S(1)} %get-tuple-element.112.ids_ref, s32[2,128]{1,0:T(2,128)S(1)} %copy-done.7, bf16[288,512]{1,0:T(8,128)(2,1)S(1)} %copy-done.4, bf16[256,512]{1,0:T(8,128)(2,1)S(1)} %collective-permute-done.1.refs_1_, ...), custom_call_target="tpu_custom_call" | custom-call | flops 1500000000 | tf_op jit(solution)/shard_map/pallas_call | solution.py:590
  24.3 1.6 %collective-permute-done.3.refs_3_ = bf16[592,128]{1,0:T(8,128)(2,1)S(1)} collective-permute-done((bf16[592,128]{1,0:T(8,128)(2,1)S(1)}, bf16[592,128]{1,0:T(8,128)(2,1)S(1)}, u32[]{:S(2)}, u32[]{:S(2)}) %collective-permute-start.3) | collective-permute-done | bytes 151584 | tf_op jit(solution)/shard_map/ppermute | solution.py:69
  26.0 0.6 shard_map.143
  26.6 0.8 %collective-permute-done.4.refs_4_ = bf16[128,512]{1,0:T(8,128)(2,1)S(1)} collective-permute-done((bf16[128,512]{1,0:T(8,128)(2,1)S(1)}, bf16[128,512]{1,0:T(8,128)(2,1)S(1)}, u32[]{:S(2)}, u32[]{:S(2)}) %collective-permute-start.4) | collective-permute-done | bytes 131104 | tf_op jit(solution)/shard_map/ppermute | solution.py:69
  27.4 2.9 %collective-permute-done.5.refs_5_ = bf16[128,512]{1,0:T(8,128)(2,1)S(1)} collective-permute-done((bf16[128,512]{1,0:T(8,128)(2,1)S(1)}, bf16[128,512]{1,0:T(8,128)(2,1)S(1)}, u32[]{:S(2)}, u32[]{:S(2)}) %collective-permute-start.5) | collective-permute-done | bytes 131104 | tf_op jit(solution)/shard_map/ppermute | solution.py:69
  30.7 1.5 %collective-permute-start.13 = (bf16[64,512]{1,0:T(8,128)(2,1)S(1)}, bf16[64,512]{1,0:T(8,128)(2,1)S(1)}, u32[]{:S(2)}, u32[]{:S(2)}) collective-permute-start(bf16[64,512]{1,0:T(8,128)(2,1)S(1)} %get-tuple-element.90), channel_id=1, source_target_pairs={{0,6},{1,7},{2,4},{3,5},{4,2},{5,3},{6,0},{7,1},{8,14},{9,15},{10,... | collective-permute-start | bytes 196616 | tf_op jit(solution)/shard_map/ppermute | solution.py:69
  32.3 1.4 %collective-permute-start.10 = (bf16[64,512]{1,0:T(8,128)(2,1)S(1)}, bf16[64,512]{1,0:T(8,128)(2,1)S(1)}, u32[]{:S(2)}, u32[]{:S(2)}) collective-permute-start(bf16[64,512]{1,0:T(8,128)(2,1)S(1)} %get-tuple-element.90), channel_id=1, source_target_pairs={{0,7},{1,6},{2,5},{3,4},{4,3},{5,2},{6,1},{7,0},{8,15},{9,14},{10,... | collective-permute-start | bytes 196616 | tf_op jit(solution)/shard_map/ppermute | solution.py:69
  34.0 2.6 %collective-permute-start.9 = (bf16[64,512]{1,0:T(8,128)(2,1)S(1)}, bf16[64,512]{1,0:T(8,128)(2,1)S(1)}, u32[]{:S(2)}, u32[]{:S(2)}) collective-permute-start(bf16[64,512]{1,0:T(8,128)(2,1)S(1)} %get-tuple-element.89), channel_id=1, source_target_pairs={{0,5},{1,4},{2,7},{3,6},{4,1},{5,0},{6,3},{7,2},{8,13},{9,12},{10,... | collective-permute-start | bytes 196616 | tf_op jit(solution)/shard_map/ppermute | solution.py:69
  37.0 1.8 %shard_map.145 = (bf16[128,512]{1,0:T(8,128)(2,1)S(1)}, bf16[128,512]{1,0:T(8,128)(2,1)S(1)}, bf16[128,512]{1,0:T(8,128)(2,1)S(1)}, bf16[128,512]{1,0:T(8,128)(2...) custom-call(s32[1]{0:T(128)} %bitcast.own_ref, s32[4]{0:T(128)S(1)} %pad_add_fusion.part_ref, ...), custom_call_target="tpu_custom_call" | custom-call | flops 2000000000 | tf_op jit(solution)/shard_map/pallas_call | solution.py:639
  38.9 1.0 %collective-permute-start.15 = (bf16[128,512]{1,0:T(8,128)(2,1)S(1)}, bf16[128,512]{1,0:T(8,128)(2,1)S(1)}, u32[]{:S(2)}, u32[]{:S(2)}) collective-permute-start(bf16[128,512]{1,0:T(8,128)(2,1)S(1)} %get-tuple-element.101), channel_id=1, source_target_pairs={{0,4},{2,6},{4,0},{6,2},{1,5},{3,7},{5,1},{7,3},{8,12},{10,14},{12... | collective-permute-start | bytes 393224 | tf_op jit(solution)/shard_map/ppermute | solution.py:69
  39.9 1.0 %collective-permute-done.7.refs_0_ = bf16[64,512]{1,0:T(8,128)(2,1)S(1)} collective-permute-done((bf16[64,512]{1,0:T(8,128)(2,1)S(1)}, bf16[64,512]{1,0:T(8,128)(2,1)S(1)}, u32[]{:S(2)}, u32[]{:S(2)}) %collective-permute-start.7) | collective-permute-done | bytes 65568 | tf_op jit(solution)/shard_map/ppermute | solution.py:69
  40.9 1.1 %collective-permute-start.16 = (bf16[128,512]{1,0:T(8,128)(2,1)S(1)}, bf16[128,512]{1,0:T(8,128)(2,1)S(1)}, u32[]{:S(2)}, u32[]{:S(2)}) collective-permute-start(bf16[128,512]{1,0:T(8,128)(2,1)S(1)} %get-tuple-element.102), channel_id=1, source_target_pairs={{0,6},{2,4},{4,2},{6,0},{1,7},{3,5},{5,3},{7,1},{8,14},{10,12},{12... | collective-permute-start | bytes 393224 | tf_op jit(solution)/shard_map/ppermute | solution.py:69
  42.0 1.6 %shard_map.146 = (bf16[2,64,512]{2,1,0:T(8,128)(2,1)S(1)}, bf16[2,64,512]{2,1,0:T(8,128)(2,1)S(1)}, bf16[2,64,512]{2,1,0:T(8,128)(2,1)S(1)}, f32[2,64,512]{2,1,0:T(8,128)S(1)}) custom-call(s32[1]{0:T(128)} %bitcast.own_ref, s32[4]{0:T(128)S(1)} %pad_add_fusion.part_ref, bf16[512,512]{1,0:T(8,128)(2,1)S(1)} %bitcast.27, bf16[512,512]{1,0:T(8,128)(2,1)S(1)} %bitcast.29, ...), custom_call_target="tpu_custom_call" | custom-call | flops 2000000000 | tf_op jit(solution)/shard_map/pallas_call | solution.py:639
  43.6 9.1 %collective-permute-start.17 = (bf16[2,64,512]{2,1,0:T(8,128)(2,1)S(1)}, bf16[2,64,512]{2,1,0:T(8,128)(2,1)S(1)}, u32[]{:S(2)}, u32[]{:S(2)}) collective-permute-start(bf16[2,64,512]{2,1,0:T(8,128)(2,1)S(1)} %get-tuple-element.107), channel_id=1, source_target_pairs={{0,24},{8,16},{16,8},{24,0},{1,25},{9,17},{17,9},{25,1},{2,26},{10... | collective-permute-start | bytes 393224 | tf_op jit(solution)/shard_map/ppermute | solution.py:69
  53.5 1.4 %shard_map.147 = (bf16[128,512]{1,0:T(8,128)(2,1)}, bf16[128,512]{1,0:T(8,128)(2,1)}) custom-call(s32[1]{0:T(128)} %bitcast.own_ref, bf16[128,512]{1,0:T(8,128)(2,1)S(1)} %get-tuple-element.98.mixed_ref, bf16[288,512]{1,0:T(8,128)(2,1)S(1)} %copy-done.4, bf16[128,512]{1,0:T(8,128)(2,1)S(1)} %get-tuple-element.99.refs_0_, ...), custom_call_target="tpu_custom_call" | custom-call | flops 1500000000 | tf_op jit(solution)/shard_map/pallas_call | solution.py:672
  54.9 2.3 %collective-permute-done.17.refs_0_ = bf16[2,64,512]{2,1,0:T(8,128)(2,1)S(1)} collective-permute-done((bf16[2,64,512]{2,1,0:T(8,128)(2,1)S(1)}, bf16[2,64,512]{2,1,0:T(8,128)(2,1)S(1)}, u32[]{:S(2)}, u32[]{:S(2)}) %collective-permute-start.17) | collective-permute-done | bytes 131104 | tf_op jit(solution)/shard_map/ppermute | solution.py:69
  57.1 8.3 %collective-permute-done.18.refs_1_ = bf16[2,64,512]{2,1,0:T(8,128)(2,1)S(1)} collective-permute-done((bf16[2,64,512]{2,1,0:T(8,128)(2,1)S(1)}, bf16[2,64,512]{2,1,0:T(8,128)(2,1)S(1)}, u32[]{:S(2)}, u32[]{:S(2)}) %collective-permute-start.18) | collective-permute-done | bytes 131104 | tf_op jit(solution)/shard_map/ppermute | solution.py:69
  65.5 0.7 %shard_map.148 = (f32[64,512]{1,0:T(8,128)}, f32[64,512]{1,0:T(8,128)}) custom-call(f32[2,64,512]{2,1,0:T(8,128)S(1)} %get-tuple-element.106.kept_ref, bf16[2,64,512]{2,1,0:T(8,128)(2,1)S(1)} %collective-permute-done.17.refs_0_, bf16[2,64,512]{2,1,0:T(8,128)(2,1)S(1)} %collective-permute-done.18.refs_1_, bf16[2,64,512]{2,1,0:T(8,128)(2,1)S(1)} %collective-permute-done.19.refs_2_), custom_call_target="tpu_custom_call" | custom-call | flops 500000000 | tf_op jit(solution)/shard_map/pallas_call | solution.py:679
  (40 shorter events, 2.9 us)
Async XLA Ops:
  3.9 11.1 %collective-permute-start = (bf16[256,512]{1,0:T(8,128)(2,1)}, bf16[256,512]{1,0:T(8,128)(2,1)S(1)}, u32[]{:S(2)}, u32[]{:S(2)}) collective-permute-start(bf16[256,512]{1,0:T(8,128)(2,1)} %get-tuple-element.60.refs_1_.refs_2_), channel_id=1, source_target_pairs={{0,8},{1,9},{8,16},{9,17},{16,24},{17,25},{2,10},{3,11},{10,18},{1... | collective-permute-start | bytes 786440 | tf_op jit(solution)/shard_map/ppermute | solution.py:532
  8.8 8.7 %collective-permute-start.2 = (bf16[288,512]{1,0:T(8,128)(2,1)}, bf16[288,512]{1,0:T(8,128)(2,1)S(1)}, u32[]{:S(2)}, u32[]{:S(2)}) collective-permute-start(bf16[288,512]{1,0:T(8,128)(2,1)} %get-tuple-element.58.refs_0_.extended_ref), channel_id=1, source_target_pairs={{0,1},{1,0},{2,3},{3,2},{4,5},{5,4},{6,7},{7,6},{8,9},{9,8},{10,11... | collective-permute-start | bytes 884744 | tf_op jit(solution)/shard_map/ppermute | solution.py:69
  10.6 0.7 %copy-start.7 = (s32[2,128]{1,0:T(2,128)S(1)}, s32[2,128]{1,0:T(2,128)}, u32[]{:S(2)}) copy-start(s32[2,128]{1,0:T(2,128)} %get-tuple-element.59.begin_ref) | copy-start | bytes 3076
  11.3 1.0 %copy-start.3 = (bf16[288,512]{1,0:T(8,128)(2,1)S(1)}, bf16[288,512]{1,0:T(8,128)(2,1)}, u32[]{:S(2)}) copy-start(bf16[288,512]{1,0:T(8,128)(2,1)} %get-tuple-element.58.refs_0_.extended_ref) | copy-start | bytes 884740
  12.3 0.9 %copy-start.5 = (bf16[256,512]{1,0:T(8,128)(2,1)S(1)}, bf16[256,512]{1,0:T(8,128)(2,1)}, u32[]{:S(2)}) copy-start(bf16[256,512]{1,0:T(8,128)(2,1)} %get-tuple-element.60.refs_1_.refs_2_) | copy-start | bytes 786436
  15.0 4.9 %collective-permute-start.1 = (bf16[256,512]{1,0:T(8,128)(2,1)S(1)}, bf16[256,512]{1,0:T(8,128)(2,1)S(1)}, u32[]{:S(2)}, u32[]{:S(2)}) collective-permute-start(bf16[256,512]{1,0:T(8,128)(2,1)S(1)} %collective-permute-done.refs_3_), channel_id=1, source_target_pairs={{8,16},{9,17},{16,24},{17,25},{10,18},{11,19},{18,26},{19,27},{12,... | collective-permute-start | bytes 786440 | tf_op jit(solution)/shard_map/ppermute | solution.py:532
  19.9 1.2 %copy-start.4 = (bf16[288,512]{1,0:T(8,128)(2,1)S(1)}, bf16[288,512]{1,0:T(8,128)(2,1)}, u32[]{:S(2)}) copy-start(bf16[288,512]{1,0:T(8,128)(2,1)} %get-tuple-element.58.refs_0_.extended_ref) | copy-start | bytes 884740
  20.7 5.3 %collective-permute-start.3 = (bf16[592,128]{1,0:T(8,128)(2,1)S(1)}, bf16[592,128]{1,0:T(8,128)(2,1)S(1)}, u32[]{:S(2)}, u32[]{:S(2)}) collective-permute-start(bf16[592,128]{1,0:T(8,128)(2,1)S(1)} %shard_map.142), channel_id=1, source_target_pairs={{0,1},{1,0},{2,3},{3,2},{4,5},{5,4},{6,7},{7,6},{8,9},{9,8},{10,11... | collective-permute-start | bytes 454664 | tf_op jit(solution)/shard_map/ppermute | solution.py:69
  21.6 5.8 %collective-permute-start.4 = (bf16[128,512]{1,0:T(8,128)(2,1)S(1)}, bf16[128,512]{1,0:T(8,128)(2,1)S(1)}, u32[]{:S(2)}, u32[]{:S(2)}) collective-permute-start(bf16[128,512]{1,0:T(8,128)(2,1)S(1)} %get-tuple-element.83), channel_id=1, source_target_pairs={{0,6},{2,4},{4,2},{6,0},{1,7},{3,5},{5,3},{7,1},{8,14},{10,12},{12... | collective-permute-start | bytes 393224 | tf_op jit(solution)/shard_map/ppermute | solution.py:69
  21.7 8.6 %collective-permute-start.5 = (bf16[128,512]{1,0:T(8,128)(2,1)S(1)}, bf16[128,512]{1,0:T(8,128)(2,1)S(1)}, u32[]{:S(2)}, u32[]{:S(2)}) collective-permute-start(bf16[128,512]{1,0:T(8,128)(2,1)S(1)} %get-tuple-element.84), channel_id=1, source_target_pairs={{0,4},{2,6},{4,0},{6,2},{1,5},{3,7},{5,1},{7,3},{8,12},{10,14},{12... | collective-permute-start | bytes 393224 | tf_op jit(solution)/shard_map/ppermute | solution.py:69
  23.3 7.0 %collective-permute-start.6 = (bf16[128,512]{1,0:T(8,128)(2,1)S(1)}, bf16[128,512]{1,0:T(8,128)(2,1)S(1)}, u32[]{:S(2)}, u32[]{:S(2)}) collective-permute-start(bf16[128,512]{1,0:T(8,128)(2,1)S(1)} %get-tuple-element.85), channel_id=1, source_target_pairs={{0,2},{2,0},{4,6},{6,4},{1,3},{3,1},{5,7},{7,5},{8,10},{10,8},{12,... | collective-permute-start | bytes 393224 | tf_op jit(solution)/shard_map/ppermute | solution.py:69
  23.6 2.4 %copy-start = (bf16[512,512]{1,0:T(8,128)(2,1)S(1)}, bf16[512,512]{1,0:T(8,128)(2,1)}, u32[]{:S(2)}) copy-start(bf16[512,512]{1,0:T(8,128)(2,1)} %proj_ref.1) | copy-start | bytes 1572868
  23.6 2.4 %copy-start.6 = (bf16[1,128,512]{2,1,0:T(8,128)(2,1)S(1)}, bf16[1,128,512]{2,1,0:T(8,128)(2,1)}, u32[]{:S(2)}) copy-start(bf16[1,128,512]{2,1,0:T(8,128)(2,1)} %param.15) | copy-start | bytes 393220
  26.0 11.0 %copy-start.1 = (bf16[1,512,512]{2,1,0:T(8,128)(2,1)S(1)}, bf16[1,512,512]{2,1,0:T(8,128)(2,1)}, u32[]{:S(2)}) copy-start(bf16[1,512,512]{2,1,0:T(8,128)(2,1)} %param.19) | copy-start | bytes 1572868
  26.0 11.0 %copy-start.2 = (bf16[1,512,512]{2,1,0:T(8,128)(2,1)S(1)}, bf16[1,512,512]{2,1,0:T(8,128)(2,1)}, u32[]{:S(2)}) copy-start(bf16[1,512,512]{2,1,0:T(8,128)(2,1)} %param.20) | copy-start | bytes 1572868
  30.3 3.6 %collective-permute-start.11 = (bf16[64,512]{1,0:T(8,128)(2,1)S(1)}, bf16[64,512]{1,0:T(8,128)(2,1)S(1)}, u32[]{:S(2)}, u32[]{:S(2)}) collective-permute-start(bf16[64,512]{1,0:T(8,128)(2,1)S(1)} %get-tuple-element.88), channel_id=1, source_target_pairs={{0,2},{1,3},{2,0},{3,1},{4,6},{5,7},{6,4},{7,5},{8,10},{9,11},{10,... | collective-permute-start | bytes 196616 | tf_op jit(solution)/shard_map/ppermute | solution.py:69
  30.4 6.2 %collective-permute-start.12 = (bf16[64,512]{1,0:T(8,128)(2,1)S(1)}, bf16[64,512]{1,0:T(8,128)(2,1)S(1)}, u32[]{:S(2)}, u32[]{:S(2)}) collective-permute-start(bf16[64,512]{1,0:T(8,128)(2,1)S(1)} %get-tuple-element.89), channel_id=1, source_target_pairs={{0,4},{1,5},{2,6},{3,7},{4,0},{5,1},{6,2},{7,3},{8,12},{9,13},{10,... | collective-permute-start | bytes 196616 | tf_op jit(solution)/shard_map/ppermute | solution.py:69
  30.7 6.2 %collective-permute-start.13 = (bf16[64,512]{1,0:T(8,128)(2,1)S(1)}, bf16[64,512]{1,0:T(8,128)(2,1)S(1)}, u32[]{:S(2)}, u32[]{:S(2)}) collective-permute-start(bf16[64,512]{1,0:T(8,128)(2,1)S(1)} %get-tuple-element.90), channel_id=1, source_target_pairs={{0,6},{1,7},{2,4},{3,5},{4,2},{5,3},{6,0},{7,1},{8,14},{9,15},{10,... | collective-permute-start | bytes 196616 | tf_op jit(solution)/shard_map/ppermute | solution.py:69
  32.3 6.6 %collective-permute-start.10 = (bf16[64,512]{1,0:T(8,128)(2,1)S(1)}, bf16[64,512]{1,0:T(8,128)(2,1)S(1)}, u32[]{:S(2)}, u32[]{:S(2)}) collective-permute-start(bf16[64,512]{1,0:T(8,128)(2,1)S(1)} %get-tuple-element.90), channel_id=1, source_target_pairs={{0,7},{1,6},{2,5},{3,4},{4,3},{5,2},{6,1},{7,0},{8,15},{9,14},{10,... | collective-permute-start | bytes 196616 | tf_op jit(solution)/shard_map/ppermute | solution.py:69
  33.7 8.3 %collective-permute-start.8 = (bf16[64,512]{1,0:T(8,128)(2,1)S(1)}, bf16[64,512]{1,0:T(8,128)(2,1)S(1)}, u32[]{:S(2)}, u32[]{:S(2)}) collective-permute-start(bf16[64,512]{1,0:T(8,128)(2,1)S(1)} %get-tuple-element.88), channel_id=1, source_target_pairs={{0,3},{1,2},{2,1},{3,0},{4,7},{5,6},{6,5},{7,4},{8,11},{9,10},{10,... | collective-permute-start | bytes 196616 | tf_op jit(solution)/shard_map/ppermute | solution.py:69
  34.0 8.0 %collective-permute-start.9 = (bf16[64,512]{1,0:T(8,128)(2,1)S(1)}, bf16[64,512]{1,0:T(8,128)(2,1)S(1)}, u32[]{:S(2)}, u32[]{:S(2)}) collective-permute-start(bf16[64,512]{1,0:T(8,128)(2,1)S(1)} %get-tuple-element.89), channel_id=1, source_target_pairs={{0,5},{1,4},{2,7},{3,6},{4,1},{5,0},{6,3},{7,2},{8,13},{9,12},{10,... | collective-permute-start | bytes 196616 | tf_op jit(solution)/shard_map/ppermute | solution.py:69
  36.6 4.3 %collective-permute-start.7 = (bf16[64,512]{1,0:T(8,128)(2,1)S(1)}, bf16[64,512]{1,0:T(8,128)(2,1)S(1)}, u32[]{:S(2)}, u32[]{:S(2)}) collective-permute-start(bf16[64,512]{1,0:T(8,128)(2,1)S(1)} %get-tuple-element.87.refs_0_), channel_id=1, source_target_pairs={{0,1},{1,0},{2,3},{3,2},{4,5},{5,4},{6,7},{7,6},{8,9},{9,8},{10,11... | collective-permute-start | bytes 196616 | tf_op jit(solution)/shard_map/ppermute | solution.py:69
  38.8 14.1 %collective-permute-start.14 = (bf16[128,512]{1,0:T(8,128)(2,1)S(1)}, bf16[128,512]{1,0:T(8,128)(2,1)S(1)}, u32[]{:S(2)}, u32[]{:S(2)}) collective-permute-start(bf16[128,512]{1,0:T(8,128)(2,1)S(1)} %get-tuple-element.100), channel_id=1, source_target_pairs={{0,2},{2,0},{4,6},{6,4},{1,3},{3,1},{5,7},{7,5},{8,10},{10,8},{12,... | collective-permute-start | bytes 393224 | tf_op jit(solution)/shard_map/ppermute | solution.py:69
  38.9 14.5 %collective-permute-start.15 = (bf16[128,512]{1,0:T(8,128)(2,1)S(1)}, bf16[128,512]{1,0:T(8,128)(2,1)S(1)}, u32[]{:S(2)}, u32[]{:S(2)}) collective-permute-start(bf16[128,512]{1,0:T(8,128)(2,1)S(1)} %get-tuple-element.101), channel_id=1, source_target_pairs={{0,4},{2,6},{4,0},{6,2},{1,5},{3,7},{5,1},{7,3},{8,12},{10,14},{12... | collective-permute-start | bytes 393224 | tf_op jit(solution)/shard_map/ppermute | solution.py:69
  40.9 12.6 %collective-permute-start.16 = (bf16[128,512]{1,0:T(8,128)(2,1)S(1)}, bf16[128,512]{1,0:T(8,128)(2,1)S(1)}, u32[]{:S(2)}, u32[]{:S(2)}) collective-permute-start(bf16[128,512]{1,0:T(8,128)(2,1)S(1)} %get-tuple-element.102), channel_id=1, source_target_pairs={{0,6},{2,4},{4,2},{6,0},{1,7},{3,5},{5,3},{7,1},{8,14},{10,12},{12... | collective-permute-start | bytes 393224 | tf_op jit(solution)/shard_map/ppermute | solution.py:69
  43.6 13.5 %collective-permute-start.17 = (bf16[2,64,512]{2,1,0:T(8,128)(2,1)S(1)}, bf16[2,64,512]{2,1,0:T(8,128)(2,1)S(1)}, u32[]{:S(2)}, u32[]{:S(2)}) collective-permute-start(bf16[2,64,512]{2,1,0:T(8,128)(2,1)S(1)} %get-tuple-element.107), channel_id=1, source_target_pairs={{0,24},{8,16},{16,8},{24,0},{1,25},{9,17},{17,9},{25,1},{2,26},{10... | collective-permute-start | bytes 393224 | tf_op jit(solution)/shard_map/ppermute | solution.py:69
  52.7 12.8 %collective-permute-start.18 = (bf16[2,64,512]{2,1,0:T(8,128)(2,1)S(1)}, bf16[2,64,512]{2,1,0:T(8,128)(2,1)S(1)}, u32[]{:S(2)}, u32[]{:S(2)}) collective-permute-start(bf16[2,64,512]{2,1,0:T(8,128)(2,1)S(1)} %get-tuple-element.108), channel_id=1, source_target_pairs={{0,16},{8,24},{16,0},{24,8},{1,17},{9,25},{17,1},{25,9},{2,18},{10... | collective-permute-start | bytes 393224 | tf_op jit(solution)/shard_map/ppermute | solution.py:69
  53.0 12.5 %collective-permute-start.19 = (bf16[2,64,512]{2,1,0:T(8,128)(2,1)S(1)}, bf16[2,64,512]{2,1,0:T(8,128)(2,1)S(1)}, u32[]{:S(2)}, u32[]{:S(2)}) collective-permute-start(bf16[2,64,512]{2,1,0:T(8,128)(2,1)S(1)} %get-tuple-element.109), channel_id=1, source_target_pairs={{0,8},{8,0},{16,24},{24,16},{1,9},{9,1},{17,25},{25,17},{2,10},{10... | collective-permute-start | bytes 393224 | tf_op jit(solution)/shard_map/ppermute | solution.py:69

commit v9 on v8

--- a/solution.py
+++ b/solution.py
@@ -109,16 +109,25 @@
     return (rows == slots).astype(jnp.float32).astype(jnp.bfloat16)
 
 
-def stack_kernel(
+def stack_kernel(key_ref, value_ref, pair_ref, sems):
+    tok = key_ref.shape[0]
+    copies = [
+        pltpu.make_async_copy(ref, pair_ref.at[pl.ds(place * tok, tok), :], sems.at[place])
+        for place, ref in enumerate((key_ref, value_ref))
+    ]
+    for copy in copies:
+        copy.start()
+    for copy in copies:
+        copy.wait()
+
+
+def extend_kernel(
     ranks_ref,
     choice_ref,
     lengths_ref,
     router_ref,
-    key_ref,
-    value_ref,
     grad_ref,
     query_ref,
-    pair_ref,
     extended_ref,
     begin_ref,
     chosen_ref,
@@ -126,12 +135,10 @@
     held_lengths_ref,
     sems,
 ):
-    tok, width = key_ref.shape
+    tok, width = query_ref.shape
     targets = (
         (choice_ref, chosen_ref),
         (lengths_ref, held_lengths_ref),
-        (key_ref, pair_ref.at[pl.ds(0, tok), :]),
-        (value_ref, pair_ref.at[pl.ds(tok, tok), :]),
         (grad_ref, extended_ref.at[pl.ds(0, tok), :]),
         (query_ref, extended_ref.at[pl.ds(tok, tok), :]),
         (router_ref, held_router_ref),
@@ -155,13 +162,13 @@
             bound = bound + held_lengths_ref[0, doc]
             begin = jnp.maximum(begin, jnp.where(position >= bound, bound, 0))
         begin_ref[k : k + 1, :] = begin
-    copies[6].wait()
+    copies[4].wait()
     routed = held_router_ref[...].astype(jnp.float32)
     spare = extended_ref.shape[0] - 2 * tok - 16 - routed.shape[0]
     if spare:
         routed = jnp.concatenate([routed, jnp.zeros((spare, width), jnp.float32)], axis=0)
     extended_ref[2 * tok + 16 :, :] = routed.astype(jnp.bfloat16)
-    for copy in copies[2:6]:
+    for copy in copies[2:4]:
         copy.wait()
 
 
@@ -195,7 +202,8 @@
         if k in spreads:
             continue
         tok = begin_ref.shape[1]
-        turned = extended_ref[tok : 2 * tok, :].T
+        first_row = 0 if extended_ref.shape[0] == tok else tok
+        turned = extended_ref[first_row : first_row + tok, :].T
         head_of_row = lax.broadcasted_iota(jnp.int32, (lanes, tok), 0) // HD
         spreads[k] = []
         for group in range(turned.shape[0] // lanes):
@@ -218,10 +226,14 @@
         visible = (key_position >= begin) & (key_position <= position)
         bias_ref[place] = jnp.where(visible, 0.0, masked_score)
         bias = bias_ref[place]
-        values = pair_ref[tok : 2 * tok, :].T
+        if isinstance(pair_ref, tuple):
+            key_ref, value_ref, first_value = pair_ref[0], pair_ref[1], 0
+        else:
+            key_ref, value_ref, first_value = pair_ref, pair_ref, tok
+        values = value_ref[first_value : first_value + tok, :].T
         for group, spread in enumerate(spreads[k]):
             columns = slice(group * lanes, (group + 1) * lanes)
-            scores = dot(pair_ref[0:tok, columns], spread)
+            scores = dot(key_ref[0:tok, columns], spread)
             weights, factors = [], []
             for head in range(per):
                 row = group * per + head
@@ -268,7 +280,10 @@
     ks = sorted({k for k, unused_pair, unused_first in plan})
     old_ks = [k for k in ks if not any(first for j, unused_pair, first in plan if j == k)]
     extended_refs, refs = dict(zip(ks, refs)), refs[len(ks) :]
-    pair_refs, refs = refs[:counts], refs[counts:]
+    if counts == 0:
+        pair_refs, refs = [tuple(refs[:2])], refs[2:]
+    else:
+        pair_refs, refs = refs[:counts], refs[counts:]
     old_refs, refs = refs[: 3 * len(old_ks)], refs[3 * len(old_ks) :]
     bias_ref, refs = refs[-1], refs[:-1]
     packed_refs, state_refs = (refs[: len(ks)], refs[len(ks) :]) if packed else ((), refs)
@@ -520,16 +535,8 @@
         [parts.target(seq_index, k) * rep_count + rep_index for k in range(seq_count)]
     ).astype(jnp.int32)
 
-    def send(array, least_seq, seq_step, rep_step, wrap):
-        pairs = []
-        for s in range(least_seq, seq_count - seq_step):
-            for r in range(rep_count):
-                to = r + rep_step
-                if wrap or 0 <= to < rep_count:
-                    pairs.append(
-                        (s * rep_count + r, (s + seq_step) * rep_count + to % rep_count)
-                    )
-        return lax.ppermute(array, ("seq", "rep"), pairs)
+    def forward(array):
+        return lax.ppermute(array, "seq", [(i, (i + 1) % seq_count) for i in range(seq_count)])
 
     reach = (seq_count + 1) // 2
     longest = (seq_count * rep_count + 1) // 2
@@ -551,34 +558,39 @@
         shape((width, tok), jnp.float32),
     ]
     tail = 16 + -(-expert_count // 16) * 16
-    pair, extended, begin = pl.pallas_call(
-        stack_kernel,
-        out_shape=[
-            shape((2 * tok, width)),
-            shape((2 * tok + tail, width)),
-            shape((rep_count, tok), jnp.int32),
-        ],
-        in_specs=[SMEM] + [HBM] * 7,
-        out_specs=[VMEM] * 3,
-        scratch_shapes=[
+    def early(body, out_shape, specs, scratch):
+        return pl.pallas_call(
+            body,
+            out_shape=out_shape,
+            in_specs=specs,
+            out_specs=jax.tree.map(lambda unused: VMEM, out_shape),
+            scratch_shapes=scratch,
+            compiler_params=pltpu.CompilerParams(vmem_limit_bytes=60 * 1024 * 1024),
+        )
+
+    pair = early(
+        stack_kernel, shape((2 * tok, width)), [HBM, HBM], [pltpu.SemaphoreType.DMA((2,))]
+    )(key_rows[0], value_rows[0])
+    extended, begin = early(
+        extend_kernel,
+        [shape((2 * tok + tail, width)), shape((rep_count, tok), jnp.int32)],
+        [SMEM] + [HBM] * 5,
+        [
             pltpu.VMEM((1, tok), jnp.int32),
             pltpu.VMEM((expert_count, width), jnp.bfloat16),
             pltpu.SMEM(doc_lengths.shape, jnp.int32),
-            pltpu.SemaphoreType.DMA((7,)),
+            pltpu.SemaphoreType.DMA((5,)),
         ],
-        compiler_params=pltpu.CompilerParams(vmem_limit_bytes=60 * 1024 * 1024),
     )(
         jnp.stack(query_ranks).astype(jnp.int32),
         choice,
         doc_lengths,
         router.T,
-        key_rows[0],
-        value_rows[0],
         grad_out[0],
         query_rows[0],
     )
 
-    def attend(plan, pairs, steps, extendeds, states, packed, cost):
+    def attend(plan, pairs, steps, extendeds, states, packed, cost, raw=False):
         ks = sorted({k for k, unused_pair, unused_first in plan})
         old = [one for k in ks if k in states for one in states[k]]
         state_out = state_shapes * len(ks)
@@ -588,7 +600,9 @@
         else:
             out_shape, scratch = state_out, []
         outs = call(
-            functools.partial(attend_kernel, plan, rep_count, len(pairs), packed),
+            functools.partial(
+                attend_kernel, plan, rep_count, 0 if raw else len(pairs), packed
+            ),
             out_shape,
             [SMEM] + [VMEM] * (1 + len(ks) + len(pairs) + len(old)),
             scratch + [pltpu.VMEM((len(plan), tok, tok), jnp.float32)],
@@ -599,12 +613,14 @@
         return {k: list(outs[3 * place : 3 * place + 3]) for place, k in enumerate(ks)}
 
     others = range(1, rep_count)
-    lines = [pair, send(pair, 0, 1, 0, False)]
+    lines = [pair, forward(pair)]
     extendeds = reps.exchange([extended] * rep_count)
-    states = attend(((0, 0, True),), [pair], [0], [extended], {}, False, 2.0)
+    states = attend(
+        ((0, 0, True),), [key_rows[0], value_rows[0]], [0], [query_rows[0]], {}, False, 2.0, True
+    )
     lines[1], *states[0] = lax.optimization_barrier((lines[1], *states[0]))
     for step in range(2, reach + 1):
-        lines.append(send(lines[-1], step - 1, 1, 0, False))
+        lines.append(forward(lines[-1]))
     middle = tuple((0, step, False) for step in range(1, reach)) + tuple(
         (k, step, step == 0) for k in others for step in range(reach)
     )
@@ -628,7 +644,6 @@
         [SMEM] + [VMEM] * (6 + len(returned)),
         cost=2.0,
     )(own, extendeds[0], residual[0], out_proj, *states[0], *returned)
-    *sent_rows, got_grads = lax.optimization_barrier((*sent_rows, got_grads))
     arrived = owners.exchange([sent_rows[k // rep_count] for k in range(owners.count)])
     got_rows = merged(arrived[0::rep_count], MOST_PERMUTES)
     got_more = [

time: 66.5 us -> 60 us (0.902)
  starting transfers between devices: 28 us -> 20.7 us
  local copies, waits for them, and re-layouts: 2.7 us -> 0.78 us
  Pallas kernels: 15 us -> 16.5 us
  waiting for transfers between devices: 18.9 us -> 20.4 us
    ppermute x18, starting transfers between devices: 22.4 us -> 17.2 us  [exchange(): got[k] = lax.ppermute(chunks[k], self.axes, pairs)]
    ppermute x2, waiting for transfers between devices: 0.01 us -> 4.79 us  [forward(): lax.ppermute(array, 'seq', [(i, (i + 1) % seq_count) for i in range(seq_c...]
    ppermute x18, waiting for transfers between devices: 18.9 us -> 15.6 us  [exchange(): got[k] = lax.ppermute(chunks[k], self.axes, pairs)]
    ppermute x2, starting transfers between devices: 5.62 us -> 3.54 us  [forward(): lax.ppermute(array, 'seq', [(i, (i + 1) % seq_count) for i in range(seq_c...]
    unnamed x16 -> x20, local copies, waits for them, and re-layouts: 2.61 us -> 0.7 us
    pallas_call x5 -> x6, Pallas kernels: 8.21 us -> 9.78 us  [the longest x4 5.57 us: attend(): call(functools.partial(attend_kernel, plan, rep_count, 0 if raw else len(...]
  transfers between devices with their start and end apart: 20 -> 20, of which waited for: 7 -> 8; matrix products, arithmetic and copies ran while one was open for 0% -> 1% of each run, Pallas kernels for 16% -> 22%
where the time goes in v9:
time: 60 us
  starting transfers between devices  20.7 us (34%)
  waiting for transfers between devices  20.4 us (34%)
  Pallas kernels  16.5 us (28%)
  other arithmetic  0.81 us (1%)
  local copies, waits for them, and re-layouts  0.78 us (1%)
  between operations  0.78 us (1%)
    ppermute x18, starting transfers between devices, exchange(): got[k] = lax.ppermute(chunks[k], self.axes, pairs)  17.2 us
    ppermute x18, waiting for transfers between devices, exchange(): got[k] = lax.ppermute(chunks[k], self.axes, pairs)  15.6 us
    pallas_call x4, Pallas kernels, attend(): call(functools.partial(attend_kernel, plan, rep_count, 0 if raw else len(...  5.57 us
    ppermute x2, waiting for transfers between devices, forward(): lax.ppermute(array, 'seq', [(i, (i + 1) % seq_count) for i in range(seq_c...  4.79 us
    ppermute x2, starting transfers between devices, forward(): lax.ppermute(array, 'seq', [(i, (i + 1) % seq_count) for i in range(seq_c...  3.54 us
    pallas_call x2, Pallas kernels, expert_call(): call(functools.partial(expert_kernel, rep_count, rep_list, expert_count,...  3.46 us
    pallas_call x1, Pallas kernels, local(): early(extend_kernel, [shape((2 * tok + tail, width)), shape((rep_count, t...  2.53 us
    pallas_call x1, Pallas kernels, local(): early(stack_kernel, shape((2 * tok, width)), [HBM, HBM], [pltpu.Semaphore...  1.68 us
  transfers between devices with their start and end apart: 20, of which 8 were waited for; matrix products, arithmetic and copies ran while one was open for 1% of the time, Pallas kernels for 22%

profile of v9, /device:TPU:0, one launch (start us, length us, event | category | flops | bytes accessed | tf_op | source)
XLA Modules:
  0.0 60.0 jit_solution(3289883758531656046)
XLA Ops:
  0.6 1.7 %shard_map.139.refs_2_ = bf16[256,512]{1,0:T(8,128)(2,1)} custom-call(bf16[128,512]{1,0:T(8,128)(2,1)} %bitcast.28, bf16[128,512]{1,0:T(8,128)(2,1)} %bitcast.30), custom_call_target="tpu_custom_call" | custom-call | tf_op jit(solution)/shard_map/pallas_call | solution.py:571
  2.3 3.1 %collective-permute-start = (bf16[256,512]{1,0:T(8,128)(2,1)}, bf16[256,512]{1,0:T(8,128)(2,1)S(1)}, u32[]{:S(2)}, u32[]{:S(2)}) collective-permute-start(bf16[256,512]{1,0:T(8,128)(2,1)} %shard_map.139.refs_2_), channel_id=1, source_target_pairs={{0,8},{8,16},{16,24},{24,0},{1,9},{9,17},{17,25},{25,1},{2,10},{10... | collective-permute-start | bytes 786440 | tf_op jit(solution)/shard_map/ppermute | solution.py:539
  5.4 0.6 pad_add_fusion.1.ranks_ref
  6.0 2.5 %shard_map.138 = (bf16[288,512]{1,0:T(8,128)(2,1)}, s32[2,128]{1,0:T(2,128)}) custom-call(s32[2]{0:T(128)} %pad_add_fusion.1.ranks_ref, s32[1,128]{1,0:T(1,128)} %bitcast.39, s32[1,8]{1,0:T(1,128)} %lengths_ref.1, bf16[4,512]{1,0:T(4,128)(2,1)} %bitcast.38, bf16[128,512]{1,0:T(8,128)(2,1)} %bitcast.37, bf16[128,512]{1,0:T(8,128)(2,1)} %bitcast.26), custom_call_target="tpu_custom_call" | custom-call | tf_op jit(solution)/shard_map/pallas_call | solution.py:574
  8.5 1.6 %collective-permute-start.2 = (bf16[288,512]{1,0:T(8,128)(2,1)}, bf16[288,512]{1,0:T(8,128)(2,1)S(1)}, u32[]{:S(2)}, u32[]{:S(2)}) collective-permute-start(bf16[288,512]{1,0:T(8,128)(2,1)} %get-tuple-element.49.refs_0_.extended_ref), channel_id=1, source_target_pairs={{0,1},{1,0},{2,3},{3,2},{4,5},{5,4},{6,7},{7,6},{8,9},{9,8},{10,11... | collective-permute-start | bytes 884744 | tf_op jit(solution)/shard_map/ppermute | solution.py:69
  10.3 0.7 %copy-done.9 = s32[2,128]{1,0:T(2,128)S(1)} copy-done((s32[2,128]{1,0:T(2,128)S(1)}, s32[2,128]{1,0:T(2,128)}, u32[]{:S(2)}) %copy-start.9) | copy-done | bytes 1048
  11.0 1.7 %shard_map.140 = (f32[16,128]{1,0:T(8,128)S(1)}, f32[16,128]{1,0:T(8,128)S(1)}, f32[512,128]{1,0:T(8,128)S(1)}) custom-call(s32[3]{0:T(128)S(1)} %pad_add_fusion.4.ids_ref, s32[2,128]{1,0:T(2,128)S(1)} %copy-done.9, bf16[128,512]{1,0:T(8,128)(2,1)S(1)} %bitcast.27, bf16[128,512]{1,0:T(8,128)(2,1)S(1)} %bitcast.29, bf16[128,512]{1,0:T(8,128)(2,1)S(1)} %bitcast.31), custom_call_target="tpu_custom_call" | custom-call | flops 2000000000 | tf_op jit(solution)/shard_map/pallas_call | solution.py:602
  12.8 1.2 %collective-permute-done.refs_3_ = bf16[256,512]{1,0:T(8,128)(2,1)S(1)} collective-permute-done((bf16[256,512]{1,0:T(8,128)(2,1)}, bf16[256,512]{1,0:T(8,128)(2,1)S(1)}, u32[]{:S(2)}, u32[]{:S(2)}) %collective-permute-start) | collective-permute-done | bytes 262176 | tf_op jit(solution)/shard_map/ppermute | solution.py:539
  14.4 2.9 %collective-permute-done.2.refs_1_.refs_0_ = bf16[288,512]{1,0:T(8,128)(2,1)S(1)} collective-permute-done((bf16[288,512]{1,0:T(8,128)(2,1)}, bf16[288,512]{1,0:T(8,128)(2,1)S(1)}, u32[]{:S(2)}, u32[]{:S(2)}) %collective-permute-start.2) | collective-permute-done | bytes 294944 | tf_op jit(solution)/shard_map/ppermute | solution.py:69
  17.3 2.3 %shard_map.141 = (f32[16,128]{1,0:T(8,128)S(1)}, f32[16,128]{1,0:T(8,128)S(1)}, f32[512,128]{1,0:T(8,128)S(1)}, f32[16,128]{1,0:T(8,128)S(1)}, f32[16,128]{1,0:T(8,128)S(1)}, /*index=5*/f32[512,128]{1,0:T(8,128)S(1)}) custom-call(s32[5]{0:T(128)S(1)} %stack.81.ids_ref, s32[2,128]{1,0:T(2,128)S(1)} %copy-done.9, bf16[288,512]{1,0:T(8,128)(2,1)S(1)} %copy-done.7, ...), custom_call_target="tpu_custom_call" | custom-call | flops 4000000000 | tf_op jit(solution)/shard_map/pallas_call | solution.py:602
  19.6 3.6 %collective-permute-done.1.refs_1_ = bf16[256,512]{1,0:T(8,128)(2,1)S(1)} collective-permute-done((bf16[256,512]{1,0:T(8,128)(2,1)S(1)}, bf16[256,512]{1,0:T(8,128)(2,1)S(1)}, u32[]{:S(2)}, u32[]{:S(2)}) %collective-permute-start.1) | collective-permute-done | bytes 262176 | tf_op jit(solution)/shard_map/ppermute | solution.py:539
  23.2 0.8 %shard_map.143 = bf16[592,128]{1,0:T(8,128)(2,1)S(1)} custom-call(s32[3]{0:T(128)S(1)} %get-tuple-element.95.ids_ref, s32[2,128]{1,0:T(2,128)S(1)} %copy-done.9, bf16[288,512]{1,0:T(8,128)(2,1)S(1)} %collective-permute-done.2.refs_1_.refs_0_, bf16[256,512]{1,0:T(8,128)(2,1)S(1)} %collective-permute-done.1.refs_1_, f32[16,128]{1,0:T(8,128)S(1)} %get-tuple-element.64.refs_2_, ...), custom_call_target="tpu_custom_call" | custom-call | flops 1500000000 | tf_op jit(solution)/shard_map/pallas_call | solution.py:602
  24.0 1.3 %collective-permute-start.3 = (bf16[592,128]{1,0:T(8,128)(2,1)S(1)}, bf16[592,128]{1,0:T(8,128)(2,1)S(1)}, u32[]{:S(2)}, u32[]{:S(2)}) collective-permute-start(bf16[592,128]{1,0:T(8,128)(2,1)S(1)} %shard_map.143), channel_id=1, source_target_pairs={{0,1},{1,0},{2,3},{3,2},{4,5},{5,4},{6,7},{7,6},{8,9},{9,8},{10,11... | collective-permute-start | bytes 454664 | tf_op jit(solution)/shard_map/ppermute | solution.py:69
  25.9 1.6 %collective-permute-start.8 = (bf16[128,512]{1,0:T(8,128)(2,1)S(1)}, bf16[128,512]{1,0:T(8,128)(2,1)S(1)}, u32[]{:S(2)}, u32[]{:S(2)}) collective-permute-start(bf16[128,512]{1,0:T(8,128)(2,1)S(1)} %get-tuple-element.73), channel_id=1, source_target_pairs={{0,6},{2,4},{4,2},{6,0},{1,7},{3,5},{5,3},{7,1},{8,14},{10,12},{12... | collective-permute-start | bytes 393224 | tf_op jit(solution)/shard_map/ppermute | solution.py:69
  28.1 0.7 %shard_map.142 = (f32[16,128]{1,0:T(8,128)S(1)}, f32[16,128]{1,0:T(8,128)S(1)}, f32[512,128]{1,0:T(8,128)S(1)}) custom-call(s32[3]{0:T(128)S(1)} %get-tuple-element.94.ids_ref, s32[2,128]{1,0:T(2,128)S(1)} %copy-done.9, bf16[288,512]{1,0:T(8,128)(2,1)S(1)} %copy-done.7, bf16[256,512]{1,0:T(8,128)(2,1)S(1)} %collective-permute-done.1.refs_1_, ...), custom_call_target="tpu_custom_call" | custom-call | flops 1500000000 | tf_op jit(solution)/shard_map/pallas_call | solution.py:602
  29.3 0.6 %shard_map.144 = (bf16[128,512]{1,0:T(8,128)(2,1)S(1)}, bf16[64,512]{1,0:T(8,128)(2,1)S(1)}, bf16[64,512]{1,0:T(8,128)(2,1)S(1)}, bf16[64,512]{1,0:T(8,128)(2,1)S(1)}, bf16[64,512]{1,0:T(8,128)(2,1)S(1)}) custom-call(s32[1]{0:T(128)} %bitcast.own_ref, bf16[288,512]{1,0:T(8,128)(2,1)S(1)} %copy-done.7, bf16[128,512]{1,0:T(8,128)(2,1)S(1)} %bitcast.36, ...), custom_call_target="tpu_custom_call" | custom-call | flops 2000000000 | tf_op jit(solution)/shard_map/pallas_call | solution.py:641
  30.0 1.5 %collective-permute-start.12 = (bf16[64,512]{1,0:T(8,128)(2,1)S(1)}, bf16[64,512]{1,0:T(8,128)(2,1)S(1)}, u32[]{:S(2)}, u32[]{:S(2)}) collective-permute-start(bf16[64,512]{1,0:T(8,128)(2,1)S(1)} %get-tuple-element.70), channel_id=1, source_target_pairs={{0,4},{1,5},{2,6},{3,7},{4,0},{5,1},{6,2},{7,3},{8,12},{9,13},{10,... | collective-permute-start | bytes 196616 | tf_op jit(solution)/shard_map/ppermute | solution.py:69
  31.9 1.2 %collective-permute-start.5 = (bf16[64,512]{1,0:T(8,128)(2,1)S(1)}, bf16[64,512]{1,0:T(8,128)(2,1)S(1)}, u32[]{:S(2)}, u32[]{:S(2)}) collective-permute-start(bf16[64,512]{1,0:T(8,128)(2,1)S(1)} %get-tuple-element.69), channel_id=1, source_target_pairs={{0,3},{1,2},{2,1},{3,0},{4,7},{5,6},{6,5},{7,4},{8,11},{9,10},{10,... | collective-permute-start | bytes 196616 | tf_op jit(solution)/shard_map/ppermute | solution.py:69
  33.1 2.1 %collective-permute-done.9.refs_5_ = bf16[128,512]{1,0:T(8,128)(2,1)S(1)} collective-permute-done((bf16[128,512]{1,0:T(8,128)(2,1)S(1)}, bf16[128,512]{1,0:T(8,128)(2,1)S(1)}, u32[]{:S(2)}, u32[]{:S(2)}) %collective-permute-start.9) | collective-permute-done | bytes 131104 | tf_op jit(solution)/shard_map/ppermute | solution.py:69
  35.2 1.5 %collective-permute-start.6 = (bf16[64,512]{1,0:T(8,128)(2,1)S(1)}, bf16[64,512]{1,0:T(8,128)(2,1)S(1)}, u32[]{:S(2)}, u32[]{:S(2)}) collective-permute-start(bf16[64,512]{1,0:T(8,128)(2,1)S(1)} %get-tuple-element.70), channel_id=1, source_target_pairs={{0,5},{1,4},{2,7},{3,6},{4,1},{5,0},{6,3},{7,2},{8,13},{9,12},{10,... | collective-permute-start | bytes 196616 | tf_op jit(solution)/shard_map/ppermute | solution.py:69
  36.7 1.6 %collective-permute-start.4 = (bf16[64,512]{1,0:T(8,128)(2,1)S(1)}, bf16[64,512]{1,0:T(8,128)(2,1)S(1)}, u32[]{:S(2)}, u32[]{:S(2)}) collective-permute-start(bf16[64,512]{1,0:T(8,128)(2,1)S(1)} %get-tuple-element.68.refs_0_), channel_id=1, source_target_pairs={{0,1},{1,0},{2,3},{3,2},{4,5},{5,4},{6,7},{7,6},{8,9},{9,8},{10,11... | collective-permute-start | bytes 196616 | tf_op jit(solution)/shard_map/ppermute | solution.py:69
  38.2 1.8 %shard_map.146 = (bf16[128,512]{1,0:T(8,128)(2,1)S(1)}, bf16[128,512]{1,0:T(8,128)(2,1)S(1)}, bf16[128,512]{1,0:T(8,128)(2,1)S(1)}, bf16[128,512]{1,0:T(8,128)(2...) custom-call(s32[1]{0:T(128)} %bitcast.own_ref, s32[4]{0:T(128)S(1)} %pad_add_fusion.part_ref, ...), custom_call_target="tpu_custom_call" | custom-call | flops 2000000000 | tf_op jit(solution)/shard_map/pallas_call | solution.py:654
  40.1 0.6 collective-permute-start.14
  40.6 2.6 %collective-permute-done.4.refs_0_ = bf16[64,512]{1,0:T(8,128)(2,1)S(1)} collective-permute-done((bf16[64,512]{1,0:T(8,128)(2,1)S(1)}, bf16[64,512]{1,0:T(8,128)(2,1)S(1)}, u32[]{:S(2)}, u32[]{:S(2)}) %collective-permute-start.4) | collective-permute-done | bytes 65568 | tf_op jit(solution)/shard_map/ppermute | solution.py:69
  43.5 0.6 %collective-permute-start.16 = (bf16[128,512]{1,0:T(8,128)(2,1)S(1)}, bf16[128,512]{1,0:T(8,128)(2,1)S(1)}, u32[]{:S(2)}, u32[]{:S(2)}) collective-permute-start(bf16[128,512]{1,0:T(8,128)(2,1)S(1)} %get-tuple-element.84), channel_id=1, source_target_pairs={{0,6},{2,4},{4,2},{6,0},{1,7},{3,5},{5,3},{7,1},{8,14},{10,12},{12... | collective-permute-start | bytes 393224 | tf_op jit(solution)/shard_map/ppermute | solution.py:69
  44.1 1.6 %shard_map.147 = (bf16[2,64,512]{2,1,0:T(8,128)(2,1)S(1)}, bf16[2,64,512]{2,1,0:T(8,128)(2,1)S(1)}, bf16[2,64,512]{2,1,0:T(8,128)(2,1)S(1)}, f32[2,64,512]{2,1,0:T(8,128)S(1)}) custom-call(s32[1]{0:T(128)} %bitcast.own_ref, s32[4]{0:T(128)S(1)} %pad_add_fusion.part_ref, bf16[512,512]{1,0:T(8,128)(2,1)S(1)} %bitcast.33, bf16[512,512]{1,0:T(8,128)(2,1)S(1)} %bitcast.35, ...), custom_call_target="tpu_custom_call" | custom-call | flops 2000000000 | tf_op jit(solution)/shard_map/pallas_call | solution.py:654
  45.8 0.8 %collective-permute-start.18 = (bf16[2,64,512]{2,1,0:T(8,128)(2,1)S(1)}, bf16[2,64,512]{2,1,0:T(8,128)(2,1)S(1)}, u32[]{:S(2)}, u32[]{:S(2)}) collective-permute-start(bf16[2,64,512]{2,1,0:T(8,128)(2,1)S(1)} %get-tuple-element.90), channel_id=1, source_target_pairs={{0,16},{8,24},{16,0},{24,8},{1,17},{9,25},{17,1},{25,9},{2,18},{10... | collective-permute-start | bytes 393224 | tf_op jit(solution)/shard_map/ppermute | solution.py:69
  46.7 3.5 %collective-permute-start.19 = (bf16[2,64,512]{2,1,0:T(8,128)(2,1)S(1)}, bf16[2,64,512]{2,1,0:T(8,128)(2,1)S(1)}, u32[]{:S(2)}, u32[]{:S(2)}) collective-permute-start(bf16[2,64,512]{2,1,0:T(8,128)(2,1)S(1)} %get-tuple-element.91), channel_id=1, source_target_pairs={{0,8},{8,0},{16,24},{24,16},{1,9},{9,1},{17,25},{25,17},{2,10},{10... | collective-permute-start | bytes 393224 | tf_op jit(solution)/shard_map/ppermute | solution.py:69
  50.2 1.4 %shard_map.148 = (bf16[128,512]{1,0:T(8,128)(2,1)}, bf16[128,512]{1,0:T(8,128)(2,1)}) custom-call(s32[1]{0:T(128)} %bitcast.own_ref, bf16[128,512]{1,0:T(8,128)(2,1)S(1)} %get-tuple-element.80.mixed_ref, bf16[288,512]{1,0:T(8,128)(2,1)S(1)} %copy-done.7, bf16[128,512]{1,0:T(8,128)(2,1)S(1)} %get-tuple-element.81.refs_0_, ...), custom_call_target="tpu_custom_call" | custom-call | flops 1500000000 | tf_op jit(solution)/shard_map/pallas_call | solution.py:687
  51.6 2.3 %collective-permute-done.17.refs_0_ = bf16[2,64,512]{2,1,0:T(8,128)(2,1)S(1)} collective-permute-done((bf16[2,64,512]{2,1,0:T(8,128)(2,1)S(1)}, bf16[2,64,512]{2,1,0:T(8,128)(2,1)S(1)}, u32[]{:S(2)}, u32[]{:S(2)}) %collective-permute-start.17) | collective-permute-done | bytes 131104 | tf_op jit(solution)/shard_map/ppermute | solution.py:69
  53.9 5.3 %collective-permute-done.18.refs_1_ = bf16[2,64,512]{2,1,0:T(8,128)(2,1)S(1)} collective-permute-done((bf16[2,64,512]{2,1,0:T(8,128)(2,1)S(1)}, bf16[2,64,512]{2,1,0:T(8,128)(2,1)S(1)}, u32[]{:S(2)}, u32[]{:S(2)}) %collective-permute-start.18) | collective-permute-done | bytes 131104 | tf_op jit(solution)/shard_map/ppermute | solution.py:69
  59.3 0.7 %shard_map.149 = (f32[64,512]{1,0:T(8,128)}, f32[64,512]{1,0:T(8,128)}) custom-call(f32[2,64,512]{2,1,0:T(8,128)S(1)} %get-tuple-element.88.kept_ref, bf16[2,64,512]{2,1,0:T(8,128)(2,1)S(1)} %collective-permute-done.17.refs_0_, bf16[2,64,512]{2,1,0:T(8,128)(2,1)S(1)} %collective-permute-done.18.refs_1_, bf16[2,64,512]{2,1,0:T(8,128)(2,1)S(1)} %collective-permute-done.19.refs_2_), custom_call_target="tpu_custom_call" | custom-call | flops 500000000 | tf_op jit(solution)/shard_map/pallas_call | solution.py:694
  (45 shorter events, 3.2 us)
Async XLA Ops:
  2.3 11.6 %collective-permute-start = (bf16[256,512]{1,0:T(8,128)(2,1)}, bf16[256,512]{1,0:T(8,128)(2,1)S(1)}, u32[]{:S(2)}, u32[]{:S(2)}) collective-permute-start(bf16[256,512]{1,0:T(8,128)(2,1)} %shard_map.139.refs_2_), channel_id=1, source_target_pairs={{0,8},{8,16},{16,24},{24,0},{1,9},{9,17},{17,25},{25,1},{2,10},{10... | collective-permute-start | bytes 786440 | tf_op jit(solution)/shard_map/ppermute | solution.py:539
  6.0 4.4 %copy-start.2 = (bf16[1,128,512]{2,1,0:T(8,128)(2,1)S(1)}, bf16[1,128,512]{2,1,0:T(8,128)(2,1)}, u32[]{:S(2)}) copy-start(bf16[1,128,512]{2,1,0:T(8,128)(2,1)} %param.12) | copy-start | bytes 393220
  6.0 4.4 %copy-start.3 = (bf16[1,128,512]{2,1,0:T(8,128)(2,1)S(1)}, bf16[1,128,512]{2,1,0:T(8,128)(2,1)}, u32[]{:S(2)}) copy-start(bf16[1,128,512]{2,1,0:T(8,128)(2,1)} %param.13) | copy-start | bytes 393220
  8.5 1.8 %copy-start.1 = (bf16[1,128,512]{2,1,0:T(8,128)(2,1)S(1)}, bf16[1,128,512]{2,1,0:T(8,128)(2,1)}, u32[]{:S(2)}) copy-start(bf16[1,128,512]{2,1,0:T(8,128)(2,1)} %param.11) | copy-start | bytes 393220
  8.5 8.7 %collective-permute-start.2 = (bf16[288,512]{1,0:T(8,128)(2,1)}, bf16[288,512]{1,0:T(8,128)(2,1)S(1)}, u32[]{:S(2)}, u32[]{:S(2)}) collective-permute-start(bf16[288,512]{1,0:T(8,128)(2,1)} %get-tuple-element.49.refs_0_.extended_ref), channel_id=1, source_target_pairs={{0,1},{1,0},{2,3},{3,2},{4,5},{5,4},{6,7},{7,6},{8,9},{9,8},{10,11... | collective-permute-start | bytes 884744 | tf_op jit(solution)/shard_map/ppermute | solution.py:69
  10.3 0.7 %copy-start.9 = (s32[2,128]{1,0:T(2,128)S(1)}, s32[2,128]{1,0:T(2,128)}, u32[]{:S(2)}) copy-start(s32[2,128]{1,0:T(2,128)} %get-tuple-element.50.begin_ref) | copy-start | bytes 3076
  11.0 6.3 %copy-start = (bf16[256,512]{1,0:T(8,128)(2,1)S(1)}, bf16[256,512]{1,0:T(8,128)(2,1)}, u32[]{:S(2)}) copy-start(bf16[256,512]{1,0:T(8,128)(2,1)} %shard_map.139.refs_2_) | copy-start | bytes 786436
  11.0 6.3 %copy-start.7 = (bf16[288,512]{1,0:T(8,128)(2,1)S(1)}, bf16[288,512]{1,0:T(8,128)(2,1)}, u32[]{:S(2)}) copy-start(bf16[288,512]{1,0:T(8,128)(2,1)} %get-tuple-element.49.refs_0_.extended_ref) | copy-start | bytes 884740
  13.9 9.3 %collective-permute-start.1 = (bf16[256,512]{1,0:T(8,128)(2,1)S(1)}, bf16[256,512]{1,0:T(8,128)(2,1)S(1)}, u32[]{:S(2)}, u32[]{:S(2)}) collective-permute-start(bf16[256,512]{1,0:T(8,128)(2,1)S(1)} %collective-permute-done.refs_3_), channel_id=1, source_target_pairs={{0,8},{8,16},{16,24},{24,0},{1,9},{9,17},{17,25},{25,1},{2,10},{10... | collective-permute-start | bytes 786440 | tf_op jit(solution)/shard_map/ppermute | solution.py:539
  24.0 5.3 %collective-permute-start.3 = (bf16[592,128]{1,0:T(8,128)(2,1)S(1)}, bf16[592,128]{1,0:T(8,128)(2,1)S(1)}, u32[]{:S(2)}, u32[]{:S(2)}) collective-permute-start(bf16[592,128]{1,0:T(8,128)(2,1)S(1)} %shard_map.143), channel_id=1, source_target_pairs={{0,1},{1,0},{2,3},{3,2},{4,5},{5,4},{6,7},{7,6},{8,9},{9,8},{10,11... | collective-permute-start | bytes 454664 | tf_op jit(solution)/shard_map/ppermute | solution.py:69
  25.9 5.6 %collective-permute-start.10 = (bf16[128,512]{1,0:T(8,128)(2,1)S(1)}, bf16[128,512]{1,0:T(8,128)(2,1)S(1)}, u32[]{:S(2)}, u32[]{:S(2)}) collective-permute-start(bf16[128,512]{1,0:T(8,128)(2,1)S(1)} %get-tuple-element.75), channel_id=1, source_target_pairs={{0,2},{2,0},{4,6},{6,4},{1,3},{3,1},{5,7},{7,5},{8,10},{10,8},{12,... | collective-permute-start | bytes 393224 | tf_op jit(solution)/shard_map/ppermute | solution.py:69
  25.9 6.0 %collective-permute-start.8 = (bf16[128,512]{1,0:T(8,128)(2,1)S(1)}, bf16[128,512]{1,0:T(8,128)(2,1)S(1)}, u32[]{:S(2)}, u32[]{:S(2)}) collective-permute-start(bf16[128,512]{1,0:T(8,128)(2,1)S(1)} %get-tuple-element.73), channel_id=1, source_target_pairs={{0,6},{2,4},{4,2},{6,0},{1,7},{3,5},{5,3},{7,1},{8,14},{10,12},{12... | collective-permute-start | bytes 393224 | tf_op jit(solution)/shard_map/ppermute | solution.py:69
  27.6 7.6 %collective-permute-start.9 = (bf16[128,512]{1,0:T(8,128)(2,1)S(1)}, bf16[128,512]{1,0:T(8,128)(2,1)S(1)}, u32[]{:S(2)}, u32[]{:S(2)}) collective-permute-start(bf16[128,512]{1,0:T(8,128)(2,1)S(1)} %get-tuple-element.74), channel_id=1, source_target_pairs={{0,4},{2,6},{4,0},{6,2},{1,5},{3,7},{5,1},{7,3},{8,12},{10,14},{12... | collective-permute-start | bytes 393224 | tf_op jit(solution)/shard_map/ppermute | solution.py:69
  28.1 1.2 %copy-start.4 = (bf16[512,512]{1,0:T(8,128)(2,1)S(1)}, bf16[512,512]{1,0:T(8,128)(2,1)}, u32[]{:S(2)}) copy-start(bf16[512,512]{1,0:T(8,128)(2,1)} %proj_ref.1) | copy-start | bytes 1572868
  28.1 1.2 %copy-start.8 = (bf16[1,128,512]{2,1,0:T(8,128)(2,1)S(1)}, bf16[1,128,512]{2,1,0:T(8,128)(2,1)}, u32[]{:S(2)}) copy-start(bf16[1,128,512]{2,1,0:T(8,128)(2,1)} %param.15) | copy-start | bytes 393220
  29.3 9.0 %copy-start.5 = (bf16[1,512,512]{2,1,0:T(8,128)(2,1)S(1)}, bf16[1,512,512]{2,1,0:T(8,128)(2,1)}, u32[]{:S(2)}) copy-start(bf16[1,512,512]{2,1,0:T(8,128)(2,1)} %param.19) | copy-start | bytes 1572868
  29.3 9.0 %copy-start.6 = (bf16[1,512,512]{2,1,0:T(8,128)(2,1)S(1)}, bf16[1,512,512]{2,1,0:T(8,128)(2,1)}, u32[]{:S(2)}) copy-start(bf16[1,512,512]{2,1,0:T(8,128)(2,1)} %param.20) | copy-start | bytes 1572868
  29.9 6.8 %collective-permute-start.11 = (bf16[64,512]{1,0:T(8,128)(2,1)S(1)}, bf16[64,512]{1,0:T(8,128)(2,1)S(1)}, u32[]{:S(2)}, u32[]{:S(2)}) collective-permute-start(bf16[64,512]{1,0:T(8,128)(2,1)S(1)} %get-tuple-element.69), channel_id=1, source_target_pairs={{0,2},{1,3},{2,0},{3,1},{4,6},{5,7},{6,4},{7,5},{8,10},{9,11},{10,... | collective-permute-start | bytes 196616 | tf_op jit(solution)/shard_map/ppermute | solution.py:69
  30.0 6.7 %collective-permute-start.12 = (bf16[64,512]{1,0:T(8,128)(2,1)S(1)}, bf16[64,512]{1,0:T(8,128)(2,1)S(1)}, u32[]{:S(2)}, u32[]{:S(2)}) collective-permute-start(bf16[64,512]{1,0:T(8,128)(2,1)S(1)} %get-tuple-element.70), channel_id=1, source_target_pairs={{0,4},{1,5},{2,6},{3,7},{4,0},{5,1},{6,2},{7,3},{8,12},{9,13},{10,... | collective-permute-start | bytes 196616 | tf_op jit(solution)/shard_map/ppermute | solution.py:69
  31.4 6.8 %collective-permute-start.13 = (bf16[64,512]{1,0:T(8,128)(2,1)S(1)}, bf16[64,512]{1,0:T(8,128)(2,1)S(1)}, u32[]{:S(2)}, u32[]{:S(2)}) collective-permute-start(bf16[64,512]{1,0:T(8,128)(2,1)S(1)} %get-tuple-element.71), channel_id=1, source_target_pairs={{0,6},{1,7},{2,4},{3,5},{4,2},{5,3},{6,0},{7,1},{8,14},{9,15},{10,... | collective-permute-start | bytes 196616 | tf_op jit(solution)/shard_map/ppermute | solution.py:69
  31.9 11.6 %collective-permute-start.5 = (bf16[64,512]{1,0:T(8,128)(2,1)S(1)}, bf16[64,512]{1,0:T(8,128)(2,1)S(1)}, u32[]{:S(2)}, u32[]{:S(2)}) collective-permute-start(bf16[64,512]{1,0:T(8,128)(2,1)S(1)} %get-tuple-element.69), channel_id=1, source_target_pairs={{0,3},{1,2},{2,1},{3,0},{4,7},{5,6},{6,5},{7,4},{8,11},{9,10},{10,... | collective-permute-start | bytes 196616 | tf_op jit(solution)/shard_map/ppermute | solution.py:69
  35.2 9.0 %collective-permute-start.6 = (bf16[64,512]{1,0:T(8,128)(2,1)S(1)}, bf16[64,512]{1,0:T(8,128)(2,1)S(1)}, u32[]{:S(2)}, u32[]{:S(2)}) collective-permute-start(bf16[64,512]{1,0:T(8,128)(2,1)S(1)} %get-tuple-element.70), channel_id=1, source_target_pairs={{0,5},{1,4},{2,7},{3,6},{4,1},{5,0},{6,3},{7,2},{8,13},{9,12},{10,... | collective-permute-start | bytes 196616 | tf_op jit(solution)/shard_map/ppermute | solution.py:69
  36.7 7.5 %collective-permute-start.7 = (bf16[64,512]{1,0:T(8,128)(2,1)S(1)}, bf16[64,512]{1,0:T(8,128)(2,1)S(1)}, u32[]{:S(2)}, u32[]{:S(2)}) collective-permute-start(bf16[64,512]{1,0:T(8,128)(2,1)S(1)} %get-tuple-element.71), channel_id=1, source_target_pairs={{0,7},{1,6},{2,5},{3,4},{4,3},{5,2},{6,1},{7,0},{8,15},{9,14},{10,... | collective-permute-start | bytes 196616 | tf_op jit(solution)/shard_map/ppermute | solution.py:69
  36.7 6.5 %collective-permute-start.4 = (bf16[64,512]{1,0:T(8,128)(2,1)S(1)}, bf16[64,512]{1,0:T(8,128)(2,1)S(1)}, u32[]{:S(2)}, u32[]{:S(2)}) collective-permute-start(bf16[64,512]{1,0:T(8,128)(2,1)S(1)} %get-tuple-element.68.refs_0_), channel_id=1, source_target_pairs={{0,1},{1,0},{2,3},{3,2},{4,5},{5,4},{6,7},{7,6},{8,9},{9,8},{10,11... | collective-permute-start | bytes 196616 | tf_op jit(solution)/shard_map/ppermute | solution.py:69
  40.1 6.6 %collective-permute-start.14 = (bf16[128,512]{1,0:T(8,128)(2,1)S(1)}, bf16[128,512]{1,0:T(8,128)(2,1)S(1)}, u32[]{:S(2)}, u32[]{:S(2)}) collective-permute-start(bf16[128,512]{1,0:T(8,128)(2,1)S(1)} %get-tuple-element.82), channel_id=1, source_target_pairs={{0,2},{2,0},{4,6},{6,4},{1,3},{3,1},{5,7},{7,5},{8,10},{10,8},{12,... | collective-permute-start | bytes 393224 | tf_op jit(solution)/shard_map/ppermute | solution.py:69
  43.2 7.0 %collective-permute-start.15 = (bf16[128,512]{1,0:T(8,128)(2,1)S(1)}, bf16[128,512]{1,0:T(8,128)(2,1)S(1)}, u32[]{:S(2)}, u32[]{:S(2)}) collective-permute-start(bf16[128,512]{1,0:T(8,128)(2,1)S(1)} %get-tuple-element.83), channel_id=1, source_target_pairs={{0,4},{2,6},{4,0},{6,2},{1,5},{3,7},{5,1},{7,3},{8,12},{10,14},{12... | collective-permute-start | bytes 393224 | tf_op jit(solution)/shard_map/ppermute | solution.py:69
  43.5 6.7 %collective-permute-start.16 = (bf16[128,512]{1,0:T(8,128)(2,1)S(1)}, bf16[128,512]{1,0:T(8,128)(2,1)S(1)}, u32[]{:S(2)}, u32[]{:S(2)}) collective-permute-start(bf16[128,512]{1,0:T(8,128)(2,1)S(1)} %get-tuple-element.84), channel_id=1, source_target_pairs={{0,6},{2,4},{4,2},{6,0},{1,7},{3,5},{5,3},{7,1},{8,14},{10,12},{12... | collective-permute-start | bytes 393224 | tf_op jit(solution)/shard_map/ppermute | solution.py:69
  45.8 8.2 %collective-permute-start.17 = (bf16[2,64,512]{2,1,0:T(8,128)(2,1)S(1)}, bf16[2,64,512]{2,1,0:T(8,128)(2,1)S(1)}, u32[]{:S(2)}, u32[]{:S(2)}) collective-permute-start(bf16[2,64,512]{2,1,0:T(8,128)(2,1)S(1)} %get-tuple-element.89), channel_id=1, source_target_pairs={{0,24},{8,16},{16,8},{24,0},{1,25},{9,17},{17,9},{25,1},{2,26},{10... | collective-permute-start | bytes 393224 | tf_op jit(solution)/shard_map/ppermute | solution.py:69
  45.8 13.4 %collective-permute-start.18 = (bf16[2,64,512]{2,1,0:T(8,128)(2,1)S(1)}, bf16[2,64,512]{2,1,0:T(8,128)(2,1)S(1)}, u32[]{:S(2)}, u32[]{:S(2)}) collective-permute-start(bf16[2,64,512]{2,1,0:T(8,128)(2,1)S(1)} %get-tuple-element.90), channel_id=1, source_target_pairs={{0,16},{8,24},{16,0},{24,8},{1,17},{9,25},{17,1},{25,9},{2,18},{10... | collective-permute-start | bytes 393224 | tf_op jit(solution)/shard_map/ppermute | solution.py:69
  46.7 12.6 %collective-permute-start.19 = (bf16[2,64,512]{2,1,0:T(8,128)(2,1)S(1)}, bf16[2,64,512]{2,1,0:T(8,128)(2,1)S(1)}, u32[]{:S(2)}, u32[]{:S(2)}) collective-permute-start(bf16[2,64,512]{2,1,0:T(8,128)(2,1)S(1)} %get-tuple-element.91), channel_id=1, source_target_pairs={{0,8},{8,0},{16,24},{24,16},{1,9},{9,1},{17,25},{25,17},{2,10},{10... | collective-permute-start | bytes 393224 | tf_op jit(solution)/shard_map/ppermute | solution.py:69

commit v10 on v9

--- a/solution.py
+++ b/solution.py
@@ -127,7 +127,6 @@
     lengths_ref,
     router_ref,
     grad_ref,
-    query_ref,
     extended_ref,
     begin_ref,
     chosen_ref,
@@ -135,12 +134,11 @@
     held_lengths_ref,
     sems,
 ):
-    tok, width = query_ref.shape
+    tok, width = grad_ref.shape
     targets = (
         (choice_ref, chosen_ref),
         (lengths_ref, held_lengths_ref),
         (grad_ref, extended_ref.at[pl.ds(0, tok), :]),
-        (query_ref, extended_ref.at[pl.ds(tok, tok), :]),
         (router_ref, held_router_ref),
     )
     copies = [
@@ -151,8 +149,8 @@
         copy.start()
     copies[0].wait()
     chosen = jnp.broadcast_to(chosen_ref[...].astype(jnp.float32), (16, tok))
-    extended_ref[2 * tok : 2 * tok + 16, 0:tok] = chosen.astype(jnp.bfloat16)
-    extended_ref[2 * tok : 2 * tok + 16, tok:width] = jnp.zeros((16, width - tok), jnp.bfloat16)
+    extended_ref[tok : tok + 16, 0:tok] = chosen.astype(jnp.bfloat16)
+    extended_ref[tok : tok + 16, tok:width] = jnp.zeros((16, width - tok), jnp.bfloat16)
     copies[1].wait()
     for k in range(begin_ref.shape[0]):
         position = ranks_ref[k] * tok + lax.broadcasted_iota(jnp.int32, (1, tok), 1)
@@ -162,22 +160,21 @@
             bound = bound + held_lengths_ref[0, doc]
             begin = jnp.maximum(begin, jnp.where(position >= bound, bound, 0))
         begin_ref[k : k + 1, :] = begin
-    copies[4].wait()
+    copies[3].wait()
     routed = held_router_ref[...].astype(jnp.float32)
-    spare = extended_ref.shape[0] - 2 * tok - 16 - routed.shape[0]
+    spare = extended_ref.shape[0] - tok - 16 - routed.shape[0]
     if spare:
         routed = jnp.concatenate([routed, jnp.zeros((spare, width), jnp.float32)], axis=0)
-    extended_ref[2 * tok + 16 :, :] = routed.astype(jnp.bfloat16)
-    for copy in copies[2:4]:
-        copy.wait()
+    extended_ref[tok + 16 :, :] = routed.astype(jnp.bfloat16)
+    copies[2].wait()
 
 
 def chosen_of(extended_ref, tok):
-    return extended_ref[2 * tok : 2 * tok + 16, 0:tok].astype(jnp.float32)[0:1].astype(jnp.int32)
+    return extended_ref[tok : tok + 16, 0:tok].astype(jnp.float32)[0:1].astype(jnp.int32)
 
 
 def router_of(extended_ref, tok, expert_count):
-    whole = extended_ref[2 * tok + 16 :, :].astype(jnp.float32)
+    whole = extended_ref[tok + 16 :, :].astype(jnp.float32)
     return whole[0:expert_count].astype(jnp.bfloat16)
 
 
@@ -198,12 +195,13 @@
     per = lanes // HD
     scale = math.log2(math.e) / math.sqrt(HD)
     spreads = {}
-    for k, extended_ref, unused_pair, unused_first in tasks:
+    lowest = {}
+    for k, query_ref, unused_pair, unused_first in tasks:
         if k in spreads:
             continue
+        lowest[k] = jnp.min(begin_ref[k : k + 1, :])
         tok = begin_ref.shape[1]
-        first_row = 0 if extended_ref.shape[0] == tok else tok
-        turned = extended_ref[first_row : first_row + tok, :].T
+        turned = query_ref[...].T
         head_of_row = lax.broadcasted_iota(jnp.int32, (lanes, tok), 0) // HD
         spreads[k] = []
         for group in range(turned.shape[0] // lanes):
@@ -258,7 +256,7 @@
                     piece = piece + sum_ref[rows, :] * factors[head]
                 sum_ref[rows, :] = piece
 
-    for place, (k, unused_extended, pair_ref, first) in enumerate(tasks):
+    for place, (k, unused_query, pair_ref, first) in enumerate(tasks):
         block = ids_ref[reps + place]
         begin = begin_ref[k : k + 1, :]
         tok = begin.shape[1]
@@ -271,15 +269,15 @@
             total_ref[...] = jnp.zeros(total_ref.shape, jnp.float32)
             sum_ref[...] = jnp.zeros(sum_ref.shape, jnp.float32)
 
-        @pl.when((block >= 0) & ((block + 1) * tok > jnp.min(begin)))
+        @pl.when((block >= 0) & ((block + 1) * tok > lowest[k]))
         def unused(place=place, k=k, pair_ref=pair_ref, block=block, begin=begin):
             fold(place, k, pair_ref, block, begin, False)
 
 
-def attend_kernel(plan, reps, counts, packed, ids_ref, begin_ref, *refs):
+def attend_kernel(plan, reps, counts, packed, ahead, ids_ref, begin_ref, *refs):
     ks = sorted({k for k, unused_pair, unused_first in plan})
     old_ks = [k for k in ks if not any(first for j, unused_pair, first in plan if j == k)]
-    extended_refs, refs = dict(zip(ks, refs)), refs[len(ks) :]
+    query_refs, refs = dict(zip(ks, refs)), refs[len(ks) + ahead :]
     if counts == 0:
         pair_refs, refs = [tuple(refs[:2])], refs[2:]
     else:
@@ -291,7 +289,7 @@
     for place, k in enumerate(old_ks):
         for old_ref, new_ref in zip(old_refs[3 * place : 3 * place + 3], states[k]):
             new_ref[...] = old_ref[...]
-    tasks = [(k, extended_refs[k], pair_refs[pair], first) for k, pair, first in plan]
+    tasks = [(k, query_refs[k], pair_refs[pair], first) for k, pair, first in plan]
     fold_blocks(ids_ref, begin_ref, tasks, reps, states, bias_ref)
     for k, packed_ref in zip(ks, packed_refs):
         top_ref, total_ref, sum_ref = states[k]
@@ -573,13 +571,13 @@
     )(key_rows[0], value_rows[0])
     extended, begin = early(
         extend_kernel,
-        [shape((2 * tok + tail, width)), shape((rep_count, tok), jnp.int32)],
-        [SMEM] + [HBM] * 5,
+        [shape((tok + tail, width)), shape((rep_count, tok), jnp.int32)],
+        [SMEM] + [HBM] * 4,
         [
             pltpu.VMEM((1, tok), jnp.int32),
             pltpu.VMEM((expert_count, width), jnp.bfloat16),
             pltpu.SMEM(doc_lengths.shape, jnp.int32),
-            pltpu.SemaphoreType.DMA((5,)),
+            pltpu.SemaphoreType.DMA((4,)),
         ],
     )(
         jnp.stack(query_ranks).astype(jnp.int32),
@@ -587,10 +585,9 @@
         doc_lengths,
         router.T,
         grad_out[0],
-        query_rows[0],
-    )
-
-    def attend(plan, pairs, steps, extendeds, states, packed, cost, raw=False):
+    )
+
+    def attend(plan, pairs, steps, queries, states, packed, cost, raw=False, ahead=()):
         ks = sorted({k for k, unused_pair, unused_first in plan})
         old = [one for k in ks if k in states for one in states[k]]
         state_out = state_shapes * len(ks)
@@ -601,22 +598,23 @@
             out_shape, scratch = state_out, []
         outs = call(
             functools.partial(
-                attend_kernel, plan, rep_count, 0 if raw else len(pairs), packed
+                attend_kernel, plan, rep_count, 0 if raw else len(pairs), packed, len(ahead)
             ),
             out_shape,
-            [SMEM] + [VMEM] * (1 + len(ks) + len(pairs) + len(old)),
+            [SMEM] + [VMEM] * (1 + len(ks) + len(ahead) + len(pairs) + len(old)),
             scratch + [pltpu.VMEM((len(plan), tok, tok), jnp.float32)],
             cost=cost,
-        )(task_ids(plan, steps), begin, *[extendeds[k] for k in ks], *pairs, *old)
+        )(task_ids(plan, steps), begin, *[queries[k] for k in ks], *ahead, *pairs, *old)
         if packed:
             return dict(zip(ks, outs))
         return {k: list(outs[3 * place : 3 * place + 3]) for place, k in enumerate(ks)}
 
     others = range(1, rep_count)
     lines = [pair, forward(pair)]
+    queries = reps.exchange([query_rows[0]] * rep_count)
     extendeds = reps.exchange([extended] * rep_count)
     states = attend(
-        ((0, 0, True),), [key_rows[0], value_rows[0]], [0], [query_rows[0]], {}, False, 2.0, True
+        ((0, 0, True),), [key_rows[0], value_rows[0]], [0], queries, {}, False, 2.0, True
     )
     lines[1], *states[0] = lax.optimization_barrier((lines[1], *states[0]))
     for step in range(2, reach + 1):
@@ -624,18 +622,25 @@
     middle = tuple((0, step, False) for step in range(1, reach)) + tuple(
         (k, step, step == 0) for k in others for step in range(reach)
     )
-    states = attend(middle, lines[:-1], list(range(reach)), extendeds, states, False, 4.0)
-    partial = attend(
-        tuple((k, 0, False) for k in others), lines[-1:], [reach], extendeds, states, True, 1.5
-    )
-    partial[1], *extendeds[1:] = lax.optimization_barrier((partial[1], *extendeds[1:]))
-    returned = reps.exchange([None] + [partial[k] for k in others], inverse=True)[1:]
-    states = attend(((0, 0, False),), lines[-1:], [reach], extendeds, states, False, 1.5)
+    states = attend(middle, lines[:-1], list(range(reach)), queries, states, False, 4.0)
+    states[1][0], *extendeds[1:] = lax.optimization_barrier((states[1][0], *extendeds[1:]))
     sent_grads = call(
         functools.partial(dispatch_kernel, rep_count, tok, hot_capacity),
         [shape((rep_count * hot_capacity, width))] * expert_count,
         [SMEM] + [VMEM] * rep_count,
     )(own, *extendeds)
+    partial = attend(
+        tuple((k, 0, False) for k in others),
+        lines[-1:],
+        [reach],
+        queries,
+        states,
+        True,
+        1.5,
+        ahead=sent_grads[:1],
+    )
+    returned = reps.exchange([None] + [partial[k] for k in others], inverse=True)[1:]
+    states = attend(((0, 0, False),), lines[-1:], [reach], queries, states, False, 1.5)
     got_grads = merged(experts.exchange(sent_grads), MOST_PERMUTES)[::-1]
 
     mixed, *sent_rows = call(

time: 60 us -> 59.2 us (0.987)
  waiting for transfers between devices: 20.4 us -> 17.2 us
  starting transfers between devices: 20.7 us -> 23.3 us
    ppermute x18 -> x19, waiting for transfers between devices: 15.6 us -> 10.4 us  [exchange(): got[k] = lax.ppermute(chunks[k], self.axes, pairs)]
    ppermute x18 -> x19, starting transfers between devices: 17.2 us -> 19.4 us  [exchange(): got[k] = lax.ppermute(chunks[k], self.axes, pairs)]
    ppermute x2, waiting for transfers between devices: 4.79 us -> 6.82 us  [forward(): lax.ppermute(array, 'seq', [(i, (i + 1) % seq_count) for i in range(seq_c...]
  transfers between devices with their start and end apart: 20 -> 21, of which waited for: 8 -> 6; matrix products, arithmetic and copies ran while one was open for 1% -> 2% of each run, Pallas kernels for 22% -> 22%
where the time goes in v10:
time: 59.2 us; the launch traced here: 59 us
  starting transfers between devices  23.3 us (39%)
  waiting for transfers between devices  17.2 us (29%)
  Pallas kernels  16 us (27%)
  other arithmetic  0.89 us (2%)
  between operations  0.86 us (1%)
  local copies, waits for them, and re-layouts  0.8 us (1%)
    ppermute x19, starting transfers between devices, exchange(): got[k] = lax.ppermute(chunks[k], self.axes, pairs)  19.4 us
    ppermute x19, waiting for transfers between devices, exchange(): got[k] = lax.ppermute(chunks[k], self.axes, pairs)  10.4 us
    ppermute x2, waiting for transfers between devices, forward(): lax.ppermute(array, 'seq', [(i, (i + 1) % seq_count) for i in range(seq_c...  6.82 us
    pallas_call x4, Pallas kernels, attend(): call(functools.partial(attend_kernel, plan, rep_count, 0 if raw else len(...  5.17 us
    ppermute x2, starting transfers between devices, forward(): lax.ppermute(array, 'seq', [(i, (i + 1) % seq_count) for i in range(seq_c...  3.85 us
    pallas_call x2, Pallas kernels, expert_call(): call(functools.partial(expert_kernel, rep_count, rep_list, expert_count,...  3.45 us
    pallas_call x1, Pallas kernels, local(): early(extend_kernel, [shape((tok + tail, width)), shape((rep_count, tok),...  2.29 us
    pallas_call x1, Pallas kernels, local(): early(stack_kernel, shape((2 * tok, width)), [HBM, HBM], [pltpu.Semaphore...  1.73 us
  transfers between devices with their start and end apart: 21, of which 6 were waited for; matrix products, arithmetic and copies ran while one was open for 2% of the time, Pallas kernels for 22%

profile of v10, /device:TPU:0, one launch (start us, length us, event | category | flops | bytes accessed | tf_op | source)
XLA Modules:
  0.0 59.0 jit_solution(16879676117231286835)
XLA Ops:
  0.7 1.7 %shard_map.139.refs_2_ = bf16[256,512]{1,0:T(8,128)(2,1)} custom-call(bf16[128,512]{1,0:T(8,128)(2,1)} %bitcast.26, bf16[128,512]{1,0:T(8,128)(2,1)} %bitcast.28), custom_call_target="tpu_custom_call" | custom-call | tf_op jit(solution)/shard_map/pallas_call | solution.py:569
  2.4 3.1 %collective-permute-start = (bf16[256,512]{1,0:T(8,128)(2,1)}, bf16[256,512]{1,0:T(8,128)(2,1)S(1)}, u32[]{:S(2)}, u32[]{:S(2)}) collective-permute-start(bf16[256,512]{1,0:T(8,128)(2,1)} %shard_map.139.refs_2_), channel_id=1, source_target_pairs={{0,8},{8,16},{16,24},{24,0},{1,9},{9,17},{17,25},{25,1},{2,10},{10... | collective-permute-start | bytes 786440 | tf_op jit(solution)/shard_map/ppermute | solution.py:537
  5.5 1.5 %collective-permute-start.2 = (bf16[128,512]{1,0:T(8,128)(2,1)S(1)}, bf16[128,512]{1,0:T(8,128)(2,1)S(1)}, u32[]{:S(2)}, u32[]{:S(2)}) collective-permute-start(bf16[128,512]{1,0:T(8,128)(2,1)S(1)} %bitcast.34), channel_id=1, source_target_pairs={{0,1},{1,0},{2,3},{3,2},{4,5},{5,4},{6,7},{7,6},{8,9},{9,8},{10,11... | collective-permute-start | bytes 393224 | tf_op jit(solution)/shard_map/ppermute | solution.py:69
  7.6 2.3 %shard_map.138 = (bf16[160,512]{1,0:T(8,128)(2,1)}, s32[2,128]{1,0:T(2,128)}) custom-call(s32[2]{0:T(128)} %pad_add_fusion.1.ranks_ref, s32[1,128]{1,0:T(1,128)} %bitcast.41, s32[1,8]{1,0:T(1,128)} %lengths_ref.1, bf16[4,512]{1,0:T(4,128)(2,1)} %bitcast.40, bf16[128,512]{1,0:T(8,128)(2,1)} %bitcast.39), custom_call_target="tpu_custom_call" | custom-call | tf_op jit(solution)/shard_map/pallas_call | solution.py:572
  10.5 0.7 %copy-done.9 = s32[2,128]{1,0:T(2,128)S(1)} copy-done((s32[2,128]{1,0:T(2,128)S(1)}, s32[2,128]{1,0:T(2,128)}, u32[]{:S(2)}) %copy-start.9) | copy-done | bytes 1048
  11.2 1.7 %shard_map.140 = (f32[16,128]{1,0:T(8,128)S(1)}, f32[16,128]{1,0:T(8,128)S(1)}, f32[512,128]{1,0:T(8,128)S(1)}) custom-call(s32[3]{0:T(128)S(1)} %pad_add_fusion.4.ids_ref, s32[2,128]{1,0:T(2,128)S(1)} %copy-done.9, bf16[128,512]{1,0:T(8,128)(2,1)S(1)} %bitcast.35, bf16[128,512]{1,0:T(8,128)(2,1)S(1)} %bitcast.27, bf16[128,512]{1,0:T(8,128)(2,1)S(1)} %bitcast.29), custom_call_target="tpu_custom_call" | custom-call | flops 2000000000 | tf_op jit(solution)/shard_map/pallas_call | solution.py:599
  13.2 0.8 %collective-permute-done.refs_3_ = bf16[256,512]{1,0:T(8,128)(2,1)S(1)} collective-permute-done((bf16[256,512]{1,0:T(8,128)(2,1)}, bf16[256,512]{1,0:T(8,128)(2,1)S(1)}, u32[]{:S(2)}, u32[]{:S(2)}) %collective-permute-start) | collective-permute-done | bytes 262176 | tf_op jit(solution)/shard_map/ppermute | solution.py:537
  14.0 0.8 %collective-permute-start.1 = (bf16[256,512]{1,0:T(8,128)(2,1)S(1)}, bf16[256,512]{1,0:T(8,128)(2,1)S(1)}, u32[]{:S(2)}, u32[]{:S(2)}) collective-permute-start(bf16[256,512]{1,0:T(8,128)(2,1)S(1)} %collective-permute-done.refs_3_), channel_id=1, source_target_pairs={{0,8},{8,16},{16,24},{24,0},{1,9},{9,17},{17,25},{25,1},{2,10},{10... | collective-permute-start | bytes 786440 | tf_op jit(solution)/shard_map/ppermute | solution.py:537
  14.8 1.9 %shard_map.141 = (f32[16,128]{1,0:T(8,128)S(1)}, f32[16,128]{1,0:T(8,128)S(1)}, f32[512,128]{1,0:T(8,128)S(1)}, f32[16,128]{1,0:T(8,128)S(1)}, f32[16,128]{1,0:T(8,128)S(1)}, /*index=5*/f32[512,128]{1,0:T(8,128)S(1)}) custom-call(s32[5]{0:T(128)S(1)} %stack.81.ids_ref, s32[2,128]{1,0:T(2,128)S(1)} %copy-done.9, bf16[128,512]{1,0:T(8,128)(2,1)S(1)} %bitcast.36, ...), custom_call_target="tpu_custom_call" | custom-call | flops 4000000000 | tf_op jit(solution)/shard_map/pallas_call | solution.py:599
  17.3 6.0 %collective-permute-done.1.refs_1_.refs_2_ = bf16[256,512]{1,0:T(8,128)(2,1)S(1)} collective-permute-done((bf16[256,512]{1,0:T(8,128)(2,1)S(1)}, bf16[256,512]{1,0:T(8,128)(2,1)S(1)}, u32[]{:S(2)}, u32[]{:S(2)}) %collective-permute-start.1) | collective-permute-done | bytes 262176 | tf_op jit(solution)/shard_map/ppermute | solution.py:537
  23.3 0.8 %shard_map.144 = bf16[592,128]{1,0:T(8,128)(2,1)S(1)} custom-call(s32[3]{0:T(128)S(1)} %pad_add_fusion.5.ids_ref, s32[2,128]{1,0:T(2,128)S(1)} %copy-done.9, bf16[128,512]{1,0:T(8,128)(2,1)S(1)} %collective-permute-done.2.refs_1_.refs_0_, bf16[128,512]{1,0:T(8,128)(2,1)S(1)} %get-tuple-element.66.refs_1_.refs_7_, ...), custom_call_target="tpu_custom_call" | custom-call | flops 1500000000 | tf_op jit(solution)/shard_map/pallas_call | solution.py:599
  24.1 1.3 %collective-permute-start.4 = (bf16[592,128]{1,0:T(8,128)(2,1)S(1)}, bf16[592,128]{1,0:T(8,128)(2,1)S(1)}, u32[]{:S(2)}, u32[]{:S(2)}) collective-permute-start(bf16[592,128]{1,0:T(8,128)(2,1)S(1)} %shard_map.144), channel_id=1, source_target_pairs={{0,1},{1,0},{2,3},{3,2},{4,5},{5,4},{6,7},{7,6},{8,9},{9,8},{10,11... | collective-permute-start | bytes 454664 | tf_op jit(solution)/shard_map/ppermute | solution.py:69
  25.5 1.5 %collective-permute-start.10 = (bf16[128,512]{1,0:T(8,128)(2,1)S(1)}, bf16[128,512]{1,0:T(8,128)(2,1)S(1)}, u32[]{:S(2)}, u32[]{:S(2)}) collective-permute-start(bf16[128,512]{1,0:T(8,128)(2,1)S(1)} %get-tuple-element.75), channel_id=1, source_target_pairs={{0,4},{2,6},{4,0},{6,2},{1,5},{3,7},{5,1},{7,3},{8,12},{10,14},{12... | collective-permute-start | bytes 393224 | tf_op jit(solution)/shard_map/ppermute | solution.py:69
  27.0 0.6 %collective-permute-start.9 = (bf16[128,512]{1,0:T(8,128)(2,1)S(1)}, bf16[128,512]{1,0:T(8,128)(2,1)S(1)}, u32[]{:S(2)}, u32[]{:S(2)}) collective-permute-start(bf16[128,512]{1,0:T(8,128)(2,1)S(1)} %get-tuple-element.74), channel_id=1, source_target_pairs={{0,6},{2,4},{4,2},{6,0},{1,7},{3,5},{5,3},{7,1},{8,14},{10,12},{12... | collective-permute-start | bytes 393224 | tf_op jit(solution)/shard_map/ppermute | solution.py:69
  27.6 0.7 %shard_map.142 = (f32[16,128]{1,0:T(8,128)S(1)}, f32[16,128]{1,0:T(8,128)S(1)}, f32[512,128]{1,0:T(8,128)S(1)}) custom-call(s32[3]{0:T(128)S(1)} %pad_add_fusion.2.ids_ref, s32[2,128]{1,0:T(2,128)S(1)} %copy-done.9, bf16[128,512]{1,0:T(8,128)(2,1)S(1)} %bitcast.37, bf16[256,512]{1,0:T(8,128)(2,1)S(1)} %collective-permute-done.1.refs_1_.refs_2_, ...), custom_call_target="tpu_custom_call" | custom-call | flops 1500000000 | tf_op jit(solution)/shard_map/pallas_call | solution.py:599
  28.4 1.0 %collective-permute-done.4.refs_3_ = bf16[592,128]{1,0:T(8,128)(2,1)S(1)} collective-permute-done((bf16[592,128]{1,0:T(8,128)(2,1)S(1)}, bf16[592,128]{1,0:T(8,128)(2,1)S(1)}, u32[]{:S(2)}, u32[]{:S(2)}) %collective-permute-start.4) | collective-permute-done | bytes 151584 | tf_op jit(solution)/shard_map/ppermute | solution.py:69
  30.0 1.3 %collective-permute-start.13 = (bf16[64,512]{1,0:T(8,128)(2,1)S(1)}, bf16[64,512]{1,0:T(8,128)(2,1)S(1)}, u32[]{:S(2)}, u32[]{:S(2)}) collective-permute-start(bf16[64,512]{1,0:T(8,128)(2,1)S(1)} %get-tuple-element.72), channel_id=1, source_target_pairs={{0,4},{1,5},{2,6},{3,7},{4,0},{5,1},{6,2},{7,3},{8,12},{9,13},{10,... | collective-permute-start | bytes 196616 | tf_op jit(solution)/shard_map/ppermute | solution.py:69
  32.0 1.5 %collective-permute-start.6 = (bf16[64,512]{1,0:T(8,128)(2,1)S(1)}, bf16[64,512]{1,0:T(8,128)(2,1)S(1)}, u32[]{:S(2)}, u32[]{:S(2)}) collective-permute-start(bf16[64,512]{1,0:T(8,128)(2,1)S(1)} %get-tuple-element.71), channel_id=1, source_target_pairs={{0,3},{1,2},{2,1},{3,0},{4,7},{5,6},{6,5},{7,4},{8,11},{9,10},{10,... | collective-permute-start | bytes 196616 | tf_op jit(solution)/shard_map/ppermute | solution.py:69
  33.5 1.1 %collective-permute-start.7 = (bf16[64,512]{1,0:T(8,128)(2,1)S(1)}, bf16[64,512]{1,0:T(8,128)(2,1)S(1)}, u32[]{:S(2)}, u32[]{:S(2)}) collective-permute-start(bf16[64,512]{1,0:T(8,128)(2,1)S(1)} %get-tuple-element.72), channel_id=1, source_target_pairs={{0,5},{1,4},{2,7},{3,6},{4,1},{5,0},{6,3},{7,2},{8,13},{9,12},{10,... | collective-permute-start | bytes 196616 | tf_op jit(solution)/shard_map/ppermute | solution.py:69
  34.7 1.2 %collective-permute-start.8 = (bf16[64,512]{1,0:T(8,128)(2,1)S(1)}, bf16[64,512]{1,0:T(8,128)(2,1)S(1)}, u32[]{:S(2)}, u32[]{:S(2)}) collective-permute-start(bf16[64,512]{1,0:T(8,128)(2,1)S(1)} %get-tuple-element.73), channel_id=1, source_target_pairs={{0,7},{1,6},{2,5},{3,4},{4,3},{5,2},{6,1},{7,0},{8,15},{9,14},{10,... | collective-permute-start | bytes 196616 | tf_op jit(solution)/shard_map/ppermute | solution.py:69
  36.4 1.8 %shard_map.146 = (bf16[128,512]{1,0:T(8,128)(2,1)S(1)}, bf16[128,512]{1,0:T(8,128)(2,1)S(1)}, bf16[128,512]{1,0:T(8,128)(2,1)S(1)}, bf16[128,512]{1,0:T(8,128)(2...) custom-call(s32[1]{0:T(128)} %bitcast.own_ref, s32[4]{0:T(128)S(1)} %pad_add_fusion.part_ref, ...), custom_call_target="tpu_custom_call" | custom-call | flops 2000000000 | tf_op jit(solution)/shard_map/pallas_call | solution.py:659
  38.3 1.6 %collective-permute-start.15 = (bf16[128,512]{1,0:T(8,128)(2,1)S(1)}, bf16[128,512]{1,0:T(8,128)(2,1)S(1)}, u32[]{:S(2)}, u32[]{:S(2)}) collective-permute-start(bf16[128,512]{1,0:T(8,128)(2,1)S(1)} %get-tuple-element.82), channel_id=1, source_target_pairs={{0,2},{2,0},{4,6},{6,4},{1,3},{3,1},{5,7},{7,5},{8,10},{10,8},{12,... | collective-permute-start | bytes 393224 | tf_op jit(solution)/shard_map/ppermute | solution.py:69
  39.8 1.4 %collective-permute-done.5.refs_0_ = bf16[64,512]{1,0:T(8,128)(2,1)S(1)} collective-permute-done((bf16[64,512]{1,0:T(8,128)(2,1)S(1)}, bf16[64,512]{1,0:T(8,128)(2,1)S(1)}, u32[]{:S(2)}, u32[]{:S(2)}) %collective-permute-start.5) | collective-permute-done | bytes 65568 | tf_op jit(solution)/shard_map/ppermute | solution.py:69
  41.3 0.8 %collective-permute-start.16 = (bf16[128,512]{1,0:T(8,128)(2,1)S(1)}, bf16[128,512]{1,0:T(8,128)(2,1)S(1)}, u32[]{:S(2)}, u32[]{:S(2)}) collective-permute-start(bf16[128,512]{1,0:T(8,128)(2,1)S(1)} %get-tuple-element.83), channel_id=1, source_target_pairs={{0,4},{2,6},{4,0},{6,2},{1,5},{3,7},{5,1},{7,3},{8,12},{10,14},{12... | collective-permute-start | bytes 393224 | tf_op jit(solution)/shard_map/ppermute | solution.py:69
  42.1 0.7 %collective-permute-start.17 = (bf16[128,512]{1,0:T(8,128)(2,1)S(1)}, bf16[128,512]{1,0:T(8,128)(2,1)S(1)}, u32[]{:S(2)}, u32[]{:S(2)}) collective-permute-start(bf16[128,512]{1,0:T(8,128)(2,1)S(1)} %get-tuple-element.84), channel_id=1, source_target_pairs={{0,6},{2,4},{4,2},{6,0},{1,7},{3,5},{5,3},{7,1},{8,14},{10,12},{12... | collective-permute-start | bytes 393224 | tf_op jit(solution)/shard_map/ppermute | solution.py:69
  42.8 1.6 %shard_map.147 = (bf16[2,64,512]{2,1,0:T(8,128)(2,1)S(1)}, bf16[2,64,512]{2,1,0:T(8,128)(2,1)S(1)}, bf16[2,64,512]{2,1,0:T(8,128)(2,1)S(1)}, f32[2,64,512]{2,1,0:T(8,128)S(1)}) custom-call(s32[1]{0:T(128)} %bitcast.own_ref, s32[4]{0:T(128)S(1)} %pad_add_fusion.part_ref, bf16[512,512]{1,0:T(8,128)(2,1)S(1)} %bitcast.31, bf16[512,512]{1,0:T(8,128)(2,1)S(1)} %bitcast.33, ...), custom_call_target="tpu_custom_call" | custom-call | flops 2000000000 | tf_op jit(solution)/shard_map/pallas_call | solution.py:659
  44.5 1.1 %collective-permute-start.19 = (bf16[2,64,512]{2,1,0:T(8,128)(2,1)S(1)}, bf16[2,64,512]{2,1,0:T(8,128)(2,1)S(1)}, u32[]{:S(2)}, u32[]{:S(2)}) collective-permute-start(bf16[2,64,512]{2,1,0:T(8,128)(2,1)S(1)} %get-tuple-element.90), channel_id=1, source_target_pairs={{0,16},{8,24},{16,0},{24,8},{1,17},{9,25},{17,1},{25,9},{2,18},{10... | collective-permute-start | bytes 393224 | tf_op jit(solution)/shard_map/ppermute | solution.py:69
  45.6 3.3 %collective-permute-start.20 = (bf16[2,64,512]{2,1,0:T(8,128)(2,1)S(1)}, bf16[2,64,512]{2,1,0:T(8,128)(2,1)S(1)}, u32[]{:S(2)}, u32[]{:S(2)}) collective-permute-start(bf16[2,64,512]{2,1,0:T(8,128)(2,1)S(1)} %get-tuple-element.91), channel_id=1, source_target_pairs={{0,8},{8,0},{16,24},{24,16},{1,9},{9,1},{17,25},{25,17},{2,10},{10... | collective-permute-start | bytes 393224 | tf_op jit(solution)/shard_map/ppermute | solution.py:69
  48.9 1.4 %shard_map.148 = (bf16[128,512]{1,0:T(8,128)(2,1)}, bf16[128,512]{1,0:T(8,128)(2,1)}) custom-call(s32[1]{0:T(128)} %bitcast.own_ref, bf16[128,512]{1,0:T(8,128)(2,1)S(1)} %get-tuple-element.80.mixed_ref, bf16[160,512]{1,0:T(8,128)(2,1)S(1)} %copy-done.6, bf16[128,512]{1,0:T(8,128)(2,1)S(1)} %get-tuple-element.81.refs_0_, ...), custom_call_target="tpu_custom_call" | custom-call | flops 1500000000 | tf_op jit(solution)/shard_map/pallas_call | solution.py:692
  50.3 2.5 %collective-permute-done.18.refs_0_ = bf16[2,64,512]{2,1,0:T(8,128)(2,1)S(1)} collective-permute-done((bf16[2,64,512]{2,1,0:T(8,128)(2,1)S(1)}, bf16[2,64,512]{2,1,0:T(8,128)(2,1)S(1)}, u32[]{:S(2)}, u32[]{:S(2)}) %collective-permute-start.18) | collective-permute-done | bytes 131104 | tf_op jit(solution)/shard_map/ppermute | solution.py:69
  52.8 5.5 %collective-permute-done.19.refs_1_ = bf16[2,64,512]{2,1,0:T(8,128)(2,1)S(1)} collective-permute-done((bf16[2,64,512]{2,1,0:T(8,128)(2,1)S(1)}, bf16[2,64,512]{2,1,0:T(8,128)(2,1)S(1)}, u32[]{:S(2)}, u32[]{:S(2)}) %collective-permute-start.19) | collective-permute-done | bytes 131104 | tf_op jit(solution)/shard_map/ppermute | solution.py:69
  58.2 0.7 %shard_map.149 = (f32[64,512]{1,0:T(8,128)}, f32[64,512]{1,0:T(8,128)}) custom-call(f32[2,64,512]{2,1,0:T(8,128)S(1)} %get-tuple-element.88.kept_ref, bf16[2,64,512]{2,1,0:T(8,128)(2,1)S(1)} %collective-permute-done.18.refs_0_, bf16[2,64,512]{2,1,0:T(8,128)(2,1)S(1)} %collective-permute-done.19.refs_1_, bf16[2,64,512]{2,1,0:T(8,128)(2,1)S(1)} %collective-permute-done.20.refs_2_), custom_call_target="tpu_custom_call" | custom-call | flops 500000000 | tf_op jit(solution)/shard_map/pallas_call | solution.py:699
  (48 shorter events, 4.0 us)
Async XLA Ops:
  0.6 4.9 %copy-start.7 = (bf16[1,128,512]{2,1,0:T(8,128)(2,1)S(1)}, bf16[1,128,512]{2,1,0:T(8,128)(2,1)}, u32[]{:S(2)}) copy-start(bf16[1,128,512]{2,1,0:T(8,128)(2,1)} %param.11) | copy-start | bytes 393220
  0.6 9.9 %copy-start.2 = (bf16[1,128,512]{2,1,0:T(8,128)(2,1)S(1)}, bf16[1,128,512]{2,1,0:T(8,128)(2,1)}, u32[]{:S(2)}) copy-start(bf16[1,128,512]{2,1,0:T(8,128)(2,1)} %param.13) | copy-start | bytes 393220
  2.4 8.2 %copy-start.1 = (bf16[1,128,512]{2,1,0:T(8,128)(2,1)S(1)}, bf16[1,128,512]{2,1,0:T(8,128)(2,1)}, u32[]{:S(2)}) copy-start(bf16[1,128,512]{2,1,0:T(8,128)(2,1)} %param.12) | copy-start | bytes 393220
  2.4 11.6 %collective-permute-start = (bf16[256,512]{1,0:T(8,128)(2,1)}, bf16[256,512]{1,0:T(8,128)(2,1)S(1)}, u32[]{:S(2)}, u32[]{:S(2)}) collective-permute-start(bf16[256,512]{1,0:T(8,128)(2,1)} %shard_map.139.refs_2_), channel_id=1, source_target_pairs={{0,8},{8,16},{16,24},{24,0},{1,9},{9,17},{17,25},{25,1},{2,10},{10... | collective-permute-start | bytes 786440 | tf_op jit(solution)/shard_map/ppermute | solution.py:537
  5.5 9.3 %collective-permute-start.2 = (bf16[128,512]{1,0:T(8,128)(2,1)S(1)}, bf16[128,512]{1,0:T(8,128)(2,1)S(1)}, u32[]{:S(2)}, u32[]{:S(2)}) collective-permute-start(bf16[128,512]{1,0:T(8,128)(2,1)S(1)} %bitcast.34), channel_id=1, source_target_pairs={{0,1},{1,0},{2,3},{3,2},{4,5},{5,4},{6,7},{7,6},{8,9},{9,8},{10,11... | collective-permute-start | bytes 393224 | tf_op jit(solution)/shard_map/ppermute | solution.py:69
  9.9 6.9 %collective-permute-start.3 = (bf16[160,512]{1,0:T(8,128)(2,1)}, bf16[160,512]{1,0:T(8,128)(2,1)S(1)}, u32[]{:S(2)}, u32[]{:S(2)}) collective-permute-start(bf16[160,512]{1,0:T(8,128)(2,1)} %get-tuple-element.49.refs_0_.extended_ref), channel_id=1, source_target_pairs={{0,1},{1,0},{2,3},{3,2},{4,5},{5,4},{6,7},{7,6},{8,9},{9,8},{10,11... | collective-permute-start | bytes 491528 | tf_op jit(solution)/shard_map/ppermute | solution.py:69
  10.5 0.7 %copy-start.9 = (s32[2,128]{1,0:T(2,128)S(1)}, s32[2,128]{1,0:T(2,128)}, u32[]{:S(2)}) copy-start(s32[2,128]{1,0:T(2,128)} %get-tuple-element.50.begin_ref) | copy-start | bytes 3076
  11.2 3.6 %copy-start = (bf16[256,512]{1,0:T(8,128)(2,1)S(1)}, bf16[256,512]{1,0:T(8,128)(2,1)}, u32[]{:S(2)}) copy-start(bf16[256,512]{1,0:T(8,128)(2,1)} %shard_map.139.refs_2_) | copy-start | bytes 786436
  14.0 2.7 %copy-start.6 = (bf16[160,512]{1,0:T(8,128)(2,1)S(1)}, bf16[160,512]{1,0:T(8,128)(2,1)}, u32[]{:S(2)}) copy-start(bf16[160,512]{1,0:T(8,128)(2,1)} %get-tuple-element.49.refs_0_.extended_ref) | copy-start | bytes 491524
  14.0 9.3 %collective-permute-start.1 = (bf16[256,512]{1,0:T(8,128)(2,1)S(1)}, bf16[256,512]{1,0:T(8,128)(2,1)S(1)}, u32[]{:S(2)}, u32[]{:S(2)}) collective-permute-start(bf16[256,512]{1,0:T(8,128)(2,1)S(1)} %collective-permute-done.refs_3_), channel_id=1, source_target_pairs={{0,8},{8,16},{16,24},{24,0},{1,9},{9,17},{17,25},{25,1},{2,10},{10... | collective-permute-start | bytes 786440 | tf_op jit(solution)/shard_map/ppermute | solution.py:537
  24.1 5.3 %collective-permute-start.4 = (bf16[592,128]{1,0:T(8,128)(2,1)S(1)}, bf16[592,128]{1,0:T(8,128)(2,1)S(1)}, u32[]{:S(2)}, u32[]{:S(2)}) collective-permute-start(bf16[592,128]{1,0:T(8,128)(2,1)S(1)} %shard_map.144), channel_id=1, source_target_pairs={{0,1},{1,0},{2,3},{3,2},{4,5},{5,4},{6,7},{7,6},{8,9},{9,8},{10,11... | collective-permute-start | bytes 454664 | tf_op jit(solution)/shard_map/ppermute | solution.py:69
  25.5 5.9 %collective-permute-start.10 = (bf16[128,512]{1,0:T(8,128)(2,1)S(1)}, bf16[128,512]{1,0:T(8,128)(2,1)S(1)}, u32[]{:S(2)}, u32[]{:S(2)}) collective-permute-start(bf16[128,512]{1,0:T(8,128)(2,1)S(1)} %get-tuple-element.75), channel_id=1, source_target_pairs={{0,4},{2,6},{4,0},{6,2},{1,5},{3,7},{5,1},{7,3},{8,12},{10,14},{12... | collective-permute-start | bytes 393224 | tf_op jit(solution)/shard_map/ppermute | solution.py:69
  27.0 5.0 %collective-permute-start.11 = (bf16[128,512]{1,0:T(8,128)(2,1)S(1)}, bf16[128,512]{1,0:T(8,128)(2,1)S(1)}, u32[]{:S(2)}, u32[]{:S(2)}) collective-permute-start(bf16[128,512]{1,0:T(8,128)(2,1)S(1)} %get-tuple-element.76), channel_id=1, source_target_pairs={{0,2},{2,0},{4,6},{6,4},{1,3},{3,1},{5,7},{7,5},{8,10},{10,8},{12,... | collective-permute-start | bytes 393224 | tf_op jit(solution)/shard_map/ppermute | solution.py:69
  27.0 6.5 %collective-permute-start.9 = (bf16[128,512]{1,0:T(8,128)(2,1)S(1)}, bf16[128,512]{1,0:T(8,128)(2,1)S(1)}, u32[]{:S(2)}, u32[]{:S(2)}) collective-permute-start(bf16[128,512]{1,0:T(8,128)(2,1)S(1)} %get-tuple-element.74), channel_id=1, source_target_pairs={{0,6},{2,4},{4,2},{6,0},{1,7},{3,5},{5,3},{7,1},{8,14},{10,12},{12... | collective-permute-start | bytes 393224 | tf_op jit(solution)/shard_map/ppermute | solution.py:69
  27.6 1.7 %copy-start.3 = (bf16[512,512]{1,0:T(8,128)(2,1)S(1)}, bf16[512,512]{1,0:T(8,128)(2,1)}, u32[]{:S(2)}) copy-start(bf16[512,512]{1,0:T(8,128)(2,1)} %proj_ref.1) | copy-start | bytes 1572868
  27.6 1.7 %copy-start.8 = (bf16[1,128,512]{2,1,0:T(8,128)(2,1)S(1)}, bf16[1,128,512]{2,1,0:T(8,128)(2,1)}, u32[]{:S(2)}) copy-start(bf16[1,128,512]{2,1,0:T(8,128)(2,1)} %param.15) | copy-start | bytes 393220
  29.3 7.1 %copy-start.4 = (bf16[1,512,512]{2,1,0:T(8,128)(2,1)S(1)}, bf16[1,512,512]{2,1,0:T(8,128)(2,1)}, u32[]{:S(2)}) copy-start(bf16[1,512,512]{2,1,0:T(8,128)(2,1)} %param.19) | copy-start | bytes 1572868
  29.3 7.1 %copy-start.5 = (bf16[1,512,512]{2,1,0:T(8,128)(2,1)S(1)}, bf16[1,512,512]{2,1,0:T(8,128)(2,1)}, u32[]{:S(2)}) copy-start(bf16[1,512,512]{2,1,0:T(8,128)(2,1)} %param.20) | copy-start | bytes 1572868
  30.0 4.7 %collective-permute-start.12 = (bf16[64,512]{1,0:T(8,128)(2,1)S(1)}, bf16[64,512]{1,0:T(8,128)(2,1)S(1)}, u32[]{:S(2)}, u32[]{:S(2)}) collective-permute-start(bf16[64,512]{1,0:T(8,128)(2,1)S(1)} %get-tuple-element.71), channel_id=1, source_target_pairs={{0,2},{1,3},{2,0},{3,1},{4,6},{5,7},{6,4},{7,5},{8,10},{9,11},{10,... | collective-permute-start | bytes 196616 | tf_op jit(solution)/shard_map/ppermute | solution.py:69
  30.0 5.8 %collective-permute-start.13 = (bf16[64,512]{1,0:T(8,128)(2,1)S(1)}, bf16[64,512]{1,0:T(8,128)(2,1)S(1)}, u32[]{:S(2)}, u32[]{:S(2)}) collective-permute-start(bf16[64,512]{1,0:T(8,128)(2,1)S(1)} %get-tuple-element.72), channel_id=1, source_target_pairs={{0,4},{1,5},{2,6},{3,7},{4,0},{5,1},{6,2},{7,3},{8,12},{9,13},{10,... | collective-permute-start | bytes 196616 | tf_op jit(solution)/shard_map/ppermute | solution.py:69
  31.4 5.0 %collective-permute-start.14 = (bf16[64,512]{1,0:T(8,128)(2,1)S(1)}, bf16[64,512]{1,0:T(8,128)(2,1)S(1)}, u32[]{:S(2)}, u32[]{:S(2)}) collective-permute-start(bf16[64,512]{1,0:T(8,128)(2,1)S(1)} %get-tuple-element.73), channel_id=1, source_target_pairs={{0,6},{1,7},{2,4},{3,5},{4,2},{5,3},{6,0},{7,1},{8,14},{9,15},{10,... | collective-permute-start | bytes 196616 | tf_op jit(solution)/shard_map/ppermute | solution.py:69
  32.0 10.1 %collective-permute-start.6 = (bf16[64,512]{1,0:T(8,128)(2,1)S(1)}, bf16[64,512]{1,0:T(8,128)(2,1)S(1)}, u32[]{:S(2)}, u32[]{:S(2)}) collective-permute-start(bf16[64,512]{1,0:T(8,128)(2,1)S(1)} %get-tuple-element.71), channel_id=1, source_target_pairs={{0,3},{1,2},{2,1},{3,0},{4,7},{5,6},{6,5},{7,4},{8,11},{9,10},{10,... | collective-permute-start | bytes 196616 | tf_op jit(solution)/shard_map/ppermute | solution.py:69
  33.5 9.2 %collective-permute-start.7 = (bf16[64,512]{1,0:T(8,128)(2,1)S(1)}, bf16[64,512]{1,0:T(8,128)(2,1)S(1)}, u32[]{:S(2)}, u32[]{:S(2)}) collective-permute-start(bf16[64,512]{1,0:T(8,128)(2,1)S(1)} %get-tuple-element.72), channel_id=1, source_target_pairs={{0,5},{1,4},{2,7},{3,6},{4,1},{5,0},{6,3},{7,2},{8,13},{9,12},{10,... | collective-permute-start | bytes 196616 | tf_op jit(solution)/shard_map/ppermute | solution.py:69
  34.7 8.1 %collective-permute-start.8 = (bf16[64,512]{1,0:T(8,128)(2,1)S(1)}, bf16[64,512]{1,0:T(8,128)(2,1)S(1)}, u32[]{:S(2)}, u32[]{:S(2)}) collective-permute-start(bf16[64,512]{1,0:T(8,128)(2,1)S(1)} %get-tuple-element.73), channel_id=1, source_target_pairs={{0,7},{1,6},{2,5},{3,4},{4,3},{5,2},{6,1},{7,0},{8,15},{9,14},{10,... | collective-permute-start | bytes 196616 | tf_op jit(solution)/shard_map/ppermute | solution.py:69
  35.9 5.4 %collective-permute-start.5 = (bf16[64,512]{1,0:T(8,128)(2,1)S(1)}, bf16[64,512]{1,0:T(8,128)(2,1)S(1)}, u32[]{:S(2)}, u32[]{:S(2)}) collective-permute-start(bf16[64,512]{1,0:T(8,128)(2,1)S(1)} %get-tuple-element.70.refs_0_), channel_id=1, source_target_pairs={{0,1},{1,0},{2,3},{3,2},{4,5},{5,4},{6,7},{7,6},{8,9},{9,8},{10,11... | collective-permute-start | bytes 196616 | tf_op jit(solution)/shard_map/ppermute | solution.py:69
  38.3 7.3 %collective-permute-start.15 = (bf16[128,512]{1,0:T(8,128)(2,1)S(1)}, bf16[128,512]{1,0:T(8,128)(2,1)S(1)}, u32[]{:S(2)}, u32[]{:S(2)}) collective-permute-start(bf16[128,512]{1,0:T(8,128)(2,1)S(1)} %get-tuple-element.82), channel_id=1, source_target_pairs={{0,2},{2,0},{4,6},{6,4},{1,3},{3,1},{5,7},{7,5},{8,10},{10,8},{12,... | collective-permute-start | bytes 393224 | tf_op jit(solution)/shard_map/ppermute | solution.py:69
  41.3 7.6 %collective-permute-start.16 = (bf16[128,512]{1,0:T(8,128)(2,1)S(1)}, bf16[128,512]{1,0:T(8,128)(2,1)S(1)}, u32[]{:S(2)}, u32[]{:S(2)}) collective-permute-start(bf16[128,512]{1,0:T(8,128)(2,1)S(1)} %get-tuple-element.83), channel_id=1, source_target_pairs={{0,4},{2,6},{4,0},{6,2},{1,5},{3,7},{5,1},{7,3},{8,12},{10,14},{12... | collective-permute-start | bytes 393224 | tf_op jit(solution)/shard_map/ppermute | solution.py:69
  42.1 6.8 %collective-permute-start.17 = (bf16[128,512]{1,0:T(8,128)(2,1)S(1)}, bf16[128,512]{1,0:T(8,128)(2,1)S(1)}, u32[]{:S(2)}, u32[]{:S(2)}) collective-permute-start(bf16[128,512]{1,0:T(8,128)(2,1)S(1)} %get-tuple-element.84), channel_id=1, source_target_pairs={{0,6},{2,4},{4,2},{6,0},{1,7},{3,5},{5,3},{7,1},{8,14},{10,12},{12... | collective-permute-start | bytes 393224 | tf_op jit(solution)/shard_map/ppermute | solution.py:69
  44.4 8.4 %collective-permute-start.18 = (bf16[2,64,512]{2,1,0:T(8,128)(2,1)S(1)}, bf16[2,64,512]{2,1,0:T(8,128)(2,1)S(1)}, u32[]{:S(2)}, u32[]{:S(2)}) collective-permute-start(bf16[2,64,512]{2,1,0:T(8,128)(2,1)S(1)} %get-tuple-element.89), channel_id=1, source_target_pairs={{0,24},{8,16},{16,8},{24,0},{1,25},{9,17},{17,9},{25,1},{2,26},{10... | collective-permute-start | bytes 393224 | tf_op jit(solution)/shard_map/ppermute | solution.py:69
  44.5 13.8 %collective-permute-start.19 = (bf16[2,64,512]{2,1,0:T(8,128)(2,1)S(1)}, bf16[2,64,512]{2,1,0:T(8,128)(2,1)S(1)}, u32[]{:S(2)}, u32[]{:S(2)}) collective-permute-start(bf16[2,64,512]{2,1,0:T(8,128)(2,1)S(1)} %get-tuple-element.90), channel_id=1, source_target_pairs={{0,16},{8,24},{16,0},{24,8},{1,17},{9,25},{17,1},{25,9},{2,18},{10... | collective-permute-start | bytes 393224 | tf_op jit(solution)/shard_map/ppermute | solution.py:69
  45.6 12.7 %collective-permute-start.20 = (bf16[2,64,512]{2,1,0:T(8,128)(2,1)S(1)}, bf16[2,64,512]{2,1,0:T(8,128)(2,1)S(1)}, u32[]{:S(2)}, u32[]{:S(2)}) collective-permute-start(bf16[2,64,512]{2,1,0:T(8,128)(2,1)S(1)} %get-tuple-element.91), channel_id=1, source_target_pairs={{0,8},{8,0},{16,24},{24,16},{1,9},{9,1},{17,25},{25,17},{2,10},{10... | collective-permute-start | bytes 393224 | tf_op jit(solution)/shard_map/ppermute | solution.py:69

commit v11 on v10

--- a/solution.py
+++ b/solution.py
@@ -109,64 +109,27 @@
     return (rows == slots).astype(jnp.float32).astype(jnp.bfloat16)
 
 
-def stack_kernel(key_ref, value_ref, pair_ref, sems):
-    tok = key_ref.shape[0]
-    copies = [
-        pltpu.make_async_copy(ref, pair_ref.at[pl.ds(place * tok, tok), :], sems.at[place])
-        for place, ref in enumerate((key_ref, value_ref))
-    ]
-    for copy in copies:
-        copy.start()
-    for copy in copies:
-        copy.wait()
-
-
 def extend_kernel(
-    ranks_ref,
-    choice_ref,
-    lengths_ref,
-    router_ref,
-    grad_ref,
-    extended_ref,
-    begin_ref,
-    chosen_ref,
-    held_router_ref,
-    held_lengths_ref,
-    sems,
+    ranks_ref, lengths_ref, choice_ref, router_ref, grad_ref, extended_ref, begin_ref
 ):
     tok, width = grad_ref.shape
-    targets = (
-        (choice_ref, chosen_ref),
-        (lengths_ref, held_lengths_ref),
-        (grad_ref, extended_ref.at[pl.ds(0, tok), :]),
-        (router_ref, held_router_ref),
-    )
-    copies = [
-        pltpu.make_async_copy(source, target, sems.at[place])
-        for place, (source, target) in enumerate(targets)
-    ]
-    for copy in copies:
-        copy.start()
-    copies[0].wait()
-    chosen = jnp.broadcast_to(chosen_ref[...].astype(jnp.float32), (16, tok))
+    extended_ref[0:tok, :] = grad_ref[...]
+    chosen = jnp.broadcast_to(choice_ref[...].astype(jnp.float32), (16, tok))
     extended_ref[tok : tok + 16, 0:tok] = chosen.astype(jnp.bfloat16)
     extended_ref[tok : tok + 16, tok:width] = jnp.zeros((16, width - tok), jnp.bfloat16)
-    copies[1].wait()
+    routed = router_ref[...].astype(jnp.float32)
+    spare = extended_ref.shape[0] - tok - 16 - routed.shape[0]
+    if spare:
+        routed = jnp.concatenate([routed, jnp.zeros((spare, width), jnp.float32)], axis=0)
+    extended_ref[tok + 16 :, :] = routed.astype(jnp.bfloat16)
     for k in range(begin_ref.shape[0]):
         position = ranks_ref[k] * tok + lax.broadcasted_iota(jnp.int32, (1, tok), 1)
         begin = jnp.zeros((1, tok), jnp.int32)
         bound = jnp.int32(0)
-        for doc in range(held_lengths_ref.shape[1] - 1):
-            bound = bound + held_lengths_ref[0, doc]
+        for doc in range(lengths_ref.shape[1] - 1):
+            bound = bound + lengths_ref[0, doc]
             begin = jnp.maximum(begin, jnp.where(position >= bound, bound, 0))
         begin_ref[k : k + 1, :] = begin
-    copies[3].wait()
-    routed = held_router_ref[...].astype(jnp.float32)
-    spare = extended_ref.shape[0] - tok - 16 - routed.shape[0]
-    if spare:
-        routed = jnp.concatenate([routed, jnp.zeros((spare, width), jnp.float32)], axis=0)
-    extended_ref[tok + 16 :, :] = routed.astype(jnp.bfloat16)
-    copies[2].wait()
 
 
 def chosen_of(extended_ref, tok):
@@ -224,14 +187,11 @@
         visible = (key_position >= begin) & (key_position <= position)
         bias_ref[place] = jnp.where(visible, 0.0, masked_score)
         bias = bias_ref[place]
-        if isinstance(pair_ref, tuple):
-            key_ref, value_ref, first_value = pair_ref[0], pair_ref[1], 0
-        else:
-            key_ref, value_ref, first_value = pair_ref, pair_ref, tok
-        values = value_ref[first_value : first_value + tok, :].T
+        key_ref, value_ref = pair_ref
+        values = value_ref[...].T
         for group, spread in enumerate(spreads[k]):
             columns = slice(group * lanes, (group + 1) * lanes)
-            scores = dot(key_ref[0:tok, columns], spread)
+            scores = dot(key_ref[:, columns], spread)
             weights, factors = [], []
             for head in range(per):
                 row = group * per + head
@@ -278,10 +238,8 @@
     ks = sorted({k for k, unused_pair, unused_first in plan})
     old_ks = [k for k in ks if not any(first for j, unused_pair, first in plan if j == k)]
     query_refs, refs = dict(zip(ks, refs)), refs[len(ks) + ahead :]
-    if counts == 0:
-        pair_refs, refs = [tuple(refs[:2])], refs[2:]
-    else:
-        pair_refs, refs = refs[:counts], refs[counts:]
+    pair_refs = [refs[2 * place : 2 * place + 2] for place in range(counts)]
+    refs = refs[2 * counts :]
     old_refs, refs = refs[: 3 * len(old_ks)], refs[3 * len(old_ks) :]
     bias_ref, refs = refs[-1], refs[:-1]
     packed_refs, state_refs = (refs[: len(ks)], refs[len(ks) :]) if packed else ((), refs)
@@ -556,38 +514,15 @@
         shape((width, tok), jnp.float32),
     ]
     tail = 16 + -(-expert_count // 16) * 16
-    def early(body, out_shape, specs, scratch):
-        return pl.pallas_call(
-            body,
-            out_shape=out_shape,
-            in_specs=specs,
-            out_specs=jax.tree.map(lambda unused: VMEM, out_shape),
-            scratch_shapes=scratch,
-            compiler_params=pltpu.CompilerParams(vmem_limit_bytes=60 * 1024 * 1024),
-        )
-
-    pair = early(
-        stack_kernel, shape((2 * tok, width)), [HBM, HBM], [pltpu.SemaphoreType.DMA((2,))]
-    )(key_rows[0], value_rows[0])
-    extended, begin = early(
+    extended, begin = call(
         extend_kernel,
         [shape((tok + tail, width)), shape((rep_count, tok), jnp.int32)],
-        [SMEM] + [HBM] * 4,
-        [
-            pltpu.VMEM((1, tok), jnp.int32),
-            pltpu.VMEM((expert_count, width), jnp.bfloat16),
-            pltpu.SMEM(doc_lengths.shape, jnp.int32),
-            pltpu.SemaphoreType.DMA((4,)),
-        ],
+        [SMEM, SMEM] + [VMEM] * 3,
     )(
-        jnp.stack(query_ranks).astype(jnp.int32),
-        choice,
-        doc_lengths,
-        router.T,
-        grad_out[0],
-    )
-
-    def attend(plan, pairs, steps, queries, states, packed, cost, raw=False, ahead=()):
+        jnp.stack(query_ranks).astype(jnp.int32), doc_lengths, choice, router.T, grad_out[0]
+    )
+
+    def attend(plan, pairs, steps, queries, states, packed, cost, ahead=()):
         ks = sorted({k for k, unused_pair, unused_first in plan})
         old = [one for k in ks if k in states for one in states[k]]
         state_out = state_shapes * len(ks)
@@ -598,31 +533,27 @@
             out_shape, scratch = state_out, []
         outs = call(
             functools.partial(
-                attend_kernel, plan, rep_count, 0 if raw else len(pairs), packed, len(ahead)
+                attend_kernel, plan, rep_count, len(pairs), packed, len(ahead)
             ),
             out_shape,
-            [SMEM] + [VMEM] * (1 + len(ks) + len(ahead) + len(pairs) + len(old)),
+            [SMEM] + [VMEM] * (1 + len(ks) + len(ahead) + 2 * len(pairs) + len(old)),
             scratch + [pltpu.VMEM((len(plan), tok, tok), jnp.float32)],
             cost=cost,
-        )(task_ids(plan, steps), begin, *[queries[k] for k in ks], *ahead, *pairs, *old)
+        )(task_ids(plan, steps), begin, *[queries[k] for k in ks], *ahead, *[one for both in pairs for one in both], *old)
         if packed:
             return dict(zip(ks, outs))
         return {k: list(outs[3 * place : 3 * place + 3]) for place, k in enumerate(ks)}
 
     others = range(1, rep_count)
-    lines = [pair, forward(pair)]
+    lines = [(key_rows[0], value_rows[0])]
+    for unused in range(reach):
+        lines.append(tuple(forward(one) for one in lines[-1]))
     queries = reps.exchange([query_rows[0]] * rep_count)
     extendeds = reps.exchange([extended] * rep_count)
-    states = attend(
-        ((0, 0, True),), [key_rows[0], value_rows[0]], [0], queries, {}, False, 2.0, True
-    )
-    lines[1], *states[0] = lax.optimization_barrier((lines[1], *states[0]))
-    for step in range(2, reach + 1):
-        lines.append(forward(lines[-1]))
-    middle = tuple((0, step, False) for step in range(1, reach)) + tuple(
+    middle = tuple((0, step, step == 0) for step in range(reach)) + tuple(
         (k, step, step == 0) for k in others for step in range(reach)
     )
-    states = attend(middle, lines[:-1], list(range(reach)), queries, states, False, 4.0)
+    states = attend(middle, lines[:-1], list(range(reach)), queries, {}, False, 5.0)
     states[1][0], *extendeds[1:] = lax.optimization_barrier((states[1][0], *extendeds[1:]))
     sent_grads = call(
         functools.partial(dispatch_kernel, rep_count, tok, hot_capacity),

time: 59.2 us -> 56.6 us (0.956)
  Pallas kernels: 16 us -> 11.8 us
  waiting for transfers between devices: 17.2 us -> 20.1 us
  starting transfers between devices: 23.3 us -> 22.1 us
  local copies, waits for them, and re-layouts: 0.8 us -> 1.68 us
    pallas_call x6 -> x4, Pallas kernels: 9.2 us -> 5.03 us  [the longest x3 4.47 us: attend(): call(functools.partial(attend_kernel, plan, rep_count, len(pairs), packed...]
    ppermute x19, waiting for transfers between devices: 10.4 us -> 13 us  [exchange(): got[k] = lax.ppermute(chunks[k], self.axes, pairs)]
    ppermute x19, starting transfers between devices: 19.4 us -> 18.5 us  [exchange(): got[k] = lax.ppermute(chunks[k], self.axes, pairs)]
    unnamed x20 -> x22, local copies, waits for them, and re-layouts: 0.71 us -> 1.6 us
    ppermute x2 -> x4, starting transfers between devices: 3.85 us -> 3.54 us  [forward(): lax.ppermute(array, 'seq', [(i, (i + 1) % seq_count) for i in range(seq_c...]
    ppermute x2 -> x4, waiting for transfers between devices: 6.82 us -> 7.05 us  [forward(): lax.ppermute(array, 'seq', [(i, (i + 1) % seq_count) for i in range(seq_c...]
  transfers between devices with their start and end apart: 21 -> 23, of which waited for: 6 -> 9; matrix products, arithmetic and copies ran while one was open for 2% -> 1% of each run, Pallas kernels for 22% -> 18%
where the time goes in v11:
time: 56.6 us; the launch traced here: 56.7 us
  starting transfers between devices  22.1 us (39%)
  waiting for transfers between devices  20.1 us (36%)
  Pallas kernels  11.8 us (21%)
  local copies, waits for them, and re-layouts  1.68 us (3%)
  between operations  0.78 us (1%)
    ppermute x19, starting transfers between devices, exchange(): got[k] = lax.ppermute(chunks[k], self.axes, pairs)  18.5 us
    ppermute x19, waiting for transfers between devices, exchange(): got[k] = lax.ppermute(chunks[k], self.axes, pairs)  13 us
    ppermute x4, waiting for transfers between devices, forward(): lax.ppermute(array, 'seq', [(i, (i + 1) % seq_count) for i in range(seq_c...  7.05 us
    pallas_call x3, Pallas kernels, attend(): call(functools.partial(attend_kernel, plan, rep_count, len(pairs), packed...  4.47 us
    ppermute x4, starting transfers between devices, forward(): lax.ppermute(array, 'seq', [(i, (i + 1) % seq_count) for i in range(seq_c...  3.54 us
    pallas_call x2, Pallas kernels, expert_call(): call(functools.partial(expert_kernel, rep_count, rep_list, expert_count,...  3.48 us
    unnamed x22, local copies, waits for them, and re-layouts  1.6 us
    pallas_call x1, Pallas kernels, local(): call(functools.partial(finish_kernel, hot_capacity, expert_count), [shape...  1.42 us
  transfers between devices with their start and end apart: 23, of which 9 were waited for; matrix products, arithmetic and copies ran while one was open for 1% of the time, Pallas kernels for 18%

profile of v11, /device:TPU:0, one launch (start us, length us, event | category | flops | bytes accessed | tf_op | source)
XLA Modules:
  0.0 56.7 jit_solution(7900901762482957741)
XLA Ops:
  0.6 3.0 %collective-permute-start.4 = (bf16[128,512]{1,0:T(8,128)(2,1)}, bf16[128,512]{1,0:T(8,128)(2,1)S(1)}, u32[]{:S(2)}, u32[]{:S(2)}) collective-permute-start(bf16[128,512]{1,0:T(8,128)(2,1)} %bitcast.35), channel_id=1, source_target_pairs={{0,1},{1,0},{2,3},{3,2},{4,5},{5,4},{6,7},{7,6},{8,9},{9,8},{10,11... | collective-permute-start | bytes 393224 | tf_op jit(solution)/shard_map/ppermute | solution.py:69
  3.6 1.6 %collective-permute-start = (bf16[128,512]{1,0:T(8,128)(2,1)}, bf16[128,512]{1,0:T(8,128)(2,1)S(1)}, u32[]{:S(2)}, u32[]{:S(2)}) collective-permute-start(bf16[128,512]{1,0:T(8,128)(2,1)} %bitcast.31), channel_id=1, source_target_pairs={{0,8},{8,16},{16,24},{24,0},{1,9},{9,17},{17,25},{25,1},{2,10},{10... | collective-permute-start | bytes 393224 | tf_op jit(solution)/shard_map/ppermute | solution.py:495
  5.2 1.6 %collective-permute-start.2 = (bf16[128,512]{1,0:T(8,128)(2,1)}, bf16[128,512]{1,0:T(8,128)(2,1)S(1)}, u32[]{:S(2)}, u32[]{:S(2)}) collective-permute-start(bf16[128,512]{1,0:T(8,128)(2,1)} %bitcast.33), channel_id=1, source_target_pairs={{0,8},{8,16},{16,24},{24,0},{1,9},{9,17},{17,25},{25,1},{2,10},{10... | collective-permute-start | bytes 393224 | tf_op jit(solution)/shard_map/ppermute | solution.py:495
  6.9 0.6 %copy-done.8 = bf16[512,4]{0,1:T(4,128)(2,1)S(1)} copy-done((bf16[512,4]{0,1:T(4,128)(2,1)S(1)}, bf16[512,4]{0,1:T(4,128)(2,1)}, u32[]{:S(2)}) %copy-start.8) | copy-done | bytes 4120
  7.5 0.9 %copy-done.3 = bf16[1,128,512]{2,1,0:T(8,128)(2,1)S(1)} copy-done((bf16[1,128,512]{2,1,0:T(8,128)(2,1)S(1)}, bf16[1,128,512]{2,1,0:T(8,128)(2,1)}, u32[]{:S(2)}) %copy-start.3) | copy-done | bytes 131096
  9.0 0.6 %collective-permute-start.5 = (bf16[160,512]{1,0:T(8,128)(2,1)S(1)}, bf16[160,512]{1,0:T(8,128)(2,1)S(1)}, u32[]{:S(2)}, u32[]{:S(2)}) collective-permute-start(bf16[160,512]{1,0:T(8,128)(2,1)S(1)} %get-tuple-element.42.refs_0_.extended_ref), channel_id=1, source_target_pairs={{0,1},{1,0},{2,3},{3,2},{4,5},{5,4},{6,7},{7,6},{8,9},{9,8},{10,11... | collective-permute-start | bytes 491528 | tf_op jit(solution)/shard_map/ppermute | solution.py:69
  9.8 2.3 %collective-permute-done.refs_4_ = bf16[128,512]{1,0:T(8,128)(2,1)S(1)} collective-permute-done((bf16[128,512]{1,0:T(8,128)(2,1)}, bf16[128,512]{1,0:T(8,128)(2,1)S(1)}, u32[]{:S(2)}, u32[]{:S(2)}) %collective-permute-start) | collective-permute-done | bytes 131104 | tf_op jit(solution)/shard_map/ppermute | solution.py:495
  12.1 1.4 %collective-permute-done.2.refs_5_ = bf16[128,512]{1,0:T(8,128)(2,1)S(1)} collective-permute-done((bf16[128,512]{1,0:T(8,128)(2,1)}, bf16[128,512]{1,0:T(8,128)(2,1)S(1)}, u32[]{:S(2)}, u32[]{:S(2)}) %collective-permute-start.2) | collective-permute-done | bytes 131104 | tf_op jit(solution)/shard_map/ppermute | solution.py:495
  13.9 3.0 %shard_map.139 = (f32[16,128]{1,0:T(8,128)S(1)}, f32[16,128]{1,0:T(8,128)S(1)}, f32[512,128]{1,0:T(8,128)S(1)}, f32[16,128]{1,0:T(8,128)S(1)}, f32[16,128]{1,0:T(8,128)S(1)}, /*index=5*/f32[512,128]{1,0:T(8,128)S(1)}) custom-call(s32[6]{0:T(128)S(1)} %stack.75.ids_ref, s32[2,128]{1,0:T(2,128)S(1)} %get-tuple-element.43.begin_ref, ...), custom_call_target="tpu_custom_call" | custom-call | flops 5000000000 | tf_op jit(solution)/shard_map/pallas_call | solution.py:534
  17.4 2.0 %collective-permute-done.1.refs_1_.refs_2_ = bf16[128,512]{1,0:T(8,128)(2,1)S(1)} collective-permute-done((bf16[128,512]{1,0:T(8,128)(2,1)S(1)}, bf16[128,512]{1,0:T(8,128)(2,1)S(1)}, u32[]{:S(2)}, u32[]{:S(2)}) %collective-permute-start.1) | collective-permute-done | bytes 131104 | tf_op jit(solution)/shard_map/ppermute | solution.py:495
  19.4 1.4 %collective-permute-done.3.refs_2_.refs_3_ = bf16[128,512]{1,0:T(8,128)(2,1)S(1)} collective-permute-done((bf16[128,512]{1,0:T(8,128)(2,1)S(1)}, bf16[128,512]{1,0:T(8,128)(2,1)S(1)}, u32[]{:S(2)}, u32[]{:S(2)}) %collective-permute-start.3) | collective-permute-done | bytes 131104 | tf_op jit(solution)/shard_map/ppermute | solution.py:495
  20.8 0.8 %shard_map.142 = bf16[592,128]{1,0:T(8,128)(2,1)S(1)} custom-call(s32[3]{0:T(128)S(1)} %pad_add_fusion.4.ids_ref, s32[2,128]{1,0:T(2,128)S(1)} %get-tuple-element.43.begin_ref, bf16[128,512]{1,0:T(8,128)(2,1)S(1)} %collective-permute-done.4.refs_1_.refs_0_, bf16[128,512]{1,0:T(8,128)(2,1)S(1)} %get-tuple-element.52.refs_1_.refs_7_, ...), custom_call_target="tpu_custom_call" | custom-call | flops 1500000000 | tf_op jit(solution)/shard_map/pallas_call | solution.py:534
  21.5 0.9 %collective-permute-start.6 = (bf16[592,128]{1,0:T(8,128)(2,1)S(1)}, bf16[592,128]{1,0:T(8,128)(2,1)S(1)}, u32[]{:S(2)}, u32[]{:S(2)}) collective-permute-start(bf16[592,128]{1,0:T(8,128)(2,1)S(1)} %shard_map.142), channel_id=1, source_target_pairs={{0,1},{1,0},{2,3},{3,2},{4,5},{5,4},{6,7},{7,6},{8,9},{9,8},{10,11... | collective-permute-start | bytes 454664 | tf_op jit(solution)/shard_map/ppermute | solution.py:69
  22.5 1.3 %collective-permute-start.12 = (bf16[128,512]{1,0:T(8,128)(2,1)S(1)}, bf16[128,512]{1,0:T(8,128)(2,1)S(1)}, u32[]{:S(2)}, u32[]{:S(2)}) collective-permute-start(bf16[128,512]{1,0:T(8,128)(2,1)S(1)} %get-tuple-element.61), channel_id=1, source_target_pairs={{0,4},{2,6},{4,0},{6,2},{1,5},{3,7},{5,1},{7,3},{8,12},{10,14},{12... | collective-permute-start | bytes 393224 | tf_op jit(solution)/shard_map/ppermute | solution.py:69
  24.4 0.7 %shard_map.140 = (f32[16,128]{1,0:T(8,128)S(1)}, f32[16,128]{1,0:T(8,128)S(1)}, f32[512,128]{1,0:T(8,128)S(1)}) custom-call(s32[3]{0:T(128)S(1)} %pad_add_fusion.2.ids_ref, s32[2,128]{1,0:T(2,128)S(1)} %get-tuple-element.43.begin_ref, bf16[128,512]{1,0:T(8,128)(2,1)S(1)} %bitcast.37, bf16[128,512]{1,0:T(8,128)(2,1)S(1)} %collective-permute-done.1.refs_1_.refs_2_, ...), custom_call_target="tpu_custom_call" | custom-call | flops 1500000000 | tf_op jit(solution)/shard_map/pallas_call | solution.py:534
  25.1 1.7 %collective-permute-done.6.refs_3_ = bf16[592,128]{1,0:T(8,128)(2,1)S(1)} collective-permute-done((bf16[592,128]{1,0:T(8,128)(2,1)S(1)}, bf16[592,128]{1,0:T(8,128)(2,1)S(1)}, u32[]{:S(2)}, u32[]{:S(2)}) %collective-permute-start.6) | collective-permute-done | bytes 151584 | tf_op jit(solution)/shard_map/ppermute | solution.py:69
  26.8 0.6 %shard_map.143 = (bf16[128,512]{1,0:T(8,128)(2,1)S(1)}, bf16[64,512]{1,0:T(8,128)(2,1)S(1)}, bf16[64,512]{1,0:T(8,128)(2,1)S(1)}, bf16[64,512]{1,0:T(8,128)(2,1)S(1)}, bf16[64,512]{1,0:T(8,128)(2,1)S(1)}) custom-call(s32[1]{0:T(128)} %bitcast.own_ref, bf16[160,512]{1,0:T(8,128)(2,1)S(1)} %get-tuple-element.42.refs_0_.extended_ref, ...), custom_call_target="tpu_custom_call" | custom-call | flops 2000000000 | tf_op jit(solution)/shard_map/pallas_call | solution.py:577
  27.5 1.6 %collective-permute-start.15 = (bf16[64,512]{1,0:T(8,128)(2,1)S(1)}, bf16[64,512]{1,0:T(8,128)(2,1)S(1)}, u32[]{:S(2)}, u32[]{:S(2)}) collective-permute-start(bf16[64,512]{1,0:T(8,128)(2,1)S(1)} %get-tuple-element.58), channel_id=1, source_target_pairs={{0,4},{1,5},{2,6},{3,7},{4,0},{5,1},{6,2},{7,3},{8,12},{9,13},{10,... | collective-permute-start | bytes 196616 | tf_op jit(solution)/shard_map/ppermute | solution.py:69
  29.5 1.3 %collective-permute-done.12.refs_5_ = bf16[128,512]{1,0:T(8,128)(2,1)S(1)} collective-permute-done((bf16[128,512]{1,0:T(8,128)(2,1)S(1)}, bf16[128,512]{1,0:T(8,128)(2,1)S(1)}, u32[]{:S(2)}, u32[]{:S(2)}) %collective-permute-start.12) | collective-permute-done | bytes 131104 | tf_op jit(solution)/shard_map/ppermute | solution.py:69
  30.7 1.0 %collective-permute-start.10 = (bf16[64,512]{1,0:T(8,128)(2,1)S(1)}, bf16[64,512]{1,0:T(8,128)(2,1)S(1)}, u32[]{:S(2)}, u32[]{:S(2)}) collective-permute-start(bf16[64,512]{1,0:T(8,128)(2,1)S(1)} %get-tuple-element.59), channel_id=1, source_target_pairs={{0,7},{1,6},{2,5},{3,4},{4,3},{5,2},{6,1},{7,0},{8,15},{9,14},{10,... | collective-permute-start | bytes 196616 | tf_op jit(solution)/shard_map/ppermute | solution.py:69
  32.2 2.8 %collective-permute-start.9 = (bf16[64,512]{1,0:T(8,128)(2,1)S(1)}, bf16[64,512]{1,0:T(8,128)(2,1)S(1)}, u32[]{:S(2)}, u32[]{:S(2)}) collective-permute-start(bf16[64,512]{1,0:T(8,128)(2,1)S(1)} %get-tuple-element.58), channel_id=1, source_target_pairs={{0,5},{1,4},{2,7},{3,6},{4,1},{5,0},{6,3},{7,2},{8,13},{9,12},{10,... | collective-permute-start | bytes 196616 | tf_op jit(solution)/shard_map/ppermute | solution.py:69
  35.5 1.9 %shard_map.144 = (bf16[128,512]{1,0:T(8,128)(2,1)S(1)}, bf16[128,512]{1,0:T(8,128)(2,1)S(1)}, bf16[128,512]{1,0:T(8,128)(2,1)S(1)}, bf16[128,512]{1,0:T(8,128)(2...) custom-call(s32[1]{0:T(128)} %bitcast.own_ref, s32[4]{0:T(128)S(1)} %pad_add_fusion.part_ref, ...), custom_call_target="tpu_custom_call" | custom-call | flops 2000000000 | tf_op jit(solution)/shard_map/pallas_call | solution.py:590
  37.8 1.6 %collective-permute-done.7.refs_0_ = bf16[64,512]{1,0:T(8,128)(2,1)S(1)} collective-permute-done((bf16[64,512]{1,0:T(8,128)(2,1)S(1)}, bf16[64,512]{1,0:T(8,128)(2,1)S(1)}, u32[]{:S(2)}, u32[]{:S(2)}) %collective-permute-start.7) | collective-permute-done | bytes 65568 | tf_op jit(solution)/shard_map/ppermute | solution.py:69
  39.3 0.7 %collective-permute-start.19 = (bf16[128,512]{1,0:T(8,128)(2,1)S(1)}, bf16[128,512]{1,0:T(8,128)(2,1)S(1)}, u32[]{:S(2)}, u32[]{:S(2)}) collective-permute-start(bf16[128,512]{1,0:T(8,128)(2,1)S(1)} %get-tuple-element.70), channel_id=1, source_target_pairs={{0,6},{2,4},{4,2},{6,0},{1,7},{3,5},{5,3},{7,1},{8,14},{10,12},{12... | collective-permute-start | bytes 393224 | tf_op jit(solution)/shard_map/ppermute | solution.py:69
  40.0 1.6 %shard_map.145 = (bf16[2,64,512]{2,1,0:T(8,128)(2,1)S(1)}, bf16[2,64,512]{2,1,0:T(8,128)(2,1)S(1)}, bf16[2,64,512]{2,1,0:T(8,128)(2,1)S(1)}, f32[2,64,512]{2,1,0:T(8,128)S(1)}) custom-call(s32[1]{0:T(128)} %bitcast.own_ref, s32[4]{0:T(128)S(1)} %pad_add_fusion.part_ref, bf16[512,512]{1,0:T(8,128)(2,1)S(1)} %bitcast.27, bf16[512,512]{1,0:T(8,128)(2,1)S(1)} %bitcast.29, ...), custom_call_target="tpu_custom_call" | custom-call | flops 2000000000 | tf_op jit(solution)/shard_map/pallas_call | solution.py:590
  41.6 1.1 %collective-permute-start.20 = (bf16[2,64,512]{2,1,0:T(8,128)(2,1)S(1)}, bf16[2,64,512]{2,1,0:T(8,128)(2,1)S(1)}, u32[]{:S(2)}, u32[]{:S(2)}) collective-permute-start(bf16[2,64,512]{2,1,0:T(8,128)(2,1)S(1)} %get-tuple-element.75), channel_id=1, source_target_pairs={{0,24},{8,16},{16,8},{24,0},{1,25},{9,17},{17,9},{25,1},{2,26},{10... | collective-permute-start | bytes 393224 | tf_op jit(solution)/shard_map/ppermute | solution.py:69
  42.7 0.9 %collective-permute-start.21 = (bf16[2,64,512]{2,1,0:T(8,128)(2,1)S(1)}, bf16[2,64,512]{2,1,0:T(8,128)(2,1)S(1)}, u32[]{:S(2)}, u32[]{:S(2)}) collective-permute-start(bf16[2,64,512]{2,1,0:T(8,128)(2,1)S(1)} %get-tuple-element.76), channel_id=1, source_target_pairs={{0,16},{8,24},{16,0},{24,8},{1,17},{9,25},{17,1},{25,9},{2,18},{10... | collective-permute-start | bytes 393224 | tf_op jit(solution)/shard_map/ppermute | solution.py:69
  43.6 2.5 %collective-permute-start.22 = (bf16[2,64,512]{2,1,0:T(8,128)(2,1)S(1)}, bf16[2,64,512]{2,1,0:T(8,128)(2,1)S(1)}, u32[]{:S(2)}, u32[]{:S(2)}) collective-permute-start(bf16[2,64,512]{2,1,0:T(8,128)(2,1)S(1)} %get-tuple-element.77), channel_id=1, source_target_pairs={{0,8},{8,0},{16,24},{24,16},{1,9},{9,1},{17,25},{25,17},{2,10},{10... | collective-permute-start | bytes 393224 | tf_op jit(solution)/shard_map/ppermute | solution.py:69
  46.1 1.4 %shard_map.146 = (bf16[128,512]{1,0:T(8,128)(2,1)}, bf16[128,512]{1,0:T(8,128)(2,1)}) custom-call(s32[1]{0:T(128)} %bitcast.own_ref, bf16[128,512]{1,0:T(8,128)(2,1)S(1)} %get-tuple-element.66.mixed_ref, bf16[160,512]{1,0:T(8,128)(2,1)S(1)} %get-tuple-element.42.refs_0_.extended_ref, bf16[128,512]{1,0:T(8,128)(2,1)S(1)} %get-tuple-element.67.refs_0_, ...), custom_call_target="tpu_custom_call" | custom-call | flops 1500000000 | tf_op jit(solution)/shard_map/pallas_call | solution.py:623
  47.5 2.5 %collective-permute-done.20.refs_0_ = bf16[2,64,512]{2,1,0:T(8,128)(2,1)S(1)} collective-permute-done((bf16[2,64,512]{2,1,0:T(8,128)(2,1)S(1)}, bf16[2,64,512]{2,1,0:T(8,128)(2,1)S(1)}, u32[]{:S(2)}, u32[]{:S(2)}) %collective-permute-start.20) | collective-permute-done | bytes 131104 | tf_op jit(solution)/shard_map/ppermute | solution.py:69
  50.0 5.9 %collective-permute-done.21.refs_1_ = bf16[2,64,512]{2,1,0:T(8,128)(2,1)S(1)} collective-permute-done((bf16[2,64,512]{2,1,0:T(8,128)(2,1)S(1)}, bf16[2,64,512]{2,1,0:T(8,128)(2,1)S(1)}, u32[]{:S(2)}, u32[]{:S(2)}) %collective-permute-start.21) | collective-permute-done | bytes 131104 | tf_op jit(solution)/shard_map/ppermute | solution.py:69
  56.0 0.7 %shard_map.147 = (f32[64,512]{1,0:T(8,128)}, f32[64,512]{1,0:T(8,128)}) custom-call(f32[2,64,512]{2,1,0:T(8,128)S(1)} %get-tuple-element.74.kept_ref, bf16[2,64,512]{2,1,0:T(8,128)(2,1)S(1)} %collective-permute-done.20.refs_0_, bf16[2,64,512]{2,1,0:T(8,128)(2,1)S(1)} %collective-permute-done.21.refs_1_, bf16[2,64,512]{2,1,0:T(8,128)(2,1)S(1)} %collective-permute-done.22.refs_2_), custom_call_target="tpu_custom_call" | custom-call | flops 500000000 | tf_op jit(solution)/shard_map/pallas_call | solution.py:630
  (51 shorter events, 4.2 us)
Async XLA Ops:
  0.6 13.2 %collective-permute-start.4 = (bf16[128,512]{1,0:T(8,128)(2,1)}, bf16[128,512]{1,0:T(8,128)(2,1)S(1)}, u32[]{:S(2)}, u32[]{:S(2)}) collective-permute-start(bf16[128,512]{1,0:T(8,128)(2,1)} %bitcast.35), channel_id=1, source_target_pairs={{0,1},{1,0},{2,3},{3,2},{4,5},{5,4},{6,7},{7,6},{8,9},{9,8},{10,11... | collective-permute-start | bytes 393224 | tf_op jit(solution)/shard_map/ppermute | solution.py:69
  3.6 8.4 %collective-permute-start = (bf16[128,512]{1,0:T(8,128)(2,1)}, bf16[128,512]{1,0:T(8,128)(2,1)S(1)}, u32[]{:S(2)}, u32[]{:S(2)}) collective-permute-start(bf16[128,512]{1,0:T(8,128)(2,1)} %bitcast.31), channel_id=1, source_target_pairs={{0,8},{8,16},{16,24},{24,0},{1,9},{9,17},{17,25},{25,1},{2,10},{10... | collective-permute-start | bytes 393224 | tf_op jit(solution)/shard_map/ppermute | solution.py:495
  5.2 8.3 %collective-permute-start.2 = (bf16[128,512]{1,0:T(8,128)(2,1)}, bf16[128,512]{1,0:T(8,128)(2,1)S(1)}, u32[]{:S(2)}, u32[]{:S(2)}) collective-permute-start(bf16[128,512]{1,0:T(8,128)(2,1)} %bitcast.33), channel_id=1, source_target_pairs={{0,8},{8,16},{16,24},{24,0},{1,9},{9,17},{17,25},{25,1},{2,10},{10... | collective-permute-start | bytes 393224 | tf_op jit(solution)/shard_map/ppermute | solution.py:495
  6.8 0.7 %copy-start.8 = (bf16[512,4]{0,1:T(4,128)(2,1)S(1)}, bf16[512,4]{0,1:T(4,128)(2,1)}, u32[]{:S(2)}) copy-start(bf16[512,4]{0,1:T(4,128)(2,1)} %param.17) | copy-start | bytes 12292
  7.5 0.9 %copy-start.3 = (bf16[1,128,512]{2,1,0:T(8,128)(2,1)S(1)}, bf16[1,128,512]{2,1,0:T(8,128)(2,1)}, u32[]{:S(2)}) copy-start(bf16[1,128,512]{2,1,0:T(8,128)(2,1)} %param.21) | copy-start | bytes 393220
  8.4 5.4 %copy-start.4 = (bf16[1,128,512]{2,1,0:T(8,128)(2,1)S(1)}, bf16[1,128,512]{2,1,0:T(8,128)(2,1)}, u32[]{:S(2)}) copy-start(bf16[1,128,512]{2,1,0:T(8,128)(2,1)} %param.12) | copy-start | bytes 393220
  8.4 5.4 %copy-start.5 = (bf16[1,128,512]{2,1,0:T(8,128)(2,1)S(1)}, bf16[1,128,512]{2,1,0:T(8,128)(2,1)}, u32[]{:S(2)}) copy-start(bf16[1,128,512]{2,1,0:T(8,128)(2,1)} %param.13) | copy-start | bytes 393220
  8.4 5.4 %copy-start.6 = (bf16[1,128,512]{2,1,0:T(8,128)(2,1)S(1)}, bf16[1,128,512]{2,1,0:T(8,128)(2,1)}, u32[]{:S(2)}) copy-start(bf16[1,128,512]{2,1,0:T(8,128)(2,1)} %param.11) | copy-start | bytes 393220
  9.0 7.8 %collective-permute-start.5 = (bf16[160,512]{1,0:T(8,128)(2,1)S(1)}, bf16[160,512]{1,0:T(8,128)(2,1)S(1)}, u32[]{:S(2)}, u32[]{:S(2)}) collective-permute-start(bf16[160,512]{1,0:T(8,128)(2,1)S(1)} %get-tuple-element.42.refs_0_.extended_ref), channel_id=1, source_target_pairs={{0,1},{1,0},{2,3},{3,2},{4,5},{5,4},{6,7},{7,6},{8,9},{9,8},{10,11... | collective-permute-start | bytes 491528 | tf_op jit(solution)/shard_map/ppermute | solution.py:69
  12.1 7.3 %collective-permute-start.1 = (bf16[128,512]{1,0:T(8,128)(2,1)S(1)}, bf16[128,512]{1,0:T(8,128)(2,1)S(1)}, u32[]{:S(2)}, u32[]{:S(2)}) collective-permute-start(bf16[128,512]{1,0:T(8,128)(2,1)S(1)} %collective-permute-done.refs_4_), channel_id=1, source_target_pairs={{0,8},{8,16},{16,24},{24,0},{1,9},{9,17},{17,25},{25,1},{2,10},{10... | collective-permute-start | bytes 393224 | tf_op jit(solution)/shard_map/ppermute | solution.py:495
  13.5 7.3 %collective-permute-start.3 = (bf16[128,512]{1,0:T(8,128)(2,1)S(1)}, bf16[128,512]{1,0:T(8,128)(2,1)S(1)}, u32[]{:S(2)}, u32[]{:S(2)}) collective-permute-start(bf16[128,512]{1,0:T(8,128)(2,1)S(1)} %collective-permute-done.2.refs_5_), channel_id=1, source_target_pairs={{0,8},{8,16},{16,24},{24,0},{1,9},{9,17},{17,25},{25,1},{2,10},{10... | collective-permute-start | bytes 393224 | tf_op jit(solution)/shard_map/ppermute | solution.py:495
  21.5 5.3 %collective-permute-start.6 = (bf16[592,128]{1,0:T(8,128)(2,1)S(1)}, bf16[592,128]{1,0:T(8,128)(2,1)S(1)}, u32[]{:S(2)}, u32[]{:S(2)}) collective-permute-start(bf16[592,128]{1,0:T(8,128)(2,1)S(1)} %shard_map.142), channel_id=1, source_target_pairs={{0,1},{1,0},{2,3},{3,2},{4,5},{5,4},{6,7},{7,6},{8,9},{9,8},{10,11... | collective-permute-start | bytes 454664 | tf_op jit(solution)/shard_map/ppermute | solution.py:69
  22.5 6.6 %collective-permute-start.11 = (bf16[128,512]{1,0:T(8,128)(2,1)S(1)}, bf16[128,512]{1,0:T(8,128)(2,1)S(1)}, u32[]{:S(2)}, u32[]{:S(2)}) collective-permute-start(bf16[128,512]{1,0:T(8,128)(2,1)S(1)} %get-tuple-element.60), channel_id=1, source_target_pairs={{0,6},{2,4},{4,2},{6,0},{1,7},{3,5},{5,3},{7,1},{8,14},{10,12},{12... | collective-permute-start | bytes 393224 | tf_op jit(solution)/shard_map/ppermute | solution.py:69
  22.5 8.2 %collective-permute-start.12 = (bf16[128,512]{1,0:T(8,128)(2,1)S(1)}, bf16[128,512]{1,0:T(8,128)(2,1)S(1)}, u32[]{:S(2)}, u32[]{:S(2)}) collective-permute-start(bf16[128,512]{1,0:T(8,128)(2,1)S(1)} %get-tuple-element.61), channel_id=1, source_target_pairs={{0,4},{2,6},{4,0},{6,2},{1,5},{3,7},{5,1},{7,3},{8,12},{10,14},{12... | collective-permute-start | bytes 393224 | tf_op jit(solution)/shard_map/ppermute | solution.py:69
  23.8 7.9 %collective-permute-start.13 = (bf16[128,512]{1,0:T(8,128)(2,1)S(1)}, bf16[128,512]{1,0:T(8,128)(2,1)S(1)}, u32[]{:S(2)}, u32[]{:S(2)}) collective-permute-start(bf16[128,512]{1,0:T(8,128)(2,1)S(1)} %get-tuple-element.62), channel_id=1, source_target_pairs={{0,2},{2,0},{4,6},{6,4},{1,3},{3,1},{5,7},{7,5},{8,10},{10,8},{12,... | collective-permute-start | bytes 393224 | tf_op jit(solution)/shard_map/ppermute | solution.py:69
  24.4 2.4 %copy-start = (bf16[512,512]{1,0:T(8,128)(2,1)S(1)}, bf16[512,512]{1,0:T(8,128)(2,1)}, u32[]{:S(2)}) copy-start(bf16[512,512]{1,0:T(8,128)(2,1)} %proj_ref.1) | copy-start | bytes 1572868
  24.4 2.4 %copy-start.7 = (bf16[1,128,512]{2,1,0:T(8,128)(2,1)S(1)}, bf16[1,128,512]{2,1,0:T(8,128)(2,1)}, u32[]{:S(2)}) copy-start(bf16[1,128,512]{2,1,0:T(8,128)(2,1)} %param.15) | copy-start | bytes 393220
  26.8 8.7 %copy-start.1 = (bf16[1,512,512]{2,1,0:T(8,128)(2,1)S(1)}, bf16[1,512,512]{2,1,0:T(8,128)(2,1)}, u32[]{:S(2)}) copy-start(bf16[1,512,512]{2,1,0:T(8,128)(2,1)} %param.19) | copy-start | bytes 1572868
  26.8 8.7 %copy-start.2 = (bf16[1,512,512]{2,1,0:T(8,128)(2,1)S(1)}, bf16[1,512,512]{2,1,0:T(8,128)(2,1)}, u32[]{:S(2)}) copy-start(bf16[1,512,512]{2,1,0:T(8,128)(2,1)} %param.20) | copy-start | bytes 1572868
  27.4 4.8 %collective-permute-start.14 = (bf16[64,512]{1,0:T(8,128)(2,1)S(1)}, bf16[64,512]{1,0:T(8,128)(2,1)S(1)}, u32[]{:S(2)}, u32[]{:S(2)}) collective-permute-start(bf16[64,512]{1,0:T(8,128)(2,1)S(1)} %get-tuple-element.57), channel_id=1, source_target_pairs={{0,2},{1,3},{2,0},{3,1},{4,6},{5,7},{6,4},{7,5},{8,10},{9,11},{10,... | collective-permute-start | bytes 196616 | tf_op jit(solution)/shard_map/ppermute | solution.py:69
  27.5 7.6 %collective-permute-start.15 = (bf16[64,512]{1,0:T(8,128)(2,1)S(1)}, bf16[64,512]{1,0:T(8,128)(2,1)S(1)}, u32[]{:S(2)}, u32[]{:S(2)}) collective-permute-start(bf16[64,512]{1,0:T(8,128)(2,1)S(1)} %get-tuple-element.58), channel_id=1, source_target_pairs={{0,4},{1,5},{2,6},{3,7},{4,0},{5,1},{6,2},{7,3},{8,12},{9,13},{10,... | collective-permute-start | bytes 196616 | tf_op jit(solution)/shard_map/ppermute | solution.py:69
  29.1 6.4 %collective-permute-start.16 = (bf16[64,512]{1,0:T(8,128)(2,1)S(1)}, bf16[64,512]{1,0:T(8,128)(2,1)S(1)}, u32[]{:S(2)}, u32[]{:S(2)}) collective-permute-start(bf16[64,512]{1,0:T(8,128)(2,1)S(1)} %get-tuple-element.59), channel_id=1, source_target_pairs={{0,6},{1,7},{2,4},{3,5},{4,2},{5,3},{6,0},{7,1},{8,14},{9,15},{10,... | collective-permute-start | bytes 196616 | tf_op jit(solution)/shard_map/ppermute | solution.py:69
  30.7 6.7 %collective-permute-start.10 = (bf16[64,512]{1,0:T(8,128)(2,1)S(1)}, bf16[64,512]{1,0:T(8,128)(2,1)S(1)}, u32[]{:S(2)}, u32[]{:S(2)}) collective-permute-start(bf16[64,512]{1,0:T(8,128)(2,1)S(1)} %get-tuple-element.59), channel_id=1, source_target_pairs={{0,7},{1,6},{2,5},{3,4},{4,3},{5,2},{6,1},{7,0},{8,15},{9,14},{10,... | collective-permute-start | bytes 196616 | tf_op jit(solution)/shard_map/ppermute | solution.py:69
  31.8 8.2 %collective-permute-start.8 = (bf16[64,512]{1,0:T(8,128)(2,1)S(1)}, bf16[64,512]{1,0:T(8,128)(2,1)S(1)}, u32[]{:S(2)}, u32[]{:S(2)}) collective-permute-start(bf16[64,512]{1,0:T(8,128)(2,1)S(1)} %get-tuple-element.57), channel_id=1, source_target_pairs={{0,3},{1,2},{2,1},{3,0},{4,7},{5,6},{6,5},{7,4},{8,11},{9,10},{10,... | collective-permute-start | bytes 196616 | tf_op jit(solution)/shard_map/ppermute | solution.py:69
  32.2 7.8 %collective-permute-start.9 = (bf16[64,512]{1,0:T(8,128)(2,1)S(1)}, bf16[64,512]{1,0:T(8,128)(2,1)S(1)}, u32[]{:S(2)}, u32[]{:S(2)}) collective-permute-start(bf16[64,512]{1,0:T(8,128)(2,1)S(1)} %get-tuple-element.58), channel_id=1, source_target_pairs={{0,5},{1,4},{2,7},{3,6},{4,1},{5,0},{6,3},{7,2},{8,13},{9,12},{10,... | collective-permute-start | bytes 196616 | tf_op jit(solution)/shard_map/ppermute | solution.py:69
  35.1 4.3 %collective-permute-start.7 = (bf16[64,512]{1,0:T(8,128)(2,1)S(1)}, bf16[64,512]{1,0:T(8,128)(2,1)S(1)}, u32[]{:S(2)}, u32[]{:S(2)}) collective-permute-start(bf16[64,512]{1,0:T(8,128)(2,1)S(1)} %get-tuple-element.56.refs_0_), channel_id=1, source_target_pairs={{0,1},{1,0},{2,3},{3,2},{4,5},{5,4},{6,7},{7,6},{8,9},{9,8},{10,11... | collective-permute-start | bytes 196616 | tf_op jit(solution)/shard_map/ppermute | solution.py:69
  37.3 6.3 %collective-permute-start.17 = (bf16[128,512]{1,0:T(8,128)(2,1)S(1)}, bf16[128,512]{1,0:T(8,128)(2,1)S(1)}, u32[]{:S(2)}, u32[]{:S(2)}) collective-permute-start(bf16[128,512]{1,0:T(8,128)(2,1)S(1)} %get-tuple-element.68), channel_id=1, source_target_pairs={{0,2},{2,0},{4,6},{6,4},{1,3},{3,1},{5,7},{7,5},{8,10},{10,8},{12,... | collective-permute-start | bytes 393224 | tf_op jit(solution)/shard_map/ppermute | solution.py:69
  37.4 8.7 %collective-permute-start.18 = (bf16[128,512]{1,0:T(8,128)(2,1)S(1)}, bf16[128,512]{1,0:T(8,128)(2,1)S(1)}, u32[]{:S(2)}, u32[]{:S(2)}) collective-permute-start(bf16[128,512]{1,0:T(8,128)(2,1)S(1)} %get-tuple-element.69), channel_id=1, source_target_pairs={{0,4},{2,6},{4,0},{6,2},{1,5},{3,7},{5,1},{7,3},{8,12},{10,14},{12... | collective-permute-start | bytes 393224 | tf_op jit(solution)/shard_map/ppermute | solution.py:69
  39.3 6.8 %collective-permute-start.19 = (bf16[128,512]{1,0:T(8,128)(2,1)S(1)}, bf16[128,512]{1,0:T(8,128)(2,1)S(1)}, u32[]{:S(2)}, u32[]{:S(2)}) collective-permute-start(bf16[128,512]{1,0:T(8,128)(2,1)S(1)} %get-tuple-element.70), channel_id=1, source_target_pairs={{0,6},{2,4},{4,2},{6,0},{1,7},{3,5},{5,3},{7,1},{8,14},{10,12},{12... | collective-permute-start | bytes 393224 | tf_op jit(solution)/shard_map/ppermute | solution.py:69
  41.6 8.4 %collective-permute-start.20 = (bf16[2,64,512]{2,1,0:T(8,128)(2,1)S(1)}, bf16[2,64,512]{2,1,0:T(8,128)(2,1)S(1)}, u32[]{:S(2)}, u32[]{:S(2)}) collective-permute-start(bf16[2,64,512]{2,1,0:T(8,128)(2,1)S(1)} %get-tuple-element.75), channel_id=1, source_target_pairs={{0,24},{8,16},{16,8},{24,0},{1,25},{9,17},{17,9},{25,1},{2,26},{10... | collective-permute-start | bytes 393224 | tf_op jit(solution)/shard_map/ppermute | solution.py:69
  42.7 13.2 %collective-permute-start.21 = (bf16[2,64,512]{2,1,0:T(8,128)(2,1)S(1)}, bf16[2,64,512]{2,1,0:T(8,128)(2,1)S(1)}, u32[]{:S(2)}, u32[]{:S(2)}) collective-permute-start(bf16[2,64,512]{2,1,0:T(8,128)(2,1)S(1)} %get-tuple-element.76), channel_id=1, source_target_pairs={{0,16},{8,24},{16,0},{24,8},{1,17},{9,25},{17,1},{25,9},{2,18},{10... | collective-permute-start | bytes 393224 | tf_op jit(solution)/shard_map/ppermute | solution.py:69
  43.6 12.4 %collective-permute-start.22 = (bf16[2,64,512]{2,1,0:T(8,128)(2,1)S(1)}, bf16[2,64,512]{2,1,0:T(8,128)(2,1)S(1)}, u32[]{:S(2)}, u32[]{:S(2)}) collective-permute-start(bf16[2,64,512]{2,1,0:T(8,128)(2,1)S(1)} %get-tuple-element.77), channel_id=1, source_target_pairs={{0,8},{8,0},{16,24},{24,16},{1,9},{9,1},{17,25},{25,17},{2,10},{10... | collective-permute-start | bytes 393224 | tf_op jit(solution)/shard_map/ppermute | solution.py:69
  (2 other events, 1.3 us)

commit v12 on v11

--- a/solution.py
+++ b/solution.py
@@ -234,10 +234,10 @@
             fold(place, k, pair_ref, block, begin, False)
 
 
-def attend_kernel(plan, reps, counts, packed, ahead, ids_ref, begin_ref, *refs):
+def attend_kernel(plan, reps, counts, packed, ids_ref, begin_ref, *refs):
     ks = sorted({k for k, unused_pair, unused_first in plan})
     old_ks = [k for k in ks if not any(first for j, unused_pair, first in plan if j == k)]
-    query_refs, refs = dict(zip(ks, refs)), refs[len(ks) + ahead :]
+    query_refs, refs = dict(zip(ks, refs)), refs[len(ks) :]
     pair_refs = [refs[2 * place : 2 * place + 2] for place in range(counts)]
     refs = refs[2 * counts :]
     old_refs, refs = refs[: 3 * len(old_ks)], refs[3 * len(old_ks) :]
@@ -301,6 +301,16 @@
     rows = dot(placed, normed).astype(jnp.bfloat16)
     for k, sent_ref in enumerate(sent_refs):
         sent_ref[...] = rows[k * hot_capacity : (k + 1) * hot_capacity]
+
+
+def grad_plan(parts):
+    if parts == 4:
+        return [[(0, 0), (1, 0), (1, 2)], [(0, 1), (1, 1), (1, 3)], [(0, 2)], [(0, 3)]]
+    return [[(0, 0), (1, 0)]] + [[(0, k), (1, k)] for k in range(1, parts)]
+
+
+def pair_kernel(kept_ref, near_ref, sent_ref):
+    sent_ref[0] = (kept_ref[2] + near_ref[2].astype(jnp.float32)).astype(jnp.bfloat16)
 
 
 def expert_kernel(
@@ -379,14 +389,10 @@
         return
     up_term = up_term + up_old[...]
     down_term = down_term + down_old[...]
-    for k in range(parts):
-        rows = slice(k * strip, (k + 1) * strip)
-        if k == 0:
-            kept_ref[0] = up_term[rows]
-            kept_ref[1] = down_term[rows]
-        else:
-            term_refs[k - 1][0] = up_term[rows].astype(jnp.bfloat16)
-            term_refs[k - 1][1] = down_term[rows].astype(jnp.bfloat16)
+    for ref, entries in zip((kept_ref, *term_refs), grad_plan(parts)):
+        for place, (kind, k) in enumerate(entries):
+            term = (up_term, down_term)[kind][k * strip : (k + 1) * strip]
+            ref[place] = term.astype(ref.dtype)
 
 
 def finish_kernel(
@@ -424,12 +430,13 @@
     grad_mixed_ref[...] = (grad_f + input_grad).astype(jnp.bfloat16)
 
 
-def sum_kernel(kept_ref, *refs):
-    term_refs, (up_ref, down_ref) = refs[:-2], refs[-2:]
-    for kind, out_ref in enumerate((up_ref, down_ref)):
-        total = kept_ref[kind]
-        for ref in term_refs:
-            total = total + ref[kind].astype(jnp.float32)
+def sum_kernel(plan, kept_ref, *refs):
+    term_refs, out_refs = refs[:-2], refs[-2:]
+    totals = [kept_ref[0], kept_ref[1]]
+    for kinds, ref in zip(plan, term_refs):
+        for place, kind in enumerate(kinds):
+            totals[kind] = totals[kind] + ref[place].astype(jnp.float32)
+    for total, out_ref in zip(totals, out_refs):
         out_ref[...] = total
 
 
@@ -522,7 +529,7 @@
         jnp.stack(query_ranks).astype(jnp.int32), doc_lengths, choice, router.T, grad_out[0]
     )
 
-    def attend(plan, pairs, steps, queries, states, packed, cost, ahead=()):
+    def attend(plan, pairs, steps, queries, states, packed, cost):
         ks = sorted({k for k, unused_pair, unused_first in plan})
         old = [one for k in ks if k in states for one in states[k]]
         state_out = state_shapes * len(ks)
@@ -533,45 +540,42 @@
             out_shape, scratch = state_out, []
         outs = call(
             functools.partial(
-                attend_kernel, plan, rep_count, len(pairs), packed, len(ahead)
+                attend_kernel, plan, rep_count, len(pairs), packed
             ),
             out_shape,
-            [SMEM] + [VMEM] * (1 + len(ks) + len(ahead) + 2 * len(pairs) + len(old)),
+            [SMEM] + [VMEM] * (1 + len(ks) + 2 * len(pairs) + len(old)),
             scratch + [pltpu.VMEM((len(plan), tok, tok), jnp.float32)],
             cost=cost,
-        )(task_ids(plan, steps), begin, *[queries[k] for k in ks], *ahead, *[one for both in pairs for one in both], *old)
+        )(task_ids(plan, steps), begin, *[queries[k] for k in ks], *[one for both in pairs for one in both], *old)
         if packed:
             return dict(zip(ks, outs))
         return {k: list(outs[3 * place : 3 * place + 3]) for place, k in enumerate(ks)}
 
     others = range(1, rep_count)
     lines = [(key_rows[0], value_rows[0])]
-    for unused in range(reach):
-        lines.append(tuple(forward(one) for one in lines[-1]))
+    lines.append(tuple(forward(one) for one in lines[0]))
     queries = reps.exchange([query_rows[0]] * rep_count)
     extendeds = reps.exchange([extended] * rep_count)
-    middle = tuple((0, step, step == 0) for step in range(reach)) + tuple(
+    states = attend(((0, 0, True),), lines[:1], [0], queries, {}, False, 2.0)
+    ahead, *states[0] = lax.optimization_barrier((lines[1][0], *states[0]))
+    lines[1] = (ahead, lines[1][1])
+    for unused in range(1, reach):
+        lines.append(tuple(forward(one) for one in lines[-1]))
+    middle = tuple((0, step, False) for step in range(1, reach)) + tuple(
         (k, step, step == 0) for k in others for step in range(reach)
     )
-    states = attend(middle, lines[:-1], list(range(reach)), queries, {}, False, 5.0)
-    states[1][0], *extendeds[1:] = lax.optimization_barrier((states[1][0], *extendeds[1:]))
+    states = attend(middle, lines[:-1], list(range(reach)), queries, states, False, 4.0)
+    partial = attend(
+        tuple((k, 0, False) for k in others), lines[-1:], [reach], queries, states, True, 1.5
+    )
+    partial[1], *extendeds[1:] = lax.optimization_barrier((partial[1], *extendeds[1:]))
+    returned = reps.exchange([None] + [partial[k] for k in others], inverse=True)[1:]
+    states = attend(((0, 0, False),), lines[-1:], [reach], queries, states, False, 1.5)
     sent_grads = call(
         functools.partial(dispatch_kernel, rep_count, tok, hot_capacity),
         [shape((rep_count * hot_capacity, width))] * expert_count,
         [SMEM] + [VMEM] * rep_count,
     )(own, *extendeds)
-    partial = attend(
-        tuple((k, 0, False) for k in others),
-        lines[-1:],
-        [reach],
-        queries,
-        states,
-        True,
-        1.5,
-        ahead=sent_grads[:1],
-    )
-    returned = reps.exchange([None] + [partial[k] for k in others], inverse=True)[1:]
-    states = attend(((0, 0, False),), lines[-1:], [reach], queries, states, False, 1.5)
     got_grads = merged(experts.exchange(sent_grads), MOST_PERMUTES)[::-1]
 
     mixed, *sent_rows = call(
@@ -615,11 +619,19 @@
     *terms, kept = expert_call(
         tuple(range(1, rep_count)),
         got_more,
-        [shape((2, strip, hidden))] * (seq_count - 1)
-        + [shape((2, strip, hidden), jnp.float32)],
+        [shape((len(entries), strip, hidden)) for entries in grad_plan(seq_count)[1:]]
+        + [shape((len(grad_plan(seq_count)[0]), strip, hidden), jnp.float32)],
         [up_acc, down_acc],
     )
-    got_terms = parts.exchange([None] + terms)[1:]
+    if seq_count == 4:
+        near, *direct = parts.exchange([None] + terms)[1:]
+        crossing = call(pair_kernel, shape((1, strip, hidden)), [VMEM, VMEM])(kept, near)
+        crossed = lax.ppermute(crossing, "seq", [(i, parts.target(i, 2)) for i in range(4)])
+        got_terms = [near, *direct, crossed]
+        plan = ((0, 1), (0,), (0,), (1,))
+    else:
+        got_terms = parts.exchange([None] + terms)[1:]
+        plan = ((0, 1),) * len(got_terms)
     layer_out, grad_mixed = call(
         functools.partial(finish_kernel, hot_capacity, expert_count),
         [shape((tok, width)), shape((tok, width))],
@@ -628,10 +640,10 @@
     )(own, mixed, extended, *got_back)
     kept, layer_out = lax.optimization_barrier((kept, layer_out))
     share_in, share_out = call(
-        sum_kernel,
+        functools.partial(sum_kernel, plan),
         [shape((strip, hidden), jnp.float32), shape((strip, width), jnp.float32)],
-        [VMEM] * seq_count,
-    )(kept, *got_terms[::-1])
+        [VMEM] * (1 + len(got_terms)),
+    )(kept, *got_terms)
     return (layer_out[None], grad_mixed[None], share_in[None], share_out[None])
 
 

time: 56.6 us -> 57.5 us (1.016)
  starting transfers between devices: 22.1 us -> 21.3 us
  Pallas kernels: 11.8 us -> 12.6 us
    ppermute x19, starting transfers between devices: 18.5 us -> 15.8 us  [exchange(): got[k] = lax.ppermute(chunks[k], self.axes, pairs)]
    ppermute x19, waiting for transfers between devices: 13 us -> 14.7 us  [exchange(): got[k] = lax.ppermute(chunks[k], self.axes, pairs)]
    ppermute x4, waiting for transfers between devices: 7.05 us -> 5.86 us  [forward(): lax.ppermute(array, 'seq', [(i, (i + 1) % seq_count) for i in range(seq_c...]
    ppermute x0 -> x1, starting transfers between devices: none -> 1.13 us  [local(): lax.ppermute(crossing, 'seq', [(i, parts.target(i, 2)) for i in range(4)])]
    ppermute x4, starting transfers between devices: 3.54 us -> 4.4 us  [forward(): lax.ppermute(array, 'seq', [(i, (i + 1) % seq_count) for i in range(seq_c...]
    pallas_call x3 -> x4, Pallas kernels: 4.47 us -> 5.19 us  [attend(): call(functools.partial(attend_kernel, plan, rep_count, len(pairs), packed...]
  transfers between devices with their start and end apart: 23 -> 24, of which waited for: 9 -> 8; matrix products, arithmetic and copies ran while one was open for 1% -> 1% of each run, Pallas kernels for 18% -> 18%
where the time goes in v12:
time: 57.5 us; the launch traced here: 57.3 us
  starting transfers between devices  21.3 us (37%)
  waiting for transfers between devices  20.6 us (36%)
  Pallas kernels  12.6 us (22%)
  local copies, waits for them, and re-layouts  1.69 us (3%)
  between operations  0.81 us (1%)
    ppermute x19, starting transfers between devices, exchange(): got[k] = lax.ppermute(chunks[k], self.axes, pairs)  15.8 us
    ppermute x19, waiting for transfers between devices, exchange(): got[k] = lax.ppermute(chunks[k], self.axes, pairs)  14.7 us
    ppermute x4, waiting for transfers between devices, forward(): lax.ppermute(array, 'seq', [(i, (i + 1) % seq_count) for i in range(seq_c...  5.86 us
    pallas_call x4, Pallas kernels, attend(): call(functools.partial(attend_kernel, plan, rep_count, len(pairs), packed...  5.19 us
    ppermute x4, starting transfers between devices, forward(): lax.ppermute(array, 'seq', [(i, (i + 1) % seq_count) for i in range(seq_c...  4.4 us
    pallas_call x2, Pallas kernels, expert_call(): call(functools.partial(expert_kernel, rep_count, rep_list, expert_count,...  3.49 us
    unnamed x22, local copies, waits for them, and re-layouts  1.6 us
    pallas_call x1, Pallas kernels, local(): call(functools.partial(finish_kernel, hot_capacity, expert_count), [shape...  1.42 us
  transfers between devices with their start and end apart: 24, of which 8 were waited for; matrix products, arithmetic and copies ran while one was open for 1% of the time, Pallas kernels for 18%

profile of v12, /device:TPU:0, one launch (start us, length us, event | category | flops | bytes accessed | tf_op | source)
XLA Modules:
  0.0 57.3 jit_solution(12704795460158140884)
XLA Ops:
  0.6 3.0 %collective-permute-start.4 = (bf16[128,512]{1,0:T(8,128)(2,1)}, bf16[128,512]{1,0:T(8,128)(2,1)S(1)}, u32[]{:S(2)}, u32[]{:S(2)}) collective-permute-start(bf16[128,512]{1,0:T(8,128)(2,1)} %bitcast.37), channel_id=1, source_target_pairs={{0,1},{1,0},{2,3},{3,2},{4,5},{5,4},{6,7},{7,6},{8,9},{9,8},{10,11... | collective-permute-start | bytes 393224 | tf_op jit(solution)/shard_map/ppermute | solution.py:69
  3.6 1.6 %collective-permute-start = (bf16[128,512]{1,0:T(8,128)(2,1)}, bf16[128,512]{1,0:T(8,128)(2,1)S(1)}, u32[]{:S(2)}, u32[]{:S(2)}) collective-permute-start(bf16[128,512]{1,0:T(8,128)(2,1)} %bitcast.31), channel_id=1, source_target_pairs={{0,8},{8,16},{16,24},{24,0},{1,9},{9,17},{17,25},{25,1},{2,10},{10... | collective-permute-start | bytes 393224 | tf_op jit(solution)/shard_map/ppermute | solution.py:502
  5.2 1.6 %collective-permute-start.2 = (bf16[128,512]{1,0:T(8,128)(2,1)}, bf16[128,512]{1,0:T(8,128)(2,1)S(1)}, u32[]{:S(2)}, u32[]{:S(2)}) collective-permute-start(bf16[128,512]{1,0:T(8,128)(2,1)} %bitcast.34), channel_id=1, source_target_pairs={{0,8},{8,16},{16,24},{24,0},{1,9},{9,17},{17,25},{25,1},{2,10},{10... | collective-permute-start | bytes 393224 | tf_op jit(solution)/shard_map/ppermute | solution.py:502
  6.9 0.6 %copy-done.8 = bf16[512,4]{0,1:T(4,128)(2,1)S(1)} copy-done((bf16[512,4]{0,1:T(4,128)(2,1)S(1)}, bf16[512,4]{0,1:T(4,128)(2,1)}, u32[]{:S(2)}) %copy-start.8) | copy-done | bytes 4120
  7.5 0.9 %copy-done.3 = bf16[1,128,512]{2,1,0:T(8,128)(2,1)S(1)} copy-done((bf16[1,128,512]{2,1,0:T(8,128)(2,1)S(1)}, bf16[1,128,512]{2,1,0:T(8,128)(2,1)}, u32[]{:S(2)}) %copy-start.3) | copy-done | bytes 131096
  9.0 0.6 %collective-permute-start.5 = (bf16[160,512]{1,0:T(8,128)(2,1)S(1)}, bf16[160,512]{1,0:T(8,128)(2,1)S(1)}, u32[]{:S(2)}, u32[]{:S(2)}) collective-permute-start(bf16[160,512]{1,0:T(8,128)(2,1)S(1)} %get-tuple-element.49.extended_ref.refs_0_), channel_id=1, source_target_pairs={{0,1},{1,0},{2,3},{3,2},{4,5},{5,4},{6,7},{7,6},{8,9},{9,8},{10,11... | collective-permute-start | bytes 491528 | tf_op jit(solution)/shard_map/ppermute | solution.py:69
  9.7 1.7 %shard_map.139 = (f32[16,128]{1,0:T(8,128)S(1)}, f32[16,128]{1,0:T(8,128)S(1)}, f32[512,128]{1,0:T(8,128)S(1)}) custom-call(s32[3]{0:T(128)S(1)} %pad_add_fusion.4.ids_ref, s32[2,128]{1,0:T(2,128)S(1)} %get-tuple-element.50.begin_ref, bf16[128,512]{1,0:T(8,128)(2,1)S(1)} %bitcast.38, bf16[128,512]{1,0:T(8,128)(2,1)S(1)} %bitcast.32, ...), custom_call_target="tpu_custom_call" | custom-call | flops 2000000000 | tf_op jit(solution)/shard_map/pallas_call | solution.py:541
  12.1 1.2 %collective-permute-start.1 = (bf16[128,512]{1,0:T(8,128)(2,1)S(1)}, bf16[128,512]{1,0:T(8,128)(2,1)S(1)}, u32[]{:S(2)}, u32[]{:S(2)}) collective-permute-start(bf16[128,512]{1,0:T(8,128)(2,1)S(1)} %collective-permute-done.refs_4_), channel_id=1, source_target_pairs={{0,8},{8,16},{16,24},{24,0},{1,9},{9,17},{17,25},{25,1},{2,10},{10... | collective-permute-start | bytes 393224 | tf_op jit(solution)/shard_map/ppermute | solution.py:502
  13.5 1.9 %shard_map.140 = (f32[16,128]{1,0:T(8,128)S(1)}, f32[16,128]{1,0:T(8,128)S(1)}, f32[512,128]{1,0:T(8,128)S(1)}, f32[16,128]{1,0:T(8,128)S(1)}, f32[16,128]{1,0:T(8,128)S(1)}, /*index=5*/f32[512,128]{1,0:T(8,128)S(1)}) custom-call(s32[5]{0:T(128)S(1)} %stack.81.ids_ref, s32[2,128]{1,0:T(2,128)S(1)} %get-tuple-element.50.begin_ref, ...), custom_call_target="tpu_custom_call" | custom-call | flops 4000000000 | tf_op jit(solution)/shard_map/pallas_call | solution.py:541
  15.4 5.4 %collective-permute-done.3.refs_2_ = bf16[128,512]{1,0:T(8,128)(2,1)S(1)} collective-permute-done((bf16[128,512]{1,0:T(8,128)(2,1)S(1)}, bf16[128,512]{1,0:T(8,128)(2,1)S(1)}, u32[]{:S(2)}, u32[]{:S(2)}) %collective-permute-start.3) | collective-permute-done | bytes 131104 | tf_op jit(solution)/shard_map/ppermute | solution.py:502
  20.8 0.8 %shard_map.142 = bf16[592,128]{1,0:T(8,128)(2,1)S(1)} custom-call(s32[3]{0:T(128)S(1)} %pad_add_fusion.5.ids_ref, s32[2,128]{1,0:T(2,128)S(1)} %get-tuple-element.50.begin_ref, bf16[128,512]{1,0:T(8,128)(2,1)S(1)} %collective-permute-done.4.refs_1_.refs_0_, bf16[128,512]{1,0:T(8,128)(2,1)S(1)} %collective-permute-done.1.refs_1_, ...), custom_call_target="tpu_custom_call" | custom-call | flops 1500000000 | tf_op jit(solution)/shard_map/pallas_call | solution.py:541
  21.6 1.2 %collective-permute-start.6 = (bf16[592,128]{1,0:T(8,128)(2,1)S(1)}, bf16[592,128]{1,0:T(8,128)(2,1)S(1)}, u32[]{:S(2)}, u32[]{:S(2)}) collective-permute-start(bf16[592,128]{1,0:T(8,128)(2,1)S(1)} %shard_map.142), channel_id=1, source_target_pairs={{0,1},{1,0},{2,3},{3,2},{4,5},{5,4},{6,7},{7,6},{8,9},{9,8},{10,11... | collective-permute-start | bytes 454664 | tf_op jit(solution)/shard_map/ppermute | solution.py:69
  23.4 1.6 %collective-permute-start.12 = (bf16[128,512]{1,0:T(8,128)(2,1)S(1)}, bf16[128,512]{1,0:T(8,128)(2,1)S(1)}, u32[]{:S(2)}, u32[]{:S(2)}) collective-permute-start(bf16[128,512]{1,0:T(8,128)(2,1)S(1)} %get-tuple-element.74), channel_id=1, source_target_pairs={{0,4},{2,6},{4,0},{6,2},{1,5},{3,7},{5,1},{7,3},{8,12},{10,14},{12... | collective-permute-start | bytes 393224 | tf_op jit(solution)/shard_map/ppermute | solution.py:69
  25.3 0.7 %shard_map.141 = (f32[16,128]{1,0:T(8,128)S(1)}, f32[16,128]{1,0:T(8,128)S(1)}, f32[512,128]{1,0:T(8,128)S(1)}) custom-call(s32[3]{0:T(128)S(1)} %pad_add_fusion.2.ids_ref, s32[2,128]{1,0:T(2,128)S(1)} %get-tuple-element.50.begin_ref, bf16[128,512]{1,0:T(8,128)(2,1)S(1)} %bitcast.40, bf16[128,512]{1,0:T(8,128)(2,1)S(1)} %collective-permute-done.1.refs_1_, ...), custom_call_target="tpu_custom_call" | custom-call | flops 1500000000 | tf_op jit(solution)/shard_map/pallas_call | solution.py:541
  26.0 0.8 %collective-permute-done.6.refs_3_ = bf16[592,128]{1,0:T(8,128)(2,1)S(1)} collective-permute-done((bf16[592,128]{1,0:T(8,128)(2,1)S(1)}, bf16[592,128]{1,0:T(8,128)(2,1)S(1)}, u32[]{:S(2)}, u32[]{:S(2)}) %collective-permute-start.6) | collective-permute-done | bytes 151584 | tf_op jit(solution)/shard_map/ppermute | solution.py:69
  26.8 0.6 %shard_map.143 = (bf16[128,512]{1,0:T(8,128)(2,1)S(1)}, bf16[64,512]{1,0:T(8,128)(2,1)S(1)}, bf16[64,512]{1,0:T(8,128)(2,1)S(1)}, bf16[64,512]{1,0:T(8,128)(2,1)S(1)}, bf16[64,512]{1,0:T(8,128)(2,1)S(1)}) custom-call(s32[1]{0:T(128)} %bitcast.own_ref, bf16[160,512]{1,0:T(8,128)(2,1)S(1)} %get-tuple-element.49.extended_ref.refs_0_, ...), custom_call_target="tpu_custom_call" | custom-call | flops 2000000000 | tf_op jit(solution)/shard_map/pallas_call | solution.py:581
  27.5 1.6 %collective-permute-start.15 = (bf16[64,512]{1,0:T(8,128)(2,1)S(1)}, bf16[64,512]{1,0:T(8,128)(2,1)S(1)}, u32[]{:S(2)}, u32[]{:S(2)}) collective-permute-start(bf16[64,512]{1,0:T(8,128)(2,1)S(1)} %get-tuple-element.70), channel_id=1, source_target_pairs={{0,4},{1,5},{2,6},{3,7},{4,0},{5,1},{6,2},{7,3},{8,12},{9,13},{10,... | collective-permute-start | bytes 196616 | tf_op jit(solution)/shard_map/ppermute | solution.py:69
  29.5 2.6 %collective-permute-done.12.refs_5_ = bf16[128,512]{1,0:T(8,128)(2,1)S(1)} collective-permute-done((bf16[128,512]{1,0:T(8,128)(2,1)S(1)}, bf16[128,512]{1,0:T(8,128)(2,1)S(1)}, u32[]{:S(2)}, u32[]{:S(2)}) %collective-permute-start.12) | collective-permute-done | bytes 131104 | tf_op jit(solution)/shard_map/ppermute | solution.py:69
  32.5 0.9 %collective-permute-start.9 = (bf16[64,512]{1,0:T(8,128)(2,1)S(1)}, bf16[64,512]{1,0:T(8,128)(2,1)S(1)}, u32[]{:S(2)}, u32[]{:S(2)}) collective-permute-start(bf16[64,512]{1,0:T(8,128)(2,1)S(1)} %get-tuple-element.70), channel_id=1, source_target_pairs={{0,5},{1,4},{2,7},{3,6},{4,1},{5,0},{6,3},{7,2},{8,13},{9,12},{10,... | collective-permute-start | bytes 196616 | tf_op jit(solution)/shard_map/ppermute | solution.py:69
  33.5 1.8 %collective-permute-start.10 = (bf16[64,512]{1,0:T(8,128)(2,1)S(1)}, bf16[64,512]{1,0:T(8,128)(2,1)S(1)}, u32[]{:S(2)}, u32[]{:S(2)}) collective-permute-start(bf16[64,512]{1,0:T(8,128)(2,1)S(1)} %get-tuple-element.71), channel_id=1, source_target_pairs={{0,7},{1,6},{2,5},{3,4},{4,3},{5,2},{6,1},{7,0},{8,15},{9,14},{10,... | collective-permute-start | bytes 196616 | tf_op jit(solution)/shard_map/ppermute | solution.py:69
  35.3 1.2 %collective-permute-start.7 = (bf16[64,512]{1,0:T(8,128)(2,1)S(1)}, bf16[64,512]{1,0:T(8,128)(2,1)S(1)}, u32[]{:S(2)}, u32[]{:S(2)}) collective-permute-start(bf16[64,512]{1,0:T(8,128)(2,1)S(1)} %get-tuple-element.68.refs_0_), channel_id=1, source_target_pairs={{0,1},{1,0},{2,3},{3,2},{4,5},{5,4},{6,7},{7,6},{8,9},{9,8},{10,11... | collective-permute-start | bytes 196616 | tf_op jit(solution)/shard_map/ppermute | solution.py:69
  36.5 1.9 %shard_map.145 = (bf16[128,512]{1,0:T(8,128)(2,1)S(1)}, bf16[128,512]{1,0:T(8,128)(2,1)S(1)}, bf16[128,512]{1,0:T(8,128)(2,1)S(1)}, bf16[128,512]{1,0:T(8,128)(2...) custom-call(s32[1]{0:T(128)} %bitcast.own_ref, s32[4]{0:T(128)S(1)} %pad_add_fusion.part_ref, ...), custom_call_target="tpu_custom_call" | custom-call | flops 2000000000 | tf_op jit(solution)/shard_map/pallas_call | solution.py:594
  38.4 2.3 %collective-permute-done.7.refs_0_ = bf16[64,512]{1,0:T(8,128)(2,1)S(1)} collective-permute-done((bf16[64,512]{1,0:T(8,128)(2,1)S(1)}, bf16[64,512]{1,0:T(8,128)(2,1)S(1)}, u32[]{:S(2)}, u32[]{:S(2)}) %collective-permute-start.7) | collective-permute-done | bytes 65568 | tf_op jit(solution)/shard_map/ppermute | solution.py:69
  40.7 1.6 %shard_map.146 = (bf16[3,64,512]{2,1,0:T(8,128)(2,1)S(1)}, bf16[1,64,512]{2,1,0:T(8,128)(2,1)S(1)}, bf16[1,64,512]{2,1,0:T(8,128)(2,1)S(1)}, f32[3,64,512]{2,1,0:T(8,128)S(1)}) custom-call(s32[1]{0:T(128)} %bitcast.own_ref, s32[4]{0:T(128)S(1)} %pad_add_fusion.part_ref, bf16[512,512]{1,0:T(8,128)(2,1)S(1)} %bitcast.27, bf16[512,512]{1,0:T(8,128)(2,1)S(1)} %bitcast.29, ...), custom_call_target="tpu_custom_call" | custom-call | flops 2000000000 | tf_op jit(solution)/shard_map/pallas_call | solution.py:594
  42.5 0.7 %collective-permute-start.18 = (bf16[128,512]{1,0:T(8,128)(2,1)S(1)}, bf16[128,512]{1,0:T(8,128)(2,1)S(1)}, u32[]{:S(2)}, u32[]{:S(2)}) collective-permute-start(bf16[128,512]{1,0:T(8,128)(2,1)S(1)} %get-tuple-element.83), channel_id=1, source_target_pairs={{0,4},{2,6},{4,0},{6,2},{1,5},{3,7},{5,1},{7,3},{8,12},{10,14},{12... | collective-permute-start | bytes 393224 | tf_op jit(solution)/shard_map/ppermute | solution.py:69
  43.2 1.1 %collective-permute-start.19 = (bf16[128,512]{1,0:T(8,128)(2,1)S(1)}, bf16[128,512]{1,0:T(8,128)(2,1)S(1)}, u32[]{:S(2)}, u32[]{:S(2)}) collective-permute-start(bf16[128,512]{1,0:T(8,128)(2,1)S(1)} %get-tuple-element.84), channel_id=1, source_target_pairs={{0,6},{2,4},{4,2},{6,0},{1,7},{3,5},{5,3},{7,1},{8,14},{10,12},{12... | collective-permute-start | bytes 393224 | tf_op jit(solution)/shard_map/ppermute | solution.py:69
  44.4 0.7 %collective-permute-start.21 = (bf16[1,64,512]{2,1,0:T(8,128)(2,1)S(1)}, bf16[1,64,512]{2,1,0:T(8,128)(2,1)S(1)}, u32[]{:S(2)}, u32[]{:S(2)}) collective-permute-start(bf16[1,64,512]{2,1,0:T(8,128)(2,1)S(1)} %get-tuple-element.90), channel_id=1, source_target_pairs={{0,16},{8,24},{16,0},{24,8},{1,17},{9,25},{17,1},{25,9},{2,18},{10... | collective-permute-start | bytes 196616 | tf_op jit(solution)/shard_map/ppermute | solution.py:69
  45.1 5.4 %collective-permute-done.20.near_ref.refs_0_ = bf16[3,64,512]{2,1,0:T(8,128)(2,1)S(1)} collective-permute-done((bf16[3,64,512]{2,1,0:T(8,128)(2,1)S(1)}, bf16[3,64,512]{2,1,0:T(8,128)(2,1)S(1)}, u32[]{:S(2)}, u32[]{:S(2)}) %collective-permute-start.20) | collective-permute-done | bytes 196640 | tf_op jit(solution)/shard_map/ppermute | solution.py:69
  50.6 1.1 %collective-permute-start.23 = (bf16[1,64,512]{2,1,0:T(8,128)(2,1)S(1)}, bf16[1,64,512]{2,1,0:T(8,128)(2,1)S(1)}, u32[]{:S(2)}, u32[]{:S(2)}) collective-permute-start(bf16[1,64,512]{2,1,0:T(8,128)(2,1)S(1)} %shard_map.148), channel_id=1, source_target_pairs={{0,16},{8,24},{16,0},{24,8},{1,17},{9,25},{17,1},{25,9},{2,18},{10... | collective-permute-start | bytes 196616 | tf_op jit(solution)/shard_map/ppermute | solution.py:629
  51.7 1.4 %shard_map.147 = (bf16[128,512]{1,0:T(8,128)(2,1)}, bf16[128,512]{1,0:T(8,128)(2,1)}) custom-call(s32[1]{0:T(128)} %bitcast.own_ref, bf16[128,512]{1,0:T(8,128)(2,1)S(1)} %get-tuple-element.80.mixed_ref, bf16[160,512]{1,0:T(8,128)(2,1)S(1)} %get-tuple-element.49.extended_ref.refs_0_, bf16[128,512]{1,0:T(8,128)(2,1)S(1)} %get-tuple-element.81.refs_0_, ...), custom_call_target="tpu_custom_call" | custom-call | flops 1500000000 | tf_op jit(solution)/shard_map/pallas_call | solution.py:635
  53.1 3.5 %collective-permute-done.22.refs_2_ = bf16[1,64,512]{2,1,0:T(8,128)(2,1)S(1)} collective-permute-done((bf16[1,64,512]{2,1,0:T(8,128)(2,1)S(1)}, bf16[1,64,512]{2,1,0:T(8,128)(2,1)S(1)}, u32[]{:S(2)}, u32[]{:S(2)}) %collective-permute-start.22) | collective-permute-done | bytes 65568 | tf_op jit(solution)/shard_map/ppermute | solution.py:69
  56.6 0.7 %shard_map.149 = (f32[64,512]{1,0:T(8,128)}, f32[64,512]{1,0:T(8,128)}) custom-call(f32[3,64,512]{2,1,0:T(8,128)S(1)} %get-tuple-element.88.kept_ref, bf16[3,64,512]{2,1,0:T(8,128)(2,1)S(1)} %collective-permute-done.20.near_ref.refs_0_, bf16[1,64,512]{2,1,0:T(8,128)(2,1)S(1)} %collective-permute-done.21.refs_1_, ...), custom_call_target="tpu_custom_call" | custom-call | flops 500000000 | tf_op jit(solution)/shard_map/pallas_call | solution.py:642
  (56 shorter events, 3.5 us)
Async XLA Ops:
  0.6 12.8 %collective-permute-start.4 = (bf16[128,512]{1,0:T(8,128)(2,1)}, bf16[128,512]{1,0:T(8,128)(2,1)S(1)}, u32[]{:S(2)}, u32[]{:S(2)}) collective-permute-start(bf16[128,512]{1,0:T(8,128)(2,1)} %bitcast.37), channel_id=1, source_target_pairs={{0,1},{1,0},{2,3},{3,2},{4,5},{5,4},{6,7},{7,6},{8,9},{9,8},{10,11... | collective-permute-start | bytes 393224 | tf_op jit(solution)/shard_map/ppermute | solution.py:69
  3.6 8.4 %collective-permute-start = (bf16[128,512]{1,0:T(8,128)(2,1)}, bf16[128,512]{1,0:T(8,128)(2,1)S(1)}, u32[]{:S(2)}, u32[]{:S(2)}) collective-permute-start(bf16[128,512]{1,0:T(8,128)(2,1)} %bitcast.31), channel_id=1, source_target_pairs={{0,8},{8,16},{16,24},{24,0},{1,9},{9,17},{17,25},{25,1},{2,10},{10... | collective-permute-start | bytes 393224 | tf_op jit(solution)/shard_map/ppermute | solution.py:502
  5.2 8.3 %collective-permute-start.2 = (bf16[128,512]{1,0:T(8,128)(2,1)}, bf16[128,512]{1,0:T(8,128)(2,1)S(1)}, u32[]{:S(2)}, u32[]{:S(2)}) collective-permute-start(bf16[128,512]{1,0:T(8,128)(2,1)} %bitcast.34), channel_id=1, source_target_pairs={{0,8},{8,16},{16,24},{24,0},{1,9},{9,17},{17,25},{25,1},{2,10},{10... | collective-permute-start | bytes 393224 | tf_op jit(solution)/shard_map/ppermute | solution.py:502
  7.5 0.9 %copy-start.3 = (bf16[1,128,512]{2,1,0:T(8,128)(2,1)S(1)}, bf16[1,128,512]{2,1,0:T(8,128)(2,1)}, u32[]{:S(2)}) copy-start(bf16[1,128,512]{2,1,0:T(8,128)(2,1)} %param.21) | copy-start | bytes 393220
  8.4 1.3 %copy-start.4 = (bf16[1,128,512]{2,1,0:T(8,128)(2,1)S(1)}, bf16[1,128,512]{2,1,0:T(8,128)(2,1)}, u32[]{:S(2)}) copy-start(bf16[1,128,512]{2,1,0:T(8,128)(2,1)} %param.12) | copy-start | bytes 393220
  8.4 1.3 %copy-start.5 = (bf16[1,128,512]{2,1,0:T(8,128)(2,1)S(1)}, bf16[1,128,512]{2,1,0:T(8,128)(2,1)}, u32[]{:S(2)}) copy-start(bf16[1,128,512]{2,1,0:T(8,128)(2,1)} %param.13) | copy-start | bytes 393220
  8.4 1.3 %copy-start.6 = (bf16[1,128,512]{2,1,0:T(8,128)(2,1)S(1)}, bf16[1,128,512]{2,1,0:T(8,128)(2,1)}, u32[]{:S(2)}) copy-start(bf16[1,128,512]{2,1,0:T(8,128)(2,1)} %param.11) | copy-start | bytes 393220
  9.0 12.5 %collective-permute-start.5 = (bf16[160,512]{1,0:T(8,128)(2,1)S(1)}, bf16[160,512]{1,0:T(8,128)(2,1)S(1)}, u32[]{:S(2)}, u32[]{:S(2)}) collective-permute-start(bf16[160,512]{1,0:T(8,128)(2,1)S(1)} %get-tuple-element.49.extended_ref.refs_0_), channel_id=1, source_target_pairs={{0,1},{1,0},{2,3},{3,2},{4,5},{5,4},{6,7},{7,6},{8,9},{9,8},{10,11... | collective-permute-start | bytes 491528 | tf_op jit(solution)/shard_map/ppermute | solution.py:69
  12.1 8.7 %collective-permute-start.1 = (bf16[128,512]{1,0:T(8,128)(2,1)S(1)}, bf16[128,512]{1,0:T(8,128)(2,1)S(1)}, u32[]{:S(2)}, u32[]{:S(2)}) collective-permute-start(bf16[128,512]{1,0:T(8,128)(2,1)S(1)} %collective-permute-done.refs_4_), channel_id=1, source_target_pairs={{0,8},{8,16},{16,24},{24,0},{1,9},{9,17},{17,25},{25,1},{2,10},{10... | collective-permute-start | bytes 393224 | tf_op jit(solution)/shard_map/ppermute | solution.py:502
  13.5 7.3 %collective-permute-start.3 = (bf16[128,512]{1,0:T(8,128)(2,1)S(1)}, bf16[128,512]{1,0:T(8,128)(2,1)S(1)}, u32[]{:S(2)}, u32[]{:S(2)}) collective-permute-start(bf16[128,512]{1,0:T(8,128)(2,1)S(1)} %collective-permute-done.2.refs_5_), channel_id=1, source_target_pairs={{0,8},{8,16},{16,24},{24,0},{1,9},{9,17},{17,25},{25,1},{2,10},{10... | collective-permute-start | bytes 393224 | tf_op jit(solution)/shard_map/ppermute | solution.py:502
  21.6 5.3 %collective-permute-start.6 = (bf16[592,128]{1,0:T(8,128)(2,1)S(1)}, bf16[592,128]{1,0:T(8,128)(2,1)S(1)}, u32[]{:S(2)}, u32[]{:S(2)}) collective-permute-start(bf16[592,128]{1,0:T(8,128)(2,1)S(1)} %shard_map.142), channel_id=1, source_target_pairs={{0,1},{1,0},{2,3},{3,2},{4,5},{5,4},{6,7},{7,6},{8,9},{9,8},{10,11... | collective-permute-start | bytes 454664 | tf_op jit(solution)/shard_map/ppermute | solution.py:69
  23.3 5.8 %collective-permute-start.11 = (bf16[128,512]{1,0:T(8,128)(2,1)S(1)}, bf16[128,512]{1,0:T(8,128)(2,1)S(1)}, u32[]{:S(2)}, u32[]{:S(2)}) collective-permute-start(bf16[128,512]{1,0:T(8,128)(2,1)S(1)} %get-tuple-element.73), channel_id=1, source_target_pairs={{0,6},{2,4},{4,2},{6,0},{1,7},{3,5},{5,3},{7,1},{8,14},{10,12},{12... | collective-permute-start | bytes 393224 | tf_op jit(solution)/shard_map/ppermute | solution.py:69
  23.4 8.7 %collective-permute-start.12 = (bf16[128,512]{1,0:T(8,128)(2,1)S(1)}, bf16[128,512]{1,0:T(8,128)(2,1)S(1)}, u32[]{:S(2)}, u32[]{:S(2)}) collective-permute-start(bf16[128,512]{1,0:T(8,128)(2,1)S(1)} %get-tuple-element.74), channel_id=1, source_target_pairs={{0,4},{2,6},{4,0},{6,2},{1,5},{3,7},{5,1},{7,3},{8,12},{10,14},{12... | collective-permute-start | bytes 393224 | tf_op jit(solution)/shard_map/ppermute | solution.py:69
  25.0 7.5 %collective-permute-start.13 = (bf16[128,512]{1,0:T(8,128)(2,1)S(1)}, bf16[128,512]{1,0:T(8,128)(2,1)S(1)}, u32[]{:S(2)}, u32[]{:S(2)}) collective-permute-start(bf16[128,512]{1,0:T(8,128)(2,1)S(1)} %get-tuple-element.75), channel_id=1, source_target_pairs={{0,2},{2,0},{4,6},{6,4},{1,3},{3,1},{5,7},{7,5},{8,10},{10,8},{12,... | collective-permute-start | bytes 393224 | tf_op jit(solution)/shard_map/ppermute | solution.py:69
  25.3 1.6 %copy-start = (bf16[512,512]{1,0:T(8,128)(2,1)S(1)}, bf16[512,512]{1,0:T(8,128)(2,1)}, u32[]{:S(2)}) copy-start(bf16[512,512]{1,0:T(8,128)(2,1)} %proj_ref.1) | copy-start | bytes 1572868
  25.3 1.6 %copy-start.7 = (bf16[1,128,512]{2,1,0:T(8,128)(2,1)S(1)}, bf16[1,128,512]{2,1,0:T(8,128)(2,1)}, u32[]{:S(2)}) copy-start(bf16[1,128,512]{2,1,0:T(8,128)(2,1)} %param.15) | copy-start | bytes 393220
  26.8 9.7 %copy-start.1 = (bf16[1,512,512]{2,1,0:T(8,128)(2,1)S(1)}, bf16[1,512,512]{2,1,0:T(8,128)(2,1)}, u32[]{:S(2)}) copy-start(bf16[1,512,512]{2,1,0:T(8,128)(2,1)} %param.19) | copy-start | bytes 1572868
  26.8 9.7 %copy-start.2 = (bf16[1,512,512]{2,1,0:T(8,128)(2,1)S(1)}, bf16[1,512,512]{2,1,0:T(8,128)(2,1)}, u32[]{:S(2)}) copy-start(bf16[1,512,512]{2,1,0:T(8,128)(2,1)} %param.20) | copy-start | bytes 1572868
  27.4 6.0 %collective-permute-start.14 = (bf16[64,512]{1,0:T(8,128)(2,1)S(1)}, bf16[64,512]{1,0:T(8,128)(2,1)S(1)}, u32[]{:S(2)}, u32[]{:S(2)}) collective-permute-start(bf16[64,512]{1,0:T(8,128)(2,1)S(1)} %get-tuple-element.69), channel_id=1, source_target_pairs={{0,2},{1,3},{2,0},{3,1},{4,6},{5,7},{6,4},{7,5},{8,10},{9,11},{10,... | collective-permute-start | bytes 196616 | tf_op jit(solution)/shard_map/ppermute | solution.py:69
  27.5 7.8 %collective-permute-start.15 = (bf16[64,512]{1,0:T(8,128)(2,1)S(1)}, bf16[64,512]{1,0:T(8,128)(2,1)S(1)}, u32[]{:S(2)}, u32[]{:S(2)}) collective-permute-start(bf16[64,512]{1,0:T(8,128)(2,1)S(1)} %get-tuple-element.70), channel_id=1, source_target_pairs={{0,4},{1,5},{2,6},{3,7},{4,0},{5,1},{6,2},{7,3},{8,12},{9,13},{10,... | collective-permute-start | bytes 196616 | tf_op jit(solution)/shard_map/ppermute | solution.py:69
  29.1 7.4 %collective-permute-start.16 = (bf16[64,512]{1,0:T(8,128)(2,1)S(1)}, bf16[64,512]{1,0:T(8,128)(2,1)S(1)}, u32[]{:S(2)}, u32[]{:S(2)}) collective-permute-start(bf16[64,512]{1,0:T(8,128)(2,1)S(1)} %get-tuple-element.71), channel_id=1, source_target_pairs={{0,6},{1,7},{2,4},{3,5},{4,2},{5,3},{6,0},{7,1},{8,14},{9,15},{10,... | collective-permute-start | bytes 196616 | tf_op jit(solution)/shard_map/ppermute | solution.py:69
  32.1 8.6 %collective-permute-start.8 = (bf16[64,512]{1,0:T(8,128)(2,1)S(1)}, bf16[64,512]{1,0:T(8,128)(2,1)S(1)}, u32[]{:S(2)}, u32[]{:S(2)}) collective-permute-start(bf16[64,512]{1,0:T(8,128)(2,1)S(1)} %get-tuple-element.69), channel_id=1, source_target_pairs={{0,3},{1,2},{2,1},{3,0},{4,7},{5,6},{6,5},{7,4},{8,11},{9,10},{10,... | collective-permute-start | bytes 196616 | tf_op jit(solution)/shard_map/ppermute | solution.py:69
  32.5 8.2 %collective-permute-start.9 = (bf16[64,512]{1,0:T(8,128)(2,1)S(1)}, bf16[64,512]{1,0:T(8,128)(2,1)S(1)}, u32[]{:S(2)}, u32[]{:S(2)}) collective-permute-start(bf16[64,512]{1,0:T(8,128)(2,1)S(1)} %get-tuple-element.70), channel_id=1, source_target_pairs={{0,5},{1,4},{2,7},{3,6},{4,1},{5,0},{6,3},{7,2},{8,13},{9,12},{10,... | collective-permute-start | bytes 196616 | tf_op jit(solution)/shard_map/ppermute | solution.py:69
  33.5 7.2 %collective-permute-start.10 = (bf16[64,512]{1,0:T(8,128)(2,1)S(1)}, bf16[64,512]{1,0:T(8,128)(2,1)S(1)}, u32[]{:S(2)}, u32[]{:S(2)}) collective-permute-start(bf16[64,512]{1,0:T(8,128)(2,1)S(1)} %get-tuple-element.71), channel_id=1, source_target_pairs={{0,7},{1,6},{2,5},{3,4},{4,3},{5,2},{6,1},{7,0},{8,15},{9,14},{10,... | collective-permute-start | bytes 196616 | tf_op jit(solution)/shard_map/ppermute | solution.py:69
  35.3 5.4 %collective-permute-start.7 = (bf16[64,512]{1,0:T(8,128)(2,1)S(1)}, bf16[64,512]{1,0:T(8,128)(2,1)S(1)}, u32[]{:S(2)}, u32[]{:S(2)}) collective-permute-start(bf16[64,512]{1,0:T(8,128)(2,1)S(1)} %get-tuple-element.68.refs_0_), channel_id=1, source_target_pairs={{0,1},{1,0},{2,3},{3,2},{4,5},{5,4},{6,7},{7,6},{8,9},{9,8},{10,11... | collective-permute-start | bytes 196616 | tf_op jit(solution)/shard_map/ppermute | solution.py:69
  42.3 8.2 %collective-permute-start.20 = (bf16[3,64,512]{2,1,0:T(8,128)(2,1)S(1)}, bf16[3,64,512]{2,1,0:T(8,128)(2,1)S(1)}, u32[]{:S(2)}, u32[]{:S(2)}) collective-permute-start(bf16[3,64,512]{2,1,0:T(8,128)(2,1)S(1)} %get-tuple-element.89), channel_id=1, source_target_pairs={{0,8},{8,0},{16,24},{24,16},{1,9},{9,1},{17,25},{25,17},{2,10},{10... | collective-permute-start | bytes 589832 | tf_op jit(solution)/shard_map/ppermute | solution.py:69
  42.4 8.2 %collective-permute-start.17 = (bf16[128,512]{1,0:T(8,128)(2,1)S(1)}, bf16[128,512]{1,0:T(8,128)(2,1)S(1)}, u32[]{:S(2)}, u32[]{:S(2)}) collective-permute-start(bf16[128,512]{1,0:T(8,128)(2,1)S(1)} %get-tuple-element.82), channel_id=1, source_target_pairs={{0,2},{2,0},{4,6},{6,4},{1,3},{3,1},{5,7},{7,5},{8,10},{10,8},{12,... | collective-permute-start | bytes 393224 | tf_op jit(solution)/shard_map/ppermute | solution.py:69
  42.5 9.2 %collective-permute-start.18 = (bf16[128,512]{1,0:T(8,128)(2,1)S(1)}, bf16[128,512]{1,0:T(8,128)(2,1)S(1)}, u32[]{:S(2)}, u32[]{:S(2)}) collective-permute-start(bf16[128,512]{1,0:T(8,128)(2,1)S(1)} %get-tuple-element.83), channel_id=1, source_target_pairs={{0,4},{2,6},{4,0},{6,2},{1,5},{3,7},{5,1},{7,3},{8,12},{10,14},{12... | collective-permute-start | bytes 393224 | tf_op jit(solution)/shard_map/ppermute | solution.py:69
  43.2 8.5 %collective-permute-start.19 = (bf16[128,512]{1,0:T(8,128)(2,1)S(1)}, bf16[128,512]{1,0:T(8,128)(2,1)S(1)}, u32[]{:S(2)}, u32[]{:S(2)}) collective-permute-start(bf16[128,512]{1,0:T(8,128)(2,1)S(1)} %get-tuple-element.84), channel_id=1, source_target_pairs={{0,6},{2,4},{4,2},{6,0},{1,7},{3,5},{5,3},{7,1},{8,14},{10,12},{12... | collective-permute-start | bytes 393224 | tf_op jit(solution)/shard_map/ppermute | solution.py:69
  44.4 8.8 %collective-permute-start.21 = (bf16[1,64,512]{2,1,0:T(8,128)(2,1)S(1)}, bf16[1,64,512]{2,1,0:T(8,128)(2,1)S(1)}, u32[]{:S(2)}, u32[]{:S(2)}) collective-permute-start(bf16[1,64,512]{2,1,0:T(8,128)(2,1)S(1)} %get-tuple-element.90), channel_id=1, source_target_pairs={{0,16},{8,24},{16,0},{24,8},{1,17},{9,25},{17,1},{25,9},{2,18},{10... | collective-permute-start | bytes 196616 | tf_op jit(solution)/shard_map/ppermute | solution.py:69
  50.5 6.1 %collective-permute-start.22 = (bf16[1,64,512]{2,1,0:T(8,128)(2,1)S(1)}, bf16[1,64,512]{2,1,0:T(8,128)(2,1)S(1)}, u32[]{:S(2)}, u32[]{:S(2)}) collective-permute-start(bf16[1,64,512]{2,1,0:T(8,128)(2,1)S(1)} %get-tuple-element.91), channel_id=1, source_target_pairs={{0,24},{8,16},{16,8},{24,0},{1,25},{9,17},{17,9},{25,1},{2,26},{10... | collective-permute-start | bytes 196616 | tf_op jit(solution)/shard_map/ppermute | solution.py:69
  50.6 6.0 %collective-permute-start.23 = (bf16[1,64,512]{2,1,0:T(8,128)(2,1)S(1)}, bf16[1,64,512]{2,1,0:T(8,128)(2,1)S(1)}, u32[]{:S(2)}, u32[]{:S(2)}) collective-permute-start(bf16[1,64,512]{2,1,0:T(8,128)(2,1)S(1)} %shard_map.148), channel_id=1, source_target_pairs={{0,16},{8,24},{16,0},{24,8},{1,17},{9,25},{17,1},{25,9},{2,18},{10... | collective-permute-start | bytes 196616 | tf_op jit(solution)/shard_map/ppermute | solution.py:629
  (3 other events, 2.0 us)

commit v13 on v12

--- a/solution.py
+++ b/solution.py
@@ -303,16 +303,6 @@
         sent_ref[...] = rows[k * hot_capacity : (k + 1) * hot_capacity]
 
 
-def grad_plan(parts):
-    if parts == 4:
-        return [[(0, 0), (1, 0), (1, 2)], [(0, 1), (1, 1), (1, 3)], [(0, 2)], [(0, 3)]]
-    return [[(0, 0), (1, 0)]] + [[(0, k), (1, k)] for k in range(1, parts)]
-
-
-def pair_kernel(kept_ref, near_ref, sent_ref):
-    sent_ref[0] = (kept_ref[2] + near_ref[2].astype(jnp.float32)).astype(jnp.bfloat16)
-
-
 def expert_kernel(
     reps,
     rep_list,
@@ -330,7 +320,7 @@
     row_count, grad_count = counts
     row_refs, refs = refs[:row_count], refs[row_count:]
     per_rep = row_count // len(rep_list)
-    grad_refs, refs = refs[:grad_count][::-1], refs[grad_count:]
+    grad_refs, refs = refs[:grad_count], refs[grad_count:]
     own_rows = rep_list[0] == 0
     held_ref, refs = refs[-1], refs[:-1]
     if own_rows:
@@ -389,10 +379,10 @@
         return
     up_term = up_term + up_old[...]
     down_term = down_term + down_old[...]
-    for ref, entries in zip((kept_ref, *term_refs), grad_plan(parts)):
-        for place, (kind, k) in enumerate(entries):
-            term = (up_term, down_term)[kind][k * strip : (k + 1) * strip]
-            ref[place] = term.astype(ref.dtype)
+    for k, ref in enumerate((kept_ref, *term_refs)):
+        rows = slice(k * strip, (k + 1) * strip)
+        ref[0] = up_term[rows].astype(ref.dtype)
+        ref[1] = down_term[rows].astype(ref.dtype)
 
 
 def finish_kernel(
@@ -430,13 +420,12 @@
     grad_mixed_ref[...] = (grad_f + input_grad).astype(jnp.bfloat16)
 
 
-def sum_kernel(plan, kept_ref, *refs):
-    term_refs, out_refs = refs[:-2], refs[-2:]
-    totals = [kept_ref[0], kept_ref[1]]
-    for kinds, ref in zip(plan, term_refs):
-        for place, kind in enumerate(kinds):
-            totals[kind] = totals[kind] + ref[place].astype(jnp.float32)
-    for total, out_ref in zip(totals, out_refs):
+def sum_kernel(kept_ref, *refs):
+    term_refs, (up_ref, down_ref) = refs[:-2], refs[-2:]
+    for kind, out_ref in enumerate((up_ref, down_ref)):
+        total = kept_ref[kind]
+        for ref in term_refs:
+            total = total + ref[kind].astype(jnp.float32)
         out_ref[...] = total
 
 
@@ -576,7 +565,7 @@
         [shape((rep_count * hot_capacity, width))] * expert_count,
         [SMEM] + [VMEM] * rep_count,
     )(own, *extendeds)
-    got_grads = merged(experts.exchange(sent_grads), MOST_PERMUTES)[::-1]
+    got_grads = merged(experts.exchange(sent_grads), MOST_PERMUTES)
 
     mixed, *sent_rows = call(
         functools.partial(mix_kernel, expert_count, hot_capacity),
@@ -619,19 +608,11 @@
     *terms, kept = expert_call(
         tuple(range(1, rep_count)),
         got_more,
-        [shape((len(entries), strip, hidden)) for entries in grad_plan(seq_count)[1:]]
-        + [shape((len(grad_plan(seq_count)[0]), strip, hidden), jnp.float32)],
+        [shape((2, strip, hidden))] * (seq_count - 1)
+        + [shape((2, strip, hidden), jnp.float32)],
         [up_acc, down_acc],
     )
-    if seq_count == 4:
-        near, *direct = parts.exchange([None] + terms)[1:]
-        crossing = call(pair_kernel, shape((1, strip, hidden)), [VMEM, VMEM])(kept, near)
-        crossed = lax.ppermute(crossing, "seq", [(i, parts.target(i, 2)) for i in range(4)])
-        got_terms = [near, *direct, crossed]
-        plan = ((0, 1), (0,), (0,), (1,))
-    else:
-        got_terms = parts.exchange([None] + terms)[1:]
-        plan = ((0, 1),) * len(got_terms)
+    got_terms = parts.exchange([None] + terms)[1:]
     layer_out, grad_mixed = call(
         functools.partial(finish_kernel, hot_capacity, expert_count),
         [shape((tok, width)), shape((tok, width))],
@@ -640,10 +621,10 @@
     )(own, mixed, extended, *got_back)
     kept, layer_out = lax.optimization_barrier((kept, layer_out))
     share_in, share_out = call(
-        functools.partial(sum_kernel, plan),
+        sum_kernel,
         [shape((strip, hidden), jnp.float32), shape((strip, width), jnp.float32)],
-        [VMEM] * (1 + len(got_terms)),
-    )(kept, *got_terms)
+        [VMEM] * seq_count,
+    )(kept, *got_terms[::-1])
     return (layer_out[None], grad_mixed[None], share_in[None], share_out[None])
 
 

time: 57.5 us -> 56.5 us (0.983)
  waiting for transfers between devices: 20.6 us -> 15.3 us
  starting transfers between devices: 21.3 us -> 25.7 us
    ppermute x19, waiting for transfers between devices: 14.7 us -> 10.1 us  [exchange(): got[k] = lax.ppermute(chunks[k], self.axes, pairs)]
    ppermute x19, starting transfers between devices: 15.8 us -> 19.4 us  [exchange(): got[k] = lax.ppermute(chunks[k], self.axes, pairs)]
    ppermute x4, starting transfers between devices: 4.4 us -> 6.31 us  [forward(): lax.ppermute(array, 'seq', [(i, (i + 1) % seq_count) for i in range(seq_c...]
    ppermute x1 -> x0, starting transfers between devices: 1.13 us -> none  [local(): lax.ppermute(crossing, 'seq', [(i, parts.target(i, 2)) for i in range(4)])]
    ppermute x4, waiting for transfers between devices: 5.86 us -> 5.15 us  [forward(): lax.ppermute(array, 'seq', [(i, (i + 1) % seq_count) for i in range(seq_c...]
  transfers between devices with their start and end apart: 24 -> 23, of which waited for: 8 -> 9; matrix products, arithmetic and copies ran while one was open for 1% -> 1% of each run, Pallas kernels for 18% -> 21%
where the time goes in v13:
time: 56.5 us; the launch traced here: 56.3 us
  starting transfers between devices  25.7 us (45%)
  waiting for transfers between devices  15.3 us (27%)
  Pallas kernels  12.5 us (22%)
  local copies, waits for them, and re-layouts  1.69 us (3%)
  between operations  0.78 us (1%)
    ppermute x19, starting transfers between devices, exchange(): got[k] = lax.ppermute(chunks[k], self.axes, pairs)  19.4 us
    ppermute x19, waiting for transfers between devices, exchange(): got[k] = lax.ppermute(chunks[k], self.axes, pairs)  10.1 us
    ppermute x4, starting transfers between devices, forward(): lax.ppermute(array, 'seq', [(i, (i + 1) % seq_count) for i in range(seq_c...  6.31 us
    pallas_call x4, Pallas kernels, attend(): call(functools.partial(attend_kernel, plan, rep_count, len(pairs), packed...  5.19 us
    ppermute x4, waiting for transfers between devices, forward(): lax.ppermute(array, 'seq', [(i, (i + 1) % seq_count) for i in range(seq_c...  5.15 us
    pallas_call x2, Pallas kernels, expert_call(): call(functools.partial(expert_kernel, rep_count, rep_list, expert_count,...  3.47 us
    unnamed x22, local copies, waits for them, and re-layouts  1.6 us
    pallas_call x1, Pallas kernels, local(): call(functools.partial(finish_kernel, hot_capacity, expert_count), [shape...  1.42 us
  transfers between devices with their start and end apart: 23, of which 9 were waited for; matrix products, arithmetic and copies ran while one was open for 1% of the time, Pallas kernels for 21%

profile of v13, /device:TPU:0, one launch (start us, length us, event | category | flops | bytes accessed | tf_op | source)
XLA Modules:
  0.0 56.3 jit_solution(15762718159813199745)
XLA Ops:
  0.6 3.1 %collective-permute-start = (bf16[128,512]{1,0:T(8,128)(2,1)}, bf16[128,512]{1,0:T(8,128)(2,1)S(1)}, u32[]{:S(2)}, u32[]{:S(2)}) collective-permute-start(bf16[128,512]{1,0:T(8,128)(2,1)} %bitcast.31), channel_id=1, source_target_pairs={{0,8},{8,16},{16,24},{24,0},{1,9},{9,17},{17,25},{25,1},{2,10},{10... | collective-permute-start | bytes 393224 | tf_op jit(solution)/shard_map/ppermute | solution.py:491
  3.7 1.5 %collective-permute-start.4 = (bf16[128,512]{1,0:T(8,128)(2,1)}, bf16[128,512]{1,0:T(8,128)(2,1)S(1)}, u32[]{:S(2)}, u32[]{:S(2)}) collective-permute-start(bf16[128,512]{1,0:T(8,128)(2,1)} %bitcast.37), channel_id=1, source_target_pairs={{0,1},{1,0},{2,3},{3,2},{4,5},{5,4},{6,7},{7,6},{8,9},{9,8},{10,11... | collective-permute-start | bytes 393224 | tf_op jit(solution)/shard_map/ppermute | solution.py:69
  5.2 1.6 %collective-permute-start.2 = (bf16[128,512]{1,0:T(8,128)(2,1)}, bf16[128,512]{1,0:T(8,128)(2,1)S(1)}, u32[]{:S(2)}, u32[]{:S(2)}) collective-permute-start(bf16[128,512]{1,0:T(8,128)(2,1)} %bitcast.34), channel_id=1, source_target_pairs={{0,8},{8,16},{16,24},{24,0},{1,9},{9,17},{17,25},{25,1},{2,10},{10... | collective-permute-start | bytes 393224 | tf_op jit(solution)/shard_map/ppermute | solution.py:491
  6.9 0.6 %copy-done.8 = bf16[512,4]{0,1:T(4,128)(2,1)S(1)} copy-done((bf16[512,4]{0,1:T(4,128)(2,1)S(1)}, bf16[512,4]{0,1:T(4,128)(2,1)}, u32[]{:S(2)}) %copy-start.8) | copy-done | bytes 4120
  7.5 0.9 %copy-done.3 = bf16[1,128,512]{2,1,0:T(8,128)(2,1)S(1)} copy-done((bf16[1,128,512]{2,1,0:T(8,128)(2,1)S(1)}, bf16[1,128,512]{2,1,0:T(8,128)(2,1)}, u32[]{:S(2)}) %copy-start.3) | copy-done | bytes 131096
  8.4 0.6 %shard_map.138 = (bf16[160,512]{1,0:T(8,128)(2,1)S(1)}, s32[2,128]{1,0:T(2,128)S(1)}) custom-call(s32[2]{0:T(128)S(1)} %pad_add_fusion.1.ranks_ref, s32[1,8]{1,0:T(1,128)S(1)} %copy-done.9, s32[1,128]{1,0:T(1,128)S(1)} %bitcast.43, bf16[4,512]{1,0:T(4,128)(2,1)S(1)} %bitcast.42, bf16[128,512]{1,0:T(8,128)(2,1)S(1)} %bitcast.30), custom_call_target="tpu_custom_call" | custom-call | flops 500000000 | tf_op jit(solution)/shard_map/pallas_call | solution.py:513
  9.0 0.6 %collective-permute-start.5 = (bf16[160,512]{1,0:T(8,128)(2,1)S(1)}, bf16[160,512]{1,0:T(8,128)(2,1)S(1)}, u32[]{:S(2)}, u32[]{:S(2)}) collective-permute-start(bf16[160,512]{1,0:T(8,128)(2,1)S(1)} %get-tuple-element.49.extended_ref.refs_0_), channel_id=1, source_target_pairs={{0,1},{1,0},{2,3},{3,2},{4,5},{5,4},{6,7},{7,6},{8,9},{9,8},{10,11... | collective-permute-start | bytes 491528 | tf_op jit(solution)/shard_map/ppermute | solution.py:69
  9.7 1.7 %shard_map.139 = (f32[16,128]{1,0:T(8,128)S(1)}, f32[16,128]{1,0:T(8,128)S(1)}, f32[512,128]{1,0:T(8,128)S(1)}) custom-call(s32[3]{0:T(128)S(1)} %pad_add_fusion.4.ids_ref, s32[2,128]{1,0:T(2,128)S(1)} %get-tuple-element.50.begin_ref, bf16[128,512]{1,0:T(8,128)(2,1)S(1)} %bitcast.38, bf16[128,512]{1,0:T(8,128)(2,1)S(1)} %bitcast.32, ...), custom_call_target="tpu_custom_call" | custom-call | flops 2000000000 | tf_op jit(solution)/shard_map/pallas_call | solution.py:530
  11.7 1.6 %collective-permute-start.1 = (bf16[128,512]{1,0:T(8,128)(2,1)S(1)}, bf16[128,512]{1,0:T(8,128)(2,1)S(1)}, u32[]{:S(2)}, u32[]{:S(2)}) collective-permute-start(bf16[128,512]{1,0:T(8,128)(2,1)S(1)} %collective-permute-done.refs_4_), channel_id=1, source_target_pairs={{0,8},{8,16},{16,24},{24,0},{1,9},{9,17},{17,25},{25,1},{2,10},{10... | collective-permute-start | bytes 393224 | tf_op jit(solution)/shard_map/ppermute | solution.py:491
  13.4 1.9 %shard_map.140 = (f32[16,128]{1,0:T(8,128)S(1)}, f32[16,128]{1,0:T(8,128)S(1)}, f32[512,128]{1,0:T(8,128)S(1)}, f32[16,128]{1,0:T(8,128)S(1)}, f32[16,128]{1,0:T(8,128)S(1)}, /*index=5*/f32[512,128]{1,0:T(8,128)S(1)}) custom-call(s32[5]{0:T(128)S(1)} %stack.81.ids_ref, s32[2,128]{1,0:T(2,128)S(1)} %get-tuple-element.50.begin_ref, ...), custom_call_target="tpu_custom_call" | custom-call | flops 4000000000 | tf_op jit(solution)/shard_map/pallas_call | solution.py:530
  15.3 3.7 %collective-permute-done.1.refs_1_ = bf16[128,512]{1,0:T(8,128)(2,1)S(1)} collective-permute-done((bf16[128,512]{1,0:T(8,128)(2,1)S(1)}, bf16[128,512]{1,0:T(8,128)(2,1)S(1)}, u32[]{:S(2)}, u32[]{:S(2)}) %collective-permute-start.1) | collective-permute-done | bytes 131104 | tf_op jit(solution)/shard_map/ppermute | solution.py:491
  19.1 1.4 %collective-permute-done.3.refs_2_ = bf16[128,512]{1,0:T(8,128)(2,1)S(1)} collective-permute-done((bf16[128,512]{1,0:T(8,128)(2,1)S(1)}, bf16[128,512]{1,0:T(8,128)(2,1)S(1)}, u32[]{:S(2)}, u32[]{:S(2)}) %collective-permute-start.3) | collective-permute-done | bytes 131104 | tf_op jit(solution)/shard_map/ppermute | solution.py:491
  20.5 0.8 %shard_map.142 = bf16[592,128]{1,0:T(8,128)(2,1)S(1)} custom-call(s32[3]{0:T(128)S(1)} %pad_add_fusion.5.ids_ref, s32[2,128]{1,0:T(2,128)S(1)} %get-tuple-element.50.begin_ref, bf16[128,512]{1,0:T(8,128)(2,1)S(1)} %collective-permute-done.4.refs_1_.refs_0_, bf16[128,512]{1,0:T(8,128)(2,1)S(1)} %collective-permute-done.1.refs_1_, ...), custom_call_target="tpu_custom_call" | custom-call | flops 1500000000 | tf_op jit(solution)/shard_map/pallas_call | solution.py:530
  21.3 1.5 %collective-permute-start.6 = (bf16[592,128]{1,0:T(8,128)(2,1)S(1)}, bf16[592,128]{1,0:T(8,128)(2,1)S(1)}, u32[]{:S(2)}, u32[]{:S(2)}) collective-permute-start(bf16[592,128]{1,0:T(8,128)(2,1)S(1)} %shard_map.142), channel_id=1, source_target_pairs={{0,1},{1,0},{2,3},{3,2},{4,5},{5,4},{6,7},{7,6},{8,9},{9,8},{10,11... | collective-permute-start | bytes 454664 | tf_op jit(solution)/shard_map/ppermute | solution.py:69
  22.8 0.5 shard_map.144
  23.4 1.6 %collective-permute-start.12 = (bf16[128,512]{1,0:T(8,128)(2,1)S(1)}, bf16[128,512]{1,0:T(8,128)(2,1)S(1)}, u32[]{:S(2)}, u32[]{:S(2)}) collective-permute-start(bf16[128,512]{1,0:T(8,128)(2,1)S(1)} %get-tuple-element.75), channel_id=1, source_target_pairs={{0,4},{2,6},{4,0},{6,2},{1,5},{3,7},{5,1},{7,3},{8,12},{10,14},{12... | collective-permute-start | bytes 393224 | tf_op jit(solution)/shard_map/ppermute | solution.py:69
  25.3 0.7 %shard_map.141 = (f32[16,128]{1,0:T(8,128)S(1)}, f32[16,128]{1,0:T(8,128)S(1)}, f32[512,128]{1,0:T(8,128)S(1)}) custom-call(s32[3]{0:T(128)S(1)} %pad_add_fusion.2.ids_ref, s32[2,128]{1,0:T(2,128)S(1)} %get-tuple-element.50.begin_ref, bf16[128,512]{1,0:T(8,128)(2,1)S(1)} %bitcast.40, bf16[128,512]{1,0:T(8,128)(2,1)S(1)} %collective-permute-done.1.refs_1_, ...), custom_call_target="tpu_custom_call" | custom-call | flops 1500000000 | tf_op jit(solution)/shard_map/pallas_call | solution.py:530
  26.5 0.6 %shard_map.143 = (bf16[128,512]{1,0:T(8,128)(2,1)S(1)}, bf16[64,512]{1,0:T(8,128)(2,1)S(1)}, bf16[64,512]{1,0:T(8,128)(2,1)S(1)}, bf16[64,512]{1,0:T(8,128)(2,1)S(1)}, bf16[64,512]{1,0:T(8,128)(2,1)S(1)}) custom-call(s32[1]{0:T(128)} %bitcast.own_ref, bf16[160,512]{1,0:T(8,128)(2,1)S(1)} %get-tuple-element.49.extended_ref.refs_0_, ...), custom_call_target="tpu_custom_call" | custom-call | flops 2000000000 | tf_op jit(solution)/shard_map/pallas_call | solution.py:570
  27.3 1.5 %collective-permute-start.15 = (bf16[64,512]{1,0:T(8,128)(2,1)S(1)}, bf16[64,512]{1,0:T(8,128)(2,1)S(1)}, u32[]{:S(2)}, u32[]{:S(2)}) collective-permute-start(bf16[64,512]{1,0:T(8,128)(2,1)S(1)} %get-tuple-element.70), channel_id=1, source_target_pairs={{0,4},{1,5},{2,6},{3,7},{4,0},{5,1},{6,2},{7,3},{8,12},{9,13},{10,... | collective-permute-start | bytes 196616 | tf_op jit(solution)/shard_map/ppermute | solution.py:69
  29.1 0.6 %collective-permute-done.12.refs_6_ = bf16[128,512]{1,0:T(8,128)(2,1)S(1)} collective-permute-done((bf16[128,512]{1,0:T(8,128)(2,1)S(1)}, bf16[128,512]{1,0:T(8,128)(2,1)S(1)}, u32[]{:S(2)}, u32[]{:S(2)}) %collective-permute-start.12) | collective-permute-done | bytes 131104 | tf_op jit(solution)/shard_map/ppermute | solution.py:69
  29.8 1.8 %collective-permute-start.10 = (bf16[64,512]{1,0:T(8,128)(2,1)S(1)}, bf16[64,512]{1,0:T(8,128)(2,1)S(1)}, u32[]{:S(2)}, u32[]{:S(2)}) collective-permute-start(bf16[64,512]{1,0:T(8,128)(2,1)S(1)} %get-tuple-element.71), channel_id=1, source_target_pairs={{0,7},{1,6},{2,5},{3,4},{4,3},{5,2},{6,1},{7,0},{8,15},{9,14},{10,... | collective-permute-start | bytes 196616 | tf_op jit(solution)/shard_map/ppermute | solution.py:69
  31.7 0.9 %collective-permute-start.8 = (bf16[64,512]{1,0:T(8,128)(2,1)S(1)}, bf16[64,512]{1,0:T(8,128)(2,1)S(1)}, u32[]{:S(2)}, u32[]{:S(2)}) collective-permute-start(bf16[64,512]{1,0:T(8,128)(2,1)S(1)} %get-tuple-element.69), channel_id=1, source_target_pairs={{0,3},{1,2},{2,1},{3,0},{4,7},{5,6},{6,5},{7,4},{8,11},{9,10},{10,... | collective-permute-start | bytes 196616 | tf_op jit(solution)/shard_map/ppermute | solution.py:69
  32.6 2.4 %collective-permute-start.9 = (bf16[64,512]{1,0:T(8,128)(2,1)S(1)}, bf16[64,512]{1,0:T(8,128)(2,1)S(1)}, u32[]{:S(2)}, u32[]{:S(2)}) collective-permute-start(bf16[64,512]{1,0:T(8,128)(2,1)S(1)} %get-tuple-element.70), channel_id=1, source_target_pairs={{0,5},{1,4},{2,7},{3,6},{4,1},{5,0},{6,3},{7,2},{8,13},{9,12},{10,... | collective-permute-start | bytes 196616 | tf_op jit(solution)/shard_map/ppermute | solution.py:69
  35.9 1.8 %shard_map.145 = (bf16[128,512]{1,0:T(8,128)(2,1)S(1)}, bf16[128,512]{1,0:T(8,128)(2,1)S(1)}, bf16[128,512]{1,0:T(8,128)(2,1)S(1)}, bf16[128,512]{1,0:T(8,128)(2...) custom-call(s32[1]{0:T(128)} %bitcast.own_ref, s32[4]{0:T(128)S(1)} %pad_add_fusion.part_ref, ...), custom_call_target="tpu_custom_call" | custom-call | flops 2000000000 | tf_op jit(solution)/shard_map/pallas_call | solution.py:583
  38.1 1.7 %collective-permute-start.18 = (bf16[128,512]{1,0:T(8,128)(2,1)S(1)}, bf16[128,512]{1,0:T(8,128)(2,1)S(1)}, u32[]{:S(2)}, u32[]{:S(2)}) collective-permute-start(bf16[128,512]{1,0:T(8,128)(2,1)S(1)} %get-tuple-element.83), channel_id=1, source_target_pairs={{0,4},{2,6},{4,0},{6,2},{1,5},{3,7},{5,1},{7,3},{8,12},{10,14},{12... | collective-permute-start | bytes 393224 | tf_op jit(solution)/shard_map/ppermute | solution.py:69
  39.9 1.6 %shard_map.146 = (bf16[2,64,512]{2,1,0:T(8,128)(2,1)S(1)}, bf16[2,64,512]{2,1,0:T(8,128)(2,1)S(1)}, bf16[2,64,512]{2,1,0:T(8,128)(2,1)S(1)}, f32[2,64,512]{2,1,0:T(8,128)S(1)}) custom-call(s32[1]{0:T(128)} %bitcast.own_ref, s32[4]{0:T(128)S(1)} %pad_add_fusion.part_ref, bf16[512,512]{1,0:T(8,128)(2,1)S(1)} %bitcast.27, bf16[512,512]{1,0:T(8,128)(2,1)S(1)} %bitcast.29, ...), custom_call_target="tpu_custom_call" | custom-call | flops 2000000000 | tf_op jit(solution)/shard_map/pallas_call | solution.py:583
  41.5 1.7 %collective-permute-start.20 = (bf16[2,64,512]{2,1,0:T(8,128)(2,1)S(1)}, bf16[2,64,512]{2,1,0:T(8,128)(2,1)S(1)}, u32[]{:S(2)}, u32[]{:S(2)}) collective-permute-start(bf16[2,64,512]{2,1,0:T(8,128)(2,1)S(1)} %get-tuple-element.89), channel_id=1, source_target_pairs={{0,24},{8,16},{16,8},{24,0},{1,25},{9,17},{17,9},{25,1},{2,26},{10... | collective-permute-start | bytes 393224 | tf_op jit(solution)/shard_map/ppermute | solution.py:69
  43.3 2.7 %collective-permute-start.22 = (bf16[2,64,512]{2,1,0:T(8,128)(2,1)S(1)}, bf16[2,64,512]{2,1,0:T(8,128)(2,1)S(1)}, u32[]{:S(2)}, u32[]{:S(2)}) collective-permute-start(bf16[2,64,512]{2,1,0:T(8,128)(2,1)S(1)} %get-tuple-element.91), channel_id=1, source_target_pairs={{0,8},{8,0},{16,24},{24,16},{1,9},{9,1},{17,25},{25,17},{2,10},{10... | collective-permute-start | bytes 393224 | tf_op jit(solution)/shard_map/ppermute | solution.py:69
  46.0 1.4 %shard_map.147 = (bf16[128,512]{1,0:T(8,128)(2,1)}, bf16[128,512]{1,0:T(8,128)(2,1)}) custom-call(s32[1]{0:T(128)} %bitcast.own_ref, bf16[128,512]{1,0:T(8,128)(2,1)S(1)} %get-tuple-element.80.mixed_ref, bf16[160,512]{1,0:T(8,128)(2,1)S(1)} %get-tuple-element.49.extended_ref.refs_0_, bf16[128,512]{1,0:T(8,128)(2,1)S(1)} %get-tuple-element.81.refs_0_, ...), custom_call_target="tpu_custom_call" | custom-call | flops 1500000000 | tf_op jit(solution)/shard_map/pallas_call | solution.py:616
  47.4 2.2 %collective-permute-done.20.refs_0_ = bf16[2,64,512]{2,1,0:T(8,128)(2,1)S(1)} collective-permute-done((bf16[2,64,512]{2,1,0:T(8,128)(2,1)S(1)}, bf16[2,64,512]{2,1,0:T(8,128)(2,1)S(1)}, u32[]{:S(2)}, u32[]{:S(2)}) %collective-permute-start.20) | collective-permute-done | bytes 131104 | tf_op jit(solution)/shard_map/ppermute | solution.py:69
  49.6 5.9 %collective-permute-done.21.refs_1_ = bf16[2,64,512]{2,1,0:T(8,128)(2,1)S(1)} collective-permute-done((bf16[2,64,512]{2,1,0:T(8,128)(2,1)S(1)}, bf16[2,64,512]{2,1,0:T(8,128)(2,1)S(1)}, u32[]{:S(2)}, u32[]{:S(2)}) %collective-permute-start.21) | collective-permute-done | bytes 131104 | tf_op jit(solution)/shard_map/ppermute | solution.py:69
  55.6 0.7 %shard_map.148 = (f32[64,512]{1,0:T(8,128)}, f32[64,512]{1,0:T(8,128)}) custom-call(f32[2,64,512]{2,1,0:T(8,128)S(1)} %get-tuple-element.88.kept_ref, bf16[2,64,512]{2,1,0:T(8,128)(2,1)S(1)} %collective-permute-done.20.refs_0_, bf16[2,64,512]{2,1,0:T(8,128)(2,1)S(1)} %collective-permute-done.21.refs_1_, bf16[2,64,512]{2,1,0:T(8,128)(2,1)S(1)} %collective-permute-done.22.refs_2_), custom_call_target="tpu_custom_call" | custom-call | flops 500000000 | tf_op jit(solution)/shard_map/pallas_call | solution.py:623
  (53 shorter events, 3.3 us)
Async XLA Ops:
  0.6 11.1 %collective-permute-start = (bf16[128,512]{1,0:T(8,128)(2,1)}, bf16[128,512]{1,0:T(8,128)(2,1)S(1)}, u32[]{:S(2)}, u32[]{:S(2)}) collective-permute-start(bf16[128,512]{1,0:T(8,128)(2,1)} %bitcast.31), channel_id=1, source_target_pairs={{0,8},{8,16},{16,24},{24,0},{1,9},{9,17},{17,25},{25,1},{2,10},{10... | collective-permute-start | bytes 393224 | tf_op jit(solution)/shard_map/ppermute | solution.py:491
  3.7 9.7 %collective-permute-start.4 = (bf16[128,512]{1,0:T(8,128)(2,1)}, bf16[128,512]{1,0:T(8,128)(2,1)S(1)}, u32[]{:S(2)}, u32[]{:S(2)}) collective-permute-start(bf16[128,512]{1,0:T(8,128)(2,1)} %bitcast.37), channel_id=1, source_target_pairs={{0,1},{1,0},{2,3},{3,2},{4,5},{5,4},{6,7},{7,6},{8,9},{9,8},{10,11... | collective-permute-start | bytes 393224 | tf_op jit(solution)/shard_map/ppermute | solution.py:69
  5.2 8.1 %collective-permute-start.2 = (bf16[128,512]{1,0:T(8,128)(2,1)}, bf16[128,512]{1,0:T(8,128)(2,1)S(1)}, u32[]{:S(2)}, u32[]{:S(2)}) collective-permute-start(bf16[128,512]{1,0:T(8,128)(2,1)} %bitcast.34), channel_id=1, source_target_pairs={{0,8},{8,16},{16,24},{24,0},{1,9},{9,17},{17,25},{25,1},{2,10},{10... | collective-permute-start | bytes 393224 | tf_op jit(solution)/shard_map/ppermute | solution.py:491
  6.8 0.7 %copy-start.8 = (bf16[512,4]{0,1:T(4,128)(2,1)S(1)}, bf16[512,4]{0,1:T(4,128)(2,1)}, u32[]{:S(2)}) copy-start(bf16[512,4]{0,1:T(4,128)(2,1)} %param.17) | copy-start | bytes 12292
  7.5 0.9 %copy-start.3 = (bf16[1,128,512]{2,1,0:T(8,128)(2,1)S(1)}, bf16[1,128,512]{2,1,0:T(8,128)(2,1)}, u32[]{:S(2)}) copy-start(bf16[1,128,512]{2,1,0:T(8,128)(2,1)} %param.21) | copy-start | bytes 393220
  8.4 1.3 %copy-start.4 = (bf16[1,128,512]{2,1,0:T(8,128)(2,1)S(1)}, bf16[1,128,512]{2,1,0:T(8,128)(2,1)}, u32[]{:S(2)}) copy-start(bf16[1,128,512]{2,1,0:T(8,128)(2,1)} %param.12) | copy-start | bytes 393220
  8.4 1.3 %copy-start.5 = (bf16[1,128,512]{2,1,0:T(8,128)(2,1)S(1)}, bf16[1,128,512]{2,1,0:T(8,128)(2,1)}, u32[]{:S(2)}) copy-start(bf16[1,128,512]{2,1,0:T(8,128)(2,1)} %param.13) | copy-start | bytes 393220
  8.4 1.3 %copy-start.6 = (bf16[1,128,512]{2,1,0:T(8,128)(2,1)S(1)}, bf16[1,128,512]{2,1,0:T(8,128)(2,1)}, u32[]{:S(2)}) copy-start(bf16[1,128,512]{2,1,0:T(8,128)(2,1)} %param.11) | copy-start | bytes 393220
  9.0 12.2 %collective-permute-start.5 = (bf16[160,512]{1,0:T(8,128)(2,1)S(1)}, bf16[160,512]{1,0:T(8,128)(2,1)S(1)}, u32[]{:S(2)}, u32[]{:S(2)}) collective-permute-start(bf16[160,512]{1,0:T(8,128)(2,1)S(1)} %get-tuple-element.49.extended_ref.refs_0_), channel_id=1, source_target_pairs={{0,1},{1,0},{2,3},{3,2},{4,5},{5,4},{6,7},{7,6},{8,9},{9,8},{10,11... | collective-permute-start | bytes 491528 | tf_op jit(solution)/shard_map/ppermute | solution.py:69
  11.7 7.4 %collective-permute-start.1 = (bf16[128,512]{1,0:T(8,128)(2,1)S(1)}, bf16[128,512]{1,0:T(8,128)(2,1)S(1)}, u32[]{:S(2)}, u32[]{:S(2)}) collective-permute-start(bf16[128,512]{1,0:T(8,128)(2,1)S(1)} %collective-permute-done.refs_4_), channel_id=1, source_target_pairs={{0,8},{8,16},{16,24},{24,0},{1,9},{9,17},{17,25},{25,1},{2,10},{10... | collective-permute-start | bytes 393224 | tf_op jit(solution)/shard_map/ppermute | solution.py:491
  13.3 7.2 %collective-permute-start.3 = (bf16[128,512]{1,0:T(8,128)(2,1)S(1)}, bf16[128,512]{1,0:T(8,128)(2,1)S(1)}, u32[]{:S(2)}, u32[]{:S(2)}) collective-permute-start(bf16[128,512]{1,0:T(8,128)(2,1)S(1)} %collective-permute-done.2.refs_5_), channel_id=1, source_target_pairs={{0,8},{8,16},{16,24},{24,0},{1,9},{9,17},{17,25},{25,1},{2,10},{10... | collective-permute-start | bytes 393224 | tf_op jit(solution)/shard_map/ppermute | solution.py:491
  21.3 5.3 %collective-permute-start.6 = (bf16[592,128]{1,0:T(8,128)(2,1)S(1)}, bf16[592,128]{1,0:T(8,128)(2,1)S(1)}, u32[]{:S(2)}, u32[]{:S(2)}) collective-permute-start(bf16[592,128]{1,0:T(8,128)(2,1)S(1)} %shard_map.142), channel_id=1, source_target_pairs={{0,1},{1,0},{2,3},{3,2},{4,5},{5,4},{6,7},{7,6},{8,9},{9,8},{10,11... | collective-permute-start | bytes 454664 | tf_op jit(solution)/shard_map/ppermute | solution.py:69
  23.3 5.6 %collective-permute-start.11 = (bf16[128,512]{1,0:T(8,128)(2,1)S(1)}, bf16[128,512]{1,0:T(8,128)(2,1)S(1)}, u32[]{:S(2)}, u32[]{:S(2)}) collective-permute-start(bf16[128,512]{1,0:T(8,128)(2,1)S(1)} %get-tuple-element.74), channel_id=1, source_target_pairs={{0,2},{2,0},{4,6},{6,4},{1,3},{3,1},{5,7},{7,5},{8,10},{10,8},{12,... | collective-permute-start | bytes 393224 | tf_op jit(solution)/shard_map/ppermute | solution.py:69
  23.4 6.4 %collective-permute-start.12 = (bf16[128,512]{1,0:T(8,128)(2,1)S(1)}, bf16[128,512]{1,0:T(8,128)(2,1)S(1)}, u32[]{:S(2)}, u32[]{:S(2)}) collective-permute-start(bf16[128,512]{1,0:T(8,128)(2,1)S(1)} %get-tuple-element.75), channel_id=1, source_target_pairs={{0,4},{2,6},{4,0},{6,2},{1,5},{3,7},{5,1},{7,3},{8,12},{10,14},{12... | collective-permute-start | bytes 393224 | tf_op jit(solution)/shard_map/ppermute | solution.py:69
  25.0 6.7 %collective-permute-start.13 = (bf16[128,512]{1,0:T(8,128)(2,1)S(1)}, bf16[128,512]{1,0:T(8,128)(2,1)S(1)}, u32[]{:S(2)}, u32[]{:S(2)}) collective-permute-start(bf16[128,512]{1,0:T(8,128)(2,1)S(1)} %get-tuple-element.76), channel_id=1, source_target_pairs={{0,6},{2,4},{4,2},{6,0},{1,7},{3,5},{5,3},{7,1},{8,14},{10,12},{12... | collective-permute-start | bytes 393224 | tf_op jit(solution)/shard_map/ppermute | solution.py:69
  25.3 1.2 %copy-start = (bf16[512,512]{1,0:T(8,128)(2,1)S(1)}, bf16[512,512]{1,0:T(8,128)(2,1)}, u32[]{:S(2)}) copy-start(bf16[512,512]{1,0:T(8,128)(2,1)} %proj_ref.1) | copy-start | bytes 1572868
  25.3 1.2 %copy-start.7 = (bf16[1,128,512]{2,1,0:T(8,128)(2,1)S(1)}, bf16[1,128,512]{2,1,0:T(8,128)(2,1)}, u32[]{:S(2)}) copy-start(bf16[1,128,512]{2,1,0:T(8,128)(2,1)} %param.15) | copy-start | bytes 393220
  26.5 9.4 %copy-start.1 = (bf16[1,512,512]{2,1,0:T(8,128)(2,1)S(1)}, bf16[1,512,512]{2,1,0:T(8,128)(2,1)}, u32[]{:S(2)}) copy-start(bf16[1,512,512]{2,1,0:T(8,128)(2,1)} %param.19) | copy-start | bytes 1572868
  26.5 9.4 %copy-start.2 = (bf16[1,512,512]{2,1,0:T(8,128)(2,1)S(1)}, bf16[1,512,512]{2,1,0:T(8,128)(2,1)}, u32[]{:S(2)}) copy-start(bf16[1,512,512]{2,1,0:T(8,128)(2,1)} %param.20) | copy-start | bytes 1572868
  27.1 5.4 %collective-permute-start.14 = (bf16[64,512]{1,0:T(8,128)(2,1)S(1)}, bf16[64,512]{1,0:T(8,128)(2,1)S(1)}, u32[]{:S(2)}, u32[]{:S(2)}) collective-permute-start(bf16[64,512]{1,0:T(8,128)(2,1)S(1)} %get-tuple-element.69), channel_id=1, source_target_pairs={{0,2},{1,3},{2,0},{3,1},{4,6},{5,7},{6,4},{7,5},{8,10},{9,11},{10,... | collective-permute-start | bytes 196616 | tf_op jit(solution)/shard_map/ppermute | solution.py:69
  27.3 8.0 %collective-permute-start.15 = (bf16[64,512]{1,0:T(8,128)(2,1)S(1)}, bf16[64,512]{1,0:T(8,128)(2,1)S(1)}, u32[]{:S(2)}, u32[]{:S(2)}) collective-permute-start(bf16[64,512]{1,0:T(8,128)(2,1)S(1)} %get-tuple-element.70), channel_id=1, source_target_pairs={{0,4},{1,5},{2,6},{3,7},{4,0},{5,1},{6,2},{7,3},{8,12},{9,13},{10,... | collective-permute-start | bytes 196616 | tf_op jit(solution)/shard_map/ppermute | solution.py:69
  28.9 7.0 %collective-permute-start.16 = (bf16[64,512]{1,0:T(8,128)(2,1)S(1)}, bf16[64,512]{1,0:T(8,128)(2,1)S(1)}, u32[]{:S(2)}, u32[]{:S(2)}) collective-permute-start(bf16[64,512]{1,0:T(8,128)(2,1)S(1)} %get-tuple-element.71), channel_id=1, source_target_pairs={{0,6},{1,7},{2,4},{3,5},{4,2},{5,3},{6,0},{7,1},{8,14},{9,15},{10,... | collective-permute-start | bytes 196616 | tf_op jit(solution)/shard_map/ppermute | solution.py:69
  29.8 8.4 %collective-permute-start.10 = (bf16[64,512]{1,0:T(8,128)(2,1)S(1)}, bf16[64,512]{1,0:T(8,128)(2,1)S(1)}, u32[]{:S(2)}, u32[]{:S(2)}) collective-permute-start(bf16[64,512]{1,0:T(8,128)(2,1)S(1)} %get-tuple-element.71), channel_id=1, source_target_pairs={{0,7},{1,6},{2,5},{3,4},{4,3},{5,2},{6,1},{7,0},{8,15},{9,14},{10,... | collective-permute-start | bytes 196616 | tf_op jit(solution)/shard_map/ppermute | solution.py:69
  31.7 8.2 %collective-permute-start.8 = (bf16[64,512]{1,0:T(8,128)(2,1)S(1)}, bf16[64,512]{1,0:T(8,128)(2,1)S(1)}, u32[]{:S(2)}, u32[]{:S(2)}) collective-permute-start(bf16[64,512]{1,0:T(8,128)(2,1)S(1)} %get-tuple-element.69), channel_id=1, source_target_pairs={{0,3},{1,2},{2,1},{3,0},{4,7},{5,6},{6,5},{7,4},{8,11},{9,10},{10,... | collective-permute-start | bytes 196616 | tf_op jit(solution)/shard_map/ppermute | solution.py:69
  32.6 7.3 %collective-permute-start.9 = (bf16[64,512]{1,0:T(8,128)(2,1)S(1)}, bf16[64,512]{1,0:T(8,128)(2,1)S(1)}, u32[]{:S(2)}, u32[]{:S(2)}) collective-permute-start(bf16[64,512]{1,0:T(8,128)(2,1)S(1)} %get-tuple-element.70), channel_id=1, source_target_pairs={{0,5},{1,4},{2,7},{3,6},{4,1},{5,0},{6,3},{7,2},{8,13},{9,12},{10,... | collective-permute-start | bytes 196616 | tf_op jit(solution)/shard_map/ppermute | solution.py:69
  35.4 4.5 %collective-permute-start.7 = (bf16[64,512]{1,0:T(8,128)(2,1)S(1)}, bf16[64,512]{1,0:T(8,128)(2,1)S(1)}, u32[]{:S(2)}, u32[]{:S(2)}) collective-permute-start(bf16[64,512]{1,0:T(8,128)(2,1)S(1)} %get-tuple-element.68.refs_0_), channel_id=1, source_target_pairs={{0,1},{1,0},{2,3},{3,2},{4,5},{5,4},{6,7},{7,6},{8,9},{9,8},{10,11... | collective-permute-start | bytes 196616 | tf_op jit(solution)/shard_map/ppermute | solution.py:69
  37.7 5.6 %collective-permute-start.17 = (bf16[128,512]{1,0:T(8,128)(2,1)S(1)}, bf16[128,512]{1,0:T(8,128)(2,1)S(1)}, u32[]{:S(2)}, u32[]{:S(2)}) collective-permute-start(bf16[128,512]{1,0:T(8,128)(2,1)S(1)} %get-tuple-element.82), channel_id=1, source_target_pairs={{0,2},{2,0},{4,6},{6,4},{1,3},{3,1},{5,7},{7,5},{8,10},{10,8},{12,... | collective-permute-start | bytes 393224 | tf_op jit(solution)/shard_map/ppermute | solution.py:69
  38.1 7.9 %collective-permute-start.18 = (bf16[128,512]{1,0:T(8,128)(2,1)S(1)}, bf16[128,512]{1,0:T(8,128)(2,1)S(1)}, u32[]{:S(2)}, u32[]{:S(2)}) collective-permute-start(bf16[128,512]{1,0:T(8,128)(2,1)S(1)} %get-tuple-element.83), channel_id=1, source_target_pairs={{0,4},{2,6},{4,0},{6,2},{1,5},{3,7},{5,1},{7,3},{8,12},{10,14},{12... | collective-permute-start | bytes 393224 | tf_op jit(solution)/shard_map/ppermute | solution.py:69
  39.9 6.1 %collective-permute-start.19 = (bf16[128,512]{1,0:T(8,128)(2,1)S(1)}, bf16[128,512]{1,0:T(8,128)(2,1)S(1)}, u32[]{:S(2)}, u32[]{:S(2)}) collective-permute-start(bf16[128,512]{1,0:T(8,128)(2,1)S(1)} %get-tuple-element.84), channel_id=1, source_target_pairs={{0,6},{2,4},{4,2},{6,0},{1,7},{3,5},{5,3},{7,1},{8,14},{10,12},{12... | collective-permute-start | bytes 393224 | tf_op jit(solution)/shard_map/ppermute | solution.py:69
  41.5 8.1 %collective-permute-start.20 = (bf16[2,64,512]{2,1,0:T(8,128)(2,1)S(1)}, bf16[2,64,512]{2,1,0:T(8,128)(2,1)S(1)}, u32[]{:S(2)}, u32[]{:S(2)}) collective-permute-start(bf16[2,64,512]{2,1,0:T(8,128)(2,1)S(1)} %get-tuple-element.89), channel_id=1, source_target_pairs={{0,24},{8,16},{16,8},{24,0},{1,25},{9,17},{17,9},{25,1},{2,26},{10... | collective-permute-start | bytes 393224 | tf_op jit(solution)/shard_map/ppermute | solution.py:69
  43.3 12.3 %collective-permute-start.21 = (bf16[2,64,512]{2,1,0:T(8,128)(2,1)S(1)}, bf16[2,64,512]{2,1,0:T(8,128)(2,1)S(1)}, u32[]{:S(2)}, u32[]{:S(2)}) collective-permute-start(bf16[2,64,512]{2,1,0:T(8,128)(2,1)S(1)} %get-tuple-element.90), channel_id=1, source_target_pairs={{0,16},{8,24},{16,0},{24,8},{1,17},{9,25},{17,1},{25,9},{2,18},{10... | collective-permute-start | bytes 393224 | tf_op jit(solution)/shard_map/ppermute | solution.py:69
  43.3 12.3 %collective-permute-start.22 = (bf16[2,64,512]{2,1,0:T(8,128)(2,1)S(1)}, bf16[2,64,512]{2,1,0:T(8,128)(2,1)S(1)}, u32[]{:S(2)}, u32[]{:S(2)}) collective-permute-start(bf16[2,64,512]{2,1,0:T(8,128)(2,1)S(1)} %get-tuple-element.91), channel_id=1, source_target_pairs={{0,8},{8,0},{16,24},{24,16},{1,9},{9,1},{17,25},{25,17},{2,10},{10... | collective-permute-start | bytes 393224 | tf_op jit(solution)/shard_map/ppermute | solution.py:69
  (2 other events, 1.3 us)

commit v14 on v13

--- a/solution.py
+++ b/solution.py
@@ -139,18 +139,6 @@
 def router_of(extended_ref, tok, expert_count):
     whole = extended_ref[tok + 16 :, :].astype(jnp.float32)
     return whole[0:expert_count].astype(jnp.bfloat16)
-
-
-def dispatch_kernel(reps, tok, hot_capacity, own_ref, *refs):
-    extended_refs, sent_refs = refs[:reps], refs[reps:]
-    for rep in range(reps):
-        choice = chosen_of(extended_refs[rep], tok)
-        placed = slot_matrix(choice, own_ref[0], len(sent_refs), hot_capacity)
-        rows = dot(placed, extended_refs[rep][0:tok, :]).astype(jnp.bfloat16)
-        for k, sent_ref in enumerate(sent_refs):
-            sent_ref[rep * hot_capacity : (rep + 1) * hot_capacity] = rows[
-                k * hot_capacity : (k + 1) * hot_capacity
-            ]
 
 
 def fold_blocks(ids_ref, begin_ref, tasks, reps, states, bias_ref):
@@ -299,17 +287,18 @@
     normed = (mixed_f * inv_rms).astype(jnp.bfloat16)
     placed = slot_matrix(chosen_of(extended_ref, tok), own_ref[0], len(sent_refs), hot_capacity)
     rows = dot(placed, normed).astype(jnp.bfloat16)
+    grads = dot(placed, extended_ref[0:tok, :]).astype(jnp.bfloat16)
     for k, sent_ref in enumerate(sent_refs):
-        sent_ref[...] = rows[k * hot_capacity : (k + 1) * hot_capacity]
+        sent_ref[0:hot_capacity] = rows[k * hot_capacity : (k + 1) * hot_capacity]
+        sent_ref[hot_capacity:] = grads[k * hot_capacity : (k + 1) * hot_capacity]
 
 
 def expert_kernel(
-    reps,
     rep_list,
     sources,
     tok,
     strip,
-    counts,
+    row_count,
     own_ref,
     part_ref,
     up_ref,
@@ -317,10 +306,8 @@
     extended_ref,
     *refs,
 ):
-    row_count, grad_count = counts
     row_refs, refs = refs[:row_count], refs[row_count:]
     per_rep = row_count // len(rep_list)
-    grad_refs, refs = refs[:grad_count], refs[grad_count:]
     own_rows = rep_list[0] == 0
     held_ref, refs = refs[-1], refs[:-1]
     if own_rows:
@@ -328,8 +315,7 @@
     else:
         up_old, down_old = refs[:2]
         term_refs, kept_ref = refs[2:-1], refs[-1]
-    total_grads = sum(ref.shape[0] for ref in grad_refs)
-    capacity = total_grads // (sources * reps)
+    capacity = sum(ref.shape[0] for ref in row_refs[:per_rep]) // (2 * sources)
     count = sources * capacity
     parts = part_ref.shape[0]
     up = up_ref[...]
@@ -346,11 +332,10 @@
         return jnp.concatenate(taken, axis=0)
 
     up_term = down_term = None
-    for place, rep in enumerate(rep_list):
-        rows = chunk_rows(
-            row_refs[place * per_rep : (place + 1) * per_rep], sources, 0, capacity
-        )
-        grads = chunk_rows(grad_refs, sources, rep * capacity, (rep + 1) * capacity)
+    for place in range(len(rep_list)):
+        chunks = row_refs[place * per_rep : (place + 1) * per_rep]
+        rows = chunk_rows(chunks, sources, 0, capacity)
+        grads = chunk_rows(chunks, sources, capacity, 2 * capacity)
         pre = dot(rows, up)
         sigmoid_pre = jax.nn.sigmoid(pre)
         activated = (pre * sigmoid_pre).astype(jnp.bfloat16)
@@ -544,7 +529,6 @@
     lines = [(key_rows[0], value_rows[0])]
     lines.append(tuple(forward(one) for one in lines[0]))
     queries = reps.exchange([query_rows[0]] * rep_count)
-    extendeds = reps.exchange([extended] * rep_count)
     states = attend(((0, 0, True),), lines[:1], [0], queries, {}, False, 2.0)
     ahead, *states[0] = lax.optimization_barrier((lines[1][0], *states[0]))
     lines[1] = (ahead, lines[1][1])
@@ -557,22 +541,14 @@
     partial = attend(
         tuple((k, 0, False) for k in others), lines[-1:], [reach], queries, states, True, 1.5
     )
-    partial[1], *extendeds[1:] = lax.optimization_barrier((partial[1], *extendeds[1:]))
     returned = reps.exchange([None] + [partial[k] for k in others], inverse=True)[1:]
     states = attend(((0, 0, False),), lines[-1:], [reach], queries, states, False, 1.5)
-    sent_grads = call(
-        functools.partial(dispatch_kernel, rep_count, tok, hot_capacity),
-        [shape((rep_count * hot_capacity, width))] * expert_count,
-        [SMEM] + [VMEM] * rep_count,
-    )(own, *extendeds)
-    got_grads = merged(experts.exchange(sent_grads), MOST_PERMUTES)
-
     mixed, *sent_rows = call(
         functools.partial(mix_kernel, expert_count, hot_capacity),
-        [shape((tok, width))] + [shape((hot_capacity, width))] * expert_count,
+        [shape((tok, width))] + [shape((2 * hot_capacity, width))] * expert_count,
         [SMEM] + [VMEM] * (6 + len(returned)),
         cost=2.0,
-    )(own, extendeds[0], residual[0], out_proj, *states[0], *returned)
+    )(own, extended, residual[0], out_proj, *states[0], *returned)
     arrived = owners.exchange([sent_rows[k // rep_count] for k in range(owners.count)])
     got_rows = merged(arrived[0::rep_count], MOST_PERMUTES)
     got_more = [
@@ -583,18 +559,17 @@
         return call(
             functools.partial(
                 expert_kernel,
-                rep_count,
                 rep_list,
                 expert_count,
                 tok,
                 strip,
-                (len(rows), len(got_grads)),
+                len(rows),
             ),
             out_shape,
-            [SMEM, SMEM] + [VMEM] * (3 + len(rows) + len(got_grads) + len(extra)),
+            [SMEM, SMEM] + [VMEM] * (3 + len(rows) + len(extra)),
             [pltpu.VMEM((2 * len(rep_list), width, expert_count * hot_capacity), jnp.bfloat16)],
             cost=2.0,
-        )(own, part_to, weight_in[0], weight_out[0], extendeds[0], *rows, *got_grads, *extra)
+        )(own, part_to, weight_in[0], weight_out[0], extended, *rows, *extra)
 
     *back, up_acc, down_acc = expert_call(
         (0,),

time: 56.5 us -> 61.4 us (1.087)
  waiting for transfers between devices: 15.3 us -> 24.8 us
  starting transfers between devices: 25.7 us -> 21.1 us
    ppermute x19 -> x15, waiting for transfers between devices: 10.1 us -> 19.5 us  [exchange(): got[k] = lax.ppermute(chunks[k], self.axes, pairs)]
    ppermute x19 -> x15, starting transfers between devices: 19.4 us -> 14.6 us  [exchange(): got[k] = lax.ppermute(chunks[k], self.axes, pairs)]
    pallas_call x3 -> x2, Pallas kernels: 4.01 us -> 3.43 us  [expert_call(): call(functools.partial(expert_kernel, rep_list, expert_count, tok, strip,...]
  transfers between devices with their start and end apart: 23 -> 19, of which waited for: 9 -> 8; matrix products, arithmetic and copies ran while one was open for 1% -> 1% of each run, Pallas kernels for 21% -> 16%
where the time goes in v14:
time: 61.4 us; the launch traced here: 61.2 us
  waiting for transfers between devices  24.8 us (40%)
  starting transfers between devices  21.1 us (34%)
  Pallas kernels  12 us (20%)
  local copies, waits for them, and re-layouts  2.13 us (3%)
  between operations  0.8 us (1%)
    ppermute x15, waiting for transfers between devices, exchange(): got[k] = lax.ppermute(chunks[k], self.axes, pairs)  19.5 us
    ppermute x15, starting transfers between devices, exchange(): got[k] = lax.ppermute(chunks[k], self.axes, pairs)  14.6 us
    ppermute x4, starting transfers between devices, forward(): lax.ppermute(array, 'seq', [(i, (i + 1) % seq_count) for i in range(seq_c...  6.45 us
    ppermute x4, waiting for transfers between devices, forward(): lax.ppermute(array, 'seq', [(i, (i + 1) % seq_count) for i in range(seq_c...  5.25 us
    pallas_call x4, Pallas kernels, attend(): call(functools.partial(attend_kernel, plan, rep_count, len(pairs), packed...  5.19 us
    pallas_call x2, Pallas kernels, expert_call(): call(functools.partial(expert_kernel, rep_list, expert_count, tok, strip,...  3.43 us
    unnamed x22, local copies, waits for them, and re-layouts  2.04 us
    pallas_call x1, Pallas kernels, local(): call(functools.partial(finish_kernel, hot_capacity, expert_count), [shape...  1.41 us
  transfers between devices with their start and end apart: 19, of which 8 were waited for; matrix products, arithmetic and copies ran while one was open for 1% of the time, Pallas kernels for 16%

profile of v14, /device:TPU:0, one launch (start us, length us, event | category | flops | bytes accessed | tf_op | source)
XLA Modules:
  0.0 61.2 jit_solution(11641497741861357966)
XLA Ops:
  0.6 3.1 %collective-permute-start = (bf16[128,512]{1,0:T(8,128)(2,1)}, bf16[128,512]{1,0:T(8,128)(2,1)S(1)}, u32[]{:S(2)}, u32[]{:S(2)}) collective-permute-start(bf16[128,512]{1,0:T(8,128)(2,1)} %bitcast.31), channel_id=1, source_target_pairs={{0,8},{8,16},{16,24},{24,0},{1,9},{9,17},{17,25},{25,1},{2,10},{10... | collective-permute-start | bytes 393224 | tf_op jit(solution)/shard_map/ppermute | solution.py:476
  3.7 1.5 %collective-permute-start.4 = (bf16[128,512]{1,0:T(8,128)(2,1)}, bf16[128,512]{1,0:T(8,128)(2,1)S(1)}, u32[]{:S(2)}, u32[]{:S(2)}) collective-permute-start(bf16[128,512]{1,0:T(8,128)(2,1)} %bitcast.37), channel_id=1, source_target_pairs={{0,1},{1,0},{2,3},{3,2},{4,5},{5,4},{6,7},{7,6},{8,9},{9,8},{10,11... | collective-permute-start | bytes 393224 | tf_op jit(solution)/shard_map/ppermute | solution.py:69
  5.2 1.6 %collective-permute-start.2 = (bf16[128,512]{1,0:T(8,128)(2,1)}, bf16[128,512]{1,0:T(8,128)(2,1)S(1)}, u32[]{:S(2)}, u32[]{:S(2)}) collective-permute-start(bf16[128,512]{1,0:T(8,128)(2,1)} %bitcast.34), channel_id=1, source_target_pairs={{0,8},{8,16},{16,24},{24,0},{1,9},{9,17},{17,25},{25,1},{2,10},{10... | collective-permute-start | bytes 393224 | tf_op jit(solution)/shard_map/ppermute | solution.py:476
  6.9 0.6 copy-done.8
  7.6 0.9 %copy-done.3 = bf16[1,128,512]{2,1,0:T(8,128)(2,1)S(1)} copy-done((bf16[1,128,512]{2,1,0:T(8,128)(2,1)S(1)}, bf16[1,128,512]{2,1,0:T(8,128)(2,1)}, u32[]{:S(2)}) %copy-start.3) | copy-done | bytes 131096
  8.5 0.6 shard_map.138
  9.5 1.7 %shard_map.139 = (f32[16,128]{1,0:T(8,128)S(1)}, f32[16,128]{1,0:T(8,128)S(1)}, f32[512,128]{1,0:T(8,128)S(1)}) custom-call(s32[3]{0:T(128)S(1)} %pad_add_fusion.4.ids_ref, s32[2,128]{1,0:T(2,128)S(1)} %get-tuple-element.44.begin_ref, bf16[128,512]{1,0:T(8,128)(2,1)S(1)} %bitcast.38, bf16[128,512]{1,0:T(8,128)(2,1)S(1)} %bitcast.32, ...), custom_call_target="tpu_custom_call" | custom-call | flops 2000000000 | tf_op jit(solution)/shard_map/pallas_call | solution.py:515
  11.5 1.6 %collective-permute-start.1 = (bf16[128,512]{1,0:T(8,128)(2,1)S(1)}, bf16[128,512]{1,0:T(8,128)(2,1)S(1)}, u32[]{:S(2)}, u32[]{:S(2)}) collective-permute-start(bf16[128,512]{1,0:T(8,128)(2,1)S(1)} %collective-permute-done.refs_4_), channel_id=1, source_target_pairs={{0,8},{8,16},{16,24},{24,0},{1,9},{9,17},{17,25},{25,1},{2,10},{10... | collective-permute-start | bytes 393224 | tf_op jit(solution)/shard_map/ppermute | solution.py:476
  13.3 1.9 %shard_map.140 = (f32[16,128]{1,0:T(8,128)S(1)}, f32[16,128]{1,0:T(8,128)S(1)}, f32[512,128]{1,0:T(8,128)S(1)}, f32[16,128]{1,0:T(8,128)S(1)}, f32[16,128]{1,0:T(8,128)S(1)}, /*index=5*/f32[512,128]{1,0:T(8,128)S(1)}) custom-call(s32[5]{0:T(128)S(1)} %stack.81.ids_ref, s32[2,128]{1,0:T(2,128)S(1)} %get-tuple-element.44.begin_ref, ...), custom_call_target="tpu_custom_call" | custom-call | flops 4000000000 | tf_op jit(solution)/shard_map/pallas_call | solution.py:515
  15.3 3.8 %collective-permute-done.1.refs_1_ = bf16[128,512]{1,0:T(8,128)(2,1)S(1)} collective-permute-done((bf16[128,512]{1,0:T(8,128)(2,1)S(1)}, bf16[128,512]{1,0:T(8,128)(2,1)S(1)}, u32[]{:S(2)}, u32[]{:S(2)}) %collective-permute-start.1) | collective-permute-done | bytes 131104 | tf_op jit(solution)/shard_map/ppermute | solution.py:476
  19.1 1.4 %collective-permute-done.3.refs_2_ = bf16[128,512]{1,0:T(8,128)(2,1)S(1)} collective-permute-done((bf16[128,512]{1,0:T(8,128)(2,1)S(1)}, bf16[128,512]{1,0:T(8,128)(2,1)S(1)}, u32[]{:S(2)}, u32[]{:S(2)}) %collective-permute-start.3) | collective-permute-done | bytes 131104 | tf_op jit(solution)/shard_map/ppermute | solution.py:476
  20.5 0.8 %shard_map.142 = bf16[592,128]{1,0:T(8,128)(2,1)S(1)} custom-call(s32[3]{0:T(128)S(1)} %pad_add_fusion.5.ids_ref, s32[2,128]{1,0:T(2,128)S(1)} %get-tuple-element.44.begin_ref, bf16[128,512]{1,0:T(8,128)(2,1)S(1)} %collective-permute-done.4.refs_1_.refs_0_, bf16[128,512]{1,0:T(8,128)(2,1)S(1)} %collective-permute-done.1.refs_1_, ...), custom_call_target="tpu_custom_call" | custom-call | flops 1500000000 | tf_op jit(solution)/shard_map/pallas_call | solution.py:515
  21.3 0.9 %collective-permute-start.5 = (bf16[592,128]{1,0:T(8,128)(2,1)S(1)}, bf16[592,128]{1,0:T(8,128)(2,1)S(1)}, u32[]{:S(2)}, u32[]{:S(2)}) collective-permute-start(bf16[592,128]{1,0:T(8,128)(2,1)S(1)} %shard_map.142), channel_id=1, source_target_pairs={{0,1},{1,0},{2,3},{3,2},{4,5},{5,4},{6,7},{7,6},{8,9},{9,8},{10,11... | collective-permute-start | bytes 454664 | tf_op jit(solution)/shard_map/ppermute | solution.py:69
  22.3 0.7 %shard_map.141 = (f32[16,128]{1,0:T(8,128)S(1)}, f32[16,128]{1,0:T(8,128)S(1)}, f32[512,128]{1,0:T(8,128)S(1)}) custom-call(s32[3]{0:T(128)S(1)} %pad_add_fusion.2.ids_ref, s32[2,128]{1,0:T(2,128)S(1)} %get-tuple-element.44.begin_ref, bf16[128,512]{1,0:T(8,128)(2,1)S(1)} %bitcast.40, bf16[128,512]{1,0:T(8,128)(2,1)S(1)} %collective-permute-done.1.refs_1_, ...), custom_call_target="tpu_custom_call" | custom-call | flops 1500000000 | tf_op jit(solution)/shard_map/pallas_call | solution.py:515
  23.1 3.5 %collective-permute-done.5.refs_3_ = bf16[592,128]{1,0:T(8,128)(2,1)S(1)} collective-permute-done((bf16[592,128]{1,0:T(8,128)(2,1)S(1)}, bf16[592,128]{1,0:T(8,128)(2,1)S(1)}, u32[]{:S(2)}, u32[]{:S(2)}) %collective-permute-start.5) | collective-permute-done | bytes 151584 | tf_op jit(solution)/shard_map/ppermute | solution.py:69
  26.6 0.7 %shard_map.143 = (bf16[128,512]{1,0:T(8,128)(2,1)S(1)}, bf16[128,512]{1,0:T(8,128)(2,1)S(1)}, bf16[128,512]{1,0:T(8,128)(2,1)S(1)}, bf16[128,512]{1,0:T(8,128)(2,1)S(1)}, bf16[128,512]{1,0:T(8,128)(2,1)S(1)}) custom-call(s32[1]{0:T(128)} %bitcast.own_ref, bf16[160,512]{1,0:T(8,128)(2,1)S(1)} %get-tuple-element.43.extended_ref, ...), custom_call_target="tpu_custom_call" | custom-call | flops 2000000000 | tf_op jit(solution)/shard_map/pallas_call | solution.py:546
  27.3 1.6 %collective-permute-start.11 = (bf16[128,512]{1,0:T(8,128)(2,1)S(1)}, bf16[128,512]{1,0:T(8,128)(2,1)S(1)}, u32[]{:S(2)}, u32[]{:S(2)}) collective-permute-start(bf16[128,512]{1,0:T(8,128)(2,1)S(1)} %get-tuple-element.63), channel_id=1, source_target_pairs={{0,4},{1,5},{2,6},{3,7},{4,0},{5,1},{6,2},{7,3},{8,12},{9,13},{10,... | collective-permute-start | bytes 393224 | tf_op jit(solution)/shard_map/ppermute | solution.py:69
  29.2 0.8 %collective-permute-start.7 = (bf16[128,512]{1,0:T(8,128)(2,1)S(1)}, bf16[128,512]{1,0:T(8,128)(2,1)S(1)}, u32[]{:S(2)}, u32[]{:S(2)}) collective-permute-start(bf16[128,512]{1,0:T(8,128)(2,1)S(1)} %get-tuple-element.62), channel_id=1, source_target_pairs={{0,3},{1,2},{2,1},{3,0},{4,7},{5,6},{6,5},{7,4},{8,11},{9,10},{10,... | collective-permute-start | bytes 393224 | tf_op jit(solution)/shard_map/ppermute | solution.py:69
  30.1 2.1 %collective-permute-start.8 = (bf16[128,512]{1,0:T(8,128)(2,1)S(1)}, bf16[128,512]{1,0:T(8,128)(2,1)S(1)}, u32[]{:S(2)}, u32[]{:S(2)}) collective-permute-start(bf16[128,512]{1,0:T(8,128)(2,1)S(1)} %get-tuple-element.63), channel_id=1, source_target_pairs={{0,5},{1,4},{2,7},{3,6},{4,1},{5,0},{6,3},{7,2},{8,13},{9,12},{10,... | collective-permute-start | bytes 393224 | tf_op jit(solution)/shard_map/ppermute | solution.py:69
  32.5 1.2 %collective-permute-done.11.refs_2_ = bf16[128,512]{1,0:T(8,128)(2,1)S(1)} collective-permute-done((bf16[128,512]{1,0:T(8,128)(2,1)S(1)}, bf16[128,512]{1,0:T(8,128)(2,1)S(1)}, u32[]{:S(2)}, u32[]{:S(2)}) %collective-permute-start.11) | collective-permute-done | bytes 131104 | tf_op jit(solution)/shard_map/ppermute | solution.py:69
  33.7 0.9 %collective-permute-start.6 = (bf16[128,512]{1,0:T(8,128)(2,1)S(1)}, bf16[128,512]{1,0:T(8,128)(2,1)S(1)}, u32[]{:S(2)}, u32[]{:S(2)}) collective-permute-start(bf16[128,512]{1,0:T(8,128)(2,1)S(1)} %get-tuple-element.61.refs_0_), channel_id=1, source_target_pairs={{0,1},{1,0},{2,3},{3,2},{4,5},{5,4},{6,7},{7,6},{8,9},{9,8},{10,11... | collective-permute-start | bytes 393224 | tf_op jit(solution)/shard_map/ppermute | solution.py:69
  34.5 6.2 %collective-permute-done.12.refs_3_ = bf16[128,512]{1,0:T(8,128)(2,1)S(1)} collective-permute-done((bf16[128,512]{1,0:T(8,128)(2,1)S(1)}, bf16[128,512]{1,0:T(8,128)(2,1)S(1)}, u32[]{:S(2)}, u32[]{:S(2)}) %collective-permute-start.12) | collective-permute-done | bytes 131104 | tf_op jit(solution)/shard_map/ppermute | solution.py:69
  40.7 1.8 %shard_map.144 = (bf16[128,512]{1,0:T(8,128)(2,1)S(1)}, bf16[128,512]{1,0:T(8,128)(2,1)S(1)}, bf16[128,512]{1,0:T(8,128)(2,1)S(1)}, bf16[128,512]{1,0:T(8,128)(2...) custom-call(s32[1]{0:T(128)} %bitcast.own_ref, s32[4]{0:T(128)S(1)} %pad_add_fusion.part_ref, ...), custom_call_target="tpu_custom_call" | custom-call | flops 2000000000 | tf_op jit(solution)/shard_map/pallas_call | solution.py:559
  42.6 0.9 %collective-permute-done.6.refs_0_ = bf16[128,512]{1,0:T(8,128)(2,1)S(1)} collective-permute-done((bf16[128,512]{1,0:T(8,128)(2,1)S(1)}, bf16[128,512]{1,0:T(8,128)(2,1)S(1)}, u32[]{:S(2)}, u32[]{:S(2)}) %collective-permute-start.6) | collective-permute-done | bytes 131104 | tf_op jit(solution)/shard_map/ppermute | solution.py:69
  43.5 1.7 %collective-permute-start.14 = (bf16[128,512]{1,0:T(8,128)(2,1)S(1)}, bf16[128,512]{1,0:T(8,128)(2,1)S(1)}, u32[]{:S(2)}, u32[]{:S(2)}) collective-permute-start(bf16[128,512]{1,0:T(8,128)(2,1)S(1)} %get-tuple-element.71), channel_id=1, source_target_pairs={{0,4},{2,6},{4,0},{6,2},{1,5},{3,7},{5,1},{7,3},{8,12},{10,14},{12... | collective-permute-start | bytes 393224 | tf_op jit(solution)/shard_map/ppermute | solution.py:69
  45.2 1.6 %shard_map.145 = (bf16[2,64,512]{2,1,0:T(8,128)(2,1)S(1)}, bf16[2,64,512]{2,1,0:T(8,128)(2,1)S(1)}, bf16[2,64,512]{2,1,0:T(8,128)(2,1)S(1)}, f32[2,64,512]{2,1,0:T(8,128)S(1)}) custom-call(s32[1]{0:T(128)} %bitcast.own_ref, s32[4]{0:T(128)S(1)} %pad_add_fusion.part_ref, bf16[512,512]{1,0:T(8,128)(2,1)S(1)} %bitcast.27, bf16[512,512]{1,0:T(8,128)(2,1)S(1)} %bitcast.29, ...), custom_call_target="tpu_custom_call" | custom-call | flops 2000000000 | tf_op jit(solution)/shard_map/pallas_call | solution.py:559
  46.8 0.8 %collective-permute-start.16 = (bf16[2,64,512]{2,1,0:T(8,128)(2,1)S(1)}, bf16[2,64,512]{2,1,0:T(8,128)(2,1)S(1)}, u32[]{:S(2)}, u32[]{:S(2)}) collective-permute-start(bf16[2,64,512]{2,1,0:T(8,128)(2,1)S(1)} %get-tuple-element.77), channel_id=1, source_target_pairs={{0,24},{8,16},{16,8},{24,0},{1,25},{9,17},{17,9},{25,1},{2,26},{10... | collective-permute-start | bytes 393224 | tf_op jit(solution)/shard_map/ppermute | solution.py:69
  48.1 3.2 %collective-permute-start.18 = (bf16[2,64,512]{2,1,0:T(8,128)(2,1)S(1)}, bf16[2,64,512]{2,1,0:T(8,128)(2,1)S(1)}, u32[]{:S(2)}, u32[]{:S(2)}) collective-permute-start(bf16[2,64,512]{2,1,0:T(8,128)(2,1)S(1)} %get-tuple-element.79), channel_id=1, source_target_pairs={{0,8},{8,0},{16,24},{24,16},{1,9},{9,1},{17,25},{25,17},{2,10},{10... | collective-permute-start | bytes 393224 | tf_op jit(solution)/shard_map/ppermute | solution.py:69
  51.3 1.4 %shard_map.146 = (bf16[128,512]{1,0:T(8,128)(2,1)}, bf16[128,512]{1,0:T(8,128)(2,1)}) custom-call(s32[1]{0:T(128)} %bitcast.own_ref, bf16[128,512]{1,0:T(8,128)(2,1)S(1)} %get-tuple-element.68.mixed_ref, bf16[160,512]{1,0:T(8,128)(2,1)S(1)} %get-tuple-element.43.extended_ref, bf16[128,512]{1,0:T(8,128)(2,1)S(1)} %get-tuple-element.69.refs_0_, ...), custom_call_target="tpu_custom_call" | custom-call | flops 1500000000 | tf_op jit(solution)/shard_map/pallas_call | solution.py:591
  52.7 2.4 %collective-permute-done.16.refs_0_ = bf16[2,64,512]{2,1,0:T(8,128)(2,1)S(1)} collective-permute-done((bf16[2,64,512]{2,1,0:T(8,128)(2,1)S(1)}, bf16[2,64,512]{2,1,0:T(8,128)(2,1)S(1)}, u32[]{:S(2)}, u32[]{:S(2)}) %collective-permute-start.16) | collective-permute-done | bytes 131104 | tf_op jit(solution)/shard_map/ppermute | solution.py:69
  55.1 5.3 %collective-permute-done.17.refs_1_ = bf16[2,64,512]{2,1,0:T(8,128)(2,1)S(1)} collective-permute-done((bf16[2,64,512]{2,1,0:T(8,128)(2,1)S(1)}, bf16[2,64,512]{2,1,0:T(8,128)(2,1)S(1)}, u32[]{:S(2)}, u32[]{:S(2)}) %collective-permute-start.17) | collective-permute-done | bytes 131104 | tf_op jit(solution)/shard_map/ppermute | solution.py:69
  60.4 0.7 %shard_map.147 = (f32[64,512]{1,0:T(8,128)}, f32[64,512]{1,0:T(8,128)}) custom-call(f32[2,64,512]{2,1,0:T(8,128)S(1)} %get-tuple-element.76.kept_ref, bf16[2,64,512]{2,1,0:T(8,128)(2,1)S(1)} %collective-permute-done.16.refs_0_, bf16[2,64,512]{2,1,0:T(8,128)(2,1)S(1)} %collective-permute-done.17.refs_1_, bf16[2,64,512]{2,1,0:T(8,128)(2,1)S(1)} %collective-permute-done.18.refs_2_), custom_call_target="tpu_custom_call" | custom-call | flops 500000000 | tf_op jit(solution)/shard_map/pallas_call | solution.py:598
  (44 shorter events, 2.5 us)
Async XLA Ops:
  0.6 10.9 %collective-permute-start = (bf16[128,512]{1,0:T(8,128)(2,1)}, bf16[128,512]{1,0:T(8,128)(2,1)S(1)}, u32[]{:S(2)}, u32[]{:S(2)}) collective-permute-start(bf16[128,512]{1,0:T(8,128)(2,1)} %bitcast.31), channel_id=1, source_target_pairs={{0,8},{8,16},{16,24},{24,0},{1,9},{9,17},{17,25},{25,1},{2,10},{10... | collective-permute-start | bytes 393224 | tf_op jit(solution)/shard_map/ppermute | solution.py:476
  3.7 9.6 %collective-permute-start.4 = (bf16[128,512]{1,0:T(8,128)(2,1)}, bf16[128,512]{1,0:T(8,128)(2,1)S(1)}, u32[]{:S(2)}, u32[]{:S(2)}) collective-permute-start(bf16[128,512]{1,0:T(8,128)(2,1)} %bitcast.37), channel_id=1, source_target_pairs={{0,1},{1,0},{2,3},{3,2},{4,5},{5,4},{6,7},{7,6},{8,9},{9,8},{10,11... | collective-permute-start | bytes 393224 | tf_op jit(solution)/shard_map/ppermute | solution.py:69
  5.2 7.9 %collective-permute-start.2 = (bf16[128,512]{1,0:T(8,128)(2,1)}, bf16[128,512]{1,0:T(8,128)(2,1)S(1)}, u32[]{:S(2)}, u32[]{:S(2)}) collective-permute-start(bf16[128,512]{1,0:T(8,128)(2,1)} %bitcast.34), channel_id=1, source_target_pairs={{0,8},{8,16},{16,24},{24,0},{1,9},{9,17},{17,25},{25,1},{2,10},{10... | collective-permute-start | bytes 393224 | tf_op jit(solution)/shard_map/ppermute | solution.py:476
  6.8 0.7 %copy-start.8 = (bf16[512,4]{0,1:T(4,128)(2,1)S(1)}, bf16[512,4]{0,1:T(4,128)(2,1)}, u32[]{:S(2)}) copy-start(bf16[512,4]{0,1:T(4,128)(2,1)} %param.17) | copy-start | bytes 12292
  6.9 0.7 %copy-start.9 = (s32[1,8]{1,0:T(1,128)S(1)}, s32[1,8]{1,0:T(1,128)}, u32[]{:S(2)}) copy-start(s32[1,8]{1,0:T(1,128)} %lengths_ref.1) | copy-start | bytes 100
  6.9 0.7 %copy-start.10 = (s32[1,128,1]{1,2,0:T(1,128)S(1)}, s32[1,128,1]{1,2,0:T(1,128)}, u32[]{:S(2)}) copy-start(s32[1,128,1]{1,2,0:T(1,128)} %param.18) | copy-start | bytes 1540
  7.6 0.9 %copy-start.3 = (bf16[1,128,512]{2,1,0:T(8,128)(2,1)S(1)}, bf16[1,128,512]{2,1,0:T(8,128)(2,1)}, u32[]{:S(2)}) copy-start(bf16[1,128,512]{2,1,0:T(8,128)(2,1)} %param.21) | copy-start | bytes 393220
  8.5 0.9 %copy-start.4 = (bf16[1,128,512]{2,1,0:T(8,128)(2,1)S(1)}, bf16[1,128,512]{2,1,0:T(8,128)(2,1)}, u32[]{:S(2)}) copy-start(bf16[1,128,512]{2,1,0:T(8,128)(2,1)} %param.12) | copy-start | bytes 393220
  8.5 1.0 %copy-start.5 = (bf16[1,128,512]{2,1,0:T(8,128)(2,1)S(1)}, bf16[1,128,512]{2,1,0:T(8,128)(2,1)}, u32[]{:S(2)}) copy-start(bf16[1,128,512]{2,1,0:T(8,128)(2,1)} %param.13) | copy-start | bytes 393220
  8.5 1.0 %copy-start.6 = (bf16[1,128,512]{2,1,0:T(8,128)(2,1)S(1)}, bf16[1,128,512]{2,1,0:T(8,128)(2,1)}, u32[]{:S(2)}) copy-start(bf16[1,128,512]{2,1,0:T(8,128)(2,1)} %param.11) | copy-start | bytes 393220
  11.5 7.6 %collective-permute-start.1 = (bf16[128,512]{1,0:T(8,128)(2,1)S(1)}, bf16[128,512]{1,0:T(8,128)(2,1)S(1)}, u32[]{:S(2)}, u32[]{:S(2)}) collective-permute-start(bf16[128,512]{1,0:T(8,128)(2,1)S(1)} %collective-permute-done.refs_4_), channel_id=1, source_target_pairs={{0,8},{8,16},{16,24},{24,0},{1,9},{9,17},{17,25},{25,1},{2,10},{10... | collective-permute-start | bytes 393224 | tf_op jit(solution)/shard_map/ppermute | solution.py:476
  13.1 7.4 %collective-permute-start.3 = (bf16[128,512]{1,0:T(8,128)(2,1)S(1)}, bf16[128,512]{1,0:T(8,128)(2,1)S(1)}, u32[]{:S(2)}, u32[]{:S(2)}) collective-permute-start(bf16[128,512]{1,0:T(8,128)(2,1)S(1)} %collective-permute-done.2.refs_5_), channel_id=1, source_target_pairs={{0,8},{8,16},{16,24},{24,0},{1,9},{9,17},{17,25},{25,1},{2,10},{10... | collective-permute-start | bytes 393224 | tf_op jit(solution)/shard_map/ppermute | solution.py:476
  21.3 5.3 %collective-permute-start.5 = (bf16[592,128]{1,0:T(8,128)(2,1)S(1)}, bf16[592,128]{1,0:T(8,128)(2,1)S(1)}, u32[]{:S(2)}, u32[]{:S(2)}) collective-permute-start(bf16[592,128]{1,0:T(8,128)(2,1)S(1)} %shard_map.142), channel_id=1, source_target_pairs={{0,1},{1,0},{2,3},{3,2},{4,5},{5,4},{6,7},{7,6},{8,9},{9,8},{10,11... | collective-permute-start | bytes 454664 | tf_op jit(solution)/shard_map/ppermute | solution.py:69
  22.3 4.2 %copy-start = (bf16[512,512]{1,0:T(8,128)(2,1)S(1)}, bf16[512,512]{1,0:T(8,128)(2,1)}, u32[]{:S(2)}) copy-start(bf16[512,512]{1,0:T(8,128)(2,1)} %proj_ref.1) | copy-start | bytes 1572868
  22.3 4.2 %copy-start.7 = (bf16[1,128,512]{2,1,0:T(8,128)(2,1)S(1)}, bf16[1,128,512]{2,1,0:T(8,128)(2,1)}, u32[]{:S(2)}) copy-start(bf16[1,128,512]{2,1,0:T(8,128)(2,1)} %param.15) | copy-start | bytes 393220
  26.5 14.2 %copy-start.1 = (bf16[1,512,512]{2,1,0:T(8,128)(2,1)S(1)}, bf16[1,512,512]{2,1,0:T(8,128)(2,1)}, u32[]{:S(2)}) copy-start(bf16[1,512,512]{2,1,0:T(8,128)(2,1)} %param.19) | copy-start | bytes 1572868
  26.5 14.2 %copy-start.2 = (bf16[1,512,512]{2,1,0:T(8,128)(2,1)S(1)}, bf16[1,512,512]{2,1,0:T(8,128)(2,1)}, u32[]{:S(2)}) copy-start(bf16[1,512,512]{2,1,0:T(8,128)(2,1)} %param.20) | copy-start | bytes 1572868
  27.2 5.0 %collective-permute-start.10 = (bf16[128,512]{1,0:T(8,128)(2,1)S(1)}, bf16[128,512]{1,0:T(8,128)(2,1)S(1)}, u32[]{:S(2)}, u32[]{:S(2)}) collective-permute-start(bf16[128,512]{1,0:T(8,128)(2,1)S(1)} %get-tuple-element.62), channel_id=1, source_target_pairs={{0,2},{1,3},{2,0},{3,1},{4,6},{5,7},{6,4},{7,5},{8,10},{9,11},{10,... | collective-permute-start | bytes 393224 | tf_op jit(solution)/shard_map/ppermute | solution.py:69
  27.3 6.4 %collective-permute-start.11 = (bf16[128,512]{1,0:T(8,128)(2,1)S(1)}, bf16[128,512]{1,0:T(8,128)(2,1)S(1)}, u32[]{:S(2)}, u32[]{:S(2)}) collective-permute-start(bf16[128,512]{1,0:T(8,128)(2,1)S(1)} %get-tuple-element.63), channel_id=1, source_target_pairs={{0,4},{1,5},{2,6},{3,7},{4,0},{5,1},{6,2},{7,3},{8,12},{9,13},{10,... | collective-permute-start | bytes 393224 | tf_op jit(solution)/shard_map/ppermute | solution.py:69
  28.9 11.8 %collective-permute-start.12 = (bf16[128,512]{1,0:T(8,128)(2,1)S(1)}, bf16[128,512]{1,0:T(8,128)(2,1)S(1)}, u32[]{:S(2)}, u32[]{:S(2)}) collective-permute-start(bf16[128,512]{1,0:T(8,128)(2,1)S(1)} %get-tuple-element.64), channel_id=1, source_target_pairs={{0,6},{1,7},{2,4},{3,5},{4,2},{5,3},{6,0},{7,1},{8,14},{9,15},{10,... | collective-permute-start | bytes 393224 | tf_op jit(solution)/shard_map/ppermute | solution.py:69
  29.2 15.9 %collective-permute-start.7 = (bf16[128,512]{1,0:T(8,128)(2,1)S(1)}, bf16[128,512]{1,0:T(8,128)(2,1)S(1)}, u32[]{:S(2)}, u32[]{:S(2)}) collective-permute-start(bf16[128,512]{1,0:T(8,128)(2,1)S(1)} %get-tuple-element.62), channel_id=1, source_target_pairs={{0,3},{1,2},{2,1},{3,0},{4,7},{5,6},{6,5},{7,4},{8,11},{9,10},{10,... | collective-permute-start | bytes 393224 | tf_op jit(solution)/shard_map/ppermute | solution.py:69
  30.1 15.1 %collective-permute-start.8 = (bf16[128,512]{1,0:T(8,128)(2,1)S(1)}, bf16[128,512]{1,0:T(8,128)(2,1)S(1)}, u32[]{:S(2)}, u32[]{:S(2)}) collective-permute-start(bf16[128,512]{1,0:T(8,128)(2,1)S(1)} %get-tuple-element.63), channel_id=1, source_target_pairs={{0,5},{1,4},{2,7},{3,6},{4,1},{5,0},{6,3},{7,2},{8,13},{9,12},{10,... | collective-permute-start | bytes 393224 | tf_op jit(solution)/shard_map/ppermute | solution.py:69
  32.2 13.0 %collective-permute-start.9 = (bf16[128,512]{1,0:T(8,128)(2,1)S(1)}, bf16[128,512]{1,0:T(8,128)(2,1)S(1)}, u32[]{:S(2)}, u32[]{:S(2)}) collective-permute-start(bf16[128,512]{1,0:T(8,128)(2,1)S(1)} %get-tuple-element.64), channel_id=1, source_target_pairs={{0,7},{1,6},{2,5},{3,4},{4,3},{5,2},{6,1},{7,0},{8,15},{9,14},{10,... | collective-permute-start | bytes 393224 | tf_op jit(solution)/shard_map/ppermute | solution.py:69
  33.7 9.8 %collective-permute-start.6 = (bf16[128,512]{1,0:T(8,128)(2,1)S(1)}, bf16[128,512]{1,0:T(8,128)(2,1)S(1)}, u32[]{:S(2)}, u32[]{:S(2)}) collective-permute-start(bf16[128,512]{1,0:T(8,128)(2,1)S(1)} %get-tuple-element.61.refs_0_), channel_id=1, source_target_pairs={{0,1},{1,0},{2,3},{3,2},{4,5},{5,4},{6,7},{7,6},{8,9},{9,8},{10,11... | collective-permute-start | bytes 393224 | tf_op jit(solution)/shard_map/ppermute | solution.py:69
  42.5 5.6 %collective-permute-start.13 = (bf16[128,512]{1,0:T(8,128)(2,1)S(1)}, bf16[128,512]{1,0:T(8,128)(2,1)S(1)}, u32[]{:S(2)}, u32[]{:S(2)}) collective-permute-start(bf16[128,512]{1,0:T(8,128)(2,1)S(1)} %get-tuple-element.70), channel_id=1, source_target_pairs={{0,2},{2,0},{4,6},{6,4},{1,3},{3,1},{5,7},{7,5},{8,10},{10,8},{12,... | collective-permute-start | bytes 393224 | tf_op jit(solution)/shard_map/ppermute | solution.py:69
  43.5 7.8 %collective-permute-start.14 = (bf16[128,512]{1,0:T(8,128)(2,1)S(1)}, bf16[128,512]{1,0:T(8,128)(2,1)S(1)}, u32[]{:S(2)}, u32[]{:S(2)}) collective-permute-start(bf16[128,512]{1,0:T(8,128)(2,1)S(1)} %get-tuple-element.71), channel_id=1, source_target_pairs={{0,4},{2,6},{4,0},{6,2},{1,5},{3,7},{5,1},{7,3},{8,12},{10,14},{12... | collective-permute-start | bytes 393224 | tf_op jit(solution)/shard_map/ppermute | solution.py:69
  45.2 6.1 %collective-permute-start.15 = (bf16[128,512]{1,0:T(8,128)(2,1)S(1)}, bf16[128,512]{1,0:T(8,128)(2,1)S(1)}, u32[]{:S(2)}, u32[]{:S(2)}) collective-permute-start(bf16[128,512]{1,0:T(8,128)(2,1)S(1)} %get-tuple-element.72), channel_id=1, source_target_pairs={{0,6},{2,4},{4,2},{6,0},{1,7},{3,5},{5,3},{7,1},{8,14},{10,12},{12... | collective-permute-start | bytes 393224 | tf_op jit(solution)/shard_map/ppermute | solution.py:69
  46.8 8.3 %collective-permute-start.16 = (bf16[2,64,512]{2,1,0:T(8,128)(2,1)S(1)}, bf16[2,64,512]{2,1,0:T(8,128)(2,1)S(1)}, u32[]{:S(2)}, u32[]{:S(2)}) collective-permute-start(bf16[2,64,512]{2,1,0:T(8,128)(2,1)S(1)} %get-tuple-element.77), channel_id=1, source_target_pairs={{0,24},{8,16},{16,8},{24,0},{1,25},{9,17},{17,9},{25,1},{2,26},{10... | collective-permute-start | bytes 393224 | tf_op jit(solution)/shard_map/ppermute | solution.py:69
  47.6 12.8 %collective-permute-start.17 = (bf16[2,64,512]{2,1,0:T(8,128)(2,1)S(1)}, bf16[2,64,512]{2,1,0:T(8,128)(2,1)S(1)}, u32[]{:S(2)}, u32[]{:S(2)}) collective-permute-start(bf16[2,64,512]{2,1,0:T(8,128)(2,1)S(1)} %get-tuple-element.78), channel_id=1, source_target_pairs={{0,16},{8,24},{16,0},{24,8},{1,17},{9,25},{17,1},{25,9},{2,18},{10... | collective-permute-start | bytes 393224 | tf_op jit(solution)/shard_map/ppermute | solution.py:69
  48.1 12.3 %collective-permute-start.18 = (bf16[2,64,512]{2,1,0:T(8,128)(2,1)S(1)}, bf16[2,64,512]{2,1,0:T(8,128)(2,1)S(1)}, u32[]{:S(2)}, u32[]{:S(2)}) collective-permute-start(bf16[2,64,512]{2,1,0:T(8,128)(2,1)S(1)} %get-tuple-element.79), channel_id=1, source_target_pairs={{0,8},{8,0},{16,24},{24,16},{1,9},{9,1},{17,25},{25,17},{2,10},{10... | collective-permute-start | bytes 393224 | tf_op jit(solution)/shard_map/ppermute | solution.py:69

commit v15 on v13

--- a/solution.py
+++ b/solution.py
@@ -324,7 +324,7 @@
     own_rows = rep_list[0] == 0
     held_ref, refs = refs[-1], refs[:-1]
     if own_rows:
-        back_refs, (up_acc, down_acc) = refs[:-2], refs[-2:]
+        activated_ref, pre_grad_ref, up_acc, down_acc = refs
     else:
         up_old, down_old = refs[:2]
         term_refs, kept_ref = refs[2:-1], refs[-1]
@@ -364,11 +364,8 @@
             jnp.bfloat16
         )
         if own_rows:
-            produced = dot(activated, down).astype(jnp.bfloat16)
-            token_grad = dot(pre_grad, up, NT).astype(jnp.bfloat16)
-            for k, back_ref in enumerate(back_refs):
-                back_ref[0:capacity] = produced[k * capacity : (k + 1) * capacity]
-                back_ref[capacity : 2 * capacity] = token_grad[k * capacity : (k + 1) * capacity]
+            activated_ref[...] = activated
+            pre_grad_ref[...] = pre_grad
         more_up = dot(strips(rows, 2 * place), pre_grad)
         more_down = dot(strips(activated, 2 * place + 1), scaled)
         up_term = more_up if up_term is None else up_term + more_up
@@ -385,13 +382,30 @@
         ref[1] = down_term[rows].astype(ref.dtype)
 
 
-def finish_kernel(
-    hot_capacity, expert_count, own_ref, mixed_ref, extended_ref, *refs
+def back_kernel(sources, up_ref, down_ref, activated_ref, pre_grad_ref, *back_refs):
+    capacity = activated_ref.shape[0] // sources
+    produced = dot(activated_ref[...], down_ref[...]).astype(jnp.bfloat16)
+    token_grad = dot(pre_grad_ref[...], up_ref[...], NT).astype(jnp.bfloat16)
+    for k, back_ref in enumerate(back_refs):
+        rows = slice(k * capacity, (k + 1) * capacity)
+        back_ref[0:capacity] = produced[rows]
+        back_ref[capacity : 2 * capacity] = token_grad[rows]
+
+
+def prepare_kernel(
+    hot_capacity,
+    expert_count,
+    own_ref,
+    mixed_ref,
+    extended_ref,
+    placed_ref,
+    factors_ref,
+    router_cols_ref,
 ):
-    back_refs, (layer_ref, grad_mixed_ref) = refs[:-2], refs[-2:]
     tok = mixed_ref.shape[0]
     choice = chosen_of(extended_ref, tok)
     placed = slot_matrix(choice, own_ref[0], expert_count, hot_capacity)
+    placed_ref[...] = placed.T
     router = router_of(extended_ref, tok, expert_count)
     mixed_f = mixed_ref[...].astype(jnp.float32)
     inv_rms = lax.rsqrt(jnp.mean(mixed_f * mixed_f, axis=1, keepdims=True) + norm_eps)
@@ -399,22 +413,40 @@
     one_hot = lax.broadcasted_iota(jnp.int32, (expert_count, tok), 0) == choice
     logits = dot(router, normed, NT)
     logit_row = jnp.sum(jnp.where(one_hot, logits, 0.0), axis=0, keepdims=True)
-    logit = jnp.broadcast_to(logit_row, (8, tok)).T[:, 0:1]
-    gate = jax.nn.sigmoid(logit)
+    gate = jax.nn.sigmoid(jnp.broadcast_to(logit_row, (8, tok)).T[:, 0:1])
+    lane = lax.broadcasted_iota(jnp.int32, factors_ref.shape, 1)
+    factors_ref[...] = jnp.where(lane == 0, inv_rms, gate)
+    router_cols_ref[...] = dot(one_hot.astype(jnp.float32).astype(jnp.bfloat16), router, TN)
+
+
+def finish_kernel(
+    hot_capacity,
+    placed_ref,
+    factors_ref,
+    router_cols_ref,
+    mixed_ref,
+    extended_ref,
+    *refs,
+):
+    back_refs, (layer_ref, grad_mixed_ref) = refs[:-2][::-1], refs[-2:]
+    tok = mixed_ref.shape[0]
+    mixed_f = mixed_ref[...].astype(jnp.float32)
+    inv_rms = factors_ref[:, 0:1]
+    gate = factors_ref[:, 1:2]
     pair = 2 * hot_capacity
     chunks = [
         ref[first : first + pair] for ref in back_refs for first in range(0, ref.shape[0], pair)
     ]
     results = jnp.concatenate([chunk[:hot_capacity] for chunk in chunks], axis=0)
     grads = jnp.concatenate([chunk[hot_capacity:] for chunk in chunks], axis=0)
-    result_f = dot(placed, results, TN)
-    normed_grad = dot(placed, grads, TN)
+    placed = placed_ref[...]
+    result_f = dot(placed, results)
+    normed_grad = dot(placed, grads)
     grad_f = extended_ref[0:tok, :].astype(jnp.float32)
     layer_ref[...] = (mixed_f + gate * result_f).astype(jnp.bfloat16)
     gate_grad = jnp.sum(grad_f * result_f, axis=1, keepdims=True)
     logit_grad = gate_grad * gate * (1.0 - gate)
-    router_cols = dot(one_hot.astype(jnp.float32).astype(jnp.bfloat16), router, TN)
-    total_grad = normed_grad + logit_grad * router_cols
+    total_grad = normed_grad + logit_grad * router_cols_ref[...]
     mean_term = jnp.mean(total_grad * mixed_f, axis=1, keepdims=True)
     input_grad = inv_rms * total_grad - mixed_f * inv_rms * inv_rms * inv_rms * mean_term
     grad_mixed_ref[...] = (grad_f + input_grad).astype(jnp.bfloat16)
@@ -596,15 +628,18 @@
             cost=2.0,
         )(own, part_to, weight_in[0], weight_out[0], extendeds[0], *rows, *got_grads, *extra)
 
-    *back, up_acc, down_acc = expert_call(
+    slots = expert_count * hot_capacity
+    activated, pre_grad, up_acc, down_acc = expert_call(
         (0,),
         got_rows,
-        [shape((2 * hot_capacity, width))] * expert_count
-        + [shape((seq_count * strip, hidden), jnp.float32)]
-        + [shape((seq_count * strip, width), jnp.float32)],
+        [
+            shape((slots, hidden)),
+            shape((slots, hidden)),
+            shape((seq_count * strip, hidden), jnp.float32),
+            shape((seq_count * strip, width), jnp.float32),
+        ],
         [],
     )
-    got_back = merged(experts.exchange(back, inverse=True), MOST_PERMUTES)
     *terms, kept = expert_call(
         tuple(range(1, rep_count)),
         got_more,
@@ -613,13 +648,30 @@
         [up_acc, down_acc],
     )
     got_terms = parts.exchange([None] + terms)[1:]
+    activated, mixed, kept = lax.optimization_barrier((activated, mixed, kept))
+    back = call(
+        functools.partial(back_kernel, expert_count),
+        [shape((2 * hot_capacity, width))] * expert_count,
+        [VMEM] * 4,
+        cost=1.0,
+    )(weight_in[0], weight_out[0], activated, pre_grad)
+    got_back = merged(experts.exchange(back, inverse=True), MOST_PERMUTES)
+    prepared = call(
+        functools.partial(prepare_kernel, hot_capacity, expert_count),
+        [
+            shape((tok, slots)),
+            shape((tok, 128), jnp.float32),
+            shape((tok, width), jnp.float32),
+        ],
+        [SMEM, VMEM, VMEM],
+        cost=1.0,
+    )(own, mixed, extended)
     layer_out, grad_mixed = call(
-        functools.partial(finish_kernel, hot_capacity, expert_count),
+        functools.partial(finish_kernel, hot_capacity),
         [shape((tok, width)), shape((tok, width))],
-        [SMEM] + [VMEM] * (2 + len(got_back)),
-        cost=1.5,
-    )(own, mixed, extended, *got_back)
-    kept, layer_out = lax.optimization_barrier((kept, layer_out))
+        [VMEM] * (5 + len(got_back)),
+        cost=1.0,
+    )(*prepared, mixed, extended, *got_back[::-1])
     share_in, share_out = call(
         sum_kernel,
         [shape((strip, hidden), jnp.float32), shape((strip, width), jnp.float32)],

time: 56.5 us -> 56.9 us (level)
  starting transfers between devices: 25.7 us -> 22.9 us
  waiting for transfers between devices: 15.3 us -> 18 us
    ppermute x19, waiting for transfers between devices: 10.1 us -> 12.1 us  [exchange(): got[k] = lax.ppermute(chunks[k], self.axes, pairs)]
    ppermute x4, starting transfers between devices: 6.31 us -> 4.4 us  [forward(): lax.ppermute(array, 'seq', [(i, (i + 1) % seq_count) for i in range(seq_c...]
    ppermute x19, starting transfers between devices: 19.4 us -> 18.5 us  [exchange(): got[k] = lax.ppermute(chunks[k], self.axes, pairs)]
    ppermute x4, waiting for transfers between devices: 5.15 us -> 5.86 us  [forward(): lax.ppermute(array, 'seq', [(i, (i + 1) % seq_count) for i in range(seq_c...]
    pallas_call x1 -> x3, Pallas kernels: 1.42 us -> 2.04 us  [the longest x1 1.14 us: local(): call(functools.partial(finish_kernel, hot_capacity), [shape((tok, width))...]
  transfers between devices with their start and end apart: 23 -> 23, of which waited for: 9 -> 9; matrix products, arithmetic and copies ran while one was open for 1% -> 1% of each run, Pallas kernels for 21% -> 18%
where the time goes in v15:
time: 56.9 us; the launch traced here: 56.7 us
  starting transfers between devices  22.9 us (40%)
  waiting for transfers between devices  18 us (32%)
  Pallas kernels  12.9 us (23%)
  local copies, waits for them, and re-layouts  1.69 us (3%)
  between operations  0.81 us (1%)
    ppermute x19, starting transfers between devices, exchange(): got[k] = lax.ppermute(chunks[k], self.axes, pairs)  18.5 us
    ppermute x19, waiting for transfers between devices, exchange(): got[k] = lax.ppermute(chunks[k], self.axes, pairs)  12.1 us
    ppermute x4, waiting for transfers between devices, forward(): lax.ppermute(array, 'seq', [(i, (i + 1) % seq_count) for i in range(seq_c...  5.86 us
    pallas_call x4, Pallas kernels, attend(): call(functools.partial(attend_kernel, plan, rep_count, len(pairs), packed...  5.19 us
    ppermute x4, starting transfers between devices, forward(): lax.ppermute(array, 'seq', [(i, (i + 1) % seq_count) for i in range(seq_c...  4.4 us
    pallas_call x2, Pallas kernels, expert_call(): call(functools.partial(expert_kernel, rep_count, rep_list, expert_count,...  3.25 us
    unnamed x22, local copies, waits for them, and re-layouts  1.6 us
    pallas_call x1, Pallas kernels, local(): call(functools.partial(finish_kernel, hot_capacity), [shape((tok, width))...  1.14 us
  transfers between devices with their start and end apart: 23, of which 9 were waited for; matrix products, arithmetic and copies ran while one was open for 1% of the time, Pallas kernels for 18%

profile of v15, /device:TPU:0, one launch (start us, length us, event | category | flops | bytes accessed | tf_op | source)
XLA Modules:
  0.0 56.7 jit_solution(6676942130934284560)
XLA Ops:
  0.6 3.0 %collective-permute-start.4 = (bf16[128,512]{1,0:T(8,128)(2,1)}, bf16[128,512]{1,0:T(8,128)(2,1)S(1)}, u32[]{:S(2)}, u32[]{:S(2)}) collective-permute-start(bf16[128,512]{1,0:T(8,128)(2,1)} %bitcast.39), channel_id=1, source_target_pairs={{0,1},{1,0},{2,3},{3,2},{4,5},{5,4},{6,7},{7,6},{8,9},{9,8},{10,11... | collective-permute-start | bytes 393224 | tf_op jit(solution)/shard_map/ppermute | solution.py:69
  3.6 1.6 %collective-permute-start = (bf16[128,512]{1,0:T(8,128)(2,1)}, bf16[128,512]{1,0:T(8,128)(2,1)S(1)}, u32[]{:S(2)}, u32[]{:S(2)}) collective-permute-start(bf16[128,512]{1,0:T(8,128)(2,1)} %bitcast.33), channel_id=1, source_target_pairs={{0,8},{8,16},{16,24},{24,0},{1,9},{9,17},{17,25},{25,1},{2,10},{10... | collective-permute-start | bytes 393224 | tf_op jit(solution)/shard_map/ppermute | solution.py:523
  5.2 1.6 %collective-permute-start.2 = (bf16[128,512]{1,0:T(8,128)(2,1)}, bf16[128,512]{1,0:T(8,128)(2,1)S(1)}, u32[]{:S(2)}, u32[]{:S(2)}) collective-permute-start(bf16[128,512]{1,0:T(8,128)(2,1)} %bitcast.36), channel_id=1, source_target_pairs={{0,8},{8,16},{16,24},{24,0},{1,9},{9,17},{17,25},{25,1},{2,10},{10... | collective-permute-start | bytes 393224 | tf_op jit(solution)/shard_map/ppermute | solution.py:523
  6.9 0.6 %copy-done.8 = bf16[512,4]{0,1:T(4,128)(2,1)S(1)} copy-done((bf16[512,4]{0,1:T(4,128)(2,1)S(1)}, bf16[512,4]{0,1:T(4,128)(2,1)}, u32[]{:S(2)}) %copy-start.8) | copy-done | bytes 4120
  7.5 0.9 %copy-done.3 = bf16[1,128,512]{2,1,0:T(8,128)(2,1)S(1)} copy-done((bf16[1,128,512]{2,1,0:T(8,128)(2,1)S(1)}, bf16[1,128,512]{2,1,0:T(8,128)(2,1)}, u32[]{:S(2)}) %copy-start.3) | copy-done | bytes 131096
  9.0 0.6 %collective-permute-start.5 = (bf16[160,512]{1,0:T(8,128)(2,1)S(1)}, bf16[160,512]{1,0:T(8,128)(2,1)S(1)}, u32[]{:S(2)}, u32[]{:S(2)}) collective-permute-start(bf16[160,512]{1,0:T(8,128)(2,1)S(1)} %get-tuple-element.55.extended_ref.refs_0_), channel_id=1, source_target_pairs={{0,1},{1,0},{2,3},{3,2},{4,5},{5,4},{6,7},{7,6},{8,9},{9,8},{10,11... | collective-permute-start | bytes 491528 | tf_op jit(solution)/shard_map/ppermute | solution.py:69
  9.7 1.7 %shard_map.139 = (f32[16,128]{1,0:T(8,128)S(1)}, f32[16,128]{1,0:T(8,128)S(1)}, f32[512,128]{1,0:T(8,128)S(1)}) custom-call(s32[3]{0:T(128)S(1)} %pad_add_fusion.4.ids_ref, s32[2,128]{1,0:T(2,128)S(1)} %get-tuple-element.56.begin_ref, bf16[128,512]{1,0:T(8,128)(2,1)S(1)} %bitcast.40, bf16[128,512]{1,0:T(8,128)(2,1)S(1)} %bitcast.34, ...), custom_call_target="tpu_custom_call" | custom-call | flops 2000000000 | tf_op jit(solution)/shard_map/pallas_call | solution.py:562
  12.1 1.2 %collective-permute-start.1 = (bf16[128,512]{1,0:T(8,128)(2,1)S(1)}, bf16[128,512]{1,0:T(8,128)(2,1)S(1)}, u32[]{:S(2)}, u32[]{:S(2)}) collective-permute-start(bf16[128,512]{1,0:T(8,128)(2,1)S(1)} %collective-permute-done.refs_4_), channel_id=1, source_target_pairs={{0,8},{8,16},{16,24},{24,0},{1,9},{9,17},{17,25},{25,1},{2,10},{10... | collective-permute-start | bytes 393224 | tf_op jit(solution)/shard_map/ppermute | solution.py:523
  13.5 1.9 %shard_map.140 = (f32[16,128]{1,0:T(8,128)S(1)}, f32[16,128]{1,0:T(8,128)S(1)}, f32[512,128]{1,0:T(8,128)S(1)}, f32[16,128]{1,0:T(8,128)S(1)}, f32[16,128]{1,0:T(8,128)S(1)}, /*index=5*/f32[512,128]{1,0:T(8,128)S(1)}) custom-call(s32[5]{0:T(128)S(1)} %stack.81.ids_ref, s32[2,128]{1,0:T(2,128)S(1)} %get-tuple-element.56.begin_ref, ...), custom_call_target="tpu_custom_call" | custom-call | flops 4000000000 | tf_op jit(solution)/shard_map/pallas_call | solution.py:562
  15.4 5.4 %collective-permute-done.3.refs_2_ = bf16[128,512]{1,0:T(8,128)(2,1)S(1)} collective-permute-done((bf16[128,512]{1,0:T(8,128)(2,1)S(1)}, bf16[128,512]{1,0:T(8,128)(2,1)S(1)}, u32[]{:S(2)}, u32[]{:S(2)}) %collective-permute-start.3) | collective-permute-done | bytes 131104 | tf_op jit(solution)/shard_map/ppermute | solution.py:523
  20.8 0.8 %shard_map.142 = bf16[592,128]{1,0:T(8,128)(2,1)S(1)} custom-call(s32[3]{0:T(128)S(1)} %pad_add_fusion.5.ids_ref, s32[2,128]{1,0:T(2,128)S(1)} %get-tuple-element.56.begin_ref, bf16[128,512]{1,0:T(8,128)(2,1)S(1)} %collective-permute-done.4.refs_1_.refs_0_, bf16[128,512]{1,0:T(8,128)(2,1)S(1)} %collective-permute-done.1.refs_1_, ...), custom_call_target="tpu_custom_call" | custom-call | flops 1500000000 | tf_op jit(solution)/shard_map/pallas_call | solution.py:562
  21.6 1.2 %collective-permute-start.6 = (bf16[592,128]{1,0:T(8,128)(2,1)S(1)}, bf16[592,128]{1,0:T(8,128)(2,1)S(1)}, u32[]{:S(2)}, u32[]{:S(2)}) collective-permute-start(bf16[592,128]{1,0:T(8,128)(2,1)S(1)} %shard_map.142), channel_id=1, source_target_pairs={{0,1},{1,0},{2,3},{3,2},{4,5},{5,4},{6,7},{7,6},{8,9},{9,8},{10,11... | collective-permute-start | bytes 454664 | tf_op jit(solution)/shard_map/ppermute | solution.py:69
  23.4 1.6 %collective-permute-start.11 = (bf16[128,512]{1,0:T(8,128)(2,1)S(1)}, bf16[128,512]{1,0:T(8,128)(2,1)S(1)}, u32[]{:S(2)}, u32[]{:S(2)}) collective-permute-start(bf16[128,512]{1,0:T(8,128)(2,1)S(1)} %get-tuple-element.81), channel_id=1, source_target_pairs={{0,4},{2,6},{4,0},{6,2},{1,5},{3,7},{5,1},{7,3},{8,12},{10,14},{12... | collective-permute-start | bytes 393224 | tf_op jit(solution)/shard_map/ppermute | solution.py:69
  25.3 0.7 %shard_map.141 = (f32[16,128]{1,0:T(8,128)S(1)}, f32[16,128]{1,0:T(8,128)S(1)}, f32[512,128]{1,0:T(8,128)S(1)}) custom-call(s32[3]{0:T(128)S(1)} %pad_add_fusion.2.ids_ref, s32[2,128]{1,0:T(2,128)S(1)} %get-tuple-element.56.begin_ref, bf16[128,512]{1,0:T(8,128)(2,1)S(1)} %bitcast.42, bf16[128,512]{1,0:T(8,128)(2,1)S(1)} %collective-permute-done.1.refs_1_, ...), custom_call_target="tpu_custom_call" | custom-call | flops 1500000000 | tf_op jit(solution)/shard_map/pallas_call | solution.py:562
  26.0 0.8 %collective-permute-done.6.refs_3_ = bf16[592,128]{1,0:T(8,128)(2,1)S(1)} collective-permute-done((bf16[592,128]{1,0:T(8,128)(2,1)S(1)}, bf16[592,128]{1,0:T(8,128)(2,1)S(1)}, u32[]{:S(2)}, u32[]{:S(2)}) %collective-permute-start.6) | collective-permute-done | bytes 151584 | tf_op jit(solution)/shard_map/ppermute | solution.py:69
  26.8 0.6 %shard_map.143 = (bf16[128,512]{1,0:T(8,128)(2,1)S(1)}, bf16[64,512]{1,0:T(8,128)(2,1)S(1)}, bf16[64,512]{1,0:T(8,128)(2,1)S(1)}, bf16[64,512]{1,0:T(8,128)(2,1)S(1)}, bf16[64,512]{1,0:T(8,128)(2,1)S(1)}) custom-call(s32[1]{0:T(128)} %bitcast.own_ref, bf16[160,512]{1,0:T(8,128)(2,1)S(1)} %get-tuple-element.55.extended_ref.refs_0_, ...), custom_call_target="tpu_custom_call" | custom-call | flops 2000000000 | tf_op jit(solution)/shard_map/pallas_call | solution.py:602
  27.5 1.6 %collective-permute-start.8 = (bf16[64,512]{1,0:T(8,128)(2,1)S(1)}, bf16[64,512]{1,0:T(8,128)(2,1)S(1)}, u32[]{:S(2)}, u32[]{:S(2)}) collective-permute-start(bf16[64,512]{1,0:T(8,128)(2,1)S(1)} %get-tuple-element.76), channel_id=1, source_target_pairs={{0,4},{1,5},{2,6},{3,7},{4,0},{5,1},{6,2},{7,3},{8,12},{9,13},{10,... | collective-permute-start | bytes 196616 | tf_op jit(solution)/shard_map/ppermute | solution.py:69
  29.8 0.8 %collective-permute-start.14 = (bf16[64,512]{1,0:T(8,128)(2,1)S(1)}, bf16[64,512]{1,0:T(8,128)(2,1)S(1)}, u32[]{:S(2)}, u32[]{:S(2)}) collective-permute-start(bf16[64,512]{1,0:T(8,128)(2,1)S(1)} %get-tuple-element.75), channel_id=1, source_target_pairs={{0,3},{1,2},{2,1},{3,0},{4,7},{5,6},{6,5},{7,4},{8,11},{9,10},{10,... | collective-permute-start | bytes 196616 | tf_op jit(solution)/shard_map/ppermute | solution.py:69
  30.6 1.1 %collective-permute-done.12.refs_7_ = bf16[128,512]{1,0:T(8,128)(2,1)S(1)} collective-permute-done((bf16[128,512]{1,0:T(8,128)(2,1)S(1)}, bf16[128,512]{1,0:T(8,128)(2,1)S(1)}, u32[]{:S(2)}, u32[]{:S(2)}) %collective-permute-start.12) | collective-permute-done | bytes 131104 | tf_op jit(solution)/shard_map/ppermute | solution.py:69
  31.7 1.8 %collective-permute-start.15 = (bf16[64,512]{1,0:T(8,128)(2,1)S(1)}, bf16[64,512]{1,0:T(8,128)(2,1)S(1)}, u32[]{:S(2)}, u32[]{:S(2)}) collective-permute-start(bf16[64,512]{1,0:T(8,128)(2,1)S(1)} %get-tuple-element.76), channel_id=1, source_target_pairs={{0,5},{1,4},{2,7},{3,6},{4,1},{5,0},{6,3},{7,2},{8,13},{9,12},{10,... | collective-permute-start | bytes 196616 | tf_op jit(solution)/shard_map/ppermute | solution.py:69
  33.5 1.2 %collective-permute-start.16 = (bf16[64,512]{1,0:T(8,128)(2,1)S(1)}, bf16[64,512]{1,0:T(8,128)(2,1)S(1)}, u32[]{:S(2)}, u32[]{:S(2)}) collective-permute-start(bf16[64,512]{1,0:T(8,128)(2,1)S(1)} %get-tuple-element.77), channel_id=1, source_target_pairs={{0,7},{1,6},{2,5},{3,4},{4,3},{5,2},{6,1},{7,0},{8,15},{9,14},{10,... | collective-permute-start | bytes 196616 | tf_op jit(solution)/shard_map/ppermute | solution.py:69
  34.7 0.9 %collective-permute-start.13 = (bf16[64,512]{1,0:T(8,128)(2,1)S(1)}, bf16[64,512]{1,0:T(8,128)(2,1)S(1)}, u32[]{:S(2)}, u32[]{:S(2)}) collective-permute-start(bf16[64,512]{1,0:T(8,128)(2,1)S(1)} %get-tuple-element.74.refs_0_), channel_id=1, source_target_pairs={{0,1},{1,0},{2,3},{3,2},{4,5},{5,4},{6,7},{7,6},{8,9},{9,8},{10,11... | collective-permute-start | bytes 196616 | tf_op jit(solution)/shard_map/ppermute | solution.py:69
  35.6 1.6 %shard_map.145 = (bf16[256,512]{1,0:T(8,128)(2,1)S(1)}, bf16[256,512]{1,0:T(8,128)(2,1)S(1)}, f32[256,512]{1,0:T(8,128)S(1)}, f32[256,512]{1,0:T(8,128)S(1)}) custom-call(s32[1]{0:T(128)} %bitcast.own_ref, s32[4]{0:T(128)S(1)} %pad_add_fusion.part_ref, bf16[512,512]{1,0:T(8,128)(2,1)S(1)} %bitcast.26, bf16[512,512]{1,0:T(8,128)(2,1)S(1)} %bitcast.29, ...), custom_call_target="tpu_custom_call" | custom-call | flops 2000000000 | tf_op jit(solution)/shard_map/pallas_call | solution.py:615
  37.2 3.0 %collective-permute-done.13.refs_0_ = bf16[64,512]{1,0:T(8,128)(2,1)S(1)} collective-permute-done((bf16[64,512]{1,0:T(8,128)(2,1)S(1)}, bf16[64,512]{1,0:T(8,128)(2,1)S(1)}, u32[]{:S(2)}, u32[]{:S(2)}) %collective-permute-start.13) | collective-permute-done | bytes 65568 | tf_op jit(solution)/shard_map/ppermute | solution.py:69
  40.2 1.6 %shard_map.146 = (bf16[2,64,512]{2,1,0:T(8,128)(2,1)S(1)}, bf16[2,64,512]{2,1,0:T(8,128)(2,1)S(1)}, bf16[2,64,512]{2,1,0:T(8,128)(2,1)S(1)}, f32[2,64,512]{2,1,0:T(8,128)S(1)}) custom-call(s32[1]{0:T(128)} %bitcast.own_ref, s32[4]{0:T(128)S(1)} %pad_add_fusion.part_ref, bf16[512,512]{1,0:T(8,128)(2,1)S(1)} %bitcast.27, bf16[512,512]{1,0:T(8,128)(2,1)S(1)} %bitcast.30, ...), custom_call_target="tpu_custom_call" | custom-call | flops 2000000000 | tf_op jit(solution)/shard_map/pallas_call | solution.py:615
  41.8 1.7 %collective-permute-start.20 = (bf16[2,64,512]{2,1,0:T(8,128)(2,1)S(1)}, bf16[2,64,512]{2,1,0:T(8,128)(2,1)S(1)}, u32[]{:S(2)}, u32[]{:S(2)}) collective-permute-start(bf16[2,64,512]{2,1,0:T(8,128)(2,1)S(1)} %get-tuple-element.101), channel_id=1, source_target_pairs={{0,24},{8,16},{16,8},{24,0},{1,25},{9,17},{17,9},{25,1},{2,26},{10... | collective-permute-start | bytes 393224 | tf_op jit(solution)/shard_map/ppermute | solution.py:69
  43.5 2.8 %collective-permute-start.22 = (bf16[2,64,512]{2,1,0:T(8,128)(2,1)S(1)}, bf16[2,64,512]{2,1,0:T(8,128)(2,1)S(1)}, u32[]{:S(2)}, u32[]{:S(2)}) collective-permute-start(bf16[2,64,512]{2,1,0:T(8,128)(2,1)S(1)} %get-tuple-element.103), channel_id=1, source_target_pairs={{0,8},{8,0},{16,24},{24,16},{1,9},{9,1},{17,25},{25,17},{2,10},{10... | collective-permute-start | bytes 393224 | tf_op jit(solution)/shard_map/ppermute | solution.py:69
  46.8 0.7 %collective-permute-start.18 = (bf16[128,512]{1,0:T(8,128)(2,1)S(1)}, bf16[128,512]{1,0:T(8,128)(2,1)S(1)}, u32[]{:S(2)}, u32[]{:S(2)}) collective-permute-start(bf16[128,512]{1,0:T(8,128)(2,1)S(1)} %get-tuple-element.95), channel_id=1, source_target_pairs={{0,4},{2,6},{4,0},{6,2},{1,5},{3,7},{5,1},{7,3},{8,12},{10,14},{12... | collective-permute-start | bytes 393224 | tf_op jit(solution)/shard_map/ppermute | solution.py:69
  47.5 2.7 %collective-permute-done.20.refs_0_ = bf16[2,64,512]{2,1,0:T(8,128)(2,1)S(1)} collective-permute-done((bf16[2,64,512]{2,1,0:T(8,128)(2,1)S(1)}, bf16[2,64,512]{2,1,0:T(8,128)(2,1)S(1)}, u32[]{:S(2)}, u32[]{:S(2)}) %collective-permute-start.20) | collective-permute-done | bytes 131104 | tf_op jit(solution)/shard_map/ppermute | solution.py:69
  50.6 4.2 %collective-permute-done.21.refs_1_ = bf16[2,64,512]{2,1,0:T(8,128)(2,1)S(1)} collective-permute-done((bf16[2,64,512]{2,1,0:T(8,128)(2,1)S(1)}, bf16[2,64,512]{2,1,0:T(8,128)(2,1)S(1)}, u32[]{:S(2)}, u32[]{:S(2)}) %collective-permute-start.21) | collective-permute-done | bytes 131104 | tf_op jit(solution)/shard_map/ppermute | solution.py:69
  54.8 0.7 %shard_map.150 = (f32[64,512]{1,0:T(8,128)}, f32[64,512]{1,0:T(8,128)}) custom-call(f32[2,64,512]{2,1,0:T(8,128)S(1)} %get-tuple-element.100.kept_ref, bf16[2,64,512]{2,1,0:T(8,128)(2,1)S(1)} %collective-permute-done.20.refs_0_, bf16[2,64,512]{2,1,0:T(8,128)(2,1)S(1)} %collective-permute-done.21.refs_1_, bf16[2,64,512]{2,1,0:T(8,128)(2,1)S(1)} %collective-permute-done.22.refs_2_), custom_call_target="tpu_custom_call" | custom-call | flops 500000000 | tf_op jit(solution)/shard_map/pallas_call | solution.py:675
  55.6 1.1 %shard_map.149 = (bf16[128,512]{1,0:T(8,128)(2,1)}, bf16[128,512]{1,0:T(8,128)(2,1)}) custom-call(bf16[128,256]{1,0:T(8,128)(2,1)S(1)} %get-tuple-element.89.placed_ref, f32[128,128]{1,0:T(8,128)S(1)} %get-tuple-element.90.factors_ref, f32[128,512]{1,0:T(8,128)S(1)} %get-tuple-element.91.router_cols_ref, bf16[128,512]{1,0:T(8,128)(2,1)S(1)} %get-tuple-element.88.mixed_ref, ...), custom_call_target="tpu_custom_call" | custom-call | flops 1000000000 | tf_op jit(solution)/shard_map/pallas_call | solution.py:669
  (55 shorter events, 4.2 us)
Async XLA Ops:
  0.6 12.8 %collective-permute-start.4 = (bf16[128,512]{1,0:T(8,128)(2,1)}, bf16[128,512]{1,0:T(8,128)(2,1)S(1)}, u32[]{:S(2)}, u32[]{:S(2)}) collective-permute-start(bf16[128,512]{1,0:T(8,128)(2,1)} %bitcast.39), channel_id=1, source_target_pairs={{0,1},{1,0},{2,3},{3,2},{4,5},{5,4},{6,7},{7,6},{8,9},{9,8},{10,11... | collective-permute-start | bytes 393224 | tf_op jit(solution)/shard_map/ppermute | solution.py:69
  3.6 8.4 %collective-permute-start = (bf16[128,512]{1,0:T(8,128)(2,1)}, bf16[128,512]{1,0:T(8,128)(2,1)S(1)}, u32[]{:S(2)}, u32[]{:S(2)}) collective-permute-start(bf16[128,512]{1,0:T(8,128)(2,1)} %bitcast.33), channel_id=1, source_target_pairs={{0,8},{8,16},{16,24},{24,0},{1,9},{9,17},{17,25},{25,1},{2,10},{10... | collective-permute-start | bytes 393224 | tf_op jit(solution)/shard_map/ppermute | solution.py:523
  5.2 8.3 %collective-permute-start.2 = (bf16[128,512]{1,0:T(8,128)(2,1)}, bf16[128,512]{1,0:T(8,128)(2,1)S(1)}, u32[]{:S(2)}, u32[]{:S(2)}) collective-permute-start(bf16[128,512]{1,0:T(8,128)(2,1)} %bitcast.36), channel_id=1, source_target_pairs={{0,8},{8,16},{16,24},{24,0},{1,9},{9,17},{17,25},{25,1},{2,10},{10... | collective-permute-start | bytes 393224 | tf_op jit(solution)/shard_map/ppermute | solution.py:523
  6.8 0.7 %copy-start.8 = (bf16[512,4]{0,1:T(4,128)(2,1)S(1)}, bf16[512,4]{0,1:T(4,128)(2,1)}, u32[]{:S(2)}) copy-start(bf16[512,4]{0,1:T(4,128)(2,1)} %param.17) | copy-start | bytes 12292
  7.5 0.9 %copy-start.3 = (bf16[1,128,512]{2,1,0:T(8,128)(2,1)S(1)}, bf16[1,128,512]{2,1,0:T(8,128)(2,1)}, u32[]{:S(2)}) copy-start(bf16[1,128,512]{2,1,0:T(8,128)(2,1)} %param.21) | copy-start | bytes 393220
  8.4 1.3 %copy-start.4 = (bf16[1,128,512]{2,1,0:T(8,128)(2,1)S(1)}, bf16[1,128,512]{2,1,0:T(8,128)(2,1)}, u32[]{:S(2)}) copy-start(bf16[1,128,512]{2,1,0:T(8,128)(2,1)} %param.12) | copy-start | bytes 393220
  8.4 1.3 %copy-start.5 = (bf16[1,128,512]{2,1,0:T(8,128)(2,1)S(1)}, bf16[1,128,512]{2,1,0:T(8,128)(2,1)}, u32[]{:S(2)}) copy-start(bf16[1,128,512]{2,1,0:T(8,128)(2,1)} %param.13) | copy-start | bytes 393220
  8.4 1.3 %copy-start.6 = (bf16[1,128,512]{2,1,0:T(8,128)(2,1)S(1)}, bf16[1,128,512]{2,1,0:T(8,128)(2,1)}, u32[]{:S(2)}) copy-start(bf16[1,128,512]{2,1,0:T(8,128)(2,1)} %param.11) | copy-start | bytes 393220
  9.0 12.5 %collective-permute-start.5 = (bf16[160,512]{1,0:T(8,128)(2,1)S(1)}, bf16[160,512]{1,0:T(8,128)(2,1)S(1)}, u32[]{:S(2)}, u32[]{:S(2)}) collective-permute-start(bf16[160,512]{1,0:T(8,128)(2,1)S(1)} %get-tuple-element.55.extended_ref.refs_0_), channel_id=1, source_target_pairs={{0,1},{1,0},{2,3},{3,2},{4,5},{5,4},{6,7},{7,6},{8,9},{9,8},{10,11... | collective-permute-start | bytes 491528 | tf_op jit(solution)/shard_map/ppermute | solution.py:69
  12.1 8.7 %collective-permute-start.1 = (bf16[128,512]{1,0:T(8,128)(2,1)S(1)}, bf16[128,512]{1,0:T(8,128)(2,1)S(1)}, u32[]{:S(2)}, u32[]{:S(2)}) collective-permute-start(bf16[128,512]{1,0:T(8,128)(2,1)S(1)} %collective-permute-done.refs_4_), channel_id=1, source_target_pairs={{0,8},{8,16},{16,24},{24,0},{1,9},{9,17},{17,25},{25,1},{2,10},{10... | collective-permute-start | bytes 393224 | tf_op jit(solution)/shard_map/ppermute | solution.py:523
  13.5 7.3 %collective-permute-start.3 = (bf16[128,512]{1,0:T(8,128)(2,1)S(1)}, bf16[128,512]{1,0:T(8,128)(2,1)S(1)}, u32[]{:S(2)}, u32[]{:S(2)}) collective-permute-start(bf16[128,512]{1,0:T(8,128)(2,1)S(1)} %collective-permute-done.2.refs_5_), channel_id=1, source_target_pairs={{0,8},{8,16},{16,24},{24,0},{1,9},{9,17},{17,25},{25,1},{2,10},{10... | collective-permute-start | bytes 393224 | tf_op jit(solution)/shard_map/ppermute | solution.py:523
  21.6 5.3 %collective-permute-start.6 = (bf16[592,128]{1,0:T(8,128)(2,1)S(1)}, bf16[592,128]{1,0:T(8,128)(2,1)S(1)}, u32[]{:S(2)}, u32[]{:S(2)}) collective-permute-start(bf16[592,128]{1,0:T(8,128)(2,1)S(1)} %shard_map.142), channel_id=1, source_target_pairs={{0,1},{1,0},{2,3},{3,2},{4,5},{5,4},{6,7},{7,6},{8,9},{9,8},{10,11... | collective-permute-start | bytes 454664 | tf_op jit(solution)/shard_map/ppermute | solution.py:69
  23.3 5.8 %collective-permute-start.10 = (bf16[128,512]{1,0:T(8,128)(2,1)S(1)}, bf16[128,512]{1,0:T(8,128)(2,1)S(1)}, u32[]{:S(2)}, u32[]{:S(2)}) collective-permute-start(bf16[128,512]{1,0:T(8,128)(2,1)S(1)} %get-tuple-element.80), channel_id=1, source_target_pairs={{0,2},{2,0},{4,6},{6,4},{1,3},{3,1},{5,7},{7,5},{8,10},{10,8},{12,... | collective-permute-start | bytes 393224 | tf_op jit(solution)/shard_map/ppermute | solution.py:69
  23.4 6.4 %collective-permute-start.11 = (bf16[128,512]{1,0:T(8,128)(2,1)S(1)}, bf16[128,512]{1,0:T(8,128)(2,1)S(1)}, u32[]{:S(2)}, u32[]{:S(2)}) collective-permute-start(bf16[128,512]{1,0:T(8,128)(2,1)S(1)} %get-tuple-element.81), channel_id=1, source_target_pairs={{0,4},{2,6},{4,0},{6,2},{1,5},{3,7},{5,1},{7,3},{8,12},{10,14},{12... | collective-permute-start | bytes 393224 | tf_op jit(solution)/shard_map/ppermute | solution.py:69
  25.0 6.7 %collective-permute-start.12 = (bf16[128,512]{1,0:T(8,128)(2,1)S(1)}, bf16[128,512]{1,0:T(8,128)(2,1)S(1)}, u32[]{:S(2)}, u32[]{:S(2)}) collective-permute-start(bf16[128,512]{1,0:T(8,128)(2,1)S(1)} %get-tuple-element.82), channel_id=1, source_target_pairs={{0,6},{2,4},{4,2},{6,0},{1,7},{3,5},{5,3},{7,1},{8,14},{10,12},{12... | collective-permute-start | bytes 393224 | tf_op jit(solution)/shard_map/ppermute | solution.py:69
  25.3 1.5 %copy-start = (bf16[512,512]{1,0:T(8,128)(2,1)S(1)}, bf16[512,512]{1,0:T(8,128)(2,1)}, u32[]{:S(2)}) copy-start(bf16[512,512]{1,0:T(8,128)(2,1)} %proj_ref.1) | copy-start | bytes 1572868
  25.3 1.5 %copy-start.7 = (bf16[1,128,512]{2,1,0:T(8,128)(2,1)S(1)}, bf16[1,128,512]{2,1,0:T(8,128)(2,1)}, u32[]{:S(2)}) copy-start(bf16[1,128,512]{2,1,0:T(8,128)(2,1)} %param.15) | copy-start | bytes 393220
  26.8 8.7 %copy-start.1 = (bf16[1,512,512]{2,1,0:T(8,128)(2,1)S(1)}, bf16[1,512,512]{2,1,0:T(8,128)(2,1)}, u32[]{:S(2)}) copy-start(bf16[1,512,512]{2,1,0:T(8,128)(2,1)} %param.19) | copy-start | bytes 1572868
  26.8 8.7 %copy-start.2 = (bf16[1,512,512]{2,1,0:T(8,128)(2,1)S(1)}, bf16[1,512,512]{2,1,0:T(8,128)(2,1)}, u32[]{:S(2)}) copy-start(bf16[1,512,512]{2,1,0:T(8,128)(2,1)} %param.20) | copy-start | bytes 1572868
  27.4 6.1 %collective-permute-start.7 = (bf16[64,512]{1,0:T(8,128)(2,1)S(1)}, bf16[64,512]{1,0:T(8,128)(2,1)S(1)}, u32[]{:S(2)}, u32[]{:S(2)}) collective-permute-start(bf16[64,512]{1,0:T(8,128)(2,1)S(1)} %get-tuple-element.75), channel_id=1, source_target_pairs={{0,2},{1,3},{2,0},{3,1},{4,6},{5,7},{6,4},{7,5},{8,10},{9,11},{10,... | collective-permute-start | bytes 196616 | tf_op jit(solution)/shard_map/ppermute | solution.py:69
  27.5 7.1 %collective-permute-start.8 = (bf16[64,512]{1,0:T(8,128)(2,1)S(1)}, bf16[64,512]{1,0:T(8,128)(2,1)S(1)}, u32[]{:S(2)}, u32[]{:S(2)}) collective-permute-start(bf16[64,512]{1,0:T(8,128)(2,1)S(1)} %get-tuple-element.76), channel_id=1, source_target_pairs={{0,4},{1,5},{2,6},{3,7},{4,0},{5,1},{6,2},{7,3},{8,12},{9,13},{10,... | collective-permute-start | bytes 196616 | tf_op jit(solution)/shard_map/ppermute | solution.py:69
  29.1 6.4 %collective-permute-start.9 = (bf16[64,512]{1,0:T(8,128)(2,1)S(1)}, bf16[64,512]{1,0:T(8,128)(2,1)S(1)}, u32[]{:S(2)}, u32[]{:S(2)}) collective-permute-start(bf16[64,512]{1,0:T(8,128)(2,1)S(1)} %get-tuple-element.77), channel_id=1, source_target_pairs={{0,6},{1,7},{2,4},{3,5},{4,2},{5,3},{6,0},{7,1},{8,14},{9,15},{10,... | collective-permute-start | bytes 196616 | tf_op jit(solution)/shard_map/ppermute | solution.py:69
  29.8 10.4 %collective-permute-start.14 = (bf16[64,512]{1,0:T(8,128)(2,1)S(1)}, bf16[64,512]{1,0:T(8,128)(2,1)S(1)}, u32[]{:S(2)}, u32[]{:S(2)}) collective-permute-start(bf16[64,512]{1,0:T(8,128)(2,1)S(1)} %get-tuple-element.75), channel_id=1, source_target_pairs={{0,3},{1,2},{2,1},{3,0},{4,7},{5,6},{6,5},{7,4},{8,11},{9,10},{10,... | collective-permute-start | bytes 196616 | tf_op jit(solution)/shard_map/ppermute | solution.py:69
  31.7 8.5 %collective-permute-start.15 = (bf16[64,512]{1,0:T(8,128)(2,1)S(1)}, bf16[64,512]{1,0:T(8,128)(2,1)S(1)}, u32[]{:S(2)}, u32[]{:S(2)}) collective-permute-start(bf16[64,512]{1,0:T(8,128)(2,1)S(1)} %get-tuple-element.76), channel_id=1, source_target_pairs={{0,5},{1,4},{2,7},{3,6},{4,1},{5,0},{6,3},{7,2},{8,13},{9,12},{10,... | collective-permute-start | bytes 196616 | tf_op jit(solution)/shard_map/ppermute | solution.py:69
  33.5 6.7 %collective-permute-start.16 = (bf16[64,512]{1,0:T(8,128)(2,1)S(1)}, bf16[64,512]{1,0:T(8,128)(2,1)S(1)}, u32[]{:S(2)}, u32[]{:S(2)}) collective-permute-start(bf16[64,512]{1,0:T(8,128)(2,1)S(1)} %get-tuple-element.77), channel_id=1, source_target_pairs={{0,7},{1,6},{2,5},{3,4},{4,3},{5,2},{6,1},{7,0},{8,15},{9,14},{10,... | collective-permute-start | bytes 196616 | tf_op jit(solution)/shard_map/ppermute | solution.py:69
  34.7 5.5 %collective-permute-start.13 = (bf16[64,512]{1,0:T(8,128)(2,1)S(1)}, bf16[64,512]{1,0:T(8,128)(2,1)S(1)}, u32[]{:S(2)}, u32[]{:S(2)}) collective-permute-start(bf16[64,512]{1,0:T(8,128)(2,1)S(1)} %get-tuple-element.74.refs_0_), channel_id=1, source_target_pairs={{0,1},{1,0},{2,3},{3,2},{4,5},{5,4},{6,7},{7,6},{8,9},{9,8},{10,11... | collective-permute-start | bytes 196616 | tf_op jit(solution)/shard_map/ppermute | solution.py:69
  41.8 8.3 %collective-permute-start.20 = (bf16[2,64,512]{2,1,0:T(8,128)(2,1)S(1)}, bf16[2,64,512]{2,1,0:T(8,128)(2,1)S(1)}, u32[]{:S(2)}, u32[]{:S(2)}) collective-permute-start(bf16[2,64,512]{2,1,0:T(8,128)(2,1)S(1)} %get-tuple-element.101), channel_id=1, source_target_pairs={{0,24},{8,16},{16,8},{24,0},{1,25},{9,17},{17,9},{25,1},{2,26},{10... | collective-permute-start | bytes 393224 | tf_op jit(solution)/shard_map/ppermute | solution.py:69
  43.5 11.3 %collective-permute-start.21 = (bf16[2,64,512]{2,1,0:T(8,128)(2,1)S(1)}, bf16[2,64,512]{2,1,0:T(8,128)(2,1)S(1)}, u32[]{:S(2)}, u32[]{:S(2)}) collective-permute-start(bf16[2,64,512]{2,1,0:T(8,128)(2,1)S(1)} %get-tuple-element.102), channel_id=1, source_target_pairs={{0,16},{8,24},{16,0},{24,8},{1,17},{9,25},{17,1},{25,9},{2,18},{10... | collective-permute-start | bytes 393224 | tf_op jit(solution)/shard_map/ppermute | solution.py:69
  43.5 11.3 %collective-permute-start.22 = (bf16[2,64,512]{2,1,0:T(8,128)(2,1)S(1)}, bf16[2,64,512]{2,1,0:T(8,128)(2,1)S(1)}, u32[]{:S(2)}, u32[]{:S(2)}) collective-permute-start(bf16[2,64,512]{2,1,0:T(8,128)(2,1)S(1)} %get-tuple-element.103), channel_id=1, source_target_pairs={{0,8},{8,0},{16,24},{24,16},{1,9},{9,1},{17,25},{25,17},{2,10},{10... | collective-permute-start | bytes 393224 | tf_op jit(solution)/shard_map/ppermute | solution.py:69
  46.7 8.8 %collective-permute-start.17 = (bf16[128,512]{1,0:T(8,128)(2,1)S(1)}, bf16[128,512]{1,0:T(8,128)(2,1)S(1)}, u32[]{:S(2)}, u32[]{:S(2)}) collective-permute-start(bf16[128,512]{1,0:T(8,128)(2,1)S(1)} %get-tuple-element.94), channel_id=1, source_target_pairs={{0,6},{2,4},{4,2},{6,0},{1,7},{3,5},{5,3},{7,1},{8,14},{10,12},{12... | collective-permute-start | bytes 393224 | tf_op jit(solution)/shard_map/ppermute | solution.py:69
  46.8 8.8 %collective-permute-start.18 = (bf16[128,512]{1,0:T(8,128)(2,1)S(1)}, bf16[128,512]{1,0:T(8,128)(2,1)S(1)}, u32[]{:S(2)}, u32[]{:S(2)}) collective-permute-start(bf16[128,512]{1,0:T(8,128)(2,1)S(1)} %get-tuple-element.95), channel_id=1, source_target_pairs={{0,4},{2,6},{4,0},{6,2},{1,5},{3,7},{5,1},{7,3},{8,12},{10,14},{12... | collective-permute-start | bytes 393224 | tf_op jit(solution)/shard_map/ppermute | solution.py:69
  50.1 5.4 %collective-permute-start.19 = (bf16[128,512]{1,0:T(8,128)(2,1)S(1)}, bf16[128,512]{1,0:T(8,128)(2,1)S(1)}, u32[]{:S(2)}, u32[]{:S(2)}) collective-permute-start(bf16[128,512]{1,0:T(8,128)(2,1)S(1)} %get-tuple-element.96), channel_id=1, source_target_pairs={{0,2},{2,0},{4,6},{6,4},{1,3},{3,1},{5,7},{7,5},{8,10},{10,8},{12,... | collective-permute-start | bytes 393224 | tf_op jit(solution)/shard_map/ppermute | solution.py:69
  (2 other events, 1.3 us)

commit v16 on v15

--- a/solution.py
+++ b/solution.py
@@ -324,10 +324,10 @@
     own_rows = rep_list[0] == 0
     held_ref, refs = refs[-1], refs[:-1]
     if own_rows:
-        activated_ref, pre_grad_ref, up_acc, down_acc = refs
+        up_old, down_old, activated_ref, pre_grad_ref = refs[:4]
+        term_refs, kept_ref = refs[4:-1], refs[-1]
     else:
-        up_old, down_old = refs[:2]
-        term_refs, kept_ref = refs[2:-1], refs[-1]
+        up_acc, down_acc = refs
     total_grads = sum(ref.shape[0] for ref in grad_refs)
     capacity = total_grads // (sources * reps)
     count = sources * capacity
@@ -370,7 +370,7 @@
         more_down = dot(strips(activated, 2 * place + 1), scaled)
         up_term = more_up if up_term is None else up_term + more_up
         down_term = more_down if down_term is None else down_term + more_down
-    if own_rows:
+    if not own_rows:
         up_acc[...] = up_term
         down_acc[...] = down_term
         return
@@ -421,6 +421,7 @@
 
 def finish_kernel(
     hot_capacity,
+    parts,
     placed_ref,
     factors_ref,
     router_cols_ref,
@@ -428,7 +429,13 @@
     extended_ref,
     *refs,
 ):
-    back_refs, (layer_ref, grad_mixed_ref) = refs[:-2][::-1], refs[-2:]
+    refs, (layer_ref, grad_mixed_ref, *share_refs) = refs[:-4], refs[-4:]
+    (kept_ref, *term_refs), back_refs = refs[:parts], refs[parts:][::-1]
+    for kind, share_ref in enumerate(share_refs):
+        total = kept_ref[kind]
+        for ref in term_refs:
+            total = total + ref[kind].astype(jnp.float32)
+        share_ref[...] = total
     tok = mixed_ref.shape[0]
     mixed_f = mixed_ref[...].astype(jnp.float32)
     inv_rms = factors_ref[:, 0:1]
@@ -450,15 +457,6 @@
     mean_term = jnp.mean(total_grad * mixed_f, axis=1, keepdims=True)
     input_grad = inv_rms * total_grad - mixed_f * inv_rms * inv_rms * inv_rms * mean_term
     grad_mixed_ref[...] = (grad_f + input_grad).astype(jnp.bfloat16)
-
-
-def sum_kernel(kept_ref, *refs):
-    term_refs, (up_ref, down_ref) = refs[:-2], refs[-2:]
-    for kind, out_ref in enumerate((up_ref, down_ref)):
-        total = kept_ref[kind]
-        for ref in term_refs:
-            total = total + ref[kind].astype(jnp.float32)
-        out_ref[...] = total
 
 
 def shape(dims, dtype=jnp.bfloat16):
@@ -629,23 +627,22 @@
         )(own, part_to, weight_in[0], weight_out[0], extendeds[0], *rows, *got_grads, *extra)
 
     slots = expert_count * hot_capacity
-    activated, pre_grad, up_acc, down_acc = expert_call(
-        (0,),
-        got_rows,
+    sums = expert_call(
+        tuple(others),
+        got_more,
         [
-            shape((slots, hidden)),
-            shape((slots, hidden)),
             shape((seq_count * strip, hidden), jnp.float32),
             shape((seq_count * strip, width), jnp.float32),
         ],
         [],
     )
-    *terms, kept = expert_call(
-        tuple(range(1, rep_count)),
-        got_more,
-        [shape((2, strip, hidden))] * (seq_count - 1)
+    activated, pre_grad, *terms, kept = expert_call(
+        (0,),
+        got_rows,
+        [shape((slots, hidden))] * 2
+        + [shape((2, strip, hidden))] * (seq_count - 1)
         + [shape((2, strip, hidden), jnp.float32)],
-        [up_acc, down_acc],
+        list(sums),
     )
     got_terms = parts.exchange([None] + terms)[1:]
     activated, mixed, kept = lax.optimization_barrier((activated, mixed, kept))
@@ -666,17 +663,17 @@
         [SMEM, VMEM, VMEM],
         cost=1.0,
     )(own, mixed, extended)
-    layer_out, grad_mixed = call(
-        functools.partial(finish_kernel, hot_capacity),
-        [shape((tok, width)), shape((tok, width))],
-        [VMEM] * (5 + len(got_back)),
+    layer_out, grad_mixed, share_in, share_out = call(
+        functools.partial(finish_kernel, hot_capacity, seq_count),
+        [
+            shape((tok, width)),
+            shape((tok, width)),
+            shape((strip, hidden), jnp.float32),
+            shape((strip, width), jnp.float32),
+        ],
+        [VMEM] * (5 + seq_count + len(got_back)),
         cost=1.0,
-    )(*prepared, mixed, extended, *got_back[::-1])
-    share_in, share_out = call(
-        sum_kernel,
-        [shape((strip, hidden), jnp.float32), shape((strip, width), jnp.float32)],
-        [VMEM] * seq_count,
-    )(kept, *got_terms[::-1])
+    )(*prepared, mixed, extended, kept, *got_terms[::-1], *got_back[::-1])
     return (layer_out[None], grad_mixed[None], share_in[None], share_out[None])
 
 

time: 56.9 us -> 56 us (0.984)
  starting transfers between devices: 22.9 us -> 23.6 us
  waiting for transfers between devices: 18 us -> 17.3 us
  Pallas kernels: 12.9 us -> 12.3 us
    ppermute x19, starting transfers between devices: 18.5 us -> 19.2 us  [exchange(): got[k] = lax.ppermute(chunks[k], self.axes, pairs)]
    ppermute x19, waiting for transfers between devices: 12.1 us -> 11.4 us  [exchange(): got[k] = lax.ppermute(chunks[k], self.axes, pairs)]
    pallas_call x2 -> x1, Pallas kernels: 1.88 us -> 1.26 us  [local(): call(functools.partial(finish_kernel, hot_capacity, seq_count), [shape((t...]
  transfers between devices with their start and end apart: 23 -> 23, of which waited for: 9 -> 9; matrix products, arithmetic and copies ran while one was open for 1% -> 1% of each run, Pallas kernels for 18% -> 17%
where the time goes in v16:
time: 56 us; the launch traced here: 56.1 us
  starting transfers between devices  23.6 us (42%)
  waiting for transfers between devices  17.3 us (31%)
  Pallas kernels  12.3 us (22%)
  local copies, waits for them, and re-layouts  1.69 us (3%)
  between operations  0.81 us (1%)
    ppermute x19, starting transfers between devices, exchange(): got[k] = lax.ppermute(chunks[k], self.axes, pairs)  19.2 us
    ppermute x19, waiting for transfers between devices, exchange(): got[k] = lax.ppermute(chunks[k], self.axes, pairs)  11.4 us
    ppermute x4, waiting for transfers between devices, forward(): lax.ppermute(array, 'seq', [(i, (i + 1) % seq_count) for i in range(seq_c...  5.86 us
    pallas_call x4, Pallas kernels, attend(): call(functools.partial(attend_kernel, plan, rep_count, len(pairs), packed...  5.19 us
    ppermute x4, starting transfers between devices, forward(): lax.ppermute(array, 'seq', [(i, (i + 1) % seq_count) for i in range(seq_c...  4.4 us
    pallas_call x2, Pallas kernels, expert_call(): call(functools.partial(expert_kernel, rep_count, rep_list, expert_count,...  3.24 us
    unnamed x22, local copies, waits for them, and re-layouts  1.6 us
    pallas_call x1, Pallas kernels, local(): call(functools.partial(finish_kernel, hot_capacity, seq_count), [shape((t...  1.26 us
  transfers between devices with their start and end apart: 23, of which 9 were waited for; matrix products, arithmetic and copies ran while one was open for 1% of the time, Pallas kernels for 17%

profile of v16, /device:TPU:0, one launch (start us, length us, event | category | flops | bytes accessed | tf_op | source)
XLA Modules:
  0.0 56.1 jit_solution(6940603182653191716)
XLA Ops:
  0.6 3.0 %collective-permute-start.4 = (bf16[128,512]{1,0:T(8,128)(2,1)}, bf16[128,512]{1,0:T(8,128)(2,1)S(1)}, u32[]{:S(2)}, u32[]{:S(2)}) collective-permute-start(bf16[128,512]{1,0:T(8,128)(2,1)} %bitcast.39), channel_id=1, source_target_pairs={{0,1},{1,0},{2,3},{3,2},{4,5},{5,4},{6,7},{7,6},{8,9},{9,8},{10,11... | collective-permute-start | bytes 393224 | tf_op jit(solution)/shard_map/ppermute | solution.py:69
  3.6 1.6 %collective-permute-start = (bf16[128,512]{1,0:T(8,128)(2,1)}, bf16[128,512]{1,0:T(8,128)(2,1)S(1)}, u32[]{:S(2)}, u32[]{:S(2)}) collective-permute-start(bf16[128,512]{1,0:T(8,128)(2,1)} %bitcast.33), channel_id=1, source_target_pairs={{0,8},{8,16},{16,24},{24,0},{1,9},{9,17},{17,25},{25,1},{2,10},{10... | collective-permute-start | bytes 393224 | tf_op jit(solution)/shard_map/ppermute | solution.py:521
  5.2 1.6 %collective-permute-start.2 = (bf16[128,512]{1,0:T(8,128)(2,1)}, bf16[128,512]{1,0:T(8,128)(2,1)S(1)}, u32[]{:S(2)}, u32[]{:S(2)}) collective-permute-start(bf16[128,512]{1,0:T(8,128)(2,1)} %bitcast.36), channel_id=1, source_target_pairs={{0,8},{8,16},{16,24},{24,0},{1,9},{9,17},{17,25},{25,1},{2,10},{10... | collective-permute-start | bytes 393224 | tf_op jit(solution)/shard_map/ppermute | solution.py:521
  6.9 0.6 %copy-done.8 = bf16[512,4]{0,1:T(4,128)(2,1)S(1)} copy-done((bf16[512,4]{0,1:T(4,128)(2,1)S(1)}, bf16[512,4]{0,1:T(4,128)(2,1)}, u32[]{:S(2)}) %copy-start.8) | copy-done | bytes 4120
  7.5 0.9 %copy-done.3 = bf16[1,128,512]{2,1,0:T(8,128)(2,1)S(1)} copy-done((bf16[1,128,512]{2,1,0:T(8,128)(2,1)S(1)}, bf16[1,128,512]{2,1,0:T(8,128)(2,1)}, u32[]{:S(2)}) %copy-start.3) | copy-done | bytes 131096
  9.0 0.6 %collective-permute-start.5 = (bf16[160,512]{1,0:T(8,128)(2,1)S(1)}, bf16[160,512]{1,0:T(8,128)(2,1)S(1)}, u32[]{:S(2)}, u32[]{:S(2)}) collective-permute-start(bf16[160,512]{1,0:T(8,128)(2,1)S(1)} %get-tuple-element.55.extended_ref.refs_0_), channel_id=1, source_target_pairs={{0,1},{1,0},{2,3},{3,2},{4,5},{5,4},{6,7},{7,6},{8,9},{9,8},{10,11... | collective-permute-start | bytes 491528 | tf_op jit(solution)/shard_map/ppermute | solution.py:69
  9.7 1.7 %shard_map.139 = (f32[16,128]{1,0:T(8,128)S(1)}, f32[16,128]{1,0:T(8,128)S(1)}, f32[512,128]{1,0:T(8,128)S(1)}) custom-call(s32[3]{0:T(128)S(1)} %pad_add_fusion.4.ids_ref, s32[2,128]{1,0:T(2,128)S(1)} %get-tuple-element.56.begin_ref, bf16[128,512]{1,0:T(8,128)(2,1)S(1)} %bitcast.40, bf16[128,512]{1,0:T(8,128)(2,1)S(1)} %bitcast.34, ...), custom_call_target="tpu_custom_call" | custom-call | flops 2000000000 | tf_op jit(solution)/shard_map/pallas_call | solution.py:560
  12.1 1.2 %collective-permute-start.1 = (bf16[128,512]{1,0:T(8,128)(2,1)S(1)}, bf16[128,512]{1,0:T(8,128)(2,1)S(1)}, u32[]{:S(2)}, u32[]{:S(2)}) collective-permute-start(bf16[128,512]{1,0:T(8,128)(2,1)S(1)} %collective-permute-done.refs_4_), channel_id=1, source_target_pairs={{0,8},{8,16},{16,24},{24,0},{1,9},{9,17},{17,25},{25,1},{2,10},{10... | collective-permute-start | bytes 393224 | tf_op jit(solution)/shard_map/ppermute | solution.py:521
  13.5 1.9 %shard_map.140 = (f32[16,128]{1,0:T(8,128)S(1)}, f32[16,128]{1,0:T(8,128)S(1)}, f32[512,128]{1,0:T(8,128)S(1)}, f32[16,128]{1,0:T(8,128)S(1)}, f32[16,128]{1,0:T(8,128)S(1)}, /*index=5*/f32[512,128]{1,0:T(8,128)S(1)}) custom-call(s32[5]{0:T(128)S(1)} %stack.81.ids_ref, s32[2,128]{1,0:T(2,128)S(1)} %get-tuple-element.56.begin_ref, ...), custom_call_target="tpu_custom_call" | custom-call | flops 4000000000 | tf_op jit(solution)/shard_map/pallas_call | solution.py:560
  15.4 5.4 %collective-permute-done.3.refs_2_ = bf16[128,512]{1,0:T(8,128)(2,1)S(1)} collective-permute-done((bf16[128,512]{1,0:T(8,128)(2,1)S(1)}, bf16[128,512]{1,0:T(8,128)(2,1)S(1)}, u32[]{:S(2)}, u32[]{:S(2)}) %collective-permute-start.3) | collective-permute-done | bytes 131104 | tf_op jit(solution)/shard_map/ppermute | solution.py:521
  20.8 0.8 %shard_map.142 = bf16[592,128]{1,0:T(8,128)(2,1)S(1)} custom-call(s32[3]{0:T(128)S(1)} %pad_add_fusion.5.ids_ref, s32[2,128]{1,0:T(2,128)S(1)} %get-tuple-element.56.begin_ref, bf16[128,512]{1,0:T(8,128)(2,1)S(1)} %collective-permute-done.4.refs_1_.refs_0_, bf16[128,512]{1,0:T(8,128)(2,1)S(1)} %collective-permute-done.1.refs_1_, ...), custom_call_target="tpu_custom_call" | custom-call | flops 1500000000 | tf_op jit(solution)/shard_map/pallas_call | solution.py:560
  21.6 1.2 %collective-permute-start.6 = (bf16[592,128]{1,0:T(8,128)(2,1)S(1)}, bf16[592,128]{1,0:T(8,128)(2,1)S(1)}, u32[]{:S(2)}, u32[]{:S(2)}) collective-permute-start(bf16[592,128]{1,0:T(8,128)(2,1)S(1)} %shard_map.142), channel_id=1, source_target_pairs={{0,1},{1,0},{2,3},{3,2},{4,5},{5,4},{6,7},{7,6},{8,9},{9,8},{10,11... | collective-permute-start | bytes 454664 | tf_op jit(solution)/shard_map/ppermute | solution.py:69
  23.4 1.6 %collective-permute-start.11 = (bf16[128,512]{1,0:T(8,128)(2,1)S(1)}, bf16[128,512]{1,0:T(8,128)(2,1)S(1)}, u32[]{:S(2)}, u32[]{:S(2)}) collective-permute-start(bf16[128,512]{1,0:T(8,128)(2,1)S(1)} %get-tuple-element.81), channel_id=1, source_target_pairs={{0,4},{2,6},{4,0},{6,2},{1,5},{3,7},{5,1},{7,3},{8,12},{10,14},{12... | collective-permute-start | bytes 393224 | tf_op jit(solution)/shard_map/ppermute | solution.py:69
  25.3 0.7 %shard_map.141 = (f32[16,128]{1,0:T(8,128)S(1)}, f32[16,128]{1,0:T(8,128)S(1)}, f32[512,128]{1,0:T(8,128)S(1)}) custom-call(s32[3]{0:T(128)S(1)} %pad_add_fusion.2.ids_ref, s32[2,128]{1,0:T(2,128)S(1)} %get-tuple-element.56.begin_ref, bf16[128,512]{1,0:T(8,128)(2,1)S(1)} %bitcast.42, bf16[128,512]{1,0:T(8,128)(2,1)S(1)} %collective-permute-done.1.refs_1_, ...), custom_call_target="tpu_custom_call" | custom-call | flops 1500000000 | tf_op jit(solution)/shard_map/pallas_call | solution.py:560
  26.0 0.8 %collective-permute-done.6.refs_3_ = bf16[592,128]{1,0:T(8,128)(2,1)S(1)} collective-permute-done((bf16[592,128]{1,0:T(8,128)(2,1)S(1)}, bf16[592,128]{1,0:T(8,128)(2,1)S(1)}, u32[]{:S(2)}, u32[]{:S(2)}) %collective-permute-start.6) | collective-permute-done | bytes 151584 | tf_op jit(solution)/shard_map/ppermute | solution.py:69
  26.8 0.6 %shard_map.143 = (bf16[128,512]{1,0:T(8,128)(2,1)S(1)}, bf16[64,512]{1,0:T(8,128)(2,1)S(1)}, bf16[64,512]{1,0:T(8,128)(2,1)S(1)}, bf16[64,512]{1,0:T(8,128)(2,1)S(1)}, bf16[64,512]{1,0:T(8,128)(2,1)S(1)}) custom-call(s32[1]{0:T(128)} %bitcast.own_ref, bf16[160,512]{1,0:T(8,128)(2,1)S(1)} %get-tuple-element.55.extended_ref.refs_0_, ...), custom_call_target="tpu_custom_call" | custom-call | flops 2000000000 | tf_op jit(solution)/shard_map/pallas_call | solution.py:600
  27.4 1.2 %collective-permute-start.13 = (bf16[64,512]{1,0:T(8,128)(2,1)S(1)}, bf16[64,512]{1,0:T(8,128)(2,1)S(1)}, u32[]{:S(2)}, u32[]{:S(2)}) collective-permute-start(bf16[64,512]{1,0:T(8,128)(2,1)S(1)} %get-tuple-element.74.refs_0_), channel_id=1, source_target_pairs={{0,1},{1,0},{2,3},{3,2},{4,5},{5,4},{6,7},{7,6},{8,9},{9,8},{10,11... | collective-permute-start | bytes 196616 | tf_op jit(solution)/shard_map/ppermute | solution.py:69
  28.7 1.8 %collective-permute-start.15 = (bf16[64,512]{1,0:T(8,128)(2,1)S(1)}, bf16[64,512]{1,0:T(8,128)(2,1)S(1)}, u32[]{:S(2)}, u32[]{:S(2)}) collective-permute-start(bf16[64,512]{1,0:T(8,128)(2,1)S(1)} %get-tuple-element.76), channel_id=1, source_target_pairs={{0,5},{1,4},{2,7},{3,6},{4,1},{5,0},{6,3},{7,2},{8,13},{9,12},{10,... | collective-permute-start | bytes 196616 | tf_op jit(solution)/shard_map/ppermute | solution.py:69
  30.5 1.4 %collective-permute-start.16 = (bf16[64,512]{1,0:T(8,128)(2,1)S(1)}, bf16[64,512]{1,0:T(8,128)(2,1)S(1)}, u32[]{:S(2)}, u32[]{:S(2)}) collective-permute-start(bf16[64,512]{1,0:T(8,128)(2,1)S(1)} %get-tuple-element.77), channel_id=1, source_target_pairs={{0,7},{1,6},{2,5},{3,4},{4,3},{5,2},{6,1},{7,0},{8,15},{9,14},{10,... | collective-permute-start | bytes 196616 | tf_op jit(solution)/shard_map/ppermute | solution.py:69
  32.3 1.5 %collective-permute-start.8 = (bf16[64,512]{1,0:T(8,128)(2,1)S(1)}, bf16[64,512]{1,0:T(8,128)(2,1)S(1)}, u32[]{:S(2)}, u32[]{:S(2)}) collective-permute-start(bf16[64,512]{1,0:T(8,128)(2,1)S(1)} %get-tuple-element.76), channel_id=1, source_target_pairs={{0,4},{1,5},{2,6},{3,7},{4,0},{5,1},{6,2},{7,3},{8,12},{9,13},{10,... | collective-permute-start | bytes 196616 | tf_op jit(solution)/shard_map/ppermute | solution.py:69
  33.8 0.8 %collective-permute-start.9 = (bf16[64,512]{1,0:T(8,128)(2,1)S(1)}, bf16[64,512]{1,0:T(8,128)(2,1)S(1)}, u32[]{:S(2)}, u32[]{:S(2)}) collective-permute-start(bf16[64,512]{1,0:T(8,128)(2,1)S(1)} %get-tuple-element.77), channel_id=1, source_target_pairs={{0,6},{1,7},{2,4},{3,5},{4,2},{5,3},{6,0},{7,1},{8,14},{9,15},{10,... | collective-permute-start | bytes 196616 | tf_op jit(solution)/shard_map/ppermute | solution.py:69
  34.6 1.2 %collective-permute-done.15.refs_2_ = bf16[64,512]{1,0:T(8,128)(2,1)S(1)} collective-permute-done((bf16[64,512]{1,0:T(8,128)(2,1)S(1)}, bf16[64,512]{1,0:T(8,128)(2,1)S(1)}, u32[]{:S(2)}, u32[]{:S(2)}) %collective-permute-start.15) | collective-permute-done | bytes 65568 | tf_op jit(solution)/shard_map/ppermute | solution.py:69
  35.8 1.1 %collective-permute-done.16.refs_3_ = bf16[64,512]{1,0:T(8,128)(2,1)S(1)} collective-permute-done((bf16[64,512]{1,0:T(8,128)(2,1)S(1)}, bf16[64,512]{1,0:T(8,128)(2,1)S(1)}, u32[]{:S(2)}, u32[]{:S(2)}) %collective-permute-start.16) | collective-permute-done | bytes 65568 | tf_op jit(solution)/shard_map/ppermute | solution.py:69
  36.9 1.6 %shard_map.145 = (f32[256,512]{1,0:T(8,128)S(1)}, f32[256,512]{1,0:T(8,128)S(1)}) custom-call(s32[1]{0:T(128)} %bitcast.own_ref, s32[4]{0:T(128)S(1)} %pad_add_fusion.part_ref, bf16[512,512]{1,0:T(8,128)(2,1)S(1)} %bitcast.26, bf16[512,512]{1,0:T(8,128)(2,1)S(1)} %bitcast.29, bf16[160,512]{1,0:T(8,128)(2,1)S(1)} %get-tuple-element.55.extended_ref.refs_0_, ...), custom_call_target="tpu_custom_call" | custom-call | flops 2000000000 | tf_op jit(solution)/shard_map/pallas_call | solution.py:613
  38.5 1.2 %collective-permute-done.9.refs_3_ = bf16[64,512]{1,0:T(8,128)(2,1)S(1)} collective-permute-done((bf16[64,512]{1,0:T(8,128)(2,1)S(1)}, bf16[64,512]{1,0:T(8,128)(2,1)S(1)}, u32[]{:S(2)}, u32[]{:S(2)}) %collective-permute-start.9) | collective-permute-done | bytes 65568 | tf_op jit(solution)/shard_map/ppermute | solution.py:69
  39.7 1.6 %shard_map.146 = (bf16[256,512]{1,0:T(8,128)(2,1)S(1)}, bf16[256,512]{1,0:T(8,128)(2,1)S(1)}, bf16[2,64,512]{2,1,0:T(8,128)(2,1)S(1)}, bf16[2,64,512]{2,1,0:T(8,...) custom-call(s32[1]{0:T(128)} %bitcast.own_ref, s32[4]{0:T(128)S(1)} %pad_add_fusion.part_ref, ...), custom_call_target="tpu_custom_call" | custom-call | flops 2000000000 | tf_op jit(solution)/shard_map/pallas_call | solution.py:613
  41.5 1.1 %collective-permute-start.18 = (bf16[2,64,512]{2,1,0:T(8,128)(2,1)S(1)}, bf16[2,64,512]{2,1,0:T(8,128)(2,1)S(1)}, u32[]{:S(2)}, u32[]{:S(2)}) collective-permute-start(bf16[2,64,512]{2,1,0:T(8,128)(2,1)S(1)} %get-tuple-element.94), channel_id=1, source_target_pairs={{0,16},{8,24},{16,0},{24,8},{1,17},{9,25},{17,1},{25,9},{2,18},{10... | collective-permute-start | bytes 393224 | tf_op jit(solution)/shard_map/ppermute | solution.py:69
  42.6 3.1 %collective-permute-start.19 = (bf16[2,64,512]{2,1,0:T(8,128)(2,1)S(1)}, bf16[2,64,512]{2,1,0:T(8,128)(2,1)S(1)}, u32[]{:S(2)}, u32[]{:S(2)}) collective-permute-start(bf16[2,64,512]{2,1,0:T(8,128)(2,1)S(1)} %get-tuple-element.95), channel_id=1, source_target_pairs={{0,8},{8,0},{16,24},{24,16},{1,9},{9,1},{17,25},{25,17},{2,10},{10... | collective-permute-start | bytes 393224 | tf_op jit(solution)/shard_map/ppermute | solution.py:69
  46.3 0.9 %collective-permute-start.21 = (bf16[128,512]{1,0:T(8,128)(2,1)S(1)}, bf16[128,512]{1,0:T(8,128)(2,1)S(1)}, u32[]{:S(2)}, u32[]{:S(2)}) collective-permute-start(bf16[128,512]{1,0:T(8,128)(2,1)S(1)} %get-tuple-element.99), channel_id=1, source_target_pairs={{0,4},{2,6},{4,0},{6,2},{1,5},{3,7},{5,1},{7,3},{8,12},{10,14},{12... | collective-permute-start | bytes 393224 | tf_op jit(solution)/shard_map/ppermute | solution.py:69
  47.2 2.5 %collective-permute-done.17.refs_1_ = bf16[2,64,512]{2,1,0:T(8,128)(2,1)S(1)} collective-permute-done((bf16[2,64,512]{2,1,0:T(8,128)(2,1)S(1)}, bf16[2,64,512]{2,1,0:T(8,128)(2,1)S(1)}, u32[]{:S(2)}, u32[]{:S(2)}) %collective-permute-start.17) | collective-permute-done | bytes 131104 | tf_op jit(solution)/shard_map/ppermute | solution.py:69
  50.1 4.7 %collective-permute-done.18.refs_2_ = bf16[2,64,512]{2,1,0:T(8,128)(2,1)S(1)} collective-permute-done((bf16[2,64,512]{2,1,0:T(8,128)(2,1)S(1)}, bf16[2,64,512]{2,1,0:T(8,128)(2,1)S(1)}, u32[]{:S(2)}, u32[]{:S(2)}) %collective-permute-start.18) | collective-permute-done | bytes 131104 | tf_op jit(solution)/shard_map/ppermute | solution.py:69
  54.8 1.3 %shard_map.149 = (bf16[128,512]{1,0:T(8,128)(2,1)}, bf16[128,512]{1,0:T(8,128)(2,1)}, f32[64,512]{1,0:T(8,128)}, f32[64,512]{1,0:T(8,128)}) custom-call(bf16[128,256]{1,0:T(8,128)(2,1)S(1)} %get-tuple-element.89.placed_ref, f32[128,128]{1,0:T(8,128)S(1)} %get-tuple-element.90.factors_ref, f32[128,512]{1,0:T(8,128)S(1)} %get-tuple-element.91.router_cols_ref, ...), custom_call_target="tpu_custom_call" | custom-call | flops 1000000000 | tf_op jit(solution)/shard_map/pallas_call | solution.py:666
  (54 shorter events, 4.0 us)
Async XLA Ops:
  0.6 12.8 %collective-permute-start.4 = (bf16[128,512]{1,0:T(8,128)(2,1)}, bf16[128,512]{1,0:T(8,128)(2,1)S(1)}, u32[]{:S(2)}, u32[]{:S(2)}) collective-permute-start(bf16[128,512]{1,0:T(8,128)(2,1)} %bitcast.39), channel_id=1, source_target_pairs={{0,1},{1,0},{2,3},{3,2},{4,5},{5,4},{6,7},{7,6},{8,9},{9,8},{10,11... | collective-permute-start | bytes 393224 | tf_op jit(solution)/shard_map/ppermute | solution.py:69
  3.6 8.4 %collective-permute-start = (bf16[128,512]{1,0:T(8,128)(2,1)}, bf16[128,512]{1,0:T(8,128)(2,1)S(1)}, u32[]{:S(2)}, u32[]{:S(2)}) collective-permute-start(bf16[128,512]{1,0:T(8,128)(2,1)} %bitcast.33), channel_id=1, source_target_pairs={{0,8},{8,16},{16,24},{24,0},{1,9},{9,17},{17,25},{25,1},{2,10},{10... | collective-permute-start | bytes 393224 | tf_op jit(solution)/shard_map/ppermute | solution.py:521
  5.2 8.3 %collective-permute-start.2 = (bf16[128,512]{1,0:T(8,128)(2,1)}, bf16[128,512]{1,0:T(8,128)(2,1)S(1)}, u32[]{:S(2)}, u32[]{:S(2)}) collective-permute-start(bf16[128,512]{1,0:T(8,128)(2,1)} %bitcast.36), channel_id=1, source_target_pairs={{0,8},{8,16},{16,24},{24,0},{1,9},{9,17},{17,25},{25,1},{2,10},{10... | collective-permute-start | bytes 393224 | tf_op jit(solution)/shard_map/ppermute | solution.py:521
  6.8 0.7 %copy-start.8 = (bf16[512,4]{0,1:T(4,128)(2,1)S(1)}, bf16[512,4]{0,1:T(4,128)(2,1)}, u32[]{:S(2)}) copy-start(bf16[512,4]{0,1:T(4,128)(2,1)} %param.17) | copy-start | bytes 12292
  7.5 0.9 %copy-start.3 = (bf16[1,128,512]{2,1,0:T(8,128)(2,1)S(1)}, bf16[1,128,512]{2,1,0:T(8,128)(2,1)}, u32[]{:S(2)}) copy-start(bf16[1,128,512]{2,1,0:T(8,128)(2,1)} %param.21) | copy-start | bytes 393220
  8.4 1.3 %copy-start.4 = (bf16[1,128,512]{2,1,0:T(8,128)(2,1)S(1)}, bf16[1,128,512]{2,1,0:T(8,128)(2,1)}, u32[]{:S(2)}) copy-start(bf16[1,128,512]{2,1,0:T(8,128)(2,1)} %param.12) | copy-start | bytes 393220
  8.4 1.3 %copy-start.5 = (bf16[1,128,512]{2,1,0:T(8,128)(2,1)S(1)}, bf16[1,128,512]{2,1,0:T(8,128)(2,1)}, u32[]{:S(2)}) copy-start(bf16[1,128,512]{2,1,0:T(8,128)(2,1)} %param.13) | copy-start | bytes 393220
  8.4 1.3 %copy-start.6 = (bf16[1,128,512]{2,1,0:T(8,128)(2,1)S(1)}, bf16[1,128,512]{2,1,0:T(8,128)(2,1)}, u32[]{:S(2)}) copy-start(bf16[1,128,512]{2,1,0:T(8,128)(2,1)} %param.11) | copy-start | bytes 393220
  9.0 12.5 %collective-permute-start.5 = (bf16[160,512]{1,0:T(8,128)(2,1)S(1)}, bf16[160,512]{1,0:T(8,128)(2,1)S(1)}, u32[]{:S(2)}, u32[]{:S(2)}) collective-permute-start(bf16[160,512]{1,0:T(8,128)(2,1)S(1)} %get-tuple-element.55.extended_ref.refs_0_), channel_id=1, source_target_pairs={{0,1},{1,0},{2,3},{3,2},{4,5},{5,4},{6,7},{7,6},{8,9},{9,8},{10,11... | collective-permute-start | bytes 491528 | tf_op jit(solution)/shard_map/ppermute | solution.py:69
  12.1 8.7 %collective-permute-start.1 = (bf16[128,512]{1,0:T(8,128)(2,1)S(1)}, bf16[128,512]{1,0:T(8,128)(2,1)S(1)}, u32[]{:S(2)}, u32[]{:S(2)}) collective-permute-start(bf16[128,512]{1,0:T(8,128)(2,1)S(1)} %collective-permute-done.refs_4_), channel_id=1, source_target_pairs={{0,8},{8,16},{16,24},{24,0},{1,9},{9,17},{17,25},{25,1},{2,10},{10... | collective-permute-start | bytes 393224 | tf_op jit(solution)/shard_map/ppermute | solution.py:521
  13.5 7.3 %collective-permute-start.3 = (bf16[128,512]{1,0:T(8,128)(2,1)S(1)}, bf16[128,512]{1,0:T(8,128)(2,1)S(1)}, u32[]{:S(2)}, u32[]{:S(2)}) collective-permute-start(bf16[128,512]{1,0:T(8,128)(2,1)S(1)} %collective-permute-done.2.refs_5_), channel_id=1, source_target_pairs={{0,8},{8,16},{16,24},{24,0},{1,9},{9,17},{17,25},{25,1},{2,10},{10... | collective-permute-start | bytes 393224 | tf_op jit(solution)/shard_map/ppermute | solution.py:521
  21.6 5.3 %collective-permute-start.6 = (bf16[592,128]{1,0:T(8,128)(2,1)S(1)}, bf16[592,128]{1,0:T(8,128)(2,1)S(1)}, u32[]{:S(2)}, u32[]{:S(2)}) collective-permute-start(bf16[592,128]{1,0:T(8,128)(2,1)S(1)} %shard_map.142), channel_id=1, source_target_pairs={{0,1},{1,0},{2,3},{3,2},{4,5},{5,4},{6,7},{7,6},{8,9},{9,8},{10,11... | collective-permute-start | bytes 454664 | tf_op jit(solution)/shard_map/ppermute | solution.py:69
  23.3 5.4 %collective-permute-start.10 = (bf16[128,512]{1,0:T(8,128)(2,1)S(1)}, bf16[128,512]{1,0:T(8,128)(2,1)S(1)}, u32[]{:S(2)}, u32[]{:S(2)}) collective-permute-start(bf16[128,512]{1,0:T(8,128)(2,1)S(1)} %get-tuple-element.80), channel_id=1, source_target_pairs={{0,2},{2,0},{4,6},{6,4},{1,3},{3,1},{5,7},{7,5},{8,10},{10,8},{12,... | collective-permute-start | bytes 393224 | tf_op jit(solution)/shard_map/ppermute | solution.py:69
  23.4 7.1 %collective-permute-start.11 = (bf16[128,512]{1,0:T(8,128)(2,1)S(1)}, bf16[128,512]{1,0:T(8,128)(2,1)S(1)}, u32[]{:S(2)}, u32[]{:S(2)}) collective-permute-start(bf16[128,512]{1,0:T(8,128)(2,1)S(1)} %get-tuple-element.81), channel_id=1, source_target_pairs={{0,4},{2,6},{4,0},{6,2},{1,5},{3,7},{5,1},{7,3},{8,12},{10,14},{12... | collective-permute-start | bytes 393224 | tf_op jit(solution)/shard_map/ppermute | solution.py:69
  25.0 7.0 %collective-permute-start.12 = (bf16[128,512]{1,0:T(8,128)(2,1)S(1)}, bf16[128,512]{1,0:T(8,128)(2,1)S(1)}, u32[]{:S(2)}, u32[]{:S(2)}) collective-permute-start(bf16[128,512]{1,0:T(8,128)(2,1)S(1)} %get-tuple-element.82), channel_id=1, source_target_pairs={{0,6},{2,4},{4,2},{6,0},{1,7},{3,5},{5,3},{7,1},{8,14},{10,12},{12... | collective-permute-start | bytes 393224 | tf_op jit(solution)/shard_map/ppermute | solution.py:69
  25.3 1.5 %copy-start = (bf16[512,512]{1,0:T(8,128)(2,1)S(1)}, bf16[512,512]{1,0:T(8,128)(2,1)}, u32[]{:S(2)}) copy-start(bf16[512,512]{1,0:T(8,128)(2,1)} %proj_ref.1) | copy-start | bytes 1572868
  25.3 1.5 %copy-start.7 = (bf16[1,128,512]{2,1,0:T(8,128)(2,1)S(1)}, bf16[1,128,512]{2,1,0:T(8,128)(2,1)}, u32[]{:S(2)}) copy-start(bf16[1,128,512]{2,1,0:T(8,128)(2,1)} %param.15) | copy-start | bytes 393220
  26.8 10.0 %copy-start.1 = (bf16[1,512,512]{2,1,0:T(8,128)(2,1)S(1)}, bf16[1,512,512]{2,1,0:T(8,128)(2,1)}, u32[]{:S(2)}) copy-start(bf16[1,512,512]{2,1,0:T(8,128)(2,1)} %param.19) | copy-start | bytes 1572868
  26.8 10.0 %copy-start.2 = (bf16[1,512,512]{2,1,0:T(8,128)(2,1)S(1)}, bf16[1,512,512]{2,1,0:T(8,128)(2,1)}, u32[]{:S(2)}) copy-start(bf16[1,512,512]{2,1,0:T(8,128)(2,1)} %param.20) | copy-start | bytes 1572868
  27.4 4.8 %collective-permute-start.13 = (bf16[64,512]{1,0:T(8,128)(2,1)S(1)}, bf16[64,512]{1,0:T(8,128)(2,1)S(1)}, u32[]{:S(2)}, u32[]{:S(2)}) collective-permute-start(bf16[64,512]{1,0:T(8,128)(2,1)S(1)} %get-tuple-element.74.refs_0_), channel_id=1, source_target_pairs={{0,1},{1,0},{2,3},{3,2},{4,5},{5,4},{6,7},{7,6},{8,9},{9,8},{10,11... | collective-permute-start | bytes 196616 | tf_op jit(solution)/shard_map/ppermute | solution.py:69
  28.7 5.1 %collective-permute-start.14 = (bf16[64,512]{1,0:T(8,128)(2,1)S(1)}, bf16[64,512]{1,0:T(8,128)(2,1)S(1)}, u32[]{:S(2)}, u32[]{:S(2)}) collective-permute-start(bf16[64,512]{1,0:T(8,128)(2,1)S(1)} %get-tuple-element.75), channel_id=1, source_target_pairs={{0,3},{1,2},{2,1},{3,0},{4,7},{5,6},{6,5},{7,4},{8,11},{9,10},{10,... | collective-permute-start | bytes 196616 | tf_op jit(solution)/shard_map/ppermute | solution.py:69
  28.7 7.1 %collective-permute-start.15 = (bf16[64,512]{1,0:T(8,128)(2,1)S(1)}, bf16[64,512]{1,0:T(8,128)(2,1)S(1)}, u32[]{:S(2)}, u32[]{:S(2)}) collective-permute-start(bf16[64,512]{1,0:T(8,128)(2,1)S(1)} %get-tuple-element.76), channel_id=1, source_target_pairs={{0,5},{1,4},{2,7},{3,6},{4,1},{5,0},{6,3},{7,2},{8,13},{9,12},{10,... | collective-permute-start | bytes 196616 | tf_op jit(solution)/shard_map/ppermute | solution.py:69
  30.5 6.3 %collective-permute-start.16 = (bf16[64,512]{1,0:T(8,128)(2,1)S(1)}, bf16[64,512]{1,0:T(8,128)(2,1)S(1)}, u32[]{:S(2)}, u32[]{:S(2)}) collective-permute-start(bf16[64,512]{1,0:T(8,128)(2,1)S(1)} %get-tuple-element.77), channel_id=1, source_target_pairs={{0,7},{1,6},{2,5},{3,4},{4,3},{5,2},{6,1},{7,0},{8,15},{9,14},{10,... | collective-permute-start | bytes 196616 | tf_op jit(solution)/shard_map/ppermute | solution.py:69
  32.0 6.5 %collective-permute-start.7 = (bf16[64,512]{1,0:T(8,128)(2,1)S(1)}, bf16[64,512]{1,0:T(8,128)(2,1)S(1)}, u32[]{:S(2)}, u32[]{:S(2)}) collective-permute-start(bf16[64,512]{1,0:T(8,128)(2,1)S(1)} %get-tuple-element.75), channel_id=1, source_target_pairs={{0,2},{1,3},{2,0},{3,1},{4,6},{5,7},{6,4},{7,5},{8,10},{9,11},{10,... | collective-permute-start | bytes 196616 | tf_op jit(solution)/shard_map/ppermute | solution.py:69
  32.3 6.2 %collective-permute-start.8 = (bf16[64,512]{1,0:T(8,128)(2,1)S(1)}, bf16[64,512]{1,0:T(8,128)(2,1)S(1)}, u32[]{:S(2)}, u32[]{:S(2)}) collective-permute-start(bf16[64,512]{1,0:T(8,128)(2,1)S(1)} %get-tuple-element.76), channel_id=1, source_target_pairs={{0,4},{1,5},{2,6},{3,7},{4,0},{5,1},{6,2},{7,3},{8,12},{9,13},{10,... | collective-permute-start | bytes 196616 | tf_op jit(solution)/shard_map/ppermute | solution.py:69
  33.8 5.9 %collective-permute-start.9 = (bf16[64,512]{1,0:T(8,128)(2,1)S(1)}, bf16[64,512]{1,0:T(8,128)(2,1)S(1)}, u32[]{:S(2)}, u32[]{:S(2)}) collective-permute-start(bf16[64,512]{1,0:T(8,128)(2,1)S(1)} %get-tuple-element.77), channel_id=1, source_target_pairs={{0,6},{1,7},{2,4},{3,5},{4,2},{5,3},{6,0},{7,1},{8,14},{9,15},{10,... | collective-permute-start | bytes 196616 | tf_op jit(solution)/shard_map/ppermute | solution.py:69
  41.3 8.3 %collective-permute-start.17 = (bf16[2,64,512]{2,1,0:T(8,128)(2,1)S(1)}, bf16[2,64,512]{2,1,0:T(8,128)(2,1)S(1)}, u32[]{:S(2)}, u32[]{:S(2)}) collective-permute-start(bf16[2,64,512]{2,1,0:T(8,128)(2,1)S(1)} %get-tuple-element.93), channel_id=1, source_target_pairs={{0,24},{8,16},{16,8},{24,0},{1,25},{9,17},{17,9},{25,1},{2,26},{10... | collective-permute-start | bytes 393224 | tf_op jit(solution)/shard_map/ppermute | solution.py:69
  41.5 13.3 %collective-permute-start.18 = (bf16[2,64,512]{2,1,0:T(8,128)(2,1)S(1)}, bf16[2,64,512]{2,1,0:T(8,128)(2,1)S(1)}, u32[]{:S(2)}, u32[]{:S(2)}) collective-permute-start(bf16[2,64,512]{2,1,0:T(8,128)(2,1)S(1)} %get-tuple-element.94), channel_id=1, source_target_pairs={{0,16},{8,24},{16,0},{24,8},{1,17},{9,25},{17,1},{25,9},{2,18},{10... | collective-permute-start | bytes 393224 | tf_op jit(solution)/shard_map/ppermute | solution.py:69
  42.6 12.2 %collective-permute-start.19 = (bf16[2,64,512]{2,1,0:T(8,128)(2,1)S(1)}, bf16[2,64,512]{2,1,0:T(8,128)(2,1)S(1)}, u32[]{:S(2)}, u32[]{:S(2)}) collective-permute-start(bf16[2,64,512]{2,1,0:T(8,128)(2,1)S(1)} %get-tuple-element.95), channel_id=1, source_target_pairs={{0,8},{8,0},{16,24},{24,16},{1,9},{9,1},{17,25},{25,17},{2,10},{10... | collective-permute-start | bytes 393224 | tf_op jit(solution)/shard_map/ppermute | solution.py:69
  46.2 8.6 %collective-permute-start.20 = (bf16[128,512]{1,0:T(8,128)(2,1)S(1)}, bf16[128,512]{1,0:T(8,128)(2,1)S(1)}, u32[]{:S(2)}, u32[]{:S(2)}) collective-permute-start(bf16[128,512]{1,0:T(8,128)(2,1)S(1)} %get-tuple-element.98), channel_id=1, source_target_pairs={{0,6},{2,4},{4,2},{6,0},{1,7},{3,5},{5,3},{7,1},{8,14},{10,12},{12... | collective-permute-start | bytes 393224 | tf_op jit(solution)/shard_map/ppermute | solution.py:69
  46.3 8.5 %collective-permute-start.21 = (bf16[128,512]{1,0:T(8,128)(2,1)S(1)}, bf16[128,512]{1,0:T(8,128)(2,1)S(1)}, u32[]{:S(2)}, u32[]{:S(2)}) collective-permute-start(bf16[128,512]{1,0:T(8,128)(2,1)S(1)} %get-tuple-element.99), channel_id=1, source_target_pairs={{0,4},{2,6},{4,0},{6,2},{1,5},{3,7},{5,1},{7,3},{8,12},{10,14},{12... | collective-permute-start | bytes 393224 | tf_op jit(solution)/shard_map/ppermute | solution.py:69
  49.7 5.2 %collective-permute-start.22 = (bf16[128,512]{1,0:T(8,128)(2,1)S(1)}, bf16[128,512]{1,0:T(8,128)(2,1)S(1)}, u32[]{:S(2)}, u32[]{:S(2)}) collective-permute-start(bf16[128,512]{1,0:T(8,128)(2,1)S(1)} %get-tuple-element.100), channel_id=1, source_target_pairs={{0,2},{2,0},{4,6},{6,4},{1,3},{3,1},{5,7},{7,5},{8,10},{10,8},{12,... | collective-permute-start | bytes 393224 | tf_op jit(solution)/shard_map/ppermute | solution.py:69
  (2 other events, 1.3 us)

commit v17 on v16

--- a/solution.py
+++ b/solution.py
@@ -303,6 +303,16 @@
         sent_ref[...] = rows[k * hot_capacity : (k + 1) * hot_capacity]
 
 
+def grad_plan(parts):
+    if parts == 4:
+        return [[(0, 0), (1, 0), (1, 2)], [(0, 1), (1, 1), (1, 3)], [(0, 2)], [(0, 3)]]
+    return [[(0, 0), (1, 0)]] + [[(0, k), (1, k)] for k in range(1, parts)]
+
+
+def pair_kernel(kept_ref, near_ref, sent_ref):
+    sent_ref[0] = (kept_ref[2] + near_ref[2].astype(jnp.float32)).astype(jnp.bfloat16)
+
+
 def expert_kernel(
     reps,
     rep_list,
@@ -376,10 +386,10 @@
         return
     up_term = up_term + up_old[...]
     down_term = down_term + down_old[...]
-    for k, ref in enumerate((kept_ref, *term_refs)):
-        rows = slice(k * strip, (k + 1) * strip)
-        ref[0] = up_term[rows].astype(ref.dtype)
-        ref[1] = down_term[rows].astype(ref.dtype)
+    for ref, entries in zip((kept_ref, *term_refs), grad_plan(parts)):
+        for place, (kind, k) in enumerate(entries):
+            term = (up_term, down_term)[kind][k * strip : (k + 1) * strip]
+            ref[place] = term.astype(ref.dtype)
 
 
 def back_kernel(sources, up_ref, down_ref, activated_ref, pre_grad_ref, *back_refs):
@@ -421,7 +431,7 @@
 
 def finish_kernel(
     hot_capacity,
-    parts,
+    plan,
     placed_ref,
     factors_ref,
     router_cols_ref,
@@ -430,11 +440,13 @@
     *refs,
 ):
     refs, (layer_ref, grad_mixed_ref, *share_refs) = refs[:-4], refs[-4:]
-    (kept_ref, *term_refs), back_refs = refs[:parts], refs[parts:][::-1]
-    for kind, share_ref in enumerate(share_refs):
-        total = kept_ref[kind]
-        for ref in term_refs:
-            total = total + ref[kind].astype(jnp.float32)
+    kept_ref, *refs = refs
+    term_refs, back_refs = refs[: len(plan)], refs[len(plan) :][::-1]
+    totals = [kept_ref[0], kept_ref[1]]
+    for kinds, ref in zip(plan, term_refs):
+        for place, kind in enumerate(kinds):
+            totals[kind] = totals[kind] + ref[place].astype(jnp.float32)
+    for total, share_ref in zip(totals, share_refs):
         share_ref[...] = total
     tok = mixed_ref.shape[0]
     mixed_f = mixed_ref[...].astype(jnp.float32)
@@ -640,11 +652,19 @@
         (0,),
         got_rows,
         [shape((slots, hidden))] * 2
-        + [shape((2, strip, hidden))] * (seq_count - 1)
-        + [shape((2, strip, hidden), jnp.float32)],
+        + [shape((len(entries), strip, hidden)) for entries in grad_plan(seq_count)[1:]]
+        + [shape((len(grad_plan(seq_count)[0]), strip, hidden), jnp.float32)],
         list(sums),
     )
-    got_terms = parts.exchange([None] + terms)[1:]
+    if seq_count == 4:
+        near, *direct = parts.exchange([None] + terms)[1:]
+        crossing = call(pair_kernel, shape((1, strip, hidden)), [VMEM, VMEM])(kept, near)
+        crossed = lax.ppermute(crossing, "seq", [(i, parts.target(i, 2)) for i in range(4)])
+        got_terms = [near, *direct, crossed]
+        plan = ((0, 1), (0,), (0,), (1,))
+    else:
+        got_terms = parts.exchange([None] + terms)[1:]
+        plan = ((0, 1),) * len(got_terms)
     activated, mixed, kept = lax.optimization_barrier((activated, mixed, kept))
     back = call(
         functools.partial(back_kernel, expert_count),
@@ -664,16 +684,16 @@
         cost=1.0,
     )(own, mixed, extended)
     layer_out, grad_mixed, share_in, share_out = call(
-        functools.partial(finish_kernel, hot_capacity, seq_count),
+        functools.partial(finish_kernel, hot_capacity, plan),
         [
             shape((tok, width)),
             shape((tok, width)),
             shape((strip, hidden), jnp.float32),
             shape((strip, width), jnp.float32),
         ],
-        [VMEM] * (5 + seq_count + len(got_back)),
+        [VMEM] * (6 + len(got_terms) + len(got_back)),
         cost=1.0,
-    )(*prepared, mixed, extended, kept, *got_terms[::-1], *got_back[::-1])
+    )(*prepared, mixed, extended, kept, *got_terms, *got_back[::-1])
     return (layer_out[None], grad_mixed[None], share_in[None], share_out[None])
 
 

time: 56 us -> 57.7 us (1.030); the launches traced: 56.1 us -> 56.7 us
  starting transfers between devices: 23.6 us -> 25 us
  waiting for transfers between devices: 17.3 us -> 16.5 us
    ppermute x19, waiting for transfers between devices: 11.4 us -> 9.03 us  [exchange(): got[k] = lax.ppermute(chunks[k], self.axes, pairs)]
    ppermute x0 -> x1, waiting for transfers between devices: none -> 1.64 us  [local(): lax.ppermute(crossing, 'seq', [(i, parts.target(i, 2)) for i in range(4)])]
    ppermute x0 -> x1, starting transfers between devices: none -> 1.38 us  [local(): lax.ppermute(crossing, 'seq', [(i, parts.target(i, 2)) for i in range(4)])]
    pallas_call x1 -> x2, Pallas kernels: 1.26 us -> 1.28 us  [the longest x1 1.26 us: local(): call(functools.partial(finish_kernel, hot_capacity, plan), [shape((tok, w...]
  transfers between devices with their start and end apart: 23 -> 24, of which waited for: 9 -> 11; matrix products, arithmetic and copies ran while one was open for 1% -> 1% of each run, Pallas kernels for 17% -> 17%
where the time goes in v17:
time: 57.7 us; the launch traced here: 56.7 us
  starting transfers between devices  25 us (43%)
  waiting for transfers between devices  16.5 us (29%)
  Pallas kernels  12.3 us (21%)
  local copies, waits for them, and re-layouts  1.69 us (3%)
  between operations  0.83 us (1%)
    ppermute x19, starting transfers between devices, exchange(): got[k] = lax.ppermute(chunks[k], self.axes, pairs)  19.2 us
    ppermute x19, waiting for transfers between devices, exchange(): got[k] = lax.ppermute(chunks[k], self.axes, pairs)  9.03 us
    ppermute x4, waiting for transfers between devices, forward(): lax.ppermute(array, 'seq', [(i, (i + 1) % seq_count) for i in range(seq_c...  5.86 us
    pallas_call x4, Pallas kernels, attend(): call(functools.partial(attend_kernel, plan, rep_count, len(pairs), packed...  5.19 us
    ppermute x4, starting transfers between devices, forward(): lax.ppermute(array, 'seq', [(i, (i + 1) % seq_count) for i in range(seq_c...  4.4 us
    pallas_call x2, Pallas kernels, expert_call(): call(functools.partial(expert_kernel, rep_count, rep_list, expert_count,...  3.24 us
    ppermute x1, waiting for transfers between devices, local(): lax.ppermute(crossing, 'seq', [(i, parts.target(i, 2)) for i in range(4)])  1.64 us
    unnamed x22, local copies, waits for them, and re-layouts  1.6 us
  transfers between devices with their start and end apart: 24, of which 11 were waited for; matrix products, arithmetic and copies ran while one was open for 1% of the time, Pallas kernels for 17%

profile of v17, /device:TPU:0, one launch (start us, length us, event | category | flops | bytes accessed | tf_op | source)
XLA Modules:
  0.0 56.7 jit_solution(4793069178922781569)
XLA Ops:
  0.6 3.0 %collective-permute-start.4 = (bf16[128,512]{1,0:T(8,128)(2,1)}, bf16[128,512]{1,0:T(8,128)(2,1)S(1)}, u32[]{:S(2)}, u32[]{:S(2)}) collective-permute-start(bf16[128,512]{1,0:T(8,128)(2,1)} %bitcast.39), channel_id=1, source_target_pairs={{0,1},{1,0},{2,3},{3,2},{4,5},{5,4},{6,7},{7,6},{8,9},{9,8},{10,11... | collective-permute-start | bytes 393224 | tf_op jit(solution)/shard_map/ppermute | solution.py:69
  3.6 1.6 %collective-permute-start = (bf16[128,512]{1,0:T(8,128)(2,1)}, bf16[128,512]{1,0:T(8,128)(2,1)S(1)}, u32[]{:S(2)}, u32[]{:S(2)}) collective-permute-start(bf16[128,512]{1,0:T(8,128)(2,1)} %bitcast.33), channel_id=1, source_target_pairs={{0,8},{8,16},{16,24},{24,0},{1,9},{9,17},{17,25},{25,1},{2,10},{10... | collective-permute-start | bytes 393224 | tf_op jit(solution)/shard_map/ppermute | solution.py:533
  5.2 1.6 %collective-permute-start.2 = (bf16[128,512]{1,0:T(8,128)(2,1)}, bf16[128,512]{1,0:T(8,128)(2,1)S(1)}, u32[]{:S(2)}, u32[]{:S(2)}) collective-permute-start(bf16[128,512]{1,0:T(8,128)(2,1)} %bitcast.36), channel_id=1, source_target_pairs={{0,8},{8,16},{16,24},{24,0},{1,9},{9,17},{17,25},{25,1},{2,10},{10... | collective-permute-start | bytes 393224 | tf_op jit(solution)/shard_map/ppermute | solution.py:533
  7.5 0.9 %copy-done.3 = bf16[1,128,512]{2,1,0:T(8,128)(2,1)S(1)} copy-done((bf16[1,128,512]{2,1,0:T(8,128)(2,1)S(1)}, bf16[1,128,512]{2,1,0:T(8,128)(2,1)}, u32[]{:S(2)}) %copy-start.3) | copy-done | bytes 131096
  9.7 1.7 %shard_map.139 = (f32[16,128]{1,0:T(8,128)S(1)}, f32[16,128]{1,0:T(8,128)S(1)}, f32[512,128]{1,0:T(8,128)S(1)}) custom-call(s32[3]{0:T(128)S(1)} %pad_add_fusion.4.ids_ref, s32[2,128]{1,0:T(2,128)S(1)} %get-tuple-element.56.begin_ref, bf16[128,512]{1,0:T(8,128)(2,1)S(1)} %bitcast.40, bf16[128,512]{1,0:T(8,128)(2,1)S(1)} %bitcast.34, ...), custom_call_target="tpu_custom_call" | custom-call | flops 2000000000 | tf_op jit(solution)/shard_map/pallas_call | solution.py:572
  12.1 1.2 %collective-permute-start.1 = (bf16[128,512]{1,0:T(8,128)(2,1)S(1)}, bf16[128,512]{1,0:T(8,128)(2,1)S(1)}, u32[]{:S(2)}, u32[]{:S(2)}) collective-permute-start(bf16[128,512]{1,0:T(8,128)(2,1)S(1)} %collective-permute-done.refs_4_), channel_id=1, source_target_pairs={{0,8},{8,16},{16,24},{24,0},{1,9},{9,17},{17,25},{25,1},{2,10},{10... | collective-permute-start | bytes 393224 | tf_op jit(solution)/shard_map/ppermute | solution.py:533
  13.5 1.9 %shard_map.140 = (f32[16,128]{1,0:T(8,128)S(1)}, f32[16,128]{1,0:T(8,128)S(1)}, f32[512,128]{1,0:T(8,128)S(1)}, f32[16,128]{1,0:T(8,128)S(1)}, f32[16,128]{1,0:T(8,128)S(1)}, /*index=5*/f32[512,128]{1,0:T(8,128)S(1)}) custom-call(s32[5]{0:T(128)S(1)} %stack.81.ids_ref, s32[2,128]{1,0:T(2,128)S(1)} %get-tuple-element.56.begin_ref, ...), custom_call_target="tpu_custom_call" | custom-call | flops 4000000000 | tf_op jit(solution)/shard_map/pallas_call | solution.py:572
  15.4 5.4 %collective-permute-done.3.refs_2_ = bf16[128,512]{1,0:T(8,128)(2,1)S(1)} collective-permute-done((bf16[128,512]{1,0:T(8,128)(2,1)S(1)}, bf16[128,512]{1,0:T(8,128)(2,1)S(1)}, u32[]{:S(2)}, u32[]{:S(2)}) %collective-permute-start.3) | collective-permute-done | bytes 131104 | tf_op jit(solution)/shard_map/ppermute | solution.py:533
  20.8 0.8 %shard_map.142 = bf16[592,128]{1,0:T(8,128)(2,1)S(1)} custom-call(s32[3]{0:T(128)S(1)} %pad_add_fusion.5.ids_ref, s32[2,128]{1,0:T(2,128)S(1)} %get-tuple-element.56.begin_ref, bf16[128,512]{1,0:T(8,128)(2,1)S(1)} %collective-permute-done.4.refs_1_.refs_0_, bf16[128,512]{1,0:T(8,128)(2,1)S(1)} %collective-permute-done.1.refs_1_, ...), custom_call_target="tpu_custom_call" | custom-call | flops 1500000000 | tf_op jit(solution)/shard_map/pallas_call | solution.py:572
  21.6 1.2 %collective-permute-start.6 = (bf16[592,128]{1,0:T(8,128)(2,1)S(1)}, bf16[592,128]{1,0:T(8,128)(2,1)S(1)}, u32[]{:S(2)}, u32[]{:S(2)}) collective-permute-start(bf16[592,128]{1,0:T(8,128)(2,1)S(1)} %shard_map.142), channel_id=1, source_target_pairs={{0,1},{1,0},{2,3},{3,2},{4,5},{5,4},{6,7},{7,6},{8,9},{9,8},{10,11... | collective-permute-start | bytes 454664 | tf_op jit(solution)/shard_map/ppermute | solution.py:69
  23.4 1.6 %collective-permute-start.11 = (bf16[128,512]{1,0:T(8,128)(2,1)S(1)}, bf16[128,512]{1,0:T(8,128)(2,1)S(1)}, u32[]{:S(2)}, u32[]{:S(2)}) collective-permute-start(bf16[128,512]{1,0:T(8,128)(2,1)S(1)} %get-tuple-element.81), channel_id=1, source_target_pairs={{0,4},{2,6},{4,0},{6,2},{1,5},{3,7},{5,1},{7,3},{8,12},{10,14},{12... | collective-permute-start | bytes 393224 | tf_op jit(solution)/shard_map/ppermute | solution.py:69
  25.3 0.7 %shard_map.141 = (f32[16,128]{1,0:T(8,128)S(1)}, f32[16,128]{1,0:T(8,128)S(1)}, f32[512,128]{1,0:T(8,128)S(1)}) custom-call(s32[3]{0:T(128)S(1)} %pad_add_fusion.2.ids_ref, s32[2,128]{1,0:T(2,128)S(1)} %get-tuple-element.56.begin_ref, bf16[128,512]{1,0:T(8,128)(2,1)S(1)} %bitcast.42, bf16[128,512]{1,0:T(8,128)(2,1)S(1)} %collective-permute-done.1.refs_1_, ...), custom_call_target="tpu_custom_call" | custom-call | flops 1500000000 | tf_op jit(solution)/shard_map/pallas_call | solution.py:572
  26.0 0.8 %collective-permute-done.6.refs_3_ = bf16[592,128]{1,0:T(8,128)(2,1)S(1)} collective-permute-done((bf16[592,128]{1,0:T(8,128)(2,1)S(1)}, bf16[592,128]{1,0:T(8,128)(2,1)S(1)}, u32[]{:S(2)}, u32[]{:S(2)}) %collective-permute-start.6) | collective-permute-done | bytes 151584 | tf_op jit(solution)/shard_map/ppermute | solution.py:69
  26.8 0.6 %shard_map.143 = (bf16[128,512]{1,0:T(8,128)(2,1)S(1)}, bf16[64,512]{1,0:T(8,128)(2,1)S(1)}, bf16[64,512]{1,0:T(8,128)(2,1)S(1)}, bf16[64,512]{1,0:T(8,128)(2,1)S(1)}, bf16[64,512]{1,0:T(8,128)(2,1)S(1)}) custom-call(s32[1]{0:T(128)} %bitcast.own_ref, bf16[160,512]{1,0:T(8,128)(2,1)S(1)} %get-tuple-element.55.extended_ref.refs_0_, ...), custom_call_target="tpu_custom_call" | custom-call | flops 2000000000 | tf_op jit(solution)/shard_map/pallas_call | solution.py:612
  27.4 1.2 %collective-permute-start.13 = (bf16[64,512]{1,0:T(8,128)(2,1)S(1)}, bf16[64,512]{1,0:T(8,128)(2,1)S(1)}, u32[]{:S(2)}, u32[]{:S(2)}) collective-permute-start(bf16[64,512]{1,0:T(8,128)(2,1)S(1)} %get-tuple-element.74.refs_0_), channel_id=1, source_target_pairs={{0,1},{1,0},{2,3},{3,2},{4,5},{5,4},{6,7},{7,6},{8,9},{9,8},{10,11... | collective-permute-start | bytes 196616 | tf_op jit(solution)/shard_map/ppermute | solution.py:69
  28.7 1.8 %collective-permute-start.15 = (bf16[64,512]{1,0:T(8,128)(2,1)S(1)}, bf16[64,512]{1,0:T(8,128)(2,1)S(1)}, u32[]{:S(2)}, u32[]{:S(2)}) collective-permute-start(bf16[64,512]{1,0:T(8,128)(2,1)S(1)} %get-tuple-element.76), channel_id=1, source_target_pairs={{0,5},{1,4},{2,7},{3,6},{4,1},{5,0},{6,3},{7,2},{8,13},{9,12},{10,... | collective-permute-start | bytes 196616 | tf_op jit(solution)/shard_map/ppermute | solution.py:69
  30.5 1.4 %collective-permute-start.16 = (bf16[64,512]{1,0:T(8,128)(2,1)S(1)}, bf16[64,512]{1,0:T(8,128)(2,1)S(1)}, u32[]{:S(2)}, u32[]{:S(2)}) collective-permute-start(bf16[64,512]{1,0:T(8,128)(2,1)S(1)} %get-tuple-element.77), channel_id=1, source_target_pairs={{0,7},{1,6},{2,5},{3,4},{4,3},{5,2},{6,1},{7,0},{8,15},{9,14},{10,... | collective-permute-start | bytes 196616 | tf_op jit(solution)/shard_map/ppermute | solution.py:69
  32.3 1.5 %collective-permute-start.8 = (bf16[64,512]{1,0:T(8,128)(2,1)S(1)}, bf16[64,512]{1,0:T(8,128)(2,1)S(1)}, u32[]{:S(2)}, u32[]{:S(2)}) collective-permute-start(bf16[64,512]{1,0:T(8,128)(2,1)S(1)} %get-tuple-element.76), channel_id=1, source_target_pairs={{0,4},{1,5},{2,6},{3,7},{4,0},{5,1},{6,2},{7,3},{8,12},{9,13},{10,... | collective-permute-start | bytes 196616 | tf_op jit(solution)/shard_map/ppermute | solution.py:69
  33.8 0.8 %collective-permute-start.9 = (bf16[64,512]{1,0:T(8,128)(2,1)S(1)}, bf16[64,512]{1,0:T(8,128)(2,1)S(1)}, u32[]{:S(2)}, u32[]{:S(2)}) collective-permute-start(bf16[64,512]{1,0:T(8,128)(2,1)S(1)} %get-tuple-element.77), channel_id=1, source_target_pairs={{0,6},{1,7},{2,4},{3,5},{4,2},{5,3},{6,0},{7,1},{8,14},{9,15},{10,... | collective-permute-start | bytes 196616 | tf_op jit(solution)/shard_map/ppermute | solution.py:69
  34.6 1.2 %collective-permute-done.15.refs_2_ = bf16[64,512]{1,0:T(8,128)(2,1)S(1)} collective-permute-done((bf16[64,512]{1,0:T(8,128)(2,1)S(1)}, bf16[64,512]{1,0:T(8,128)(2,1)S(1)}, u32[]{:S(2)}, u32[]{:S(2)}) %collective-permute-start.15) | collective-permute-done | bytes 65568 | tf_op jit(solution)/shard_map/ppermute | solution.py:69
  35.8 1.1 %collective-permute-done.16.refs_3_ = bf16[64,512]{1,0:T(8,128)(2,1)S(1)} collective-permute-done((bf16[64,512]{1,0:T(8,128)(2,1)S(1)}, bf16[64,512]{1,0:T(8,128)(2,1)S(1)}, u32[]{:S(2)}, u32[]{:S(2)}) %collective-permute-start.16) | collective-permute-done | bytes 65568 | tf_op jit(solution)/shard_map/ppermute | solution.py:69
  36.9 1.6 %shard_map.145 = (f32[256,512]{1,0:T(8,128)S(1)}, f32[256,512]{1,0:T(8,128)S(1)}) custom-call(s32[1]{0:T(128)} %bitcast.own_ref, s32[4]{0:T(128)S(1)} %pad_add_fusion.part_ref, bf16[512,512]{1,0:T(8,128)(2,1)S(1)} %bitcast.26, bf16[512,512]{1,0:T(8,128)(2,1)S(1)} %bitcast.29, bf16[160,512]{1,0:T(8,128)(2,1)S(1)} %get-tuple-element.55.extended_ref.refs_0_, ...), custom_call_target="tpu_custom_call" | custom-call | flops 2000000000 | tf_op jit(solution)/shard_map/pallas_call | solution.py:625
  38.5 1.2 %collective-permute-done.9.refs_3_ = bf16[64,512]{1,0:T(8,128)(2,1)S(1)} collective-permute-done((bf16[64,512]{1,0:T(8,128)(2,1)S(1)}, bf16[64,512]{1,0:T(8,128)(2,1)S(1)}, u32[]{:S(2)}, u32[]{:S(2)}) %collective-permute-start.9) | collective-permute-done | bytes 65568 | tf_op jit(solution)/shard_map/ppermute | solution.py:69
  39.7 1.6 %shard_map.146 = (bf16[256,512]{1,0:T(8,128)(2,1)S(1)}, bf16[256,512]{1,0:T(8,128)(2,1)S(1)}, bf16[3,64,512]{2,1,0:T(8,128)(2,1)S(1)}, bf16[1,64,512]{2,1,0:T(8,...) custom-call(s32[1]{0:T(128)} %bitcast.own_ref, s32[4]{0:T(128)S(1)} %pad_add_fusion.part_ref, ...), custom_call_target="tpu_custom_call" | custom-call | flops 2000000000 | tf_op jit(solution)/shard_map/pallas_call | solution.py:625
  41.4 1.4 %collective-permute-start.18 = (bf16[1,64,512]{2,1,0:T(8,128)(2,1)S(1)}, bf16[1,64,512]{2,1,0:T(8,128)(2,1)S(1)}, u32[]{:S(2)}, u32[]{:S(2)}) collective-permute-start(bf16[1,64,512]{2,1,0:T(8,128)(2,1)S(1)} %get-tuple-element.94), channel_id=1, source_target_pairs={{0,16},{8,24},{16,0},{24,8},{1,17},{9,25},{17,1},{25,9},{2,18},{10... | collective-permute-start | bytes 196616 | tf_op jit(solution)/shard_map/ppermute | solution.py:69
  42.8 3.0 %collective-permute-start.19 = (bf16[1,64,512]{2,1,0:T(8,128)(2,1)S(1)}, bf16[1,64,512]{2,1,0:T(8,128)(2,1)S(1)}, u32[]{:S(2)}, u32[]{:S(2)}) collective-permute-start(bf16[1,64,512]{2,1,0:T(8,128)(2,1)S(1)} %get-tuple-element.95), channel_id=1, source_target_pairs={{0,24},{8,16},{16,8},{24,0},{1,25},{9,17},{17,9},{25,1},{2,26},{10... | collective-permute-start | bytes 196616 | tf_op jit(solution)/shard_map/ppermute | solution.py:69
  46.3 0.9 %collective-permute-start.22 = (bf16[128,512]{1,0:T(8,128)(2,1)S(1)}, bf16[128,512]{1,0:T(8,128)(2,1)S(1)}, u32[]{:S(2)}, u32[]{:S(2)}) collective-permute-start(bf16[128,512]{1,0:T(8,128)(2,1)S(1)} %get-tuple-element.99), channel_id=1, source_target_pairs={{0,4},{2,6},{4,0},{6,2},{1,5},{3,7},{5,1},{7,3},{8,12},{10,14},{12... | collective-permute-start | bytes 393224 | tf_op jit(solution)/shard_map/ppermute | solution.py:69
  47.2 2.8 %collective-permute-done.17.near_ref.refs_1_ = bf16[3,64,512]{2,1,0:T(8,128)(2,1)S(1)} collective-permute-done((bf16[3,64,512]{2,1,0:T(8,128)(2,1)S(1)}, bf16[3,64,512]{2,1,0:T(8,128)(2,1)S(1)}, u32[]{:S(2)}, u32[]{:S(2)}) %collective-permute-start.17) | collective-permute-done | bytes 196640 | tf_op jit(solution)/shard_map/ppermute | solution.py:69
  50.0 1.4 %collective-permute-start.20 = (bf16[1,64,512]{2,1,0:T(8,128)(2,1)S(1)}, bf16[1,64,512]{2,1,0:T(8,128)(2,1)S(1)}, u32[]{:S(2)}, u32[]{:S(2)}) collective-permute-start(bf16[1,64,512]{2,1,0:T(8,128)(2,1)S(1)} %shard_map.148), channel_id=1, source_target_pairs={{0,16},{8,24},{16,0},{24,8},{1,17},{9,25},{17,1},{25,9},{2,18},{10... | collective-permute-start | bytes 196616 | tf_op jit(solution)/shard_map/ppermute | solution.py:662
  52.0 1.8 %collective-permute-done.22.refs_6_ = bf16[128,512]{1,0:T(8,128)(2,1)S(1)} collective-permute-done((bf16[128,512]{1,0:T(8,128)(2,1)S(1)}, bf16[128,512]{1,0:T(8,128)(2,1)S(1)}, u32[]{:S(2)}, u32[]{:S(2)}) %collective-permute-start.22) | collective-permute-done | bytes 131104 | tf_op jit(solution)/shard_map/ppermute | solution.py:69
  53.8 1.6 %collective-permute-done.20.refs_4_ = bf16[1,64,512]{2,1,0:T(8,128)(2,1)S(1)} collective-permute-done((bf16[1,64,512]{2,1,0:T(8,128)(2,1)S(1)}, bf16[1,64,512]{2,1,0:T(8,128)(2,1)S(1)}, u32[]{:S(2)}, u32[]{:S(2)}) %collective-permute-start.20) | collective-permute-done | bytes 65568 | tf_op jit(solution)/shard_map/ppermute | solution.py:662
  55.5 1.3 %shard_map.150 = (bf16[128,512]{1,0:T(8,128)(2,1)}, bf16[128,512]{1,0:T(8,128)(2,1)}, f32[64,512]{1,0:T(8,128)}, f32[64,512]{1,0:T(8,128)}) custom-call(bf16[128,256]{1,0:T(8,128)(2,1)S(1)} %get-tuple-element.89.placed_ref, f32[128,128]{1,0:T(8,128)S(1)} %get-tuple-element.90.factors_ref, f32[128,512]{1,0:T(8,128)S(1)} %get-tuple-element.91.router_cols_ref, ...), custom_call_target="tpu_custom_call" | custom-call | flops 1000000000 | tf_op jit(solution)/shard_map/pallas_call | solution.py:686
  (57 shorter events, 5.2 us)
Async XLA Ops:
  0.6 12.8 %collective-permute-start.4 = (bf16[128,512]{1,0:T(8,128)(2,1)}, bf16[128,512]{1,0:T(8,128)(2,1)S(1)}, u32[]{:S(2)}, u32[]{:S(2)}) collective-permute-start(bf16[128,512]{1,0:T(8,128)(2,1)} %bitcast.39), channel_id=1, source_target_pairs={{0,1},{1,0},{2,3},{3,2},{4,5},{5,4},{6,7},{7,6},{8,9},{9,8},{10,11... | collective-permute-start | bytes 393224 | tf_op jit(solution)/shard_map/ppermute | solution.py:69
  3.6 8.4 %collective-permute-start = (bf16[128,512]{1,0:T(8,128)(2,1)}, bf16[128,512]{1,0:T(8,128)(2,1)S(1)}, u32[]{:S(2)}, u32[]{:S(2)}) collective-permute-start(bf16[128,512]{1,0:T(8,128)(2,1)} %bitcast.33), channel_id=1, source_target_pairs={{0,8},{8,16},{16,24},{24,0},{1,9},{9,17},{17,25},{25,1},{2,10},{10... | collective-permute-start | bytes 393224 | tf_op jit(solution)/shard_map/ppermute | solution.py:533
  5.2 8.3 %collective-permute-start.2 = (bf16[128,512]{1,0:T(8,128)(2,1)}, bf16[128,512]{1,0:T(8,128)(2,1)S(1)}, u32[]{:S(2)}, u32[]{:S(2)}) collective-permute-start(bf16[128,512]{1,0:T(8,128)(2,1)} %bitcast.36), channel_id=1, source_target_pairs={{0,8},{8,16},{16,24},{24,0},{1,9},{9,17},{17,25},{25,1},{2,10},{10... | collective-permute-start | bytes 393224 | tf_op jit(solution)/shard_map/ppermute | solution.py:533
  7.5 0.9 %copy-start.3 = (bf16[1,128,512]{2,1,0:T(8,128)(2,1)S(1)}, bf16[1,128,512]{2,1,0:T(8,128)(2,1)}, u32[]{:S(2)}) copy-start(bf16[1,128,512]{2,1,0:T(8,128)(2,1)} %param.21) | copy-start | bytes 393220
  8.4 1.3 %copy-start.4 = (bf16[1,128,512]{2,1,0:T(8,128)(2,1)S(1)}, bf16[1,128,512]{2,1,0:T(8,128)(2,1)}, u32[]{:S(2)}) copy-start(bf16[1,128,512]{2,1,0:T(8,128)(2,1)} %param.12) | copy-start | bytes 393220
  8.4 1.3 %copy-start.5 = (bf16[1,128,512]{2,1,0:T(8,128)(2,1)S(1)}, bf16[1,128,512]{2,1,0:T(8,128)(2,1)}, u32[]{:S(2)}) copy-start(bf16[1,128,512]{2,1,0:T(8,128)(2,1)} %param.13) | copy-start | bytes 393220
  8.4 1.3 %copy-start.6 = (bf16[1,128,512]{2,1,0:T(8,128)(2,1)S(1)}, bf16[1,128,512]{2,1,0:T(8,128)(2,1)}, u32[]{:S(2)}) copy-start(bf16[1,128,512]{2,1,0:T(8,128)(2,1)} %param.11) | copy-start | bytes 393220
  9.0 12.5 %collective-permute-start.5 = (bf16[160,512]{1,0:T(8,128)(2,1)S(1)}, bf16[160,512]{1,0:T(8,128)(2,1)S(1)}, u32[]{:S(2)}, u32[]{:S(2)}) collective-permute-start(bf16[160,512]{1,0:T(8,128)(2,1)S(1)} %get-tuple-element.55.extended_ref.refs_0_), channel_id=1, source_target_pairs={{0,1},{1,0},{2,3},{3,2},{4,5},{5,4},{6,7},{7,6},{8,9},{9,8},{10,11... | collective-permute-start | bytes 491528 | tf_op jit(solution)/shard_map/ppermute | solution.py:69
  12.1 8.7 %collective-permute-start.1 = (bf16[128,512]{1,0:T(8,128)(2,1)S(1)}, bf16[128,512]{1,0:T(8,128)(2,1)S(1)}, u32[]{:S(2)}, u32[]{:S(2)}) collective-permute-start(bf16[128,512]{1,0:T(8,128)(2,1)S(1)} %collective-permute-done.refs_4_), channel_id=1, source_target_pairs={{0,8},{8,16},{16,24},{24,0},{1,9},{9,17},{17,25},{25,1},{2,10},{10... | collective-permute-start | bytes 393224 | tf_op jit(solution)/shard_map/ppermute | solution.py:533
  13.5 7.3 %collective-permute-start.3 = (bf16[128,512]{1,0:T(8,128)(2,1)S(1)}, bf16[128,512]{1,0:T(8,128)(2,1)S(1)}, u32[]{:S(2)}, u32[]{:S(2)}) collective-permute-start(bf16[128,512]{1,0:T(8,128)(2,1)S(1)} %collective-permute-done.2.refs_5_), channel_id=1, source_target_pairs={{0,8},{8,16},{16,24},{24,0},{1,9},{9,17},{17,25},{25,1},{2,10},{10... | collective-permute-start | bytes 393224 | tf_op jit(solution)/shard_map/ppermute | solution.py:533
  21.6 5.3 %collective-permute-start.6 = (bf16[592,128]{1,0:T(8,128)(2,1)S(1)}, bf16[592,128]{1,0:T(8,128)(2,1)S(1)}, u32[]{:S(2)}, u32[]{:S(2)}) collective-permute-start(bf16[592,128]{1,0:T(8,128)(2,1)S(1)} %shard_map.142), channel_id=1, source_target_pairs={{0,1},{1,0},{2,3},{3,2},{4,5},{5,4},{6,7},{7,6},{8,9},{9,8},{10,11... | collective-permute-start | bytes 454664 | tf_op jit(solution)/shard_map/ppermute | solution.py:69
  23.3 5.4 %collective-permute-start.10 = (bf16[128,512]{1,0:T(8,128)(2,1)S(1)}, bf16[128,512]{1,0:T(8,128)(2,1)S(1)}, u32[]{:S(2)}, u32[]{:S(2)}) collective-permute-start(bf16[128,512]{1,0:T(8,128)(2,1)S(1)} %get-tuple-element.80), channel_id=1, source_target_pairs={{0,2},{2,0},{4,6},{6,4},{1,3},{3,1},{5,7},{7,5},{8,10},{10,8},{12,... | collective-permute-start | bytes 393224 | tf_op jit(solution)/shard_map/ppermute | solution.py:69
  23.4 7.1 %collective-permute-start.11 = (bf16[128,512]{1,0:T(8,128)(2,1)S(1)}, bf16[128,512]{1,0:T(8,128)(2,1)S(1)}, u32[]{:S(2)}, u32[]{:S(2)}) collective-permute-start(bf16[128,512]{1,0:T(8,128)(2,1)S(1)} %get-tuple-element.81), channel_id=1, source_target_pairs={{0,4},{2,6},{4,0},{6,2},{1,5},{3,7},{5,1},{7,3},{8,12},{10,14},{12... | collective-permute-start | bytes 393224 | tf_op jit(solution)/shard_map/ppermute | solution.py:69
  25.0 7.0 %collective-permute-start.12 = (bf16[128,512]{1,0:T(8,128)(2,1)S(1)}, bf16[128,512]{1,0:T(8,128)(2,1)S(1)}, u32[]{:S(2)}, u32[]{:S(2)}) collective-permute-start(bf16[128,512]{1,0:T(8,128)(2,1)S(1)} %get-tuple-element.82), channel_id=1, source_target_pairs={{0,6},{2,4},{4,2},{6,0},{1,7},{3,5},{5,3},{7,1},{8,14},{10,12},{12... | collective-permute-start | bytes 393224 | tf_op jit(solution)/shard_map/ppermute | solution.py:69
  25.3 1.5 %copy-start = (bf16[512,512]{1,0:T(8,128)(2,1)S(1)}, bf16[512,512]{1,0:T(8,128)(2,1)}, u32[]{:S(2)}) copy-start(bf16[512,512]{1,0:T(8,128)(2,1)} %proj_ref.1) | copy-start | bytes 1572868
  25.3 1.5 %copy-start.7 = (bf16[1,128,512]{2,1,0:T(8,128)(2,1)S(1)}, bf16[1,128,512]{2,1,0:T(8,128)(2,1)}, u32[]{:S(2)}) copy-start(bf16[1,128,512]{2,1,0:T(8,128)(2,1)} %param.15) | copy-start | bytes 393220
  26.8 10.0 %copy-start.1 = (bf16[1,512,512]{2,1,0:T(8,128)(2,1)S(1)}, bf16[1,512,512]{2,1,0:T(8,128)(2,1)}, u32[]{:S(2)}) copy-start(bf16[1,512,512]{2,1,0:T(8,128)(2,1)} %param.19) | copy-start | bytes 1572868
  26.8 10.0 %copy-start.2 = (bf16[1,512,512]{2,1,0:T(8,128)(2,1)S(1)}, bf16[1,512,512]{2,1,0:T(8,128)(2,1)}, u32[]{:S(2)}) copy-start(bf16[1,512,512]{2,1,0:T(8,128)(2,1)} %param.20) | copy-start | bytes 1572868
  27.4 4.8 %collective-permute-start.13 = (bf16[64,512]{1,0:T(8,128)(2,1)S(1)}, bf16[64,512]{1,0:T(8,128)(2,1)S(1)}, u32[]{:S(2)}, u32[]{:S(2)}) collective-permute-start(bf16[64,512]{1,0:T(8,128)(2,1)S(1)} %get-tuple-element.74.refs_0_), channel_id=1, source_target_pairs={{0,1},{1,0},{2,3},{3,2},{4,5},{5,4},{6,7},{7,6},{8,9},{9,8},{10,11... | collective-permute-start | bytes 196616 | tf_op jit(solution)/shard_map/ppermute | solution.py:69
  28.7 5.1 %collective-permute-start.14 = (bf16[64,512]{1,0:T(8,128)(2,1)S(1)}, bf16[64,512]{1,0:T(8,128)(2,1)S(1)}, u32[]{:S(2)}, u32[]{:S(2)}) collective-permute-start(bf16[64,512]{1,0:T(8,128)(2,1)S(1)} %get-tuple-element.75), channel_id=1, source_target_pairs={{0,3},{1,2},{2,1},{3,0},{4,7},{5,6},{6,5},{7,4},{8,11},{9,10},{10,... | collective-permute-start | bytes 196616 | tf_op jit(solution)/shard_map/ppermute | solution.py:69
  28.7 7.1 %collective-permute-start.15 = (bf16[64,512]{1,0:T(8,128)(2,1)S(1)}, bf16[64,512]{1,0:T(8,128)(2,1)S(1)}, u32[]{:S(2)}, u32[]{:S(2)}) collective-permute-start(bf16[64,512]{1,0:T(8,128)(2,1)S(1)} %get-tuple-element.76), channel_id=1, source_target_pairs={{0,5},{1,4},{2,7},{3,6},{4,1},{5,0},{6,3},{7,2},{8,13},{9,12},{10,... | collective-permute-start | bytes 196616 | tf_op jit(solution)/shard_map/ppermute | solution.py:69
  30.5 6.3 %collective-permute-start.16 = (bf16[64,512]{1,0:T(8,128)(2,1)S(1)}, bf16[64,512]{1,0:T(8,128)(2,1)S(1)}, u32[]{:S(2)}, u32[]{:S(2)}) collective-permute-start(bf16[64,512]{1,0:T(8,128)(2,1)S(1)} %get-tuple-element.77), channel_id=1, source_target_pairs={{0,7},{1,6},{2,5},{3,4},{4,3},{5,2},{6,1},{7,0},{8,15},{9,14},{10,... | collective-permute-start | bytes 196616 | tf_op jit(solution)/shard_map/ppermute | solution.py:69
  32.0 6.5 %collective-permute-start.7 = (bf16[64,512]{1,0:T(8,128)(2,1)S(1)}, bf16[64,512]{1,0:T(8,128)(2,1)S(1)}, u32[]{:S(2)}, u32[]{:S(2)}) collective-permute-start(bf16[64,512]{1,0:T(8,128)(2,1)S(1)} %get-tuple-element.75), channel_id=1, source_target_pairs={{0,2},{1,3},{2,0},{3,1},{4,6},{5,7},{6,4},{7,5},{8,10},{9,11},{10,... | collective-permute-start | bytes 196616 | tf_op jit(solution)/shard_map/ppermute | solution.py:69
  32.3 6.2 %collective-permute-start.8 = (bf16[64,512]{1,0:T(8,128)(2,1)S(1)}, bf16[64,512]{1,0:T(8,128)(2,1)S(1)}, u32[]{:S(2)}, u32[]{:S(2)}) collective-permute-start(bf16[64,512]{1,0:T(8,128)(2,1)S(1)} %get-tuple-element.76), channel_id=1, source_target_pairs={{0,4},{1,5},{2,6},{3,7},{4,0},{5,1},{6,2},{7,3},{8,12},{9,13},{10,... | collective-permute-start | bytes 196616 | tf_op jit(solution)/shard_map/ppermute | solution.py:69
  33.8 5.9 %collective-permute-start.9 = (bf16[64,512]{1,0:T(8,128)(2,1)S(1)}, bf16[64,512]{1,0:T(8,128)(2,1)S(1)}, u32[]{:S(2)}, u32[]{:S(2)}) collective-permute-start(bf16[64,512]{1,0:T(8,128)(2,1)S(1)} %get-tuple-element.77), channel_id=1, source_target_pairs={{0,6},{1,7},{2,4},{3,5},{4,2},{5,3},{6,0},{7,1},{8,14},{9,15},{10,... | collective-permute-start | bytes 196616 | tf_op jit(solution)/shard_map/ppermute | solution.py:69
  41.3 8.7 %collective-permute-start.17 = (bf16[3,64,512]{2,1,0:T(8,128)(2,1)S(1)}, bf16[3,64,512]{2,1,0:T(8,128)(2,1)S(1)}, u32[]{:S(2)}, u32[]{:S(2)}) collective-permute-start(bf16[3,64,512]{2,1,0:T(8,128)(2,1)S(1)} %get-tuple-element.93), channel_id=1, source_target_pairs={{0,8},{8,0},{16,24},{24,16},{1,9},{9,1},{17,25},{25,17},{2,10},{10... | collective-permute-start | bytes 589832 | tf_op jit(solution)/shard_map/ppermute | solution.py:69
  41.4 8.6 %collective-permute-start.18 = (bf16[1,64,512]{2,1,0:T(8,128)(2,1)S(1)}, bf16[1,64,512]{2,1,0:T(8,128)(2,1)S(1)}, u32[]{:S(2)}, u32[]{:S(2)}) collective-permute-start(bf16[1,64,512]{2,1,0:T(8,128)(2,1)S(1)} %get-tuple-element.94), channel_id=1, source_target_pairs={{0,16},{8,24},{16,0},{24,8},{1,17},{9,25},{17,1},{25,9},{2,18},{10... | collective-permute-start | bytes 196616 | tf_op jit(solution)/shard_map/ppermute | solution.py:69
  42.8 9.1 %collective-permute-start.19 = (bf16[1,64,512]{2,1,0:T(8,128)(2,1)S(1)}, bf16[1,64,512]{2,1,0:T(8,128)(2,1)S(1)}, u32[]{:S(2)}, u32[]{:S(2)}) collective-permute-start(bf16[1,64,512]{2,1,0:T(8,128)(2,1)S(1)} %get-tuple-element.95), channel_id=1, source_target_pairs={{0,24},{8,16},{16,8},{24,0},{1,25},{9,17},{17,9},{25,1},{2,26},{10... | collective-permute-start | bytes 196616 | tf_op jit(solution)/shard_map/ppermute | solution.py:69
  46.2 5.8 %collective-permute-start.21 = (bf16[128,512]{1,0:T(8,128)(2,1)S(1)}, bf16[128,512]{1,0:T(8,128)(2,1)S(1)}, u32[]{:S(2)}, u32[]{:S(2)}) collective-permute-start(bf16[128,512]{1,0:T(8,128)(2,1)S(1)} %get-tuple-element.98), channel_id=1, source_target_pairs={{0,6},{2,4},{4,2},{6,0},{1,7},{3,5},{5,3},{7,1},{8,14},{10,12},{12... | collective-permute-start | bytes 393224 | tf_op jit(solution)/shard_map/ppermute | solution.py:69
  46.3 7.6 %collective-permute-start.22 = (bf16[128,512]{1,0:T(8,128)(2,1)S(1)}, bf16[128,512]{1,0:T(8,128)(2,1)S(1)}, u32[]{:S(2)}, u32[]{:S(2)}) collective-permute-start(bf16[128,512]{1,0:T(8,128)(2,1)S(1)} %get-tuple-element.99), channel_id=1, source_target_pairs={{0,4},{2,6},{4,0},{6,2},{1,5},{3,7},{5,1},{7,3},{8,12},{10,14},{12... | collective-permute-start | bytes 393224 | tf_op jit(solution)/shard_map/ppermute | solution.py:69
  50.0 3.9 %collective-permute-start.23 = (bf16[128,512]{1,0:T(8,128)(2,1)S(1)}, bf16[128,512]{1,0:T(8,128)(2,1)S(1)}, u32[]{:S(2)}, u32[]{:S(2)}) collective-permute-start(bf16[128,512]{1,0:T(8,128)(2,1)S(1)} %get-tuple-element.100), channel_id=1, source_target_pairs={{0,2},{2,0},{4,6},{6,4},{1,3},{3,1},{5,7},{7,5},{8,10},{10,8},{12,... | collective-permute-start | bytes 393224 | tf_op jit(solution)/shard_map/ppermute | solution.py:69
  50.0 5.5 %collective-permute-start.20 = (bf16[1,64,512]{2,1,0:T(8,128)(2,1)S(1)}, bf16[1,64,512]{2,1,0:T(8,128)(2,1)S(1)}, u32[]{:S(2)}, u32[]{:S(2)}) collective-permute-start(bf16[1,64,512]{2,1,0:T(8,128)(2,1)S(1)} %shard_map.148), channel_id=1, source_target_pairs={{0,16},{8,24},{16,0},{24,8},{1,17},{9,25},{17,1},{25,9},{2,18},{10... | collective-permute-start | bytes 196616 | tf_op jit(solution)/shard_map/ppermute | solution.py:662
  (3 other events, 2.0 us)

commit v18 on v16

--- a/solution.py
+++ b/solution.py
@@ -234,10 +234,10 @@
             fold(place, k, pair_ref, block, begin, False)
 
 
-def attend_kernel(plan, reps, counts, packed, ids_ref, begin_ref, *refs):
+def attend_kernel(plan, reps, counts, packed, ahead, ids_ref, begin_ref, *refs):
     ks = sorted({k for k, unused_pair, unused_first in plan})
     old_ks = [k for k in ks if not any(first for j, unused_pair, first in plan if j == k)]
-    query_refs, refs = dict(zip(ks, refs)), refs[len(ks) :]
+    query_refs, refs = dict(zip(ks, refs)), refs[len(ks) + ahead :]
     pair_refs = [refs[2 * place : 2 * place + 2] for place in range(counts)]
     refs = refs[2 * counts :]
     old_refs, refs = refs[: 3 * len(old_ks)], refs[3 * len(old_ks) :]
@@ -548,7 +548,7 @@
         jnp.stack(query_ranks).astype(jnp.int32), doc_lengths, choice, router.T, grad_out[0]
     )
 
-    def attend(plan, pairs, steps, queries, states, packed, cost):
+    def attend(plan, pairs, steps, queries, states, packed, cost, ahead=()):
         ks = sorted({k for k, unused_pair, unused_first in plan})
         old = [one for k in ks if k in states for one in states[k]]
         state_out = state_shapes * len(ks)
@@ -559,13 +559,13 @@
             out_shape, scratch = state_out, []
         outs = call(
             functools.partial(
-                attend_kernel, plan, rep_count, len(pairs), packed
+                attend_kernel, plan, rep_count, len(pairs), packed, len(ahead)
             ),
             out_shape,
-            [SMEM] + [VMEM] * (1 + len(ks) + 2 * len(pairs) + len(old)),
+            [SMEM] + [VMEM] * (1 + len(ks) + len(ahead) + 2 * len(pairs) + len(old)),
             scratch + [pltpu.VMEM((len(plan), tok, tok), jnp.float32)],
             cost=cost,
-        )(task_ids(plan, steps), begin, *[queries[k] for k in ks], *[one for both in pairs for one in both], *old)
+        )(task_ids(plan, steps), begin, *[queries[k] for k in ks], *ahead, *[one for both in pairs for one in both], *old)
         if packed:
             return dict(zip(ks, outs))
         return {k: list(outs[3 * place : 3 * place + 3]) for place, k in enumerate(ks)}
@@ -584,17 +584,24 @@
         (k, step, step == 0) for k in others for step in range(reach)
     )
     states = attend(middle, lines[:-1], list(range(reach)), queries, states, False, 4.0)
-    partial = attend(
-        tuple((k, 0, False) for k in others), lines[-1:], [reach], queries, states, True, 1.5
-    )
-    partial[1], *extendeds[1:] = lax.optimization_barrier((partial[1], *extendeds[1:]))
-    returned = reps.exchange([None] + [partial[k] for k in others], inverse=True)[1:]
-    states = attend(((0, 0, False),), lines[-1:], [reach], queries, states, False, 1.5)
+    states[1][0], *extendeds[1:] = lax.optimization_barrier((states[1][0], *extendeds[1:]))
     sent_grads = call(
         functools.partial(dispatch_kernel, rep_count, tok, hot_capacity),
         [shape((rep_count * hot_capacity, width))] * expert_count,
         [SMEM] + [VMEM] * rep_count,
     )(own, *extendeds)
+    partial = attend(
+        tuple((k, 0, False) for k in others),
+        lines[-1:],
+        [reach],
+        queries,
+        states,
+        True,
+        1.5,
+        ahead=sent_grads[:1],
+    )
+    returned = reps.exchange([None] + [partial[k] for k in others], inverse=True)[1:]
+    states = attend(((0, 0, False),), lines[-1:], [reach], queries, states, False, 1.5)
     got_grads = merged(experts.exchange(sent_grads), MOST_PERMUTES)
 
     mixed, *sent_rows = call(

time: 56 us -> 55.7 us (level)
  transfers between devices with their start and end apart: 23 -> 23, of which waited for: 9 -> 9; matrix products, arithmetic and copies ran while one was open for 1% -> 1% of each run, Pallas kernels for 17% -> 16%
where the time goes in v18:
time: 55.7 us; the launch traced here: 55.6 us
  starting transfers between devices  23.6 us (42%)
  waiting for transfers between devices  16.8 us (30%)
  Pallas kernels  12.3 us (22%)
  local copies, waits for them, and re-layouts  1.69 us (3%)
  between operations  0.88 us (2%)
    ppermute x19, starting transfers between devices, exchange(): got[k] = lax.ppermute(chunks[k], self.axes, pairs)  19.2 us
    ppermute x19, waiting for transfers between devices, exchange(): got[k] = lax.ppermute(chunks[k], self.axes, pairs)  11.4 us
    ppermute x4, waiting for transfers between devices, forward(): lax.ppermute(array, 'seq', [(i, (i + 1) % seq_count) for i in range(seq_c...  5.34 us
    pallas_call x4, Pallas kernels, attend(): call(functools.partial(attend_kernel, plan, rep_count, len(pairs), packed...  5.2 us
    ppermute x4, starting transfers between devices, forward(): lax.ppermute(array, 'seq', [(i, (i + 1) % seq_count) for i in range(seq_c...  4.37 us
    pallas_call x2, Pallas kernels, expert_call(): call(functools.partial(expert_kernel, rep_count, rep_list, expert_count,...  3.24 us
    unnamed x22, local copies, waits for them, and re-layouts  1.6 us
    pallas_call x1, Pallas kernels, local(): call(functools.partial(finish_kernel, hot_capacity, seq_count), [shape((t...  1.25 us
  transfers between devices with their start and end apart: 23, of which 9 were waited for; matrix products, arithmetic and copies ran while one was open for 1% of the time, Pallas kernels for 16%

profile of v18, /device:TPU:0, one launch (start us, length us, event | category | flops | bytes accessed | tf_op | source)
XLA Modules:
  0.0 55.6 jit_solution(15162562061936196333)
XLA Ops:
  0.6 3.0 %collective-permute-start.4 = (bf16[128,512]{1,0:T(8,128)(2,1)}, bf16[128,512]{1,0:T(8,128)(2,1)S(1)}, u32[]{:S(2)}, u32[]{:S(2)}) collective-permute-start(bf16[128,512]{1,0:T(8,128)(2,1)} %bitcast.39), channel_id=1, source_target_pairs={{0,1},{1,0},{2,3},{3,2},{4,5},{5,4},{6,7},{7,6},{8,9},{9,8},{10,11... | collective-permute-start | bytes 393224 | tf_op jit(solution)/shard_map/ppermute | solution.py:69
  3.6 1.6 %collective-permute-start = (bf16[128,512]{1,0:T(8,128)(2,1)}, bf16[128,512]{1,0:T(8,128)(2,1)S(1)}, u32[]{:S(2)}, u32[]{:S(2)}) collective-permute-start(bf16[128,512]{1,0:T(8,128)(2,1)} %bitcast.33), channel_id=1, source_target_pairs={{0,8},{8,16},{16,24},{24,0},{1,9},{9,17},{17,25},{25,1},{2,10},{10... | collective-permute-start | bytes 393224 | tf_op jit(solution)/shard_map/ppermute | solution.py:521
  5.2 1.6 %collective-permute-start.2 = (bf16[128,512]{1,0:T(8,128)(2,1)}, bf16[128,512]{1,0:T(8,128)(2,1)S(1)}, u32[]{:S(2)}, u32[]{:S(2)}) collective-permute-start(bf16[128,512]{1,0:T(8,128)(2,1)} %bitcast.36), channel_id=1, source_target_pairs={{0,8},{8,16},{16,24},{24,0},{1,9},{9,17},{17,25},{25,1},{2,10},{10... | collective-permute-start | bytes 393224 | tf_op jit(solution)/shard_map/ppermute | solution.py:521
  6.9 0.6 %copy-done.8 = bf16[512,4]{0,1:T(4,128)(2,1)S(1)} copy-done((bf16[512,4]{0,1:T(4,128)(2,1)S(1)}, bf16[512,4]{0,1:T(4,128)(2,1)}, u32[]{:S(2)}) %copy-start.8) | copy-done | bytes 4120
  7.5 0.9 %copy-done.3 = bf16[1,128,512]{2,1,0:T(8,128)(2,1)S(1)} copy-done((bf16[1,128,512]{2,1,0:T(8,128)(2,1)S(1)}, bf16[1,128,512]{2,1,0:T(8,128)(2,1)}, u32[]{:S(2)}) %copy-start.3) | copy-done | bytes 131096
  9.0 0.6 %collective-permute-start.5 = (bf16[160,512]{1,0:T(8,128)(2,1)S(1)}, bf16[160,512]{1,0:T(8,128)(2,1)S(1)}, u32[]{:S(2)}, u32[]{:S(2)}) collective-permute-start(bf16[160,512]{1,0:T(8,128)(2,1)S(1)} %get-tuple-element.55.refs_0_.extended_ref), channel_id=1, source_target_pairs={{0,1},{1,0},{2,3},{3,2},{4,5},{5,4},{6,7},{7,6},{8,9},{9,8},{10,11... | collective-permute-start | bytes 491528 | tf_op jit(solution)/shard_map/ppermute | solution.py:69
  9.7 1.8 %shard_map.139 = (f32[16,128]{1,0:T(8,128)S(1)}, f32[16,128]{1,0:T(8,128)S(1)}, f32[512,128]{1,0:T(8,128)S(1)}) custom-call(s32[3]{0:T(128)S(1)} %pad_add_fusion.4.ids_ref, s32[2,128]{1,0:T(2,128)S(1)} %get-tuple-element.56.begin_ref, bf16[128,512]{1,0:T(8,128)(2,1)S(1)} %bitcast.40, bf16[128,512]{1,0:T(8,128)(2,1)S(1)} %bitcast.34, ...), custom_call_target="tpu_custom_call" | custom-call | flops 2000000000 | tf_op jit(solution)/shard_map/pallas_call | solution.py:560
  12.1 1.2 %collective-permute-start.1 = (bf16[128,512]{1,0:T(8,128)(2,1)S(1)}, bf16[128,512]{1,0:T(8,128)(2,1)S(1)}, u32[]{:S(2)}, u32[]{:S(2)}) collective-permute-start(bf16[128,512]{1,0:T(8,128)(2,1)S(1)} %collective-permute-done.refs_4_), channel_id=1, source_target_pairs={{0,8},{8,16},{16,24},{24,0},{1,9},{9,17},{17,25},{25,1},{2,10},{10... | collective-permute-start | bytes 393224 | tf_op jit(solution)/shard_map/ppermute | solution.py:521
  13.5 1.9 %shard_map.140 = (f32[16,128]{1,0:T(8,128)S(1)}, f32[16,128]{1,0:T(8,128)S(1)}, f32[512,128]{1,0:T(8,128)S(1)}, f32[16,128]{1,0:T(8,128)S(1)}, f32[16,128]{1,0:T(8,128)S(1)}, /*index=5*/f32[512,128]{1,0:T(8,128)S(1)}) custom-call(s32[5]{0:T(128)S(1)} %stack.81.ids_ref, s32[2,128]{1,0:T(2,128)S(1)} %get-tuple-element.56.begin_ref, ...), custom_call_target="tpu_custom_call" | custom-call | flops 4000000000 | tf_op jit(solution)/shard_map/pallas_call | solution.py:560
  16.0 4.8 %collective-permute-done.3.refs_2_.refs_3_ = bf16[128,512]{1,0:T(8,128)(2,1)S(1)} collective-permute-done((bf16[128,512]{1,0:T(8,128)(2,1)S(1)}, bf16[128,512]{1,0:T(8,128)(2,1)S(1)}, u32[]{:S(2)}, u32[]{:S(2)}) %collective-permute-start.3) | collective-permute-done | bytes 131104 | tf_op jit(solution)/shard_map/ppermute | solution.py:521
  20.8 0.8 %shard_map.143 = bf16[592,128]{1,0:T(8,128)(2,1)S(1)} custom-call(s32[3]{0:T(128)S(1)} %pad_add_fusion.5.ids_ref, s32[2,128]{1,0:T(2,128)S(1)} %get-tuple-element.56.begin_ref, bf16[128,512]{1,0:T(8,128)(2,1)S(1)} %collective-permute-done.4.refs_1_.refs_0_, bf16[128,512]{1,0:T(8,128)(2,1)S(1)} %get-tuple-element.72.refs_1_.refs_4_, ...), custom_call_target="tpu_custom_call" | custom-call | flops 1500000000 | tf_op jit(solution)/shard_map/pallas_call | solution.py:560
  21.6 1.2 %collective-permute-start.6 = (bf16[592,128]{1,0:T(8,128)(2,1)S(1)}, bf16[592,128]{1,0:T(8,128)(2,1)S(1)}, u32[]{:S(2)}, u32[]{:S(2)}) collective-permute-start(bf16[592,128]{1,0:T(8,128)(2,1)S(1)} %shard_map.143), channel_id=1, source_target_pairs={{0,1},{1,0},{2,3},{3,2},{4,5},{5,4},{6,7},{7,6},{8,9},{9,8},{10,11... | collective-permute-start | bytes 454664 | tf_op jit(solution)/shard_map/ppermute | solution.py:69
  22.9 1.6 %collective-permute-start.11 = (bf16[128,512]{1,0:T(8,128)(2,1)S(1)}, bf16[128,512]{1,0:T(8,128)(2,1)S(1)}, u32[]{:S(2)}, u32[]{:S(2)}) collective-permute-start(bf16[128,512]{1,0:T(8,128)(2,1)S(1)} %get-tuple-element.81), channel_id=1, source_target_pairs={{0,4},{2,6},{4,0},{6,2},{1,5},{3,7},{5,1},{7,3},{8,12},{10,14},{12... | collective-permute-start | bytes 393224 | tf_op jit(solution)/shard_map/ppermute | solution.py:69
  24.7 0.7 %shard_map.141 = (f32[16,128]{1,0:T(8,128)S(1)}, f32[16,128]{1,0:T(8,128)S(1)}, f32[512,128]{1,0:T(8,128)S(1)}) custom-call(s32[3]{0:T(128)S(1)} %pad_add_fusion.2.ids_ref, s32[2,128]{1,0:T(2,128)S(1)} %get-tuple-element.56.begin_ref, bf16[128,512]{1,0:T(8,128)(2,1)S(1)} %bitcast.42, bf16[128,512]{1,0:T(8,128)(2,1)S(1)} %collective-permute-done.1.refs_1_.refs_2_, ...), custom_call_target="tpu_custom_call" | custom-call | flops 1500000000 | tf_op jit(solution)/shard_map/pallas_call | solution.py:560
  25.5 1.3 %collective-permute-done.6.refs_3_ = bf16[592,128]{1,0:T(8,128)(2,1)S(1)} collective-permute-done((bf16[592,128]{1,0:T(8,128)(2,1)S(1)}, bf16[592,128]{1,0:T(8,128)(2,1)S(1)}, u32[]{:S(2)}, u32[]{:S(2)}) %collective-permute-start.6) | collective-permute-done | bytes 151584 | tf_op jit(solution)/shard_map/ppermute | solution.py:69
  26.8 0.6 %shard_map.144 = (bf16[128,512]{1,0:T(8,128)(2,1)S(1)}, bf16[64,512]{1,0:T(8,128)(2,1)S(1)}, bf16[64,512]{1,0:T(8,128)(2,1)S(1)}, bf16[64,512]{1,0:T(8,128)(2,1)S(1)}, bf16[64,512]{1,0:T(8,128)(2,1)S(1)}) custom-call(s32[1]{0:T(128)} %bitcast.own_ref, bf16[160,512]{1,0:T(8,128)(2,1)S(1)} %get-tuple-element.55.refs_0_.extended_ref, ...), custom_call_target="tpu_custom_call" | custom-call | flops 2000000000 | tf_op jit(solution)/shard_map/pallas_call | solution.py:607
  27.4 1.2 %collective-permute-start.13 = (bf16[64,512]{1,0:T(8,128)(2,1)S(1)}, bf16[64,512]{1,0:T(8,128)(2,1)S(1)}, u32[]{:S(2)}, u32[]{:S(2)}) collective-permute-start(bf16[64,512]{1,0:T(8,128)(2,1)S(1)} %get-tuple-element.76.refs_0_), channel_id=1, source_target_pairs={{0,1},{1,0},{2,3},{3,2},{4,5},{5,4},{6,7},{7,6},{8,9},{9,8},{10,11... | collective-permute-start | bytes 196616 | tf_op jit(solution)/shard_map/ppermute | solution.py:69
  28.6 1.8 %collective-permute-start.15 = (bf16[64,512]{1,0:T(8,128)(2,1)S(1)}, bf16[64,512]{1,0:T(8,128)(2,1)S(1)}, u32[]{:S(2)}, u32[]{:S(2)}) collective-permute-start(bf16[64,512]{1,0:T(8,128)(2,1)S(1)} %get-tuple-element.78), channel_id=1, source_target_pairs={{0,5},{1,4},{2,7},{3,6},{4,1},{5,0},{6,3},{7,2},{8,13},{9,12},{10,... | collective-permute-start | bytes 196616 | tf_op jit(solution)/shard_map/ppermute | solution.py:69
  30.5 1.4 %collective-permute-start.16 = (bf16[64,512]{1,0:T(8,128)(2,1)S(1)}, bf16[64,512]{1,0:T(8,128)(2,1)S(1)}, u32[]{:S(2)}, u32[]{:S(2)}) collective-permute-start(bf16[64,512]{1,0:T(8,128)(2,1)S(1)} %get-tuple-element.79), channel_id=1, source_target_pairs={{0,7},{1,6},{2,5},{3,4},{4,3},{5,2},{6,1},{7,0},{8,15},{9,14},{10,... | collective-permute-start | bytes 196616 | tf_op jit(solution)/shard_map/ppermute | solution.py:69
  32.0 1.6 %collective-permute-start.8 = (bf16[64,512]{1,0:T(8,128)(2,1)S(1)}, bf16[64,512]{1,0:T(8,128)(2,1)S(1)}, u32[]{:S(2)}, u32[]{:S(2)}) collective-permute-start(bf16[64,512]{1,0:T(8,128)(2,1)S(1)} %get-tuple-element.78), channel_id=1, source_target_pairs={{0,4},{1,5},{2,6},{3,7},{4,0},{5,1},{6,2},{7,3},{8,12},{9,13},{10,... | collective-permute-start | bytes 196616 | tf_op jit(solution)/shard_map/ppermute | solution.py:69
  33.6 1.0 %collective-permute-start.9 = (bf16[64,512]{1,0:T(8,128)(2,1)S(1)}, bf16[64,512]{1,0:T(8,128)(2,1)S(1)}, u32[]{:S(2)}, u32[]{:S(2)}) collective-permute-start(bf16[64,512]{1,0:T(8,128)(2,1)S(1)} %get-tuple-element.79), channel_id=1, source_target_pairs={{0,6},{1,7},{2,4},{3,5},{4,2},{5,3},{6,0},{7,1},{8,14},{9,15},{10,... | collective-permute-start | bytes 196616 | tf_op jit(solution)/shard_map/ppermute | solution.py:69
  34.6 1.2 %collective-permute-done.15.refs_2_ = bf16[64,512]{1,0:T(8,128)(2,1)S(1)} collective-permute-done((bf16[64,512]{1,0:T(8,128)(2,1)S(1)}, bf16[64,512]{1,0:T(8,128)(2,1)S(1)}, u32[]{:S(2)}, u32[]{:S(2)}) %collective-permute-start.15) | collective-permute-done | bytes 65568 | tf_op jit(solution)/shard_map/ppermute | solution.py:69
  35.8 1.0 %collective-permute-done.16.refs_3_ = bf16[64,512]{1,0:T(8,128)(2,1)S(1)} collective-permute-done((bf16[64,512]{1,0:T(8,128)(2,1)S(1)}, bf16[64,512]{1,0:T(8,128)(2,1)S(1)}, u32[]{:S(2)}, u32[]{:S(2)}) %collective-permute-start.16) | collective-permute-done | bytes 65568 | tf_op jit(solution)/shard_map/ppermute | solution.py:69
  36.8 1.6 %shard_map.145 = (f32[256,512]{1,0:T(8,128)S(1)}, f32[256,512]{1,0:T(8,128)S(1)}) custom-call(s32[1]{0:T(128)} %bitcast.own_ref, s32[4]{0:T(128)S(1)} %pad_add_fusion.part_ref, bf16[512,512]{1,0:T(8,128)(2,1)S(1)} %bitcast.26, bf16[512,512]{1,0:T(8,128)(2,1)S(1)} %bitcast.29, bf16[160,512]{1,0:T(8,128)(2,1)S(1)} %get-tuple-element.55.refs_0_.extended_ref, ...), custom_call_target="tpu_custom_call" | custom-call | flops 2000000000 | tf_op jit(solution)/shard_map/pallas_call | solution.py:620
  38.5 1.2 %collective-permute-done.9.refs_3_ = bf16[64,512]{1,0:T(8,128)(2,1)S(1)} collective-permute-done((bf16[64,512]{1,0:T(8,128)(2,1)S(1)}, bf16[64,512]{1,0:T(8,128)(2,1)S(1)}, u32[]{:S(2)}, u32[]{:S(2)}) %collective-permute-start.9) | collective-permute-done | bytes 65568 | tf_op jit(solution)/shard_map/ppermute | solution.py:69
  39.7 1.6 %shard_map.146 = (bf16[256,512]{1,0:T(8,128)(2,1)S(1)}, bf16[256,512]{1,0:T(8,128)(2,1)S(1)}, bf16[2,64,512]{2,1,0:T(8,128)(2,1)S(1)}, bf16[2,64,512]{2,1,0:T(8,...) custom-call(s32[1]{0:T(128)} %bitcast.own_ref, s32[4]{0:T(128)S(1)} %pad_add_fusion.part_ref, ...), custom_call_target="tpu_custom_call" | custom-call | flops 2000000000 | tf_op jit(solution)/shard_map/pallas_call | solution.py:620
  41.5 0.8 %collective-permute-start.18 = (bf16[2,64,512]{2,1,0:T(8,128)(2,1)S(1)}, bf16[2,64,512]{2,1,0:T(8,128)(2,1)S(1)}, u32[]{:S(2)}, u32[]{:S(2)}) collective-permute-start(bf16[2,64,512]{2,1,0:T(8,128)(2,1)S(1)} %get-tuple-element.94), channel_id=1, source_target_pairs={{0,16},{8,24},{16,0},{24,8},{1,17},{9,25},{17,1},{25,9},{2,18},{10... | collective-permute-start | bytes 393224 | tf_op jit(solution)/shard_map/ppermute | solution.py:69
  42.3 3.5 %collective-permute-start.19 = (bf16[2,64,512]{2,1,0:T(8,128)(2,1)S(1)}, bf16[2,64,512]{2,1,0:T(8,128)(2,1)S(1)}, u32[]{:S(2)}, u32[]{:S(2)}) collective-permute-start(bf16[2,64,512]{2,1,0:T(8,128)(2,1)S(1)} %get-tuple-element.95), channel_id=1, source_target_pairs={{0,8},{8,0},{16,24},{24,16},{1,9},{9,1},{17,25},{25,17},{2,10},{10... | collective-permute-start | bytes 393224 | tf_op jit(solution)/shard_map/ppermute | solution.py:69
  46.3 0.9 %collective-permute-start.21 = (bf16[128,512]{1,0:T(8,128)(2,1)S(1)}, bf16[128,512]{1,0:T(8,128)(2,1)S(1)}, u32[]{:S(2)}, u32[]{:S(2)}) collective-permute-start(bf16[128,512]{1,0:T(8,128)(2,1)S(1)} %get-tuple-element.99), channel_id=1, source_target_pairs={{0,4},{2,6},{4,0},{6,2},{1,5},{3,7},{5,1},{7,3},{8,12},{10,14},{12... | collective-permute-start | bytes 393224 | tf_op jit(solution)/shard_map/ppermute | solution.py:69
  47.2 2.5 %collective-permute-done.17.refs_1_ = bf16[2,64,512]{2,1,0:T(8,128)(2,1)S(1)} collective-permute-done((bf16[2,64,512]{2,1,0:T(8,128)(2,1)S(1)}, bf16[2,64,512]{2,1,0:T(8,128)(2,1)S(1)}, u32[]{:S(2)}, u32[]{:S(2)}) %collective-permute-start.17) | collective-permute-done | bytes 131104 | tf_op jit(solution)/shard_map/ppermute | solution.py:69
  50.1 4.1 %collective-permute-done.18.refs_2_ = bf16[2,64,512]{2,1,0:T(8,128)(2,1)S(1)} collective-permute-done((bf16[2,64,512]{2,1,0:T(8,128)(2,1)S(1)}, bf16[2,64,512]{2,1,0:T(8,128)(2,1)S(1)}, u32[]{:S(2)}, u32[]{:S(2)}) %collective-permute-start.18) | collective-permute-done | bytes 131104 | tf_op jit(solution)/shard_map/ppermute | solution.py:69
  54.3 1.3 %shard_map.149 = (bf16[128,512]{1,0:T(8,128)(2,1)}, bf16[128,512]{1,0:T(8,128)(2,1)}, f32[64,512]{1,0:T(8,128)}, f32[64,512]{1,0:T(8,128)}) custom-call(bf16[128,256]{1,0:T(8,128)(2,1)S(1)} %get-tuple-element.89.placed_ref, f32[128,128]{1,0:T(8,128)S(1)} %get-tuple-element.90.factors_ref, f32[128,512]{1,0:T(8,128)S(1)} %get-tuple-element.91.router_cols_ref, ...), custom_call_target="tpu_custom_call" | custom-call | flops 1000000000 | tf_op jit(solution)/shard_map/pallas_call | solution.py:673
  (54 shorter events, 3.7 us)
Async XLA Ops:
  0.6 12.8 %collective-permute-start.4 = (bf16[128,512]{1,0:T(8,128)(2,1)}, bf16[128,512]{1,0:T(8,128)(2,1)S(1)}, u32[]{:S(2)}, u32[]{:S(2)}) collective-permute-start(bf16[128,512]{1,0:T(8,128)(2,1)} %bitcast.39), channel_id=1, source_target_pairs={{0,1},{1,0},{2,3},{3,2},{4,5},{5,4},{6,7},{7,6},{8,9},{9,8},{10,11... | collective-permute-start | bytes 393224 | tf_op jit(solution)/shard_map/ppermute | solution.py:69
  3.6 8.4 %collective-permute-start = (bf16[128,512]{1,0:T(8,128)(2,1)}, bf16[128,512]{1,0:T(8,128)(2,1)S(1)}, u32[]{:S(2)}, u32[]{:S(2)}) collective-permute-start(bf16[128,512]{1,0:T(8,128)(2,1)} %bitcast.33), channel_id=1, source_target_pairs={{0,8},{8,16},{16,24},{24,0},{1,9},{9,17},{17,25},{25,1},{2,10},{10... | collective-permute-start | bytes 393224 | tf_op jit(solution)/shard_map/ppermute | solution.py:521
  5.2 8.3 %collective-permute-start.2 = (bf16[128,512]{1,0:T(8,128)(2,1)}, bf16[128,512]{1,0:T(8,128)(2,1)S(1)}, u32[]{:S(2)}, u32[]{:S(2)}) collective-permute-start(bf16[128,512]{1,0:T(8,128)(2,1)} %bitcast.36), channel_id=1, source_target_pairs={{0,8},{8,16},{16,24},{24,0},{1,9},{9,17},{17,25},{25,1},{2,10},{10... | collective-permute-start | bytes 393224 | tf_op jit(solution)/shard_map/ppermute | solution.py:521
  6.8 0.7 %copy-start.8 = (bf16[512,4]{0,1:T(4,128)(2,1)S(1)}, bf16[512,4]{0,1:T(4,128)(2,1)}, u32[]{:S(2)}) copy-start(bf16[512,4]{0,1:T(4,128)(2,1)} %param.17) | copy-start | bytes 12292
  7.5 0.9 %copy-start.3 = (bf16[1,128,512]{2,1,0:T(8,128)(2,1)S(1)}, bf16[1,128,512]{2,1,0:T(8,128)(2,1)}, u32[]{:S(2)}) copy-start(bf16[1,128,512]{2,1,0:T(8,128)(2,1)} %param.21) | copy-start | bytes 393220
  8.4 1.3 %copy-start.4 = (bf16[1,128,512]{2,1,0:T(8,128)(2,1)S(1)}, bf16[1,128,512]{2,1,0:T(8,128)(2,1)}, u32[]{:S(2)}) copy-start(bf16[1,128,512]{2,1,0:T(8,128)(2,1)} %param.12) | copy-start | bytes 393220
  8.4 1.3 %copy-start.5 = (bf16[1,128,512]{2,1,0:T(8,128)(2,1)S(1)}, bf16[1,128,512]{2,1,0:T(8,128)(2,1)}, u32[]{:S(2)}) copy-start(bf16[1,128,512]{2,1,0:T(8,128)(2,1)} %param.13) | copy-start | bytes 393220
  8.4 1.3 %copy-start.6 = (bf16[1,128,512]{2,1,0:T(8,128)(2,1)S(1)}, bf16[1,128,512]{2,1,0:T(8,128)(2,1)}, u32[]{:S(2)}) copy-start(bf16[1,128,512]{2,1,0:T(8,128)(2,1)} %param.11) | copy-start | bytes 393220
  9.0 6.4 %collective-permute-start.5 = (bf16[160,512]{1,0:T(8,128)(2,1)S(1)}, bf16[160,512]{1,0:T(8,128)(2,1)S(1)}, u32[]{:S(2)}, u32[]{:S(2)}) collective-permute-start(bf16[160,512]{1,0:T(8,128)(2,1)S(1)} %get-tuple-element.55.refs_0_.extended_ref), channel_id=1, source_target_pairs={{0,1},{1,0},{2,3},{3,2},{4,5},{5,4},{6,7},{7,6},{8,9},{9,8},{10,11... | collective-permute-start | bytes 491528 | tf_op jit(solution)/shard_map/ppermute | solution.py:69
  12.1 8.7 %collective-permute-start.1 = (bf16[128,512]{1,0:T(8,128)(2,1)S(1)}, bf16[128,512]{1,0:T(8,128)(2,1)S(1)}, u32[]{:S(2)}, u32[]{:S(2)}) collective-permute-start(bf16[128,512]{1,0:T(8,128)(2,1)S(1)} %collective-permute-done.refs_4_), channel_id=1, source_target_pairs={{0,8},{8,16},{16,24},{24,0},{1,9},{9,17},{17,25},{25,1},{2,10},{10... | collective-permute-start | bytes 393224 | tf_op jit(solution)/shard_map/ppermute | solution.py:521
  13.5 7.3 %collective-permute-start.3 = (bf16[128,512]{1,0:T(8,128)(2,1)S(1)}, bf16[128,512]{1,0:T(8,128)(2,1)S(1)}, u32[]{:S(2)}, u32[]{:S(2)}) collective-permute-start(bf16[128,512]{1,0:T(8,128)(2,1)S(1)} %collective-permute-done.2.refs_5_), channel_id=1, source_target_pairs={{0,8},{8,16},{16,24},{24,0},{1,9},{9,17},{17,25},{25,1},{2,10},{10... | collective-permute-start | bytes 393224 | tf_op jit(solution)/shard_map/ppermute | solution.py:521
  21.6 5.3 %collective-permute-start.6 = (bf16[592,128]{1,0:T(8,128)(2,1)S(1)}, bf16[592,128]{1,0:T(8,128)(2,1)S(1)}, u32[]{:S(2)}, u32[]{:S(2)}) collective-permute-start(bf16[592,128]{1,0:T(8,128)(2,1)S(1)} %shard_map.143), channel_id=1, source_target_pairs={{0,1},{1,0},{2,3},{3,2},{4,5},{5,4},{6,7},{7,6},{8,9},{9,8},{10,11... | collective-permute-start | bytes 454664 | tf_op jit(solution)/shard_map/ppermute | solution.py:69
  22.8 5.8 %collective-permute-start.10 = (bf16[128,512]{1,0:T(8,128)(2,1)S(1)}, bf16[128,512]{1,0:T(8,128)(2,1)S(1)}, u32[]{:S(2)}, u32[]{:S(2)}) collective-permute-start(bf16[128,512]{1,0:T(8,128)(2,1)S(1)} %get-tuple-element.80), channel_id=1, source_target_pairs={{0,2},{2,0},{4,6},{6,4},{1,3},{3,1},{5,7},{7,5},{8,10},{10,8},{12,... | collective-permute-start | bytes 393224 | tf_op jit(solution)/shard_map/ppermute | solution.py:69
  22.9 7.6 %collective-permute-start.11 = (bf16[128,512]{1,0:T(8,128)(2,1)S(1)}, bf16[128,512]{1,0:T(8,128)(2,1)S(1)}, u32[]{:S(2)}, u32[]{:S(2)}) collective-permute-start(bf16[128,512]{1,0:T(8,128)(2,1)S(1)} %get-tuple-element.81), channel_id=1, source_target_pairs={{0,4},{2,6},{4,0},{6,2},{1,5},{3,7},{5,1},{7,3},{8,12},{10,14},{12... | collective-permute-start | bytes 393224 | tf_op jit(solution)/shard_map/ppermute | solution.py:69
  24.4 7.5 %collective-permute-start.12 = (bf16[128,512]{1,0:T(8,128)(2,1)S(1)}, bf16[128,512]{1,0:T(8,128)(2,1)S(1)}, u32[]{:S(2)}, u32[]{:S(2)}) collective-permute-start(bf16[128,512]{1,0:T(8,128)(2,1)S(1)} %get-tuple-element.82), channel_id=1, source_target_pairs={{0,6},{2,4},{4,2},{6,0},{1,7},{3,5},{5,3},{7,1},{8,14},{10,12},{12... | collective-permute-start | bytes 393224 | tf_op jit(solution)/shard_map/ppermute | solution.py:69
  24.7 2.1 %copy-start = (bf16[512,512]{1,0:T(8,128)(2,1)S(1)}, bf16[512,512]{1,0:T(8,128)(2,1)}, u32[]{:S(2)}) copy-start(bf16[512,512]{1,0:T(8,128)(2,1)} %proj_ref.1) | copy-start | bytes 1572868
  24.7 2.1 %copy-start.7 = (bf16[1,128,512]{2,1,0:T(8,128)(2,1)S(1)}, bf16[1,128,512]{2,1,0:T(8,128)(2,1)}, u32[]{:S(2)}) copy-start(bf16[1,128,512]{2,1,0:T(8,128)(2,1)} %param.15) | copy-start | bytes 393220
  26.8 10.0 %copy-start.1 = (bf16[1,512,512]{2,1,0:T(8,128)(2,1)S(1)}, bf16[1,512,512]{2,1,0:T(8,128)(2,1)}, u32[]{:S(2)}) copy-start(bf16[1,512,512]{2,1,0:T(8,128)(2,1)} %param.19) | copy-start | bytes 1572868
  26.8 10.0 %copy-start.2 = (bf16[1,512,512]{2,1,0:T(8,128)(2,1)S(1)}, bf16[1,512,512]{2,1,0:T(8,128)(2,1)}, u32[]{:S(2)}) copy-start(bf16[1,512,512]{2,1,0:T(8,128)(2,1)} %param.20) | copy-start | bytes 1572868
  27.4 4.6 %collective-permute-start.13 = (bf16[64,512]{1,0:T(8,128)(2,1)S(1)}, bf16[64,512]{1,0:T(8,128)(2,1)S(1)}, u32[]{:S(2)}, u32[]{:S(2)}) collective-permute-start(bf16[64,512]{1,0:T(8,128)(2,1)S(1)} %get-tuple-element.76.refs_0_), channel_id=1, source_target_pairs={{0,1},{1,0},{2,3},{3,2},{4,5},{5,4},{6,7},{7,6},{8,9},{9,8},{10,11... | collective-permute-start | bytes 196616 | tf_op jit(solution)/shard_map/ppermute | solution.py:69
  28.6 5.0 %collective-permute-start.14 = (bf16[64,512]{1,0:T(8,128)(2,1)S(1)}, bf16[64,512]{1,0:T(8,128)(2,1)S(1)}, u32[]{:S(2)}, u32[]{:S(2)}) collective-permute-start(bf16[64,512]{1,0:T(8,128)(2,1)S(1)} %get-tuple-element.77), channel_id=1, source_target_pairs={{0,3},{1,2},{2,1},{3,0},{4,7},{5,6},{6,5},{7,4},{8,11},{9,10},{10,... | collective-permute-start | bytes 196616 | tf_op jit(solution)/shard_map/ppermute | solution.py:69
  28.6 7.2 %collective-permute-start.15 = (bf16[64,512]{1,0:T(8,128)(2,1)S(1)}, bf16[64,512]{1,0:T(8,128)(2,1)S(1)}, u32[]{:S(2)}, u32[]{:S(2)}) collective-permute-start(bf16[64,512]{1,0:T(8,128)(2,1)S(1)} %get-tuple-element.78), channel_id=1, source_target_pairs={{0,5},{1,4},{2,7},{3,6},{4,1},{5,0},{6,3},{7,2},{8,13},{9,12},{10,... | collective-permute-start | bytes 196616 | tf_op jit(solution)/shard_map/ppermute | solution.py:69
  30.5 6.3 %collective-permute-start.16 = (bf16[64,512]{1,0:T(8,128)(2,1)S(1)}, bf16[64,512]{1,0:T(8,128)(2,1)S(1)}, u32[]{:S(2)}, u32[]{:S(2)}) collective-permute-start(bf16[64,512]{1,0:T(8,128)(2,1)S(1)} %get-tuple-element.79), channel_id=1, source_target_pairs={{0,7},{1,6},{2,5},{3,4},{4,3},{5,2},{6,1},{7,0},{8,15},{9,14},{10,... | collective-permute-start | bytes 196616 | tf_op jit(solution)/shard_map/ppermute | solution.py:69
  32.0 6.5 %collective-permute-start.7 = (bf16[64,512]{1,0:T(8,128)(2,1)S(1)}, bf16[64,512]{1,0:T(8,128)(2,1)S(1)}, u32[]{:S(2)}, u32[]{:S(2)}) collective-permute-start(bf16[64,512]{1,0:T(8,128)(2,1)S(1)} %get-tuple-element.77), channel_id=1, source_target_pairs={{0,2},{1,3},{2,0},{3,1},{4,6},{5,7},{6,4},{7,5},{8,10},{9,11},{10,... | collective-permute-start | bytes 196616 | tf_op jit(solution)/shard_map/ppermute | solution.py:69
  32.0 6.4 %collective-permute-start.8 = (bf16[64,512]{1,0:T(8,128)(2,1)S(1)}, bf16[64,512]{1,0:T(8,128)(2,1)S(1)}, u32[]{:S(2)}, u32[]{:S(2)}) collective-permute-start(bf16[64,512]{1,0:T(8,128)(2,1)S(1)} %get-tuple-element.78), channel_id=1, source_target_pairs={{0,4},{1,5},{2,6},{3,7},{4,0},{5,1},{6,2},{7,3},{8,12},{9,13},{10,... | collective-permute-start | bytes 196616 | tf_op jit(solution)/shard_map/ppermute | solution.py:69
  33.6 6.1 %collective-permute-start.9 = (bf16[64,512]{1,0:T(8,128)(2,1)S(1)}, bf16[64,512]{1,0:T(8,128)(2,1)S(1)}, u32[]{:S(2)}, u32[]{:S(2)}) collective-permute-start(bf16[64,512]{1,0:T(8,128)(2,1)S(1)} %get-tuple-element.79), channel_id=1, source_target_pairs={{0,6},{1,7},{2,4},{3,5},{4,2},{5,3},{6,0},{7,1},{8,14},{9,15},{10,... | collective-permute-start | bytes 196616 | tf_op jit(solution)/shard_map/ppermute | solution.py:69
  41.3 8.3 %collective-permute-start.17 = (bf16[2,64,512]{2,1,0:T(8,128)(2,1)S(1)}, bf16[2,64,512]{2,1,0:T(8,128)(2,1)S(1)}, u32[]{:S(2)}, u32[]{:S(2)}) collective-permute-start(bf16[2,64,512]{2,1,0:T(8,128)(2,1)S(1)} %get-tuple-element.93), channel_id=1, source_target_pairs={{0,24},{8,16},{16,8},{24,0},{1,25},{9,17},{17,9},{25,1},{2,26},{10... | collective-permute-start | bytes 393224 | tf_op jit(solution)/shard_map/ppermute | solution.py:69
  41.5 12.8 %collective-permute-start.18 = (bf16[2,64,512]{2,1,0:T(8,128)(2,1)S(1)}, bf16[2,64,512]{2,1,0:T(8,128)(2,1)S(1)}, u32[]{:S(2)}, u32[]{:S(2)}) collective-permute-start(bf16[2,64,512]{2,1,0:T(8,128)(2,1)S(1)} %get-tuple-element.94), channel_id=1, source_target_pairs={{0,16},{8,24},{16,0},{24,8},{1,17},{9,25},{17,1},{25,9},{2,18},{10... | collective-permute-start | bytes 393224 | tf_op jit(solution)/shard_map/ppermute | solution.py:69
  42.3 12.0 %collective-permute-start.19 = (bf16[2,64,512]{2,1,0:T(8,128)(2,1)S(1)}, bf16[2,64,512]{2,1,0:T(8,128)(2,1)S(1)}, u32[]{:S(2)}, u32[]{:S(2)}) collective-permute-start(bf16[2,64,512]{2,1,0:T(8,128)(2,1)S(1)} %get-tuple-element.95), channel_id=1, source_target_pairs={{0,8},{8,0},{16,24},{24,16},{1,9},{9,1},{17,25},{25,17},{2,10},{10... | collective-permute-start | bytes 393224 | tf_op jit(solution)/shard_map/ppermute | solution.py:69
  46.2 8.1 %collective-permute-start.20 = (bf16[128,512]{1,0:T(8,128)(2,1)S(1)}, bf16[128,512]{1,0:T(8,128)(2,1)S(1)}, u32[]{:S(2)}, u32[]{:S(2)}) collective-permute-start(bf16[128,512]{1,0:T(8,128)(2,1)S(1)} %get-tuple-element.98), channel_id=1, source_target_pairs={{0,6},{2,4},{4,2},{6,0},{1,7},{3,5},{5,3},{7,1},{8,14},{10,12},{12... | collective-permute-start | bytes 393224 | tf_op jit(solution)/shard_map/ppermute | solution.py:69
  46.3 8.0 %collective-permute-start.21 = (bf16[128,512]{1,0:T(8,128)(2,1)S(1)}, bf16[128,512]{1,0:T(8,128)(2,1)S(1)}, u32[]{:S(2)}, u32[]{:S(2)}) collective-permute-start(bf16[128,512]{1,0:T(8,128)(2,1)S(1)} %get-tuple-element.99), channel_id=1, source_target_pairs={{0,4},{2,6},{4,0},{6,2},{1,5},{3,7},{5,1},{7,3},{8,12},{10,14},{12... | collective-permute-start | bytes 393224 | tf_op jit(solution)/shard_map/ppermute | solution.py:69
  49.7 4.6 %collective-permute-start.22 = (bf16[128,512]{1,0:T(8,128)(2,1)S(1)}, bf16[128,512]{1,0:T(8,128)(2,1)S(1)}, u32[]{:S(2)}, u32[]{:S(2)}) collective-permute-start(bf16[128,512]{1,0:T(8,128)(2,1)S(1)} %get-tuple-element.100), channel_id=1, source_target_pairs={{0,2},{2,0},{4,6},{6,4},{1,3},{3,1},{5,7},{7,5},{8,10},{10,8},{12,... | collective-permute-start | bytes 393224 | tf_op jit(solution)/shard_map/ppermute | solution.py:69
  (2 other events, 1.3 us)

commit v19 on v18

--- a/solution.py
+++ b/solution.py
@@ -318,7 +318,7 @@
     *refs,
 ):
     row_count, grad_count = counts
-    row_refs, refs = refs[:row_count], refs[row_count:]
+    row_refs, refs = refs[:row_count][::-1], refs[row_count:]
     per_rep = row_count // len(rep_list)
     grad_refs, refs = refs[:grad_count], refs[grad_count:]
     own_rows = rep_list[0] == 0
@@ -631,7 +631,7 @@
             [SMEM, SMEM] + [VMEM] * (3 + len(rows) + len(got_grads) + len(extra)),
             [pltpu.VMEM((2 * len(rep_list), width, expert_count * hot_capacity), jnp.bfloat16)],
             cost=2.0,
-        )(own, part_to, weight_in[0], weight_out[0], extendeds[0], *rows, *got_grads, *extra)
+        )(own, part_to, weight_in[0], weight_out[0], extendeds[0], *rows[::-1], *got_grads, *extra)
 
     slots = expert_count * hot_capacity
     sums = expert_call(

time: 55.7 us -> 56.2 us (level)
  transfers between devices with their start and end apart: 23 -> 23, of which waited for: 9 -> 11; matrix products, arithmetic and copies ran while one was open for 1% -> 1% of each run, Pallas kernels for 16% -> 15%
where the time goes in v19:
time: 56.2 us; the launch traced here: 56 us
  starting transfers between devices  24.1 us (43%)
  waiting for transfers between devices  16.7 us (30%)
  Pallas kernels  12.3 us (22%)
  local copies, waits for them, and re-layouts  1.69 us (3%)
  between operations  0.84 us (1%)
    ppermute x19, starting transfers between devices, exchange(): got[k] = lax.ppermute(chunks[k], self.axes, pairs)  19.7 us
    ppermute x19, waiting for transfers between devices, exchange(): got[k] = lax.ppermute(chunks[k], self.axes, pairs)  11.3 us
    ppermute x4, waiting for transfers between devices, forward(): lax.ppermute(array, 'seq', [(i, (i + 1) % seq_count) for i in range(seq_c...  5.34 us
    pallas_call x4, Pallas kernels, attend(): call(functools.partial(attend_kernel, plan, rep_count, len(pairs), packed...  5.2 us
    ppermute x4, starting transfers between devices, forward(): lax.ppermute(array, 'seq', [(i, (i + 1) % seq_count) for i in range(seq_c...  4.37 us
    pallas_call x2, Pallas kernels, expert_call(): call(functools.partial(expert_kernel, rep_count, rep_list, expert_count,...  3.24 us
    unnamed x22, local copies, waits for them, and re-layouts  1.6 us
    pallas_call x1, Pallas kernels, local(): call(functools.partial(finish_kernel, hot_capacity, seq_count), [shape((t...  1.25 us
  transfers between devices with their start and end apart: 23, of which 11 were waited for; matrix products, arithmetic and copies ran while one was open for 1% of the time, Pallas kernels for 15%

profile of v19, /device:TPU:0, one launch (start us, length us, event | category | flops | bytes accessed | tf_op | source)
XLA Modules:
  0.0 56.0 jit_solution(17779558378511683084)
XLA Ops:
  0.6 3.0 %collective-permute-start.4 = (bf16[128,512]{1,0:T(8,128)(2,1)}, bf16[128,512]{1,0:T(8,128)(2,1)S(1)}, u32[]{:S(2)}, u32[]{:S(2)}) collective-permute-start(bf16[128,512]{1,0:T(8,128)(2,1)} %bitcast.39), channel_id=1, source_target_pairs={{0,1},{1,0},{2,3},{3,2},{4,5},{5,4},{6,7},{7,6},{8,9},{9,8},{10,11... | collective-permute-start | bytes 393224 | tf_op jit(solution)/shard_map/ppermute | solution.py:69
  3.6 1.6 %collective-permute-start = (bf16[128,512]{1,0:T(8,128)(2,1)}, bf16[128,512]{1,0:T(8,128)(2,1)S(1)}, u32[]{:S(2)}, u32[]{:S(2)}) collective-permute-start(bf16[128,512]{1,0:T(8,128)(2,1)} %bitcast.33), channel_id=1, source_target_pairs={{0,8},{8,16},{16,24},{24,0},{1,9},{9,17},{17,25},{25,1},{2,10},{10... | collective-permute-start | bytes 393224 | tf_op jit(solution)/shard_map/ppermute | solution.py:521
  5.2 1.6 %collective-permute-start.2 = (bf16[128,512]{1,0:T(8,128)(2,1)}, bf16[128,512]{1,0:T(8,128)(2,1)S(1)}, u32[]{:S(2)}, u32[]{:S(2)}) collective-permute-start(bf16[128,512]{1,0:T(8,128)(2,1)} %bitcast.36), channel_id=1, source_target_pairs={{0,8},{8,16},{16,24},{24,0},{1,9},{9,17},{17,25},{25,1},{2,10},{10... | collective-permute-start | bytes 393224 | tf_op jit(solution)/shard_map/ppermute | solution.py:521
  6.9 0.6 %copy-done.8 = bf16[512,4]{0,1:T(4,128)(2,1)S(1)} copy-done((bf16[512,4]{0,1:T(4,128)(2,1)S(1)}, bf16[512,4]{0,1:T(4,128)(2,1)}, u32[]{:S(2)}) %copy-start.8) | copy-done | bytes 4120
  7.5 0.9 %copy-done.3 = bf16[1,128,512]{2,1,0:T(8,128)(2,1)S(1)} copy-done((bf16[1,128,512]{2,1,0:T(8,128)(2,1)S(1)}, bf16[1,128,512]{2,1,0:T(8,128)(2,1)}, u32[]{:S(2)}) %copy-start.3) | copy-done | bytes 131096
  9.7 1.8 %shard_map.139 = (f32[16,128]{1,0:T(8,128)S(1)}, f32[16,128]{1,0:T(8,128)S(1)}, f32[512,128]{1,0:T(8,128)S(1)}) custom-call(s32[3]{0:T(128)S(1)} %pad_add_fusion.4.ids_ref, s32[2,128]{1,0:T(2,128)S(1)} %get-tuple-element.56.begin_ref, bf16[128,512]{1,0:T(8,128)(2,1)S(1)} %bitcast.40, bf16[128,512]{1,0:T(8,128)(2,1)S(1)} %bitcast.34, ...), custom_call_target="tpu_custom_call" | custom-call | flops 2000000000 | tf_op jit(solution)/shard_map/pallas_call | solution.py:560
  12.1 1.2 %collective-permute-start.1 = (bf16[128,512]{1,0:T(8,128)(2,1)S(1)}, bf16[128,512]{1,0:T(8,128)(2,1)S(1)}, u32[]{:S(2)}, u32[]{:S(2)}) collective-permute-start(bf16[128,512]{1,0:T(8,128)(2,1)S(1)} %collective-permute-done.refs_4_), channel_id=1, source_target_pairs={{0,8},{8,16},{16,24},{24,0},{1,9},{9,17},{17,25},{25,1},{2,10},{10... | collective-permute-start | bytes 393224 | tf_op jit(solution)/shard_map/ppermute | solution.py:521
  13.5 1.9 %shard_map.140 = (f32[16,128]{1,0:T(8,128)S(1)}, f32[16,128]{1,0:T(8,128)S(1)}, f32[512,128]{1,0:T(8,128)S(1)}, f32[16,128]{1,0:T(8,128)S(1)}, f32[16,128]{1,0:T(8,128)S(1)}, /*index=5*/f32[512,128]{1,0:T(8,128)S(1)}) custom-call(s32[5]{0:T(128)S(1)} %stack.81.ids_ref, s32[2,128]{1,0:T(2,128)S(1)} %get-tuple-element.56.begin_ref, ...), custom_call_target="tpu_custom_call" | custom-call | flops 4000000000 | tf_op jit(solution)/shard_map/pallas_call | solution.py:560
  16.0 4.8 %collective-permute-done.3.refs_2_.refs_3_ = bf16[128,512]{1,0:T(8,128)(2,1)S(1)} collective-permute-done((bf16[128,512]{1,0:T(8,128)(2,1)S(1)}, bf16[128,512]{1,0:T(8,128)(2,1)S(1)}, u32[]{:S(2)}, u32[]{:S(2)}) %collective-permute-start.3) | collective-permute-done | bytes 131104 | tf_op jit(solution)/shard_map/ppermute | solution.py:521
  20.8 0.8 %shard_map.143 = bf16[592,128]{1,0:T(8,128)(2,1)S(1)} custom-call(s32[3]{0:T(128)S(1)} %pad_add_fusion.5.ids_ref, s32[2,128]{1,0:T(2,128)S(1)} %get-tuple-element.56.begin_ref, bf16[128,512]{1,0:T(8,128)(2,1)S(1)} %collective-permute-done.4.refs_1_.refs_0_, bf16[128,512]{1,0:T(8,128)(2,1)S(1)} %get-tuple-element.72.refs_1_.refs_4_, ...), custom_call_target="tpu_custom_call" | custom-call | flops 1500000000 | tf_op jit(solution)/shard_map/pallas_call | solution.py:560
  21.6 1.2 %collective-permute-start.6 = (bf16[592,128]{1,0:T(8,128)(2,1)S(1)}, bf16[592,128]{1,0:T(8,128)(2,1)S(1)}, u32[]{:S(2)}, u32[]{:S(2)}) collective-permute-start(bf16[592,128]{1,0:T(8,128)(2,1)S(1)} %shard_map.143), channel_id=1, source_target_pairs={{0,1},{1,0},{2,3},{3,2},{4,5},{5,4},{6,7},{7,6},{8,9},{9,8},{10,11... | collective-permute-start | bytes 454664 | tf_op jit(solution)/shard_map/ppermute | solution.py:69
  22.9 1.6 %collective-permute-start.11 = (bf16[128,512]{1,0:T(8,128)(2,1)S(1)}, bf16[128,512]{1,0:T(8,128)(2,1)S(1)}, u32[]{:S(2)}, u32[]{:S(2)}) collective-permute-start(bf16[128,512]{1,0:T(8,128)(2,1)S(1)} %get-tuple-element.81), channel_id=1, source_target_pairs={{0,4},{2,6},{4,0},{6,2},{1,5},{3,7},{5,1},{7,3},{8,12},{10,14},{12... | collective-permute-start | bytes 393224 | tf_op jit(solution)/shard_map/ppermute | solution.py:69
  24.7 0.7 %shard_map.141 = (f32[16,128]{1,0:T(8,128)S(1)}, f32[16,128]{1,0:T(8,128)S(1)}, f32[512,128]{1,0:T(8,128)S(1)}) custom-call(s32[3]{0:T(128)S(1)} %pad_add_fusion.2.ids_ref, s32[2,128]{1,0:T(2,128)S(1)} %get-tuple-element.56.begin_ref, bf16[128,512]{1,0:T(8,128)(2,1)S(1)} %bitcast.42, bf16[128,512]{1,0:T(8,128)(2,1)S(1)} %collective-permute-done.1.refs_1_.refs_2_, ...), custom_call_target="tpu_custom_call" | custom-call | flops 1500000000 | tf_op jit(solution)/shard_map/pallas_call | solution.py:560
  25.5 1.3 %collective-permute-done.6.refs_3_ = bf16[592,128]{1,0:T(8,128)(2,1)S(1)} collective-permute-done((bf16[592,128]{1,0:T(8,128)(2,1)S(1)}, bf16[592,128]{1,0:T(8,128)(2,1)S(1)}, u32[]{:S(2)}, u32[]{:S(2)}) %collective-permute-start.6) | collective-permute-done | bytes 151584 | tf_op jit(solution)/shard_map/ppermute | solution.py:69
  26.8 0.6 %shard_map.144 = (bf16[128,512]{1,0:T(8,128)(2,1)S(1)}, bf16[64,512]{1,0:T(8,128)(2,1)S(1)}, bf16[64,512]{1,0:T(8,128)(2,1)S(1)}, bf16[64,512]{1,0:T(8,128)(2,1)S(1)}, bf16[64,512]{1,0:T(8,128)(2,1)S(1)}) custom-call(s32[1]{0:T(128)} %bitcast.own_ref, bf16[160,512]{1,0:T(8,128)(2,1)S(1)} %get-tuple-element.55.refs_0_.extended_ref, ...), custom_call_target="tpu_custom_call" | custom-call | flops 2000000000 | tf_op jit(solution)/shard_map/pallas_call | solution.py:607
  27.4 0.8 %collective-permute-start.13 = (bf16[64,512]{1,0:T(8,128)(2,1)S(1)}, bf16[64,512]{1,0:T(8,128)(2,1)S(1)}, u32[]{:S(2)}, u32[]{:S(2)}) collective-permute-start(bf16[64,512]{1,0:T(8,128)(2,1)S(1)} %get-tuple-element.76), channel_id=1, source_target_pairs={{0,7},{1,6},{2,5},{3,4},{4,3},{5,2},{6,1},{7,0},{8,15},{9,14},{10,... | collective-permute-start | bytes 196616 | tf_op jit(solution)/shard_map/ppermute | solution.py:69
  28.3 1.4 %collective-permute-start.14 = (bf16[64,512]{1,0:T(8,128)(2,1)S(1)}, bf16[64,512]{1,0:T(8,128)(2,1)S(1)}, u32[]{:S(2)}, u32[]{:S(2)}) collective-permute-start(bf16[64,512]{1,0:T(8,128)(2,1)S(1)} %get-tuple-element.77), channel_id=1, source_target_pairs={{0,5},{1,4},{2,7},{3,6},{4,1},{5,0},{6,3},{7,2},{8,13},{9,12},{10,... | collective-permute-start | bytes 196616 | tf_op jit(solution)/shard_map/ppermute | solution.py:69
  29.7 1.3 %collective-permute-start.15 = (bf16[64,512]{1,0:T(8,128)(2,1)S(1)}, bf16[64,512]{1,0:T(8,128)(2,1)S(1)}, u32[]{:S(2)}, u32[]{:S(2)}) collective-permute-start(bf16[64,512]{1,0:T(8,128)(2,1)S(1)} %get-tuple-element.78), channel_id=1, source_target_pairs={{0,3},{1,2},{2,1},{3,0},{4,7},{5,6},{6,5},{7,4},{8,11},{9,10},{10,... | collective-permute-start | bytes 196616 | tf_op jit(solution)/shard_map/ppermute | solution.py:69
  31.0 0.9 %collective-permute-start.16 = (bf16[64,512]{1,0:T(8,128)(2,1)S(1)}, bf16[64,512]{1,0:T(8,128)(2,1)S(1)}, u32[]{:S(2)}, u32[]{:S(2)}) collective-permute-start(bf16[64,512]{1,0:T(8,128)(2,1)S(1)} %get-tuple-element.79.refs_3_), channel_id=1, source_target_pairs={{0,1},{1,0},{2,3},{3,2},{4,5},{5,4},{6,7},{7,6},{8,9},{9,8},{10,11... | collective-permute-start | bytes 196616 | tf_op jit(solution)/shard_map/ppermute | solution.py:69
  32.0 1.5 %collective-permute-done.12.refs_7_ = bf16[128,512]{1,0:T(8,128)(2,1)S(1)} collective-permute-done((bf16[128,512]{1,0:T(8,128)(2,1)S(1)}, bf16[128,512]{1,0:T(8,128)(2,1)S(1)}, u32[]{:S(2)}, u32[]{:S(2)}) %collective-permute-start.12) | collective-permute-done | bytes 131104 | tf_op jit(solution)/shard_map/ppermute | solution.py:69
  33.5 2.1 %collective-permute-start.7 = (bf16[64,512]{1,0:T(8,128)(2,1)S(1)}, bf16[64,512]{1,0:T(8,128)(2,1)S(1)}, u32[]{:S(2)}, u32[]{:S(2)}) collective-permute-start(bf16[64,512]{1,0:T(8,128)(2,1)S(1)} %get-tuple-element.76), channel_id=1, source_target_pairs={{0,6},{1,7},{2,4},{3,5},{4,2},{5,3},{6,0},{7,1},{8,14},{9,15},{10,... | collective-permute-start | bytes 196616 | tf_op jit(solution)/shard_map/ppermute | solution.py:69
  36.3 1.6 %shard_map.145 = (f32[256,512]{1,0:T(8,128)S(1)}, f32[256,512]{1,0:T(8,128)S(1)}) custom-call(s32[1]{0:T(128)} %bitcast.own_ref, s32[4]{0:T(128)S(1)} %pad_add_fusion.part_ref, bf16[512,512]{1,0:T(8,128)(2,1)S(1)} %bitcast.26, bf16[512,512]{1,0:T(8,128)(2,1)S(1)} %bitcast.29, bf16[160,512]{1,0:T(8,128)(2,1)S(1)} %get-tuple-element.55.refs_0_.extended_ref, ...), custom_call_target="tpu_custom_call" | custom-call | flops 2000000000 | tf_op jit(solution)/shard_map/pallas_call | solution.py:620
  37.9 1.9 %collective-permute-done.8.refs_1_ = bf16[64,512]{1,0:T(8,128)(2,1)S(1)} collective-permute-done((bf16[64,512]{1,0:T(8,128)(2,1)S(1)}, bf16[64,512]{1,0:T(8,128)(2,1)S(1)}, u32[]{:S(2)}, u32[]{:S(2)}) %collective-permute-start.8) | collective-permute-done | bytes 65568 | tf_op jit(solution)/shard_map/ppermute | solution.py:69
  39.8 1.6 %shard_map.146 = (bf16[256,512]{1,0:T(8,128)(2,1)S(1)}, bf16[256,512]{1,0:T(8,128)(2,1)S(1)}, bf16[2,64,512]{2,1,0:T(8,128)(2,1)S(1)}, bf16[2,64,512]{2,1,0:T(8,...) custom-call(s32[1]{0:T(128)} %bitcast.own_ref, s32[4]{0:T(128)S(1)} %pad_add_fusion.part_ref, ...), custom_call_target="tpu_custom_call" | custom-call | flops 2000000000 | tf_op jit(solution)/shard_map/pallas_call | solution.py:620
  41.4 0.6 %collective-permute-start.17 = (bf16[2,64,512]{2,1,0:T(8,128)(2,1)S(1)}, bf16[2,64,512]{2,1,0:T(8,128)(2,1)S(1)}, u32[]{:S(2)}, u32[]{:S(2)}) collective-permute-start(bf16[2,64,512]{2,1,0:T(8,128)(2,1)S(1)} %get-tuple-element.93), channel_id=1, source_target_pairs={{0,24},{8,16},{16,8},{24,0},{1,25},{9,17},{17,9},{25,1},{2,26},{10... | collective-permute-start | bytes 393224 | tf_op jit(solution)/shard_map/ppermute | solution.py:69
  42.1 0.7 %collective-permute-start.18 = (bf16[2,64,512]{2,1,0:T(8,128)(2,1)S(1)}, bf16[2,64,512]{2,1,0:T(8,128)(2,1)S(1)}, u32[]{:S(2)}, u32[]{:S(2)}) collective-permute-start(bf16[2,64,512]{2,1,0:T(8,128)(2,1)S(1)} %get-tuple-element.94), channel_id=1, source_target_pairs={{0,16},{8,24},{16,0},{24,8},{1,17},{9,25},{17,1},{25,9},{2,18},{10... | collective-permute-start | bytes 393224 | tf_op jit(solution)/shard_map/ppermute | solution.py:69
  42.7 3.2 %collective-permute-start.19 = (bf16[2,64,512]{2,1,0:T(8,128)(2,1)S(1)}, bf16[2,64,512]{2,1,0:T(8,128)(2,1)S(1)}, u32[]{:S(2)}, u32[]{:S(2)}) collective-permute-start(bf16[2,64,512]{2,1,0:T(8,128)(2,1)S(1)} %get-tuple-element.95), channel_id=1, source_target_pairs={{0,8},{8,0},{16,24},{24,16},{1,9},{9,1},{17,25},{25,17},{2,10},{10... | collective-permute-start | bytes 393224 | tf_op jit(solution)/shard_map/ppermute | solution.py:69
  46.4 1.4 %collective-permute-start.21 = (bf16[128,512]{1,0:T(8,128)(2,1)S(1)}, bf16[128,512]{1,0:T(8,128)(2,1)S(1)}, u32[]{:S(2)}, u32[]{:S(2)}) collective-permute-start(bf16[128,512]{1,0:T(8,128)(2,1)S(1)} %get-tuple-element.99), channel_id=1, source_target_pairs={{0,4},{2,6},{4,0},{6,2},{1,5},{3,7},{5,1},{7,3},{8,12},{10,14},{12... | collective-permute-start | bytes 393224 | tf_op jit(solution)/shard_map/ppermute | solution.py:69
  47.8 2.0 %collective-permute-done.17.refs_1_ = bf16[2,64,512]{2,1,0:T(8,128)(2,1)S(1)} collective-permute-done((bf16[2,64,512]{2,1,0:T(8,128)(2,1)S(1)}, bf16[2,64,512]{2,1,0:T(8,128)(2,1)S(1)}, u32[]{:S(2)}, u32[]{:S(2)}) %collective-permute-start.17) | collective-permute-done | bytes 131104 | tf_op jit(solution)/shard_map/ppermute | solution.py:69
  50.2 3.9 %collective-permute-done.18.refs_2_ = bf16[2,64,512]{2,1,0:T(8,128)(2,1)S(1)} collective-permute-done((bf16[2,64,512]{2,1,0:T(8,128)(2,1)S(1)}, bf16[2,64,512]{2,1,0:T(8,128)(2,1)S(1)}, u32[]{:S(2)}, u32[]{:S(2)}) %collective-permute-start.18) | collective-permute-done | bytes 131104 | tf_op jit(solution)/shard_map/ppermute | solution.py:69
  54.1 0.6 %collective-permute-done.21.refs_5_ = bf16[128,512]{1,0:T(8,128)(2,1)S(1)} collective-permute-done((bf16[128,512]{1,0:T(8,128)(2,1)S(1)}, bf16[128,512]{1,0:T(8,128)(2,1)S(1)}, u32[]{:S(2)}, u32[]{:S(2)}) %collective-permute-start.21) | collective-permute-done | bytes 131104 | tf_op jit(solution)/shard_map/ppermute | solution.py:69
  54.7 1.2 %shard_map.149 = (bf16[128,512]{1,0:T(8,128)(2,1)}, bf16[128,512]{1,0:T(8,128)(2,1)}, f32[64,512]{1,0:T(8,128)}, f32[64,512]{1,0:T(8,128)}) custom-call(bf16[128,256]{1,0:T(8,128)(2,1)S(1)} %get-tuple-element.89.placed_ref, f32[128,128]{1,0:T(8,128)S(1)} %get-tuple-element.90.factors_ref, f32[128,512]{1,0:T(8,128)S(1)} %get-tuple-element.91.router_cols_ref, ...), custom_call_target="tpu_custom_call" | custom-call | flops 1000000000 | tf_op jit(solution)/shard_map/pallas_call | solution.py:673
  (54 shorter events, 4.9 us)
Async XLA Ops:
  0.6 12.8 %collective-permute-start.4 = (bf16[128,512]{1,0:T(8,128)(2,1)}, bf16[128,512]{1,0:T(8,128)(2,1)S(1)}, u32[]{:S(2)}, u32[]{:S(2)}) collective-permute-start(bf16[128,512]{1,0:T(8,128)(2,1)} %bitcast.39), channel_id=1, source_target_pairs={{0,1},{1,0},{2,3},{3,2},{4,5},{5,4},{6,7},{7,6},{8,9},{9,8},{10,11... | collective-permute-start | bytes 393224 | tf_op jit(solution)/shard_map/ppermute | solution.py:69
  3.6 8.4 %collective-permute-start = (bf16[128,512]{1,0:T(8,128)(2,1)}, bf16[128,512]{1,0:T(8,128)(2,1)S(1)}, u32[]{:S(2)}, u32[]{:S(2)}) collective-permute-start(bf16[128,512]{1,0:T(8,128)(2,1)} %bitcast.33), channel_id=1, source_target_pairs={{0,8},{8,16},{16,24},{24,0},{1,9},{9,17},{17,25},{25,1},{2,10},{10... | collective-permute-start | bytes 393224 | tf_op jit(solution)/shard_map/ppermute | solution.py:521
  5.2 8.3 %collective-permute-start.2 = (bf16[128,512]{1,0:T(8,128)(2,1)}, bf16[128,512]{1,0:T(8,128)(2,1)S(1)}, u32[]{:S(2)}, u32[]{:S(2)}) collective-permute-start(bf16[128,512]{1,0:T(8,128)(2,1)} %bitcast.36), channel_id=1, source_target_pairs={{0,8},{8,16},{16,24},{24,0},{1,9},{9,17},{17,25},{25,1},{2,10},{10... | collective-permute-start | bytes 393224 | tf_op jit(solution)/shard_map/ppermute | solution.py:521
  6.8 0.7 %copy-start.8 = (bf16[512,4]{0,1:T(4,128)(2,1)S(1)}, bf16[512,4]{0,1:T(4,128)(2,1)}, u32[]{:S(2)}) copy-start(bf16[512,4]{0,1:T(4,128)(2,1)} %param.17) | copy-start | bytes 12292
  7.5 0.9 %copy-start.3 = (bf16[1,128,512]{2,1,0:T(8,128)(2,1)S(1)}, bf16[1,128,512]{2,1,0:T(8,128)(2,1)}, u32[]{:S(2)}) copy-start(bf16[1,128,512]{2,1,0:T(8,128)(2,1)} %param.21) | copy-start | bytes 393220
  8.4 1.3 %copy-start.4 = (bf16[1,128,512]{2,1,0:T(8,128)(2,1)S(1)}, bf16[1,128,512]{2,1,0:T(8,128)(2,1)}, u32[]{:S(2)}) copy-start(bf16[1,128,512]{2,1,0:T(8,128)(2,1)} %param.12) | copy-start | bytes 393220
  8.4 1.3 %copy-start.5 = (bf16[1,128,512]{2,1,0:T(8,128)(2,1)S(1)}, bf16[1,128,512]{2,1,0:T(8,128)(2,1)}, u32[]{:S(2)}) copy-start(bf16[1,128,512]{2,1,0:T(8,128)(2,1)} %param.13) | copy-start | bytes 393220
  8.4 1.3 %copy-start.6 = (bf16[1,128,512]{2,1,0:T(8,128)(2,1)S(1)}, bf16[1,128,512]{2,1,0:T(8,128)(2,1)}, u32[]{:S(2)}) copy-start(bf16[1,128,512]{2,1,0:T(8,128)(2,1)} %param.11) | copy-start | bytes 393220
  9.0 6.4 %collective-permute-start.5 = (bf16[160,512]{1,0:T(8,128)(2,1)S(1)}, bf16[160,512]{1,0:T(8,128)(2,1)S(1)}, u32[]{:S(2)}, u32[]{:S(2)}) collective-permute-start(bf16[160,512]{1,0:T(8,128)(2,1)S(1)} %get-tuple-element.55.refs_0_.extended_ref), channel_id=1, source_target_pairs={{0,1},{1,0},{2,3},{3,2},{4,5},{5,4},{6,7},{7,6},{8,9},{9,8},{10,11... | collective-permute-start | bytes 491528 | tf_op jit(solution)/shard_map/ppermute | solution.py:69
  12.1 8.7 %collective-permute-start.1 = (bf16[128,512]{1,0:T(8,128)(2,1)S(1)}, bf16[128,512]{1,0:T(8,128)(2,1)S(1)}, u32[]{:S(2)}, u32[]{:S(2)}) collective-permute-start(bf16[128,512]{1,0:T(8,128)(2,1)S(1)} %collective-permute-done.refs_4_), channel_id=1, source_target_pairs={{0,8},{8,16},{16,24},{24,0},{1,9},{9,17},{17,25},{25,1},{2,10},{10... | collective-permute-start | bytes 393224 | tf_op jit(solution)/shard_map/ppermute | solution.py:521
  13.5 7.3 %collective-permute-start.3 = (bf16[128,512]{1,0:T(8,128)(2,1)S(1)}, bf16[128,512]{1,0:T(8,128)(2,1)S(1)}, u32[]{:S(2)}, u32[]{:S(2)}) collective-permute-start(bf16[128,512]{1,0:T(8,128)(2,1)S(1)} %collective-permute-done.2.refs_5_), channel_id=1, source_target_pairs={{0,8},{8,16},{16,24},{24,0},{1,9},{9,17},{17,25},{25,1},{2,10},{10... | collective-permute-start | bytes 393224 | tf_op jit(solution)/shard_map/ppermute | solution.py:521
  21.6 5.3 %collective-permute-start.6 = (bf16[592,128]{1,0:T(8,128)(2,1)S(1)}, bf16[592,128]{1,0:T(8,128)(2,1)S(1)}, u32[]{:S(2)}, u32[]{:S(2)}) collective-permute-start(bf16[592,128]{1,0:T(8,128)(2,1)S(1)} %shard_map.143), channel_id=1, source_target_pairs={{0,1},{1,0},{2,3},{3,2},{4,5},{5,4},{6,7},{7,6},{8,9},{9,8},{10,11... | collective-permute-start | bytes 454664 | tf_op jit(solution)/shard_map/ppermute | solution.py:69
  22.8 6.8 %collective-permute-start.10 = (bf16[128,512]{1,0:T(8,128)(2,1)S(1)}, bf16[128,512]{1,0:T(8,128)(2,1)S(1)}, u32[]{:S(2)}, u32[]{:S(2)}) collective-permute-start(bf16[128,512]{1,0:T(8,128)(2,1)S(1)} %get-tuple-element.80), channel_id=1, source_target_pairs={{0,2},{2,0},{4,6},{6,4},{1,3},{3,1},{5,7},{7,5},{8,10},{10,8},{12,... | collective-permute-start | bytes 393224 | tf_op jit(solution)/shard_map/ppermute | solution.py:69
  22.9 8.1 %collective-permute-start.11 = (bf16[128,512]{1,0:T(8,128)(2,1)S(1)}, bf16[128,512]{1,0:T(8,128)(2,1)S(1)}, u32[]{:S(2)}, u32[]{:S(2)}) collective-permute-start(bf16[128,512]{1,0:T(8,128)(2,1)S(1)} %get-tuple-element.81), channel_id=1, source_target_pairs={{0,4},{2,6},{4,0},{6,2},{1,5},{3,7},{5,1},{7,3},{8,12},{10,14},{12... | collective-permute-start | bytes 393224 | tf_op jit(solution)/shard_map/ppermute | solution.py:69
  24.4 9.0 %collective-permute-start.12 = (bf16[128,512]{1,0:T(8,128)(2,1)S(1)}, bf16[128,512]{1,0:T(8,128)(2,1)S(1)}, u32[]{:S(2)}, u32[]{:S(2)}) collective-permute-start(bf16[128,512]{1,0:T(8,128)(2,1)S(1)} %get-tuple-element.82), channel_id=1, source_target_pairs={{0,6},{2,4},{4,2},{6,0},{1,7},{3,5},{5,3},{7,1},{8,14},{10,12},{12... | collective-permute-start | bytes 393224 | tf_op jit(solution)/shard_map/ppermute | solution.py:69
  24.7 2.1 %copy-start = (bf16[512,512]{1,0:T(8,128)(2,1)S(1)}, bf16[512,512]{1,0:T(8,128)(2,1)}, u32[]{:S(2)}) copy-start(bf16[512,512]{1,0:T(8,128)(2,1)} %proj_ref.1) | copy-start | bytes 1572868
  24.7 2.1 %copy-start.7 = (bf16[1,128,512]{2,1,0:T(8,128)(2,1)S(1)}, bf16[1,128,512]{2,1,0:T(8,128)(2,1)}, u32[]{:S(2)}) copy-start(bf16[1,128,512]{2,1,0:T(8,128)(2,1)} %param.15) | copy-start | bytes 393220
  26.8 9.5 %copy-start.1 = (bf16[1,512,512]{2,1,0:T(8,128)(2,1)S(1)}, bf16[1,512,512]{2,1,0:T(8,128)(2,1)}, u32[]{:S(2)}) copy-start(bf16[1,512,512]{2,1,0:T(8,128)(2,1)} %param.19) | copy-start | bytes 1572868
  26.8 9.5 %copy-start.2 = (bf16[1,512,512]{2,1,0:T(8,128)(2,1)S(1)}, bf16[1,512,512]{2,1,0:T(8,128)(2,1)}, u32[]{:S(2)}) copy-start(bf16[1,512,512]{2,1,0:T(8,128)(2,1)} %param.20) | copy-start | bytes 1572868
  27.4 8.1 %collective-permute-start.13 = (bf16[64,512]{1,0:T(8,128)(2,1)S(1)}, bf16[64,512]{1,0:T(8,128)(2,1)S(1)}, u32[]{:S(2)}, u32[]{:S(2)}) collective-permute-start(bf16[64,512]{1,0:T(8,128)(2,1)S(1)} %get-tuple-element.76), channel_id=1, source_target_pairs={{0,7},{1,6},{2,5},{3,4},{4,3},{5,2},{6,1},{7,0},{8,15},{9,14},{10,... | collective-permute-start | bytes 196616 | tf_op jit(solution)/shard_map/ppermute | solution.py:69
  28.3 7.9 %collective-permute-start.14 = (bf16[64,512]{1,0:T(8,128)(2,1)S(1)}, bf16[64,512]{1,0:T(8,128)(2,1)S(1)}, u32[]{:S(2)}, u32[]{:S(2)}) collective-permute-start(bf16[64,512]{1,0:T(8,128)(2,1)S(1)} %get-tuple-element.77), channel_id=1, source_target_pairs={{0,5},{1,4},{2,7},{3,6},{4,1},{5,0},{6,3},{7,2},{8,13},{9,12},{10,... | collective-permute-start | bytes 196616 | tf_op jit(solution)/shard_map/ppermute | solution.py:69
  29.7 6.5 %collective-permute-start.15 = (bf16[64,512]{1,0:T(8,128)(2,1)S(1)}, bf16[64,512]{1,0:T(8,128)(2,1)S(1)}, u32[]{:S(2)}, u32[]{:S(2)}) collective-permute-start(bf16[64,512]{1,0:T(8,128)(2,1)S(1)} %get-tuple-element.78), channel_id=1, source_target_pairs={{0,3},{1,2},{2,1},{3,0},{4,7},{5,6},{6,5},{7,4},{8,11},{9,10},{10,... | collective-permute-start | bytes 196616 | tf_op jit(solution)/shard_map/ppermute | solution.py:69
  31.0 5.3 %collective-permute-start.16 = (bf16[64,512]{1,0:T(8,128)(2,1)S(1)}, bf16[64,512]{1,0:T(8,128)(2,1)S(1)}, u32[]{:S(2)}, u32[]{:S(2)}) collective-permute-start(bf16[64,512]{1,0:T(8,128)(2,1)S(1)} %get-tuple-element.79.refs_3_), channel_id=1, source_target_pairs={{0,1},{1,0},{2,3},{3,2},{4,5},{5,4},{6,7},{7,6},{8,9},{9,8},{10,11... | collective-permute-start | bytes 196616 | tf_op jit(solution)/shard_map/ppermute | solution.py:69
  33.5 4.5 %collective-permute-start.7 = (bf16[64,512]{1,0:T(8,128)(2,1)S(1)}, bf16[64,512]{1,0:T(8,128)(2,1)S(1)}, u32[]{:S(2)}, u32[]{:S(2)}) collective-permute-start(bf16[64,512]{1,0:T(8,128)(2,1)S(1)} %get-tuple-element.76), channel_id=1, source_target_pairs={{0,6},{1,7},{2,4},{3,5},{4,2},{5,3},{6,0},{7,1},{8,14},{9,15},{10,... | collective-permute-start | bytes 196616 | tf_op jit(solution)/shard_map/ppermute | solution.py:69
  35.5 4.3 %collective-permute-start.8 = (bf16[64,512]{1,0:T(8,128)(2,1)S(1)}, bf16[64,512]{1,0:T(8,128)(2,1)S(1)}, u32[]{:S(2)}, u32[]{:S(2)}) collective-permute-start(bf16[64,512]{1,0:T(8,128)(2,1)S(1)} %get-tuple-element.77), channel_id=1, source_target_pairs={{0,4},{1,5},{2,6},{3,7},{4,0},{5,1},{6,2},{7,3},{8,12},{9,13},{10,... | collective-permute-start | bytes 196616 | tf_op jit(solution)/shard_map/ppermute | solution.py:69
  36.1 3.7 %collective-permute-start.9 = (bf16[64,512]{1,0:T(8,128)(2,1)S(1)}, bf16[64,512]{1,0:T(8,128)(2,1)S(1)}, u32[]{:S(2)}, u32[]{:S(2)}) collective-permute-start(bf16[64,512]{1,0:T(8,128)(2,1)S(1)} %get-tuple-element.78), channel_id=1, source_target_pairs={{0,2},{1,3},{2,0},{3,1},{4,6},{5,7},{6,4},{7,5},{8,10},{9,11},{10,... | collective-permute-start | bytes 196616 | tf_op jit(solution)/shard_map/ppermute | solution.py:69
  41.4 8.3 %collective-permute-start.17 = (bf16[2,64,512]{2,1,0:T(8,128)(2,1)S(1)}, bf16[2,64,512]{2,1,0:T(8,128)(2,1)S(1)}, u32[]{:S(2)}, u32[]{:S(2)}) collective-permute-start(bf16[2,64,512]{2,1,0:T(8,128)(2,1)S(1)} %get-tuple-element.93), channel_id=1, source_target_pairs={{0,24},{8,16},{16,8},{24,0},{1,25},{9,17},{17,9},{25,1},{2,26},{10... | collective-permute-start | bytes 393224 | tf_op jit(solution)/shard_map/ppermute | solution.py:69
  42.1 12.0 %collective-permute-start.18 = (bf16[2,64,512]{2,1,0:T(8,128)(2,1)S(1)}, bf16[2,64,512]{2,1,0:T(8,128)(2,1)S(1)}, u32[]{:S(2)}, u32[]{:S(2)}) collective-permute-start(bf16[2,64,512]{2,1,0:T(8,128)(2,1)S(1)} %get-tuple-element.94), channel_id=1, source_target_pairs={{0,16},{8,24},{16,0},{24,8},{1,17},{9,25},{17,1},{25,9},{2,18},{10... | collective-permute-start | bytes 393224 | tf_op jit(solution)/shard_map/ppermute | solution.py:69
  42.7 11.4 %collective-permute-start.19 = (bf16[2,64,512]{2,1,0:T(8,128)(2,1)S(1)}, bf16[2,64,512]{2,1,0:T(8,128)(2,1)S(1)}, u32[]{:S(2)}, u32[]{:S(2)}) collective-permute-start(bf16[2,64,512]{2,1,0:T(8,128)(2,1)S(1)} %get-tuple-element.95), channel_id=1, source_target_pairs={{0,8},{8,0},{16,24},{24,16},{1,9},{9,1},{17,25},{25,17},{2,10},{10... | collective-permute-start | bytes 393224 | tf_op jit(solution)/shard_map/ppermute | solution.py:69
  46.3 7.8 %collective-permute-start.20 = (bf16[128,512]{1,0:T(8,128)(2,1)S(1)}, bf16[128,512]{1,0:T(8,128)(2,1)S(1)}, u32[]{:S(2)}, u32[]{:S(2)}) collective-permute-start(bf16[128,512]{1,0:T(8,128)(2,1)S(1)} %get-tuple-element.98), channel_id=1, source_target_pairs={{0,6},{2,4},{4,2},{6,0},{1,7},{3,5},{5,3},{7,1},{8,14},{10,12},{12... | collective-permute-start | bytes 393224 | tf_op jit(solution)/shard_map/ppermute | solution.py:69
  46.4 8.3 %collective-permute-start.21 = (bf16[128,512]{1,0:T(8,128)(2,1)S(1)}, bf16[128,512]{1,0:T(8,128)(2,1)S(1)}, u32[]{:S(2)}, u32[]{:S(2)}) collective-permute-start(bf16[128,512]{1,0:T(8,128)(2,1)S(1)} %get-tuple-element.99), channel_id=1, source_target_pairs={{0,4},{2,6},{4,0},{6,2},{1,5},{3,7},{5,1},{7,3},{8,12},{10,14},{12... | collective-permute-start | bytes 393224 | tf_op jit(solution)/shard_map/ppermute | solution.py:69
  49.7 5.0 %collective-permute-start.22 = (bf16[128,512]{1,0:T(8,128)(2,1)S(1)}, bf16[128,512]{1,0:T(8,128)(2,1)S(1)}, u32[]{:S(2)}, u32[]{:S(2)}) collective-permute-start(bf16[128,512]{1,0:T(8,128)(2,1)S(1)} %get-tuple-element.100), channel_id=1, source_target_pairs={{0,2},{2,0},{4,6},{6,4},{1,3},{3,1},{5,7},{7,5},{8,10},{10,8},{12,... | collective-permute-start | bytes 393224 | tf_op jit(solution)/shard_map/ppermute | solution.py:69
  (2 other events, 1.3 us)

commit v20 on v18

--- a/solution.py
+++ b/solution.py
@@ -320,6 +320,8 @@
     row_count, grad_count = counts
     row_refs, refs = refs[:row_count], refs[row_count:]
     per_rep = row_count // len(rep_list)
+    if rep_list == (0,) and per_rep == sources:
+        row_refs = row_refs[:1] + row_refs[1:][::-1]
     grad_refs, refs = refs[:grad_count], refs[grad_count:]
     own_rows = rep_list[0] == 0
     held_ref, refs = refs[-1], refs[:-1]
@@ -645,7 +647,7 @@
     )
     activated, pre_grad, *terms, kept = expert_call(
         (0,),
-        got_rows,
+        got_rows[:1] + got_rows[1:][::-1],
         [shape((slots, hidden))] * 2
         + [shape((2, strip, hidden))] * (seq_count - 1)
         + [shape((2, strip, hidden), jnp.float32)],

time: 55.7 us -> 54.3 us (0.975)
  starting transfers between devices: 23.6 us -> 22.7 us
  waiting for transfers between devices: 16.8 us -> 16.1 us
    ppermute x19, starting transfers between devices: 19.2 us -> 18.3 us  [exchange(): got[k] = lax.ppermute(chunks[k], self.axes, pairs)]
    ppermute x19, waiting for transfers between devices: 11.4 us -> 10.8 us  [exchange(): got[k] = lax.ppermute(chunks[k], self.axes, pairs)]
  transfers between devices with their start and end apart: 23 -> 23, of which waited for: 9 -> 10; matrix products, arithmetic and copies ran while one was open for 1% -> 1% of each run, Pallas kernels for 16% -> 16%
where the time goes in v20:
time: 54.3 us; the launch traced here: 54 us
  starting transfers between devices  22.7 us (42%)
  waiting for transfers between devices  16.1 us (30%)
  Pallas kernels  12.3 us (23%)
  local copies, waits for them, and re-layouts  1.69 us (3%)
  between operations  0.86 us (2%)
    ppermute x19, starting transfers between devices, exchange(): got[k] = lax.ppermute(chunks[k], self.axes, pairs)  18.3 us
    ppermute x19, waiting for transfers between devices, exchange(): got[k] = lax.ppermute(chunks[k], self.axes, pairs)  10.8 us
    ppermute x4, waiting for transfers between devices, forward(): lax.ppermute(array, 'seq', [(i, (i + 1) % seq_count) for i in range(seq_c...  5.34 us
    pallas_call x4, Pallas kernels, attend(): call(functools.partial(attend_kernel, plan, rep_count, len(pairs), packed...  5.2 us
    ppermute x4, starting transfers between devices, forward(): lax.ppermute(array, 'seq', [(i, (i + 1) % seq_count) for i in range(seq_c...  4.37 us
    pallas_call x2, Pallas kernels, expert_call(): call(functools.partial(expert_kernel, rep_count, rep_list, expert_count,...  3.24 us
    unnamed x22, local copies, waits for them, and re-layouts  1.6 us
    pallas_call x1, Pallas kernels, local(): call(functools.partial(finish_kernel, hot_capacity, seq_count), [shape((t...  1.25 us
  transfers between devices with their start and end apart: 23, of which 10 were waited for; matrix products, arithmetic and copies ran while one was open for 1% of the time, Pallas kernels for 16%

profile of v20, /device:TPU:0, one launch (start us, length us, event | category | flops | bytes accessed | tf_op | source)
XLA Modules:
  0.0 54.0 jit_solution(11196805699764443932)
XLA Ops:
  0.6 3.0 %collective-permute-start.4 = (bf16[128,512]{1,0:T(8,128)(2,1)}, bf16[128,512]{1,0:T(8,128)(2,1)S(1)}, u32[]{:S(2)}, u32[]{:S(2)}) collective-permute-start(bf16[128,512]{1,0:T(8,128)(2,1)} %bitcast.39), channel_id=1, source_target_pairs={{0,1},{1,0},{2,3},{3,2},{4,5},{5,4},{6,7},{7,6},{8,9},{9,8},{10,11... | collective-permute-start | bytes 393224 | tf_op jit(solution)/shard_map/ppermute | solution.py:69
  3.6 1.6 %collective-permute-start = (bf16[128,512]{1,0:T(8,128)(2,1)}, bf16[128,512]{1,0:T(8,128)(2,1)S(1)}, u32[]{:S(2)}, u32[]{:S(2)}) collective-permute-start(bf16[128,512]{1,0:T(8,128)(2,1)} %bitcast.33), channel_id=1, source_target_pairs={{0,8},{8,16},{16,24},{24,0},{1,9},{9,17},{17,25},{25,1},{2,10},{10... | collective-permute-start | bytes 393224 | tf_op jit(solution)/shard_map/ppermute | solution.py:523
  5.2 1.6 %collective-permute-start.2 = (bf16[128,512]{1,0:T(8,128)(2,1)}, bf16[128,512]{1,0:T(8,128)(2,1)S(1)}, u32[]{:S(2)}, u32[]{:S(2)}) collective-permute-start(bf16[128,512]{1,0:T(8,128)(2,1)} %bitcast.36), channel_id=1, source_target_pairs={{0,8},{8,16},{16,24},{24,0},{1,9},{9,17},{17,25},{25,1},{2,10},{10... | collective-permute-start | bytes 393224 | tf_op jit(solution)/shard_map/ppermute | solution.py:523
  6.9 0.6 %copy-done.8 = bf16[512,4]{0,1:T(4,128)(2,1)S(1)} copy-done((bf16[512,4]{0,1:T(4,128)(2,1)S(1)}, bf16[512,4]{0,1:T(4,128)(2,1)}, u32[]{:S(2)}) %copy-start.8) | copy-done | bytes 4120
  7.5 0.9 %copy-done.3 = bf16[1,128,512]{2,1,0:T(8,128)(2,1)S(1)} copy-done((bf16[1,128,512]{2,1,0:T(8,128)(2,1)S(1)}, bf16[1,128,512]{2,1,0:T(8,128)(2,1)}, u32[]{:S(2)}) %copy-start.3) | copy-done | bytes 131096
  8.4 0.6 %shard_map.138 = (bf16[160,512]{1,0:T(8,128)(2,1)S(1)}, s32[2,128]{1,0:T(2,128)S(1)}) custom-call(s32[2]{0:T(128)S(1)} %pad_add_fusion.1.ranks_ref, s32[1,8]{1,0:T(1,128)S(1)} %copy-done.9, s32[1,128]{1,0:T(1,128)S(1)} %bitcast.45, bf16[4,512]{1,0:T(4,128)(2,1)S(1)} %bitcast.44, bf16[128,512]{1,0:T(8,128)(2,1)S(1)} %bitcast.32), custom_call_target="tpu_custom_call" | custom-call | flops 500000000 | tf_op jit(solution)/shard_map/pallas_call | solution.py:545
  9.0 0.6 %collective-permute-start.5 = (bf16[160,512]{1,0:T(8,128)(2,1)S(1)}, bf16[160,512]{1,0:T(8,128)(2,1)S(1)}, u32[]{:S(2)}, u32[]{:S(2)}) collective-permute-start(bf16[160,512]{1,0:T(8,128)(2,1)S(1)} %get-tuple-element.55.refs_0_.extended_ref), channel_id=1, source_target_pairs={{0,1},{1,0},{2,3},{3,2},{4,5},{5,4},{6,7},{7,6},{8,9},{9,8},{10,11... | collective-permute-start | bytes 491528 | tf_op jit(solution)/shard_map/ppermute | solution.py:69
  9.7 1.8 %shard_map.139 = (f32[16,128]{1,0:T(8,128)S(1)}, f32[16,128]{1,0:T(8,128)S(1)}, f32[512,128]{1,0:T(8,128)S(1)}) custom-call(s32[3]{0:T(128)S(1)} %pad_add_fusion.4.ids_ref, s32[2,128]{1,0:T(2,128)S(1)} %get-tuple-element.56.begin_ref, bf16[128,512]{1,0:T(8,128)(2,1)S(1)} %bitcast.40, bf16[128,512]{1,0:T(8,128)(2,1)S(1)} %bitcast.34, ...), custom_call_target="tpu_custom_call" | custom-call | flops 2000000000 | tf_op jit(solution)/shard_map/pallas_call | solution.py:562
  12.1 1.2 %collective-permute-start.1 = (bf16[128,512]{1,0:T(8,128)(2,1)S(1)}, bf16[128,512]{1,0:T(8,128)(2,1)S(1)}, u32[]{:S(2)}, u32[]{:S(2)}) collective-permute-start(bf16[128,512]{1,0:T(8,128)(2,1)S(1)} %collective-permute-done.refs_4_), channel_id=1, source_target_pairs={{0,8},{8,16},{16,24},{24,0},{1,9},{9,17},{17,25},{25,1},{2,10},{10... | collective-permute-start | bytes 393224 | tf_op jit(solution)/shard_map/ppermute | solution.py:523
  13.5 1.9 %shard_map.140 = (f32[16,128]{1,0:T(8,128)S(1)}, f32[16,128]{1,0:T(8,128)S(1)}, f32[512,128]{1,0:T(8,128)S(1)}, f32[16,128]{1,0:T(8,128)S(1)}, f32[16,128]{1,0:T(8,128)S(1)}, /*index=5*/f32[512,128]{1,0:T(8,128)S(1)}) custom-call(s32[5]{0:T(128)S(1)} %stack.81.ids_ref, s32[2,128]{1,0:T(2,128)S(1)} %get-tuple-element.56.begin_ref, ...), custom_call_target="tpu_custom_call" | custom-call | flops 4000000000 | tf_op jit(solution)/shard_map/pallas_call | solution.py:562
  16.0 4.8 %collective-permute-done.3.refs_2_.refs_3_ = bf16[128,512]{1,0:T(8,128)(2,1)S(1)} collective-permute-done((bf16[128,512]{1,0:T(8,128)(2,1)S(1)}, bf16[128,512]{1,0:T(8,128)(2,1)S(1)}, u32[]{:S(2)}, u32[]{:S(2)}) %collective-permute-start.3) | collective-permute-done | bytes 131104 | tf_op jit(solution)/shard_map/ppermute | solution.py:523
  20.8 0.8 %shard_map.143 = bf16[592,128]{1,0:T(8,128)(2,1)S(1)} custom-call(s32[3]{0:T(128)S(1)} %pad_add_fusion.5.ids_ref, s32[2,128]{1,0:T(2,128)S(1)} %get-tuple-element.56.begin_ref, bf16[128,512]{1,0:T(8,128)(2,1)S(1)} %collective-permute-done.4.refs_1_.refs_0_, bf16[128,512]{1,0:T(8,128)(2,1)S(1)} %get-tuple-element.72.refs_1_.refs_4_, ...), custom_call_target="tpu_custom_call" | custom-call | flops 1500000000 | tf_op jit(solution)/shard_map/pallas_call | solution.py:562
  21.6 1.2 %collective-permute-start.6 = (bf16[592,128]{1,0:T(8,128)(2,1)S(1)}, bf16[592,128]{1,0:T(8,128)(2,1)S(1)}, u32[]{:S(2)}, u32[]{:S(2)}) collective-permute-start(bf16[592,128]{1,0:T(8,128)(2,1)S(1)} %shard_map.143), channel_id=1, source_target_pairs={{0,1},{1,0},{2,3},{3,2},{4,5},{5,4},{6,7},{7,6},{8,9},{9,8},{10,11... | collective-permute-start | bytes 454664 | tf_op jit(solution)/shard_map/ppermute | solution.py:69
  22.9 1.6 %collective-permute-start.11 = (bf16[128,512]{1,0:T(8,128)(2,1)S(1)}, bf16[128,512]{1,0:T(8,128)(2,1)S(1)}, u32[]{:S(2)}, u32[]{:S(2)}) collective-permute-start(bf16[128,512]{1,0:T(8,128)(2,1)S(1)} %get-tuple-element.81), channel_id=1, source_target_pairs={{0,4},{2,6},{4,0},{6,2},{1,5},{3,7},{5,1},{7,3},{8,12},{10,14},{12... | collective-permute-start | bytes 393224 | tf_op jit(solution)/shard_map/ppermute | solution.py:69
  24.7 0.7 %shard_map.141 = (f32[16,128]{1,0:T(8,128)S(1)}, f32[16,128]{1,0:T(8,128)S(1)}, f32[512,128]{1,0:T(8,128)S(1)}) custom-call(s32[3]{0:T(128)S(1)} %pad_add_fusion.2.ids_ref, s32[2,128]{1,0:T(2,128)S(1)} %get-tuple-element.56.begin_ref, bf16[128,512]{1,0:T(8,128)(2,1)S(1)} %bitcast.42, bf16[128,512]{1,0:T(8,128)(2,1)S(1)} %collective-permute-done.1.refs_1_.refs_2_, ...), custom_call_target="tpu_custom_call" | custom-call | flops 1500000000 | tf_op jit(solution)/shard_map/pallas_call | solution.py:562
  25.5 1.3 %collective-permute-done.6.refs_3_ = bf16[592,128]{1,0:T(8,128)(2,1)S(1)} collective-permute-done((bf16[592,128]{1,0:T(8,128)(2,1)S(1)}, bf16[592,128]{1,0:T(8,128)(2,1)S(1)}, u32[]{:S(2)}, u32[]{:S(2)}) %collective-permute-start.6) | collective-permute-done | bytes 151584 | tf_op jit(solution)/shard_map/ppermute | solution.py:69
  26.8 0.6 %shard_map.144 = (bf16[128,512]{1,0:T(8,128)(2,1)S(1)}, bf16[64,512]{1,0:T(8,128)(2,1)S(1)}, bf16[64,512]{1,0:T(8,128)(2,1)S(1)}, bf16[64,512]{1,0:T(8,128)(2,1)S(1)}, bf16[64,512]{1,0:T(8,128)(2,1)S(1)}) custom-call(s32[1]{0:T(128)} %bitcast.own_ref, bf16[160,512]{1,0:T(8,128)(2,1)S(1)} %get-tuple-element.55.refs_0_.extended_ref, ...), custom_call_target="tpu_custom_call" | custom-call | flops 2000000000 | tf_op jit(solution)/shard_map/pallas_call | solution.py:609
  27.4 1.2 %collective-permute-start.13 = (bf16[64,512]{1,0:T(8,128)(2,1)S(1)}, bf16[64,512]{1,0:T(8,128)(2,1)S(1)}, u32[]{:S(2)}, u32[]{:S(2)}) collective-permute-start(bf16[64,512]{1,0:T(8,128)(2,1)S(1)} %get-tuple-element.76.refs_0_), channel_id=1, source_target_pairs={{0,1},{1,0},{2,3},{3,2},{4,5},{5,4},{6,7},{7,6},{8,9},{9,8},{10,11... | collective-permute-start | bytes 196616 | tf_op jit(solution)/shard_map/ppermute | solution.py:69
  29.1 1.4 %collective-permute-start.15 = (bf16[64,512]{1,0:T(8,128)(2,1)S(1)}, bf16[64,512]{1,0:T(8,128)(2,1)S(1)}, u32[]{:S(2)}, u32[]{:S(2)}) collective-permute-start(bf16[64,512]{1,0:T(8,128)(2,1)S(1)} %get-tuple-element.78), channel_id=1, source_target_pairs={{0,5},{1,4},{2,7},{3,6},{4,1},{5,0},{6,3},{7,2},{8,13},{9,12},{10,... | collective-permute-start | bytes 196616 | tf_op jit(solution)/shard_map/ppermute | solution.py:69
  30.5 1.4 %collective-permute-start.14 = (bf16[64,512]{1,0:T(8,128)(2,1)S(1)}, bf16[64,512]{1,0:T(8,128)(2,1)S(1)}, u32[]{:S(2)}, u32[]{:S(2)}) collective-permute-start(bf16[64,512]{1,0:T(8,128)(2,1)S(1)} %get-tuple-element.79), channel_id=1, source_target_pairs={{0,3},{1,2},{2,1},{3,0},{4,7},{5,6},{6,5},{7,4},{8,11},{9,10},{10,... | collective-permute-start | bytes 196616 | tf_op jit(solution)/shard_map/ppermute | solution.py:69
  32.0 0.8 %collective-permute-start.7 = (bf16[64,512]{1,0:T(8,128)(2,1)S(1)}, bf16[64,512]{1,0:T(8,128)(2,1)S(1)}, u32[]{:S(2)}, u32[]{:S(2)}) collective-permute-start(bf16[64,512]{1,0:T(8,128)(2,1)S(1)} %get-tuple-element.77), channel_id=1, source_target_pairs={{0,6},{1,7},{2,4},{3,5},{4,2},{5,3},{6,0},{7,1},{8,14},{9,15},{10,... | collective-permute-start | bytes 196616 | tf_op jit(solution)/shard_map/ppermute | solution.py:69
  32.8 0.8 %collective-permute-start.8 = (bf16[64,512]{1,0:T(8,128)(2,1)S(1)}, bf16[64,512]{1,0:T(8,128)(2,1)S(1)}, u32[]{:S(2)}, u32[]{:S(2)}) collective-permute-start(bf16[64,512]{1,0:T(8,128)(2,1)S(1)} %get-tuple-element.78), channel_id=1, source_target_pairs={{0,4},{1,5},{2,6},{3,7},{4,0},{5,1},{6,2},{7,3},{8,12},{9,13},{10,... | collective-permute-start | bytes 196616 | tf_op jit(solution)/shard_map/ppermute | solution.py:69
  34.0 1.6 %collective-permute-done.15.refs_2_ = bf16[64,512]{1,0:T(8,128)(2,1)S(1)} collective-permute-done((bf16[64,512]{1,0:T(8,128)(2,1)S(1)}, bf16[64,512]{1,0:T(8,128)(2,1)S(1)}, u32[]{:S(2)}, u32[]{:S(2)}) %collective-permute-start.15) | collective-permute-done | bytes 65568 | tf_op jit(solution)/shard_map/ppermute | solution.py:69
  36.1 1.6 %shard_map.145 = (f32[256,512]{1,0:T(8,128)S(1)}, f32[256,512]{1,0:T(8,128)S(1)}) custom-call(s32[1]{0:T(128)} %bitcast.own_ref, s32[4]{0:T(128)S(1)} %pad_add_fusion.part_ref, bf16[512,512]{1,0:T(8,128)(2,1)S(1)} %bitcast.26, bf16[512,512]{1,0:T(8,128)(2,1)S(1)} %bitcast.29, bf16[160,512]{1,0:T(8,128)(2,1)S(1)} %get-tuple-element.55.refs_0_.extended_ref, ...), custom_call_target="tpu_custom_call" | custom-call | flops 2000000000 | tf_op jit(solution)/shard_map/pallas_call | solution.py:622
  37.7 0.6 %collective-permute-done.8.refs_2_ = bf16[64,512]{1,0:T(8,128)(2,1)S(1)} collective-permute-done((bf16[64,512]{1,0:T(8,128)(2,1)S(1)}, bf16[64,512]{1,0:T(8,128)(2,1)S(1)}, u32[]{:S(2)}, u32[]{:S(2)}) %collective-permute-start.8) | collective-permute-done | bytes 65568 | tf_op jit(solution)/shard_map/ppermute | solution.py:69
  38.3 1.6 %shard_map.146 = (bf16[256,512]{1,0:T(8,128)(2,1)S(1)}, bf16[256,512]{1,0:T(8,128)(2,1)S(1)}, bf16[2,64,512]{2,1,0:T(8,128)(2,1)S(1)}, bf16[2,64,512]{2,1,0:T(8,...) custom-call(s32[1]{0:T(128)} %bitcast.own_ref, s32[4]{0:T(128)S(1)} %pad_add_fusion.part_ref, ...), custom_call_target="tpu_custom_call" | custom-call | flops 2000000000 | tf_op jit(solution)/shard_map/pallas_call | solution.py:622
  40.0 1.2 %collective-permute-start.17 = (bf16[2,64,512]{2,1,0:T(8,128)(2,1)S(1)}, bf16[2,64,512]{2,1,0:T(8,128)(2,1)S(1)}, u32[]{:S(2)}, u32[]{:S(2)}) collective-permute-start(bf16[2,64,512]{2,1,0:T(8,128)(2,1)S(1)} %get-tuple-element.93), channel_id=1, source_target_pairs={{0,24},{8,16},{16,8},{24,0},{1,25},{9,17},{17,9},{25,1},{2,26},{10... | collective-permute-start | bytes 393224 | tf_op jit(solution)/shard_map/ppermute | solution.py:69
  41.1 3.3 %collective-permute-start.19 = (bf16[2,64,512]{2,1,0:T(8,128)(2,1)S(1)}, bf16[2,64,512]{2,1,0:T(8,128)(2,1)S(1)}, u32[]{:S(2)}, u32[]{:S(2)}) collective-permute-start(bf16[2,64,512]{2,1,0:T(8,128)(2,1)S(1)} %get-tuple-element.95), channel_id=1, source_target_pairs={{0,8},{8,0},{16,24},{24,16},{1,9},{9,1},{17,25},{25,17},{2,10},{10... | collective-permute-start | bytes 393224 | tf_op jit(solution)/shard_map/ppermute | solution.py:69
  44.9 0.9 %collective-permute-start.21 = (bf16[128,512]{1,0:T(8,128)(2,1)S(1)}, bf16[128,512]{1,0:T(8,128)(2,1)S(1)}, u32[]{:S(2)}, u32[]{:S(2)}) collective-permute-start(bf16[128,512]{1,0:T(8,128)(2,1)S(1)} %get-tuple-element.99), channel_id=1, source_target_pairs={{0,4},{2,6},{4,0},{6,2},{1,5},{3,7},{5,1},{7,3},{8,12},{10,14},{12... | collective-permute-start | bytes 393224 | tf_op jit(solution)/shard_map/ppermute | solution.py:69
  45.8 2.5 %collective-permute-done.17.refs_1_ = bf16[2,64,512]{2,1,0:T(8,128)(2,1)S(1)} collective-permute-done((bf16[2,64,512]{2,1,0:T(8,128)(2,1)S(1)}, bf16[2,64,512]{2,1,0:T(8,128)(2,1)S(1)}, u32[]{:S(2)}, u32[]{:S(2)}) %collective-permute-start.17) | collective-permute-done | bytes 131104 | tf_op jit(solution)/shard_map/ppermute | solution.py:69
  48.8 3.9 %collective-permute-done.18.refs_2_ = bf16[2,64,512]{2,1,0:T(8,128)(2,1)S(1)} collective-permute-done((bf16[2,64,512]{2,1,0:T(8,128)(2,1)S(1)}, bf16[2,64,512]{2,1,0:T(8,128)(2,1)S(1)}, u32[]{:S(2)}, u32[]{:S(2)}) %collective-permute-start.18) | collective-permute-done | bytes 131104 | tf_op jit(solution)/shard_map/ppermute | solution.py:69
  52.7 1.3 %shard_map.149 = (bf16[128,512]{1,0:T(8,128)(2,1)}, bf16[128,512]{1,0:T(8,128)(2,1)}, f32[64,512]{1,0:T(8,128)}, f32[64,512]{1,0:T(8,128)}) custom-call(bf16[128,256]{1,0:T(8,128)(2,1)S(1)} %get-tuple-element.89.placed_ref, f32[128,128]{1,0:T(8,128)S(1)} %get-tuple-element.90.factors_ref, f32[128,512]{1,0:T(8,128)S(1)} %get-tuple-element.91.router_cols_ref, ...), custom_call_target="tpu_custom_call" | custom-call | flops 1000000000 | tf_op jit(solution)/shard_map/pallas_call | solution.py:675
  (54 shorter events, 4.4 us)
Async XLA Ops:
  0.6 12.8 %collective-permute-start.4 = (bf16[128,512]{1,0:T(8,128)(2,1)}, bf16[128,512]{1,0:T(8,128)(2,1)S(1)}, u32[]{:S(2)}, u32[]{:S(2)}) collective-permute-start(bf16[128,512]{1,0:T(8,128)(2,1)} %bitcast.39), channel_id=1, source_target_pairs={{0,1},{1,0},{2,3},{3,2},{4,5},{5,4},{6,7},{7,6},{8,9},{9,8},{10,11... | collective-permute-start | bytes 393224 | tf_op jit(solution)/shard_map/ppermute | solution.py:69
  3.6 8.4 %collective-permute-start = (bf16[128,512]{1,0:T(8,128)(2,1)}, bf16[128,512]{1,0:T(8,128)(2,1)S(1)}, u32[]{:S(2)}, u32[]{:S(2)}) collective-permute-start(bf16[128,512]{1,0:T(8,128)(2,1)} %bitcast.33), channel_id=1, source_target_pairs={{0,8},{8,16},{16,24},{24,0},{1,9},{9,17},{17,25},{25,1},{2,10},{10... | collective-permute-start | bytes 393224 | tf_op jit(solution)/shard_map/ppermute | solution.py:523
  5.2 8.3 %collective-permute-start.2 = (bf16[128,512]{1,0:T(8,128)(2,1)}, bf16[128,512]{1,0:T(8,128)(2,1)S(1)}, u32[]{:S(2)}, u32[]{:S(2)}) collective-permute-start(bf16[128,512]{1,0:T(8,128)(2,1)} %bitcast.36), channel_id=1, source_target_pairs={{0,8},{8,16},{16,24},{24,0},{1,9},{9,17},{17,25},{25,1},{2,10},{10... | collective-permute-start | bytes 393224 | tf_op jit(solution)/shard_map/ppermute | solution.py:523
  6.8 0.7 %copy-start.8 = (bf16[512,4]{0,1:T(4,128)(2,1)S(1)}, bf16[512,4]{0,1:T(4,128)(2,1)}, u32[]{:S(2)}) copy-start(bf16[512,4]{0,1:T(4,128)(2,1)} %param.17) | copy-start | bytes 12292
  7.5 0.9 %copy-start.3 = (bf16[1,128,512]{2,1,0:T(8,128)(2,1)S(1)}, bf16[1,128,512]{2,1,0:T(8,128)(2,1)}, u32[]{:S(2)}) copy-start(bf16[1,128,512]{2,1,0:T(8,128)(2,1)} %param.21) | copy-start | bytes 393220
  8.4 1.3 %copy-start.4 = (bf16[1,128,512]{2,1,0:T(8,128)(2,1)S(1)}, bf16[1,128,512]{2,1,0:T(8,128)(2,1)}, u32[]{:S(2)}) copy-start(bf16[1,128,512]{2,1,0:T(8,128)(2,1)} %param.12) | copy-start | bytes 393220
  8.4 1.3 %copy-start.5 = (bf16[1,128,512]{2,1,0:T(8,128)(2,1)S(1)}, bf16[1,128,512]{2,1,0:T(8,128)(2,1)}, u32[]{:S(2)}) copy-start(bf16[1,128,512]{2,1,0:T(8,128)(2,1)} %param.13) | copy-start | bytes 393220
  8.4 1.3 %copy-start.6 = (bf16[1,128,512]{2,1,0:T(8,128)(2,1)S(1)}, bf16[1,128,512]{2,1,0:T(8,128)(2,1)}, u32[]{:S(2)}) copy-start(bf16[1,128,512]{2,1,0:T(8,128)(2,1)} %param.11) | copy-start | bytes 393220
  9.0 6.4 %collective-permute-start.5 = (bf16[160,512]{1,0:T(8,128)(2,1)S(1)}, bf16[160,512]{1,0:T(8,128)(2,1)S(1)}, u32[]{:S(2)}, u32[]{:S(2)}) collective-permute-start(bf16[160,512]{1,0:T(8,128)(2,1)S(1)} %get-tuple-element.55.refs_0_.extended_ref), channel_id=1, source_target_pairs={{0,1},{1,0},{2,3},{3,2},{4,5},{5,4},{6,7},{7,6},{8,9},{9,8},{10,11... | collective-permute-start | bytes 491528 | tf_op jit(solution)/shard_map/ppermute | solution.py:69
  12.1 8.7 %collective-permute-start.1 = (bf16[128,512]{1,0:T(8,128)(2,1)S(1)}, bf16[128,512]{1,0:T(8,128)(2,1)S(1)}, u32[]{:S(2)}, u32[]{:S(2)}) collective-permute-start(bf16[128,512]{1,0:T(8,128)(2,1)S(1)} %collective-permute-done.refs_4_), channel_id=1, source_target_pairs={{0,8},{8,16},{16,24},{24,0},{1,9},{9,17},{17,25},{25,1},{2,10},{10... | collective-permute-start | bytes 393224 | tf_op jit(solution)/shard_map/ppermute | solution.py:523
  13.5 7.3 %collective-permute-start.3 = (bf16[128,512]{1,0:T(8,128)(2,1)S(1)}, bf16[128,512]{1,0:T(8,128)(2,1)S(1)}, u32[]{:S(2)}, u32[]{:S(2)}) collective-permute-start(bf16[128,512]{1,0:T(8,128)(2,1)S(1)} %collective-permute-done.2.refs_5_), channel_id=1, source_target_pairs={{0,8},{8,16},{16,24},{24,0},{1,9},{9,17},{17,25},{25,1},{2,10},{10... | collective-permute-start | bytes 393224 | tf_op jit(solution)/shard_map/ppermute | solution.py:523
  21.6 5.3 %collective-permute-start.6 = (bf16[592,128]{1,0:T(8,128)(2,1)S(1)}, bf16[592,128]{1,0:T(8,128)(2,1)S(1)}, u32[]{:S(2)}, u32[]{:S(2)}) collective-permute-start(bf16[592,128]{1,0:T(8,128)(2,1)S(1)} %shard_map.143), channel_id=1, source_target_pairs={{0,1},{1,0},{2,3},{3,2},{4,5},{5,4},{6,7},{7,6},{8,9},{9,8},{10,11... | collective-permute-start | bytes 454664 | tf_op jit(solution)/shard_map/ppermute | solution.py:69
  22.8 6.3 %collective-permute-start.10 = (bf16[128,512]{1,0:T(8,128)(2,1)S(1)}, bf16[128,512]{1,0:T(8,128)(2,1)S(1)}, u32[]{:S(2)}, u32[]{:S(2)}) collective-permute-start(bf16[128,512]{1,0:T(8,128)(2,1)S(1)} %get-tuple-element.80), channel_id=1, source_target_pairs={{0,2},{2,0},{4,6},{6,4},{1,3},{3,1},{5,7},{7,5},{8,10},{10,8},{12,... | collective-permute-start | bytes 393224 | tf_op jit(solution)/shard_map/ppermute | solution.py:69
  22.9 7.7 %collective-permute-start.11 = (bf16[128,512]{1,0:T(8,128)(2,1)S(1)}, bf16[128,512]{1,0:T(8,128)(2,1)S(1)}, u32[]{:S(2)}, u32[]{:S(2)}) collective-permute-start(bf16[128,512]{1,0:T(8,128)(2,1)S(1)} %get-tuple-element.81), channel_id=1, source_target_pairs={{0,4},{2,6},{4,0},{6,2},{1,5},{3,7},{5,1},{7,3},{8,12},{10,14},{12... | collective-permute-start | bytes 393224 | tf_op jit(solution)/shard_map/ppermute | solution.py:69
  24.4 7.5 %collective-permute-start.12 = (bf16[128,512]{1,0:T(8,128)(2,1)S(1)}, bf16[128,512]{1,0:T(8,128)(2,1)S(1)}, u32[]{:S(2)}, u32[]{:S(2)}) collective-permute-start(bf16[128,512]{1,0:T(8,128)(2,1)S(1)} %get-tuple-element.82), channel_id=1, source_target_pairs={{0,6},{2,4},{4,2},{6,0},{1,7},{3,5},{5,3},{7,1},{8,14},{10,12},{12... | collective-permute-start | bytes 393224 | tf_op jit(solution)/shard_map/ppermute | solution.py:69
  24.7 2.1 %copy-start = (bf16[512,512]{1,0:T(8,128)(2,1)S(1)}, bf16[512,512]{1,0:T(8,128)(2,1)}, u32[]{:S(2)}) copy-start(bf16[512,512]{1,0:T(8,128)(2,1)} %proj_ref.1) | copy-start | bytes 1572868
  24.7 2.1 %copy-start.7 = (bf16[1,128,512]{2,1,0:T(8,128)(2,1)S(1)}, bf16[1,128,512]{2,1,0:T(8,128)(2,1)}, u32[]{:S(2)}) copy-start(bf16[1,128,512]{2,1,0:T(8,128)(2,1)} %param.15) | copy-start | bytes 393220
  26.8 9.3 %copy-start.1 = (bf16[1,512,512]{2,1,0:T(8,128)(2,1)S(1)}, bf16[1,512,512]{2,1,0:T(8,128)(2,1)}, u32[]{:S(2)}) copy-start(bf16[1,512,512]{2,1,0:T(8,128)(2,1)} %param.19) | copy-start | bytes 1572868
  26.8 9.3 %copy-start.2 = (bf16[1,512,512]{2,1,0:T(8,128)(2,1)S(1)}, bf16[1,512,512]{2,1,0:T(8,128)(2,1)}, u32[]{:S(2)}) copy-start(bf16[1,512,512]{2,1,0:T(8,128)(2,1)} %param.20) | copy-start | bytes 1572868
  27.4 5.4 %collective-permute-start.13 = (bf16[64,512]{1,0:T(8,128)(2,1)S(1)}, bf16[64,512]{1,0:T(8,128)(2,1)S(1)}, u32[]{:S(2)}, u32[]{:S(2)}) collective-permute-start(bf16[64,512]{1,0:T(8,128)(2,1)S(1)} %get-tuple-element.76.refs_0_), channel_id=1, source_target_pairs={{0,1},{1,0},{2,3},{3,2},{4,5},{5,4},{6,7},{7,6},{8,9},{9,8},{10,11... | collective-permute-start | bytes 196616 | tf_op jit(solution)/shard_map/ppermute | solution.py:69
  28.6 5.2 %collective-permute-start.16 = (bf16[64,512]{1,0:T(8,128)(2,1)S(1)}, bf16[64,512]{1,0:T(8,128)(2,1)S(1)}, u32[]{:S(2)}, u32[]{:S(2)}) collective-permute-start(bf16[64,512]{1,0:T(8,128)(2,1)S(1)} %get-tuple-element.77), channel_id=1, source_target_pairs={{0,7},{1,6},{2,5},{3,4},{4,3},{5,2},{6,1},{7,0},{8,15},{9,14},{10,... | collective-permute-start | bytes 196616 | tf_op jit(solution)/shard_map/ppermute | solution.py:69
  29.1 6.4 %collective-permute-start.15 = (bf16[64,512]{1,0:T(8,128)(2,1)S(1)}, bf16[64,512]{1,0:T(8,128)(2,1)S(1)}, u32[]{:S(2)}, u32[]{:S(2)}) collective-permute-start(bf16[64,512]{1,0:T(8,128)(2,1)S(1)} %get-tuple-element.78), channel_id=1, source_target_pairs={{0,5},{1,4},{2,7},{3,6},{4,1},{5,0},{6,3},{7,2},{8,13},{9,12},{10,... | collective-permute-start | bytes 196616 | tf_op jit(solution)/shard_map/ppermute | solution.py:69
  30.5 5.6 %collective-permute-start.14 = (bf16[64,512]{1,0:T(8,128)(2,1)S(1)}, bf16[64,512]{1,0:T(8,128)(2,1)S(1)}, u32[]{:S(2)}, u32[]{:S(2)}) collective-permute-start(bf16[64,512]{1,0:T(8,128)(2,1)S(1)} %get-tuple-element.79), channel_id=1, source_target_pairs={{0,3},{1,2},{2,1},{3,0},{4,7},{5,6},{6,5},{7,4},{8,11},{9,10},{10,... | collective-permute-start | bytes 196616 | tf_op jit(solution)/shard_map/ppermute | solution.py:69
  32.0 5.7 %collective-permute-start.7 = (bf16[64,512]{1,0:T(8,128)(2,1)S(1)}, bf16[64,512]{1,0:T(8,128)(2,1)S(1)}, u32[]{:S(2)}, u32[]{:S(2)}) collective-permute-start(bf16[64,512]{1,0:T(8,128)(2,1)S(1)} %get-tuple-element.77), channel_id=1, source_target_pairs={{0,6},{1,7},{2,4},{3,5},{4,2},{5,3},{6,0},{7,1},{8,14},{9,15},{10,... | collective-permute-start | bytes 196616 | tf_op jit(solution)/shard_map/ppermute | solution.py:69
  32.8 5.5 %collective-permute-start.8 = (bf16[64,512]{1,0:T(8,128)(2,1)S(1)}, bf16[64,512]{1,0:T(8,128)(2,1)S(1)}, u32[]{:S(2)}, u32[]{:S(2)}) collective-permute-start(bf16[64,512]{1,0:T(8,128)(2,1)S(1)} %get-tuple-element.78), channel_id=1, source_target_pairs={{0,4},{1,5},{2,6},{3,7},{4,0},{5,1},{6,2},{7,3},{8,12},{9,13},{10,... | collective-permute-start | bytes 196616 | tf_op jit(solution)/shard_map/ppermute | solution.py:69
  33.9 4.5 %collective-permute-start.9 = (bf16[64,512]{1,0:T(8,128)(2,1)S(1)}, bf16[64,512]{1,0:T(8,128)(2,1)S(1)}, u32[]{:S(2)}, u32[]{:S(2)}) collective-permute-start(bf16[64,512]{1,0:T(8,128)(2,1)S(1)} %get-tuple-element.79), channel_id=1, source_target_pairs={{0,2},{1,3},{2,0},{3,1},{4,6},{5,7},{6,4},{7,5},{8,10},{9,11},{10,... | collective-permute-start | bytes 196616 | tf_op jit(solution)/shard_map/ppermute | solution.py:69
  40.0 8.3 %collective-permute-start.17 = (bf16[2,64,512]{2,1,0:T(8,128)(2,1)S(1)}, bf16[2,64,512]{2,1,0:T(8,128)(2,1)S(1)}, u32[]{:S(2)}, u32[]{:S(2)}) collective-permute-start(bf16[2,64,512]{2,1,0:T(8,128)(2,1)S(1)} %get-tuple-element.93), channel_id=1, source_target_pairs={{0,24},{8,16},{16,8},{24,0},{1,25},{9,17},{17,9},{25,1},{2,26},{10... | collective-permute-start | bytes 393224 | tf_op jit(solution)/shard_map/ppermute | solution.py:69
  41.1 11.6 %collective-permute-start.18 = (bf16[2,64,512]{2,1,0:T(8,128)(2,1)S(1)}, bf16[2,64,512]{2,1,0:T(8,128)(2,1)S(1)}, u32[]{:S(2)}, u32[]{:S(2)}) collective-permute-start(bf16[2,64,512]{2,1,0:T(8,128)(2,1)S(1)} %get-tuple-element.94), channel_id=1, source_target_pairs={{0,16},{8,24},{16,0},{24,8},{1,17},{9,25},{17,1},{25,9},{2,18},{10... | collective-permute-start | bytes 393224 | tf_op jit(solution)/shard_map/ppermute | solution.py:69
  41.1 11.6 %collective-permute-start.19 = (bf16[2,64,512]{2,1,0:T(8,128)(2,1)S(1)}, bf16[2,64,512]{2,1,0:T(8,128)(2,1)S(1)}, u32[]{:S(2)}, u32[]{:S(2)}) collective-permute-start(bf16[2,64,512]{2,1,0:T(8,128)(2,1)S(1)} %get-tuple-element.95), channel_id=1, source_target_pairs={{0,8},{8,0},{16,24},{24,16},{1,9},{9,1},{17,25},{25,17},{2,10},{10... | collective-permute-start | bytes 393224 | tf_op jit(solution)/shard_map/ppermute | solution.py:69
  44.9 7.9 %collective-permute-start.20 = (bf16[128,512]{1,0:T(8,128)(2,1)S(1)}, bf16[128,512]{1,0:T(8,128)(2,1)S(1)}, u32[]{:S(2)}, u32[]{:S(2)}) collective-permute-start(bf16[128,512]{1,0:T(8,128)(2,1)S(1)} %get-tuple-element.98), channel_id=1, source_target_pairs={{0,6},{2,4},{4,2},{6,0},{1,7},{3,5},{5,3},{7,1},{8,14},{10,12},{12... | collective-permute-start | bytes 393224 | tf_op jit(solution)/shard_map/ppermute | solution.py:69
  44.9 7.8 %collective-permute-start.21 = (bf16[128,512]{1,0:T(8,128)(2,1)S(1)}, bf16[128,512]{1,0:T(8,128)(2,1)S(1)}, u32[]{:S(2)}, u32[]{:S(2)}) collective-permute-start(bf16[128,512]{1,0:T(8,128)(2,1)S(1)} %get-tuple-element.99), channel_id=1, source_target_pairs={{0,4},{2,6},{4,0},{6,2},{1,5},{3,7},{5,1},{7,3},{8,12},{10,14},{12... | collective-permute-start | bytes 393224 | tf_op jit(solution)/shard_map/ppermute | solution.py:69
  48.3 4.4 %collective-permute-start.22 = (bf16[128,512]{1,0:T(8,128)(2,1)S(1)}, bf16[128,512]{1,0:T(8,128)(2,1)S(1)}, u32[]{:S(2)}, u32[]{:S(2)}) collective-permute-start(bf16[128,512]{1,0:T(8,128)(2,1)S(1)} %get-tuple-element.100), channel_id=1, source_target_pairs={{0,2},{2,0},{4,6},{6,4},{1,3},{3,1},{5,7},{7,5},{8,10},{10,8},{12,... | collective-permute-start | bytes 393224 | tf_op jit(solution)/shard_map/ppermute | solution.py:69
  (2 other events, 1.3 us)

commit v21 on v20

--- a/solution.py
+++ b/solution.py
@@ -582,10 +582,9 @@
     lines[1] = (ahead, lines[1][1])
     for unused in range(1, reach):
         lines.append(tuple(forward(one) for one in lines[-1]))
-    middle = tuple((0, step, False) for step in range(1, reach)) + tuple(
-        (k, step, step == 0) for k in others for step in range(reach)
-    )
-    states = attend(middle, lines[:-1], list(range(reach)), queries, states, False, 4.0)
+    own_state = states
+    middle = tuple((k, step, step == 0) for k in others for step in range(reach))
+    states = attend(middle, lines[:-1], list(range(reach)), queries, {}, False, 3.0)
     states[1][0], *extendeds[1:] = lax.optimization_barrier((states[1][0], *extendeds[1:]))
     sent_grads = call(
         functools.partial(dispatch_kernel, rep_count, tok, hot_capacity),
@@ -603,7 +602,15 @@
         ahead=sent_grads[:1],
     )
     returned = reps.exchange([None] + [partial[k] for k in others], inverse=True)[1:]
-    states = attend(((0, 0, False),), lines[-1:], [reach], queries, states, False, 1.5)
+    states = attend(
+        tuple((0, step, False) for step in range(reach)),
+        lines[1:],
+        list(range(1, reach + 1)),
+        queries,
+        own_state,
+        False,
+        2.5,
+    )
     got_grads = merged(experts.exchange(sent_grads), MOST_PERMUTES)
 
     mixed, *sent_rows = call(

time: 54.3 us -> 55.5 us (1.022)
  waiting for transfers between devices: 16.1 us -> 17.5 us
    ppermute x19, waiting for transfers between devices: 10.8 us -> 14 us  [exchange(): got[k] = lax.ppermute(chunks[k], self.axes, pairs)]
    ppermute x4, waiting for transfers between devices: 5.34 us -> 3.44 us  [forward(): lax.ppermute(array, 'seq', [(i, (i + 1) % seq_count) for i in range(seq_c...]
  transfers between devices with their start and end apart: 23 -> 23, of which waited for: 10 -> 10; matrix products, arithmetic and copies ran while one was open for 1% -> 1% of each run, Pallas kernels for 16% -> 17%
where the time goes in v21:
time: 55.5 us; the launch traced here: 55.3 us
  starting transfers between devices  22.7 us (41%)
  waiting for transfers between devices  17.5 us (32%)
  Pallas kernels  12.3 us (22%)
  local copies, waits for them, and re-layouts  1.61 us (3%)
  between operations  0.81 us (1%)
    ppermute x19, starting transfers between devices, exchange(): got[k] = lax.ppermute(chunks[k], self.axes, pairs)  18.3 us
    ppermute x19, waiting for transfers between devices, exchange(): got[k] = lax.ppermute(chunks[k], self.axes, pairs)  14 us
    pallas_call x4, Pallas kernels, attend(): call(functools.partial(attend_kernel, plan, rep_count, len(pairs), packed...  5.17 us
    ppermute x4, starting transfers between devices, forward(): lax.ppermute(array, 'seq', [(i, (i + 1) % seq_count) for i in range(seq_c...  4.37 us
    ppermute x4, waiting for transfers between devices, forward(): lax.ppermute(array, 'seq', [(i, (i + 1) % seq_count) for i in range(seq_c...  3.44 us
    pallas_call x2, Pallas kernels, expert_call(): call(functools.partial(expert_kernel, rep_count, rep_list, expert_count,...  3.26 us
    unnamed x22, local copies, waits for them, and re-layouts  1.61 us
    pallas_call x1, Pallas kernels, local(): call(functools.partial(finish_kernel, hot_capacity, seq_count), [shape((t...  1.26 us
  transfers between devices with their start and end apart: 23, of which 10 were waited for; matrix products, arithmetic and copies ran while one was open for 1% of the time, Pallas kernels for 17%

profile of v21, /device:TPU:0, one launch (start us, length us, event | category | flops | bytes accessed | tf_op | source)
XLA Modules:
  0.0 55.3 jit_solution(5750955341173389447)
XLA Ops:
  0.6 3.0 %collective-permute-start.4 = (bf16[128,512]{1,0:T(8,128)(2,1)}, bf16[128,512]{1,0:T(8,128)(2,1)S(1)}, u32[]{:S(2)}, u32[]{:S(2)}) collective-permute-start(bf16[128,512]{1,0:T(8,128)(2,1)} %bitcast.39), channel_id=1, source_target_pairs={{0,1},{1,0},{2,3},{3,2},{4,5},{5,4},{6,7},{7,6},{8,9},{9,8},{10,11... | collective-permute-start | bytes 393224 | tf_op jit(solution)/shard_map/ppermute | solution.py:69
  3.6 1.6 %collective-permute-start = (bf16[128,512]{1,0:T(8,128)(2,1)}, bf16[128,512]{1,0:T(8,128)(2,1)S(1)}, u32[]{:S(2)}, u32[]{:S(2)}) collective-permute-start(bf16[128,512]{1,0:T(8,128)(2,1)} %bitcast.33), channel_id=1, source_target_pairs={{0,8},{8,16},{16,24},{24,0},{1,9},{9,17},{17,25},{25,1},{2,10},{10... | collective-permute-start | bytes 393224 | tf_op jit(solution)/shard_map/ppermute | solution.py:523
  5.2 1.6 %collective-permute-start.1 = (bf16[128,512]{1,0:T(8,128)(2,1)}, bf16[128,512]{1,0:T(8,128)(2,1)S(1)}, u32[]{:S(2)}, u32[]{:S(2)}) collective-permute-start(bf16[128,512]{1,0:T(8,128)(2,1)} %bitcast.36), channel_id=1, source_target_pairs={{0,8},{8,16},{16,24},{24,0},{1,9},{9,17},{17,25},{25,1},{2,10},{10... | collective-permute-start | bytes 393224 | tf_op jit(solution)/shard_map/ppermute | solution.py:523
  6.9 0.6 %copy-done.8 = bf16[512,4]{0,1:T(4,128)(2,1)S(1)} copy-done((bf16[512,4]{0,1:T(4,128)(2,1)S(1)}, bf16[512,4]{0,1:T(4,128)(2,1)}, u32[]{:S(2)}) %copy-start.8) | copy-done | bytes 4120
  7.5 0.9 %copy-done.3 = bf16[1,128,512]{2,1,0:T(8,128)(2,1)S(1)} copy-done((bf16[1,128,512]{2,1,0:T(8,128)(2,1)S(1)}, bf16[1,128,512]{2,1,0:T(8,128)(2,1)}, u32[]{:S(2)}) %copy-start.3) | copy-done | bytes 131096
  8.4 0.6 %shard_map.138 = (bf16[160,512]{1,0:T(8,128)(2,1)S(1)}, s32[2,128]{1,0:T(2,128)S(1)}) custom-call(s32[2]{0:T(128)S(1)} %pad_add_fusion.1.ranks_ref, s32[1,8]{1,0:T(1,128)S(1)} %copy-done.9, s32[1,128]{1,0:T(1,128)S(1)} %bitcast.44, bf16[4,512]{1,0:T(4,128)(2,1)S(1)} %bitcast.43, bf16[128,512]{1,0:T(8,128)(2,1)S(1)} %bitcast.32), custom_call_target="tpu_custom_call" | custom-call | flops 500000000 | tf_op jit(solution)/shard_map/pallas_call | solution.py:545
  9.0 0.6 %collective-permute-start.5 = (bf16[160,512]{1,0:T(8,128)(2,1)S(1)}, bf16[160,512]{1,0:T(8,128)(2,1)S(1)}, u32[]{:S(2)}, u32[]{:S(2)}) collective-permute-start(bf16[160,512]{1,0:T(8,128)(2,1)S(1)} %get-tuple-element.52.refs_0_.extended_ref), channel_id=1, source_target_pairs={{0,1},{1,0},{2,3},{3,2},{4,5},{5,4},{6,7},{7,6},{8,9},{9,8},{10,11... | collective-permute-start | bytes 491528 | tf_op jit(solution)/shard_map/ppermute | solution.py:69
  9.8 1.7 %shard_map.139 = (f32[16,128]{1,0:T(8,128)S(1)}, f32[16,128]{1,0:T(8,128)S(1)}, f32[512,128]{1,0:T(8,128)S(1)}) custom-call(s32[3]{0:T(128)S(1)} %pad_add_fusion.4.ids_ref, s32[2,128]{1,0:T(2,128)S(1)} %get-tuple-element.53.begin_ref, bf16[128,512]{1,0:T(8,128)(2,1)S(1)} %bitcast.40, bf16[128,512]{1,0:T(8,128)(2,1)S(1)} %bitcast.34, ...), custom_call_target="tpu_custom_call" | custom-call | flops 2000000000 | tf_op jit(solution)/shard_map/pallas_call | solution.py:562
  12.1 1.2 %collective-permute-start.2 = (bf16[128,512]{1,0:T(8,128)(2,1)S(1)}, bf16[128,512]{1,0:T(8,128)(2,1)S(1)}, u32[]{:S(2)}, u32[]{:S(2)}) collective-permute-start(bf16[128,512]{1,0:T(8,128)(2,1)S(1)} %collective-permute-done.refs_1_.refs_3_), channel_id=1, source_target_pairs={{0,8},{8,16},{16,24},{24,0},{1,9},{9,17},{17,25},{25,1},{2,10},{10... | collective-permute-start | bytes 393224 | tf_op jit(solution)/shard_map/ppermute | solution.py:523
  13.5 1.9 %shard_map.141 = (f32[16,128]{1,0:T(8,128)S(1)}, f32[16,128]{1,0:T(8,128)S(1)}, f32[512,128]{1,0:T(8,128)S(1)}) custom-call(s32[4]{0:T(128)S(1)} %pad_add_fusion.7.ids_ref, s32[2,128]{1,0:T(2,128)S(1)} %get-tuple-element.53.begin_ref, bf16[128,512]{1,0:T(8,128)(2,1)S(1)} %collective-permute-done.4.refs_0_, bf16[128,512]{1,0:T(8,128)(2,1)S(1)} %bitcast.35, ...), custom_call_target="tpu_custom_call" | custom-call | flops 3000000000 | tf_op jit(solution)/shard_map/pallas_call | solution.py:562
  16.0 1.6 %collective-permute-start.11 = (bf16[128,512]{1,0:T(8,128)(2,1)S(1)}, bf16[128,512]{1,0:T(8,128)(2,1)S(1)}, u32[]{:S(2)}, u32[]{:S(2)}) collective-permute-start(bf16[128,512]{1,0:T(8,128)(2,1)S(1)} %get-tuple-element.75), channel_id=1, source_target_pairs={{0,4},{2,6},{4,0},{6,2},{1,5},{3,7},{5,1},{7,3},{8,12},{10,14},{12... | collective-permute-start | bytes 393224 | tf_op jit(solution)/shard_map/ppermute | solution.py:69
  17.9 2.9 %collective-permute-done.3.refs_4_.refs_3_ = bf16[128,512]{1,0:T(8,128)(2,1)S(1)} collective-permute-done((bf16[128,512]{1,0:T(8,128)(2,1)S(1)}, bf16[128,512]{1,0:T(8,128)(2,1)S(1)}, u32[]{:S(2)}, u32[]{:S(2)}) %collective-permute-start.3) | collective-permute-done | bytes 131104 | tf_op jit(solution)/shard_map/ppermute | solution.py:523
  20.8 0.8 %shard_map.143 = bf16[592,128]{1,0:T(8,128)(2,1)S(1)} custom-call(s32[3]{0:T(128)S(1)} %pad_add_fusion.6.ids_ref, s32[2,128]{1,0:T(2,128)S(1)} %get-tuple-element.53.begin_ref, bf16[128,512]{1,0:T(8,128)(2,1)S(1)} %collective-permute-done.4.refs_0_, bf16[128,512]{1,0:T(8,128)(2,1)S(1)} %get-tuple-element.66.refs_1_.refs_4_, ...), custom_call_target="tpu_custom_call" | custom-call | flops 1500000000 | tf_op jit(solution)/shard_map/pallas_call | solution.py:562
  21.6 1.2 %collective-permute-start.6 = (bf16[592,128]{1,0:T(8,128)(2,1)S(1)}, bf16[592,128]{1,0:T(8,128)(2,1)S(1)}, u32[]{:S(2)}, u32[]{:S(2)}) collective-permute-start(bf16[592,128]{1,0:T(8,128)(2,1)S(1)} %shard_map.143), channel_id=1, source_target_pairs={{0,1},{1,0},{2,3},{3,2},{4,5},{5,4},{6,7},{7,6},{8,9},{9,8},{10,11... | collective-permute-start | bytes 454664 | tf_op jit(solution)/shard_map/ppermute | solution.py:69
  22.8 0.8 %shard_map.140 = (f32[16,128]{1,0:T(8,128)S(1)}, f32[16,128]{1,0:T(8,128)S(1)}, f32[512,128]{1,0:T(8,128)S(1)}) custom-call(s32[4]{0:T(128)S(1)} %pad_add_fusion.2.ids_ref, s32[2,128]{1,0:T(2,128)S(1)} %get-tuple-element.53.begin_ref, bf16[128,512]{1,0:T(8,128)(2,1)S(1)} %bitcast.41, bf16[128,512]{1,0:T(8,128)(2,1)S(1)} %collective-permute-done.refs_1_.refs_3_, ...), custom_call_target="tpu_custom_call" | custom-call | flops 2500000000 | tf_op jit(solution)/shard_map/pallas_call | solution.py:562
  23.5 3.3 %collective-permute-done.6.refs_3_ = bf16[592,128]{1,0:T(8,128)(2,1)S(1)} collective-permute-done((bf16[592,128]{1,0:T(8,128)(2,1)S(1)}, bf16[592,128]{1,0:T(8,128)(2,1)S(1)}, u32[]{:S(2)}, u32[]{:S(2)}) %collective-permute-start.6) | collective-permute-done | bytes 151584 | tf_op jit(solution)/shard_map/ppermute | solution.py:69
  26.8 0.6 %shard_map.144 = (bf16[128,512]{1,0:T(8,128)(2,1)S(1)}, bf16[64,512]{1,0:T(8,128)(2,1)S(1)}, bf16[64,512]{1,0:T(8,128)(2,1)S(1)}, bf16[64,512]{1,0:T(8,128)(2,1)S(1)}, bf16[64,512]{1,0:T(8,128)(2,1)S(1)}) custom-call(s32[1]{0:T(128)} %bitcast.own_ref, bf16[160,512]{1,0:T(8,128)(2,1)S(1)} %get-tuple-element.52.refs_0_.extended_ref, ...), custom_call_target="tpu_custom_call" | custom-call | flops 2000000000 | tf_op jit(solution)/shard_map/pallas_call | solution.py:616
  27.5 1.2 %collective-permute-start.13 = (bf16[64,512]{1,0:T(8,128)(2,1)S(1)}, bf16[64,512]{1,0:T(8,128)(2,1)S(1)}, u32[]{:S(2)}, u32[]{:S(2)}) collective-permute-start(bf16[64,512]{1,0:T(8,128)(2,1)S(1)} %get-tuple-element.70.refs_0_), channel_id=1, source_target_pairs={{0,1},{1,0},{2,3},{3,2},{4,5},{5,4},{6,7},{7,6},{8,9},{9,8},{10,11... | collective-permute-start | bytes 196616 | tf_op jit(solution)/shard_map/ppermute | solution.py:69
  28.7 1.9 %collective-permute-start.15 = (bf16[64,512]{1,0:T(8,128)(2,1)S(1)}, bf16[64,512]{1,0:T(8,128)(2,1)S(1)}, u32[]{:S(2)}, u32[]{:S(2)}) collective-permute-start(bf16[64,512]{1,0:T(8,128)(2,1)S(1)} %get-tuple-element.72), channel_id=1, source_target_pairs={{0,5},{1,4},{2,7},{3,6},{4,1},{5,0},{6,3},{7,2},{8,13},{9,12},{10,... | collective-permute-start | bytes 196616 | tf_op jit(solution)/shard_map/ppermute | solution.py:69
  30.5 1.4 %collective-permute-start.14 = (bf16[64,512]{1,0:T(8,128)(2,1)S(1)}, bf16[64,512]{1,0:T(8,128)(2,1)S(1)}, u32[]{:S(2)}, u32[]{:S(2)}) collective-permute-start(bf16[64,512]{1,0:T(8,128)(2,1)S(1)} %get-tuple-element.73), channel_id=1, source_target_pairs={{0,3},{1,2},{2,1},{3,0},{4,7},{5,6},{6,5},{7,4},{8,11},{9,10},{10,... | collective-permute-start | bytes 196616 | tf_op jit(solution)/shard_map/ppermute | solution.py:69
  32.0 0.6 %collective-permute-start.7 = (bf16[64,512]{1,0:T(8,128)(2,1)S(1)}, bf16[64,512]{1,0:T(8,128)(2,1)S(1)}, u32[]{:S(2)}, u32[]{:S(2)}) collective-permute-start(bf16[64,512]{1,0:T(8,128)(2,1)S(1)} %get-tuple-element.71), channel_id=1, source_target_pairs={{0,6},{1,7},{2,4},{3,5},{4,2},{5,3},{6,0},{7,1},{8,14},{9,15},{10,... | collective-permute-start | bytes 196616 | tf_op jit(solution)/shard_map/ppermute | solution.py:69
  32.6 1.0 %collective-permute-start.8 = (bf16[64,512]{1,0:T(8,128)(2,1)S(1)}, bf16[64,512]{1,0:T(8,128)(2,1)S(1)}, u32[]{:S(2)}, u32[]{:S(2)}) collective-permute-start(bf16[64,512]{1,0:T(8,128)(2,1)S(1)} %get-tuple-element.72), channel_id=1, source_target_pairs={{0,4},{1,5},{2,6},{3,7},{4,0},{5,1},{6,2},{7,3},{8,12},{9,13},{10,... | collective-permute-start | bytes 196616 | tf_op jit(solution)/shard_map/ppermute | solution.py:69
  34.0 1.6 %collective-permute-done.15.refs_2_ = bf16[64,512]{1,0:T(8,128)(2,1)S(1)} collective-permute-done((bf16[64,512]{1,0:T(8,128)(2,1)S(1)}, bf16[64,512]{1,0:T(8,128)(2,1)S(1)}, u32[]{:S(2)}, u32[]{:S(2)}) %collective-permute-start.15) | collective-permute-done | bytes 65568 | tf_op jit(solution)/shard_map/ppermute | solution.py:69
  36.1 1.6 %shard_map.145 = (f32[256,512]{1,0:T(8,128)S(1)}, f32[256,512]{1,0:T(8,128)S(1)}) custom-call(s32[1]{0:T(128)} %bitcast.own_ref, s32[4]{0:T(128)S(1)} %pad_add_fusion.part_ref, bf16[512,512]{1,0:T(8,128)(2,1)S(1)} %bitcast.26, bf16[512,512]{1,0:T(8,128)(2,1)S(1)} %bitcast.29, bf16[160,512]{1,0:T(8,128)(2,1)S(1)} %get-tuple-element.52.refs_0_.extended_ref, ...), custom_call_target="tpu_custom_call" | custom-call | flops 2000000000 | tf_op jit(solution)/shard_map/pallas_call | solution.py:629
  37.8 0.6 %collective-permute-done.8.refs_2_ = bf16[64,512]{1,0:T(8,128)(2,1)S(1)} collective-permute-done((bf16[64,512]{1,0:T(8,128)(2,1)S(1)}, bf16[64,512]{1,0:T(8,128)(2,1)S(1)}, u32[]{:S(2)}, u32[]{:S(2)}) %collective-permute-start.8) | collective-permute-done | bytes 65568 | tf_op jit(solution)/shard_map/ppermute | solution.py:69
  38.4 1.6 %shard_map.146 = (bf16[256,512]{1,0:T(8,128)(2,1)S(1)}, bf16[256,512]{1,0:T(8,128)(2,1)S(1)}, bf16[2,64,512]{2,1,0:T(8,128)(2,1)S(1)}, bf16[2,64,512]{2,1,0:T(8,...) custom-call(s32[1]{0:T(128)} %bitcast.own_ref, s32[4]{0:T(128)S(1)} %pad_add_fusion.part_ref, ...), custom_call_target="tpu_custom_call" | custom-call | flops 2000000000 | tf_op jit(solution)/shard_map/pallas_call | solution.py:629
  40.0 2.0 %collective-permute-start.17 = (bf16[2,64,512]{2,1,0:T(8,128)(2,1)S(1)}, bf16[2,64,512]{2,1,0:T(8,128)(2,1)S(1)}, u32[]{:S(2)}, u32[]{:S(2)}) collective-permute-start(bf16[2,64,512]{2,1,0:T(8,128)(2,1)S(1)} %get-tuple-element.87), channel_id=1, source_target_pairs={{0,24},{8,16},{16,8},{24,0},{1,25},{9,17},{17,9},{25,1},{2,26},{10... | collective-permute-start | bytes 393224 | tf_op jit(solution)/shard_map/ppermute | solution.py:69
  42.2 2.3 %collective-permute-start.19 = (bf16[2,64,512]{2,1,0:T(8,128)(2,1)S(1)}, bf16[2,64,512]{2,1,0:T(8,128)(2,1)S(1)}, u32[]{:S(2)}, u32[]{:S(2)}) collective-permute-start(bf16[2,64,512]{2,1,0:T(8,128)(2,1)S(1)} %get-tuple-element.89), channel_id=1, source_target_pairs={{0,8},{8,0},{16,24},{24,16},{1,9},{9,1},{17,25},{25,17},{2,10},{10... | collective-permute-start | bytes 393224 | tf_op jit(solution)/shard_map/ppermute | solution.py:69
  45.0 0.9 %collective-permute-start.21 = (bf16[128,512]{1,0:T(8,128)(2,1)S(1)}, bf16[128,512]{1,0:T(8,128)(2,1)S(1)}, u32[]{:S(2)}, u32[]{:S(2)}) collective-permute-start(bf16[128,512]{1,0:T(8,128)(2,1)S(1)} %get-tuple-element.93), channel_id=1, source_target_pairs={{0,4},{2,6},{4,0},{6,2},{1,5},{3,7},{5,1},{7,3},{8,12},{10,14},{12... | collective-permute-start | bytes 393224 | tf_op jit(solution)/shard_map/ppermute | solution.py:69
  45.9 2.5 %collective-permute-done.17.refs_1_ = bf16[2,64,512]{2,1,0:T(8,128)(2,1)S(1)} collective-permute-done((bf16[2,64,512]{2,1,0:T(8,128)(2,1)S(1)}, bf16[2,64,512]{2,1,0:T(8,128)(2,1)S(1)}, u32[]{:S(2)}, u32[]{:S(2)}) %collective-permute-start.17) | collective-permute-done | bytes 131104 | tf_op jit(solution)/shard_map/ppermute | solution.py:69
  48.8 5.2 %collective-permute-done.18.refs_2_ = bf16[2,64,512]{2,1,0:T(8,128)(2,1)S(1)} collective-permute-done((bf16[2,64,512]{2,1,0:T(8,128)(2,1)S(1)}, bf16[2,64,512]{2,1,0:T(8,128)(2,1)S(1)}, u32[]{:S(2)}, u32[]{:S(2)}) %collective-permute-start.18) | collective-permute-done | bytes 131104 | tf_op jit(solution)/shard_map/ppermute | solution.py:69
  54.1 1.3 %shard_map.149 = (bf16[128,512]{1,0:T(8,128)(2,1)}, bf16[128,512]{1,0:T(8,128)(2,1)}, f32[64,512]{1,0:T(8,128)}, f32[64,512]{1,0:T(8,128)}) custom-call(bf16[128,256]{1,0:T(8,128)(2,1)S(1)} %get-tuple-element.83.placed_ref, f32[128,128]{1,0:T(8,128)S(1)} %get-tuple-element.84.factors_ref, f32[128,512]{1,0:T(8,128)S(1)} %get-tuple-element.85.router_cols_ref, ...), custom_call_target="tpu_custom_call" | custom-call | flops 1000000000 | tf_op jit(solution)/shard_map/pallas_call | solution.py:682
  (54 shorter events, 4.1 us)
Async XLA Ops:
  0.6 12.8 %collective-permute-start.4 = (bf16[128,512]{1,0:T(8,128)(2,1)}, bf16[128,512]{1,0:T(8,128)(2,1)S(1)}, u32[]{:S(2)}, u32[]{:S(2)}) collective-permute-start(bf16[128,512]{1,0:T(8,128)(2,1)} %bitcast.39), channel_id=1, source_target_pairs={{0,1},{1,0},{2,3},{3,2},{4,5},{5,4},{6,7},{7,6},{8,9},{9,8},{10,11... | collective-permute-start | bytes 393224 | tf_op jit(solution)/shard_map/ppermute | solution.py:69
  3.6 8.4 %collective-permute-start = (bf16[128,512]{1,0:T(8,128)(2,1)}, bf16[128,512]{1,0:T(8,128)(2,1)S(1)}, u32[]{:S(2)}, u32[]{:S(2)}) collective-permute-start(bf16[128,512]{1,0:T(8,128)(2,1)} %bitcast.33), channel_id=1, source_target_pairs={{0,8},{8,16},{16,24},{24,0},{1,9},{9,17},{17,25},{25,1},{2,10},{10... | collective-permute-start | bytes 393224 | tf_op jit(solution)/shard_map/ppermute | solution.py:523
  5.2 8.3 %collective-permute-start.1 = (bf16[128,512]{1,0:T(8,128)(2,1)}, bf16[128,512]{1,0:T(8,128)(2,1)S(1)}, u32[]{:S(2)}, u32[]{:S(2)}) collective-permute-start(bf16[128,512]{1,0:T(8,128)(2,1)} %bitcast.36), channel_id=1, source_target_pairs={{0,8},{8,16},{16,24},{24,0},{1,9},{9,17},{17,25},{25,1},{2,10},{10... | collective-permute-start | bytes 393224 | tf_op jit(solution)/shard_map/ppermute | solution.py:523
  6.8 0.7 %copy-start.8 = (bf16[512,4]{0,1:T(4,128)(2,1)S(1)}, bf16[512,4]{0,1:T(4,128)(2,1)}, u32[]{:S(2)}) copy-start(bf16[512,4]{0,1:T(4,128)(2,1)} %param.17) | copy-start | bytes 12292
  7.5 0.9 %copy-start.3 = (bf16[1,128,512]{2,1,0:T(8,128)(2,1)S(1)}, bf16[1,128,512]{2,1,0:T(8,128)(2,1)}, u32[]{:S(2)}) copy-start(bf16[1,128,512]{2,1,0:T(8,128)(2,1)} %param.21) | copy-start | bytes 393220
  8.4 1.3 %copy-start.4 = (bf16[1,128,512]{2,1,0:T(8,128)(2,1)S(1)}, bf16[1,128,512]{2,1,0:T(8,128)(2,1)}, u32[]{:S(2)}) copy-start(bf16[1,128,512]{2,1,0:T(8,128)(2,1)} %param.12) | copy-start | bytes 393220
  8.4 1.3 %copy-start.5 = (bf16[1,128,512]{2,1,0:T(8,128)(2,1)S(1)}, bf16[1,128,512]{2,1,0:T(8,128)(2,1)}, u32[]{:S(2)}) copy-start(bf16[1,128,512]{2,1,0:T(8,128)(2,1)} %param.13) | copy-start | bytes 393220
  8.4 1.3 %copy-start.6 = (bf16[1,128,512]{2,1,0:T(8,128)(2,1)S(1)}, bf16[1,128,512]{2,1,0:T(8,128)(2,1)}, u32[]{:S(2)}) copy-start(bf16[1,128,512]{2,1,0:T(8,128)(2,1)} %param.11) | copy-start | bytes 393220
  9.0 6.4 %collective-permute-start.5 = (bf16[160,512]{1,0:T(8,128)(2,1)S(1)}, bf16[160,512]{1,0:T(8,128)(2,1)S(1)}, u32[]{:S(2)}, u32[]{:S(2)}) collective-permute-start(bf16[160,512]{1,0:T(8,128)(2,1)S(1)} %get-tuple-element.52.refs_0_.extended_ref), channel_id=1, source_target_pairs={{0,1},{1,0},{2,3},{3,2},{4,5},{5,4},{6,7},{7,6},{8,9},{9,8},{10,11... | collective-permute-start | bytes 491528 | tf_op jit(solution)/shard_map/ppermute | solution.py:69
  12.1 8.7 %collective-permute-start.2 = (bf16[128,512]{1,0:T(8,128)(2,1)S(1)}, bf16[128,512]{1,0:T(8,128)(2,1)S(1)}, u32[]{:S(2)}, u32[]{:S(2)}) collective-permute-start(bf16[128,512]{1,0:T(8,128)(2,1)S(1)} %collective-permute-done.refs_1_.refs_3_), channel_id=1, source_target_pairs={{0,8},{8,16},{16,24},{24,0},{1,9},{9,17},{17,25},{25,1},{2,10},{10... | collective-permute-start | bytes 393224 | tf_op jit(solution)/shard_map/ppermute | solution.py:523
  13.5 7.3 %collective-permute-start.3 = (bf16[128,512]{1,0:T(8,128)(2,1)S(1)}, bf16[128,512]{1,0:T(8,128)(2,1)S(1)}, u32[]{:S(2)}, u32[]{:S(2)}) collective-permute-start(bf16[128,512]{1,0:T(8,128)(2,1)S(1)} %collective-permute-done.1.refs_2_.refs_4_), channel_id=1, source_target_pairs={{0,8},{8,16},{16,24},{24,0},{1,9},{9,17},{17,25},{25,1},{2,10},{10... | collective-permute-start | bytes 393224 | tf_op jit(solution)/shard_map/ppermute | solution.py:523
  16.0 12.7 %collective-permute-start.10 = (bf16[128,512]{1,0:T(8,128)(2,1)S(1)}, bf16[128,512]{1,0:T(8,128)(2,1)S(1)}, u32[]{:S(2)}, u32[]{:S(2)}) collective-permute-start(bf16[128,512]{1,0:T(8,128)(2,1)S(1)} %get-tuple-element.74), channel_id=1, source_target_pairs={{0,2},{2,0},{4,6},{6,4},{1,3},{3,1},{5,7},{7,5},{8,10},{10,8},{12,... | collective-permute-start | bytes 393224 | tf_op jit(solution)/shard_map/ppermute | solution.py:69
  16.0 14.5 %collective-permute-start.11 = (bf16[128,512]{1,0:T(8,128)(2,1)S(1)}, bf16[128,512]{1,0:T(8,128)(2,1)S(1)}, u32[]{:S(2)}, u32[]{:S(2)}) collective-permute-start(bf16[128,512]{1,0:T(8,128)(2,1)S(1)} %get-tuple-element.75), channel_id=1, source_target_pairs={{0,4},{2,6},{4,0},{6,2},{1,5},{3,7},{5,1},{7,3},{8,12},{10,14},{12... | collective-permute-start | bytes 393224 | tf_op jit(solution)/shard_map/ppermute | solution.py:69
  17.7 14.3 %collective-permute-start.12 = (bf16[128,512]{1,0:T(8,128)(2,1)S(1)}, bf16[128,512]{1,0:T(8,128)(2,1)S(1)}, u32[]{:S(2)}, u32[]{:S(2)}) collective-permute-start(bf16[128,512]{1,0:T(8,128)(2,1)S(1)} %get-tuple-element.76), channel_id=1, source_target_pairs={{0,6},{2,4},{4,2},{6,0},{1,7},{3,5},{5,3},{7,1},{8,14},{10,12},{12... | collective-permute-start | bytes 393224 | tf_op jit(solution)/shard_map/ppermute | solution.py:69
  21.6 5.3 %copy-start = (bf16[512,512]{1,0:T(8,128)(2,1)S(1)}, bf16[512,512]{1,0:T(8,128)(2,1)}, u32[]{:S(2)}) copy-start(bf16[512,512]{1,0:T(8,128)(2,1)} %proj_ref.1) | copy-start | bytes 1572868
  21.6 5.3 %copy-start.7 = (bf16[1,128,512]{2,1,0:T(8,128)(2,1)S(1)}, bf16[1,128,512]{2,1,0:T(8,128)(2,1)}, u32[]{:S(2)}) copy-start(bf16[1,128,512]{2,1,0:T(8,128)(2,1)} %param.15) | copy-start | bytes 393220
  21.6 5.3 %collective-permute-start.6 = (bf16[592,128]{1,0:T(8,128)(2,1)S(1)}, bf16[592,128]{1,0:T(8,128)(2,1)S(1)}, u32[]{:S(2)}, u32[]{:S(2)}) collective-permute-start(bf16[592,128]{1,0:T(8,128)(2,1)S(1)} %shard_map.143), channel_id=1, source_target_pairs={{0,1},{1,0},{2,3},{3,2},{4,5},{5,4},{6,7},{7,6},{8,9},{9,8},{10,11... | collective-permute-start | bytes 454664 | tf_op jit(solution)/shard_map/ppermute | solution.py:69
  26.8 9.3 %copy-start.1 = (bf16[1,512,512]{2,1,0:T(8,128)(2,1)S(1)}, bf16[1,512,512]{2,1,0:T(8,128)(2,1)}, u32[]{:S(2)}) copy-start(bf16[1,512,512]{2,1,0:T(8,128)(2,1)} %param.19) | copy-start | bytes 1572868
  26.8 9.3 %copy-start.2 = (bf16[1,512,512]{2,1,0:T(8,128)(2,1)S(1)}, bf16[1,512,512]{2,1,0:T(8,128)(2,1)}, u32[]{:S(2)}) copy-start(bf16[1,512,512]{2,1,0:T(8,128)(2,1)} %param.20) | copy-start | bytes 1572868
  27.5 5.2 %collective-permute-start.13 = (bf16[64,512]{1,0:T(8,128)(2,1)S(1)}, bf16[64,512]{1,0:T(8,128)(2,1)S(1)}, u32[]{:S(2)}, u32[]{:S(2)}) collective-permute-start(bf16[64,512]{1,0:T(8,128)(2,1)S(1)} %get-tuple-element.70.refs_0_), channel_id=1, source_target_pairs={{0,1},{1,0},{2,3},{3,2},{4,5},{5,4},{6,7},{7,6},{8,9},{9,8},{10,11... | collective-permute-start | bytes 196616 | tf_op jit(solution)/shard_map/ppermute | solution.py:69
  28.7 5.2 %collective-permute-start.16 = (bf16[64,512]{1,0:T(8,128)(2,1)S(1)}, bf16[64,512]{1,0:T(8,128)(2,1)S(1)}, u32[]{:S(2)}, u32[]{:S(2)}) collective-permute-start(bf16[64,512]{1,0:T(8,128)(2,1)S(1)} %get-tuple-element.71), channel_id=1, source_target_pairs={{0,7},{1,6},{2,5},{3,4},{4,3},{5,2},{6,1},{7,0},{8,15},{9,14},{10,... | collective-permute-start | bytes 196616 | tf_op jit(solution)/shard_map/ppermute | solution.py:69
  28.7 6.9 %collective-permute-start.15 = (bf16[64,512]{1,0:T(8,128)(2,1)S(1)}, bf16[64,512]{1,0:T(8,128)(2,1)S(1)}, u32[]{:S(2)}, u32[]{:S(2)}) collective-permute-start(bf16[64,512]{1,0:T(8,128)(2,1)S(1)} %get-tuple-element.72), channel_id=1, source_target_pairs={{0,5},{1,4},{2,7},{3,6},{4,1},{5,0},{6,3},{7,2},{8,13},{9,12},{10,... | collective-permute-start | bytes 196616 | tf_op jit(solution)/shard_map/ppermute | solution.py:69
  30.5 5.6 %collective-permute-start.14 = (bf16[64,512]{1,0:T(8,128)(2,1)S(1)}, bf16[64,512]{1,0:T(8,128)(2,1)S(1)}, u32[]{:S(2)}, u32[]{:S(2)}) collective-permute-start(bf16[64,512]{1,0:T(8,128)(2,1)S(1)} %get-tuple-element.73), channel_id=1, source_target_pairs={{0,3},{1,2},{2,1},{3,0},{4,7},{5,6},{6,5},{7,4},{8,11},{9,10},{10,... | collective-permute-start | bytes 196616 | tf_op jit(solution)/shard_map/ppermute | solution.py:69
  32.0 5.7 %collective-permute-start.7 = (bf16[64,512]{1,0:T(8,128)(2,1)S(1)}, bf16[64,512]{1,0:T(8,128)(2,1)S(1)}, u32[]{:S(2)}, u32[]{:S(2)}) collective-permute-start(bf16[64,512]{1,0:T(8,128)(2,1)S(1)} %get-tuple-element.71), channel_id=1, source_target_pairs={{0,6},{1,7},{2,4},{3,5},{4,2},{5,3},{6,0},{7,1},{8,14},{9,15},{10,... | collective-permute-start | bytes 196616 | tf_op jit(solution)/shard_map/ppermute | solution.py:69
  32.6 5.7 %collective-permute-start.8 = (bf16[64,512]{1,0:T(8,128)(2,1)S(1)}, bf16[64,512]{1,0:T(8,128)(2,1)S(1)}, u32[]{:S(2)}, u32[]{:S(2)}) collective-permute-start(bf16[64,512]{1,0:T(8,128)(2,1)S(1)} %get-tuple-element.72), channel_id=1, source_target_pairs={{0,4},{1,5},{2,6},{3,7},{4,0},{5,1},{6,2},{7,3},{8,12},{9,13},{10,... | collective-permute-start | bytes 196616 | tf_op jit(solution)/shard_map/ppermute | solution.py:69
  33.9 4.5 %collective-permute-start.9 = (bf16[64,512]{1,0:T(8,128)(2,1)S(1)}, bf16[64,512]{1,0:T(8,128)(2,1)S(1)}, u32[]{:S(2)}, u32[]{:S(2)}) collective-permute-start(bf16[64,512]{1,0:T(8,128)(2,1)S(1)} %get-tuple-element.73), channel_id=1, source_target_pairs={{0,2},{1,3},{2,0},{3,1},{4,6},{5,7},{6,4},{7,5},{8,10},{9,11},{10,... | collective-permute-start | bytes 196616 | tf_op jit(solution)/shard_map/ppermute | solution.py:69
  40.0 8.3 %collective-permute-start.17 = (bf16[2,64,512]{2,1,0:T(8,128)(2,1)S(1)}, bf16[2,64,512]{2,1,0:T(8,128)(2,1)S(1)}, u32[]{:S(2)}, u32[]{:S(2)}) collective-permute-start(bf16[2,64,512]{2,1,0:T(8,128)(2,1)S(1)} %get-tuple-element.87), channel_id=1, source_target_pairs={{0,24},{8,16},{16,8},{24,0},{1,25},{9,17},{17,9},{25,1},{2,26},{10... | collective-permute-start | bytes 393224 | tf_op jit(solution)/shard_map/ppermute | solution.py:69
  42.0 12.0 %collective-permute-start.18 = (bf16[2,64,512]{2,1,0:T(8,128)(2,1)S(1)}, bf16[2,64,512]{2,1,0:T(8,128)(2,1)S(1)}, u32[]{:S(2)}, u32[]{:S(2)}) collective-permute-start(bf16[2,64,512]{2,1,0:T(8,128)(2,1)S(1)} %get-tuple-element.88), channel_id=1, source_target_pairs={{0,16},{8,24},{16,0},{24,8},{1,17},{9,25},{17,1},{25,9},{2,18},{10... | collective-permute-start | bytes 393224 | tf_op jit(solution)/shard_map/ppermute | solution.py:69
  42.2 11.9 %collective-permute-start.19 = (bf16[2,64,512]{2,1,0:T(8,128)(2,1)S(1)}, bf16[2,64,512]{2,1,0:T(8,128)(2,1)S(1)}, u32[]{:S(2)}, u32[]{:S(2)}) collective-permute-start(bf16[2,64,512]{2,1,0:T(8,128)(2,1)S(1)} %get-tuple-element.89), channel_id=1, source_target_pairs={{0,8},{8,0},{16,24},{24,16},{1,9},{9,1},{17,25},{25,17},{2,10},{10... | collective-permute-start | bytes 393224 | tf_op jit(solution)/shard_map/ppermute | solution.py:69
  44.9 9.2 %collective-permute-start.20 = (bf16[128,512]{1,0:T(8,128)(2,1)S(1)}, bf16[128,512]{1,0:T(8,128)(2,1)S(1)}, u32[]{:S(2)}, u32[]{:S(2)}) collective-permute-start(bf16[128,512]{1,0:T(8,128)(2,1)S(1)} %get-tuple-element.92), channel_id=1, source_target_pairs={{0,6},{2,4},{4,2},{6,0},{1,7},{3,5},{5,3},{7,1},{8,14},{10,12},{12... | collective-permute-start | bytes 393224 | tf_op jit(solution)/shard_map/ppermute | solution.py:69
  45.0 9.1 %collective-permute-start.21 = (bf16[128,512]{1,0:T(8,128)(2,1)S(1)}, bf16[128,512]{1,0:T(8,128)(2,1)S(1)}, u32[]{:S(2)}, u32[]{:S(2)}) collective-permute-start(bf16[128,512]{1,0:T(8,128)(2,1)S(1)} %get-tuple-element.93), channel_id=1, source_target_pairs={{0,4},{2,6},{4,0},{6,2},{1,5},{3,7},{5,1},{7,3},{8,12},{10,14},{12... | collective-permute-start | bytes 393224 | tf_op jit(solution)/shard_map/ppermute | solution.py:69
  48.4 5.7 %collective-permute-start.22 = (bf16[128,512]{1,0:T(8,128)(2,1)S(1)}, bf16[128,512]{1,0:T(8,128)(2,1)S(1)}, u32[]{:S(2)}, u32[]{:S(2)}) collective-permute-start(bf16[128,512]{1,0:T(8,128)(2,1)S(1)} %get-tuple-element.94), channel_id=1, source_target_pairs={{0,2},{2,0},{4,6},{6,4},{1,3},{3,1},{5,7},{7,5},{8,10},{10,8},{12,... | collective-permute-start | bytes 393224 | tf_op jit(solution)/shard_map/ppermute | solution.py:69
  (2 other events, 1.3 us)

commit v22 on v21

--- a/solution.py
+++ b/solution.py
@@ -609,7 +609,7 @@
         queries,
         own_state,
         False,
-        2.5,
+        1.5,
     )
     got_grads = merged(experts.exchange(sent_grads), MOST_PERMUTES)
 

time: 55.5 us -> 54.5 us (0.982)
  waiting for transfers between devices: 17.5 us -> 16.5 us
    ppermute x19, waiting for transfers between devices: 14 us -> 11 us  [exchange(): got[k] = lax.ppermute(chunks[k], self.axes, pairs)]
    ppermute x4, waiting for transfers between devices: 3.44 us -> 5.52 us  [forward(): lax.ppermute(array, 'seq', [(i, (i + 1) % seq_count) for i in range(seq_c...]
  transfers between devices with their start and end apart: 23 -> 23, of which waited for: 10 -> 10; matrix products, arithmetic and copies ran while one was open for 1% -> 1% of each run, Pallas kernels for 17% -> 16%
where the time goes in v22:
time: 54.5 us; the launch traced here: 54.3 us
  starting transfers between devices  22.6 us (41%)
  waiting for transfers between devices  16.5 us (30%)
  Pallas kernels  12.3 us (23%)
  local copies, waits for them, and re-layouts  1.6 us (3%)
  between operations  0.79 us (1%)
    ppermute x19, starting transfers between devices, exchange(): got[k] = lax.ppermute(chunks[k], self.axes, pairs)  18.3 us
    ppermute x19, waiting for transfers between devices, exchange(): got[k] = lax.ppermute(chunks[k], self.axes, pairs)  11 us
    ppermute x4, waiting for transfers between devices, forward(): lax.ppermute(array, 'seq', [(i, (i + 1) % seq_count) for i in range(seq_c...  5.52 us
    pallas_call x4, Pallas kernels, attend(): call(functools.partial(attend_kernel, plan, rep_count, len(pairs), packed...  5.18 us
    ppermute x4, starting transfers between devices, forward(): lax.ppermute(array, 'seq', [(i, (i + 1) % seq_count) for i in range(seq_c...  4.3 us
    pallas_call x2, Pallas kernels, expert_call(): call(functools.partial(expert_kernel, rep_count, rep_list, expert_count,...  3.23 us
    unnamed x22, local copies, waits for them, and re-layouts  1.6 us
    pallas_call x1, Pallas kernels, local(): call(functools.partial(finish_kernel, hot_capacity, seq_count), [shape((t...  1.26 us
  transfers between devices with their start and end apart: 23, of which 10 were waited for; matrix products, arithmetic and copies ran while one was open for 1% of the time, Pallas kernels for 16%

profile of v22, /device:TPU:0, one launch (start us, length us, event | category | flops | bytes accessed | tf_op | source)
XLA Modules:
  0.0 54.3 jit_solution(14173232052165398624)
XLA Ops:
  0.6 3.0 %collective-permute-start.4 = (bf16[128,512]{1,0:T(8,128)(2,1)}, bf16[128,512]{1,0:T(8,128)(2,1)S(1)}, u32[]{:S(2)}, u32[]{:S(2)}) collective-permute-start(bf16[128,512]{1,0:T(8,128)(2,1)} %bitcast.39), channel_id=1, source_target_pairs={{0,1},{1,0},{2,3},{3,2},{4,5},{5,4},{6,7},{7,6},{8,9},{9,8},{10,11... | collective-permute-start | bytes 393224 | tf_op jit(solution)/shard_map/ppermute | solution.py:69
  3.6 1.6 %collective-permute-start = (bf16[128,512]{1,0:T(8,128)(2,1)}, bf16[128,512]{1,0:T(8,128)(2,1)S(1)}, u32[]{:S(2)}, u32[]{:S(2)}) collective-permute-start(bf16[128,512]{1,0:T(8,128)(2,1)} %bitcast.33), channel_id=1, source_target_pairs={{0,8},{8,16},{16,24},{24,0},{1,9},{9,17},{17,25},{25,1},{2,10},{10... | collective-permute-start | bytes 393224 | tf_op jit(solution)/shard_map/ppermute | solution.py:523
  5.2 1.6 %collective-permute-start.1 = (bf16[128,512]{1,0:T(8,128)(2,1)}, bf16[128,512]{1,0:T(8,128)(2,1)S(1)}, u32[]{:S(2)}, u32[]{:S(2)}) collective-permute-start(bf16[128,512]{1,0:T(8,128)(2,1)} %bitcast.36), channel_id=1, source_target_pairs={{0,8},{8,16},{16,24},{24,0},{1,9},{9,17},{17,25},{25,1},{2,10},{10... | collective-permute-start | bytes 393224 | tf_op jit(solution)/shard_map/ppermute | solution.py:523
  6.9 0.6 %copy-done.8 = bf16[512,4]{0,1:T(4,128)(2,1)S(1)} copy-done((bf16[512,4]{0,1:T(4,128)(2,1)S(1)}, bf16[512,4]{0,1:T(4,128)(2,1)}, u32[]{:S(2)}) %copy-start.8) | copy-done | bytes 4120
  7.5 0.9 %copy-done.3 = bf16[1,128,512]{2,1,0:T(8,128)(2,1)S(1)} copy-done((bf16[1,128,512]{2,1,0:T(8,128)(2,1)S(1)}, bf16[1,128,512]{2,1,0:T(8,128)(2,1)}, u32[]{:S(2)}) %copy-start.3) | copy-done | bytes 131096
  8.4 0.6 %shard_map.138 = (bf16[160,512]{1,0:T(8,128)(2,1)S(1)}, s32[2,128]{1,0:T(2,128)S(1)}) custom-call(s32[2]{0:T(128)S(1)} %pad_add_fusion.1.ranks_ref, s32[1,8]{1,0:T(1,128)S(1)} %copy-done.9, s32[1,128]{1,0:T(1,128)S(1)} %bitcast.44, bf16[4,512]{1,0:T(4,128)(2,1)S(1)} %bitcast.43, bf16[128,512]{1,0:T(8,128)(2,1)S(1)} %bitcast.32), custom_call_target="tpu_custom_call" | custom-call | flops 500000000 | tf_op jit(solution)/shard_map/pallas_call | solution.py:545
  9.0 0.6 %collective-permute-start.5 = (bf16[160,512]{1,0:T(8,128)(2,1)S(1)}, bf16[160,512]{1,0:T(8,128)(2,1)S(1)}, u32[]{:S(2)}, u32[]{:S(2)}) collective-permute-start(bf16[160,512]{1,0:T(8,128)(2,1)S(1)} %get-tuple-element.52.refs_0_.extended_ref), channel_id=1, source_target_pairs={{0,1},{1,0},{2,3},{3,2},{4,5},{5,4},{6,7},{7,6},{8,9},{9,8},{10,11... | collective-permute-start | bytes 491528 | tf_op jit(solution)/shard_map/ppermute | solution.py:69
  9.7 1.8 %shard_map.139 = (f32[16,128]{1,0:T(8,128)S(1)}, f32[16,128]{1,0:T(8,128)S(1)}, f32[512,128]{1,0:T(8,128)S(1)}) custom-call(s32[3]{0:T(128)S(1)} %pad_add_fusion.4.ids_ref, s32[2,128]{1,0:T(2,128)S(1)} %get-tuple-element.53.begin_ref, bf16[128,512]{1,0:T(8,128)(2,1)S(1)} %bitcast.40, bf16[128,512]{1,0:T(8,128)(2,1)S(1)} %bitcast.34, ...), custom_call_target="tpu_custom_call" | custom-call | flops 2000000000 | tf_op jit(solution)/shard_map/pallas_call | solution.py:562
  12.1 1.1 %collective-permute-start.2 = (bf16[128,512]{1,0:T(8,128)(2,1)S(1)}, bf16[128,512]{1,0:T(8,128)(2,1)S(1)}, u32[]{:S(2)}, u32[]{:S(2)}) collective-permute-start(bf16[128,512]{1,0:T(8,128)(2,1)S(1)} %collective-permute-done.refs_1_.refs_3_), channel_id=1, source_target_pairs={{0,8},{8,16},{16,24},{24,0},{1,9},{9,17},{17,25},{25,1},{2,10},{10... | collective-permute-start | bytes 393224 | tf_op jit(solution)/shard_map/ppermute | solution.py:523
  13.5 1.9 %shard_map.141 = (f32[16,128]{1,0:T(8,128)S(1)}, f32[16,128]{1,0:T(8,128)S(1)}, f32[512,128]{1,0:T(8,128)S(1)}) custom-call(s32[4]{0:T(128)S(1)} %pad_add_fusion.7.ids_ref, s32[2,128]{1,0:T(2,128)S(1)} %get-tuple-element.53.begin_ref, bf16[128,512]{1,0:T(8,128)(2,1)S(1)} %collective-permute-done.4.refs_0_, bf16[128,512]{1,0:T(8,128)(2,1)S(1)} %bitcast.35, ...), custom_call_target="tpu_custom_call" | custom-call | flops 3000000000 | tf_op jit(solution)/shard_map/pallas_call | solution.py:562
  16.0 4.8 %collective-permute-done.3.refs_4_.refs_3_ = bf16[128,512]{1,0:T(8,128)(2,1)S(1)} collective-permute-done((bf16[128,512]{1,0:T(8,128)(2,1)S(1)}, bf16[128,512]{1,0:T(8,128)(2,1)S(1)}, u32[]{:S(2)}, u32[]{:S(2)}) %collective-permute-start.3) | collective-permute-done | bytes 131104 | tf_op jit(solution)/shard_map/ppermute | solution.py:523
  20.8 0.8 %shard_map.143 = bf16[592,128]{1,0:T(8,128)(2,1)S(1)} custom-call(s32[3]{0:T(128)S(1)} %pad_add_fusion.6.ids_ref, s32[2,128]{1,0:T(2,128)S(1)} %get-tuple-element.53.begin_ref, bf16[128,512]{1,0:T(8,128)(2,1)S(1)} %collective-permute-done.4.refs_0_, bf16[128,512]{1,0:T(8,128)(2,1)S(1)} %get-tuple-element.66.refs_1_.refs_4_, ...), custom_call_target="tpu_custom_call" | custom-call | flops 1500000000 | tf_op jit(solution)/shard_map/pallas_call | solution.py:562
  21.6 1.1 %collective-permute-start.6 = (bf16[592,128]{1,0:T(8,128)(2,1)S(1)}, bf16[592,128]{1,0:T(8,128)(2,1)S(1)}, u32[]{:S(2)}, u32[]{:S(2)}) collective-permute-start(bf16[592,128]{1,0:T(8,128)(2,1)S(1)} %shard_map.143), channel_id=1, source_target_pairs={{0,1},{1,0},{2,3},{3,2},{4,5},{5,4},{6,7},{7,6},{8,9},{9,8},{10,11... | collective-permute-start | bytes 454664 | tf_op jit(solution)/shard_map/ppermute | solution.py:69
  22.8 1.6 %collective-permute-start.11 = (bf16[128,512]{1,0:T(8,128)(2,1)S(1)}, bf16[128,512]{1,0:T(8,128)(2,1)S(1)}, u32[]{:S(2)}, u32[]{:S(2)}) collective-permute-start(bf16[128,512]{1,0:T(8,128)(2,1)S(1)} %get-tuple-element.75), channel_id=1, source_target_pairs={{0,4},{2,6},{4,0},{6,2},{1,5},{3,7},{5,1},{7,3},{8,12},{10,14},{12... | collective-permute-start | bytes 393224 | tf_op jit(solution)/shard_map/ppermute | solution.py:69
  24.7 0.8 %shard_map.140 = (f32[16,128]{1,0:T(8,128)S(1)}, f32[16,128]{1,0:T(8,128)S(1)}, f32[512,128]{1,0:T(8,128)S(1)}) custom-call(s32[4]{0:T(128)S(1)} %pad_add_fusion.2.ids_ref, s32[2,128]{1,0:T(2,128)S(1)} %get-tuple-element.53.begin_ref, bf16[128,512]{1,0:T(8,128)(2,1)S(1)} %bitcast.41, bf16[128,512]{1,0:T(8,128)(2,1)S(1)} %collective-permute-done.refs_1_.refs_3_, ...), custom_call_target="tpu_custom_call" | custom-call | flops 1500000000 | tf_op jit(solution)/shard_map/pallas_call | solution.py:562
  25.4 1.4 %collective-permute-done.6.refs_3_ = bf16[592,128]{1,0:T(8,128)(2,1)S(1)} collective-permute-done((bf16[592,128]{1,0:T(8,128)(2,1)S(1)}, bf16[592,128]{1,0:T(8,128)(2,1)S(1)}, u32[]{:S(2)}, u32[]{:S(2)}) %collective-permute-start.6) | collective-permute-done | bytes 151584 | tf_op jit(solution)/shard_map/ppermute | solution.py:69
  26.8 0.6 %shard_map.144 = (bf16[128,512]{1,0:T(8,128)(2,1)S(1)}, bf16[64,512]{1,0:T(8,128)(2,1)S(1)}, bf16[64,512]{1,0:T(8,128)(2,1)S(1)}, bf16[64,512]{1,0:T(8,128)(2,1)S(1)}, bf16[64,512]{1,0:T(8,128)(2,1)S(1)}) custom-call(s32[1]{0:T(128)} %bitcast.own_ref, bf16[160,512]{1,0:T(8,128)(2,1)S(1)} %get-tuple-element.52.refs_0_.extended_ref, ...), custom_call_target="tpu_custom_call" | custom-call | flops 2000000000 | tf_op jit(solution)/shard_map/pallas_call | solution.py:616
  27.4 1.1 %collective-permute-start.13 = (bf16[64,512]{1,0:T(8,128)(2,1)S(1)}, bf16[64,512]{1,0:T(8,128)(2,1)S(1)}, u32[]{:S(2)}, u32[]{:S(2)}) collective-permute-start(bf16[64,512]{1,0:T(8,128)(2,1)S(1)} %get-tuple-element.70.refs_0_), channel_id=1, source_target_pairs={{0,1},{1,0},{2,3},{3,2},{4,5},{5,4},{6,7},{7,6},{8,9},{9,8},{10,11... | collective-permute-start | bytes 196616 | tf_op jit(solution)/shard_map/ppermute | solution.py:69
  28.8 1.7 %collective-permute-start.15 = (bf16[64,512]{1,0:T(8,128)(2,1)S(1)}, bf16[64,512]{1,0:T(8,128)(2,1)S(1)}, u32[]{:S(2)}, u32[]{:S(2)}) collective-permute-start(bf16[64,512]{1,0:T(8,128)(2,1)S(1)} %get-tuple-element.72), channel_id=1, source_target_pairs={{0,5},{1,4},{2,7},{3,6},{4,1},{5,0},{6,3},{7,2},{8,13},{9,12},{10,... | collective-permute-start | bytes 196616 | tf_op jit(solution)/shard_map/ppermute | solution.py:69
  30.5 1.4 %collective-permute-start.14 = (bf16[64,512]{1,0:T(8,128)(2,1)S(1)}, bf16[64,512]{1,0:T(8,128)(2,1)S(1)}, u32[]{:S(2)}, u32[]{:S(2)}) collective-permute-start(bf16[64,512]{1,0:T(8,128)(2,1)S(1)} %get-tuple-element.73), channel_id=1, source_target_pairs={{0,3},{1,2},{2,1},{3,0},{4,7},{5,6},{6,5},{7,4},{8,11},{9,10},{10,... | collective-permute-start | bytes 196616 | tf_op jit(solution)/shard_map/ppermute | solution.py:69
  32.0 0.8 %collective-permute-start.7 = (bf16[64,512]{1,0:T(8,128)(2,1)S(1)}, bf16[64,512]{1,0:T(8,128)(2,1)S(1)}, u32[]{:S(2)}, u32[]{:S(2)}) collective-permute-start(bf16[64,512]{1,0:T(8,128)(2,1)S(1)} %get-tuple-element.71), channel_id=1, source_target_pairs={{0,6},{1,7},{2,4},{3,5},{4,2},{5,3},{6,0},{7,1},{8,14},{9,15},{10,... | collective-permute-start | bytes 196616 | tf_op jit(solution)/shard_map/ppermute | solution.py:69
  32.8 0.9 %collective-permute-start.8 = (bf16[64,512]{1,0:T(8,128)(2,1)S(1)}, bf16[64,512]{1,0:T(8,128)(2,1)S(1)}, u32[]{:S(2)}, u32[]{:S(2)}) collective-permute-start(bf16[64,512]{1,0:T(8,128)(2,1)S(1)} %get-tuple-element.72), channel_id=1, source_target_pairs={{0,4},{1,5},{2,6},{3,7},{4,0},{5,1},{6,2},{7,3},{8,12},{9,13},{10,... | collective-permute-start | bytes 196616 | tf_op jit(solution)/shard_map/ppermute | solution.py:69
  33.9 1.6 %collective-permute-done.15.refs_2_ = bf16[64,512]{1,0:T(8,128)(2,1)S(1)} collective-permute-done((bf16[64,512]{1,0:T(8,128)(2,1)S(1)}, bf16[64,512]{1,0:T(8,128)(2,1)S(1)}, u32[]{:S(2)}, u32[]{:S(2)}) %collective-permute-start.15) | collective-permute-done | bytes 65568 | tf_op jit(solution)/shard_map/ppermute | solution.py:69
  36.0 1.6 %shard_map.145 = (f32[256,512]{1,0:T(8,128)S(1)}, f32[256,512]{1,0:T(8,128)S(1)}) custom-call(s32[1]{0:T(128)} %bitcast.own_ref, s32[4]{0:T(128)S(1)} %pad_add_fusion.part_ref, bf16[512,512]{1,0:T(8,128)(2,1)S(1)} %bitcast.26, bf16[512,512]{1,0:T(8,128)(2,1)S(1)} %bitcast.29, bf16[160,512]{1,0:T(8,128)(2,1)S(1)} %get-tuple-element.52.refs_0_.extended_ref, ...), custom_call_target="tpu_custom_call" | custom-call | flops 2000000000 | tf_op jit(solution)/shard_map/pallas_call | solution.py:629
  37.6 0.7 %collective-permute-done.8.refs_2_ = bf16[64,512]{1,0:T(8,128)(2,1)S(1)} collective-permute-done((bf16[64,512]{1,0:T(8,128)(2,1)S(1)}, bf16[64,512]{1,0:T(8,128)(2,1)S(1)}, u32[]{:S(2)}, u32[]{:S(2)}) %collective-permute-start.8) | collective-permute-done | bytes 65568 | tf_op jit(solution)/shard_map/ppermute | solution.py:69
  38.3 1.6 %shard_map.146 = (bf16[256,512]{1,0:T(8,128)(2,1)S(1)}, bf16[256,512]{1,0:T(8,128)(2,1)S(1)}, bf16[2,64,512]{2,1,0:T(8,128)(2,1)S(1)}, bf16[2,64,512]{2,1,0:T(8,...) custom-call(s32[1]{0:T(128)} %bitcast.own_ref, s32[4]{0:T(128)S(1)} %pad_add_fusion.part_ref, ...), custom_call_target="tpu_custom_call" | custom-call | flops 2000000000 | tf_op jit(solution)/shard_map/pallas_call | solution.py:629
  40.0 2.4 %collective-permute-start.17 = (bf16[2,64,512]{2,1,0:T(8,128)(2,1)S(1)}, bf16[2,64,512]{2,1,0:T(8,128)(2,1)S(1)}, u32[]{:S(2)}, u32[]{:S(2)}) collective-permute-start(bf16[2,64,512]{2,1,0:T(8,128)(2,1)S(1)} %get-tuple-element.87), channel_id=1, source_target_pairs={{0,24},{8,16},{16,8},{24,0},{1,25},{9,17},{17,9},{25,1},{2,26},{10... | collective-permute-start | bytes 393224 | tf_op jit(solution)/shard_map/ppermute | solution.py:69
  42.3 2.1 %collective-permute-start.19 = (bf16[2,64,512]{2,1,0:T(8,128)(2,1)S(1)}, bf16[2,64,512]{2,1,0:T(8,128)(2,1)S(1)}, u32[]{:S(2)}, u32[]{:S(2)}) collective-permute-start(bf16[2,64,512]{2,1,0:T(8,128)(2,1)S(1)} %get-tuple-element.89), channel_id=1, source_target_pairs={{0,8},{8,0},{16,24},{24,16},{1,9},{9,1},{17,25},{25,17},{2,10},{10... | collective-permute-start | bytes 393224 | tf_op jit(solution)/shard_map/ppermute | solution.py:69
  44.9 0.9 %collective-permute-start.21 = (bf16[128,512]{1,0:T(8,128)(2,1)S(1)}, bf16[128,512]{1,0:T(8,128)(2,1)S(1)}, u32[]{:S(2)}, u32[]{:S(2)}) collective-permute-start(bf16[128,512]{1,0:T(8,128)(2,1)S(1)} %get-tuple-element.93), channel_id=1, source_target_pairs={{0,4},{2,6},{4,0},{6,2},{1,5},{3,7},{5,1},{7,3},{8,12},{10,14},{12... | collective-permute-start | bytes 393224 | tf_op jit(solution)/shard_map/ppermute | solution.py:69
  45.8 2.5 %collective-permute-done.17.refs_1_ = bf16[2,64,512]{2,1,0:T(8,128)(2,1)S(1)} collective-permute-done((bf16[2,64,512]{2,1,0:T(8,128)(2,1)S(1)}, bf16[2,64,512]{2,1,0:T(8,128)(2,1)S(1)}, u32[]{:S(2)}, u32[]{:S(2)}) %collective-permute-start.17) | collective-permute-done | bytes 131104 | tf_op jit(solution)/shard_map/ppermute | solution.py:69
  48.8 4.2 %collective-permute-done.18.refs_2_ = bf16[2,64,512]{2,1,0:T(8,128)(2,1)S(1)} collective-permute-done((bf16[2,64,512]{2,1,0:T(8,128)(2,1)S(1)}, bf16[2,64,512]{2,1,0:T(8,128)(2,1)S(1)}, u32[]{:S(2)}, u32[]{:S(2)}) %collective-permute-start.18) | collective-permute-done | bytes 131104 | tf_op jit(solution)/shard_map/ppermute | solution.py:69
  53.0 1.3 %shard_map.149 = (bf16[128,512]{1,0:T(8,128)(2,1)}, bf16[128,512]{1,0:T(8,128)(2,1)}, f32[64,512]{1,0:T(8,128)}, f32[64,512]{1,0:T(8,128)}) custom-call(bf16[128,256]{1,0:T(8,128)(2,1)S(1)} %get-tuple-element.83.placed_ref, f32[128,128]{1,0:T(8,128)S(1)} %get-tuple-element.84.factors_ref, f32[128,512]{1,0:T(8,128)S(1)} %get-tuple-element.85.router_cols_ref, ...), custom_call_target="tpu_custom_call" | custom-call | flops 1000000000 | tf_op jit(solution)/shard_map/pallas_call | solution.py:682
  (54 shorter events, 4.1 us)
Async XLA Ops:
  0.6 12.8 %collective-permute-start.4 = (bf16[128,512]{1,0:T(8,128)(2,1)}, bf16[128,512]{1,0:T(8,128)(2,1)S(1)}, u32[]{:S(2)}, u32[]{:S(2)}) collective-permute-start(bf16[128,512]{1,0:T(8,128)(2,1)} %bitcast.39), channel_id=1, source_target_pairs={{0,1},{1,0},{2,3},{3,2},{4,5},{5,4},{6,7},{7,6},{8,9},{9,8},{10,11... | collective-permute-start | bytes 393224 | tf_op jit(solution)/shard_map/ppermute | solution.py:69
  3.6 8.4 %collective-permute-start = (bf16[128,512]{1,0:T(8,128)(2,1)}, bf16[128,512]{1,0:T(8,128)(2,1)S(1)}, u32[]{:S(2)}, u32[]{:S(2)}) collective-permute-start(bf16[128,512]{1,0:T(8,128)(2,1)} %bitcast.33), channel_id=1, source_target_pairs={{0,8},{8,16},{16,24},{24,0},{1,9},{9,17},{17,25},{25,1},{2,10},{10... | collective-permute-start | bytes 393224 | tf_op jit(solution)/shard_map/ppermute | solution.py:523
  5.2 8.3 %collective-permute-start.1 = (bf16[128,512]{1,0:T(8,128)(2,1)}, bf16[128,512]{1,0:T(8,128)(2,1)S(1)}, u32[]{:S(2)}, u32[]{:S(2)}) collective-permute-start(bf16[128,512]{1,0:T(8,128)(2,1)} %bitcast.36), channel_id=1, source_target_pairs={{0,8},{8,16},{16,24},{24,0},{1,9},{9,17},{17,25},{25,1},{2,10},{10... | collective-permute-start | bytes 393224 | tf_op jit(solution)/shard_map/ppermute | solution.py:523
  6.8 0.7 %copy-start.8 = (bf16[512,4]{0,1:T(4,128)(2,1)S(1)}, bf16[512,4]{0,1:T(4,128)(2,1)}, u32[]{:S(2)}) copy-start(bf16[512,4]{0,1:T(4,128)(2,1)} %param.17) | copy-start | bytes 12292
  7.5 0.9 %copy-start.3 = (bf16[1,128,512]{2,1,0:T(8,128)(2,1)S(1)}, bf16[1,128,512]{2,1,0:T(8,128)(2,1)}, u32[]{:S(2)}) copy-start(bf16[1,128,512]{2,1,0:T(8,128)(2,1)} %param.21) | copy-start | bytes 393220
  8.4 1.3 %copy-start.4 = (bf16[1,128,512]{2,1,0:T(8,128)(2,1)S(1)}, bf16[1,128,512]{2,1,0:T(8,128)(2,1)}, u32[]{:S(2)}) copy-start(bf16[1,128,512]{2,1,0:T(8,128)(2,1)} %param.12) | copy-start | bytes 393220
  8.4 1.3 %copy-start.5 = (bf16[1,128,512]{2,1,0:T(8,128)(2,1)S(1)}, bf16[1,128,512]{2,1,0:T(8,128)(2,1)}, u32[]{:S(2)}) copy-start(bf16[1,128,512]{2,1,0:T(8,128)(2,1)} %param.13) | copy-start | bytes 393220
  8.4 1.3 %copy-start.6 = (bf16[1,128,512]{2,1,0:T(8,128)(2,1)S(1)}, bf16[1,128,512]{2,1,0:T(8,128)(2,1)}, u32[]{:S(2)}) copy-start(bf16[1,128,512]{2,1,0:T(8,128)(2,1)} %param.11) | copy-start | bytes 393220
  9.0 6.4 %collective-permute-start.5 = (bf16[160,512]{1,0:T(8,128)(2,1)S(1)}, bf16[160,512]{1,0:T(8,128)(2,1)S(1)}, u32[]{:S(2)}, u32[]{:S(2)}) collective-permute-start(bf16[160,512]{1,0:T(8,128)(2,1)S(1)} %get-tuple-element.52.refs_0_.extended_ref), channel_id=1, source_target_pairs={{0,1},{1,0},{2,3},{3,2},{4,5},{5,4},{6,7},{7,6},{8,9},{9,8},{10,11... | collective-permute-start | bytes 491528 | tf_op jit(solution)/shard_map/ppermute | solution.py:69
  12.1 8.7 %collective-permute-start.2 = (bf16[128,512]{1,0:T(8,128)(2,1)S(1)}, bf16[128,512]{1,0:T(8,128)(2,1)S(1)}, u32[]{:S(2)}, u32[]{:S(2)}) collective-permute-start(bf16[128,512]{1,0:T(8,128)(2,1)S(1)} %collective-permute-done.refs_1_.refs_3_), channel_id=1, source_target_pairs={{0,8},{8,16},{16,24},{24,0},{1,9},{9,17},{17,25},{25,1},{2,10},{10... | collective-permute-start | bytes 393224 | tf_op jit(solution)/shard_map/ppermute | solution.py:523
  13.5 7.3 %collective-permute-start.3 = (bf16[128,512]{1,0:T(8,128)(2,1)S(1)}, bf16[128,512]{1,0:T(8,128)(2,1)S(1)}, u32[]{:S(2)}, u32[]{:S(2)}) collective-permute-start(bf16[128,512]{1,0:T(8,128)(2,1)S(1)} %collective-permute-done.1.refs_2_.refs_4_), channel_id=1, source_target_pairs={{0,8},{8,16},{16,24},{24,0},{1,9},{9,17},{17,25},{25,1},{2,10},{10... | collective-permute-start | bytes 393224 | tf_op jit(solution)/shard_map/ppermute | solution.py:523
  21.6 5.3 %collective-permute-start.6 = (bf16[592,128]{1,0:T(8,128)(2,1)S(1)}, bf16[592,128]{1,0:T(8,128)(2,1)S(1)}, u32[]{:S(2)}, u32[]{:S(2)}) collective-permute-start(bf16[592,128]{1,0:T(8,128)(2,1)S(1)} %shard_map.143), channel_id=1, source_target_pairs={{0,1},{1,0},{2,3},{3,2},{4,5},{5,4},{6,7},{7,6},{8,9},{9,8},{10,11... | collective-permute-start | bytes 454664 | tf_op jit(solution)/shard_map/ppermute | solution.py:69
  22.8 6.1 %collective-permute-start.10 = (bf16[128,512]{1,0:T(8,128)(2,1)S(1)}, bf16[128,512]{1,0:T(8,128)(2,1)S(1)}, u32[]{:S(2)}, u32[]{:S(2)}) collective-permute-start(bf16[128,512]{1,0:T(8,128)(2,1)S(1)} %get-tuple-element.74), channel_id=1, source_target_pairs={{0,2},{2,0},{4,6},{6,4},{1,3},{3,1},{5,7},{7,5},{8,10},{10,8},{12,... | collective-permute-start | bytes 393224 | tf_op jit(solution)/shard_map/ppermute | solution.py:69
  22.8 7.7 %collective-permute-start.11 = (bf16[128,512]{1,0:T(8,128)(2,1)S(1)}, bf16[128,512]{1,0:T(8,128)(2,1)S(1)}, u32[]{:S(2)}, u32[]{:S(2)}) collective-permute-start(bf16[128,512]{1,0:T(8,128)(2,1)S(1)} %get-tuple-element.75), channel_id=1, source_target_pairs={{0,4},{2,6},{4,0},{6,2},{1,5},{3,7},{5,1},{7,3},{8,12},{10,14},{12... | collective-permute-start | bytes 393224 | tf_op jit(solution)/shard_map/ppermute | solution.py:69
  24.4 2.4 %copy-start = (bf16[512,512]{1,0:T(8,128)(2,1)S(1)}, bf16[512,512]{1,0:T(8,128)(2,1)}, u32[]{:S(2)}) copy-start(bf16[512,512]{1,0:T(8,128)(2,1)} %proj_ref.1) | copy-start | bytes 1572868
  24.4 2.4 %copy-start.7 = (bf16[1,128,512]{2,1,0:T(8,128)(2,1)S(1)}, bf16[1,128,512]{2,1,0:T(8,128)(2,1)}, u32[]{:S(2)}) copy-start(bf16[1,128,512]{2,1,0:T(8,128)(2,1)} %param.15) | copy-start | bytes 393220
  24.4 7.6 %collective-permute-start.12 = (bf16[128,512]{1,0:T(8,128)(2,1)S(1)}, bf16[128,512]{1,0:T(8,128)(2,1)S(1)}, u32[]{:S(2)}, u32[]{:S(2)}) collective-permute-start(bf16[128,512]{1,0:T(8,128)(2,1)S(1)} %get-tuple-element.76), channel_id=1, source_target_pairs={{0,6},{2,4},{4,2},{6,0},{1,7},{3,5},{5,3},{7,1},{8,14},{10,12},{12... | collective-permute-start | bytes 393224 | tf_op jit(solution)/shard_map/ppermute | solution.py:69
  26.8 9.2 %copy-start.1 = (bf16[1,512,512]{2,1,0:T(8,128)(2,1)S(1)}, bf16[1,512,512]{2,1,0:T(8,128)(2,1)}, u32[]{:S(2)}) copy-start(bf16[1,512,512]{2,1,0:T(8,128)(2,1)} %param.19) | copy-start | bytes 1572868
  26.8 9.2 %copy-start.2 = (bf16[1,512,512]{2,1,0:T(8,128)(2,1)S(1)}, bf16[1,512,512]{2,1,0:T(8,128)(2,1)}, u32[]{:S(2)}) copy-start(bf16[1,512,512]{2,1,0:T(8,128)(2,1)} %param.20) | copy-start | bytes 1572868
  27.4 5.3 %collective-permute-start.13 = (bf16[64,512]{1,0:T(8,128)(2,1)S(1)}, bf16[64,512]{1,0:T(8,128)(2,1)S(1)}, u32[]{:S(2)}, u32[]{:S(2)}) collective-permute-start(bf16[64,512]{1,0:T(8,128)(2,1)S(1)} %get-tuple-element.70.refs_0_), channel_id=1, source_target_pairs={{0,1},{1,0},{2,3},{3,2},{4,5},{5,4},{6,7},{7,6},{8,9},{9,8},{10,11... | collective-permute-start | bytes 196616 | tf_op jit(solution)/shard_map/ppermute | solution.py:69
  28.6 5.2 %collective-permute-start.16 = (bf16[64,512]{1,0:T(8,128)(2,1)S(1)}, bf16[64,512]{1,0:T(8,128)(2,1)S(1)}, u32[]{:S(2)}, u32[]{:S(2)}) collective-permute-start(bf16[64,512]{1,0:T(8,128)(2,1)S(1)} %get-tuple-element.71), channel_id=1, source_target_pairs={{0,7},{1,6},{2,5},{3,4},{4,3},{5,2},{6,1},{7,0},{8,15},{9,14},{10,... | collective-permute-start | bytes 196616 | tf_op jit(solution)/shard_map/ppermute | solution.py:69
  28.8 6.7 %collective-permute-start.15 = (bf16[64,512]{1,0:T(8,128)(2,1)S(1)}, bf16[64,512]{1,0:T(8,128)(2,1)S(1)}, u32[]{:S(2)}, u32[]{:S(2)}) collective-permute-start(bf16[64,512]{1,0:T(8,128)(2,1)S(1)} %get-tuple-element.72), channel_id=1, source_target_pairs={{0,5},{1,4},{2,7},{3,6},{4,1},{5,0},{6,3},{7,2},{8,13},{9,12},{10,... | collective-permute-start | bytes 196616 | tf_op jit(solution)/shard_map/ppermute | solution.py:69
  30.5 5.5 %collective-permute-start.14 = (bf16[64,512]{1,0:T(8,128)(2,1)S(1)}, bf16[64,512]{1,0:T(8,128)(2,1)S(1)}, u32[]{:S(2)}, u32[]{:S(2)}) collective-permute-start(bf16[64,512]{1,0:T(8,128)(2,1)S(1)} %get-tuple-element.73), channel_id=1, source_target_pairs={{0,3},{1,2},{2,1},{3,0},{4,7},{5,6},{6,5},{7,4},{8,11},{9,10},{10,... | collective-permute-start | bytes 196616 | tf_op jit(solution)/shard_map/ppermute | solution.py:69
  32.0 5.7 %collective-permute-start.7 = (bf16[64,512]{1,0:T(8,128)(2,1)S(1)}, bf16[64,512]{1,0:T(8,128)(2,1)S(1)}, u32[]{:S(2)}, u32[]{:S(2)}) collective-permute-start(bf16[64,512]{1,0:T(8,128)(2,1)S(1)} %get-tuple-element.71), channel_id=1, source_target_pairs={{0,6},{1,7},{2,4},{3,5},{4,2},{5,3},{6,0},{7,1},{8,14},{9,15},{10,... | collective-permute-start | bytes 196616 | tf_op jit(solution)/shard_map/ppermute | solution.py:69
  32.8 5.6 %collective-permute-start.8 = (bf16[64,512]{1,0:T(8,128)(2,1)S(1)}, bf16[64,512]{1,0:T(8,128)(2,1)S(1)}, u32[]{:S(2)}, u32[]{:S(2)}) collective-permute-start(bf16[64,512]{1,0:T(8,128)(2,1)S(1)} %get-tuple-element.72), channel_id=1, source_target_pairs={{0,4},{1,5},{2,6},{3,7},{4,0},{5,1},{6,2},{7,3},{8,12},{9,13},{10,... | collective-permute-start | bytes 196616 | tf_op jit(solution)/shard_map/ppermute | solution.py:69
  33.8 4.6 %collective-permute-start.9 = (bf16[64,512]{1,0:T(8,128)(2,1)S(1)}, bf16[64,512]{1,0:T(8,128)(2,1)S(1)}, u32[]{:S(2)}, u32[]{:S(2)}) collective-permute-start(bf16[64,512]{1,0:T(8,128)(2,1)S(1)} %get-tuple-element.73), channel_id=1, source_target_pairs={{0,2},{1,3},{2,0},{3,1},{4,6},{5,7},{6,4},{7,5},{8,10},{9,11},{10,... | collective-permute-start | bytes 196616 | tf_op jit(solution)/shard_map/ppermute | solution.py:69
  40.0 8.3 %collective-permute-start.17 = (bf16[2,64,512]{2,1,0:T(8,128)(2,1)S(1)}, bf16[2,64,512]{2,1,0:T(8,128)(2,1)S(1)}, u32[]{:S(2)}, u32[]{:S(2)}) collective-permute-start(bf16[2,64,512]{2,1,0:T(8,128)(2,1)S(1)} %get-tuple-element.87), channel_id=1, source_target_pairs={{0,24},{8,16},{16,8},{24,0},{1,25},{9,17},{17,9},{25,1},{2,26},{10... | collective-permute-start | bytes 393224 | tf_op jit(solution)/shard_map/ppermute | solution.py:69
  42.3 10.7 %collective-permute-start.18 = (bf16[2,64,512]{2,1,0:T(8,128)(2,1)S(1)}, bf16[2,64,512]{2,1,0:T(8,128)(2,1)S(1)}, u32[]{:S(2)}, u32[]{:S(2)}) collective-permute-start(bf16[2,64,512]{2,1,0:T(8,128)(2,1)S(1)} %get-tuple-element.88), channel_id=1, source_target_pairs={{0,16},{8,24},{16,0},{24,8},{1,17},{9,25},{17,1},{25,9},{2,18},{10... | collective-permute-start | bytes 393224 | tf_op jit(solution)/shard_map/ppermute | solution.py:69
  42.3 10.7 %collective-permute-start.19 = (bf16[2,64,512]{2,1,0:T(8,128)(2,1)S(1)}, bf16[2,64,512]{2,1,0:T(8,128)(2,1)S(1)}, u32[]{:S(2)}, u32[]{:S(2)}) collective-permute-start(bf16[2,64,512]{2,1,0:T(8,128)(2,1)S(1)} %get-tuple-element.89), channel_id=1, source_target_pairs={{0,8},{8,0},{16,24},{24,16},{1,9},{9,1},{17,25},{25,17},{2,10},{10... | collective-permute-start | bytes 393224 | tf_op jit(solution)/shard_map/ppermute | solution.py:69
  44.9 8.1 %collective-permute-start.20 = (bf16[128,512]{1,0:T(8,128)(2,1)S(1)}, bf16[128,512]{1,0:T(8,128)(2,1)S(1)}, u32[]{:S(2)}, u32[]{:S(2)}) collective-permute-start(bf16[128,512]{1,0:T(8,128)(2,1)S(1)} %get-tuple-element.92), channel_id=1, source_target_pairs={{0,6},{2,4},{4,2},{6,0},{1,7},{3,5},{5,3},{7,1},{8,14},{10,12},{12... | collective-permute-start | bytes 393224 | tf_op jit(solution)/shard_map/ppermute | solution.py:69
  44.9 8.1 %collective-permute-start.21 = (bf16[128,512]{1,0:T(8,128)(2,1)S(1)}, bf16[128,512]{1,0:T(8,128)(2,1)S(1)}, u32[]{:S(2)}, u32[]{:S(2)}) collective-permute-start(bf16[128,512]{1,0:T(8,128)(2,1)S(1)} %get-tuple-element.93), channel_id=1, source_target_pairs={{0,4},{2,6},{4,0},{6,2},{1,5},{3,7},{5,1},{7,3},{8,12},{10,14},{12... | collective-permute-start | bytes 393224 | tf_op jit(solution)/shard_map/ppermute | solution.py:69
  48.3 4.7 %collective-permute-start.22 = (bf16[128,512]{1,0:T(8,128)(2,1)S(1)}, bf16[128,512]{1,0:T(8,128)(2,1)S(1)}, u32[]{:S(2)}, u32[]{:S(2)}) collective-permute-start(bf16[128,512]{1,0:T(8,128)(2,1)S(1)} %get-tuple-element.94), channel_id=1, source_target_pairs={{0,2},{2,0},{4,6},{6,4},{1,3},{3,1},{5,7},{7,5},{8,10},{10,8},{12,... | collective-permute-start | bytes 393224 | tf_op jit(solution)/shard_map/ppermute | solution.py:69
  (2 other events, 1.3 us)

commit v23 on v22

--- a/solution.py
+++ b/solution.py
@@ -577,12 +577,8 @@
     lines.append(tuple(forward(one) for one in lines[0]))
     queries = reps.exchange([query_rows[0]] * rep_count)
     extendeds = reps.exchange([extended] * rep_count)
-    states = attend(((0, 0, True),), lines[:1], [0], queries, {}, False, 2.0)
-    ahead, *states[0] = lax.optimization_barrier((lines[1][0], *states[0]))
-    lines[1] = (ahead, lines[1][1])
     for unused in range(1, reach):
         lines.append(tuple(forward(one) for one in lines[-1]))
-    own_state = states
     middle = tuple((k, step, step == 0) for k in others for step in range(reach))
     states = attend(middle, lines[:-1], list(range(reach)), queries, {}, False, 3.0)
     states[1][0], *extendeds[1:] = lax.optimization_barrier((states[1][0], *extendeds[1:]))
@@ -603,11 +599,11 @@
     )
     returned = reps.exchange([None] + [partial[k] for k in others], inverse=True)[1:]
     states = attend(
-        tuple((0, step, False) for step in range(reach)),
-        lines[1:],
-        list(range(1, reach + 1)),
+        tuple((0, step, step == 0) for step in range(reach + 1)),
+        lines,
+        list(range(reach + 1)),
         queries,
-        own_state,
+        {},
         False,
         1.5,
     )

time: 54.5 us -> 54.7 us (level)
  waiting for transfers between devices: 16.5 us -> 18.8 us
  starting transfers between devices: 22.6 us -> 21.7 us
  Pallas kernels: 12.3 us -> 11.5 us
    ppermute x4, waiting for transfers between devices: 5.52 us -> 8.12 us  [forward(): lax.ppermute(array, 'seq', [(i, (i + 1) % seq_count) for i in range(seq_c...]
    ppermute x4, starting transfers between devices: 4.3 us -> 3.54 us  [forward(): lax.ppermute(array, 'seq', [(i, (i + 1) % seq_count) for i in range(seq_c...]
    pallas_call x4 -> x3, Pallas kernels: 5.18 us -> 4.43 us  [attend(): call(functools.partial(attend_kernel, plan, rep_count, len(pairs), packed...]
  transfers between devices with their start and end apart: 23 -> 23, of which waited for: 10 -> 10; matrix products, arithmetic and copies ran while one was open for 1% -> 1% of each run, Pallas kernels for 16% -> 14%
where the time goes in v23:
time: 54.7 us; the launch traced here: 54.8 us
  starting transfers between devices  21.7 us (40%)
  waiting for transfers between devices  18.8 us (34%)
  Pallas kernels  11.5 us (21%)
  local copies, waits for them, and re-layouts  1.68 us (3%)
  between operations  0.78 us (1%)
    ppermute x19, starting transfers between devices, exchange(): got[k] = lax.ppermute(chunks[k], self.axes, pairs)  18.2 us
    ppermute x19, waiting for transfers between devices, exchange(): got[k] = lax.ppermute(chunks[k], self.axes, pairs)  10.7 us
    ppermute x4, waiting for transfers between devices, forward(): lax.ppermute(array, 'seq', [(i, (i + 1) % seq_count) for i in range(seq_c...  8.12 us
    pallas_call x3, Pallas kernels, attend(): call(functools.partial(attend_kernel, plan, rep_count, len(pairs), packed...  4.43 us
    ppermute x4, starting transfers between devices, forward(): lax.ppermute(array, 'seq', [(i, (i + 1) % seq_count) for i in range(seq_c...  3.54 us
    pallas_call x2, Pallas kernels, expert_call(): call(functools.partial(expert_kernel, rep_count, rep_list, expert_count,...  3.23 us
    unnamed x22, local copies, waits for them, and re-layouts  1.6 us
    pallas_call x1, Pallas kernels, local(): call(functools.partial(finish_kernel, hot_capacity, seq_count), [shape((t...  1.26 us
  transfers between devices with their start and end apart: 23, of which 10 were waited for; matrix products, arithmetic and copies ran while one was open for 1% of the time, Pallas kernels for 14%

profile of v23, /device:TPU:0, one launch (start us, length us, event | category | flops | bytes accessed | tf_op | source)
XLA Modules:
  0.0 54.8 jit_solution(6465579112219590825)
XLA Ops:
  0.6 3.0 %collective-permute-start.4 = (bf16[128,512]{1,0:T(8,128)(2,1)}, bf16[128,512]{1,0:T(8,128)(2,1)S(1)}, u32[]{:S(2)}, u32[]{:S(2)}) collective-permute-start(bf16[128,512]{1,0:T(8,128)(2,1)} %bitcast.33), channel_id=1, source_target_pairs={{0,1},{1,0},{2,3},{3,2},{4,5},{5,4},{6,7},{7,6},{8,9},{9,8},{10,11... | collective-permute-start | bytes 393224 | tf_op jit(solution)/shard_map/ppermute | solution.py:69
  3.6 1.6 %collective-permute-start = (bf16[128,512]{1,0:T(8,128)(2,1)}, bf16[128,512]{1,0:T(8,128)(2,1)S(1)}, u32[]{:S(2)}, u32[]{:S(2)}) collective-permute-start(bf16[128,512]{1,0:T(8,128)(2,1)} %bitcast.35), channel_id=1, source_target_pairs={{0,8},{8,16},{16,24},{24,0},{1,9},{9,17},{17,25},{25,1},{2,10},{10... | collective-permute-start | bytes 393224 | tf_op jit(solution)/shard_map/ppermute | solution.py:523
  5.2 1.6 %collective-permute-start.1 = (bf16[128,512]{1,0:T(8,128)(2,1)}, bf16[128,512]{1,0:T(8,128)(2,1)S(1)}, u32[]{:S(2)}, u32[]{:S(2)}) collective-permute-start(bf16[128,512]{1,0:T(8,128)(2,1)} %bitcast.38), channel_id=1, source_target_pairs={{0,8},{8,16},{16,24},{24,0},{1,9},{9,17},{17,25},{25,1},{2,10},{10... | collective-permute-start | bytes 393224 | tf_op jit(solution)/shard_map/ppermute | solution.py:523
  6.9 0.6 %copy-done.8 = bf16[512,4]{0,1:T(4,128)(2,1)S(1)} copy-done((bf16[512,4]{0,1:T(4,128)(2,1)S(1)}, bf16[512,4]{0,1:T(4,128)(2,1)}, u32[]{:S(2)}) %copy-start.8) | copy-done | bytes 4120
  7.5 0.9 %copy-done.3 = bf16[1,128,512]{2,1,0:T(8,128)(2,1)S(1)} copy-done((bf16[1,128,512]{2,1,0:T(8,128)(2,1)S(1)}, bf16[1,128,512]{2,1,0:T(8,128)(2,1)}, u32[]{:S(2)}) %copy-start.3) | copy-done | bytes 131096
  9.0 0.6 %collective-permute-start.5 = (bf16[160,512]{1,0:T(8,128)(2,1)S(1)}, bf16[160,512]{1,0:T(8,128)(2,1)S(1)}, u32[]{:S(2)}, u32[]{:S(2)}) collective-permute-start(bf16[160,512]{1,0:T(8,128)(2,1)S(1)} %get-tuple-element.45.refs_0_.extended_ref), channel_id=1, source_target_pairs={{0,1},{1,0},{2,3},{3,2},{4,5},{5,4},{6,7},{7,6},{8,9},{9,8},{10,11... | collective-permute-start | bytes 491528 | tf_op jit(solution)/shard_map/ppermute | solution.py:69
  9.8 2.3 %collective-permute-done.refs_3_ = bf16[128,512]{1,0:T(8,128)(2,1)S(1)} collective-permute-done((bf16[128,512]{1,0:T(8,128)(2,1)}, bf16[128,512]{1,0:T(8,128)(2,1)S(1)}, u32[]{:S(2)}, u32[]{:S(2)}) %collective-permute-start) | collective-permute-done | bytes 131104 | tf_op jit(solution)/shard_map/ppermute | solution.py:523
  12.1 1.4 %collective-permute-done.1.refs_4_ = bf16[128,512]{1,0:T(8,128)(2,1)S(1)} collective-permute-done((bf16[128,512]{1,0:T(8,128)(2,1)}, bf16[128,512]{1,0:T(8,128)(2,1)S(1)}, u32[]{:S(2)}, u32[]{:S(2)}) %collective-permute-start.1) | collective-permute-done | bytes 131104 | tf_op jit(solution)/shard_map/ppermute | solution.py:523
  13.9 1.9 %shard_map.140 = (f32[16,128]{1,0:T(8,128)S(1)}, f32[16,128]{1,0:T(8,128)S(1)}, f32[512,128]{1,0:T(8,128)S(1)}) custom-call(s32[4]{0:T(128)S(1)} %pad_add_fusion.3.ids_ref, s32[2,128]{1,0:T(2,128)S(1)} %get-tuple-element.46.begin_ref, bf16[128,512]{1,0:T(8,128)(2,1)S(1)} %collective-permute-done.4.refs_0_, bf16[128,512]{1,0:T(8,128)(2,1)S(1)} %bitcast.36, ...), custom_call_target="tpu_custom_call" | custom-call | flops 3000000000 | tf_op jit(solution)/shard_map/pallas_call | solution.py:562
  16.4 3.0 %collective-permute-done.2.refs_5_.refs_2_ = bf16[128,512]{1,0:T(8,128)(2,1)S(1)} collective-permute-done((bf16[128,512]{1,0:T(8,128)(2,1)S(1)}, bf16[128,512]{1,0:T(8,128)(2,1)S(1)}, u32[]{:S(2)}, u32[]{:S(2)}) %collective-permute-start.2) | collective-permute-done | bytes 131104 | tf_op jit(solution)/shard_map/ppermute | solution.py:523
  19.4 1.4 %collective-permute-done.3.refs_6_.refs_3_ = bf16[128,512]{1,0:T(8,128)(2,1)S(1)} collective-permute-done((bf16[128,512]{1,0:T(8,128)(2,1)S(1)}, bf16[128,512]{1,0:T(8,128)(2,1)S(1)}, u32[]{:S(2)}, u32[]{:S(2)}) %collective-permute-start.3) | collective-permute-done | bytes 131104 | tf_op jit(solution)/shard_map/ppermute | solution.py:523
  20.8 0.8 %shard_map.142 = bf16[592,128]{1,0:T(8,128)(2,1)S(1)} custom-call(s32[3]{0:T(128)S(1)} %pad_add_fusion.2.ids_ref, s32[2,128]{1,0:T(2,128)S(1)} %get-tuple-element.46.begin_ref, bf16[128,512]{1,0:T(8,128)(2,1)S(1)} %collective-permute-done.4.refs_0_, bf16[128,512]{1,0:T(8,128)(2,1)S(1)} %get-tuple-element.52.refs_1_.refs_4_, ...), custom_call_target="tpu_custom_call" | custom-call | flops 1500000000 | tf_op jit(solution)/shard_map/pallas_call | solution.py:562
  21.6 0.9 %collective-permute-start.6 = (bf16[592,128]{1,0:T(8,128)(2,1)S(1)}, bf16[592,128]{1,0:T(8,128)(2,1)S(1)}, u32[]{:S(2)}, u32[]{:S(2)}) collective-permute-start(bf16[592,128]{1,0:T(8,128)(2,1)S(1)} %shard_map.142), channel_id=1, source_target_pairs={{0,1},{1,0},{2,3},{3,2},{4,5},{5,4},{6,7},{7,6},{8,9},{9,8},{10,11... | collective-permute-start | bytes 454664 | tf_op jit(solution)/shard_map/ppermute | solution.py:69
  22.5 1.3 %collective-permute-start.11 = (bf16[128,512]{1,0:T(8,128)(2,1)S(1)}, bf16[128,512]{1,0:T(8,128)(2,1)S(1)}, u32[]{:S(2)}, u32[]{:S(2)}) collective-permute-start(bf16[128,512]{1,0:T(8,128)(2,1)S(1)} %get-tuple-element.61), channel_id=1, source_target_pairs={{0,4},{2,6},{4,0},{6,2},{1,5},{3,7},{5,1},{7,3},{8,12},{10,14},{12... | collective-permute-start | bytes 393224 | tf_op jit(solution)/shard_map/ppermute | solution.py:69
  24.4 1.8 %shard_map.139 = (f32[16,128]{1,0:T(8,128)S(1)}, f32[16,128]{1,0:T(8,128)S(1)}, f32[512,128]{1,0:T(8,128)S(1)}) custom-call(s32[5]{0:T(128)S(1)} %stack.72.ids_ref, s32[2,128]{1,0:T(2,128)S(1)} %get-tuple-element.46.begin_ref, bf16[128,512]{1,0:T(8,128)(2,1)S(1)} %bitcast.34, bf16[128,512]{1,0:T(8,128)(2,1)S(1)} %bitcast.37, bf16[128,512]{1,0:T(8,128)(2,1)S(1)} %bitcast.40, ...), custom_call_target="tpu_custom_call" | custom-call | flops 1500000000 | tf_op jit(solution)/shard_map/pallas_call | solution.py:562
  26.1 0.7 %collective-permute-done.6.refs_3_ = bf16[592,128]{1,0:T(8,128)(2,1)S(1)} collective-permute-done((bf16[592,128]{1,0:T(8,128)(2,1)S(1)}, bf16[592,128]{1,0:T(8,128)(2,1)S(1)}, u32[]{:S(2)}, u32[]{:S(2)}) %collective-permute-start.6) | collective-permute-done | bytes 151584 | tf_op jit(solution)/shard_map/ppermute | solution.py:69
  26.8 0.6 %shard_map.143 = (bf16[128,512]{1,0:T(8,128)(2,1)S(1)}, bf16[64,512]{1,0:T(8,128)(2,1)S(1)}, bf16[64,512]{1,0:T(8,128)(2,1)S(1)}, bf16[64,512]{1,0:T(8,128)(2,1)S(1)}, bf16[64,512]{1,0:T(8,128)(2,1)S(1)}) custom-call(s32[1]{0:T(128)} %bitcast.own_ref, bf16[160,512]{1,0:T(8,128)(2,1)S(1)} %get-tuple-element.45.refs_0_.extended_ref, ...), custom_call_target="tpu_custom_call" | custom-call | flops 2000000000 | tf_op jit(solution)/shard_map/pallas_call | solution.py:612
  27.4 0.9 %collective-permute-start.13 = (bf16[64,512]{1,0:T(8,128)(2,1)S(1)}, bf16[64,512]{1,0:T(8,128)(2,1)S(1)}, u32[]{:S(2)}, u32[]{:S(2)}) collective-permute-start(bf16[64,512]{1,0:T(8,128)(2,1)S(1)} %get-tuple-element.56.refs_0_), channel_id=1, source_target_pairs={{0,1},{1,0},{2,3},{3,2},{4,5},{5,4},{6,7},{7,6},{8,9},{9,8},{10,11... | collective-permute-start | bytes 196616 | tf_op jit(solution)/shard_map/ppermute | solution.py:69
  28.3 1.0 %collective-permute-start.16 = (bf16[64,512]{1,0:T(8,128)(2,1)S(1)}, bf16[64,512]{1,0:T(8,128)(2,1)S(1)}, u32[]{:S(2)}, u32[]{:S(2)}) collective-permute-start(bf16[64,512]{1,0:T(8,128)(2,1)S(1)} %get-tuple-element.57), channel_id=1, source_target_pairs={{0,7},{1,6},{2,5},{3,4},{4,3},{5,2},{6,1},{7,0},{8,15},{9,14},{10,... | collective-permute-start | bytes 196616 | tf_op jit(solution)/shard_map/ppermute | solution.py:69
  29.3 1.4 %collective-permute-start.15 = (bf16[64,512]{1,0:T(8,128)(2,1)S(1)}, bf16[64,512]{1,0:T(8,128)(2,1)S(1)}, u32[]{:S(2)}, u32[]{:S(2)}) collective-permute-start(bf16[64,512]{1,0:T(8,128)(2,1)S(1)} %get-tuple-element.58), channel_id=1, source_target_pairs={{0,5},{1,4},{2,7},{3,6},{4,1},{5,0},{6,3},{7,2},{8,13},{9,12},{10,... | collective-permute-start | bytes 196616 | tf_op jit(solution)/shard_map/ppermute | solution.py:69
  30.7 1.2 %collective-permute-start.14 = (bf16[64,512]{1,0:T(8,128)(2,1)S(1)}, bf16[64,512]{1,0:T(8,128)(2,1)S(1)}, u32[]{:S(2)}, u32[]{:S(2)}) collective-permute-start(bf16[64,512]{1,0:T(8,128)(2,1)S(1)} %get-tuple-element.59), channel_id=1, source_target_pairs={{0,3},{1,2},{2,1},{3,0},{4,7},{5,6},{6,5},{7,4},{8,11},{9,10},{10,... | collective-permute-start | bytes 196616 | tf_op jit(solution)/shard_map/ppermute | solution.py:69
  32.6 1.3 %collective-permute-start.8 = (bf16[64,512]{1,0:T(8,128)(2,1)S(1)}, bf16[64,512]{1,0:T(8,128)(2,1)S(1)}, u32[]{:S(2)}, u32[]{:S(2)}) collective-permute-start(bf16[64,512]{1,0:T(8,128)(2,1)S(1)} %get-tuple-element.58), channel_id=1, source_target_pairs={{0,4},{1,5},{2,6},{3,7},{4,0},{5,1},{6,2},{7,3},{8,12},{9,13},{10,... | collective-permute-start | bytes 196616 | tf_op jit(solution)/shard_map/ppermute | solution.py:69
  33.9 1.6 %collective-permute-done.15.refs_2_ = bf16[64,512]{1,0:T(8,128)(2,1)S(1)} collective-permute-done((bf16[64,512]{1,0:T(8,128)(2,1)S(1)}, bf16[64,512]{1,0:T(8,128)(2,1)S(1)}, u32[]{:S(2)}, u32[]{:S(2)}) %collective-permute-start.15) | collective-permute-done | bytes 65568 | tf_op jit(solution)/shard_map/ppermute | solution.py:69
  36.0 1.6 %shard_map.144 = (f32[256,512]{1,0:T(8,128)S(1)}, f32[256,512]{1,0:T(8,128)S(1)}) custom-call(s32[1]{0:T(128)} %bitcast.own_ref, s32[4]{0:T(128)S(1)} %pad_add_fusion.part_ref, bf16[512,512]{1,0:T(8,128)(2,1)S(1)} %bitcast.26, bf16[512,512]{1,0:T(8,128)(2,1)S(1)} %bitcast.29, bf16[160,512]{1,0:T(8,128)(2,1)S(1)} %get-tuple-element.45.refs_0_.extended_ref, ...), custom_call_target="tpu_custom_call" | custom-call | flops 2000000000 | tf_op jit(solution)/shard_map/pallas_call | solution.py:625
  37.6 0.7 %collective-permute-done.8.refs_2_ = bf16[64,512]{1,0:T(8,128)(2,1)S(1)} collective-permute-done((bf16[64,512]{1,0:T(8,128)(2,1)S(1)}, bf16[64,512]{1,0:T(8,128)(2,1)S(1)}, u32[]{:S(2)}, u32[]{:S(2)}) %collective-permute-start.8) | collective-permute-done | bytes 65568 | tf_op jit(solution)/shard_map/ppermute | solution.py:69
  38.3 1.6 %shard_map.145 = (bf16[256,512]{1,0:T(8,128)(2,1)S(1)}, bf16[256,512]{1,0:T(8,128)(2,1)S(1)}, bf16[2,64,512]{2,1,0:T(8,128)(2,1)S(1)}, bf16[2,64,512]{2,1,0:T(8,...) custom-call(s32[1]{0:T(128)} %bitcast.own_ref, s32[4]{0:T(128)S(1)} %pad_add_fusion.part_ref, ...), custom_call_target="tpu_custom_call" | custom-call | flops 2000000000 | tf_op jit(solution)/shard_map/pallas_call | solution.py:625
  40.0 1.6 %collective-permute-start.17 = (bf16[2,64,512]{2,1,0:T(8,128)(2,1)S(1)}, bf16[2,64,512]{2,1,0:T(8,128)(2,1)S(1)}, u32[]{:S(2)}, u32[]{:S(2)}) collective-permute-start(bf16[2,64,512]{2,1,0:T(8,128)(2,1)S(1)} %get-tuple-element.73), channel_id=1, source_target_pairs={{0,24},{8,16},{16,8},{24,0},{1,25},{9,17},{17,9},{25,1},{2,26},{10... | collective-permute-start | bytes 393224 | tf_op jit(solution)/shard_map/ppermute | solution.py:69
  41.6 2.8 %collective-permute-start.19 = (bf16[2,64,512]{2,1,0:T(8,128)(2,1)S(1)}, bf16[2,64,512]{2,1,0:T(8,128)(2,1)S(1)}, u32[]{:S(2)}, u32[]{:S(2)}) collective-permute-start(bf16[2,64,512]{2,1,0:T(8,128)(2,1)S(1)} %get-tuple-element.75), channel_id=1, source_target_pairs={{0,8},{8,0},{16,24},{24,16},{1,9},{9,1},{17,25},{25,17},{2,10},{10... | collective-permute-start | bytes 393224 | tf_op jit(solution)/shard_map/ppermute | solution.py:69
  44.9 0.9 %collective-permute-start.21 = (bf16[128,512]{1,0:T(8,128)(2,1)S(1)}, bf16[128,512]{1,0:T(8,128)(2,1)S(1)}, u32[]{:S(2)}, u32[]{:S(2)}) collective-permute-start(bf16[128,512]{1,0:T(8,128)(2,1)S(1)} %get-tuple-element.79), channel_id=1, source_target_pairs={{0,4},{2,6},{4,0},{6,2},{1,5},{3,7},{5,1},{7,3},{8,12},{10,14},{12... | collective-permute-start | bytes 393224 | tf_op jit(solution)/shard_map/ppermute | solution.py:69
  45.8 2.5 %collective-permute-done.17.refs_1_ = bf16[2,64,512]{2,1,0:T(8,128)(2,1)S(1)} collective-permute-done((bf16[2,64,512]{2,1,0:T(8,128)(2,1)S(1)}, bf16[2,64,512]{2,1,0:T(8,128)(2,1)S(1)}, u32[]{:S(2)}, u32[]{:S(2)}) %collective-permute-start.17) | collective-permute-done | bytes 131104 | tf_op jit(solution)/shard_map/ppermute | solution.py:69
  48.8 4.7 %collective-permute-done.18.refs_2_ = bf16[2,64,512]{2,1,0:T(8,128)(2,1)S(1)} collective-permute-done((bf16[2,64,512]{2,1,0:T(8,128)(2,1)S(1)}, bf16[2,64,512]{2,1,0:T(8,128)(2,1)S(1)}, u32[]{:S(2)}, u32[]{:S(2)}) %collective-permute-start.18) | collective-permute-done | bytes 131104 | tf_op jit(solution)/shard_map/ppermute | solution.py:69
  53.5 1.3 %shard_map.148 = (bf16[128,512]{1,0:T(8,128)(2,1)}, bf16[128,512]{1,0:T(8,128)(2,1)}, f32[64,512]{1,0:T(8,128)}, f32[64,512]{1,0:T(8,128)}) custom-call(bf16[128,256]{1,0:T(8,128)(2,1)S(1)} %get-tuple-element.69.placed_ref, f32[128,128]{1,0:T(8,128)S(1)} %get-tuple-element.70.factors_ref, f32[128,512]{1,0:T(8,128)S(1)} %get-tuple-element.71.router_cols_ref, ...), custom_call_target="tpu_custom_call" | custom-call | flops 1000000000 | tf_op jit(solution)/shard_map/pallas_call | solution.py:678
  (52 shorter events, 4.7 us)
Async XLA Ops:
  0.6 13.2 %collective-permute-start.4 = (bf16[128,512]{1,0:T(8,128)(2,1)}, bf16[128,512]{1,0:T(8,128)(2,1)S(1)}, u32[]{:S(2)}, u32[]{:S(2)}) collective-permute-start(bf16[128,512]{1,0:T(8,128)(2,1)} %bitcast.33), channel_id=1, source_target_pairs={{0,1},{1,0},{2,3},{3,2},{4,5},{5,4},{6,7},{7,6},{8,9},{9,8},{10,11... | collective-permute-start | bytes 393224 | tf_op jit(solution)/shard_map/ppermute | solution.py:69
  3.6 8.4 %collective-permute-start = (bf16[128,512]{1,0:T(8,128)(2,1)}, bf16[128,512]{1,0:T(8,128)(2,1)S(1)}, u32[]{:S(2)}, u32[]{:S(2)}) collective-permute-start(bf16[128,512]{1,0:T(8,128)(2,1)} %bitcast.35), channel_id=1, source_target_pairs={{0,8},{8,16},{16,24},{24,0},{1,9},{9,17},{17,25},{25,1},{2,10},{10... | collective-permute-start | bytes 393224 | tf_op jit(solution)/shard_map/ppermute | solution.py:523
  5.2 8.3 %collective-permute-start.1 = (bf16[128,512]{1,0:T(8,128)(2,1)}, bf16[128,512]{1,0:T(8,128)(2,1)S(1)}, u32[]{:S(2)}, u32[]{:S(2)}) collective-permute-start(bf16[128,512]{1,0:T(8,128)(2,1)} %bitcast.38), channel_id=1, source_target_pairs={{0,8},{8,16},{16,24},{24,0},{1,9},{9,17},{17,25},{25,1},{2,10},{10... | collective-permute-start | bytes 393224 | tf_op jit(solution)/shard_map/ppermute | solution.py:523
  6.8 0.7 %copy-start.8 = (bf16[512,4]{0,1:T(4,128)(2,1)S(1)}, bf16[512,4]{0,1:T(4,128)(2,1)}, u32[]{:S(2)}) copy-start(bf16[512,4]{0,1:T(4,128)(2,1)} %param.17) | copy-start | bytes 12292
  7.5 0.9 %copy-start.3 = (bf16[1,128,512]{2,1,0:T(8,128)(2,1)S(1)}, bf16[1,128,512]{2,1,0:T(8,128)(2,1)}, u32[]{:S(2)}) copy-start(bf16[1,128,512]{2,1,0:T(8,128)(2,1)} %param.21) | copy-start | bytes 393220
  8.4 5.4 %copy-start.5 = (bf16[1,128,512]{2,1,0:T(8,128)(2,1)S(1)}, bf16[1,128,512]{2,1,0:T(8,128)(2,1)}, u32[]{:S(2)}) copy-start(bf16[1,128,512]{2,1,0:T(8,128)(2,1)} %param.12) | copy-start | bytes 393220
  8.4 5.4 %copy-start.6 = (bf16[1,128,512]{2,1,0:T(8,128)(2,1)S(1)}, bf16[1,128,512]{2,1,0:T(8,128)(2,1)}, u32[]{:S(2)}) copy-start(bf16[1,128,512]{2,1,0:T(8,128)(2,1)} %param.13) | copy-start | bytes 393220
  9.0 6.8 %collective-permute-start.5 = (bf16[160,512]{1,0:T(8,128)(2,1)S(1)}, bf16[160,512]{1,0:T(8,128)(2,1)S(1)}, u32[]{:S(2)}, u32[]{:S(2)}) collective-permute-start(bf16[160,512]{1,0:T(8,128)(2,1)S(1)} %get-tuple-element.45.refs_0_.extended_ref), channel_id=1, source_target_pairs={{0,1},{1,0},{2,3},{3,2},{4,5},{5,4},{6,7},{7,6},{8,9},{9,8},{10,11... | collective-permute-start | bytes 491528 | tf_op jit(solution)/shard_map/ppermute | solution.py:69
  12.1 7.3 %collective-permute-start.2 = (bf16[128,512]{1,0:T(8,128)(2,1)S(1)}, bf16[128,512]{1,0:T(8,128)(2,1)S(1)}, u32[]{:S(2)}, u32[]{:S(2)}) collective-permute-start(bf16[128,512]{1,0:T(8,128)(2,1)S(1)} %collective-permute-done.refs_3_), channel_id=1, source_target_pairs={{0,8},{8,16},{16,24},{24,0},{1,9},{9,17},{17,25},{25,1},{2,10},{10... | collective-permute-start | bytes 393224 | tf_op jit(solution)/shard_map/ppermute | solution.py:523
  13.5 7.3 %collective-permute-start.3 = (bf16[128,512]{1,0:T(8,128)(2,1)S(1)}, bf16[128,512]{1,0:T(8,128)(2,1)S(1)}, u32[]{:S(2)}, u32[]{:S(2)}) collective-permute-start(bf16[128,512]{1,0:T(8,128)(2,1)S(1)} %collective-permute-done.1.refs_4_), channel_id=1, source_target_pairs={{0,8},{8,16},{16,24},{24,0},{1,9},{9,17},{17,25},{25,1},{2,10},{10... | collective-permute-start | bytes 393224 | tf_op jit(solution)/shard_map/ppermute | solution.py:523
  20.8 3.6 %copy-start.4 = (bf16[1,128,512]{2,1,0:T(8,128)(2,1)S(1)}, bf16[1,128,512]{2,1,0:T(8,128)(2,1)}, u32[]{:S(2)}) copy-start(bf16[1,128,512]{2,1,0:T(8,128)(2,1)} %param.11) | copy-start | bytes 393220
  21.6 5.3 %collective-permute-start.6 = (bf16[592,128]{1,0:T(8,128)(2,1)S(1)}, bf16[592,128]{1,0:T(8,128)(2,1)S(1)}, u32[]{:S(2)}, u32[]{:S(2)}) collective-permute-start(bf16[592,128]{1,0:T(8,128)(2,1)S(1)} %shard_map.142), channel_id=1, source_target_pairs={{0,1},{1,0},{2,3},{3,2},{4,5},{5,4},{6,7},{7,6},{8,9},{9,8},{10,11... | collective-permute-start | bytes 454664 | tf_op jit(solution)/shard_map/ppermute | solution.py:69
  22.5 6.8 %collective-permute-start.10 = (bf16[128,512]{1,0:T(8,128)(2,1)S(1)}, bf16[128,512]{1,0:T(8,128)(2,1)S(1)}, u32[]{:S(2)}, u32[]{:S(2)}) collective-permute-start(bf16[128,512]{1,0:T(8,128)(2,1)S(1)} %get-tuple-element.60), channel_id=1, source_target_pairs={{0,2},{2,0},{4,6},{6,4},{1,3},{3,1},{5,7},{7,5},{8,10},{10,8},{12,... | collective-permute-start | bytes 393224 | tf_op jit(solution)/shard_map/ppermute | solution.py:69
  22.5 8.2 %collective-permute-start.11 = (bf16[128,512]{1,0:T(8,128)(2,1)S(1)}, bf16[128,512]{1,0:T(8,128)(2,1)S(1)}, u32[]{:S(2)}, u32[]{:S(2)}) collective-permute-start(bf16[128,512]{1,0:T(8,128)(2,1)S(1)} %get-tuple-element.61), channel_id=1, source_target_pairs={{0,4},{2,6},{4,0},{6,2},{1,5},{3,7},{5,1},{7,3},{8,12},{10,14},{12... | collective-permute-start | bytes 393224 | tf_op jit(solution)/shard_map/ppermute | solution.py:69
  23.8 3.0 %copy-start = (bf16[512,512]{1,0:T(8,128)(2,1)S(1)}, bf16[512,512]{1,0:T(8,128)(2,1)}, u32[]{:S(2)}) copy-start(bf16[512,512]{1,0:T(8,128)(2,1)} %proj_ref.1) | copy-start | bytes 1572868
  23.8 3.0 %copy-start.7 = (bf16[1,128,512]{2,1,0:T(8,128)(2,1)S(1)}, bf16[1,128,512]{2,1,0:T(8,128)(2,1)}, u32[]{:S(2)}) copy-start(bf16[1,128,512]{2,1,0:T(8,128)(2,1)} %param.15) | copy-start | bytes 393220
  23.8 8.1 %collective-permute-start.12 = (bf16[128,512]{1,0:T(8,128)(2,1)S(1)}, bf16[128,512]{1,0:T(8,128)(2,1)S(1)}, u32[]{:S(2)}, u32[]{:S(2)}) collective-permute-start(bf16[128,512]{1,0:T(8,128)(2,1)S(1)} %get-tuple-element.62), channel_id=1, source_target_pairs={{0,6},{2,4},{4,2},{6,0},{1,7},{3,5},{5,3},{7,1},{8,14},{10,12},{12... | collective-permute-start | bytes 393224 | tf_op jit(solution)/shard_map/ppermute | solution.py:69
  26.8 9.2 %copy-start.1 = (bf16[1,512,512]{2,1,0:T(8,128)(2,1)S(1)}, bf16[1,512,512]{2,1,0:T(8,128)(2,1)}, u32[]{:S(2)}) copy-start(bf16[1,512,512]{2,1,0:T(8,128)(2,1)} %param.19) | copy-start | bytes 1572868
  26.8 9.2 %copy-start.2 = (bf16[1,512,512]{2,1,0:T(8,128)(2,1)S(1)}, bf16[1,512,512]{2,1,0:T(8,128)(2,1)}, u32[]{:S(2)}) copy-start(bf16[1,512,512]{2,1,0:T(8,128)(2,1)} %param.20) | copy-start | bytes 1572868
  27.4 5.1 %collective-permute-start.13 = (bf16[64,512]{1,0:T(8,128)(2,1)S(1)}, bf16[64,512]{1,0:T(8,128)(2,1)S(1)}, u32[]{:S(2)}, u32[]{:S(2)}) collective-permute-start(bf16[64,512]{1,0:T(8,128)(2,1)S(1)} %get-tuple-element.56.refs_0_), channel_id=1, source_target_pairs={{0,1},{1,0},{2,3},{3,2},{4,5},{5,4},{6,7},{7,6},{8,9},{9,8},{10,11... | collective-permute-start | bytes 196616 | tf_op jit(solution)/shard_map/ppermute | solution.py:69
  28.3 5.5 %collective-permute-start.16 = (bf16[64,512]{1,0:T(8,128)(2,1)S(1)}, bf16[64,512]{1,0:T(8,128)(2,1)S(1)}, u32[]{:S(2)}, u32[]{:S(2)}) collective-permute-start(bf16[64,512]{1,0:T(8,128)(2,1)S(1)} %get-tuple-element.57), channel_id=1, source_target_pairs={{0,7},{1,6},{2,5},{3,4},{4,3},{5,2},{6,1},{7,0},{8,15},{9,14},{10,... | collective-permute-start | bytes 196616 | tf_op jit(solution)/shard_map/ppermute | solution.py:69
  29.3 6.3 %collective-permute-start.15 = (bf16[64,512]{1,0:T(8,128)(2,1)S(1)}, bf16[64,512]{1,0:T(8,128)(2,1)S(1)}, u32[]{:S(2)}, u32[]{:S(2)}) collective-permute-start(bf16[64,512]{1,0:T(8,128)(2,1)S(1)} %get-tuple-element.58), channel_id=1, source_target_pairs={{0,5},{1,4},{2,7},{3,6},{4,1},{5,0},{6,3},{7,2},{8,13},{9,12},{10,... | collective-permute-start | bytes 196616 | tf_op jit(solution)/shard_map/ppermute | solution.py:69
  30.7 5.3 %collective-permute-start.14 = (bf16[64,512]{1,0:T(8,128)(2,1)S(1)}, bf16[64,512]{1,0:T(8,128)(2,1)S(1)}, u32[]{:S(2)}, u32[]{:S(2)}) collective-permute-start(bf16[64,512]{1,0:T(8,128)(2,1)S(1)} %get-tuple-element.59), channel_id=1, source_target_pairs={{0,3},{1,2},{2,1},{3,0},{4,7},{5,6},{6,5},{7,4},{8,11},{9,10},{10,... | collective-permute-start | bytes 196616 | tf_op jit(solution)/shard_map/ppermute | solution.py:69
  32.0 5.6 %collective-permute-start.7 = (bf16[64,512]{1,0:T(8,128)(2,1)S(1)}, bf16[64,512]{1,0:T(8,128)(2,1)S(1)}, u32[]{:S(2)}, u32[]{:S(2)}) collective-permute-start(bf16[64,512]{1,0:T(8,128)(2,1)S(1)} %get-tuple-element.57), channel_id=1, source_target_pairs={{0,6},{1,7},{2,4},{3,5},{4,2},{5,3},{6,0},{7,1},{8,14},{9,15},{10,... | collective-permute-start | bytes 196616 | tf_op jit(solution)/shard_map/ppermute | solution.py:69
  32.6 5.8 %collective-permute-start.8 = (bf16[64,512]{1,0:T(8,128)(2,1)S(1)}, bf16[64,512]{1,0:T(8,128)(2,1)S(1)}, u32[]{:S(2)}, u32[]{:S(2)}) collective-permute-start(bf16[64,512]{1,0:T(8,128)(2,1)S(1)} %get-tuple-element.58), channel_id=1, source_target_pairs={{0,4},{1,5},{2,6},{3,7},{4,0},{5,1},{6,2},{7,3},{8,12},{9,13},{10,... | collective-permute-start | bytes 196616 | tf_op jit(solution)/shard_map/ppermute | solution.py:69
  33.8 4.5 %collective-permute-start.9 = (bf16[64,512]{1,0:T(8,128)(2,1)S(1)}, bf16[64,512]{1,0:T(8,128)(2,1)S(1)}, u32[]{:S(2)}, u32[]{:S(2)}) collective-permute-start(bf16[64,512]{1,0:T(8,128)(2,1)S(1)} %get-tuple-element.59), channel_id=1, source_target_pairs={{0,2},{1,3},{2,0},{3,1},{4,6},{5,7},{6,4},{7,5},{8,10},{9,11},{10,... | collective-permute-start | bytes 196616 | tf_op jit(solution)/shard_map/ppermute | solution.py:69
  40.0 8.3 %collective-permute-start.17 = (bf16[2,64,512]{2,1,0:T(8,128)(2,1)S(1)}, bf16[2,64,512]{2,1,0:T(8,128)(2,1)S(1)}, u32[]{:S(2)}, u32[]{:S(2)}) collective-permute-start(bf16[2,64,512]{2,1,0:T(8,128)(2,1)S(1)} %get-tuple-element.73), channel_id=1, source_target_pairs={{0,24},{8,16},{16,8},{24,0},{1,25},{9,17},{17,9},{25,1},{2,26},{10... | collective-permute-start | bytes 393224 | tf_op jit(solution)/shard_map/ppermute | solution.py:69
  41.6 11.9 %collective-permute-start.18 = (bf16[2,64,512]{2,1,0:T(8,128)(2,1)S(1)}, bf16[2,64,512]{2,1,0:T(8,128)(2,1)S(1)}, u32[]{:S(2)}, u32[]{:S(2)}) collective-permute-start(bf16[2,64,512]{2,1,0:T(8,128)(2,1)S(1)} %get-tuple-element.74), channel_id=1, source_target_pairs={{0,16},{8,24},{16,0},{24,8},{1,17},{9,25},{17,1},{25,9},{2,18},{10... | collective-permute-start | bytes 393224 | tf_op jit(solution)/shard_map/ppermute | solution.py:69
  41.6 11.9 %collective-permute-start.19 = (bf16[2,64,512]{2,1,0:T(8,128)(2,1)S(1)}, bf16[2,64,512]{2,1,0:T(8,128)(2,1)S(1)}, u32[]{:S(2)}, u32[]{:S(2)}) collective-permute-start(bf16[2,64,512]{2,1,0:T(8,128)(2,1)S(1)} %get-tuple-element.75), channel_id=1, source_target_pairs={{0,8},{8,0},{16,24},{24,16},{1,9},{9,1},{17,25},{25,17},{2,10},{10... | collective-permute-start | bytes 393224 | tf_op jit(solution)/shard_map/ppermute | solution.py:69
  44.9 8.7 %collective-permute-start.20 = (bf16[128,512]{1,0:T(8,128)(2,1)S(1)}, bf16[128,512]{1,0:T(8,128)(2,1)S(1)}, u32[]{:S(2)}, u32[]{:S(2)}) collective-permute-start(bf16[128,512]{1,0:T(8,128)(2,1)S(1)} %get-tuple-element.78), channel_id=1, source_target_pairs={{0,6},{2,4},{4,2},{6,0},{1,7},{3,5},{5,3},{7,1},{8,14},{10,12},{12... | collective-permute-start | bytes 393224 | tf_op jit(solution)/shard_map/ppermute | solution.py:69
  44.9 8.6 %collective-permute-start.21 = (bf16[128,512]{1,0:T(8,128)(2,1)S(1)}, bf16[128,512]{1,0:T(8,128)(2,1)S(1)}, u32[]{:S(2)}, u32[]{:S(2)}) collective-permute-start(bf16[128,512]{1,0:T(8,128)(2,1)S(1)} %get-tuple-element.79), channel_id=1, source_target_pairs={{0,4},{2,6},{4,0},{6,2},{1,5},{3,7},{5,1},{7,3},{8,12},{10,14},{12... | collective-permute-start | bytes 393224 | tf_op jit(solution)/shard_map/ppermute | solution.py:69
  48.3 5.2 %collective-permute-start.22 = (bf16[128,512]{1,0:T(8,128)(2,1)S(1)}, bf16[128,512]{1,0:T(8,128)(2,1)S(1)}, u32[]{:S(2)}, u32[]{:S(2)}) collective-permute-start(bf16[128,512]{1,0:T(8,128)(2,1)S(1)} %get-tuple-element.80), channel_id=1, source_target_pairs={{0,2},{2,0},{4,6},{6,4},{1,3},{3,1},{5,7},{7,5},{8,10},{10,8},{12,... | collective-permute-start | bytes 393224 | tf_op jit(solution)/shard_map/ppermute | solution.py:69
  (2 other events, 1.3 us)

commit v24 on v22

--- a/solution.py
+++ b/solution.py
@@ -577,9 +577,10 @@
     lines.append(tuple(forward(one) for one in lines[0]))
     queries = reps.exchange([query_rows[0]] * rep_count)
     extendeds = reps.exchange([extended] * rep_count)
+    ahead, begin = lax.optimization_barrier((lines[1][0], begin))
     states = attend(((0, 0, True),), lines[:1], [0], queries, {}, False, 2.0)
-    ahead, *states[0] = lax.optimization_barrier((lines[1][0], *states[0]))
-    lines[1] = (ahead, lines[1][1])
+    behind, *states[0] = lax.optimization_barrier((lines[1][1], *states[0]))
+    lines[1] = (ahead, behind)
     for unused in range(1, reach):
         lines.append(tuple(forward(one) for one in lines[-1]))
     own_state = states

time: 54.5 us -> 54.7 us (level)
  transfers between devices with their start and end apart: 23 -> 23, of which waited for: 10 -> 9; matrix products, arithmetic and copies ran while one was open for 1% -> 1% of each run, Pallas kernels for 16% -> 16%
where the time goes in v24:
time: 54.7 us; the launch traced here: 54.4 us
  starting transfers between devices  23 us (42%)
  waiting for transfers between devices  16.3 us (30%)
  Pallas kernels  12.3 us (22%)
  local copies, waits for them, and re-layouts  1.6 us (3%)
  between operations  0.8 us (1%)
    ppermute x19, starting transfers between devices, exchange(): got[k] = lax.ppermute(chunks[k], self.axes, pairs)  18.4 us
    ppermute x19, waiting for transfers between devices, exchange(): got[k] = lax.ppermute(chunks[k], self.axes, pairs)  11.1 us
    ppermute x4, waiting for transfers between devices, forward(): lax.ppermute(array, 'seq', [(i, (i + 1) % seq_count) for i in range(seq_c...  5.25 us
    pallas_call x4, Pallas kernels, attend(): call(functools.partial(attend_kernel, plan, rep_count, len(pairs), packed...  5.17 us
    ppermute x4, starting transfers between devices, forward(): lax.ppermute(array, 'seq', [(i, (i + 1) % seq_count) for i in range(seq_c...  4.57 us
    pallas_call x2, Pallas kernels, expert_call(): call(functools.partial(expert_kernel, rep_count, rep_list, expert_count,...  3.25 us
    unnamed x22, local copies, waits for them, and re-layouts  1.6 us
    pallas_call x1, Pallas kernels, local(): call(functools.partial(finish_kernel, hot_capacity, seq_count), [shape((t...  1.26 us
  transfers between devices with their start and end apart: 23, of which 9 were waited for; matrix products, arithmetic and copies ran while one was open for 1% of the time, Pallas kernels for 16%

profile of v24, /device:TPU:0, one launch (start us, length us, event | category | flops | bytes accessed | tf_op | source)
XLA Modules:
  0.0 54.4 jit_solution(10196266982626623184)
XLA Ops:
  0.6 3.0 %collective-permute-start.4 = (bf16[128,512]{1,0:T(8,128)(2,1)}, bf16[128,512]{1,0:T(8,128)(2,1)S(1)}, u32[]{:S(2)}, u32[]{:S(2)}) collective-permute-start(bf16[128,512]{1,0:T(8,128)(2,1)} %bitcast.39), channel_id=1, source_target_pairs={{0,1},{1,0},{2,3},{3,2},{4,5},{5,4},{6,7},{7,6},{8,9},{9,8},{10,11... | collective-permute-start | bytes 393224 | tf_op jit(solution)/shard_map/ppermute | solution.py:69
  3.6 1.6 %collective-permute-start = (bf16[128,512]{1,0:T(8,128)(2,1)}, bf16[128,512]{1,0:T(8,128)(2,1)S(1)}, u32[]{:S(2)}, u32[]{:S(2)}) collective-permute-start(bf16[128,512]{1,0:T(8,128)(2,1)} %bitcast.33), channel_id=1, source_target_pairs={{0,8},{8,16},{16,24},{24,0},{1,9},{9,17},{17,25},{25,1},{2,10},{10... | collective-permute-start | bytes 393224 | tf_op jit(solution)/shard_map/ppermute | solution.py:523
  5.2 1.6 %collective-permute-start.1 = (bf16[128,512]{1,0:T(8,128)(2,1)}, bf16[128,512]{1,0:T(8,128)(2,1)S(1)}, u32[]{:S(2)}, u32[]{:S(2)}) collective-permute-start(bf16[128,512]{1,0:T(8,128)(2,1)} %bitcast.36), channel_id=1, source_target_pairs={{0,8},{8,16},{16,24},{24,0},{1,9},{9,17},{17,25},{25,1},{2,10},{10... | collective-permute-start | bytes 393224 | tf_op jit(solution)/shard_map/ppermute | solution.py:523
  6.9 0.6 %copy-done.8 = bf16[512,4]{0,1:T(4,128)(2,1)S(1)} copy-done((bf16[512,4]{0,1:T(4,128)(2,1)S(1)}, bf16[512,4]{0,1:T(4,128)(2,1)}, u32[]{:S(2)}) %copy-start.8) | copy-done | bytes 4120
  7.5 0.9 %copy-done.3 = bf16[1,128,512]{2,1,0:T(8,128)(2,1)S(1)} copy-done((bf16[1,128,512]{2,1,0:T(8,128)(2,1)S(1)}, bf16[1,128,512]{2,1,0:T(8,128)(2,1)}, u32[]{:S(2)}) %copy-start.3) | copy-done | bytes 131096
  9.9 2.2 %collective-permute-done.refs_1_.refs_3_ = bf16[128,512]{1,0:T(8,128)(2,1)S(1)} collective-permute-done((bf16[128,512]{1,0:T(8,128)(2,1)}, bf16[128,512]{1,0:T(8,128)(2,1)S(1)}, u32[]{:S(2)}, u32[]{:S(2)}) %collective-permute-start) | collective-permute-done | bytes 131104 | tf_op jit(solution)/shard_map/ppermute | solution.py:523
  12.1 1.7 %shard_map.139 = (f32[16,128]{1,0:T(8,128)S(1)}, f32[16,128]{1,0:T(8,128)S(1)}, f32[512,128]{1,0:T(8,128)S(1)}) custom-call(s32[3]{0:T(128)S(1)} %pad_add_fusion.4.ids_ref, s32[2,128]{1,0:T(2,128)S(1)} %get-tuple-element.56.begin_ref, bf16[128,512]{1,0:T(8,128)(2,1)S(1)} %bitcast.40, bf16[128,512]{1,0:T(8,128)(2,1)S(1)} %bitcast.34, ...), custom_call_target="tpu_custom_call" | custom-call | flops 2000000000 | tf_op jit(solution)/shard_map/pallas_call | solution.py:562
  13.8 1.4 %collective-permute-start.3 = (bf16[128,512]{1,0:T(8,128)(2,1)S(1)}, bf16[128,512]{1,0:T(8,128)(2,1)S(1)}, u32[]{:S(2)}, u32[]{:S(2)}) collective-permute-start(bf16[128,512]{1,0:T(8,128)(2,1)S(1)} %collective-permute-done.1.refs_2_.refs_4_), channel_id=1, source_target_pairs={{0,8},{8,16},{16,24},{24,0},{1,9},{9,17},{17,25},{25,1},{2,10},{10... | collective-permute-start | bytes 393224 | tf_op jit(solution)/shard_map/ppermute | solution.py:523
  15.3 1.9 %shard_map.141 = (f32[16,128]{1,0:T(8,128)S(1)}, f32[16,128]{1,0:T(8,128)S(1)}, f32[512,128]{1,0:T(8,128)S(1)}) custom-call(s32[4]{0:T(128)S(1)} %pad_add_fusion.7.ids_ref, s32[2,128]{1,0:T(2,128)S(1)} %get-tuple-element.56.begin_ref, bf16[128,512]{1,0:T(8,128)(2,1)S(1)} %collective-permute-done.4.refs_0_, bf16[128,512]{1,0:T(8,128)(2,1)S(1)} %bitcast.35, ...), custom_call_target="tpu_custom_call" | custom-call | flops 3000000000 | tf_op jit(solution)/shard_map/pallas_call | solution.py:562
  17.7 1.6 %collective-permute-done.2.refs_3_.refs_2_ = bf16[128,512]{1,0:T(8,128)(2,1)S(1)} collective-permute-done((bf16[128,512]{1,0:T(8,128)(2,1)S(1)}, bf16[128,512]{1,0:T(8,128)(2,1)S(1)}, u32[]{:S(2)}, u32[]{:S(2)}) %collective-permute-start.2) | collective-permute-done | bytes 131104 | tf_op jit(solution)/shard_map/ppermute | solution.py:523
  19.4 1.4 %collective-permute-done.3.refs_4_.refs_3_ = bf16[128,512]{1,0:T(8,128)(2,1)S(1)} collective-permute-done((bf16[128,512]{1,0:T(8,128)(2,1)S(1)}, bf16[128,512]{1,0:T(8,128)(2,1)S(1)}, u32[]{:S(2)}, u32[]{:S(2)}) %collective-permute-start.3) | collective-permute-done | bytes 131104 | tf_op jit(solution)/shard_map/ppermute | solution.py:523
  20.8 0.8 %shard_map.143 = bf16[592,128]{1,0:T(8,128)(2,1)S(1)} custom-call(s32[3]{0:T(128)S(1)} %pad_add_fusion.6.ids_ref, s32[2,128]{1,0:T(2,128)S(1)} %get-tuple-element.56.begin_ref, bf16[128,512]{1,0:T(8,128)(2,1)S(1)} %collective-permute-done.4.refs_0_, bf16[128,512]{1,0:T(8,128)(2,1)S(1)} %get-tuple-element.70.refs_1_.refs_4_, ...), custom_call_target="tpu_custom_call" | custom-call | flops 1500000000 | tf_op jit(solution)/shard_map/pallas_call | solution.py:562
  21.5 1.1 %collective-permute-start.6 = (bf16[592,128]{1,0:T(8,128)(2,1)S(1)}, bf16[592,128]{1,0:T(8,128)(2,1)S(1)}, u32[]{:S(2)}, u32[]{:S(2)}) collective-permute-start(bf16[592,128]{1,0:T(8,128)(2,1)S(1)} %shard_map.143), channel_id=1, source_target_pairs={{0,1},{1,0},{2,3},{3,2},{4,5},{5,4},{6,7},{7,6},{8,9},{9,8},{10,11... | collective-permute-start | bytes 454664 | tf_op jit(solution)/shard_map/ppermute | solution.py:69
  22.7 1.6 %collective-permute-start.11 = (bf16[128,512]{1,0:T(8,128)(2,1)S(1)}, bf16[128,512]{1,0:T(8,128)(2,1)S(1)}, u32[]{:S(2)}, u32[]{:S(2)}) collective-permute-start(bf16[128,512]{1,0:T(8,128)(2,1)S(1)} %get-tuple-element.79), channel_id=1, source_target_pairs={{0,4},{2,6},{4,0},{6,2},{1,5},{3,7},{5,1},{7,3},{8,12},{10,14},{12... | collective-permute-start | bytes 393224 | tf_op jit(solution)/shard_map/ppermute | solution.py:69
  24.6 0.8 %shard_map.140 = (f32[16,128]{1,0:T(8,128)S(1)}, f32[16,128]{1,0:T(8,128)S(1)}, f32[512,128]{1,0:T(8,128)S(1)}) custom-call(s32[4]{0:T(128)S(1)} %pad_add_fusion.2.ids_ref, s32[2,128]{1,0:T(2,128)S(1)} %get-tuple-element.56.begin_ref, bf16[128,512]{1,0:T(8,128)(2,1)S(1)} %bitcast.41, bf16[128,512]{1,0:T(8,128)(2,1)S(1)} %collective-permute-done.refs_1_.refs_3_, ...), custom_call_target="tpu_custom_call" | custom-call | flops 1500000000 | tf_op jit(solution)/shard_map/pallas_call | solution.py:562
  25.4 1.4 %collective-permute-done.6.refs_3_ = bf16[592,128]{1,0:T(8,128)(2,1)S(1)} collective-permute-done((bf16[592,128]{1,0:T(8,128)(2,1)S(1)}, bf16[592,128]{1,0:T(8,128)(2,1)S(1)}, u32[]{:S(2)}, u32[]{:S(2)}) %collective-permute-start.6) | collective-permute-done | bytes 151584 | tf_op jit(solution)/shard_map/ppermute | solution.py:69
  26.8 0.6 %shard_map.144 = (bf16[128,512]{1,0:T(8,128)(2,1)S(1)}, bf16[64,512]{1,0:T(8,128)(2,1)S(1)}, bf16[64,512]{1,0:T(8,128)(2,1)S(1)}, bf16[64,512]{1,0:T(8,128)(2,1)S(1)}, bf16[64,512]{1,0:T(8,128)(2,1)S(1)}) custom-call(s32[1]{0:T(128)} %bitcast.own_ref, bf16[160,512]{1,0:T(8,128)(2,1)S(1)} %get-tuple-element.54.refs_0_.extended_ref, ...), custom_call_target="tpu_custom_call" | custom-call | flops 2000000000 | tf_op jit(solution)/shard_map/pallas_call | solution.py:617
  27.4 1.1 %collective-permute-start.13 = (bf16[64,512]{1,0:T(8,128)(2,1)S(1)}, bf16[64,512]{1,0:T(8,128)(2,1)S(1)}, u32[]{:S(2)}, u32[]{:S(2)}) collective-permute-start(bf16[64,512]{1,0:T(8,128)(2,1)S(1)} %get-tuple-element.74.refs_0_), channel_id=1, source_target_pairs={{0,1},{1,0},{2,3},{3,2},{4,5},{5,4},{6,7},{7,6},{8,9},{9,8},{10,11... | collective-permute-start | bytes 196616 | tf_op jit(solution)/shard_map/ppermute | solution.py:69
  28.7 1.8 %collective-permute-start.15 = (bf16[64,512]{1,0:T(8,128)(2,1)S(1)}, bf16[64,512]{1,0:T(8,128)(2,1)S(1)}, u32[]{:S(2)}, u32[]{:S(2)}) collective-permute-start(bf16[64,512]{1,0:T(8,128)(2,1)S(1)} %get-tuple-element.76), channel_id=1, source_target_pairs={{0,5},{1,4},{2,7},{3,6},{4,1},{5,0},{6,3},{7,2},{8,13},{9,12},{10,... | collective-permute-start | bytes 196616 | tf_op jit(solution)/shard_map/ppermute | solution.py:69
  30.5 1.4 %collective-permute-start.14 = (bf16[64,512]{1,0:T(8,128)(2,1)S(1)}, bf16[64,512]{1,0:T(8,128)(2,1)S(1)}, u32[]{:S(2)}, u32[]{:S(2)}) collective-permute-start(bf16[64,512]{1,0:T(8,128)(2,1)S(1)} %get-tuple-element.77), channel_id=1, source_target_pairs={{0,3},{1,2},{2,1},{3,0},{4,7},{5,6},{6,5},{7,4},{8,11},{9,10},{10,... | collective-permute-start | bytes 196616 | tf_op jit(solution)/shard_map/ppermute | solution.py:69
  32.0 0.7 %collective-permute-start.7 = (bf16[64,512]{1,0:T(8,128)(2,1)S(1)}, bf16[64,512]{1,0:T(8,128)(2,1)S(1)}, u32[]{:S(2)}, u32[]{:S(2)}) collective-permute-start(bf16[64,512]{1,0:T(8,128)(2,1)S(1)} %get-tuple-element.75), channel_id=1, source_target_pairs={{0,6},{1,7},{2,4},{3,5},{4,2},{5,3},{6,0},{7,1},{8,14},{9,15},{10,... | collective-permute-start | bytes 196616 | tf_op jit(solution)/shard_map/ppermute | solution.py:69
  32.7 1.0 %collective-permute-start.8 = (bf16[64,512]{1,0:T(8,128)(2,1)S(1)}, bf16[64,512]{1,0:T(8,128)(2,1)S(1)}, u32[]{:S(2)}, u32[]{:S(2)}) collective-permute-start(bf16[64,512]{1,0:T(8,128)(2,1)S(1)} %get-tuple-element.76), channel_id=1, source_target_pairs={{0,4},{1,5},{2,6},{3,7},{4,0},{5,1},{6,2},{7,3},{8,12},{9,13},{10,... | collective-permute-start | bytes 196616 | tf_op jit(solution)/shard_map/ppermute | solution.py:69
  33.9 1.6 %collective-permute-done.15.refs_2_ = bf16[64,512]{1,0:T(8,128)(2,1)S(1)} collective-permute-done((bf16[64,512]{1,0:T(8,128)(2,1)S(1)}, bf16[64,512]{1,0:T(8,128)(2,1)S(1)}, u32[]{:S(2)}, u32[]{:S(2)}) %collective-permute-start.15) | collective-permute-done | bytes 65568 | tf_op jit(solution)/shard_map/ppermute | solution.py:69
  36.0 1.6 %shard_map.145 = (f32[256,512]{1,0:T(8,128)S(1)}, f32[256,512]{1,0:T(8,128)S(1)}) custom-call(s32[1]{0:T(128)} %bitcast.own_ref, s32[4]{0:T(128)S(1)} %pad_add_fusion.part_ref, bf16[512,512]{1,0:T(8,128)(2,1)S(1)} %bitcast.26, bf16[512,512]{1,0:T(8,128)(2,1)S(1)} %bitcast.29, bf16[160,512]{1,0:T(8,128)(2,1)S(1)} %get-tuple-element.54.refs_0_.extended_ref, ...), custom_call_target="tpu_custom_call" | custom-call | flops 2000000000 | tf_op jit(solution)/shard_map/pallas_call | solution.py:630
  37.6 0.7 %collective-permute-done.8.refs_2_ = bf16[64,512]{1,0:T(8,128)(2,1)S(1)} collective-permute-done((bf16[64,512]{1,0:T(8,128)(2,1)S(1)}, bf16[64,512]{1,0:T(8,128)(2,1)S(1)}, u32[]{:S(2)}, u32[]{:S(2)}) %collective-permute-start.8) | collective-permute-done | bytes 65568 | tf_op jit(solution)/shard_map/ppermute | solution.py:69
  38.3 1.6 %shard_map.146 = (bf16[256,512]{1,0:T(8,128)(2,1)S(1)}, bf16[256,512]{1,0:T(8,128)(2,1)S(1)}, bf16[2,64,512]{2,1,0:T(8,128)(2,1)S(1)}, bf16[2,64,512]{2,1,0:T(8,...) custom-call(s32[1]{0:T(128)} %bitcast.own_ref, s32[4]{0:T(128)S(1)} %pad_add_fusion.part_ref, ...), custom_call_target="tpu_custom_call" | custom-call | flops 2000000000 | tf_op jit(solution)/shard_map/pallas_call | solution.py:630
  40.0 1.6 %collective-permute-start.17 = (bf16[2,64,512]{2,1,0:T(8,128)(2,1)S(1)}, bf16[2,64,512]{2,1,0:T(8,128)(2,1)S(1)}, u32[]{:S(2)}, u32[]{:S(2)}) collective-permute-start(bf16[2,64,512]{2,1,0:T(8,128)(2,1)S(1)} %get-tuple-element.91), channel_id=1, source_target_pairs={{0,24},{8,16},{16,8},{24,0},{1,25},{9,17},{17,9},{25,1},{2,26},{10... | collective-permute-start | bytes 393224 | tf_op jit(solution)/shard_map/ppermute | solution.py:69
  41.6 2.8 %collective-permute-start.19 = (bf16[2,64,512]{2,1,0:T(8,128)(2,1)S(1)}, bf16[2,64,512]{2,1,0:T(8,128)(2,1)S(1)}, u32[]{:S(2)}, u32[]{:S(2)}) collective-permute-start(bf16[2,64,512]{2,1,0:T(8,128)(2,1)S(1)} %get-tuple-element.93), channel_id=1, source_target_pairs={{0,8},{8,0},{16,24},{24,16},{1,9},{9,1},{17,25},{25,17},{2,10},{10... | collective-permute-start | bytes 393224 | tf_op jit(solution)/shard_map/ppermute | solution.py:69
  44.9 0.9 %collective-permute-start.21 = (bf16[128,512]{1,0:T(8,128)(2,1)S(1)}, bf16[128,512]{1,0:T(8,128)(2,1)S(1)}, u32[]{:S(2)}, u32[]{:S(2)}) collective-permute-start(bf16[128,512]{1,0:T(8,128)(2,1)S(1)} %get-tuple-element.97), channel_id=1, source_target_pairs={{0,4},{2,6},{4,0},{6,2},{1,5},{3,7},{5,1},{7,3},{8,12},{10,14},{12... | collective-permute-start | bytes 393224 | tf_op jit(solution)/shard_map/ppermute | solution.py:69
  45.8 2.5 %collective-permute-done.17.refs_1_ = bf16[2,64,512]{2,1,0:T(8,128)(2,1)S(1)} collective-permute-done((bf16[2,64,512]{2,1,0:T(8,128)(2,1)S(1)}, bf16[2,64,512]{2,1,0:T(8,128)(2,1)S(1)}, u32[]{:S(2)}, u32[]{:S(2)}) %collective-permute-start.17) | collective-permute-done | bytes 131104 | tf_op jit(solution)/shard_map/ppermute | solution.py:69
  48.8 4.3 %collective-permute-done.18.refs_2_ = bf16[2,64,512]{2,1,0:T(8,128)(2,1)S(1)} collective-permute-done((bf16[2,64,512]{2,1,0:T(8,128)(2,1)S(1)}, bf16[2,64,512]{2,1,0:T(8,128)(2,1)S(1)}, u32[]{:S(2)}, u32[]{:S(2)}) %collective-permute-start.18) | collective-permute-done | bytes 131104 | tf_op jit(solution)/shard_map/ppermute | solution.py:69
  53.2 1.3 %shard_map.149 = (bf16[128,512]{1,0:T(8,128)(2,1)}, bf16[128,512]{1,0:T(8,128)(2,1)}, f32[64,512]{1,0:T(8,128)}, f32[64,512]{1,0:T(8,128)}) custom-call(bf16[128,256]{1,0:T(8,128)(2,1)S(1)} %get-tuple-element.87.placed_ref, f32[128,128]{1,0:T(8,128)S(1)} %get-tuple-element.88.factors_ref, f32[128,512]{1,0:T(8,128)S(1)} %get-tuple-element.89.router_cols_ref, ...), custom_call_target="tpu_custom_call" | custom-call | flops 1000000000 | tf_op jit(solution)/shard_map/pallas_call | solution.py:683
  (54 shorter events, 4.5 us)
Async XLA Ops:
  0.6 14.6 %collective-permute-start.4 = (bf16[128,512]{1,0:T(8,128)(2,1)}, bf16[128,512]{1,0:T(8,128)(2,1)S(1)}, u32[]{:S(2)}, u32[]{:S(2)}) collective-permute-start(bf16[128,512]{1,0:T(8,128)(2,1)} %bitcast.39), channel_id=1, source_target_pairs={{0,1},{1,0},{2,3},{3,2},{4,5},{5,4},{6,7},{7,6},{8,9},{9,8},{10,11... | collective-permute-start | bytes 393224 | tf_op jit(solution)/shard_map/ppermute | solution.py:69
  3.6 8.4 %collective-permute-start = (bf16[128,512]{1,0:T(8,128)(2,1)}, bf16[128,512]{1,0:T(8,128)(2,1)S(1)}, u32[]{:S(2)}, u32[]{:S(2)}) collective-permute-start(bf16[128,512]{1,0:T(8,128)(2,1)} %bitcast.33), channel_id=1, source_target_pairs={{0,8},{8,16},{16,24},{24,0},{1,9},{9,17},{17,25},{25,1},{2,10},{10... | collective-permute-start | bytes 393224 | tf_op jit(solution)/shard_map/ppermute | solution.py:523
  5.2 8.6 %collective-permute-start.1 = (bf16[128,512]{1,0:T(8,128)(2,1)}, bf16[128,512]{1,0:T(8,128)(2,1)S(1)}, u32[]{:S(2)}, u32[]{:S(2)}) collective-permute-start(bf16[128,512]{1,0:T(8,128)(2,1)} %bitcast.36), channel_id=1, source_target_pairs={{0,8},{8,16},{16,24},{24,0},{1,9},{9,17},{17,25},{25,1},{2,10},{10... | collective-permute-start | bytes 393224 | tf_op jit(solution)/shard_map/ppermute | solution.py:523
  6.8 0.7 %copy-start.8 = (bf16[512,4]{0,1:T(4,128)(2,1)S(1)}, bf16[512,4]{0,1:T(4,128)(2,1)}, u32[]{:S(2)}) copy-start(bf16[512,4]{0,1:T(4,128)(2,1)} %param.17) | copy-start | bytes 12292
  7.5 0.9 %copy-start.3 = (bf16[1,128,512]{2,1,0:T(8,128)(2,1)S(1)}, bf16[1,128,512]{2,1,0:T(8,128)(2,1)}, u32[]{:S(2)}) copy-start(bf16[1,128,512]{2,1,0:T(8,128)(2,1)} %param.21) | copy-start | bytes 393220
  8.4 3.6 %copy-start.4 = (bf16[1,128,512]{2,1,0:T(8,128)(2,1)S(1)}, bf16[1,128,512]{2,1,0:T(8,128)(2,1)}, u32[]{:S(2)}) copy-start(bf16[1,128,512]{2,1,0:T(8,128)(2,1)} %param.12) | copy-start | bytes 393220
  8.4 3.6 %copy-start.5 = (bf16[1,128,512]{2,1,0:T(8,128)(2,1)S(1)}, bf16[1,128,512]{2,1,0:T(8,128)(2,1)}, u32[]{:S(2)}) copy-start(bf16[1,128,512]{2,1,0:T(8,128)(2,1)} %param.13) | copy-start | bytes 393220
  8.4 3.6 %copy-start.6 = (bf16[1,128,512]{2,1,0:T(8,128)(2,1)S(1)}, bf16[1,128,512]{2,1,0:T(8,128)(2,1)}, u32[]{:S(2)}) copy-start(bf16[1,128,512]{2,1,0:T(8,128)(2,1)} %param.11) | copy-start | bytes 393220
  9.0 8.2 %collective-permute-start.5 = (bf16[160,512]{1,0:T(8,128)(2,1)S(1)}, bf16[160,512]{1,0:T(8,128)(2,1)S(1)}, u32[]{:S(2)}, u32[]{:S(2)}) collective-permute-start(bf16[160,512]{1,0:T(8,128)(2,1)S(1)} %get-tuple-element.54.refs_0_.extended_ref), channel_id=1, source_target_pairs={{0,1},{1,0},{2,3},{3,2},{4,5},{5,4},{6,7},{7,6},{8,9},{9,8},{10,11... | collective-permute-start | bytes 491528 | tf_op jit(solution)/shard_map/ppermute | solution.py:69
  12.1 7.3 %collective-permute-start.2 = (bf16[128,512]{1,0:T(8,128)(2,1)S(1)}, bf16[128,512]{1,0:T(8,128)(2,1)S(1)}, u32[]{:S(2)}, u32[]{:S(2)}) collective-permute-start(bf16[128,512]{1,0:T(8,128)(2,1)S(1)} %collective-permute-done.refs_1_.refs_3_), channel_id=1, source_target_pairs={{0,8},{8,16},{16,24},{24,0},{1,9},{9,17},{17,25},{25,1},{2,10},{10... | collective-permute-start | bytes 393224 | tf_op jit(solution)/shard_map/ppermute | solution.py:523
  13.8 6.9 %collective-permute-start.3 = (bf16[128,512]{1,0:T(8,128)(2,1)S(1)}, bf16[128,512]{1,0:T(8,128)(2,1)S(1)}, u32[]{:S(2)}, u32[]{:S(2)}) collective-permute-start(bf16[128,512]{1,0:T(8,128)(2,1)S(1)} %collective-permute-done.1.refs_2_.refs_4_), channel_id=1, source_target_pairs={{0,8},{8,16},{16,24},{24,0},{1,9},{9,17},{17,25},{25,1},{2,10},{10... | collective-permute-start | bytes 393224 | tf_op jit(solution)/shard_map/ppermute | solution.py:523
  21.5 5.3 %collective-permute-start.6 = (bf16[592,128]{1,0:T(8,128)(2,1)S(1)}, bf16[592,128]{1,0:T(8,128)(2,1)S(1)}, u32[]{:S(2)}, u32[]{:S(2)}) collective-permute-start(bf16[592,128]{1,0:T(8,128)(2,1)S(1)} %shard_map.143), channel_id=1, source_target_pairs={{0,1},{1,0},{2,3},{3,2},{4,5},{5,4},{6,7},{7,6},{8,9},{9,8},{10,11... | collective-permute-start | bytes 454664 | tf_op jit(solution)/shard_map/ppermute | solution.py:69
  22.7 6.0 %collective-permute-start.10 = (bf16[128,512]{1,0:T(8,128)(2,1)S(1)}, bf16[128,512]{1,0:T(8,128)(2,1)S(1)}, u32[]{:S(2)}, u32[]{:S(2)}) collective-permute-start(bf16[128,512]{1,0:T(8,128)(2,1)S(1)} %get-tuple-element.78), channel_id=1, source_target_pairs={{0,2},{2,0},{4,6},{6,4},{1,3},{3,1},{5,7},{7,5},{8,10},{10,8},{12,... | collective-permute-start | bytes 393224 | tf_op jit(solution)/shard_map/ppermute | solution.py:69
  22.7 7.8 %collective-permute-start.11 = (bf16[128,512]{1,0:T(8,128)(2,1)S(1)}, bf16[128,512]{1,0:T(8,128)(2,1)S(1)}, u32[]{:S(2)}, u32[]{:S(2)}) collective-permute-start(bf16[128,512]{1,0:T(8,128)(2,1)S(1)} %get-tuple-element.79), channel_id=1, source_target_pairs={{0,4},{2,6},{4,0},{6,2},{1,5},{3,7},{5,1},{7,3},{8,12},{10,14},{12... | collective-permute-start | bytes 393224 | tf_op jit(solution)/shard_map/ppermute | solution.py:69
  24.3 2.5 %copy-start = (bf16[512,512]{1,0:T(8,128)(2,1)S(1)}, bf16[512,512]{1,0:T(8,128)(2,1)}, u32[]{:S(2)}) copy-start(bf16[512,512]{1,0:T(8,128)(2,1)} %proj_ref.1) | copy-start | bytes 1572868
  24.3 2.5 %copy-start.7 = (bf16[1,128,512]{2,1,0:T(8,128)(2,1)S(1)}, bf16[1,128,512]{2,1,0:T(8,128)(2,1)}, u32[]{:S(2)}) copy-start(bf16[1,128,512]{2,1,0:T(8,128)(2,1)} %param.15) | copy-start | bytes 393220
  24.3 7.7 %collective-permute-start.12 = (bf16[128,512]{1,0:T(8,128)(2,1)S(1)}, bf16[128,512]{1,0:T(8,128)(2,1)S(1)}, u32[]{:S(2)}, u32[]{:S(2)}) collective-permute-start(bf16[128,512]{1,0:T(8,128)(2,1)S(1)} %get-tuple-element.80), channel_id=1, source_target_pairs={{0,6},{2,4},{4,2},{6,0},{1,7},{3,5},{5,3},{7,1},{8,14},{10,12},{12... | collective-permute-start | bytes 393224 | tf_op jit(solution)/shard_map/ppermute | solution.py:69
  26.8 9.2 %copy-start.1 = (bf16[1,512,512]{2,1,0:T(8,128)(2,1)S(1)}, bf16[1,512,512]{2,1,0:T(8,128)(2,1)}, u32[]{:S(2)}) copy-start(bf16[1,512,512]{2,1,0:T(8,128)(2,1)} %param.19) | copy-start | bytes 1572868
  26.8 9.2 %copy-start.2 = (bf16[1,512,512]{2,1,0:T(8,128)(2,1)S(1)}, bf16[1,512,512]{2,1,0:T(8,128)(2,1)}, u32[]{:S(2)}) copy-start(bf16[1,512,512]{2,1,0:T(8,128)(2,1)} %param.20) | copy-start | bytes 1572868
  27.4 5.3 %collective-permute-start.13 = (bf16[64,512]{1,0:T(8,128)(2,1)S(1)}, bf16[64,512]{1,0:T(8,128)(2,1)S(1)}, u32[]{:S(2)}, u32[]{:S(2)}) collective-permute-start(bf16[64,512]{1,0:T(8,128)(2,1)S(1)} %get-tuple-element.74.refs_0_), channel_id=1, source_target_pairs={{0,1},{1,0},{2,3},{3,2},{4,5},{5,4},{6,7},{7,6},{8,9},{9,8},{10,11... | collective-permute-start | bytes 196616 | tf_op jit(solution)/shard_map/ppermute | solution.py:69
  28.5 5.2 %collective-permute-start.16 = (bf16[64,512]{1,0:T(8,128)(2,1)S(1)}, bf16[64,512]{1,0:T(8,128)(2,1)S(1)}, u32[]{:S(2)}, u32[]{:S(2)}) collective-permute-start(bf16[64,512]{1,0:T(8,128)(2,1)S(1)} %get-tuple-element.75), channel_id=1, source_target_pairs={{0,7},{1,6},{2,5},{3,4},{4,3},{5,2},{6,1},{7,0},{8,15},{9,14},{10,... | collective-permute-start | bytes 196616 | tf_op jit(solution)/shard_map/ppermute | solution.py:69
  28.7 6.8 %collective-permute-start.15 = (bf16[64,512]{1,0:T(8,128)(2,1)S(1)}, bf16[64,512]{1,0:T(8,128)(2,1)S(1)}, u32[]{:S(2)}, u32[]{:S(2)}) collective-permute-start(bf16[64,512]{1,0:T(8,128)(2,1)S(1)} %get-tuple-element.76), channel_id=1, source_target_pairs={{0,5},{1,4},{2,7},{3,6},{4,1},{5,0},{6,3},{7,2},{8,13},{9,12},{10,... | collective-permute-start | bytes 196616 | tf_op jit(solution)/shard_map/ppermute | solution.py:69
  30.5 5.5 %collective-permute-start.14 = (bf16[64,512]{1,0:T(8,128)(2,1)S(1)}, bf16[64,512]{1,0:T(8,128)(2,1)S(1)}, u32[]{:S(2)}, u32[]{:S(2)}) collective-permute-start(bf16[64,512]{1,0:T(8,128)(2,1)S(1)} %get-tuple-element.77), channel_id=1, source_target_pairs={{0,3},{1,2},{2,1},{3,0},{4,7},{5,6},{6,5},{7,4},{8,11},{9,10},{10,... | collective-permute-start | bytes 196616 | tf_op jit(solution)/shard_map/ppermute | solution.py:69
  32.0 5.6 %collective-permute-start.7 = (bf16[64,512]{1,0:T(8,128)(2,1)S(1)}, bf16[64,512]{1,0:T(8,128)(2,1)S(1)}, u32[]{:S(2)}, u32[]{:S(2)}) collective-permute-start(bf16[64,512]{1,0:T(8,128)(2,1)S(1)} %get-tuple-element.75), channel_id=1, source_target_pairs={{0,6},{1,7},{2,4},{3,5},{4,2},{5,3},{6,0},{7,1},{8,14},{9,15},{10,... | collective-permute-start | bytes 196616 | tf_op jit(solution)/shard_map/ppermute | solution.py:69
  32.7 5.6 %collective-permute-start.8 = (bf16[64,512]{1,0:T(8,128)(2,1)S(1)}, bf16[64,512]{1,0:T(8,128)(2,1)S(1)}, u32[]{:S(2)}, u32[]{:S(2)}) collective-permute-start(bf16[64,512]{1,0:T(8,128)(2,1)S(1)} %get-tuple-element.76), channel_id=1, source_target_pairs={{0,4},{1,5},{2,6},{3,7},{4,0},{5,1},{6,2},{7,3},{8,12},{9,13},{10,... | collective-permute-start | bytes 196616 | tf_op jit(solution)/shard_map/ppermute | solution.py:69
  33.7 4.6 %collective-permute-start.9 = (bf16[64,512]{1,0:T(8,128)(2,1)S(1)}, bf16[64,512]{1,0:T(8,128)(2,1)S(1)}, u32[]{:S(2)}, u32[]{:S(2)}) collective-permute-start(bf16[64,512]{1,0:T(8,128)(2,1)S(1)} %get-tuple-element.77), channel_id=1, source_target_pairs={{0,2},{1,3},{2,0},{3,1},{4,6},{5,7},{6,4},{7,5},{8,10},{9,11},{10,... | collective-permute-start | bytes 196616 | tf_op jit(solution)/shard_map/ppermute | solution.py:69
  40.0 8.3 %collective-permute-start.17 = (bf16[2,64,512]{2,1,0:T(8,128)(2,1)S(1)}, bf16[2,64,512]{2,1,0:T(8,128)(2,1)S(1)}, u32[]{:S(2)}, u32[]{:S(2)}) collective-permute-start(bf16[2,64,512]{2,1,0:T(8,128)(2,1)S(1)} %get-tuple-element.91), channel_id=1, source_target_pairs={{0,24},{8,16},{16,8},{24,0},{1,25},{9,17},{17,9},{25,1},{2,26},{10... | collective-permute-start | bytes 393224 | tf_op jit(solution)/shard_map/ppermute | solution.py:69
  41.6 11.5 %collective-permute-start.18 = (bf16[2,64,512]{2,1,0:T(8,128)(2,1)S(1)}, bf16[2,64,512]{2,1,0:T(8,128)(2,1)S(1)}, u32[]{:S(2)}, u32[]{:S(2)}) collective-permute-start(bf16[2,64,512]{2,1,0:T(8,128)(2,1)S(1)} %get-tuple-element.92), channel_id=1, source_target_pairs={{0,16},{8,24},{16,0},{24,8},{1,17},{9,25},{17,1},{25,9},{2,18},{10... | collective-permute-start | bytes 393224 | tf_op jit(solution)/shard_map/ppermute | solution.py:69
  41.6 11.5 %collective-permute-start.19 = (bf16[2,64,512]{2,1,0:T(8,128)(2,1)S(1)}, bf16[2,64,512]{2,1,0:T(8,128)(2,1)S(1)}, u32[]{:S(2)}, u32[]{:S(2)}) collective-permute-start(bf16[2,64,512]{2,1,0:T(8,128)(2,1)S(1)} %get-tuple-element.93), channel_id=1, source_target_pairs={{0,8},{8,0},{16,24},{24,16},{1,9},{9,1},{17,25},{25,17},{2,10},{10... | collective-permute-start | bytes 393224 | tf_op jit(solution)/shard_map/ppermute | solution.py:69
  44.9 8.3 %collective-permute-start.20 = (bf16[128,512]{1,0:T(8,128)(2,1)S(1)}, bf16[128,512]{1,0:T(8,128)(2,1)S(1)}, u32[]{:S(2)}, u32[]{:S(2)}) collective-permute-start(bf16[128,512]{1,0:T(8,128)(2,1)S(1)} %get-tuple-element.96), channel_id=1, source_target_pairs={{0,6},{2,4},{4,2},{6,0},{1,7},{3,5},{5,3},{7,1},{8,14},{10,12},{12... | collective-permute-start | bytes 393224 | tf_op jit(solution)/shard_map/ppermute | solution.py:69
  44.9 8.2 %collective-permute-start.21 = (bf16[128,512]{1,0:T(8,128)(2,1)S(1)}, bf16[128,512]{1,0:T(8,128)(2,1)S(1)}, u32[]{:S(2)}, u32[]{:S(2)}) collective-permute-start(bf16[128,512]{1,0:T(8,128)(2,1)S(1)} %get-tuple-element.97), channel_id=1, source_target_pairs={{0,4},{2,6},{4,0},{6,2},{1,5},{3,7},{5,1},{7,3},{8,12},{10,14},{12... | collective-permute-start | bytes 393224 | tf_op jit(solution)/shard_map/ppermute | solution.py:69
  48.3 4.8 %collective-permute-start.22 = (bf16[128,512]{1,0:T(8,128)(2,1)S(1)}, bf16[128,512]{1,0:T(8,128)(2,1)S(1)}, u32[]{:S(2)}, u32[]{:S(2)}) collective-permute-start(bf16[128,512]{1,0:T(8,128)(2,1)S(1)} %get-tuple-element.98), channel_id=1, source_target_pairs={{0,2},{2,0},{4,6},{6,4},{1,3},{3,1},{5,7},{7,5},{8,10},{10,8},{12,... | collective-permute-start | bytes 393224 | tf_op jit(solution)/shard_map/ppermute | solution.py:69
  (2 other events, 1.3 us)

commit v25 on v20

--- a/solution.py
+++ b/solution.py
@@ -321,7 +321,7 @@
     row_refs, refs = refs[:row_count], refs[row_count:]
     per_rep = row_count // len(rep_list)
     if rep_list == (0,) and per_rep == sources:
-        row_refs = row_refs[:1] + row_refs[1:][::-1]
+        row_refs = row_refs[:1] + row_refs[-1:] + row_refs[1:-1]
     grad_refs, refs = refs[:grad_count], refs[grad_count:]
     own_rows = rep_list[0] == 0
     held_ref, refs = refs[-1], refs[:-1]
@@ -647,7 +647,7 @@
     )
     activated, pre_grad, *terms, kept = expert_call(
         (0,),
-        got_rows[:1] + got_rows[1:][::-1],
+        got_rows[:1] + got_rows[2:] + got_rows[1:2],
         [shape((slots, hidden))] * 2
         + [shape((2, strip, hidden))] * (seq_count - 1)
         + [shape((2, strip, hidden), jnp.float32)],

time: 54.3 us -> 54.6 us (level)
  starting transfers between devices: 22.7 us -> 23.6 us
    ppermute x19, starting transfers between devices: 18.3 us -> 19.3 us  [exchange(): got[k] = lax.ppermute(chunks[k], self.axes, pairs)]
  transfers between devices with their start and end apart: 23 -> 23, of which waited for: 10 -> 9; matrix products, arithmetic and copies ran while one was open for 1% -> 1% of each run, Pallas kernels for 16% -> 16%
where the time goes in v25:
time: 54.6 us; the launch traced here: 54.5 us
  starting transfers between devices  23.6 us (43%)
  waiting for transfers between devices  15.6 us (29%)
  Pallas kernels  12.3 us (23%)
  local copies, waits for them, and re-layouts  1.69 us (3%)
  between operations  0.86 us (2%)
    ppermute x19, starting transfers between devices, exchange(): got[k] = lax.ppermute(chunks[k], self.axes, pairs)  19.3 us
    ppermute x19, waiting for transfers between devices, exchange(): got[k] = lax.ppermute(chunks[k], self.axes, pairs)  10.3 us
    ppermute x4, waiting for transfers between devices, forward(): lax.ppermute(array, 'seq', [(i, (i + 1) % seq_count) for i in range(seq_c...  5.34 us
    pallas_call x4, Pallas kernels, attend(): call(functools.partial(attend_kernel, plan, rep_count, len(pairs), packed...  5.2 us
    ppermute x4, starting transfers between devices, forward(): lax.ppermute(array, 'seq', [(i, (i + 1) % seq_count) for i in range(seq_c...  4.37 us
    pallas_call x2, Pallas kernels, expert_call(): call(functools.partial(expert_kernel, rep_count, rep_list, expert_count,...  3.24 us
    unnamed x22, local copies, waits for them, and re-layouts  1.6 us
    pallas_call x1, Pallas kernels, local(): call(functools.partial(finish_kernel, hot_capacity, seq_count), [shape((t...  1.25 us
  transfers between devices with their start and end apart: 23, of which 9 were waited for; matrix products, arithmetic and copies ran while one was open for 1% of the time, Pallas kernels for 16%

profile of v25, /device:TPU:0, one launch (start us, length us, event | category | flops | bytes accessed | tf_op | source)
XLA Modules:
  0.0 54.5 jit_solution(7254885062959333436)
XLA Ops:
  0.6 3.0 %collective-permute-start.4 = (bf16[128,512]{1,0:T(8,128)(2,1)}, bf16[128,512]{1,0:T(8,128)(2,1)S(1)}, u32[]{:S(2)}, u32[]{:S(2)}) collective-permute-start(bf16[128,512]{1,0:T(8,128)(2,1)} %bitcast.39), channel_id=1, source_target_pairs={{0,1},{1,0},{2,3},{3,2},{4,5},{5,4},{6,7},{7,6},{8,9},{9,8},{10,11... | collective-permute-start | bytes 393224 | tf_op jit(solution)/shard_map/ppermute | solution.py:69
  3.6 1.6 %collective-permute-start = (bf16[128,512]{1,0:T(8,128)(2,1)}, bf16[128,512]{1,0:T(8,128)(2,1)S(1)}, u32[]{:S(2)}, u32[]{:S(2)}) collective-permute-start(bf16[128,512]{1,0:T(8,128)(2,1)} %bitcast.33), channel_id=1, source_target_pairs={{0,8},{8,16},{16,24},{24,0},{1,9},{9,17},{17,25},{25,1},{2,10},{10... | collective-permute-start | bytes 393224 | tf_op jit(solution)/shard_map/ppermute | solution.py:523
  5.2 1.6 %collective-permute-start.2 = (bf16[128,512]{1,0:T(8,128)(2,1)}, bf16[128,512]{1,0:T(8,128)(2,1)S(1)}, u32[]{:S(2)}, u32[]{:S(2)}) collective-permute-start(bf16[128,512]{1,0:T(8,128)(2,1)} %bitcast.36), channel_id=1, source_target_pairs={{0,8},{8,16},{16,24},{24,0},{1,9},{9,17},{17,25},{25,1},{2,10},{10... | collective-permute-start | bytes 393224 | tf_op jit(solution)/shard_map/ppermute | solution.py:523
  6.9 0.6 %copy-done.8 = bf16[512,4]{0,1:T(4,128)(2,1)S(1)} copy-done((bf16[512,4]{0,1:T(4,128)(2,1)S(1)}, bf16[512,4]{0,1:T(4,128)(2,1)}, u32[]{:S(2)}) %copy-start.8) | copy-done | bytes 4120
  7.5 0.9 %copy-done.3 = bf16[1,128,512]{2,1,0:T(8,128)(2,1)S(1)} copy-done((bf16[1,128,512]{2,1,0:T(8,128)(2,1)S(1)}, bf16[1,128,512]{2,1,0:T(8,128)(2,1)}, u32[]{:S(2)}) %copy-start.3) | copy-done | bytes 131096
  8.4 0.6 %shard_map.138 = (bf16[160,512]{1,0:T(8,128)(2,1)S(1)}, s32[2,128]{1,0:T(2,128)S(1)}) custom-call(s32[2]{0:T(128)S(1)} %pad_add_fusion.1.ranks_ref, s32[1,8]{1,0:T(1,128)S(1)} %copy-done.9, s32[1,128]{1,0:T(1,128)S(1)} %bitcast.45, bf16[4,512]{1,0:T(4,128)(2,1)S(1)} %bitcast.44, bf16[128,512]{1,0:T(8,128)(2,1)S(1)} %bitcast.32), custom_call_target="tpu_custom_call" | custom-call | flops 500000000 | tf_op jit(solution)/shard_map/pallas_call | solution.py:545
  9.0 0.6 %collective-permute-start.5 = (bf16[160,512]{1,0:T(8,128)(2,1)S(1)}, bf16[160,512]{1,0:T(8,128)(2,1)S(1)}, u32[]{:S(2)}, u32[]{:S(2)}) collective-permute-start(bf16[160,512]{1,0:T(8,128)(2,1)S(1)} %get-tuple-element.55.refs_0_.extended_ref), channel_id=1, source_target_pairs={{0,1},{1,0},{2,3},{3,2},{4,5},{5,4},{6,7},{7,6},{8,9},{9,8},{10,11... | collective-permute-start | bytes 491528 | tf_op jit(solution)/shard_map/ppermute | solution.py:69
  9.7 1.8 %shard_map.139 = (f32[16,128]{1,0:T(8,128)S(1)}, f32[16,128]{1,0:T(8,128)S(1)}, f32[512,128]{1,0:T(8,128)S(1)}) custom-call(s32[3]{0:T(128)S(1)} %pad_add_fusion.4.ids_ref, s32[2,128]{1,0:T(2,128)S(1)} %get-tuple-element.56.begin_ref, bf16[128,512]{1,0:T(8,128)(2,1)S(1)} %bitcast.40, bf16[128,512]{1,0:T(8,128)(2,1)S(1)} %bitcast.34, ...), custom_call_target="tpu_custom_call" | custom-call | flops 2000000000 | tf_op jit(solution)/shard_map/pallas_call | solution.py:562
  12.1 1.2 %collective-permute-start.1 = (bf16[128,512]{1,0:T(8,128)(2,1)S(1)}, bf16[128,512]{1,0:T(8,128)(2,1)S(1)}, u32[]{:S(2)}, u32[]{:S(2)}) collective-permute-start(bf16[128,512]{1,0:T(8,128)(2,1)S(1)} %collective-permute-done.refs_4_), channel_id=1, source_target_pairs={{0,8},{8,16},{16,24},{24,0},{1,9},{9,17},{17,25},{25,1},{2,10},{10... | collective-permute-start | bytes 393224 | tf_op jit(solution)/shard_map/ppermute | solution.py:523
  13.5 1.9 %shard_map.140 = (f32[16,128]{1,0:T(8,128)S(1)}, f32[16,128]{1,0:T(8,128)S(1)}, f32[512,128]{1,0:T(8,128)S(1)}, f32[16,128]{1,0:T(8,128)S(1)}, f32[16,128]{1,0:T(8,128)S(1)}, /*index=5*/f32[512,128]{1,0:T(8,128)S(1)}) custom-call(s32[5]{0:T(128)S(1)} %stack.81.ids_ref, s32[2,128]{1,0:T(2,128)S(1)} %get-tuple-element.56.begin_ref, ...), custom_call_target="tpu_custom_call" | custom-call | flops 4000000000 | tf_op jit(solution)/shard_map/pallas_call | solution.py:562
  16.0 4.8 %collective-permute-done.3.refs_2_.refs_3_ = bf16[128,512]{1,0:T(8,128)(2,1)S(1)} collective-permute-done((bf16[128,512]{1,0:T(8,128)(2,1)S(1)}, bf16[128,512]{1,0:T(8,128)(2,1)S(1)}, u32[]{:S(2)}, u32[]{:S(2)}) %collective-permute-start.3) | collective-permute-done | bytes 131104 | tf_op jit(solution)/shard_map/ppermute | solution.py:523
  20.8 0.8 %shard_map.143 = bf16[592,128]{1,0:T(8,128)(2,1)S(1)} custom-call(s32[3]{0:T(128)S(1)} %pad_add_fusion.5.ids_ref, s32[2,128]{1,0:T(2,128)S(1)} %get-tuple-element.56.begin_ref, bf16[128,512]{1,0:T(8,128)(2,1)S(1)} %collective-permute-done.4.refs_1_.refs_0_, bf16[128,512]{1,0:T(8,128)(2,1)S(1)} %get-tuple-element.72.refs_1_.refs_4_, ...), custom_call_target="tpu_custom_call" | custom-call | flops 1500000000 | tf_op jit(solution)/shard_map/pallas_call | solution.py:562
  21.6 1.2 %collective-permute-start.6 = (bf16[592,128]{1,0:T(8,128)(2,1)S(1)}, bf16[592,128]{1,0:T(8,128)(2,1)S(1)}, u32[]{:S(2)}, u32[]{:S(2)}) collective-permute-start(bf16[592,128]{1,0:T(8,128)(2,1)S(1)} %shard_map.143), channel_id=1, source_target_pairs={{0,1},{1,0},{2,3},{3,2},{4,5},{5,4},{6,7},{7,6},{8,9},{9,8},{10,11... | collective-permute-start | bytes 454664 | tf_op jit(solution)/shard_map/ppermute | solution.py:69
  22.9 1.6 %collective-permute-start.11 = (bf16[128,512]{1,0:T(8,128)(2,1)S(1)}, bf16[128,512]{1,0:T(8,128)(2,1)S(1)}, u32[]{:S(2)}, u32[]{:S(2)}) collective-permute-start(bf16[128,512]{1,0:T(8,128)(2,1)S(1)} %get-tuple-element.81), channel_id=1, source_target_pairs={{0,4},{2,6},{4,0},{6,2},{1,5},{3,7},{5,1},{7,3},{8,12},{10,14},{12... | collective-permute-start | bytes 393224 | tf_op jit(solution)/shard_map/ppermute | solution.py:69
  24.7 0.7 %shard_map.141 = (f32[16,128]{1,0:T(8,128)S(1)}, f32[16,128]{1,0:T(8,128)S(1)}, f32[512,128]{1,0:T(8,128)S(1)}) custom-call(s32[3]{0:T(128)S(1)} %pad_add_fusion.2.ids_ref, s32[2,128]{1,0:T(2,128)S(1)} %get-tuple-element.56.begin_ref, bf16[128,512]{1,0:T(8,128)(2,1)S(1)} %bitcast.42, bf16[128,512]{1,0:T(8,128)(2,1)S(1)} %collective-permute-done.1.refs_1_.refs_2_, ...), custom_call_target="tpu_custom_call" | custom-call | flops 1500000000 | tf_op jit(solution)/shard_map/pallas_call | solution.py:562
  25.5 1.3 %collective-permute-done.6.refs_3_ = bf16[592,128]{1,0:T(8,128)(2,1)S(1)} collective-permute-done((bf16[592,128]{1,0:T(8,128)(2,1)S(1)}, bf16[592,128]{1,0:T(8,128)(2,1)S(1)}, u32[]{:S(2)}, u32[]{:S(2)}) %collective-permute-start.6) | collective-permute-done | bytes 151584 | tf_op jit(solution)/shard_map/ppermute | solution.py:69
  26.8 0.6 %shard_map.144 = (bf16[128,512]{1,0:T(8,128)(2,1)S(1)}, bf16[64,512]{1,0:T(8,128)(2,1)S(1)}, bf16[64,512]{1,0:T(8,128)(2,1)S(1)}, bf16[64,512]{1,0:T(8,128)(2,1)S(1)}, bf16[64,512]{1,0:T(8,128)(2,1)S(1)}) custom-call(s32[1]{0:T(128)} %bitcast.own_ref, bf16[160,512]{1,0:T(8,128)(2,1)S(1)} %get-tuple-element.55.refs_0_.extended_ref, ...), custom_call_target="tpu_custom_call" | custom-call | flops 2000000000 | tf_op jit(solution)/shard_map/pallas_call | solution.py:609
  27.4 1.2 %collective-permute-start.13 = (bf16[64,512]{1,0:T(8,128)(2,1)S(1)}, bf16[64,512]{1,0:T(8,128)(2,1)S(1)}, u32[]{:S(2)}, u32[]{:S(2)}) collective-permute-start(bf16[64,512]{1,0:T(8,128)(2,1)S(1)} %get-tuple-element.76.refs_0_), channel_id=1, source_target_pairs={{0,1},{1,0},{2,3},{3,2},{4,5},{5,4},{6,7},{7,6},{8,9},{9,8},{10,11... | collective-permute-start | bytes 196616 | tf_op jit(solution)/shard_map/ppermute | solution.py:69
  28.6 1.8 %collective-permute-start.15 = (bf16[64,512]{1,0:T(8,128)(2,1)S(1)}, bf16[64,512]{1,0:T(8,128)(2,1)S(1)}, u32[]{:S(2)}, u32[]{:S(2)}) collective-permute-start(bf16[64,512]{1,0:T(8,128)(2,1)S(1)} %get-tuple-element.77), channel_id=1, source_target_pairs={{0,5},{1,4},{2,7},{3,6},{4,1},{5,0},{6,3},{7,2},{8,13},{9,12},{10,... | collective-permute-start | bytes 196616 | tf_op jit(solution)/shard_map/ppermute | solution.py:69
  30.5 1.7 %collective-permute-start.14 = (bf16[64,512]{1,0:T(8,128)(2,1)S(1)}, bf16[64,512]{1,0:T(8,128)(2,1)S(1)}, u32[]{:S(2)}, u32[]{:S(2)}) collective-permute-start(bf16[64,512]{1,0:T(8,128)(2,1)S(1)} %get-tuple-element.79), channel_id=1, source_target_pairs={{0,3},{1,2},{2,1},{3,0},{4,7},{5,6},{6,5},{7,4},{8,11},{9,10},{10,... | collective-permute-start | bytes 196616 | tf_op jit(solution)/shard_map/ppermute | solution.py:69
  32.3 1.5 %collective-permute-start.7 = (bf16[64,512]{1,0:T(8,128)(2,1)S(1)}, bf16[64,512]{1,0:T(8,128)(2,1)S(1)}, u32[]{:S(2)}, u32[]{:S(2)}) collective-permute-start(bf16[64,512]{1,0:T(8,128)(2,1)S(1)} %get-tuple-element.77), channel_id=1, source_target_pairs={{0,4},{1,5},{2,6},{3,7},{4,0},{5,1},{6,2},{7,3},{8,12},{9,13},{10,... | collective-permute-start | bytes 196616 | tf_op jit(solution)/shard_map/ppermute | solution.py:69
  33.8 0.6 %collective-permute-start.9 = (bf16[64,512]{1,0:T(8,128)(2,1)S(1)}, bf16[64,512]{1,0:T(8,128)(2,1)S(1)}, u32[]{:S(2)}, u32[]{:S(2)}) collective-permute-start(bf16[64,512]{1,0:T(8,128)(2,1)S(1)} %get-tuple-element.79), channel_id=1, source_target_pairs={{0,2},{1,3},{2,0},{3,1},{4,6},{5,7},{6,4},{7,5},{8,10},{9,11},{10,... | collective-permute-start | bytes 196616 | tf_op jit(solution)/shard_map/ppermute | solution.py:69
  34.4 0.8 %collective-permute-done.16.refs_3_ = bf16[64,512]{1,0:T(8,128)(2,1)S(1)} collective-permute-done((bf16[64,512]{1,0:T(8,128)(2,1)S(1)}, bf16[64,512]{1,0:T(8,128)(2,1)S(1)}, u32[]{:S(2)}, u32[]{:S(2)}) %collective-permute-start.16) | collective-permute-done | bytes 65568 | tf_op jit(solution)/shard_map/ppermute | solution.py:69
  35.2 1.0 %collective-permute-done.14.refs_1_ = bf16[64,512]{1,0:T(8,128)(2,1)S(1)} collective-permute-done((bf16[64,512]{1,0:T(8,128)(2,1)S(1)}, bf16[64,512]{1,0:T(8,128)(2,1)S(1)}, u32[]{:S(2)}, u32[]{:S(2)}) %collective-permute-start.14) | collective-permute-done | bytes 65568 | tf_op jit(solution)/shard_map/ppermute | solution.py:69
  36.2 1.6 %shard_map.145 = (f32[256,512]{1,0:T(8,128)S(1)}, f32[256,512]{1,0:T(8,128)S(1)}) custom-call(s32[1]{0:T(128)} %bitcast.own_ref, s32[4]{0:T(128)S(1)} %pad_add_fusion.part_ref, bf16[512,512]{1,0:T(8,128)(2,1)S(1)} %bitcast.26, bf16[512,512]{1,0:T(8,128)(2,1)S(1)} %bitcast.29, bf16[160,512]{1,0:T(8,128)(2,1)S(1)} %get-tuple-element.55.refs_0_.extended_ref, ...), custom_call_target="tpu_custom_call" | custom-call | flops 2000000000 | tf_op jit(solution)/shard_map/pallas_call | solution.py:622
  38.0 1.6 %shard_map.146 = (bf16[256,512]{1,0:T(8,128)(2,1)S(1)}, bf16[256,512]{1,0:T(8,128)(2,1)S(1)}, bf16[2,64,512]{2,1,0:T(8,128)(2,1)S(1)}, bf16[2,64,512]{2,1,0:T(8,...) custom-call(s32[1]{0:T(128)} %bitcast.own_ref, s32[4]{0:T(128)S(1)} %pad_add_fusion.part_ref, ...), custom_call_target="tpu_custom_call" | custom-call | flops 2000000000 | tf_op jit(solution)/shard_map/pallas_call | solution.py:622
  39.6 1.6 %collective-permute-start.17 = (bf16[2,64,512]{2,1,0:T(8,128)(2,1)S(1)}, bf16[2,64,512]{2,1,0:T(8,128)(2,1)S(1)}, u32[]{:S(2)}, u32[]{:S(2)}) collective-permute-start(bf16[2,64,512]{2,1,0:T(8,128)(2,1)S(1)} %get-tuple-element.93), channel_id=1, source_target_pairs={{0,24},{8,16},{16,8},{24,0},{1,25},{9,17},{17,9},{25,1},{2,26},{10... | collective-permute-start | bytes 393224 | tf_op jit(solution)/shard_map/ppermute | solution.py:69
  41.3 2.9 %collective-permute-start.19 = (bf16[2,64,512]{2,1,0:T(8,128)(2,1)S(1)}, bf16[2,64,512]{2,1,0:T(8,128)(2,1)S(1)}, u32[]{:S(2)}, u32[]{:S(2)}) collective-permute-start(bf16[2,64,512]{2,1,0:T(8,128)(2,1)S(1)} %get-tuple-element.95), channel_id=1, source_target_pairs={{0,8},{8,0},{16,24},{24,16},{1,9},{9,1},{17,25},{25,17},{2,10},{10... | collective-permute-start | bytes 393224 | tf_op jit(solution)/shard_map/ppermute | solution.py:69
  44.7 1.1 %collective-permute-start.21 = (bf16[128,512]{1,0:T(8,128)(2,1)S(1)}, bf16[128,512]{1,0:T(8,128)(2,1)S(1)}, u32[]{:S(2)}, u32[]{:S(2)}) collective-permute-start(bf16[128,512]{1,0:T(8,128)(2,1)S(1)} %get-tuple-element.99), channel_id=1, source_target_pairs={{0,4},{2,6},{4,0},{6,2},{1,5},{3,7},{5,1},{7,3},{8,12},{10,14},{12... | collective-permute-start | bytes 393224 | tf_op jit(solution)/shard_map/ppermute | solution.py:69
  45.8 2.2 %collective-permute-done.17.refs_1_ = bf16[2,64,512]{2,1,0:T(8,128)(2,1)S(1)} collective-permute-done((bf16[2,64,512]{2,1,0:T(8,128)(2,1)S(1)}, bf16[2,64,512]{2,1,0:T(8,128)(2,1)S(1)}, u32[]{:S(2)}, u32[]{:S(2)}) %collective-permute-start.17) | collective-permute-done | bytes 131104 | tf_op jit(solution)/shard_map/ppermute | solution.py:69
  48.5 4.7 %collective-permute-done.18.refs_2_ = bf16[2,64,512]{2,1,0:T(8,128)(2,1)S(1)} collective-permute-done((bf16[2,64,512]{2,1,0:T(8,128)(2,1)S(1)}, bf16[2,64,512]{2,1,0:T(8,128)(2,1)S(1)}, u32[]{:S(2)}, u32[]{:S(2)}) %collective-permute-start.18) | collective-permute-done | bytes 131104 | tf_op jit(solution)/shard_map/ppermute | solution.py:69
  53.2 1.3 %shard_map.149 = (bf16[128,512]{1,0:T(8,128)(2,1)}, bf16[128,512]{1,0:T(8,128)(2,1)}, f32[64,512]{1,0:T(8,128)}, f32[64,512]{1,0:T(8,128)}) custom-call(bf16[128,256]{1,0:T(8,128)(2,1)S(1)} %get-tuple-element.89.placed_ref, f32[128,128]{1,0:T(8,128)S(1)} %get-tuple-element.90.factors_ref, f32[128,512]{1,0:T(8,128)S(1)} %get-tuple-element.91.router_cols_ref, ...), custom_call_target="tpu_custom_call" | custom-call | flops 1000000000 | tf_op jit(solution)/shard_map/pallas_call | solution.py:675
  (54 shorter events, 3.2 us)
Async XLA Ops:
  0.6 12.8 %collective-permute-start.4 = (bf16[128,512]{1,0:T(8,128)(2,1)}, bf16[128,512]{1,0:T(8,128)(2,1)S(1)}, u32[]{:S(2)}, u32[]{:S(2)}) collective-permute-start(bf16[128,512]{1,0:T(8,128)(2,1)} %bitcast.39), channel_id=1, source_target_pairs={{0,1},{1,0},{2,3},{3,2},{4,5},{5,4},{6,7},{7,6},{8,9},{9,8},{10,11... | collective-permute-start | bytes 393224 | tf_op jit(solution)/shard_map/ppermute | solution.py:69
  3.6 8.4 %collective-permute-start = (bf16[128,512]{1,0:T(8,128)(2,1)}, bf16[128,512]{1,0:T(8,128)(2,1)S(1)}, u32[]{:S(2)}, u32[]{:S(2)}) collective-permute-start(bf16[128,512]{1,0:T(8,128)(2,1)} %bitcast.33), channel_id=1, source_target_pairs={{0,8},{8,16},{16,24},{24,0},{1,9},{9,17},{17,25},{25,1},{2,10},{10... | collective-permute-start | bytes 393224 | tf_op jit(solution)/shard_map/ppermute | solution.py:523
  5.2 8.3 %collective-permute-start.2 = (bf16[128,512]{1,0:T(8,128)(2,1)}, bf16[128,512]{1,0:T(8,128)(2,1)S(1)}, u32[]{:S(2)}, u32[]{:S(2)}) collective-permute-start(bf16[128,512]{1,0:T(8,128)(2,1)} %bitcast.36), channel_id=1, source_target_pairs={{0,8},{8,16},{16,24},{24,0},{1,9},{9,17},{17,25},{25,1},{2,10},{10... | collective-permute-start | bytes 393224 | tf_op jit(solution)/shard_map/ppermute | solution.py:523
  6.8 0.7 %copy-start.8 = (bf16[512,4]{0,1:T(4,128)(2,1)S(1)}, bf16[512,4]{0,1:T(4,128)(2,1)}, u32[]{:S(2)}) copy-start(bf16[512,4]{0,1:T(4,128)(2,1)} %param.17) | copy-start | bytes 12292
  7.5 0.9 %copy-start.3 = (bf16[1,128,512]{2,1,0:T(8,128)(2,1)S(1)}, bf16[1,128,512]{2,1,0:T(8,128)(2,1)}, u32[]{:S(2)}) copy-start(bf16[1,128,512]{2,1,0:T(8,128)(2,1)} %param.21) | copy-start | bytes 393220
  8.4 1.3 %copy-start.4 = (bf16[1,128,512]{2,1,0:T(8,128)(2,1)S(1)}, bf16[1,128,512]{2,1,0:T(8,128)(2,1)}, u32[]{:S(2)}) copy-start(bf16[1,128,512]{2,1,0:T(8,128)(2,1)} %param.12) | copy-start | bytes 393220
  8.4 1.3 %copy-start.5 = (bf16[1,128,512]{2,1,0:T(8,128)(2,1)S(1)}, bf16[1,128,512]{2,1,0:T(8,128)(2,1)}, u32[]{:S(2)}) copy-start(bf16[1,128,512]{2,1,0:T(8,128)(2,1)} %param.13) | copy-start | bytes 393220
  8.4 1.3 %copy-start.6 = (bf16[1,128,512]{2,1,0:T(8,128)(2,1)S(1)}, bf16[1,128,512]{2,1,0:T(8,128)(2,1)}, u32[]{:S(2)}) copy-start(bf16[1,128,512]{2,1,0:T(8,128)(2,1)} %param.11) | copy-start | bytes 393220
  9.0 6.4 %collective-permute-start.5 = (bf16[160,512]{1,0:T(8,128)(2,1)S(1)}, bf16[160,512]{1,0:T(8,128)(2,1)S(1)}, u32[]{:S(2)}, u32[]{:S(2)}) collective-permute-start(bf16[160,512]{1,0:T(8,128)(2,1)S(1)} %get-tuple-element.55.refs_0_.extended_ref), channel_id=1, source_target_pairs={{0,1},{1,0},{2,3},{3,2},{4,5},{5,4},{6,7},{7,6},{8,9},{9,8},{10,11... | collective-permute-start | bytes 491528 | tf_op jit(solution)/shard_map/ppermute | solution.py:69
  12.1 8.7 %collective-permute-start.1 = (bf16[128,512]{1,0:T(8,128)(2,1)S(1)}, bf16[128,512]{1,0:T(8,128)(2,1)S(1)}, u32[]{:S(2)}, u32[]{:S(2)}) collective-permute-start(bf16[128,512]{1,0:T(8,128)(2,1)S(1)} %collective-permute-done.refs_4_), channel_id=1, source_target_pairs={{0,8},{8,16},{16,24},{24,0},{1,9},{9,17},{17,25},{25,1},{2,10},{10... | collective-permute-start | bytes 393224 | tf_op jit(solution)/shard_map/ppermute | solution.py:523
  13.5 7.3 %collective-permute-start.3 = (bf16[128,512]{1,0:T(8,128)(2,1)S(1)}, bf16[128,512]{1,0:T(8,128)(2,1)S(1)}, u32[]{:S(2)}, u32[]{:S(2)}) collective-permute-start(bf16[128,512]{1,0:T(8,128)(2,1)S(1)} %collective-permute-done.2.refs_5_), channel_id=1, source_target_pairs={{0,8},{8,16},{16,24},{24,0},{1,9},{9,17},{17,25},{25,1},{2,10},{10... | collective-permute-start | bytes 393224 | tf_op jit(solution)/shard_map/ppermute | solution.py:523
  21.6 5.3 %collective-permute-start.6 = (bf16[592,128]{1,0:T(8,128)(2,1)S(1)}, bf16[592,128]{1,0:T(8,128)(2,1)S(1)}, u32[]{:S(2)}, u32[]{:S(2)}) collective-permute-start(bf16[592,128]{1,0:T(8,128)(2,1)S(1)} %shard_map.143), channel_id=1, source_target_pairs={{0,1},{1,0},{2,3},{3,2},{4,5},{5,4},{6,7},{7,6},{8,9},{9,8},{10,11... | collective-permute-start | bytes 454664 | tf_op jit(solution)/shard_map/ppermute | solution.py:69
  22.8 7.7 %collective-permute-start.10 = (bf16[128,512]{1,0:T(8,128)(2,1)S(1)}, bf16[128,512]{1,0:T(8,128)(2,1)S(1)}, u32[]{:S(2)}, u32[]{:S(2)}) collective-permute-start(bf16[128,512]{1,0:T(8,128)(2,1)S(1)} %get-tuple-element.80), channel_id=1, source_target_pairs={{0,2},{2,0},{4,6},{6,4},{1,3},{3,1},{5,7},{7,5},{8,10},{10,8},{12,... | collective-permute-start | bytes 393224 | tf_op jit(solution)/shard_map/ppermute | solution.py:69
  22.9 7.6 %collective-permute-start.11 = (bf16[128,512]{1,0:T(8,128)(2,1)S(1)}, bf16[128,512]{1,0:T(8,128)(2,1)S(1)}, u32[]{:S(2)}, u32[]{:S(2)}) collective-permute-start(bf16[128,512]{1,0:T(8,128)(2,1)S(1)} %get-tuple-element.81), channel_id=1, source_target_pairs={{0,4},{2,6},{4,0},{6,2},{1,5},{3,7},{5,1},{7,3},{8,12},{10,14},{12... | collective-permute-start | bytes 393224 | tf_op jit(solution)/shard_map/ppermute | solution.py:69
  24.4 7.8 %collective-permute-start.12 = (bf16[128,512]{1,0:T(8,128)(2,1)S(1)}, bf16[128,512]{1,0:T(8,128)(2,1)S(1)}, u32[]{:S(2)}, u32[]{:S(2)}) collective-permute-start(bf16[128,512]{1,0:T(8,128)(2,1)S(1)} %get-tuple-element.82), channel_id=1, source_target_pairs={{0,6},{2,4},{4,2},{6,0},{1,7},{3,5},{5,3},{7,1},{8,14},{10,12},{12... | collective-permute-start | bytes 393224 | tf_op jit(solution)/shard_map/ppermute | solution.py:69
  24.7 2.1 %copy-start = (bf16[512,512]{1,0:T(8,128)(2,1)S(1)}, bf16[512,512]{1,0:T(8,128)(2,1)}, u32[]{:S(2)}) copy-start(bf16[512,512]{1,0:T(8,128)(2,1)} %proj_ref.1) | copy-start | bytes 1572868
  24.7 2.1 %copy-start.7 = (bf16[1,128,512]{2,1,0:T(8,128)(2,1)S(1)}, bf16[1,128,512]{2,1,0:T(8,128)(2,1)}, u32[]{:S(2)}) copy-start(bf16[1,128,512]{2,1,0:T(8,128)(2,1)} %param.15) | copy-start | bytes 393220
  26.8 9.4 %copy-start.1 = (bf16[1,512,512]{2,1,0:T(8,128)(2,1)S(1)}, bf16[1,512,512]{2,1,0:T(8,128)(2,1)}, u32[]{:S(2)}) copy-start(bf16[1,512,512]{2,1,0:T(8,128)(2,1)} %param.19) | copy-start | bytes 1572868
  26.8 9.4 %copy-start.2 = (bf16[1,512,512]{2,1,0:T(8,128)(2,1)S(1)}, bf16[1,512,512]{2,1,0:T(8,128)(2,1)}, u32[]{:S(2)}) copy-start(bf16[1,512,512]{2,1,0:T(8,128)(2,1)} %param.20) | copy-start | bytes 1572868
  27.4 6.4 %collective-permute-start.13 = (bf16[64,512]{1,0:T(8,128)(2,1)S(1)}, bf16[64,512]{1,0:T(8,128)(2,1)S(1)}, u32[]{:S(2)}, u32[]{:S(2)}) collective-permute-start(bf16[64,512]{1,0:T(8,128)(2,1)S(1)} %get-tuple-element.76.refs_0_), channel_id=1, source_target_pairs={{0,1},{1,0},{2,3},{3,2},{4,5},{5,4},{6,7},{7,6},{8,9},{9,8},{10,11... | collective-permute-start | bytes 196616 | tf_op jit(solution)/shard_map/ppermute | solution.py:69
  28.6 5.2 %collective-permute-start.15 = (bf16[64,512]{1,0:T(8,128)(2,1)S(1)}, bf16[64,512]{1,0:T(8,128)(2,1)S(1)}, u32[]{:S(2)}, u32[]{:S(2)}) collective-permute-start(bf16[64,512]{1,0:T(8,128)(2,1)S(1)} %get-tuple-element.77), channel_id=1, source_target_pairs={{0,5},{1,4},{2,7},{3,6},{4,1},{5,0},{6,3},{7,2},{8,13},{9,12},{10,... | collective-permute-start | bytes 196616 | tf_op jit(solution)/shard_map/ppermute | solution.py:69
  30.5 4.7 %collective-permute-start.16 = (bf16[64,512]{1,0:T(8,128)(2,1)S(1)}, bf16[64,512]{1,0:T(8,128)(2,1)S(1)}, u32[]{:S(2)}, u32[]{:S(2)}) collective-permute-start(bf16[64,512]{1,0:T(8,128)(2,1)S(1)} %get-tuple-element.78), channel_id=1, source_target_pairs={{0,7},{1,6},{2,5},{3,4},{4,3},{5,2},{6,1},{7,0},{8,15},{9,14},{10,... | collective-permute-start | bytes 196616 | tf_op jit(solution)/shard_map/ppermute | solution.py:69
  30.5 5.7 %collective-permute-start.14 = (bf16[64,512]{1,0:T(8,128)(2,1)S(1)}, bf16[64,512]{1,0:T(8,128)(2,1)S(1)}, u32[]{:S(2)}, u32[]{:S(2)}) collective-permute-start(bf16[64,512]{1,0:T(8,128)(2,1)S(1)} %get-tuple-element.79), channel_id=1, source_target_pairs={{0,3},{1,2},{2,1},{3,0},{4,7},{5,6},{6,5},{7,4},{8,11},{9,10},{10,... | collective-permute-start | bytes 196616 | tf_op jit(solution)/shard_map/ppermute | solution.py:69
  32.3 5.6 %collective-permute-start.7 = (bf16[64,512]{1,0:T(8,128)(2,1)S(1)}, bf16[64,512]{1,0:T(8,128)(2,1)S(1)}, u32[]{:S(2)}, u32[]{:S(2)}) collective-permute-start(bf16[64,512]{1,0:T(8,128)(2,1)S(1)} %get-tuple-element.77), channel_id=1, source_target_pairs={{0,4},{1,5},{2,6},{3,7},{4,0},{5,1},{6,2},{7,3},{8,12},{9,13},{10,... | collective-permute-start | bytes 196616 | tf_op jit(solution)/shard_map/ppermute | solution.py:69
  33.8 4.2 %collective-permute-start.8 = (bf16[64,512]{1,0:T(8,128)(2,1)S(1)}, bf16[64,512]{1,0:T(8,128)(2,1)S(1)}, u32[]{:S(2)}, u32[]{:S(2)}) collective-permute-start(bf16[64,512]{1,0:T(8,128)(2,1)S(1)} %get-tuple-element.78), channel_id=1, source_target_pairs={{0,6},{1,7},{2,4},{3,5},{4,2},{5,3},{6,0},{7,1},{8,14},{9,15},{10,... | collective-permute-start | bytes 196616 | tf_op jit(solution)/shard_map/ppermute | solution.py:69
  33.8 4.2 %collective-permute-start.9 = (bf16[64,512]{1,0:T(8,128)(2,1)S(1)}, bf16[64,512]{1,0:T(8,128)(2,1)S(1)}, u32[]{:S(2)}, u32[]{:S(2)}) collective-permute-start(bf16[64,512]{1,0:T(8,128)(2,1)S(1)} %get-tuple-element.79), channel_id=1, source_target_pairs={{0,2},{1,3},{2,0},{3,1},{4,6},{5,7},{6,4},{7,5},{8,10},{9,11},{10,... | collective-permute-start | bytes 196616 | tf_op jit(solution)/shard_map/ppermute | solution.py:69
  39.6 8.3 %collective-permute-start.17 = (bf16[2,64,512]{2,1,0:T(8,128)(2,1)S(1)}, bf16[2,64,512]{2,1,0:T(8,128)(2,1)S(1)}, u32[]{:S(2)}, u32[]{:S(2)}) collective-permute-start(bf16[2,64,512]{2,1,0:T(8,128)(2,1)S(1)} %get-tuple-element.93), channel_id=1, source_target_pairs={{0,24},{8,16},{16,8},{24,0},{1,25},{9,17},{17,9},{25,1},{2,26},{10... | collective-permute-start | bytes 393224 | tf_op jit(solution)/shard_map/ppermute | solution.py:69
  41.2 11.9 %collective-permute-start.18 = (bf16[2,64,512]{2,1,0:T(8,128)(2,1)S(1)}, bf16[2,64,512]{2,1,0:T(8,128)(2,1)S(1)}, u32[]{:S(2)}, u32[]{:S(2)}) collective-permute-start(bf16[2,64,512]{2,1,0:T(8,128)(2,1)S(1)} %get-tuple-element.94), channel_id=1, source_target_pairs={{0,16},{8,24},{16,0},{24,8},{1,17},{9,25},{17,1},{25,9},{2,18},{10... | collective-permute-start | bytes 393224 | tf_op jit(solution)/shard_map/ppermute | solution.py:69
  41.3 11.9 %collective-permute-start.19 = (bf16[2,64,512]{2,1,0:T(8,128)(2,1)S(1)}, bf16[2,64,512]{2,1,0:T(8,128)(2,1)S(1)}, u32[]{:S(2)}, u32[]{:S(2)}) collective-permute-start(bf16[2,64,512]{2,1,0:T(8,128)(2,1)S(1)} %get-tuple-element.95), channel_id=1, source_target_pairs={{0,8},{8,0},{16,24},{24,16},{1,9},{9,1},{17,25},{25,17},{2,10},{10... | collective-permute-start | bytes 393224 | tf_op jit(solution)/shard_map/ppermute | solution.py:69
  44.6 8.6 %collective-permute-start.20 = (bf16[128,512]{1,0:T(8,128)(2,1)S(1)}, bf16[128,512]{1,0:T(8,128)(2,1)S(1)}, u32[]{:S(2)}, u32[]{:S(2)}) collective-permute-start(bf16[128,512]{1,0:T(8,128)(2,1)S(1)} %get-tuple-element.98), channel_id=1, source_target_pairs={{0,6},{2,4},{4,2},{6,0},{1,7},{3,5},{5,3},{7,1},{8,14},{10,12},{12... | collective-permute-start | bytes 393224 | tf_op jit(solution)/shard_map/ppermute | solution.py:69
  44.7 8.5 %collective-permute-start.21 = (bf16[128,512]{1,0:T(8,128)(2,1)S(1)}, bf16[128,512]{1,0:T(8,128)(2,1)S(1)}, u32[]{:S(2)}, u32[]{:S(2)}) collective-permute-start(bf16[128,512]{1,0:T(8,128)(2,1)S(1)} %get-tuple-element.99), channel_id=1, source_target_pairs={{0,4},{2,6},{4,0},{6,2},{1,5},{3,7},{5,1},{7,3},{8,12},{10,14},{12... | collective-permute-start | bytes 393224 | tf_op jit(solution)/shard_map/ppermute | solution.py:69
  48.0 5.2 %collective-permute-start.22 = (bf16[128,512]{1,0:T(8,128)(2,1)S(1)}, bf16[128,512]{1,0:T(8,128)(2,1)S(1)}, u32[]{:S(2)}, u32[]{:S(2)}) collective-permute-start(bf16[128,512]{1,0:T(8,128)(2,1)S(1)} %get-tuple-element.100), channel_id=1, source_target_pairs={{0,2},{2,0},{4,6},{6,4},{1,3},{3,1},{5,7},{7,5},{8,10},{10,8},{12,... | collective-permute-start | bytes 393224 | tf_op jit(solution)/shard_map/ppermute | solution.py:69
  (2 other events, 1.3 us)
